TPU v7x, 32 devices: a whole 2x2x4 slice. The times are simulated.
32 devices in a mesh: frames: 8 (over z, y), atoms: 4 (over x, core).
Axes of the slice: x: 2, y: 2, z: 4, core: 2. Of those that a mesh axis runs over, the one named last changes fastest.
Arguments:
- frames: float32 [512, 3, 4096], P('frames', None, 'atoms'), may hold values from -40 to 40
- mean_structure: float32 [3, 4096], P(None, 'atoms'), may hold values from -8 to 8
- eigvecs: bfloat16 [3, 4096, 256], P(None, 'atoms'), may hold values from -0.0546875 to 0.0546875
Outputs:
- covariance: float32 [3, 4096, 3, 4096], P(None, 'atoms', None, 'frames')
- projections: float32 [512, 256], P('frames', 'atoms')
All inputs are finite; a program needn't handle non-finite values.
Results may differ from a plain program's by a relative error of at most 0.0039.
Values may be sent and summed in bfloat16 or wider, within the bound.
No kernel may reach another device: no remote copies, remote signals or barrier semaphores. Data moves between devices by JAX's collectives and lax.ppermute only.
A program may use at most 128 MiB of HBM per device.

v0:
```python
import jax
import jax.numpy as jnp
from jax import lax
from jax.sharding import PartitionSpec as P

ATOMS = 4096
POLAR = 6


def polar_factor(start):
    eye = jnp.eye(3, dtype=jnp.float32)
    current = start
    for step in range(POLAR):
        gram = jnp.einsum("fki,fkj->fij", current, current, precision=lax.Precision.HIGHEST)
        current = 0.5 * jnp.einsum(
            "fik,fkj->fij", current, 3.0 * eye - gram, precision=lax.Precision.HIGHEST
        )
    return current


def per_device(frames, mean_structure, eigvecs):
    local_frames = frames.shape[0]
    local_atoms = frames.shape[2]
    frame_count = lax.axis_size("frames")
    ref_sum = jnp.sum(mean_structure, axis=1)
    ref_squares = jnp.sum(mean_structure * mean_structure)
    frame_sum = jnp.sum(frames, axis=2)
    frame_sum, ref_sum, ref_squares = lax.psum((frame_sum, ref_sum, ref_squares), "atoms")
    centre = frame_sum / ATOMS
    ref_centre = ref_sum / ATOMS
    centred = frames - centre[:, :, None]
    centred_ref = mean_structure - ref_centre[:, None]
    corr_part = jnp.einsum("fia,ja->fij", centred, centred_ref, precision=lax.Precision.HIGHEST)
    spread_part = jnp.sum(centred * centred, axis=(1, 2))
    corr, spread = lax.psum((corr_part, spread_part), "atoms")
    ref_spread = ref_squares - ATOMS * jnp.sum(ref_centre * ref_centre)
    start = corr / jnp.sqrt(spread * ref_spread + 1e-06)[:, None, None]
    rotation = polar_factor(start)
    aligned = jnp.einsum("fji,fja->fia", rotation, centred, precision=lax.Precision.HIGHEST)
    displaced = (aligned - centred_ref[None]).astype(jnp.bfloat16)
    proj_part = jnp.dot(
        displaced.reshape(local_frames, 3 * local_atoms),
        eigvecs.reshape(3 * local_atoms, eigvecs.shape[2]),
        preferred_element_type=jnp.float32,
    )
    projections = lax.psum_scatter(proj_part, "atoms", scatter_dimension=1, tiled=True)
    whole = lax.all_gather(displaced, "atoms", axis=2, tiled=True)
    col_width = ATOMS // frame_count
    total_frames = local_frames * frame_count
    blocks = whole.reshape(local_frames, 3, frame_count, col_width)
    columns = lax.all_to_all(blocks, "frames", split_axis=2, concat_axis=0, tiled=True).reshape(
        total_frames, 3, col_width
    )
    strip = jnp.einsum(
        "fcp,fdq->cpdq",
        lax.all_gather(displaced, "frames", axis=0, tiled=True),
        columns,
        preferred_element_type=jnp.float32,
    )
    covariance = strip / total_frames
    return (covariance, projections)


def solution(mesh):
    placed = (P("frames", None, "atoms"), P(None, "atoms"), P(None, "atoms", None))
    return jax.shard_map(
        per_device,
        mesh=mesh,
        in_specs=placed,
        out_specs=(P(None, "atoms", None, "frames"), P("frames", "atoms")),
        check_vma=False,
    )
```

profile of v0, /device:TPU:0, one launch (start us, length us, event | category | flops | bytes accessed | tf_op | source)
XLA Modules:
  0.0 176.8 jit_solution(14537264909150210428)
XLA Ops:
  7.2 0.0 copy-start
  7.2 0.0 all-gather.5.cloned.1.call-start
  7.2 1.5 multiply_reduce_fusion.1
  8.7 1.3 reduce_sum.45
  10.0 8.3 %all-reduce.1 = (f32[64,3]{0,1:T(4,128)S(1)}, f32[3]{0:T(128)S(1)}) all-reduce(f32[64,3]{0,1:T(4,128)S(1)} %reduce_sum.45, f32[3]{0:T(128)S(1)} %get-tuple-element.3), channel_id=1, replica_groups=mesh['frames'=8,'atoms'=4] {'atoms'}, use_global_device_ids=true, to_apply=%region_1.0 | all-reduce | flops 195 | bytes 1560 | tf_op jit(solution)/shard_map/psum | solution.py:28
  18.3 0.6 multiply_reduce_fusion.2
  18.9 0.8 broadcast_subtract_fusion.1
  19.7 1.4 multiply_reduce_fusion
  21.8 0.9 fusion.3
  22.7 6.5 %all-reduce = (f32[64,3,3]{0,2,1:T(4,128)S(1)}, f32[64]{0:T(128)S(1)}, f32[]{:T(128)}) all-reduce(f32[64,3,3]{0,2,1:T(4,128)S(1)} %fusion.3, f32[64]{0:T(128)S(1)} %get-tuple-element.9, f32[]{:T(128)} %get-tuple-element.2), channel_id=1, replica_groups=mesh['frames'=8,'atoms'=4] {'atoms'}, use_global_device_ids=true, to_apply=%region_4.0 | all-reduce | flops 641 | bytes 5128 | tf_op jit(solution)/shard_map/psum | solution.py:35
  29.9 0.1 copy.20
  30.0 0.7 convolution_subtract_fusion.6
  30.7 0.6 convolution_multiply_fusion.5
  31.3 0.7 convolution_subtract_fusion.5
  32.0 0.6 convolution_multiply_fusion.4
  32.5 0.7 convolution_subtract_fusion.4
  33.2 0.6 convolution_multiply_fusion.3
  33.8 0.7 convolution_subtract_fusion.3
  34.5 0.6 convolution_multiply_fusion.2
  35.0 0.7 convolution_subtract_fusion.2
  35.7 0.6 convolution_multiply_fusion.1
  36.3 0.7 convolution_subtract_fusion.1
  37.0 0.6 convolution_multiply_fusion
  37.6 3.5 %fusion.1 = bf16[64,3,1024]{2,1,0:T(4,128)(2,1)} fusion(f32[64,3,3]{2,1,0:T(4,128)S(1)} %convolution_multiply_fusion, f32[64,3,1024]{2,0,1:T(8,128)S(1)} %get-tuple-element.10, f32[3,1024]{1,0:T(4,128)S(1)} %broadcast_subtract_fusion.1), kind=kOutput, calls=%fused_computation.3 | convolution fusion | flops 7471104 | bytes 1194240 | tf_op jit(solution)/shard_map/fji,fja->fia/dot_general | solution.py:39
  41.1 0.0 all-gather.5.cloned.1.call-update
  41.1 0.2 reduce-scatter.4.cloned.1.call-start
  41.3 1.2 copy.28
  42.5 0.0 copy-start.1
  42.6 0.0 copy-done
  42.6 1.4 convolution_bitcast_fusion
  43.9 0.0 reduce-scatter.4.cloned.1.call-update
  44.0 0.0 all-gather.3.cloned.1.call-start
  44.0 0.0 copy-done.1
  44.0 0.7 all-gather.3.cloned.1.call-update
  44.7 19.6 %all-gather.5.cloned.1.call-done = bf16[64,3,4096]{2,1,0:T(4,128)(2,1)} async-done(((bf16[64,3,1024]{2,1,0:T(4,128)(2,1)}), bf16[64,3,4096]{2,1,0:T(4,128)(2,1)}) %all-gather.5.cloned.1.call-update) | async-done | bytes 1572880 | tf_op jit(solution)/shard_map/all_gather | solution.py:47
  64.3 4.4 %reshape.31 = bf16[64,3,8,512]{3,2,1,0:T(8,128)(2,1)S(1)} reshape(bf16[64,3,4096]{2,1,0:T(4,128)(2,1)} %all-gather.5.cloned.1.call-done) | data formatting | bytes 3145728 | tf_op jit(solution)/shard_map/reshape | solution.py:50
  68.7 1.6 copy.30
  70.4 5.5 %all-to-all-start = ((bf16[64,3,8,512]{3,0,1,2:T(8,128)(2,1)}), bf16[64,3,8,512]{3,0,1,2:T(8,128)(2,1)S(1)}, u32[]{:S(2)}, u32[]{:S(2)}) async-start(bf16[64,3,8,512]{3,0,1,2:T(8,128)(2,1)} %copy.30), calls=%async_computation | async-start | bytes 3145728 | tf_op jit(solution)/shard_map/all_to_all | solution.py:51
  75.9 10.5 %reduce-scatter.4.cloned.1.call-done = f32[64,64]{1,0:T(8,128)} async-done(((f32[256,64]{1,0:T(8,128)}), f32[64,64]{1,0:T(8,128)}) %reduce-scatter.4.cloned.1.call-update) | async-done | bytes 16400
  86.3 1.5 copy.43
  87.8 38.1 %all-to-all-done = bf16[64,3,8,512]{3,0,1,2:T(8,128)(2,1)S(1)} async-done(((bf16[64,3,8,512]{3,0,1,2:T(8,128)(2,1)}), bf16[64,3,8,512]{3,0,1,2:T(8,128)(2,1)S(1)}, u32[]{:S(2)}, u32[]{:S(2)}) %all-to-all-start) | async-done | bytes 1572896 | tf_op jit(solution)/shard_map/all_to_all | solution.py:51
  125.9 1.3 copy.31
  127.2 31.7 %all-gather.3.cloned.1.call-done = bf16[512,3,1024]{2,0,1:T(8,128)(2,1)} async-done(((bf16[64,3,1024]{2,0,1:T(8,128)(2,1)}), bf16[512,3,1024]{2,0,1:T(8,128)(2,1)}) %all-gather.3.cloned.1.call-update) | async-done | bytes 3145744 | tf_op jit(solution)/shard_map/all_gather | solution.py:56
  158.9 11.4 %broadcast_multiply_fusion = f32[3,1024,3,512]{3,1,2,0:T(8,128)} fusion(bf16[512,3,512,1]{2,0,1,3:T(8,128)(2,1)} %bitcast.50, bf16[512,3,1024]{2,0,1:T(8,128)(2,1)} %all-gather.3.cloned.1.call-done), kind=kOutput, calls=%fused_computation | convolution fusion | flops 4836556800 | bytes 23592960 | tf_op jit(solution)/shard_map/fcp,fdq->cpdq/dot_general | solution.py:54
  (4 shorter events, 0.0 us)
Async XLA Ops:
  7.2 35.4 %copy-start = (bf16[3,1024,256]{2,1,0:T(8,128)(2,1)S(1)}, bf16[3,1024,256]{2,1,0:T(8,128)(2,1)}, u32[]{:S(2)}) copy-start(bf16[3,1024,256]{2,1,0:T(8,128)(2,1)} %param.5) | copy-start | bytes 4718596
  7.2 57.1 %all-gather.5.cloned.1.call-start = ((), (), s32[]{:S(2)}) async-start(), calls=%async_computation.3 | async-start | bytes 2621440 | tf_op jit(solution)/shard_map/all_gather | solution.py:47
  41.1 45.2 %reduce-scatter.4.cloned.1.call-start = ((), (), s32[]{:S(2)}) async-start(), calls=%async_computation.4 | async-start | bytes 163840
  42.5 1.5 copy-start.1
  44.0 114.9 %all-gather.3.cloned.1.call-start = ((), (), s32[]{:S(2)}) async-start(), calls=%async_computation.2 | async-start | bytes 3538944 | tf_op jit(solution)/shard_map/all_gather | solution.py:56
  70.4 55.6 %all-to-all-start = ((bf16[64,3,8,512]{3,0,1,2:T(8,128)(2,1)}), bf16[64,3,8,512]{3,0,1,2:T(8,128)(2,1)S(1)}, u32[]{:S(2)}, u32[]{:S(2)}) async-start(bf16[64,3,8,512]{3,0,1,2:T(8,128)(2,1)} %copy.30), calls=%async_computation | async-start | bytes 3145728 | tf_op jit(solution)/shard_map/all_to_all | solution.py:51
Sparse Core Ops, SparseCore 0:
  41.2 23.0 all-gather.4
  66.7 19.5 reduce-scatter.3
  88.7 70.1 all-gather.2
where the time goes:
time: 177 us
  waiting for transfers between devices  101 us (57%)
  matrix products  24.6 us (14%)
  between operations  15.2 us (9%)
  blocking collectives  14.9 us (8%)
  local copies, waits for them, and re-layouts  10.1 us (6%)
  starting transfers between devices  5.82 us (3%)
  other arithmetic  5.56 us (3%)
    all_to_all x1, waiting for transfers between devices, per_device(): lax.all_to_all(blocks, 'frames', split_axis=2, concat_axis=0, tiled=True)  38.1 us
    all_gather x1, waiting for transfers between devices, per_device(): lax.all_gather(displaced, 'frames', axis=0, tiled=True)  31.7 us
    all_gather x1, waiting for transfers between devices, per_device(): whole = lax.all_gather(displaced, 'atoms', axis=2, tiled=True)  19.6 us
    dot_general x1, matrix products, per_device(): jnp.einsum('fcp,fdq->cpdq', lax.all_gather(displaced, 'frames', axis=0, t...  11.4 us
    unnamed x4, waiting for transfers between devices  11.2 us
    psum x1, blocking collectives, per_device(): lax.psum((frame_sum, ref_sum, ref_squares), 'atoms')  8.34 us
    psum x1, blocking collectives, per_device(): corr, spread = lax.psum((corr_part, spread_part), 'atoms')  6.54 us
    reshape x2, local copies, waits for them, and re-layouts, per_device(): blocks = whole.reshape(local_frames, 3, frame_count, col_width)  6.04 us
  transfers between devices with their start and end apart: 4, of which 4 were waited for; matrix products, arithmetic and copies ran while one was open for 6% of the time, Pallas kernels for 0%

commit v1 on v0

v1 whole, which is shorter than its diff:
```python
import functools

import jax
import jax.numpy as jnp
from jax import lax
from jax.experimental import pallas as pl
from jax.experimental.pallas import tpu as pltpu
from jax.sharding import PartitionSpec as P

POLAR = 6
LANES = 128
VMEM = pl.BlockSpec(memory_space=pltpu.VMEM)
SMEM = pl.BlockSpec(memory_space=pltpu.SMEM)
ANY = pl.BlockSpec(memory_space=pl.ANY)
BIG = pltpu.CompilerParams(vmem_limit_bytes=48 * 1024 * 1024)


def lane_mean(value):
    return jnp.sum(value, axis=1, keepdims=True) * (1.0 / value.shape[1])


def stats_kernel(x_ref, ref_ref, out_ref):
    values = []
    centred = []
    for i in range(3):
        x = x_ref[i]
        mean = lane_mean(x)
        values.append(mean)
        centred.append(x - mean)
    spread = sum(jnp.sum(c * c, axis=1, keepdims=True) for c in centred)
    values.append(spread)
    ref_mean = [lane_mean(ref_ref[j : j + 1, :]) for j in range(3)]
    ref_centred = [ref_ref[j : j + 1, :] - ref_mean[j] for j in range(3)]
    for i in range(3):
        for j in range(3):
            values.append(jnp.sum(centred[i] * ref_centred[j], axis=1, keepdims=True))
    values += ref_mean
    values.append(sum(jnp.sum(c * c, axis=1, keepdims=True) for c in ref_centred))
    lane = lax.broadcasted_iota(jnp.int32, out_ref.shape, 1)
    out = jnp.zeros(out_ref.shape, jnp.float32)
    for k, value in enumerate(values):
        out = jnp.where(lane == k, jnp.broadcast_to(value, out.shape), out)
    out_ref[...] = out


def align_kernel(parts, atoms, half_ref, *refs):
    stats = refs[:parts]
    x_ref, ref_ref, first_ref, second_ref, cols_ref = refs[parts:]
    local = x_ref.shape[2]
    rows = x_ref.shape[1]

    def columns(at):
        return [s[:, at : at + 1] for s in stats]

    means = [columns(i) for i in range(3)]
    ref_means = [columns(13 + j) for j in range(3)]
    centre = [sum(m) * (1.0 / parts) for m in means]
    ref_centre = [sum(r) * (1.0 / parts) for r in ref_means]
    off = [[m - centre[i] for m in means[i]] for i in range(3)]
    ref_off = [[r - ref_centre[j] for r in ref_means[j]] for j in range(3)]
    spread = sum(columns(3)) + local * sum(o * o for i in range(3) for o in off[i])
    ref_spread = sum(columns(16)) + local * sum(o * o for j in range(3) for o in ref_off[j])
    scale = 1.0 / jnp.sqrt(spread * ref_spread + 1e-06)
    now = [
        [
            (sum(columns(4 + 3 * i + j)) + local * sum(o * r for o, r in zip(off[i], ref_off[j]))) * scale
            for j in range(3)
        ]
        for i in range(3)
    ]
    for _ in range(POLAR):
        gram = {}
        for i in range(3):
            for j in range(i, 3):
                gram[i, j] = sum(now[k][i] * now[k][j] for k in range(3))
                gram[j, i] = gram[i, j]
        left = [
            [(3.0 if k == j else 0.0) - gram[k, j] for j in range(3)] for k in range(3)
        ]
        now = [
            [0.5 * sum(now[i][k] * left[k][j] for k in range(3)) for j in range(3)]
            for i in range(3)
        ]
    centred = [x_ref[j] - centre[j] for j in range(3)]
    block = cols_ref.shape[2]
    for i in range(3):
        target = ref_ref[i : i + 1, :] - ref_centre[i][0:1, :]
        moved = sum(now[j][i] * centred[j] for j in range(3)) - target
        moved = moved.astype(jnp.bfloat16)
        first_ref[i] = moved[: rows // 2]
        second_ref[i] = moved[rows // 2 :]
    start = pl.multiple_of(half_ref[0] * block, LANES)
    for i in range(3):
        cols_ref[i, : rows // 2, :] = first_ref[i, :, pl.ds(start, block)]
        cols_ref[i, rows // 2 :, :] = second_ref[i, :, pl.ds(start, block)]


def pick_kernel(half_ref, first_ref, second_ref, cols_ref):
    block = cols_ref.shape[2]
    rows = first_ref.shape[1]
    start = pl.multiple_of(half_ref[0] * block, LANES)
    for i in range(3):
        cols_ref[i, :rows, :] = first_ref[i, :, pl.ds(start, block)]
        cols_ref[i, rows:, :] = second_ref[i, :, pl.ds(start, block)]


def covariance_kernel(steps, parts, scale, role_ref, *refs):
    rows = refs[: 2 * steps]
    choices = [
        refs[2 * steps + p * steps : 2 * steps + (p + 1) * steps] for p in range(parts)
    ]
    out_ref, cols, sem = refs[2 * steps + parts * steps :]
    depth = choices[0][0].shape[1]

    @pl.when((pl.program_id(0) == 0) & (pl.program_id(1) == 0))
    def _():
        for p in range(parts):

            @pl.when(role_ref[0] == p)
            def _(p=p):
                copies = [
                    pltpu.make_async_copy(
                        choices[p][s], cols.at[:, pl.ds(s * depth, depth), :], sem.at[s]
                    )
                    for s in range(steps)
                ]
                for copy in copies:
                    copy.start()
                for copy in copies:
                    copy.wait()

    tile = out_ref.shape[2]
    at = pl.multiple_of(pl.program_id(1) * tile, LANES)
    left = jnp.concatenate([r[0, :, pl.ds(at, tile)] for r in rows], axis=0)
    for d in range(3):
        out_ref[0, d] = scale * lax.dot_general(
            left, cols[d], (((0,), (0,)), ((), ())), preferred_element_type=jnp.float32
        )


def ring_order(count):
    return list(range(0, count, 2)) + list(range(1, count, 2))[::-1]


def project(first, second, eigvecs, me_a, atom_axis):
    flat = jnp.concatenate([first, second], axis=1)
    proj = jnp.einsum("cfa,cak->fk", flat, eigvecs, preferred_element_type=jnp.float32)
    width = proj.shape[1] // atom_axis
    total = lax.dynamic_slice_in_dim(proj, me_a * width, width, axis=1)
    for d in range(1, atom_axis):
        share = lax.dynamic_slice_in_dim(
            proj, lax.bitwise_xor(me_a, jnp.int32(d)) * width, width, axis=1
        )
        total = total + lax.ppermute(
            share, "atoms", [(a, a ^ d) for a in range(atom_axis)]
        )
    return total


def long_axis_covariance(first, second, half, role, block, spread_pairs, scale):
    flat = jnp.concatenate([first, second], axis=1)
    rows = lax.all_gather(flat, "frames", axis=1, tiled=True)
    cut = lax.dynamic_slice_in_dim(rows, half * block, block, axis=2)
    cols = jnp.where(role == 0, cut, jnp.zeros_like(cut))
    for d, pairs in enumerate(spread_pairs):
        sent = lax.ppermute(cut, ("frames", "atoms"), pairs)
        cols = jnp.where(role == d + 1, sent, cols)
    return scale * jnp.einsum(
        "cfp,dfq->cpdq", rows, cols, preferred_element_type=jnp.float32
    )


def per_device(frames, mean_structure, eigvecs):
    local_frames, _, local_atoms = frames.shape
    frame_axis = lax.axis_size("frames")
    atom_axis = lax.axis_size("atoms")
    total_frames = local_frames * frame_axis
    block = local_atoms * atom_axis // frame_axis
    blocks = frame_axis // atom_axis
    me_f = lax.axis_index("frames")
    me_a = lax.axis_index("atoms")
    half = lax.rem(me_f, blocks).astype(jnp.int32).reshape(1)
    owner = lax.div(me_f, blocks)
    role = lax.bitwise_xor(me_a, owner).astype(jnp.int32).reshape(1)
    x = jnp.transpose(frames, (1, 0, 2))

    stats = pl.pallas_call(
        stats_kernel,
        out_shape=jax.ShapeDtypeStruct((local_frames, LANES), jnp.float32),
        in_specs=[VMEM, VMEM],
        out_specs=VMEM,
        compiler_params=BIG,
        name="local_moments",
    )(x, mean_structure)
    others = [
        lax.ppermute(stats, "atoms", [(a, a ^ d) for a in range(atom_axis)])
        for d in range(1, atom_axis)
    ]
    piece = jax.ShapeDtypeStruct((3, local_frames // 2, local_atoms), jnp.bfloat16)
    col_piece = jax.ShapeDtypeStruct((3, local_frames, block), jnp.bfloat16)
    first, second, cols = pl.pallas_call(
        functools.partial(align_kernel, atom_axis, local_atoms * atom_axis),
        out_shape=(piece, piece, col_piece),
        in_specs=[SMEM] + [VMEM] * (atom_axis + 2),
        out_specs=(VMEM, VMEM, VMEM),
        compiler_params=BIG,
        name="polar_align",
    )(half, stats, *others, x, mean_structure)

    order = ring_order(frame_axis)
    forward = [(order[i], order[(i + 1) % frame_axis]) for i in range(frame_axis)]
    backward = [(b, a) for a, b in forward]
    spread_pairs = [
        [
            (f * atom_axis + f // blocks, f * atom_axis + ((f // blocks) ^ d))
            for f in range(frame_axis)
        ]
        for d in range(1, atom_axis)
    ]

    projections = project(first, second, eigvecs, me_a, atom_axis)
    if block % LANES or frame_axis > 16:
        covariance = long_axis_covariance(
            first, second, half[0], role[0], block, spread_pairs, 1.0 / total_frames
        )
        return covariance, projections

    rows = [first, second]
    choices = [[] for _ in range(atom_axis)]

    def spread(value):
        choices[0].append(value)
        for d, pairs in enumerate(spread_pairs):
            choices[d + 1].append(lax.ppermute(value, ("frames", "atoms"), pairs))

    spread(cols)
    up, down = first, second
    for step in range(1, frame_axis):
        up = lax.ppermute(up, "frames", forward)
        down = lax.ppermute(down, "frames", backward)
        rows += [up, down]
        spread(
            pl.pallas_call(
                pick_kernel,
                out_shape=col_piece,
                in_specs=[SMEM, VMEM, VMEM],
                out_specs=VMEM,
                compiler_params=BIG,
                name="pick_columns",
            )(half, up, down)
        )

    tile = 256
    steps = frame_axis
    covariance = pl.pallas_call(
        functools.partial(covariance_kernel, steps, atom_axis, 1.0 / total_frames),
        grid=(3, local_atoms // tile),
        out_shape=jax.ShapeDtypeStruct((3, 3, local_atoms, block), jnp.float32),
        in_specs=[SMEM]
        + [pl.BlockSpec((1, local_frames // 2, local_atoms), lambda c, t: (c, 0, 0))] * (2 * steps)
        + [ANY] * (atom_axis * steps),
        out_specs=pl.BlockSpec((1, 3, tile, block), lambda c, t: (c, 0, t, 0)),
        scratch_shapes=[
            pltpu.VMEM((3, total_frames, block), jnp.bfloat16),
            pltpu.SemaphoreType.DMA((steps,)),
        ],
        compiler_params=BIG,
        name="covariance_tile",
    )(role, *rows, *[c for per_role in choices for c in per_role])
    return jnp.transpose(covariance, (0, 2, 1, 3)), projections


def solution(mesh):
    placed = (P("frames", None, "atoms"), P(None, "atoms"), P(None, "atoms", None))
    return jax.shard_map(
        per_device,
        mesh=mesh,
        in_specs=placed,
        out_specs=(P(None, "atoms", None, "frames"), P("frames", "atoms")),
        check_vma=False,
    )
```

time: 177 us -> 124 us (0.70)
  waiting for transfers between devices: 101 us -> 19.6 us
  starting transfers between devices: 5.82 us -> 57.1 us
  matrix products: 24.6 us -> 0.37 us
  Pallas kernels: 0 us -> 20.3 us
  blocking collectives: 14.9 us -> 0 us
  between operations: 15.2 us -> 1.39 us
  local copies, waits for them, and re-layouts: 10.1 us -> 22.9 us
  other arithmetic: 5.56 us -> 1.51 us
    ppermute x0 -> x44, starting transfers between devices: none -> 57.1 us  [the longest x24 38.6 us: spread(): choices[d + 1].append(lax.ppermute(value, ('frames', 'atoms'), pairs))]
    all_gather x2 -> x0, waiting for transfers between devices: 51.3 us -> none  [the longest x1 31.7 us: per_device(): lax.all_gather(displaced, 'frames', axis=0, tiled=True)]
    all_to_all x1 -> x0, waiting for transfers between devices: 38.1 us -> none  [per_device(): lax.all_to_all(blocks, 'frames', split_axis=2, concat_axis=0, tiled=True)]
    dot_general x16 -> x1, matrix products: 24.6 us -> 0.37 us  [project(): jnp.einsum('cfa,cak->fk', flat, eigvecs, preferred_element_type=jnp.float32)]
    unnamed x5 -> x106, local copies, waits for them, and re-layouts: 1.47 us -> 22.8 us
    pallas_call x0 -> x10, Pallas kernels: none -> 20.3 us  [the longest x1 12.7 us: per_device(): pl.pallas_call(functools.partial(covariance_kernel, steps, atom_axis, 1.0...]
    ppermute x0 -> x44, waiting for transfers between devices: none -> 19.6 us  [the longest x3 7.65 us: project(): lax.ppermute(share, 'atoms', [(a, a ^ d) for a in range(atom_axis)])]
    psum x2 -> x0, blocking collectives: 14.9 us -> none  [the longest x1 8.34 us: per_device(): lax.psum((frame_sum, ref_sum, ref_squares), 'atoms')]
  transfers between devices with their start and end apart: 4 -> 44, of which waited for: 4 -> 9; matrix products, arithmetic and copies ran while one was open for 6% -> 2% of each run, Pallas kernels for 0% -> 2%
where the time goes in v1:
time: 124 us; the launch traced here: 123 us
  starting transfers between devices  57.1 us (46%)
  local copies, waits for them, and re-layouts  22.9 us (18%)
  Pallas kernels  20.3 us (16%)
  waiting for transfers between devices  19.6 us (16%)
  other arithmetic  1.51 us (1%)
  between operations  1.39 us (1%)
    ppermute x24, starting transfers between devices, spread(): choices[d + 1].append(lax.ppermute(value, ('frames', 'atoms'), pairs))  38.6 us
    unnamed x106, local copies, waits for them, and re-layouts  22.8 us
    pallas_call x1, Pallas kernels, per_device(): pl.pallas_call(functools.partial(covariance_kernel, steps, atom_axis, 1.0...  12.7 us
    ppermute x7, starting transfers between devices, per_device(): down = lax.ppermute(down, 'frames', backward)  9.47 us
    ppermute x3, waiting for transfers between devices, project(): lax.ppermute(share, 'atoms', [(a, a ^ d) for a in range(atom_axis)])  7.65 us
    ppermute x7, waiting for transfers between devices, per_device(): up = lax.ppermute(up, 'frames', forward)  5.73 us
    ppermute x7, starting transfers between devices, per_device(): up = lax.ppermute(up, 'frames', forward)  4.96 us
    pallas_call x1, Pallas kernels, per_device(): pl.pallas_call(functools.partial(align_kernel, atom_axis, local_atoms * a...  4.95 us
  transfers between devices with their start and end apart: 44, of which 9 were waited for; matrix products, arithmetic and copies ran while one was open for 2% of the time, Pallas kernels for 2%

profile of v1, /device:TPU:0, one launch (start us, length us, event | category | flops | bytes accessed | tf_op | source)
XLA Modules:
  0.0 123.1 jit_solution(14221731872817790672)
XLA Ops:
  0.7 1.2 %copy-done.1 = f32[64,3,1024]{2,0,1:T(8,128)S(1)} copy-done((f32[64,3,1024]{2,0,1:T(8,128)S(1)}, f32[64,3,1024]{2,0,1:T(8,128)}, u32[]{:S(2)}) %copy-start.1) | copy-done | bytes 786456
  1.9 0.7 copy-done.33
  3.6 2.6 %collective-permute-start.1 = (f32[64,128]{1,0:T(8,128)S(1)}, f32[64,128]{1,0:T(8,128)S(1)}, u32[]{:S(2)}, u32[]{:S(2)}) collective-permute-start(f32[64,128]{1,0:T(8,128)S(1)} %local_moments.1.refs_0_), channel_id=1, source_target_pairs={{0,2},{1,3},{2,0},{3,1},{4,6},{5,7},{6,4},{7,5},{8,10},{9,11},{10,... | collective-permute-start | bytes 98312 | tf_op jit(solution)/shard_map/ppermute | solution.py:196
  6.2 1.9 %collective-permute-done.1.refs_2_ = f32[64,128]{1,0:T(8,128)S(1)} collective-permute-done((f32[64,128]{1,0:T(8,128)S(1)}, f32[64,128]{1,0:T(8,128)S(1)}, u32[]{:S(2)}, u32[]{:S(2)}) %collective-permute-start.1) | collective-permute-done | bytes 32800 | tf_op jit(solution)/shard_map/ppermute | solution.py:196
  8.1 1.4 %collective-permute-done.2.refs_3_ = f32[64,128]{1,0:T(8,128)S(1)} collective-permute-done((f32[64,128]{1,0:T(8,128)S(1)}, f32[64,128]{1,0:T(8,128)S(1)}, u32[]{:S(2)}, u32[]{:S(2)}) %collective-permute-start.2) | collective-permute-done | bytes 32800 | tf_op jit(solution)/shard_map/ppermute | solution.py:196
  9.5 1.1 copy-done.2
  11.3 4.9 %polar_align.1 = (bf16[3,32,1024]{2,1,0:T(8,128)(2,1)S(1)}, bf16[3,32,1024]{2,1,0:T(8,128)(2,1)S(1)}, bf16[3,64,512]{2,1,0:T(8,128)(2,1)}) custom-call(s32[1]{0:T(128)} %bitcast.1.half_ref, f32[64,128]{1,0:T(8,128)S(1)} %local_moments.1.refs_0_, f32[64,128]{1,0:T(8,128)S(1)} %collective-permute-done.refs_1_, f32[64,128]{1,0:T(8,128)S(1)} %collective-permute-done.1.refs_2_, ...), custom_call_target="tpu_custom_call" | custom-call | tf_op jit(solution)/shard_map/polar_align/pallas_call | solution.py:201
  16.3 1.6 %collective-permute-start.3 = (bf16[3,32,1024]{2,1,0:T(8,128)(2,1)S(1)}, bf16[3,32,1024]{2,1,0:T(8,128)(2,1)S(1)}, u32[]{:S(2)}, u32[]{:S(2)}) collective-permute-start(bf16[3,32,1024]{2,1,0:T(8,128)(2,1)S(1)} %get-tuple-element.5.refs_0_), channel_id=1, source_target_pairs={{0,8},{8,16},{16,24},{24,28},{28,20},{20,12},{12,4},{4,0},{1,9},{9... | collective-permute-start | bytes 589832 | tf_op jit(solution)/shard_map/ppermute | solution.py:239
  18.3 4.9 %collective-permute-done.3.first_ref.refs_2_ = bf16[3,32,1024]{2,1,0:T(8,128)(2,1)S(1)} collective-permute-done((bf16[3,32,1024]{2,1,0:T(8,128)(2,1)S(1)}, bf16[3,32,1024]{2,1,0:T(8,128)(2,1)S(1)}, u32[]{:S(2)}, u32[]{:S(2)}) %collective-permute-start.3) | collective-permute-done | bytes 196640 | tf_op jit(solution)/shard_map/ppermute | solution.py:239
  23.3 1.6 %collective-permute-start.5 = (bf16[3,32,1024]{2,1,0:T(8,128)(2,1)S(1)}, bf16[3,32,1024]{2,1,0:T(8,128)(2,1)S(1)}, u32[]{:S(2)}, u32[]{:S(2)}) collective-permute-start(bf16[3,32,1024]{2,1,0:T(8,128)(2,1)S(1)} %collective-permute-done.3.first_ref.refs_2_), channel_id=1, source_target_pairs={{0,8},{8,16},{16,24},{24,28},{28,20},{20,12},{12,4},{4,0},{1,9},{9... | collective-permute-start | bytes 589832 | tf_op jit(solution)/shard_map/ppermute | solution.py:239
  25.3 1.3 %collective-permute-start.17 = (bf16[3,64,512]{2,1,0:T(8,128)(2,1)}, bf16[3,64,512]{2,1,0:T(8,128)(2,1)S(1)}, u32[]{:S(2)}, u32[]{:S(2)}) collective-permute-start(bf16[3,64,512]{2,1,0:T(8,128)(2,1)} %get-tuple-element.7.refs_16_), channel_id=1, source_target_pairs={{0,1},{4,5},{9,8},{13,12},{18,19},{22,23},{27,26},{31,30}} | collective-permute-start | bytes 589832 | tf_op jit(solution)/shard_map/ppermute | solution.py:234
  26.6 2.0 %collective-permute-start.25 = (bf16[3,64,512]{2,1,0:T(8,128)(2,1)}, bf16[3,64,512]{2,1,0:T(8,128)(2,1)S(1)}, u32[]{:S(2)}, u32[]{:S(2)}) collective-permute-start(bf16[3,64,512]{2,1,0:T(8,128)(2,1)} %get-tuple-element.7.refs_16_), channel_id=1, source_target_pairs={{0,2},{4,6},{9,11},{13,15},{18,16},{22,20},{27,25},{31,29}} | collective-permute-start | bytes 589832 | tf_op jit(solution)/shard_map/ppermute | solution.py:234
  28.6 0.8 collective-permute-done.5.first_ref.refs_4_
  29.4 1.6 %collective-permute-start.7 = (bf16[3,32,1024]{2,1,0:T(8,128)(2,1)S(1)}, bf16[3,32,1024]{2,1,0:T(8,128)(2,1)S(1)}, u32[]{:S(2)}, u32[]{:S(2)}) collective-permute-start(bf16[3,32,1024]{2,1,0:T(8,128)(2,1)S(1)} %collective-permute-done.5.first_ref.refs_4_), channel_id=1, source_target_pairs={{0,8},{8,16},{16,24},{24,28},{28,20},{20,12},{12,4},{4,0},{1,9},{9... | collective-permute-start | bytes 589832 | tf_op jit(solution)/shard_map/ppermute | solution.py:239
  32.0 1.2 collective-permute-done.41
  33.2 0.8 collective-permute-start.42
  34.0 3.2 %collective-permute-done.42 = f32[64,64]{1,0:T(8,128)S(1)} collective-permute-done((f32[64,64]{1,0:T(8,128)S(1)}, f32[64,64]{1,0:T(8,128)S(1)}, u32[]{:S(2)}, u32[]{:S(2)}) %collective-permute-start.42) | collective-permute-done | bytes 16416 | tf_op jit(solution)/shard_map/ppermute | solution.py:154
  37.2 3.3 %collective-permute-done.43 = f32[64,64]{1,0:T(8,128)S(1)} collective-permute-done((f32[64,64]{1,0:T(8,128)S(1)}, f32[64,64]{1,0:T(8,128)S(1)}, u32[]{:S(2)}, u32[]{:S(2)}) %collective-permute-start.43) | collective-permute-done | bytes 16416 | tf_op jit(solution)/shard_map/ppermute | solution.py:154
  40.5 2.4 %collective-permute-start.33 = (bf16[3,64,512]{2,1,0:T(8,128)(2,1)}, bf16[3,64,512]{2,1,0:T(8,128)(2,1)S(1)}, u32[]{:S(2)}, u32[]{:S(2)}) collective-permute-start(bf16[3,64,512]{2,1,0:T(8,128)(2,1)} %get-tuple-element.7.refs_16_), channel_id=1, source_target_pairs={{0,3},{4,7},{9,10},{13,14},{18,17},{22,21},{27,24},{31,28}} | collective-permute-start | bytes 589832 | tf_op jit(solution)/shard_map/ppermute | solution.py:234
  43.0 1.3 %collective-permute-start.18 = (bf16[3,64,512]{2,1,0:T(8,128)(2,1)S(1)}, bf16[3,64,512]{2,1,0:T(8,128)(2,1)S(1)}, u32[]{:S(2)}, u32[]{:S(2)}) collective-permute-start(bf16[3,64,512]{2,1,0:T(8,128)(2,1)S(1)} %pick_columns.7.refs_17_), channel_id=1, source_target_pairs={{0,1},{4,5},{9,8},{13,12},{18,19},{22,23},{27,26},{31,30}} | collective-permute-start | bytes 589832 | tf_op jit(solution)/shard_map/ppermute | solution.py:234
  44.3 1.3 %collective-permute-start.26 = (bf16[3,64,512]{2,1,0:T(8,128)(2,1)S(1)}, bf16[3,64,512]{2,1,0:T(8,128)(2,1)S(1)}, u32[]{:S(2)}, u32[]{:S(2)}) collective-permute-start(bf16[3,64,512]{2,1,0:T(8,128)(2,1)S(1)} %pick_columns.7.refs_17_), channel_id=1, source_target_pairs={{0,2},{4,6},{9,11},{13,15},{18,16},{22,20},{27,25},{31,29}} | collective-permute-start | bytes 589832 | tf_op jit(solution)/shard_map/ppermute | solution.py:234
  45.7 2.0 %collective-permute-start.10 = (bf16[3,32,1024]{2,1,0:T(8,128)(2,1)S(1)}, bf16[3,32,1024]{2,1,0:T(8,128)(2,1)S(1)}, u32[]{:S(2)}, u32[]{:S(2)}) collective-permute-start(bf16[3,32,1024]{2,1,0:T(8,128)(2,1)S(1)} %collective-permute-done.8.second_ref.refs_7_), channel_id=1, source_target_pairs={{8,0},{16,8},{24,16},{28,24},{20,28},{12,20},{4,12},{0,4},{9,1},{1... | collective-permute-start | bytes 589832 | tf_op jit(solution)/shard_map/ppermute | solution.py:240
  47.8 2.6 %collective-permute-start.34 = (bf16[3,64,512]{2,1,0:T(8,128)(2,1)S(1)}, bf16[3,64,512]{2,1,0:T(8,128)(2,1)S(1)}, u32[]{:S(2)}, u32[]{:S(2)}) collective-permute-start(bf16[3,64,512]{2,1,0:T(8,128)(2,1)S(1)} %pick_columns.7.refs_17_), channel_id=1, source_target_pairs={{0,3},{4,7},{9,10},{13,14},{18,17},{22,21},{27,24},{31,28}} | collective-permute-start | bytes 589832 | tf_op jit(solution)/shard_map/ppermute | solution.py:234
  50.4 1.3 %collective-permute-start.19 = (bf16[3,64,512]{2,1,0:T(8,128)(2,1)S(1)}, bf16[3,64,512]{2,1,0:T(8,128)(2,1)S(1)}, u32[]{:S(2)}, u32[]{:S(2)}) collective-permute-start(bf16[3,64,512]{2,1,0:T(8,128)(2,1)S(1)} %pick_columns.8.refs_18_), channel_id=1, source_target_pairs={{0,1},{4,5},{9,8},{13,12},{18,19},{22,23},{27,26},{31,30}} | collective-permute-start | bytes 589832 | tf_op jit(solution)/shard_map/ppermute | solution.py:234
  51.8 1.4 %collective-permute-start.27 = (bf16[3,64,512]{2,1,0:T(8,128)(2,1)S(1)}, bf16[3,64,512]{2,1,0:T(8,128)(2,1)S(1)}, u32[]{:S(2)}, u32[]{:S(2)}) collective-permute-start(bf16[3,64,512]{2,1,0:T(8,128)(2,1)S(1)} %pick_columns.8.refs_18_), channel_id=1, source_target_pairs={{0,2},{4,6},{9,11},{13,15},{18,16},{22,20},{27,25},{31,29}} | collective-permute-start | bytes 589832 | tf_op jit(solution)/shard_map/ppermute | solution.py:234
  53.3 2.0 %collective-permute-start.12 = (bf16[3,32,1024]{2,1,0:T(8,128)(2,1)S(1)}, bf16[3,32,1024]{2,1,0:T(8,128)(2,1)S(1)}, u32[]{:S(2)}, u32[]{:S(2)}) collective-permute-start(bf16[3,32,1024]{2,1,0:T(8,128)(2,1)S(1)} %collective-permute-done.10.second_ref.refs_9_), channel_id=1, source_target_pairs={{8,0},{16,8},{24,16},{28,24},{20,28},{12,20},{4,12},{0,4},{9,1},{1... | collective-permute-start | bytes 589832 | tf_op jit(solution)/shard_map/ppermute | solution.py:240
  55.4 2.0 %collective-permute-start.35 = (bf16[3,64,512]{2,1,0:T(8,128)(2,1)S(1)}, bf16[3,64,512]{2,1,0:T(8,128)(2,1)S(1)}, u32[]{:S(2)}, u32[]{:S(2)}) collective-permute-start(bf16[3,64,512]{2,1,0:T(8,128)(2,1)S(1)} %pick_columns.8.refs_18_), channel_id=1, source_target_pairs={{0,3},{4,7},{9,10},{13,14},{18,17},{22,21},{27,24},{31,28}} | collective-permute-start | bytes 589832 | tf_op jit(solution)/shard_map/ppermute | solution.py:234
  58.1 1.3 %collective-permute-start.20 = (bf16[3,64,512]{2,1,0:T(8,128)(2,1)S(1)}, bf16[3,64,512]{2,1,0:T(8,128)(2,1)S(1)}, u32[]{:S(2)}, u32[]{:S(2)}) collective-permute-start(bf16[3,64,512]{2,1,0:T(8,128)(2,1)S(1)} %pick_columns.9.refs_19_), channel_id=1, source_target_pairs={{0,1},{4,5},{9,8},{13,12},{18,19},{22,23},{27,26},{31,30}} | collective-permute-start | bytes 589832 | tf_op jit(solution)/shard_map/ppermute | solution.py:234
  59.4 1.3 %collective-permute-start.28 = (bf16[3,64,512]{2,1,0:T(8,128)(2,1)S(1)}, bf16[3,64,512]{2,1,0:T(8,128)(2,1)S(1)}, u32[]{:S(2)}, u32[]{:S(2)}) collective-permute-start(bf16[3,64,512]{2,1,0:T(8,128)(2,1)S(1)} %pick_columns.9.refs_19_), channel_id=1, source_target_pairs={{0,2},{4,6},{9,11},{13,15},{18,16},{22,20},{27,25},{31,29}} | collective-permute-start | bytes 589832 | tf_op jit(solution)/shard_map/ppermute | solution.py:234
  60.8 2.0 %collective-permute-start.14 = (bf16[3,32,1024]{2,1,0:T(8,128)(2,1)S(1)}, bf16[3,32,1024]{2,1,0:T(8,128)(2,1)S(1)}, u32[]{:S(2)}, u32[]{:S(2)}) collective-permute-start(bf16[3,32,1024]{2,1,0:T(8,128)(2,1)S(1)} %collective-permute-done.12.second_ref.refs_11_), channel_id=1, source_target_pairs={{8,0},{16,8},{24,16},{28,24},{20,28},{12,20},{4,12},{0,4},{9,1},{1... | collective-permute-start | bytes 589832 | tf_op jit(solution)/shard_map/ppermute | solution.py:240
  63.6 1.3 %collective-permute-start.36 = (bf16[3,64,512]{2,1,0:T(8,128)(2,1)S(1)}, bf16[3,64,512]{2,1,0:T(8,128)(2,1)S(1)}, u32[]{:S(2)}, u32[]{:S(2)}) collective-permute-start(bf16[3,64,512]{2,1,0:T(8,128)(2,1)S(1)} %pick_columns.9.refs_19_), channel_id=1, source_target_pairs={{0,3},{4,7},{9,10},{13,14},{18,17},{22,21},{27,24},{31,28}} | collective-permute-start | bytes 589832 | tf_op jit(solution)/shard_map/ppermute | solution.py:234
  65.6 1.3 %collective-permute-start.21 = (bf16[3,64,512]{2,1,0:T(8,128)(2,1)}, bf16[3,64,512]{2,1,0:T(8,128)(2,1)S(1)}, u32[]{:S(2)}, u32[]{:S(2)}) collective-permute-start(bf16[3,64,512]{2,1,0:T(8,128)(2,1)} %pick_columns.10.refs_20_), channel_id=1, source_target_pairs={{0,1},{4,5},{9,8},{13,12},{18,19},{22,23},{27,26},{31,30}} | collective-permute-start | bytes 589832 | tf_op jit(solution)/shard_map/ppermute | solution.py:234
  66.9 1.4 %collective-permute-start.29 = (bf16[3,64,512]{2,1,0:T(8,128)(2,1)}, bf16[3,64,512]{2,1,0:T(8,128)(2,1)S(1)}, u32[]{:S(2)}, u32[]{:S(2)}) collective-permute-start(bf16[3,64,512]{2,1,0:T(8,128)(2,1)} %pick_columns.10.refs_20_), channel_id=1, source_target_pairs={{0,2},{4,6},{9,11},{13,15},{18,16},{22,20},{27,25},{31,29}} | collective-permute-start | bytes 589832 | tf_op jit(solution)/shard_map/ppermute | solution.py:234
  68.4 2.0 %collective-permute-start.16 = (bf16[3,32,1024]{2,1,0:T(8,128)(2,1)S(1)}, bf16[3,32,1024]{2,1,0:T(8,128)(2,1)S(1)}, u32[]{:S(2)}, u32[]{:S(2)}) collective-permute-start(bf16[3,32,1024]{2,1,0:T(8,128)(2,1)S(1)} %collective-permute-done.14.second_ref.refs_13_), channel_id=1, source_target_pairs={{8,0},{16,8},{24,16},{28,24},{20,28},{12,20},{4,12},{0,4},{9,1},{1... | collective-permute-start | bytes 589832 | tf_op jit(solution)/shard_map/ppermute | solution.py:240
  71.9 2.0 %collective-permute-start.37 = (bf16[3,64,512]{2,1,0:T(8,128)(2,1)}, bf16[3,64,512]{2,1,0:T(8,128)(2,1)}, u32[]{:S(2)}, u32[]{:S(2)}) collective-permute-start(bf16[3,64,512]{2,1,0:T(8,128)(2,1)} %pick_columns.10.refs_20_), channel_id=1, source_target_pairs={{0,3},{4,7},{9,10},{13,14},{18,17},{22,21},{27,24},{31,28}} | collective-permute-start | bytes 589832 | tf_op jit(solution)/shard_map/ppermute | solution.py:234
  74.5 2.0 %collective-permute-start.22 = (bf16[3,64,512]{2,1,0:T(8,128)(2,1)}, bf16[3,64,512]{2,1,0:T(8,128)(2,1)}, u32[]{:S(2)}, u32[]{:S(2)}) collective-permute-start(bf16[3,64,512]{2,1,0:T(8,128)(2,1)} %pick_columns.11.refs_21_), channel_id=1, source_target_pairs={{0,1},{4,5},{9,8},{13,12},{18,19},{22,23},{27,26},{31,30}} | collective-permute-start | bytes 589832 | tf_op jit(solution)/shard_map/ppermute | solution.py:234
  76.5 2.0 %collective-permute-start.30 = (bf16[3,64,512]{2,1,0:T(8,128)(2,1)}, bf16[3,64,512]{2,1,0:T(8,128)(2,1)}, u32[]{:S(2)}, u32[]{:S(2)}) collective-permute-start(bf16[3,64,512]{2,1,0:T(8,128)(2,1)} %pick_columns.11.refs_21_), channel_id=1, source_target_pairs={{0,2},{4,6},{9,11},{13,15},{18,16},{22,20},{27,25},{31,29}} | collective-permute-start | bytes 589832 | tf_op jit(solution)/shard_map/ppermute | solution.py:234
  79.2 2.0 %collective-permute-start.38 = (bf16[3,64,512]{2,1,0:T(8,128)(2,1)}, bf16[3,64,512]{2,1,0:T(8,128)(2,1)}, u32[]{:S(2)}, u32[]{:S(2)}) collective-permute-start(bf16[3,64,512]{2,1,0:T(8,128)(2,1)} %pick_columns.11.refs_21_), channel_id=1, source_target_pairs={{0,3},{4,7},{9,10},{13,14},{18,17},{22,21},{27,24},{31,28}} | collective-permute-start | bytes 589832 | tf_op jit(solution)/shard_map/ppermute | solution.py:234
  81.9 2.0 %collective-permute-start.23 = (bf16[3,64,512]{2,1,0:T(8,128)(2,1)}, bf16[3,64,512]{2,1,0:T(8,128)(2,1)}, u32[]{:S(2)}, u32[]{:S(2)}) collective-permute-start(bf16[3,64,512]{2,1,0:T(8,128)(2,1)} %pick_columns.12.refs_22_), channel_id=1, source_target_pairs={{0,1},{4,5},{9,8},{13,12},{18,19},{22,23},{27,26},{31,30}} | collective-permute-start | bytes 589832 | tf_op jit(solution)/shard_map/ppermute | solution.py:234
  83.8 0.9 copy-done.14
  84.8 0.9 copy-done.17
  85.7 1.3 %collective-permute-start.31 = (bf16[3,64,512]{2,1,0:T(8,128)(2,1)}, bf16[3,64,512]{2,1,0:T(8,128)(2,1)S(1)}, u32[]{:S(2)}, u32[]{:S(2)}) collective-permute-start(bf16[3,64,512]{2,1,0:T(8,128)(2,1)} %pick_columns.12.refs_22_), channel_id=1, source_target_pairs={{0,2},{4,6},{9,11},{13,15},{18,16},{22,20},{27,25},{31,29}} | collective-permute-start | bytes 589832 | tf_op jit(solution)/shard_map/ppermute | solution.py:234
  87.0 1.3 %collective-permute-start.39 = (bf16[3,64,512]{2,1,0:T(8,128)(2,1)}, bf16[3,64,512]{2,1,0:T(8,128)(2,1)S(1)}, u32[]{:S(2)}, u32[]{:S(2)}) collective-permute-start(bf16[3,64,512]{2,1,0:T(8,128)(2,1)} %pick_columns.12.refs_22_), channel_id=1, source_target_pairs={{0,3},{4,7},{9,10},{13,14},{18,17},{22,21},{27,24},{31,28}} | collective-permute-start | bytes 589832 | tf_op jit(solution)/shard_map/ppermute | solution.py:234
  88.4 1.3 %collective-permute-start.24 = (bf16[3,64,512]{2,1,0:T(8,128)(2,1)S(1)}, bf16[3,64,512]{2,1,0:T(8,128)(2,1)S(1)}, u32[]{:S(2)}, u32[]{:S(2)}) collective-permute-start(bf16[3,64,512]{2,1,0:T(8,128)(2,1)S(1)} %pick_columns.13.refs_23_), channel_id=1, source_target_pairs={{0,1},{4,5},{9,8},{13,12},{18,19},{22,23},{27,26},{31,30}} | collective-permute-start | bytes 589832 | tf_op jit(solution)/shard_map/ppermute | solution.py:234
  89.7 1.3 %collective-permute-start.32 = (bf16[3,64,512]{2,1,0:T(8,128)(2,1)S(1)}, bf16[3,64,512]{2,1,0:T(8,128)(2,1)S(1)}, u32[]{:S(2)}, u32[]{:S(2)}) collective-permute-start(bf16[3,64,512]{2,1,0:T(8,128)(2,1)S(1)} %pick_columns.13.refs_23_), channel_id=1, source_target_pairs={{0,2},{4,6},{9,11},{13,15},{18,16},{22,20},{27,25},{31,29}} | collective-permute-start | bytes 589832 | tf_op jit(solution)/shard_map/ppermute | solution.py:234
  91.0 1.3 %collective-permute-start.40 = (bf16[3,64,512]{2,1,0:T(8,128)(2,1)S(1)}, bf16[3,64,512]{2,1,0:T(8,128)(2,1)S(1)}, u32[]{:S(2)}, u32[]{:S(2)}) collective-permute-start(bf16[3,64,512]{2,1,0:T(8,128)(2,1)S(1)} %pick_columns.13.refs_23_), channel_id=1, source_target_pairs={{0,3},{4,7},{9,10},{13,14},{18,17},{22,21},{27,24},{31,28}} | collective-permute-start | bytes 589832 | tf_op jit(solution)/shard_map/ppermute | solution.py:234
  92.3 1.5 %add_add_fusion = f32[64,64]{1,0:T(8,128)} fusion(f32[64,64]{1,0:T(8,128)} %copy-done.52, f32[64,64]{1,0:T(8,128)} %copy-done.51, f32[64,64]{1,0:T(8,128)} %copy-done.50, f32[64,256]{1,0:T(8,128)} %copy-done.35, s32[]{:T(128)S(6)} %select_n.12), kind=kLoop, calls=%fused_computation.4 | loop fusion | flops 12288 | bytes 81924 | tf_op jit(solution)/shard_map/add | solution.py:154
  93.9 0.8 collective-permute-done.32.refs_39_
  94.6 2.1 %collective-permute-done.40.refs_47_ = bf16[3,64,512]{2,1,0:T(8,128)(2,1)S(1)} collective-permute-done((bf16[3,64,512]{2,1,0:T(8,128)(2,1)S(1)}, bf16[3,64,512]{2,1,0:T(8,128)(2,1)S(1)}, u32[]{:S(2)}, u32[]{:S(2)}) %collective-permute-start.40) | collective-permute-done | bytes 196640 | tf_op jit(solution)/shard_map/ppermute | solution.py:234
  97.4 0.9 copy-done.4
  98.3 0.9 copy-done.6
  99.2 0.9 copy-done.8
  100.2 0.9 copy-done.10
  101.1 0.9 copy-done.12
  102.0 0.9 copy-done.15
  103.0 0.9 copy-done.18
  103.9 0.9 copy-done.20
  104.8 0.9 copy-done.22
  105.7 0.9 copy-done.24
  106.7 0.9 copy-done.26
  107.6 0.9 copy-done.28
  108.5 0.9 copy-done.30
  109.4 0.9 copy-done.32
  110.4 12.7 %covariance_tile.1 = f32[3,3,1024,512]{3,2,1,0:T(8,128)} custom-call(s32[1]{0:T(128)} %bitcast.role_ref, bf16[3,32,1024]{2,1,0:T(8,128)(2,1)S(1)} %copy-done.20, bf16[3,32,1024]{2,1,0:T(8,128)(2,1)S(1)} %copy-done.22, bf16[3,32,1024]{2,1,0:T(8,128)(2,1)S(1)} %collective-permute-done.3.first_ref.refs_2_, ...), custom_call_target="tpu_custom_call" | custom-call | tf_op jit(solution)/shard_map/covariance_tile/pallas_call | solution.py:255
  (143 shorter events, 10.4 us)
Async XLA Ops:
  0.6 30.8 %copy-start = (bf16[3,1024,256]{2,1,0:T(8,128)(2,1)S(1)}, bf16[3,1024,256]{2,1,0:T(8,128)(2,1)}, u32[]{:S(2)}) copy-start(bf16[3,1024,256]{2,1,0:T(8,128)(2,1)} %param.5) | copy-start | bytes 4718596
  3.1 3.2 %collective-permute-start = (f32[64,128]{1,0:T(8,128)S(1)}, f32[64,128]{1,0:T(8,128)S(1)}, u32[]{:S(2)}, u32[]{:S(2)}) collective-permute-start(f32[64,128]{1,0:T(8,128)S(1)} %local_moments.1.refs_0_), channel_id=1, source_target_pairs={{0,1},{1,0},{2,3},{3,2},{4,5},{5,4},{6,7},{7,6},{8,9},{9,8},{10,11... | collective-permute-start | bytes 98312 | tf_op jit(solution)/shard_map/ppermute | solution.py:196
  3.6 4.5 %collective-permute-start.1 = (f32[64,128]{1,0:T(8,128)S(1)}, f32[64,128]{1,0:T(8,128)S(1)}, u32[]{:S(2)}, u32[]{:S(2)}) collective-permute-start(f32[64,128]{1,0:T(8,128)S(1)} %local_moments.1.refs_0_), channel_id=1, source_target_pairs={{0,2},{1,3},{2,0},{3,1},{4,6},{5,7},{6,4},{7,5},{8,10},{9,11},{10,... | collective-permute-start | bytes 98312 | tf_op jit(solution)/shard_map/ppermute | solution.py:196
  6.1 3.3 %collective-permute-start.2 = (f32[64,128]{1,0:T(8,128)S(1)}, f32[64,128]{1,0:T(8,128)S(1)}, u32[]{:S(2)}, u32[]{:S(2)}) collective-permute-start(f32[64,128]{1,0:T(8,128)S(1)} %local_moments.1.refs_0_), channel_id=1, source_target_pairs={{0,3},{1,2},{2,1},{3,0},{4,7},{5,6},{6,5},{7,4},{8,11},{9,10},{10,... | collective-permute-start | bytes 98312 | tf_op jit(solution)/shard_map/ppermute | solution.py:196
  16.3 20.8 %copy-start.19 = (bf16[3,32,1024]{2,1,0:T(8,128)(2,1)}, bf16[3,32,1024]{2,1,0:T(8,128)(2,1)S(1)}, u32[]{:S(2)}) copy-start(bf16[3,32,1024]{2,1,0:T(8,128)(2,1)S(1)} %get-tuple-element.5.refs_0_) | copy-start | bytes 589828
  16.3 29.3 %copy-start.21 = (bf16[3,32,1024]{2,1,0:T(8,128)(2,1)}, bf16[3,32,1024]{2,1,0:T(8,128)(2,1)S(1)}, u32[]{:S(2)}) copy-start(bf16[3,32,1024]{2,1,0:T(8,128)(2,1)S(1)} %get-tuple-element.6.refs_1_) | copy-start | bytes 589828
  16.3 7.0 %collective-permute-start.3 = (bf16[3,32,1024]{2,1,0:T(8,128)(2,1)S(1)}, bf16[3,32,1024]{2,1,0:T(8,128)(2,1)S(1)}, u32[]{:S(2)}, u32[]{:S(2)}) collective-permute-start(bf16[3,32,1024]{2,1,0:T(8,128)(2,1)S(1)} %get-tuple-element.5.refs_0_), channel_id=1, source_target_pairs={{0,8},{8,16},{16,24},{24,28},{28,20},{20,12},{12,4},{4,0},{1,9},{9... | collective-permute-start | bytes 589832 | tf_op jit(solution)/shard_map/ppermute | solution.py:239
  17.9 7.0 %collective-permute-start.4 = (bf16[3,32,1024]{2,1,0:T(8,128)(2,1)S(1)}, bf16[3,32,1024]{2,1,0:T(8,128)(2,1)S(1)}, u32[]{:S(2)}, u32[]{:S(2)}) collective-permute-start(bf16[3,32,1024]{2,1,0:T(8,128)(2,1)S(1)} %get-tuple-element.6.refs_1_), channel_id=1, source_target_pairs={{8,0},{16,8},{24,16},{28,24},{20,28},{12,20},{4,12},{0,4},{9,1},{1... | collective-permute-start | bytes 589832 | tf_op jit(solution)/shard_map/ppermute | solution.py:240
  23.3 6.1 %collective-permute-start.5 = (bf16[3,32,1024]{2,1,0:T(8,128)(2,1)S(1)}, bf16[3,32,1024]{2,1,0:T(8,128)(2,1)S(1)}, u32[]{:S(2)}, u32[]{:S(2)}) collective-permute-start(bf16[3,32,1024]{2,1,0:T(8,128)(2,1)S(1)} %collective-permute-done.3.first_ref.refs_2_), channel_id=1, source_target_pairs={{0,8},{8,16},{16,24},{24,28},{28,20},{20,12},{12,4},{4,0},{1,9},{9... | collective-permute-start | bytes 589832 | tf_op jit(solution)/shard_map/ppermute | solution.py:239
  24.8 6.1 %collective-permute-start.6 = (bf16[3,32,1024]{2,1,0:T(8,128)(2,1)S(1)}, bf16[3,32,1024]{2,1,0:T(8,128)(2,1)S(1)}, u32[]{:S(2)}, u32[]{:S(2)}) collective-permute-start(bf16[3,32,1024]{2,1,0:T(8,128)(2,1)S(1)} %collective-permute-done.4.second_ref.refs_3_), channel_id=1, source_target_pairs={{8,0},{16,8},{24,16},{28,24},{20,28},{12,20},{4,12},{0,4},{9,1},{1... | collective-permute-start | bytes 589832 | tf_op jit(solution)/shard_map/ppermute | solution.py:240
  25.3 17.7 %collective-permute-start.17 = (bf16[3,64,512]{2,1,0:T(8,128)(2,1)}, bf16[3,64,512]{2,1,0:T(8,128)(2,1)S(1)}, u32[]{:S(2)}, u32[]{:S(2)}) collective-permute-start(bf16[3,64,512]{2,1,0:T(8,128)(2,1)} %get-tuple-element.7.refs_16_), channel_id=1, source_target_pairs={{0,1},{4,5},{9,8},{13,12},{18,19},{22,23},{27,26},{31,30}} | collective-permute-start | bytes 589832 | tf_op jit(solution)/shard_map/ppermute | solution.py:234
  26.6 17.7 %collective-permute-start.25 = (bf16[3,64,512]{2,1,0:T(8,128)(2,1)}, bf16[3,64,512]{2,1,0:T(8,128)(2,1)S(1)}, u32[]{:S(2)}, u32[]{:S(2)}) collective-permute-start(bf16[3,64,512]{2,1,0:T(8,128)(2,1)} %get-tuple-element.7.refs_16_), channel_id=1, source_target_pairs={{0,2},{4,6},{9,11},{13,15},{18,16},{22,20},{27,25},{31,29}} | collective-permute-start | bytes 589832 | tf_op jit(solution)/shard_map/ppermute | solution.py:234
  29.4 16.2 %collective-permute-start.7 = (bf16[3,32,1024]{2,1,0:T(8,128)(2,1)S(1)}, bf16[3,32,1024]{2,1,0:T(8,128)(2,1)S(1)}, u32[]{:S(2)}, u32[]{:S(2)}) collective-permute-start(bf16[3,32,1024]{2,1,0:T(8,128)(2,1)S(1)} %collective-permute-done.5.first_ref.refs_4_), channel_id=1, source_target_pairs={{0,8},{8,16},{16,24},{24,28},{28,20},{20,12},{12,4},{4,0},{1,9},{9... | collective-permute-start | bytes 589832 | tf_op jit(solution)/shard_map/ppermute | solution.py:239
  31.0 14.7 %collective-permute-start.8 = (bf16[3,32,1024]{2,1,0:T(8,128)(2,1)S(1)}, bf16[3,32,1024]{2,1,0:T(8,128)(2,1)S(1)}, u32[]{:S(2)}, u32[]{:S(2)}) collective-permute-start(bf16[3,32,1024]{2,1,0:T(8,128)(2,1)S(1)} %collective-permute-done.6.second_ref.refs_5_), channel_id=1, source_target_pairs={{8,0},{16,8},{24,16},{28,24},{20,28},{12,20},{4,12},{0,4},{9,1},{1... | collective-permute-start | bytes 589832 | tf_op jit(solution)/shard_map/ppermute | solution.py:240
  31.8 5.3 %copy-start.35 = (f32[64,256]{1,0:T(8,128)}, f32[64,256]{1,0:T(8,128)S(1)}, u32[]{:S(2)}) copy-start(f32[64,256]{1,0:T(8,128)S(1)} %convolution_bitcast_fusion) | copy-start | bytes 196612
  31.9 1.3 %collective-permute-start.41 = (f32[64,64]{1,0:T(8,128)S(1)}, f32[64,64]{1,0:T(8,128)S(1)}, u32[]{:S(2)}, u32[]{:S(2)}) collective-permute-start(f32[64,64]{1,0:T(8,128)S(1)} %get-tuple-element.8), channel_id=1, source_target_pairs={{0,1},{1,0},{2,3},{3,2},{4,5},{5,4},{6,7},{7,6},{8,9},{9,8},{10,11... | collective-permute-start | bytes 49160 | tf_op jit(solution)/shard_map/ppermute | solution.py:154
  33.2 9.7 %copy-start.50 = (f32[64,64]{1,0:T(8,128)}, f32[64,64]{1,0:T(8,128)S(1)}, u32[]{:S(2)}) copy-start(f32[64,64]{1,0:T(8,128)S(1)} %collective-permute-done.41) | copy-start | bytes 49156
  33.2 3.9 %collective-permute-start.42 = (f32[64,64]{1,0:T(8,128)S(1)}, f32[64,64]{1,0:T(8,128)S(1)}, u32[]{:S(2)}, u32[]{:S(2)}) collective-permute-start(f32[64,64]{1,0:T(8,128)S(1)} %get-tuple-element.10), channel_id=1, source_target_pairs={{0,2},{1,3},{2,0},{3,1},{4,6},{5,7},{6,4},{7,5},{8,10},{9,11},{10,... | collective-permute-start | bytes 49160 | tf_op jit(solution)/shard_map/ppermute | solution.py:154
  37.1 5.8 %copy-start.51 = (f32[64,64]{1,0:T(8,128)}, f32[64,64]{1,0:T(8,128)S(1)}, u32[]{:S(2)}) copy-start(f32[64,64]{1,0:T(8,128)S(1)} %collective-permute-done.42) | copy-start | bytes 49156
  37.1 3.4 %collective-permute-start.43 = (f32[64,64]{1,0:T(8,128)S(1)}, f32[64,64]{1,0:T(8,128)S(1)}, u32[]{:S(2)}, u32[]{:S(2)}) collective-permute-start(f32[64,64]{1,0:T(8,128)S(1)} %get-tuple-element.9), channel_id=1, source_target_pairs={{0,3},{1,2},{2,1},{3,0},{4,7},{5,6},{6,5},{7,4},{8,11},{9,10},{10,... | collective-permute-start | bytes 49160 | tf_op jit(solution)/shard_map/ppermute | solution.py:154
  40.5 7.2 %collective-permute-start.33 = (bf16[3,64,512]{2,1,0:T(8,128)(2,1)}, bf16[3,64,512]{2,1,0:T(8,128)(2,1)S(1)}, u32[]{:S(2)}, u32[]{:S(2)}) collective-permute-start(bf16[3,64,512]{2,1,0:T(8,128)(2,1)} %get-tuple-element.7.refs_16_), channel_id=1, source_target_pairs={{0,3},{4,7},{9,10},{13,14},{18,17},{22,21},{27,24},{31,28}} | collective-permute-start | bytes 589832 | tf_op jit(solution)/shard_map/ppermute | solution.py:234
  43.0 10.3 %copy-start.23 = (bf16[3,64,512]{2,1,0:T(8,128)(2,1)}, bf16[3,64,512]{2,1,0:T(8,128)(2,1)S(1)}, u32[]{:S(2)}) copy-start(bf16[3,64,512]{2,1,0:T(8,128)(2,1)S(1)} %collective-permute-done.17.refs_24_) | copy-start | bytes 589828
  43.0 7.4 %collective-permute-start.18 = (bf16[3,64,512]{2,1,0:T(8,128)(2,1)S(1)}, bf16[3,64,512]{2,1,0:T(8,128)(2,1)S(1)}, u32[]{:S(2)}, u32[]{:S(2)}) collective-permute-start(bf16[3,64,512]{2,1,0:T(8,128)(2,1)S(1)} %pick_columns.7.refs_17_), channel_id=1, source_target_pairs={{0,1},{4,5},{9,8},{13,12},{18,19},{22,23},{27,26},{31,30}} | collective-permute-start | bytes 589832 | tf_op jit(solution)/shard_map/ppermute | solution.py:234
  44.3 7.4 %collective-permute-start.26 = (bf16[3,64,512]{2,1,0:T(8,128)(2,1)S(1)}, bf16[3,64,512]{2,1,0:T(8,128)(2,1)S(1)}, u32[]{:S(2)}, u32[]{:S(2)}) collective-permute-start(bf16[3,64,512]{2,1,0:T(8,128)(2,1)S(1)} %pick_columns.7.refs_17_), channel_id=1, source_target_pairs={{0,2},{4,6},{9,11},{13,15},{18,16},{22,20},{27,25},{31,29}} | collective-permute-start | bytes 589832 | tf_op jit(solution)/shard_map/ppermute | solution.py:234
  45.6 7.5 %collective-permute-start.9 = (bf16[3,32,1024]{2,1,0:T(8,128)(2,1)S(1)}, bf16[3,32,1024]{2,1,0:T(8,128)(2,1)S(1)}, u32[]{:S(2)}, u32[]{:S(2)}) collective-permute-start(bf16[3,32,1024]{2,1,0:T(8,128)(2,1)S(1)} %collective-permute-done.7.first_ref.refs_6_), channel_id=1, source_target_pairs={{0,8},{8,16},{16,24},{24,28},{28,20},{20,12},{12,4},{4,0},{1,9},{9... | collective-permute-start | bytes 589832 | tf_op jit(solution)/shard_map/ppermute | solution.py:239
  45.7 7.5 %collective-permute-start.10 = (bf16[3,32,1024]{2,1,0:T(8,128)(2,1)S(1)}, bf16[3,32,1024]{2,1,0:T(8,128)(2,1)S(1)}, u32[]{:S(2)}, u32[]{:S(2)}) collective-permute-start(bf16[3,32,1024]{2,1,0:T(8,128)(2,1)S(1)} %collective-permute-done.8.second_ref.refs_7_), channel_id=1, source_target_pairs={{8,0},{16,8},{24,16},{28,24},{20,28},{12,20},{4,12},{0,4},{9,1},{1... | collective-permute-start | bytes 589832 | tf_op jit(solution)/shard_map/ppermute | solution.py:240
  47.8 5.5 %copy-start.37 = (bf16[3,64,512]{2,1,0:T(8,128)(2,1)}, bf16[3,64,512]{2,1,0:T(8,128)(2,1)S(1)}, u32[]{:S(2)}) copy-start(bf16[3,64,512]{2,1,0:T(8,128)(2,1)S(1)} %collective-permute-done.33.refs_40_) | copy-start | bytes 589828
  47.8 7.6 %collective-permute-start.34 = (bf16[3,64,512]{2,1,0:T(8,128)(2,1)S(1)}, bf16[3,64,512]{2,1,0:T(8,128)(2,1)S(1)}, u32[]{:S(2)}, u32[]{:S(2)}) collective-permute-start(bf16[3,64,512]{2,1,0:T(8,128)(2,1)S(1)} %pick_columns.7.refs_17_), channel_id=1, source_target_pairs={{0,3},{4,7},{9,10},{13,14},{18,17},{22,21},{27,24},{31,28}} | collective-permute-start | bytes 589832 | tf_op jit(solution)/shard_map/ppermute | solution.py:234
  50.4 17.9 %copy-start.25 = (bf16[3,64,512]{2,1,0:T(8,128)(2,1)}, bf16[3,64,512]{2,1,0:T(8,128)(2,1)S(1)}, u32[]{:S(2)}) copy-start(bf16[3,64,512]{2,1,0:T(8,128)(2,1)S(1)} %collective-permute-done.18.refs_25_) | copy-start | bytes 589828
  50.4 7.0 %collective-permute-start.19 = (bf16[3,64,512]{2,1,0:T(8,128)(2,1)S(1)}, bf16[3,64,512]{2,1,0:T(8,128)(2,1)S(1)}, u32[]{:S(2)}, u32[]{:S(2)}) collective-permute-start(bf16[3,64,512]{2,1,0:T(8,128)(2,1)S(1)} %pick_columns.8.refs_18_), channel_id=1, source_target_pairs={{0,1},{4,5},{9,8},{13,12},{18,19},{22,23},{27,26},{31,30}} | collective-permute-start | bytes 589832 | tf_op jit(solution)/shard_map/ppermute | solution.py:234
  51.8 7.6 %collective-permute-start.27 = (bf16[3,64,512]{2,1,0:T(8,128)(2,1)S(1)}, bf16[3,64,512]{2,1,0:T(8,128)(2,1)S(1)}, u32[]{:S(2)}, u32[]{:S(2)}) collective-permute-start(bf16[3,64,512]{2,1,0:T(8,128)(2,1)S(1)} %pick_columns.8.refs_18_), channel_id=1, source_target_pairs={{0,2},{4,6},{9,11},{13,15},{18,16},{22,20},{27,25},{31,29}} | collective-permute-start | bytes 589832 | tf_op jit(solution)/shard_map/ppermute | solution.py:234
  53.2 7.5 %collective-permute-start.11 = (bf16[3,32,1024]{2,1,0:T(8,128)(2,1)S(1)}, bf16[3,32,1024]{2,1,0:T(8,128)(2,1)S(1)}, u32[]{:S(2)}, u32[]{:S(2)}) collective-permute-start(bf16[3,32,1024]{2,1,0:T(8,128)(2,1)S(1)} %collective-permute-done.9.first_ref.refs_8_), channel_id=1, source_target_pairs={{0,8},{8,16},{16,24},{24,28},{28,20},{20,12},{12,4},{4,0},{1,9},{9... | collective-permute-start | bytes 589832 | tf_op jit(solution)/shard_map/ppermute | solution.py:239
  53.3 7.5 %collective-permute-start.12 = (bf16[3,32,1024]{2,1,0:T(8,128)(2,1)S(1)}, bf16[3,32,1024]{2,1,0:T(8,128)(2,1)S(1)}, u32[]{:S(2)}, u32[]{:S(2)}) collective-permute-start(bf16[3,32,1024]{2,1,0:T(8,128)(2,1)S(1)} %collective-permute-done.10.second_ref.refs_9_), channel_id=1, source_target_pairs={{8,0},{16,8},{24,16},{28,24},{20,28},{12,20},{4,12},{0,4},{9,1},{1... | collective-permute-start | bytes 589832 | tf_op jit(solution)/shard_map/ppermute | solution.py:240
  55.4 15.8 %copy-start.7 = (bf16[3,64,512]{2,1,0:T(8,128)(2,1)}, bf16[3,64,512]{2,1,0:T(8,128)(2,1)S(1)}, u32[]{:S(2)}) copy-start(bf16[3,64,512]{2,1,0:T(8,128)(2,1)S(1)} %pick_columns.9.refs_19_) | copy-start | bytes 589828
  55.4 8.2 %collective-permute-start.35 = (bf16[3,64,512]{2,1,0:T(8,128)(2,1)S(1)}, bf16[3,64,512]{2,1,0:T(8,128)(2,1)S(1)}, u32[]{:S(2)}, u32[]{:S(2)}) collective-permute-start(bf16[3,64,512]{2,1,0:T(8,128)(2,1)S(1)} %pick_columns.8.refs_18_), channel_id=1, source_target_pairs={{0,3},{4,7},{9,10},{13,14},{18,17},{22,21},{27,24},{31,28}} | collective-permute-start | bytes 589832 | tf_op jit(solution)/shard_map/ppermute | solution.py:234
  58.1 6.8 %collective-permute-start.20 = (bf16[3,64,512]{2,1,0:T(8,128)(2,1)S(1)}, bf16[3,64,512]{2,1,0:T(8,128)(2,1)S(1)}, u32[]{:S(2)}, u32[]{:S(2)}) collective-permute-start(bf16[3,64,512]{2,1,0:T(8,128)(2,1)S(1)} %pick_columns.9.refs_19_), channel_id=1, source_target_pairs={{0,1},{4,5},{9,8},{13,12},{18,19},{22,23},{27,26},{31,30}} | collective-permute-start | bytes 589832 | tf_op jit(solution)/shard_map/ppermute | solution.py:234
  59.4 7.5 %collective-permute-start.28 = (bf16[3,64,512]{2,1,0:T(8,128)(2,1)S(1)}, bf16[3,64,512]{2,1,0:T(8,128)(2,1)S(1)}, u32[]{:S(2)}, u32[]{:S(2)}) collective-permute-start(bf16[3,64,512]{2,1,0:T(8,128)(2,1)S(1)} %pick_columns.9.refs_19_), channel_id=1, source_target_pairs={{0,2},{4,6},{9,11},{13,15},{18,16},{22,20},{27,25},{31,29}} | collective-permute-start | bytes 589832 | tf_op jit(solution)/shard_map/ppermute | solution.py:234
  60.7 9.7 %copy-start.3 = (bf16[3,32,1024]{2,1,0:T(8,128)(2,1)}, bf16[3,32,1024]{2,1,0:T(8,128)(2,1)S(1)}, u32[]{:S(2)}) copy-start(bf16[3,32,1024]{2,1,0:T(8,128)(2,1)S(1)} %collective-permute-done.11.first_ref.refs_10_) | copy-start | bytes 589828
  60.7 7.5 %collective-permute-start.13 = (bf16[3,32,1024]{2,1,0:T(8,128)(2,1)S(1)}, bf16[3,32,1024]{2,1,0:T(8,128)(2,1)S(1)}, u32[]{:S(2)}, u32[]{:S(2)}) collective-permute-start(bf16[3,32,1024]{2,1,0:T(8,128)(2,1)S(1)} %collective-permute-done.11.first_ref.refs_10_), channel_id=1, source_target_pairs={{0,8},{8,16},{16,24},{24,28},{28,20},{20,12},{12,4},{4,0},{1,9},{9... | collective-permute-start | bytes 589832 | tf_op jit(solution)/shard_map/ppermute | solution.py:239
  60.8 9.6 %copy-start.5 = (bf16[3,32,1024]{2,1,0:T(8,128)(2,1)}, bf16[3,32,1024]{2,1,0:T(8,128)(2,1)S(1)}, u32[]{:S(2)}) copy-start(bf16[3,32,1024]{2,1,0:T(8,128)(2,1)S(1)} %collective-permute-done.12.second_ref.refs_11_) | copy-start | bytes 589828
  60.8 7.5 %collective-permute-start.14 = (bf16[3,32,1024]{2,1,0:T(8,128)(2,1)S(1)}, bf16[3,32,1024]{2,1,0:T(8,128)(2,1)S(1)}, u32[]{:S(2)}, u32[]{:S(2)}) collective-permute-start(bf16[3,32,1024]{2,1,0:T(8,128)(2,1)S(1)} %collective-permute-done.12.second_ref.refs_11_), channel_id=1, source_target_pairs={{8,0},{16,8},{24,16},{28,24},{20,28},{12,20},{4,12},{0,4},{9,1},{1... | collective-permute-start | bytes 589832 | tf_op jit(solution)/shard_map/ppermute | solution.py:240
  63.6 4.8 %copy-start.41 = (bf16[3,64,512]{2,1,0:T(8,128)(2,1)}, bf16[3,64,512]{2,1,0:T(8,128)(2,1)S(1)}, u32[]{:S(2)}) copy-start(bf16[3,64,512]{2,1,0:T(8,128)(2,1)S(1)} %collective-permute-done.35.refs_42_) | copy-start | bytes 589828
  63.6 8.3 %collective-permute-start.36 = (bf16[3,64,512]{2,1,0:T(8,128)(2,1)S(1)}, bf16[3,64,512]{2,1,0:T(8,128)(2,1)S(1)}, u32[]{:S(2)}, u32[]{:S(2)}) collective-permute-start(bf16[3,64,512]{2,1,0:T(8,128)(2,1)S(1)} %pick_columns.9.refs_19_), channel_id=1, source_target_pairs={{0,3},{4,7},{9,10},{13,14},{18,17},{22,21},{27,24},{31,28}} | collective-permute-start | bytes 589832 | tf_op jit(solution)/shard_map/ppermute | solution.py:234
  65.6 8.3 %collective-permute-start.21 = (bf16[3,64,512]{2,1,0:T(8,128)(2,1)}, bf16[3,64,512]{2,1,0:T(8,128)(2,1)S(1)}, u32[]{:S(2)}, u32[]{:S(2)}) collective-permute-start(bf16[3,64,512]{2,1,0:T(8,128)(2,1)} %pick_columns.10.refs_20_), channel_id=1, source_target_pairs={{0,1},{4,5},{9,8},{13,12},{18,19},{22,23},{27,26},{31,30}} | collective-permute-start | bytes 589832 | tf_op jit(solution)/shard_map/ppermute | solution.py:234
  66.9 14.3 %copy-start.42 = (bf16[3,64,512]{2,1,0:T(8,128)(2,1)}, bf16[3,64,512]{2,1,0:T(8,128)(2,1)S(1)}, u32[]{:S(2)}) copy-start(bf16[3,64,512]{2,1,0:T(8,128)(2,1)S(1)} %collective-permute-done.28.refs_35_) | copy-start | bytes 589828
  66.9 9.6 %collective-permute-start.29 = (bf16[3,64,512]{2,1,0:T(8,128)(2,1)}, bf16[3,64,512]{2,1,0:T(8,128)(2,1)S(1)}, u32[]{:S(2)}, u32[]{:S(2)}) collective-permute-start(bf16[3,64,512]{2,1,0:T(8,128)(2,1)} %pick_columns.10.refs_20_), channel_id=1, source_target_pairs={{0,2},{4,6},{9,11},{13,15},{18,16},{22,20},{27,25},{31,29}} | collective-permute-start | bytes 589832 | tf_op jit(solution)/shard_map/ppermute | solution.py:234
  68.3 3.6 %copy-start.9 = (bf16[3,32,1024]{2,1,0:T(8,128)(2,1)}, bf16[3,32,1024]{2,1,0:T(8,128)(2,1)S(1)}, u32[]{:S(2)}) copy-start(bf16[3,32,1024]{2,1,0:T(8,128)(2,1)S(1)} %collective-permute-done.13.first_ref.refs_12_) | copy-start | bytes 589828
  68.3 10.1 %collective-permute-start.15 = (bf16[3,32,1024]{2,1,0:T(8,128)(2,1)S(1)}, bf16[3,32,1024]{2,1,0:T(8,128)(2,1)S(1)}, u32[]{:S(2)}, u32[]{:S(2)}) collective-permute-start(bf16[3,32,1024]{2,1,0:T(8,128)(2,1)S(1)} %collective-permute-done.13.first_ref.refs_12_), channel_id=1, source_target_pairs={{0,8},{8,16},{16,24},{24,28},{28,20},{20,12},{12,4},{4,0},{1,9},{9... | collective-permute-start | bytes 589832 | tf_op jit(solution)/shard_map/ppermute | solution.py:239
  68.4 10.1 %copy-start.11 = (bf16[3,32,1024]{2,1,0:T(8,128)(2,1)}, bf16[3,32,1024]{2,1,0:T(8,128)(2,1)S(1)}, u32[]{:S(2)}) copy-start(bf16[3,32,1024]{2,1,0:T(8,128)(2,1)S(1)} %collective-permute-done.14.second_ref.refs_13_) | copy-start | bytes 589828
  68.4 12.8 %collective-permute-start.16 = (bf16[3,32,1024]{2,1,0:T(8,128)(2,1)S(1)}, bf16[3,32,1024]{2,1,0:T(8,128)(2,1)S(1)}, u32[]{:S(2)}, u32[]{:S(2)}) collective-permute-start(bf16[3,32,1024]{2,1,0:T(8,128)(2,1)S(1)} %collective-permute-done.14.second_ref.refs_13_), channel_id=1, source_target_pairs={{8,0},{16,8},{24,16},{28,24},{20,28},{12,20},{4,12},{0,4},{9,1},{1... | collective-permute-start | bytes 589832 | tf_op jit(solution)/shard_map/ppermute | solution.py:240
  71.9 9.3 %copy-start.43 = (bf16[3,64,512]{2,1,0:T(8,128)(2,1)}, bf16[3,64,512]{2,1,0:T(8,128)(2,1)S(1)}, u32[]{:S(2)}) copy-start(bf16[3,64,512]{2,1,0:T(8,128)(2,1)S(1)} %collective-permute-done.36.refs_43_) | copy-start | bytes 589828
  71.9 13.8 %collective-permute-start.37 = (bf16[3,64,512]{2,1,0:T(8,128)(2,1)}, bf16[3,64,512]{2,1,0:T(8,128)(2,1)}, u32[]{:S(2)}, u32[]{:S(2)}) collective-permute-start(bf16[3,64,512]{2,1,0:T(8,128)(2,1)} %pick_columns.10.refs_20_), channel_id=1, source_target_pairs={{0,3},{4,7},{9,10},{13,14},{18,17},{22,21},{27,24},{31,28}} | collective-permute-start | bytes 589832 | tf_op jit(solution)/shard_map/ppermute | solution.py:234
  74.5 12.5 %collective-permute-start.22 = (bf16[3,64,512]{2,1,0:T(8,128)(2,1)}, bf16[3,64,512]{2,1,0:T(8,128)(2,1)}, u32[]{:S(2)}, u32[]{:S(2)}) collective-permute-start(bf16[3,64,512]{2,1,0:T(8,128)(2,1)} %pick_columns.11.refs_21_), channel_id=1, source_target_pairs={{0,1},{4,5},{9,8},{13,12},{18,19},{22,23},{27,26},{31,30}} | collective-permute-start | bytes 589832 | tf_op jit(solution)/shard_map/ppermute | solution.py:234
  76.5 4.7 %copy-start.44 = (bf16[3,64,512]{2,1,0:T(8,128)(2,1)}, bf16[3,64,512]{2,1,0:T(8,128)(2,1)S(1)}, u32[]{:S(2)}) copy-start(bf16[3,64,512]{2,1,0:T(8,128)(2,1)S(1)} %collective-permute-done.29.refs_36_) | copy-start | bytes 589828
  76.5 11.9 %collective-permute-start.30 = (bf16[3,64,512]{2,1,0:T(8,128)(2,1)}, bf16[3,64,512]{2,1,0:T(8,128)(2,1)}, u32[]{:S(2)}, u32[]{:S(2)}) collective-permute-start(bf16[3,64,512]{2,1,0:T(8,128)(2,1)} %pick_columns.11.refs_21_), channel_id=1, source_target_pairs={{0,2},{4,6},{9,11},{13,15},{18,16},{22,20},{27,25},{31,29}} | collective-permute-start | bytes 589832 | tf_op jit(solution)/shard_map/ppermute | solution.py:234
  79.2 10.5 %collective-permute-start.38 = (bf16[3,64,512]{2,1,0:T(8,128)(2,1)}, bf16[3,64,512]{2,1,0:T(8,128)(2,1)}, u32[]{:S(2)}, u32[]{:S(2)}) collective-permute-start(bf16[3,64,512]{2,1,0:T(8,128)(2,1)} %pick_columns.11.refs_21_), channel_id=1, source_target_pairs={{0,3},{4,7},{9,10},{13,14},{18,17},{22,21},{27,24},{31,28}} | collective-permute-start | bytes 589832 | tf_op jit(solution)/shard_map/ppermute | solution.py:234
  81.9 9.1 %collective-permute-start.23 = (bf16[3,64,512]{2,1,0:T(8,128)(2,1)}, bf16[3,64,512]{2,1,0:T(8,128)(2,1)}, u32[]{:S(2)}, u32[]{:S(2)}) collective-permute-start(bf16[3,64,512]{2,1,0:T(8,128)(2,1)} %pick_columns.12.refs_22_), channel_id=1, source_target_pairs={{0,1},{4,5},{9,8},{13,12},{18,19},{22,23},{27,26},{31,30}} | collective-permute-start | bytes 589832 | tf_op jit(solution)/shard_map/ppermute | solution.py:234
  85.7 8.1 %collective-permute-start.31 = (bf16[3,64,512]{2,1,0:T(8,128)(2,1)}, bf16[3,64,512]{2,1,0:T(8,128)(2,1)S(1)}, u32[]{:S(2)}, u32[]{:S(2)}) collective-permute-start(bf16[3,64,512]{2,1,0:T(8,128)(2,1)} %pick_columns.12.refs_22_), channel_id=1, source_target_pairs={{0,2},{4,6},{9,11},{13,15},{18,16},{22,20},{27,25},{31,29}} | collective-permute-start | bytes 589832 | tf_op jit(solution)/shard_map/ppermute | solution.py:234
  87.0 6.8 %collective-permute-start.39 = (bf16[3,64,512]{2,1,0:T(8,128)(2,1)}, bf16[3,64,512]{2,1,0:T(8,128)(2,1)S(1)}, u32[]{:S(2)}, u32[]{:S(2)}) collective-permute-start(bf16[3,64,512]{2,1,0:T(8,128)(2,1)} %pick_columns.12.refs_22_), channel_id=1, source_target_pairs={{0,3},{4,7},{9,10},{13,14},{18,17},{22,21},{27,24},{31,28}} | collective-permute-start | bytes 589832 | tf_op jit(solution)/shard_map/ppermute | solution.py:234
  88.4 5.5 %collective-permute-start.24 = (bf16[3,64,512]{2,1,0:T(8,128)(2,1)S(1)}, bf16[3,64,512]{2,1,0:T(8,128)(2,1)S(1)}, u32[]{:S(2)}, u32[]{:S(2)}) collective-permute-start(bf16[3,64,512]{2,1,0:T(8,128)(2,1)S(1)} %pick_columns.13.refs_23_), channel_id=1, source_target_pairs={{0,1},{4,5},{9,8},{13,12},{18,19},{22,23},{27,26},{31,30}} | collective-permute-start | bytes 589832 | tf_op jit(solution)/shard_map/ppermute | solution.py:234
  89.7 4.9 %collective-permute-start.32 = (bf16[3,64,512]{2,1,0:T(8,128)(2,1)S(1)}, bf16[3,64,512]{2,1,0:T(8,128)(2,1)S(1)}, u32[]{:S(2)}, u32[]{:S(2)}) collective-permute-start(bf16[3,64,512]{2,1,0:T(8,128)(2,1)S(1)} %pick_columns.13.refs_23_), channel_id=1, source_target_pairs={{0,2},{4,6},{9,11},{13,15},{18,16},{22,20},{27,25},{31,29}} | collective-permute-start | bytes 589832 | tf_op jit(solution)/shard_map/ppermute | solution.py:234
  91.0 5.7 %collective-permute-start.40 = (bf16[3,64,512]{2,1,0:T(8,128)(2,1)S(1)}, bf16[3,64,512]{2,1,0:T(8,128)(2,1)S(1)}, u32[]{:S(2)}, u32[]{:S(2)}) collective-permute-start(bf16[3,64,512]{2,1,0:T(8,128)(2,1)S(1)} %pick_columns.13.refs_23_), channel_id=1, source_target_pairs={{0,3},{4,7},{9,10},{13,14},{18,17},{22,21},{27,24},{31,28}} | collective-permute-start | bytes 589832 | tf_op jit(solution)/shard_map/ppermute | solution.py:234
  93.8 2.9 %copy-start.45 = (bf16[3,64,512]{2,1,0:T(8,128)(2,1)}, bf16[3,64,512]{2,1,0:T(8,128)(2,1)S(1)}, u32[]{:S(2)}) copy-start(bf16[3,64,512]{2,1,0:T(8,128)(2,1)S(1)} %collective-permute-done.31.refs_38_) | copy-start | bytes 589828
  93.8 2.9 %copy-start.46 = (bf16[3,64,512]{2,1,0:T(8,128)(2,1)}, bf16[3,64,512]{2,1,0:T(8,128)(2,1)S(1)}, u32[]{:S(2)}) copy-start(bf16[3,64,512]{2,1,0:T(8,128)(2,1)S(1)} %collective-permute-done.39.refs_46_) | copy-start | bytes 589828
  (33 other events, 36.5 us)

commit v2 on v1

v2 whole, which is shorter than its diff:
```python
import functools

import jax
import jax.numpy as jnp
from jax import lax
from jax.experimental import pallas as pl
from jax.experimental.pallas import tpu as pltpu
from jax.sharding import PartitionSpec as P

POLAR = 6
LANES = 128
STATS = 24
TILE = 256
VMEM = pl.BlockSpec(memory_space=pltpu.VMEM)
SMEM = pl.BlockSpec(memory_space=pltpu.SMEM)
ANY = pl.BlockSpec(memory_space=pl.ANY)
MIB = 1024 * 1024


def params(mib):
    return pltpu.CompilerParams(vmem_limit_bytes=mib * MIB)


def lane_mean(value):
    return jnp.sum(value, axis=1, keepdims=True) * (1.0 / value.shape[1])


def run_copies(copies):
    for copy in copies:
        copy.start()
    for copy in copies:
        copy.wait()


def stats_kernel(x_hbm, ref_hbm, out_ref, x_ref, ref_ref, sem):
    run_copies(
        [
            pltpu.make_async_copy(ref_hbm, ref_ref, sem.at[0]),
            pltpu.make_async_copy(x_hbm, x_ref, sem.at[1]),
        ]
    )
    values = []
    centred = []
    for i in range(3):
        x = x_ref[i]
        mean = lane_mean(x)
        values.append(mean)
        centred.append(x - mean)
    values.append(sum(jnp.sum(c * c, axis=1, keepdims=True) for c in centred))
    ref_mean = [lane_mean(ref_ref[j : j + 1, :]) for j in range(3)]
    ref_centred = [ref_ref[j : j + 1, :] - ref_mean[j] for j in range(3)]
    for i in range(3):
        for j in range(3):
            values.append(jnp.sum(centred[i] * ref_centred[j], axis=1, keepdims=True))
    values += ref_mean
    values.append(sum(jnp.sum(c * c, axis=1, keepdims=True) for c in ref_centred))
    shape = (x_ref.shape[1], LANES)
    lane = lax.broadcasted_iota(jnp.int32, shape, 1)
    out = jnp.zeros(shape, jnp.float32)
    for k, value in enumerate(values):
        out = jnp.where(lane == k, jnp.broadcast_to(value, shape), out)
    out_ref[...] = out.T[:STATS]


def align_kernel(parts, atoms, *refs):
    stats = refs[:parts]
    x_hbm, ref_hbm, first_ref, second_ref, x_ref, ref_ref, turn, sem = refs[parts:]
    copies = [
        pltpu.make_async_copy(ref_hbm, ref_ref, sem.at[0]),
        pltpu.make_async_copy(x_hbm, x_ref, sem.at[1]),
    ]
    for copy in copies:
        copy.start()
    local = x_ref.shape[2]
    rows = x_ref.shape[1]

    def row(at):
        return [s[at : at + 1, :] for s in stats]

    means = [row(i) for i in range(3)]
    ref_means = [row(13 + j) for j in range(3)]
    centre = [sum(m) * (1.0 / parts) for m in means]
    ref_centre = [sum(r) * (1.0 / parts) for r in ref_means]
    off = [[m - centre[i] for m in means[i]] for i in range(3)]
    ref_off = [[r - ref_centre[j] for r in ref_means[j]] for j in range(3)]
    spread = sum(row(3)) + local * sum(o * o for i in range(3) for o in off[i])
    ref_spread = sum(row(16)) + local * sum(o * o for j in range(3) for o in ref_off[j])
    scale = 1.0 / jnp.sqrt(spread * ref_spread + 1e-06)
    now = [
        [
            (sum(row(4 + 3 * i + j)) + local * sum(o * r for o, r in zip(off[i], ref_off[j])))
            * scale
            for j in range(3)
        ]
        for i in range(3)
    ]
    for _ in range(POLAR):
        gram = {}
        for i in range(3):
            for j in range(i, 3):
                gram[i, j] = sum(now[k][i] * now[k][j] for k in range(3))
                gram[j, i] = gram[i, j]
        left = [
            [(1.5 if k == j else 0.0) - 0.5 * gram[k, j] for j in range(3)] for k in range(3)
        ]
        now = [
            [sum(now[i][k] * left[k][j] for k in range(3)) for j in range(3)]
            for i in range(3)
        ]
    for k, value in enumerate(sum(now, []) + centre + ref_centre):
        turn[k : k + 1, :rows] = value
    turned = turn[...].T
    column = [turned[:rows, k : k + 1] for k in range(12)]
    for copy in copies:
        copy.wait()
    centred = [x_ref[j] - column[9 + j] for j in range(3)]
    for i in range(3):
        target = ref_ref[i : i + 1, :] - turned[0:1, 12 + i : 13 + i]
        moved = sum(column[3 * j + i] * centred[j] for j in range(3)) - target
        moved = moved.astype(jnp.bfloat16)
        first_ref[i] = moved[: rows // 2]
        second_ref[i] = moved[rows // 2 :]


def cut_kernel(pieces, half_ref, *refs):
    sources, cols_ref, sem = refs[:pieces], refs[pieces], refs[pieces + 1]
    block = cols_ref.shape[2]
    rows = sources[0].shape[1]
    start = pl.multiple_of(half_ref[0] * block, LANES)
    run_copies(
        [
            pltpu.make_async_copy(
                source.at[:, :, pl.ds(start, block)],
                cols_ref.at[:, pl.ds(k * rows, rows), :],
                sem.at[k],
            )
            for k, source in enumerate(sources)
        ]
    )


def fetch(role_ref, rows_in, groups, rows, cols, sem):
    height = rows_in[0].shape[1]
    copies = [
        pltpu.make_async_copy(piece, rows.at[:, pl.ds(k * height, height), :], sem.at[k])
        for k, piece in enumerate(rows_in)
    ]
    for copy in copies:
        copy.start()
    used = len(rows_in)
    for role in range(len(groups[0][0])):

        @pl.when(role_ref[0] == role)
        def _(role=role):
            run_copies(
                [
                    pltpu.make_async_copy(
                        arrays[role].at[:, pl.ds(at, count), :],
                        cols.at[:, pl.ds(to, count), :],
                        sem.at[used + k],
                    )
                    for k, (arrays, at, count, to) in enumerate(groups)
                ]
            )

    for copy in copies:
        copy.wait()


def unpack(refs, pieces, roles, spans):
    role_ref, rows_in = refs[0], refs[1 : 1 + pieces]
    at = 1 + pieces
    groups = []
    for span in spans:
        groups.append((refs[at : at + roles],) + span)
        at += roles
    return role_ref, rows_in, groups, refs[at:]


def product(rows, cols, c, start, d):
    left = rows[c, :, pl.ds(start, TILE)]
    return lax.dot_general(
        left, cols[d], (((0,), (0,)), ((), ())), preferred_element_type=jnp.float32
    )


def first_kernel(pieces, roles, spans, *refs):
    role_ref, rows_in, groups, (acc, rows, cols, sem) = unpack(refs, pieces, roles, spans)
    fetch(role_ref, rows_in, groups, rows, cols, sem)
    tiles = acc.shape[2] // TILE

    @pl.loop(0, 3 * tiles)
    def _(i):
        c = lax.div(i, tiles)
        start = pl.multiple_of(lax.rem(i, tiles) * TILE, TILE)
        for d in range(3):
            acc[c, d, pl.ds(start, TILE), :] = product(rows, cols, c, start, d)


def second_kernel(pieces, roles, spans, scale, *refs):
    role_ref, rows_in, groups, rest = unpack(refs, pieces, roles, spans)
    acc, out_ref, rows, cols, done, sem, out_sem = rest
    fetch(role_ref, rows_in, groups, rows, cols, sem)
    tiles = acc.shape[2] // TILE

    def write(i):
        c = lax.div(i, tiles)
        start = pl.multiple_of(lax.rem(i, tiles) * TILE, TILE)
        slot = lax.rem(i, 2)
        return pltpu.make_async_copy(
            done.at[slot], out_ref.at[c, :, pl.ds(start, TILE), :], out_sem.at[slot]
        )

    @pl.loop(0, 3 * tiles)
    def _(i):
        c = lax.div(i, tiles)
        start = pl.multiple_of(lax.rem(i, tiles) * TILE, TILE)
        slot = lax.rem(i, 2)

        @pl.when(i >= 2)
        def _():
            write(i - 2).wait()

        for d in range(3):
            done[slot, d] = scale * (
                acc[c, d, pl.ds(start, TILE), :] + product(rows, cols, c, start, d)
            )
        write(i).start()

    write(3 * tiles - 2).wait()
    write(3 * tiles - 1).wait()


def ring_order(count):
    return list(range(0, count, 2)) + list(range(1, count, 2))[::-1]


def long_axis_covariance(first, second, half, role, block, spread_pairs, scale):
    flat = jnp.concatenate([first, second], axis=1)
    rows = lax.all_gather(flat, "frames", axis=1, tiled=True)
    cut = lax.dynamic_slice_in_dim(rows, half * block, block, axis=2)
    cols = jnp.where(role == 0, cut, jnp.zeros_like(cut))
    for d, pairs in enumerate(spread_pairs):
        sent = lax.ppermute(cut, ("frames", "atoms"), pairs)
        cols = jnp.where(role == d + 1, sent, cols)
    return scale * jnp.einsum(
        "cfp,dfq->cpdq", rows, cols, preferred_element_type=jnp.float32
    )


def per_device(frames, mean_structure, eigvecs):
    local_frames, _, local_atoms = frames.shape
    frame_axis = lax.axis_size("frames")
    atom_axis = lax.axis_size("atoms")
    total_frames = local_frames * frame_axis
    block = local_atoms * atom_axis // frame_axis
    blocks = frame_axis // atom_axis
    me_f = lax.axis_index("frames")
    me_a = lax.axis_index("atoms")
    half = lax.rem(me_f, blocks).astype(jnp.int32).reshape(1)
    owner = lax.div(me_f, blocks)
    role = lax.bitwise_xor(me_a, owner).astype(jnp.int32).reshape(1)
    x = jnp.transpose(frames, (1, 0, 2))
    x_copy = [
        pltpu.VMEM(x.shape, jnp.float32),
        pltpu.VMEM(mean_structure.shape, jnp.float32),
    ]

    stats = pl.pallas_call(
        stats_kernel,
        out_shape=jax.ShapeDtypeStruct((STATS, local_frames), jnp.float32),
        in_specs=[ANY, ANY],
        out_specs=VMEM,
        scratch_shapes=x_copy + [pltpu.SemaphoreType.DMA((2,))],
        compiler_params=params(8),
        name="local_moments",
    )(x, mean_structure)
    others = [
        lax.ppermute(stats, "atoms", [(a, a ^ d) for a in range(atom_axis)])
        for d in range(1, atom_axis)
    ]
    height = local_frames // 2
    piece = jax.ShapeDtypeStruct((3, height, local_atoms), jnp.bfloat16)
    first, second = pl.pallas_call(
        functools.partial(align_kernel, atom_axis, local_atoms * atom_axis),
        out_shape=(piece, piece),
        in_specs=[VMEM] * atom_axis + [ANY, ANY],
        out_specs=(VMEM, VMEM),
        scratch_shapes=x_copy
        + [pltpu.VMEM((LANES, LANES), jnp.float32), pltpu.SemaphoreType.DMA((2,))],
        compiler_params=params(8),
        name="polar_align",
    )(stats, *others, x, mean_structure)

    proj = jnp.einsum(
        "cfa,cak->fk",
        jnp.concatenate([first, second], axis=1),
        eigvecs,
        preferred_element_type=jnp.float32,
    )
    projections = lax.psum_scatter(proj, "atoms", scatter_dimension=1, tiled=True)

    def pairs(source, target):
        return [
            (
                f * atom_axis + ((f // blocks) ^ source),
                f * atom_axis + ((f // blocks) ^ target),
            )
            for f in range(frame_axis)
        ]

    if block % LANES or frame_axis != 8 or atom_axis != 4:
        spread_pairs = [pairs(0, d) for d in range(1, atom_axis)]
        covariance = long_axis_covariance(
            first, second, half[0], role[0], block, spread_pairs, 1.0 / total_frames
        )
        return covariance, projections

    def spread(pieces):
        frames_in = len(pieces) * height
        cut = pl.pallas_call(
            functools.partial(cut_kernel, len(pieces)),
            out_shape=jax.ShapeDtypeStruct((3, frames_in, block), jnp.bfloat16),
            in_specs=[SMEM] + [ANY] * len(pieces),
            out_specs=ANY,
            scratch_shapes=[pltpu.SemaphoreType.DMA((len(pieces),))],
            compiler_params=params(8),
            name="cut_columns",
        )(half, *pieces)
        axes = ("frames", "atoms")
        across = lax.ppermute(cut, axes, pairs(0, 2))
        beside = lax.ppermute(cut, axes, pairs(0, 1))
        last = lax.ppermute(across, axes, pairs(2, 3))
        return [cut, beside, across, last]

    order = ring_order(frame_axis)
    forward = [(order[i], order[(i + 1) % frame_axis]) for i in range(frame_axis)]
    backward = [(b, a) for a, b in forward]

    def hop(arrays, way):
        return [lax.ppermute(a, "frames", way) for a in arrays]

    own = [first, second]
    up, down = own, own
    ups, downs = [], []
    for _ in range(1, frame_axis // 2):
        up, down = hop(up, forward), hop(down, backward)
        ups.append(up)
        downs.append(down)
    far = hop(up[:1], forward) + hop(down[1:], backward)
    lots = [own + ups[0] + downs[0], ups[1] + downs[1], ups[2] + downs[2], far]
    cuts = [spread(lot) for lot in lots]

    early = lots[0] + ups[1]
    late = downs[1] + lots[2] + far
    early_spans = [(0, 6 * height, 0), (0, 2 * height, 6 * height)]
    early_cuts = cuts[0] + cuts[1]
    late_spans = [
        (2 * height, 2 * height, 0),
        (0, 4 * height, 2 * height),
        (0, 2 * height, 6 * height),
    ]
    late_cuts = cuts[1] + cuts[2] + cuts[3]
    depth = 8 * height
    operand_scratch = [
        pltpu.VMEM((3, depth, local_atoms), jnp.bfloat16),
        pltpu.VMEM((3, depth, block), jnp.bfloat16),
    ]
    shape = (3, 3, local_atoms, block)
    flops = 2 * 9 * local_atoms * block * depth
    acc = pl.pallas_call(
        functools.partial(first_kernel, len(early), atom_axis, early_spans),
        out_shape=pltpu.VMEM(shape, jnp.float32),
        in_specs=[SMEM] + [ANY] * (len(early) + len(early_cuts)),
        out_specs=VMEM,
        scratch_shapes=operand_scratch + [pltpu.SemaphoreType.DMA((len(early) + 2,))],
        compiler_params=params(40),
        cost_estimate=pl.CostEstimate(flops=flops, bytes_accessed=4 * MIB, transcendentals=0),
        name="covariance_first",
    )(role, *early, *early_cuts)
    covariance = pl.pallas_call(
        functools.partial(
            second_kernel, len(late), atom_axis, late_spans, 1.0 / total_frames
        ),
        out_shape=jax.ShapeDtypeStruct(shape, jnp.float32),
        in_specs=[SMEM] + [ANY] * (len(late) + len(late_cuts)) + [VMEM],
        out_specs=ANY,
        scratch_shapes=operand_scratch
        + [
            pltpu.VMEM((2, 3, TILE, block), jnp.float32),
            pltpu.SemaphoreType.DMA((len(late) + 3,)),
            pltpu.SemaphoreType.DMA((2,)),
        ],
        compiler_params=params(40),
        cost_estimate=pl.CostEstimate(flops=flops, bytes_accessed=20 * MIB, transcendentals=0),
        name="covariance_second",
    )(role, *late, *late_cuts, acc)
    return jnp.transpose(covariance, (0, 2, 1, 3)), projections


def solution(mesh):
    placed = (P("frames", None, "atoms"), P(None, "atoms"), P(None, "atoms", None))
    return jax.shard_map(
        per_device,
        mesh=mesh,
        in_specs=placed,
        out_specs=(P(None, "atoms", None, "frames"), P("frames", "atoms")),
        check_vma=False,
    )
```

time: 124 us -> 129 us (1.040)
  starting transfers between devices: 57.1 us -> 41.6 us
  waiting for transfers between devices: 19.6 us -> 33.2 us
  between operations: 1.39 us -> 14.5 us
  local copies, waits for them, and re-layouts: 22.9 us -> 9.98 us
  Pallas kernels: 20.3 us -> 28.1 us
  other arithmetic: 1.51 us -> 0 us
    unnamed x0 -> x2, waiting for transfers between devices: none -> 18.7 us
    ppermute x41 -> x26, starting transfers between devices: 53.9 us -> 38.4 us  [the longest x14 14.4 us: hop(): return [lax.ppermute(a, 'frames', way) for a in arrays]]
    unnamed x106 -> x57, local copies, waits for them, and re-layouts: 22.8 us -> 9.98 us
    pallas_call x9 -> x7, Pallas kernels: 15.3 us -> 27.5 us  [the longest x1 18.1 us: per_device(): pl.pallas_call(functools.partial(second_kernel, len(late), atom_axis, lat...]
    ppermute x41 -> x26, waiting for transfers between devices: 16.3 us -> 11.4 us  [the longest x14 11.4 us: hop(): return [lax.ppermute(a, 'frames', way) for a in arrays]]
    pallas_call x1, Pallas kernels: 4.95 us -> 0.58 us  [per_device(): pl.pallas_call(functools.partial(align_kernel, atom_axis, local_atoms * a...]
    add x1 -> x0, other arithmetic: 1.51 us -> none  [project(): total + lax.ppermute(share, 'atoms', [(a, a ^ d) for a in range(atom_axis)])]
  transfers between devices with their start and end apart: 44 -> 30, of which waited for: 9 -> 7; matrix products, arithmetic and copies ran while one was open for 2% -> 2% of each run, Pallas kernels for 2% -> 7%
where the time goes in v2:
time: 129 us
  starting transfers between devices  41.6 us (32%)
  waiting for transfers between devices  33.2 us (26%)
  Pallas kernels  28.1 us (22%)
  between operations  14.5 us (11%)
  local copies, waits for them, and re-layouts  9.98 us (8%)
  matrix products  1.37 us (1%)
    unnamed x2, waiting for transfers between devices  18.7 us
    pallas_call x1, Pallas kernels, per_device(): pl.pallas_call(functools.partial(second_kernel, len(late), atom_axis, lat...  18.1 us
    ppermute x14, starting transfers between devices, hop(): return [lax.ppermute(a, 'frames', way) for a in arrays]  14.4 us
    ppermute x4, starting transfers between devices, spread(): across = lax.ppermute(cut, axes, pairs(0, 2))  13.1 us
    ppermute x14, waiting for transfers between devices, hop(): return [lax.ppermute(a, 'frames', way) for a in arrays]  11.4 us
    unnamed x57, local copies, waits for them, and re-layouts  9.98 us
    pallas_call x1, Pallas kernels, per_device(): pl.pallas_call(functools.partial(first_kernel, len(early), atom_axis, ear...  6.9 us
    ppermute x4, starting transfers between devices, spread(): beside = lax.ppermute(cut, axes, pairs(0, 1))  5.95 us
  transfers between devices with their start and end apart: 30, of which 7 were waited for; matrix products, arithmetic and copies ran while one was open for 2% of the time, Pallas kernels for 7%

profile of v2, /device:TPU:0, one launch (start us, length us, event | category | flops | bytes accessed | tf_op | source)
XLA Modules:
  0.0 128.7 jit_solution(13523952207401331177)
XLA Ops:
  7.2 0.0 copy-start
  7.2 0.0 reduce-scatter.4.cloned.1.call-start
  7.2 1.2 copy-done.4
  8.5 0.7 copy-done.26
  9.2 0.6 local_moments.1.refs_0_
  9.8 2.4 %collective-permute-start.2 = (f32[24,64]{1,0:T(8,128)S(1)}, f32[24,64]{1,0:T(8,128)S(1)}, u32[]{:S(2)}, u32[]{:S(2)}) collective-permute-start(f32[24,64]{1,0:T(8,128)S(1)} %local_moments.1.refs_0_), channel_id=1, source_target_pairs={{0,3},{1,2},{2,1},{3,0},{4,7},{5,6},{6,5},{7,4},{8,11},{9,10},{10,... | collective-permute-start | bytes 18440 | tf_op jit(solution)/shard_map/ppermute | solution.py:279
  12.2 0.6 collective-permute-start.1
  12.8 0.0 collective-permute-start
  12.9 0.7 collective-permute-done.2.refs_3_
  13.6 2.3 %collective-permute-done.1.refs_2_ = f32[24,64]{1,0:T(8,128)S(1)} collective-permute-done((f32[24,64]{1,0:T(8,128)S(1)}, f32[24,64]{1,0:T(8,128)S(1)}, u32[]{:S(2)}, u32[]{:S(2)}) %collective-permute-start.1) | collective-permute-done | bytes 6176 | tf_op jit(solution)/shard_map/ppermute | solution.py:279
  15.9 0.0 collective-permute-done.refs_1_
  15.9 0.6 polar_align.1
  16.5 1.6 %collective-permute-start.7 = (bf16[3,32,1024]{2,1,0:T(8,128)(2,1)S(1)}, bf16[3,32,1024]{2,1,0:T(8,128)(2,1)S(1)}, u32[]{:S(2)}, u32[]{:S(2)}) collective-permute-start(bf16[3,32,1024]{2,1,0:T(8,128)(2,1)S(1)} %get-tuple-element.4.refs_0_.refs_1_), channel_id=1, source_target_pairs={{0,8},{8,16},{16,24},{24,28},{28,20},{20,12},{12,4},{4,0},{1,9},{9... | collective-permute-start | bytes 589832 | tf_op jit(solution)/shard_map/ppermute | solution.py:341
  18.1 0.4 collective-permute-start.3
  18.6 1.5 %collective-permute-start.5 = (bf16[3,32,1024]{2,1,0:T(8,128)(2,1)S(1)}, bf16[3,32,1024]{2,1,0:T(8,128)(2,1)S(1)}, u32[]{:S(2)}, u32[]{:S(2)}) collective-permute-start(bf16[3,32,1024]{2,1,0:T(8,128)(2,1)S(1)} %get-tuple-element.5.refs_1_.refs_2_), channel_id=1, source_target_pairs={{8,0},{16,8},{24,16},{28,24},{20,28},{12,20},{4,12},{0,4},{9,1},{1... | collective-permute-start | bytes 589832 | tf_op jit(solution)/shard_map/ppermute | solution.py:341
  20.1 0.5 collective-permute-start.10
  20.6 3.7 %collective-permute-done.7.refs_2_.refs_3_ = bf16[3,32,1024]{2,1,0:T(8,128)(2,1)S(1)} collective-permute-done((bf16[3,32,1024]{2,1,0:T(8,128)(2,1)S(1)}, bf16[3,32,1024]{2,1,0:T(8,128)(2,1)S(1)}, u32[]{:S(2)}, u32[]{:S(2)}) %collective-permute-start.7) | collective-permute-done | bytes 196640 | tf_op jit(solution)/shard_map/ppermute | solution.py:341
  24.4 1.6 %collective-permute-start.8 = (bf16[3,32,1024]{2,1,0:T(8,128)(2,1)S(1)}, bf16[3,32,1024]{2,1,0:T(8,128)(2,1)}, u32[]{:S(2)}, u32[]{:S(2)}) collective-permute-start(bf16[3,32,1024]{2,1,0:T(8,128)(2,1)S(1)} %collective-permute-done.7.refs_2_.refs_3_), channel_id=1, source_target_pairs={{0,8},{8,16},{16,24},{24,28},{28,20},{20,12},{12,4},{4,0},{1,9},{9... | collective-permute-start | bytes 589832 | tf_op jit(solution)/shard_map/ppermute | solution.py:341
  26.0 0.0 collective-permute-done.3.refs_4_.refs_5_
  26.0 0.4 collective-permute-start.4
  26.4 3.8 %collective-permute-done.5.refs_5_.refs_6_ = bf16[3,32,1024]{2,1,0:T(8,128)(2,1)S(1)} collective-permute-done((bf16[3,32,1024]{2,1,0:T(8,128)(2,1)S(1)}, bf16[3,32,1024]{2,1,0:T(8,128)(2,1)S(1)}, u32[]{:S(2)}, u32[]{:S(2)}) %collective-permute-start.5) | collective-permute-done | bytes 196640 | tf_op jit(solution)/shard_map/ppermute | solution.py:341
  30.2 0.4 collective-permute-start.6
  30.6 0.0 collective-permute-done.10.refs_3_.refs_4_
  30.6 1.6 %collective-permute-start.11 = (bf16[3,32,1024]{2,1,0:T(8,128)(2,1)S(1)}, bf16[3,32,1024]{2,1,0:T(8,128)(2,1)}, u32[]{:S(2)}, u32[]{:S(2)}) collective-permute-start(bf16[3,32,1024]{2,1,0:T(8,128)(2,1)S(1)} %collective-permute-done.10.refs_3_.refs_4_), channel_id=1, source_target_pairs={{0,8},{8,16},{16,24},{24,28},{28,20},{20,12},{12,4},{4,0},{1,9},{9... | collective-permute-start | bytes 589832 | tf_op jit(solution)/shard_map/ppermute | solution.py:341
  32.2 0.1 cut_columns.7.refs_9_
  32.4 0.0 copy-start.5
  32.4 3.4 %collective-permute-start.27 = (bf16[3,192,512]{2,1,0:T(8,128)(2,1)S(1)}, bf16[3,192,512]{2,1,0:T(8,128)(2,1)}, u32[]{:S(2)}, u32[]{:S(2)}) collective-permute-start(bf16[3,192,512]{2,1,0:T(8,128)(2,1)S(1)} %cut_columns.7.refs_9_), channel_id=1, source_target_pairs={{0,2},{4,6},{9,11},{13,15},{18,16},{22,20},{27,25},{31,29}} | collective-permute-start | bytes 1769480 | tf_op jit(solution)/shard_map/ppermute | solution.py:331
  35.8 0.0 collective-permute-done.8.refs_0_.refs_7_
  35.8 0.0 collective-permute-start.9
  35.8 0.0 collective-permute-done.4.refs_2_.refs_1_
  35.8 2.0 %collective-permute-start.13 = (bf16[3,32,1024]{2,1,0:T(8,128)(2,1)S(1)}, bf16[3,32,1024]{2,1,0:T(8,128)(2,1)S(1)}, u32[]{:S(2)}, u32[]{:S(2)}) collective-permute-start(bf16[3,32,1024]{2,1,0:T(8,128)(2,1)S(1)} %collective-permute-done.4.refs_2_.refs_1_), channel_id=1, source_target_pairs={{8,0},{16,8},{24,16},{28,24},{20,28},{12,20},{4,12},{0,4},{9,1},{1... | collective-permute-start | bytes 589832 | tf_op jit(solution)/shard_map/ppermute | solution.py:341
  37.8 0.4 collective-permute-done.6.refs_3_.refs_2_
  38.2 0.6 collective-permute-start.14
  38.8 1.5 %collective-permute-start.12 = (bf16[3,32,1024]{2,1,0:T(8,128)(2,1)}, bf16[3,32,1024]{2,1,0:T(8,128)(2,1)S(1)}, u32[]{:S(2)}, u32[]{:S(2)}) collective-permute-start(bf16[3,32,1024]{2,1,0:T(8,128)(2,1)} %collective-permute-done.11.refs_1_.refs_8_), channel_id=1, source_target_pairs={{0,8},{8,16},{16,24},{24,28},{28,20},{20,12},{12,4},{4,0},{1,9},{9... | collective-permute-start | bytes 589832 | tf_op jit(solution)/shard_map/ppermute | solution.py:341
  40.3 3.5 %collective-permute-done.9.refs_0_.refs_3_ = bf16[3,32,1024]{2,1,0:T(8,128)(2,1)S(1)} collective-permute-done((bf16[3,32,1024]{2,1,0:T(8,128)(2,1)}, bf16[3,32,1024]{2,1,0:T(8,128)(2,1)S(1)}, u32[]{:S(2)}, u32[]{:S(2)}) %collective-permute-start.9) | collective-permute-done | bytes 196640 | tf_op jit(solution)/shard_map/ppermute | solution.py:341
  43.8 0.2 collective-permute-start.15
  44.0 1.3 %collective-permute-start.26 = (bf16[3,192,512]{2,1,0:T(8,128)(2,1)S(1)}, bf16[3,192,512]{2,1,0:T(8,128)(2,1)S(1)}, u32[]{:S(2)}, u32[]{:S(2)}) collective-permute-start(bf16[3,192,512]{2,1,0:T(8,128)(2,1)S(1)} %cut_columns.7.refs_9_), channel_id=1, source_target_pairs={{0,1},{4,5},{9,8},{13,12},{18,19},{22,23},{27,26},{31,30}} | collective-permute-start | bytes 1769480 | tf_op jit(solution)/shard_map/ppermute | solution.py:332
  45.4 1.9 %collective-permute-start.16 = (bf16[3,32,1024]{2,1,0:T(8,128)(2,1)S(1)}, bf16[3,32,1024]{2,1,0:T(8,128)(2,1)S(1)}, u32[]{:S(2)}, u32[]{:S(2)}) collective-permute-start(bf16[3,32,1024]{2,1,0:T(8,128)(2,1)S(1)} %collective-permute-done.14.refs_3_.refs_6_), channel_id=1, source_target_pairs={{8,0},{16,8},{24,16},{28,24},{20,28},{12,20},{4,12},{0,4},{9,1},{1... | collective-permute-start | bytes 589832 | tf_op jit(solution)/shard_map/ppermute | solution.py:341
  47.3 1.0 cut_columns.4.refs_13_.refs_9_
  48.3 2.9 %collective-permute-start.18 = (bf16[3,128,512]{2,1,0:T(8,128)(2,1)S(1)}, bf16[3,128,512]{2,1,0:T(8,128)(2,1)}, u32[]{:S(2)}, u32[]{:S(2)}) collective-permute-start(bf16[3,128,512]{2,1,0:T(8,128)(2,1)S(1)} %cut_columns.4.refs_13_.refs_9_), channel_id=1, source_target_pairs={{0,2},{4,6},{9,11},{13,15},{18,16},{22,20},{27,25},{31,29}} | collective-permute-start | bytes 1179656 | tf_op jit(solution)/shard_map/ppermute | solution.py:331
  51.3 1.3 %collective-permute-start.17 = (bf16[3,128,512]{2,1,0:T(8,128)(2,1)S(1)}, bf16[3,128,512]{2,1,0:T(8,128)(2,1)S(1)}, u32[]{:S(2)}, u32[]{:S(2)}) collective-permute-start(bf16[3,128,512]{2,1,0:T(8,128)(2,1)S(1)} %cut_columns.4.refs_13_.refs_9_), channel_id=1, source_target_pairs={{0,1},{4,5},{9,8},{13,12},{18,19},{22,23},{27,26},{31,30}} | collective-permute-start | bytes 1179656 | tf_op jit(solution)/shard_map/ppermute | solution.py:332
  52.6 0.1 cut_columns.5.refs_13_
  52.7 3.1 %collective-permute-start.21 = (bf16[3,128,512]{2,1,0:T(8,128)(2,1)S(1)}, bf16[3,128,512]{2,1,0:T(8,128)(2,1)}, u32[]{:S(2)}, u32[]{:S(2)}) collective-permute-start(bf16[3,128,512]{2,1,0:T(8,128)(2,1)S(1)} %cut_columns.5.refs_13_), channel_id=1, source_target_pairs={{0,2},{4,6},{9,11},{13,15},{18,16},{22,20},{27,25},{31,29}} | collective-permute-start | bytes 1179656 | tf_op jit(solution)/shard_map/ppermute | solution.py:331
  55.8 1.5 %collective-permute-start.28 = (bf16[3,192,512]{2,1,0:T(8,128)(2,1)}, bf16[3,192,512]{2,1,0:T(8,128)(2,1)}, u32[]{:S(2)}, u32[]{:S(2)}) collective-permute-start(bf16[3,192,512]{2,1,0:T(8,128)(2,1)} %collective-permute-done.27.refs_11_), channel_id=1, source_target_pairs={{2,3},{6,7},{11,10},{15,14},{16,17},{20,21},{25,24},{29,28}} | collective-permute-start | bytes 1769480 | tf_op jit(solution)/shard_map/ppermute | solution.py:333
  57.3 0.0 collective-permute-done.18.refs_15_.refs_11_
  57.3 1.4 %collective-permute-start.19 = (bf16[3,128,512]{2,1,0:T(8,128)(2,1)}, bf16[3,128,512]{2,1,0:T(8,128)(2,1)}, u32[]{:S(2)}, u32[]{:S(2)}) collective-permute-start(bf16[3,128,512]{2,1,0:T(8,128)(2,1)} %collective-permute-done.18.refs_15_.refs_11_), channel_id=1, source_target_pairs={{2,3},{6,7},{11,10},{15,14},{16,17},{20,21},{25,24},{29,28}} | collective-permute-start | bytes 1179656 | tf_op jit(solution)/shard_map/ppermute | solution.py:333
  58.7 0.7 cut_columns.6.refs_17_
  59.4 0.0 collective-permute-done.17.refs_14_.refs_10_
  59.4 2.0 %collective-permute-start.20 = (bf16[3,128,512]{2,1,0:T(8,128)(2,1)S(1)}, bf16[3,128,512]{2,1,0:T(8,128)(2,1)}, u32[]{:S(2)}, u32[]{:S(2)}) collective-permute-start(bf16[3,128,512]{2,1,0:T(8,128)(2,1)S(1)} %cut_columns.5.refs_13_), channel_id=1, source_target_pairs={{0,1},{4,5},{9,8},{13,12},{18,19},{22,23},{27,26},{31,30}} | collective-permute-start | bytes 1179656 | tf_op jit(solution)/shard_map/ppermute | solution.py:332
  61.5 3.6 %collective-permute-start.24 = (bf16[3,64,512]{2,1,0:T(8,128)(2,1)}, bf16[3,64,512]{2,1,0:T(8,128)(2,1)}, u32[]{:S(2)}, u32[]{:S(2)}) collective-permute-start(bf16[3,64,512]{2,1,0:T(8,128)(2,1)} %cut_columns.6.refs_17_), channel_id=1, source_target_pairs={{0,2},{4,6},{9,11},{13,15},{18,16},{22,20},{27,25},{31,29}} | collective-permute-start | bytes 589832 | tf_op jit(solution)/shard_map/ppermute | solution.py:331
  65.1 0.0 collective-permute-done.21.refs_15_
  65.2 1.4 %collective-permute-start.22 = (bf16[3,128,512]{2,1,0:T(8,128)(2,1)}, bf16[3,128,512]{2,1,0:T(8,128)(2,1)}, u32[]{:S(2)}, u32[]{:S(2)}) collective-permute-start(bf16[3,128,512]{2,1,0:T(8,128)(2,1)} %collective-permute-done.21.refs_15_), channel_id=1, source_target_pairs={{2,3},{6,7},{11,10},{15,14},{16,17},{20,21},{25,24},{29,28}} | collective-permute-start | bytes 1179656 | tf_op jit(solution)/shard_map/ppermute | solution.py:333
  66.6 1.4 %convolution_bitcast_fusion = f32[256,64]{1,0:T(8,128)} fusion(bf16[3,1024,256]{2,1,0:T(8,128)(2,1)S(1)} %copy-done, bf16[3,32,1024]{2,1,0:T(8,128)(2,1)S(1)} %get-tuple-element.5.refs_1_.refs_2_, bf16[3,32,1024]{2,1,0:T(8,128)(2,1)S(1)} %get-tuple-element.4.refs_0_.refs_1_), kind=kOutput, calls=%fused_computation | convolution fusion | flops 101449728 | bytes 2031616 | tf_op jit(solution)/shard_map/cfa,cak->fk/dot_general | solution.py:295
  68.0 0.0 reduce-scatter.4.cloned.1.call-update
  68.0 18.7 %reduce-scatter.4.cloned.1.call-done = f32[64,64]{1,0:T(8,128)} async-done(((f32[256,64]{1,0:T(8,128)}), f32[64,64]{1,0:T(8,128)}) %reduce-scatter.4.cloned.1.call-update) | async-done | bytes 16400
  86.7 1.5 %copy.6 = f32[64,64]{1,0:T(8,128)} copy(f32[64,64]{0,1:T(8,128)} %bitcast.14) | data formatting | bytes 32768
  88.2 1.3 %collective-permute-start.23 = (bf16[3,64,512]{2,1,0:T(8,128)(2,1)}, bf16[3,64,512]{2,1,0:T(8,128)(2,1)S(1)}, u32[]{:S(2)}, u32[]{:S(2)}) collective-permute-start(bf16[3,64,512]{2,1,0:T(8,128)(2,1)} %cut_columns.6.refs_17_), channel_id=1, source_target_pairs={{0,1},{4,5},{9,8},{13,12},{18,19},{22,23},{27,26},{31,30}} | collective-permute-start | bytes 589832 | tf_op jit(solution)/shard_map/ppermute | solution.py:332
  89.5 0.0 collective-permute-done.19.refs_16_.refs_12_
  89.5 0.7 collective-permute-start.25
  90.2 0.0 collective-permute-done.28.refs_12_
  90.3 6.9 %covariance_first.1.refs_21_ = f32[3,3,1024,512]{3,2,1,0:T(8,128)S(1)} custom-call(s32[1]{0:T(128)} %bitcast.refs_0_, bf16[3,32,1024]{2,1,0:T(8,128)(2,1)} %copy-done.6, bf16[3,32,1024]{2,1,0:T(8,128)(2,1)} %copy-done.7, bf16[3,32,1024]{2,1,0:T(8,128)(2,1)} %copy-done.12, bf16[3,32,1024]{2,1,0:T(8,128)(2,1)} %copy-done.17, bf16[3,32,1024]{2,1,0:T(8,128)(2,1)} %copy-done.13, ...), custom_call_target="tpu_custom_call" | custom-call | flops 2415919104 | bytes 4194304 | tf_op jit(solution)/shard_map/covariance_first/pallas_call | solution.py:371
  97.2 6.5 %copy-done.1 = f32[3,3,1024,512]{3,2,1,0:T(8,128)} copy-done((f32[3,3,1024,512]{3,2,1,0:T(8,128)}, f32[3,3,1024,512]{3,2,1,0:T(8,128)S(1)}, u32[]{:S(2)}) %copy-start.1) | copy-done | bytes 18874392
  103.7 0.0 collective-permute-done.22.refs_16_
  103.8 18.1 %covariance_second.1 = f32[3,3,1024,512]{3,2,1,0:T(8,128)} custom-call(s32[1]{0:T(128)} %bitcast.refs_0_, bf16[3,32,1024]{2,1,0:T(8,128)(2,1)S(1)} %copy-done.15, bf16[3,32,1024]{2,1,0:T(8,128)(2,1)} %collective-permute-done.6.refs_3_.refs_2_, bf16[3,32,1024]{2,1,0:T(8,128)(2,1)S(1)} %copy-done.19, bf16[3,32,1024]{2,1,0:T(8,128)(2,1)S(1)} %copy-done.25, ...), custom_call_target="tpu_custom_call" | custom-call | flops 2415919104 | bytes 20971520 | tf_op jit(solution)/shard_map/covariance_second/pallas_call | solution.py:381
  (63 shorter events, 0.1 us)
Async XLA Ops:
  7.2 59.4 %copy-start = (bf16[3,1024,256]{2,1,0:T(8,128)(2,1)S(1)}, bf16[3,1024,256]{2,1,0:T(8,128)(2,1)}, u32[]{:S(2)}) copy-start(bf16[3,1024,256]{2,1,0:T(8,128)(2,1)} %param.5) | copy-start | bytes 4718596
  7.2 79.6 %reduce-scatter.4.cloned.1.call-start = ((), (), s32[]{:S(2)}) async-start(), calls=%async_computation.1 | async-start | bytes 163840
  7.2 1.2 copy-start.4
  8.5 0.7 copy-start.26
  9.8 3.8 %collective-permute-start.2 = (f32[24,64]{1,0:T(8,128)S(1)}, f32[24,64]{1,0:T(8,128)S(1)}, u32[]{:S(2)}, u32[]{:S(2)}) collective-permute-start(f32[24,64]{1,0:T(8,128)S(1)} %local_moments.1.refs_0_), channel_id=1, source_target_pairs={{0,3},{1,2},{2,1},{3,0},{4,7},{5,6},{6,5},{7,4},{8,11},{9,10},{10,... | collective-permute-start | bytes 18440 | tf_op jit(solution)/shard_map/ppermute | solution.py:279
  12.2 3.7 %collective-permute-start.1 = (f32[24,64]{1,0:T(8,128)S(1)}, f32[24,64]{1,0:T(8,128)S(1)}, u32[]{:S(2)}, u32[]{:S(2)}) collective-permute-start(f32[24,64]{1,0:T(8,128)S(1)} %local_moments.1.refs_0_), channel_id=1, source_target_pairs={{0,2},{1,3},{2,0},{3,1},{4,6},{5,7},{6,4},{7,5},{8,10},{9,11},{10,... | collective-permute-start | bytes 18440 | tf_op jit(solution)/shard_map/ppermute | solution.py:279
  12.8 3.1 %collective-permute-start = (f32[24,64]{1,0:T(8,128)S(1)}, f32[24,64]{1,0:T(8,128)S(1)}, u32[]{:S(2)}, u32[]{:S(2)}) collective-permute-start(f32[24,64]{1,0:T(8,128)S(1)} %local_moments.1.refs_0_), channel_id=1, source_target_pairs={{0,1},{1,0},{2,3},{3,2},{4,5},{5,4},{6,7},{7,6},{8,9},{9,8},{10,11... | collective-permute-start | bytes 18440 | tf_op jit(solution)/shard_map/ppermute | solution.py:279
  16.5 50.1 %copy-start.6 = (bf16[3,32,1024]{2,1,0:T(8,128)(2,1)}, bf16[3,32,1024]{2,1,0:T(8,128)(2,1)S(1)}, u32[]{:S(2)}) copy-start(bf16[3,32,1024]{2,1,0:T(8,128)(2,1)S(1)} %get-tuple-element.4.refs_0_.refs_1_) | copy-start | bytes 589828
  16.5 50.1 %copy-start.7 = (bf16[3,32,1024]{2,1,0:T(8,128)(2,1)}, bf16[3,32,1024]{2,1,0:T(8,128)(2,1)S(1)}, u32[]{:S(2)}) copy-start(bf16[3,32,1024]{2,1,0:T(8,128)(2,1)S(1)} %get-tuple-element.5.refs_1_.refs_2_) | copy-start | bytes 589828
  16.5 7.9 %collective-permute-start.7 = (bf16[3,32,1024]{2,1,0:T(8,128)(2,1)S(1)}, bf16[3,32,1024]{2,1,0:T(8,128)(2,1)S(1)}, u32[]{:S(2)}, u32[]{:S(2)}) collective-permute-start(bf16[3,32,1024]{2,1,0:T(8,128)(2,1)S(1)} %get-tuple-element.4.refs_0_.refs_1_), channel_id=1, source_target_pairs={{0,8},{8,16},{16,24},{24,28},{28,20},{20,12},{12,4},{4,0},{1,9},{9... | collective-permute-start | bytes 589832 | tf_op jit(solution)/shard_map/ppermute | solution.py:341
  18.1 7.8 %collective-permute-start.3 = (bf16[3,32,1024]{2,1,0:T(8,128)(2,1)S(1)}, bf16[3,32,1024]{2,1,0:T(8,128)(2,1)S(1)}, u32[]{:S(2)}, u32[]{:S(2)}) collective-permute-start(bf16[3,32,1024]{2,1,0:T(8,128)(2,1)S(1)} %get-tuple-element.4.refs_0_.refs_1_), channel_id=1, source_target_pairs={{8,0},{16,8},{24,16},{28,24},{20,28},{12,20},{4,12},{0,4},{9,1},{1... | collective-permute-start | bytes 589832 | tf_op jit(solution)/shard_map/ppermute | solution.py:341
  18.6 11.6 %collective-permute-start.5 = (bf16[3,32,1024]{2,1,0:T(8,128)(2,1)S(1)}, bf16[3,32,1024]{2,1,0:T(8,128)(2,1)S(1)}, u32[]{:S(2)}, u32[]{:S(2)}) collective-permute-start(bf16[3,32,1024]{2,1,0:T(8,128)(2,1)S(1)} %get-tuple-element.5.refs_1_.refs_2_), channel_id=1, source_target_pairs={{8,0},{16,8},{24,16},{28,24},{20,28},{12,20},{4,12},{0,4},{9,1},{1... | collective-permute-start | bytes 589832 | tf_op jit(solution)/shard_map/ppermute | solution.py:341
  20.1 10.5 %collective-permute-start.10 = (bf16[3,32,1024]{2,1,0:T(8,128)(2,1)S(1)}, bf16[3,32,1024]{2,1,0:T(8,128)(2,1)S(1)}, u32[]{:S(2)}, u32[]{:S(2)}) collective-permute-start(bf16[3,32,1024]{2,1,0:T(8,128)(2,1)S(1)} %get-tuple-element.5.refs_1_.refs_2_), channel_id=1, source_target_pairs={{0,8},{8,16},{16,24},{24,28},{28,20},{20,12},{12,4},{4,0},{1,9},{9... | collective-permute-start | bytes 589832 | tf_op jit(solution)/shard_map/ppermute | solution.py:341
  24.4 21.0 %copy-start.12 = (bf16[3,32,1024]{2,1,0:T(8,128)(2,1)}, bf16[3,32,1024]{2,1,0:T(8,128)(2,1)S(1)}, u32[]{:S(2)}) copy-start(bf16[3,32,1024]{2,1,0:T(8,128)(2,1)S(1)} %collective-permute-done.7.refs_2_.refs_3_) | copy-start | bytes 589828
  24.4 11.4 %collective-permute-start.8 = (bf16[3,32,1024]{2,1,0:T(8,128)(2,1)S(1)}, bf16[3,32,1024]{2,1,0:T(8,128)(2,1)}, u32[]{:S(2)}, u32[]{:S(2)}) collective-permute-start(bf16[3,32,1024]{2,1,0:T(8,128)(2,1)S(1)} %collective-permute-done.7.refs_2_.refs_3_), channel_id=1, source_target_pairs={{0,8},{8,16},{16,24},{24,28},{28,20},{20,12},{12,4},{4,0},{1,9},{9... | collective-permute-start | bytes 589832 | tf_op jit(solution)/shard_map/ppermute | solution.py:341
  26.0 19.4 %copy-start.13 = (bf16[3,32,1024]{2,1,0:T(8,128)(2,1)}, bf16[3,32,1024]{2,1,0:T(8,128)(2,1)S(1)}, u32[]{:S(2)}) copy-start(bf16[3,32,1024]{2,1,0:T(8,128)(2,1)S(1)} %collective-permute-done.3.refs_4_.refs_5_) | copy-start | bytes 589828
  26.0 9.8 %collective-permute-start.4 = (bf16[3,32,1024]{2,1,0:T(8,128)(2,1)S(1)}, bf16[3,32,1024]{2,1,0:T(8,128)(2,1)S(1)}, u32[]{:S(2)}, u32[]{:S(2)}) collective-permute-start(bf16[3,32,1024]{2,1,0:T(8,128)(2,1)S(1)} %collective-permute-done.3.refs_4_.refs_5_), channel_id=1, source_target_pairs={{8,0},{16,8},{24,16},{28,24},{20,28},{12,20},{4,12},{0,4},{9,1},{1... | collective-permute-start | bytes 589832 | tf_op jit(solution)/shard_map/ppermute | solution.py:341
  30.2 21.1 %copy-start.16 = (bf16[3,32,1024]{2,1,0:T(8,128)(2,1)}, bf16[3,32,1024]{2,1,0:T(8,128)(2,1)S(1)}, u32[]{:S(2)}) copy-start(bf16[3,32,1024]{2,1,0:T(8,128)(2,1)S(1)} %collective-permute-done.5.refs_5_.refs_6_) | copy-start | bytes 589828
  30.2 8.0 %collective-permute-start.6 = (bf16[3,32,1024]{2,1,0:T(8,128)(2,1)S(1)}, bf16[3,32,1024]{2,1,0:T(8,128)(2,1)}, u32[]{:S(2)}, u32[]{:S(2)}) collective-permute-start(bf16[3,32,1024]{2,1,0:T(8,128)(2,1)S(1)} %collective-permute-done.5.refs_5_.refs_6_), channel_id=1, source_target_pairs={{8,0},{16,8},{24,16},{28,24},{20,28},{12,20},{4,12},{0,4},{9,1},{1... | collective-permute-start | bytes 589832 | tf_op jit(solution)/shard_map/ppermute | solution.py:341
  30.6 9.7 %copy-start.17 = (bf16[3,32,1024]{2,1,0:T(8,128)(2,1)}, bf16[3,32,1024]{2,1,0:T(8,128)(2,1)S(1)}, u32[]{:S(2)}) copy-start(bf16[3,32,1024]{2,1,0:T(8,128)(2,1)S(1)} %collective-permute-done.10.refs_3_.refs_4_) | copy-start | bytes 589828
  30.6 8.2 %collective-permute-start.11 = (bf16[3,32,1024]{2,1,0:T(8,128)(2,1)S(1)}, bf16[3,32,1024]{2,1,0:T(8,128)(2,1)}, u32[]{:S(2)}, u32[]{:S(2)}) collective-permute-start(bf16[3,32,1024]{2,1,0:T(8,128)(2,1)S(1)} %collective-permute-done.10.refs_3_.refs_4_), channel_id=1, source_target_pairs={{0,8},{8,16},{16,24},{24,28},{28,20},{20,12},{12,4},{4,0},{1,9},{9... | collective-permute-start | bytes 589832 | tf_op jit(solution)/shard_map/ppermute | solution.py:341
  32.4 35.6 %copy-start.5 = (bf16[3,192,512]{2,1,0:T(8,128)(2,1)}, bf16[3,192,512]{2,1,0:T(8,128)(2,1)S(1)}, u32[]{:S(2)}) copy-start(bf16[3,192,512]{2,1,0:T(8,128)(2,1)S(1)} %cut_columns.7.refs_9_) | copy-start | bytes 1769476
  32.4 23.4 %collective-permute-start.27 = (bf16[3,192,512]{2,1,0:T(8,128)(2,1)S(1)}, bf16[3,192,512]{2,1,0:T(8,128)(2,1)}, u32[]{:S(2)}, u32[]{:S(2)}) collective-permute-start(bf16[3,192,512]{2,1,0:T(8,128)(2,1)S(1)} %cut_columns.7.refs_9_), channel_id=1, source_target_pairs={{0,2},{4,6},{9,11},{13,15},{18,16},{22,20},{27,25},{31,29}} | collective-permute-start | bytes 1769480 | tf_op jit(solution)/shard_map/ppermute | solution.py:331
  35.8 8.0 %collective-permute-start.9 = (bf16[3,32,1024]{2,1,0:T(8,128)(2,1)}, bf16[3,32,1024]{2,1,0:T(8,128)(2,1)S(1)}, u32[]{:S(2)}, u32[]{:S(2)}) collective-permute-start(bf16[3,32,1024]{2,1,0:T(8,128)(2,1)} %collective-permute-done.8.refs_0_.refs_7_), channel_id=1, source_target_pairs={{0,8},{8,16},{16,24},{24,28},{28,20},{20,12},{12,4},{4,0},{1,9},{9... | collective-permute-start | bytes 589832 | tf_op jit(solution)/shard_map/ppermute | solution.py:341
  35.8 15.5 %copy-start.14 = (bf16[3,32,1024]{2,1,0:T(8,128)(2,1)}, bf16[3,32,1024]{2,1,0:T(8,128)(2,1)S(1)}, u32[]{:S(2)}) copy-start(bf16[3,32,1024]{2,1,0:T(8,128)(2,1)S(1)} %collective-permute-done.4.refs_2_.refs_1_) | copy-start | bytes 589828
  35.8 8.2 %collective-permute-start.13 = (bf16[3,32,1024]{2,1,0:T(8,128)(2,1)S(1)}, bf16[3,32,1024]{2,1,0:T(8,128)(2,1)S(1)}, u32[]{:S(2)}, u32[]{:S(2)}) collective-permute-start(bf16[3,32,1024]{2,1,0:T(8,128)(2,1)S(1)} %collective-permute-done.4.refs_2_.refs_1_), channel_id=1, source_target_pairs={{8,0},{16,8},{24,16},{28,24},{20,28},{12,20},{4,12},{0,4},{9,1},{1... | collective-permute-start | bytes 589832 | tf_op jit(solution)/shard_map/ppermute | solution.py:341
  38.2 7.2 %collective-permute-start.14 = (bf16[3,32,1024]{2,1,0:T(8,128)(2,1)}, bf16[3,32,1024]{2,1,0:T(8,128)(2,1)S(1)}, u32[]{:S(2)}, u32[]{:S(2)}) collective-permute-start(bf16[3,32,1024]{2,1,0:T(8,128)(2,1)} %collective-permute-done.6.refs_3_.refs_2_), channel_id=1, source_target_pairs={{8,0},{16,8},{24,16},{28,24},{20,28},{12,20},{4,12},{0,4},{9,1},{1... | collective-permute-start | bytes 589832 | tf_op jit(solution)/shard_map/ppermute | solution.py:341
  38.8 9.5 %collective-permute-start.12 = (bf16[3,32,1024]{2,1,0:T(8,128)(2,1)}, bf16[3,32,1024]{2,1,0:T(8,128)(2,1)S(1)}, u32[]{:S(2)}, u32[]{:S(2)}) collective-permute-start(bf16[3,32,1024]{2,1,0:T(8,128)(2,1)} %collective-permute-done.11.refs_1_.refs_8_), channel_id=1, source_target_pairs={{0,8},{8,16},{16,24},{24,28},{28,20},{20,12},{12,4},{4,0},{1,9},{9... | collective-permute-start | bytes 589832 | tf_op jit(solution)/shard_map/ppermute | solution.py:341
  43.8 21.3 %copy-start.18 = (bf16[3,32,1024]{2,1,0:T(8,128)(2,1)}, bf16[3,32,1024]{2,1,0:T(8,128)(2,1)S(1)}, u32[]{:S(2)}) copy-start(bf16[3,32,1024]{2,1,0:T(8,128)(2,1)S(1)} %collective-permute-done.9.refs_0_.refs_3_) | copy-start | bytes 589828
  43.8 7.5 %collective-permute-start.15 = (bf16[3,32,1024]{2,1,0:T(8,128)(2,1)S(1)}, bf16[3,32,1024]{2,1,0:T(8,128)(2,1)S(1)}, u32[]{:S(2)}, u32[]{:S(2)}) collective-permute-start(bf16[3,32,1024]{2,1,0:T(8,128)(2,1)S(1)} %collective-permute-done.9.refs_0_.refs_3_), channel_id=1, source_target_pairs={{0,8},{8,16},{16,24},{24,28},{28,20},{20,12},{12,4},{4,0},{1,9},{9... | collective-permute-start | bytes 589832 | tf_op jit(solution)/shard_map/ppermute | solution.py:341
  44.0 21.1 %copy-start.20 = (bf16[3,32,1024]{2,1,0:T(8,128)(2,1)}, bf16[3,32,1024]{2,1,0:T(8,128)(2,1)S(1)}, u32[]{:S(2)}) copy-start(bf16[3,32,1024]{2,1,0:T(8,128)(2,1)S(1)} %collective-permute-done.13.refs_2_.refs_5_) | copy-start | bytes 589828
  44.0 17.5 %collective-permute-start.26 = (bf16[3,192,512]{2,1,0:T(8,128)(2,1)S(1)}, bf16[3,192,512]{2,1,0:T(8,128)(2,1)S(1)}, u32[]{:S(2)}, u32[]{:S(2)}) collective-permute-start(bf16[3,192,512]{2,1,0:T(8,128)(2,1)S(1)} %cut_columns.7.refs_9_), channel_id=1, source_target_pairs={{0,1},{4,5},{9,8},{13,12},{18,19},{22,23},{27,26},{31,30}} | collective-permute-start | bytes 1769480 | tf_op jit(solution)/shard_map/ppermute | solution.py:332
  45.4 11.9 %copy-start.22 = (bf16[3,32,1024]{2,1,0:T(8,128)(2,1)}, bf16[3,32,1024]{2,1,0:T(8,128)(2,1)S(1)}, u32[]{:S(2)}) copy-start(bf16[3,32,1024]{2,1,0:T(8,128)(2,1)S(1)} %collective-permute-done.14.refs_3_.refs_6_) | copy-start | bytes 589828
  45.4 7.3 %collective-permute-start.16 = (bf16[3,32,1024]{2,1,0:T(8,128)(2,1)S(1)}, bf16[3,32,1024]{2,1,0:T(8,128)(2,1)S(1)}, u32[]{:S(2)}, u32[]{:S(2)}) collective-permute-start(bf16[3,32,1024]{2,1,0:T(8,128)(2,1)S(1)} %collective-permute-done.14.refs_3_.refs_6_), channel_id=1, source_target_pairs={{8,0},{16,8},{24,16},{28,24},{20,28},{12,20},{4,12},{0,4},{9,1},{1... | collective-permute-start | bytes 589832 | tf_op jit(solution)/shard_map/ppermute | solution.py:341
  48.3 19.7 %copy-start.2 = (bf16[3,128,512]{2,1,0:T(8,128)(2,1)}, bf16[3,128,512]{2,1,0:T(8,128)(2,1)S(1)}, u32[]{:S(2)}) copy-start(bf16[3,128,512]{2,1,0:T(8,128)(2,1)S(1)} %cut_columns.4.refs_13_.refs_9_) | copy-start | bytes 1179652
  48.3 16.8 %copy-start.24 = (bf16[3,32,1024]{2,1,0:T(8,128)(2,1)}, bf16[3,32,1024]{2,1,0:T(8,128)(2,1)S(1)}, u32[]{:S(2)}) copy-start(bf16[3,32,1024]{2,1,0:T(8,128)(2,1)S(1)} %collective-permute-done.12.refs_1_.refs_4_) | copy-start | bytes 589828
  48.3 9.0 %collective-permute-start.18 = (bf16[3,128,512]{2,1,0:T(8,128)(2,1)S(1)}, bf16[3,128,512]{2,1,0:T(8,128)(2,1)}, u32[]{:S(2)}, u32[]{:S(2)}) collective-permute-start(bf16[3,128,512]{2,1,0:T(8,128)(2,1)S(1)} %cut_columns.4.refs_13_.refs_9_), channel_id=1, source_target_pairs={{0,2},{4,6},{9,11},{13,15},{18,16},{22,20},{27,25},{31,29}} | collective-permute-start | bytes 1179656 | tf_op jit(solution)/shard_map/ppermute | solution.py:331
  51.3 8.2 %collective-permute-start.17 = (bf16[3,128,512]{2,1,0:T(8,128)(2,1)S(1)}, bf16[3,128,512]{2,1,0:T(8,128)(2,1)S(1)}, u32[]{:S(2)}, u32[]{:S(2)}) collective-permute-start(bf16[3,128,512]{2,1,0:T(8,128)(2,1)S(1)} %cut_columns.4.refs_13_.refs_9_), channel_id=1, source_target_pairs={{0,1},{4,5},{9,8},{13,12},{18,19},{22,23},{27,26},{31,30}} | collective-permute-start | bytes 1179656 | tf_op jit(solution)/shard_map/ppermute | solution.py:332
  52.7 12.4 %copy-start.10 = (bf16[3,32,1024]{2,1,0:T(8,128)(2,1)}, bf16[3,32,1024]{2,1,0:T(8,128)(2,1)S(1)}, u32[]{:S(2)}) copy-start(bf16[3,32,1024]{2,1,0:T(8,128)(2,1)S(1)} %collective-permute-done.16.refs_1_.refs_8_) | copy-start | bytes 589828
  52.7 12.4 %collective-permute-start.21 = (bf16[3,128,512]{2,1,0:T(8,128)(2,1)S(1)}, bf16[3,128,512]{2,1,0:T(8,128)(2,1)}, u32[]{:S(2)}, u32[]{:S(2)}) collective-permute-start(bf16[3,128,512]{2,1,0:T(8,128)(2,1)S(1)} %cut_columns.5.refs_13_), channel_id=1, source_target_pairs={{0,2},{4,6},{9,11},{13,15},{18,16},{22,20},{27,25},{31,29}} | collective-permute-start | bytes 1179656 | tf_op jit(solution)/shard_map/ppermute | solution.py:331
  55.8 34.4 %collective-permute-start.28 = (bf16[3,192,512]{2,1,0:T(8,128)(2,1)}, bf16[3,192,512]{2,1,0:T(8,128)(2,1)}, u32[]{:S(2)}, u32[]{:S(2)}) collective-permute-start(bf16[3,192,512]{2,1,0:T(8,128)(2,1)} %collective-permute-done.27.refs_11_), channel_id=1, source_target_pairs={{2,3},{6,7},{11,10},{15,14},{16,17},{20,21},{25,24},{29,28}} | collective-permute-start | bytes 1769480 | tf_op jit(solution)/shard_map/ppermute | solution.py:333
  57.3 32.2 %collective-permute-start.19 = (bf16[3,128,512]{2,1,0:T(8,128)(2,1)}, bf16[3,128,512]{2,1,0:T(8,128)(2,1)}, u32[]{:S(2)}, u32[]{:S(2)}) collective-permute-start(bf16[3,128,512]{2,1,0:T(8,128)(2,1)} %collective-permute-done.18.refs_15_.refs_11_), channel_id=1, source_target_pairs={{2,3},{6,7},{11,10},{15,14},{16,17},{20,21},{25,24},{29,28}} | collective-permute-start | bytes 1179656 | tf_op jit(solution)/shard_map/ppermute | solution.py:333
  59.4 5.7 %copy-start.8 = (bf16[3,128,512]{2,1,0:T(8,128)(2,1)}, bf16[3,128,512]{2,1,0:T(8,128)(2,1)S(1)}, u32[]{:S(2)}) copy-start(bf16[3,128,512]{2,1,0:T(8,128)(2,1)S(1)} %collective-permute-done.17.refs_14_.refs_10_) | copy-start | bytes 1179652
  59.4 44.2 %collective-permute-start.20 = (bf16[3,128,512]{2,1,0:T(8,128)(2,1)S(1)}, bf16[3,128,512]{2,1,0:T(8,128)(2,1)}, u32[]{:S(2)}, u32[]{:S(2)}) collective-permute-start(bf16[3,128,512]{2,1,0:T(8,128)(2,1)S(1)} %cut_columns.5.refs_13_), channel_id=1, source_target_pairs={{0,1},{4,5},{9,8},{13,12},{18,19},{22,23},{27,26},{31,30}} | collective-permute-start | bytes 1179656 | tf_op jit(solution)/shard_map/ppermute | solution.py:332
  61.5 3.7 %copy-start.27 = (bf16[3,192,512]{2,1,0:T(8,128)(2,1)}, bf16[3,192,512]{2,1,0:T(8,128)(2,1)S(1)}, u32[]{:S(2)}) copy-start(bf16[3,192,512]{2,1,0:T(8,128)(2,1)S(1)} %collective-permute-done.26.refs_10_) | copy-start | bytes 1769476
  61.5 26.7 %collective-permute-start.24 = (bf16[3,64,512]{2,1,0:T(8,128)(2,1)}, bf16[3,64,512]{2,1,0:T(8,128)(2,1)}, u32[]{:S(2)}, u32[]{:S(2)}) collective-permute-start(bf16[3,64,512]{2,1,0:T(8,128)(2,1)} %cut_columns.6.refs_17_), channel_id=1, source_target_pairs={{0,2},{4,6},{9,11},{13,15},{18,16},{22,20},{27,25},{31,29}} | collective-permute-start | bytes 589832 | tf_op jit(solution)/shard_map/ppermute | solution.py:331
  65.2 38.5 %collective-permute-start.22 = (bf16[3,128,512]{2,1,0:T(8,128)(2,1)}, bf16[3,128,512]{2,1,0:T(8,128)(2,1)}, u32[]{:S(2)}, u32[]{:S(2)}) collective-permute-start(bf16[3,128,512]{2,1,0:T(8,128)(2,1)} %collective-permute-done.21.refs_15_), channel_id=1, source_target_pairs={{2,3},{6,7},{11,10},{15,14},{16,17},{20,21},{25,24},{29,28}} | collective-permute-start | bytes 1179656 | tf_op jit(solution)/shard_map/ppermute | solution.py:333
  88.2 15.5 %collective-permute-start.23 = (bf16[3,64,512]{2,1,0:T(8,128)(2,1)}, bf16[3,64,512]{2,1,0:T(8,128)(2,1)S(1)}, u32[]{:S(2)}, u32[]{:S(2)}) collective-permute-start(bf16[3,64,512]{2,1,0:T(8,128)(2,1)} %cut_columns.6.refs_17_), channel_id=1, source_target_pairs={{0,1},{4,5},{9,8},{13,12},{18,19},{22,23},{27,26},{31,30}} | collective-permute-start | bytes 589832 | tf_op jit(solution)/shard_map/ppermute | solution.py:332
  89.5 14.2 %collective-permute-start.25 = (bf16[3,64,512]{2,1,0:T(8,128)(2,1)}, bf16[3,64,512]{2,1,0:T(8,128)(2,1)S(1)}, u32[]{:S(2)}, u32[]{:S(2)}) collective-permute-start(bf16[3,64,512]{2,1,0:T(8,128)(2,1)} %collective-permute-done.24.refs_19_), channel_id=1, source_target_pairs={{2,3},{6,7},{11,10},{15,14},{16,17},{20,21},{25,24},{29,28}} | collective-permute-start | bytes 589832 | tf_op jit(solution)/shard_map/ppermute | solution.py:333
  90.2 13.5 %copy-start.3 = (bf16[3,128,512]{2,1,0:T(8,128)(2,1)S(1)}, bf16[3,128,512]{2,1,0:T(8,128)(2,1)}, u32[]{:S(2)}) copy-start(bf16[3,128,512]{2,1,0:T(8,128)(2,1)} %copy-done.2) | copy-start | bytes 1179652
  90.2 13.5 %copy-start.9 = (bf16[3,128,512]{2,1,0:T(8,128)(2,1)S(1)}, bf16[3,128,512]{2,1,0:T(8,128)(2,1)}, u32[]{:S(2)}) copy-start(bf16[3,128,512]{2,1,0:T(8,128)(2,1)} %copy-done.8) | copy-start | bytes 1179652
  90.2 13.5 %copy-start.11 = (bf16[3,32,1024]{2,1,0:T(8,128)(2,1)S(1)}, bf16[3,32,1024]{2,1,0:T(8,128)(2,1)}, u32[]{:S(2)}) copy-start(bf16[3,32,1024]{2,1,0:T(8,128)(2,1)} %copy-done.10) | copy-start | bytes 589828
  90.2 13.5 %copy-start.15 = (bf16[3,32,1024]{2,1,0:T(8,128)(2,1)S(1)}, bf16[3,32,1024]{2,1,0:T(8,128)(2,1)}, u32[]{:S(2)}) copy-start(bf16[3,32,1024]{2,1,0:T(8,128)(2,1)} %copy-done.14) | copy-start | bytes 589828
  90.2 13.5 %copy-start.19 = (bf16[3,32,1024]{2,1,0:T(8,128)(2,1)S(1)}, bf16[3,32,1024]{2,1,0:T(8,128)(2,1)}, u32[]{:S(2)}) copy-start(bf16[3,32,1024]{2,1,0:T(8,128)(2,1)} %copy-done.18) | copy-start | bytes 589828
  90.3 13.5 %copy-start.21 = (bf16[3,32,1024]{2,1,0:T(8,128)(2,1)S(1)}, bf16[3,32,1024]{2,1,0:T(8,128)(2,1)}, u32[]{:S(2)}) copy-start(bf16[3,32,1024]{2,1,0:T(8,128)(2,1)} %copy-done.20) | copy-start | bytes 589828
  90.3 13.5 %copy-start.23 = (bf16[3,32,1024]{2,1,0:T(8,128)(2,1)S(1)}, bf16[3,32,1024]{2,1,0:T(8,128)(2,1)}, u32[]{:S(2)}) copy-start(bf16[3,32,1024]{2,1,0:T(8,128)(2,1)} %copy-done.22) | copy-start | bytes 589828
  90.3 13.5 %copy-start.25 = (bf16[3,32,1024]{2,1,0:T(8,128)(2,1)S(1)}, bf16[3,32,1024]{2,1,0:T(8,128)(2,1)}, u32[]{:S(2)}) copy-start(bf16[3,32,1024]{2,1,0:T(8,128)(2,1)} %copy-done.24) | copy-start | bytes 589828
  97.2 6.5 %copy-start.1 = (f32[3,3,1024,512]{3,2,1,0:T(8,128)}, f32[3,3,1024,512]{3,2,1,0:T(8,128)S(1)}, u32[]{:S(2)}) copy-start(f32[3,3,1024,512]{3,2,1,0:T(8,128)S(1)} %covariance_first.1.refs_21_) | copy-start | bytes 56623108
Sparse Core Ops, SparseCore 0:
  68.1 18.5 reduce-scatter.3

commit v3 on v2

v3 whole, which is shorter than its diff:
```python
import functools

import jax
import jax.numpy as jnp
from jax import lax
from jax.experimental import pallas as pl
from jax.experimental.pallas import tpu as pltpu
from jax.sharding import PartitionSpec as P

POLAR = 6
LANES = 128
STATS = 24
VMEM = pl.BlockSpec(memory_space=pltpu.VMEM)
SMEM = pl.BlockSpec(memory_space=pltpu.SMEM)
HBM = pl.BlockSpec(memory_space=pltpu.HBM)
ANY = pl.BlockSpec(memory_space=pl.ANY)
MIB = 1024 * 1024


def params(mib):
    return pltpu.CompilerParams(vmem_limit_bytes=mib * MIB)


def lane_mean(value):
    return jnp.sum(value, axis=1, keepdims=True) * (1.0 / value.shape[1])


def run_copies(copies):
    for copy in copies:
        copy.start()
    for copy in copies:
        copy.wait()


def stats_kernel(x_hbm, ref_hbm, out_ref, x_ref, ref_ref, sem):
    run_copies(
        [
            pltpu.make_async_copy(ref_hbm, ref_ref, sem.at[0]),
            pltpu.make_async_copy(x_hbm, x_ref, sem.at[1]),
        ]
    )
    values = []
    centred = []
    for i in range(3):
        x = x_ref[i]
        mean = lane_mean(x)
        values.append(mean)
        centred.append(x - mean)
    values.append(sum(jnp.sum(c * c, axis=1, keepdims=True) for c in centred))
    ref_mean = [lane_mean(ref_ref[j : j + 1, :]) for j in range(3)]
    ref_centred = [ref_ref[j : j + 1, :] - ref_mean[j] for j in range(3)]
    for i in range(3):
        for j in range(3):
            values.append(jnp.sum(centred[i] * ref_centred[j], axis=1, keepdims=True))
    values += ref_mean
    values.append(sum(jnp.sum(c * c, axis=1, keepdims=True) for c in ref_centred))
    shape = (x_ref.shape[1], LANES)
    lane = lax.broadcasted_iota(jnp.int32, shape, 1)
    out = jnp.zeros(shape, jnp.float32)
    for k, value in enumerate(values):
        out = jnp.where(lane == k, jnp.broadcast_to(value, shape), out)
    out_ref[...] = out.T[:STATS]


def align_kernel(parts, atoms, *refs):
    stats = refs[:parts]
    x_hbm, ref_hbm, first_ref, second_ref, flat_ref, x_ref, ref_ref, turn, sem = refs[parts:]
    copies = [
        pltpu.make_async_copy(ref_hbm, ref_ref, sem.at[0]),
        pltpu.make_async_copy(x_hbm, x_ref, sem.at[1]),
    ]
    for copy in copies:
        copy.start()
    local = x_ref.shape[2]
    rows = x_ref.shape[1]

    def row(at):
        return [s[at : at + 1, :] for s in stats]

    means = [row(i) for i in range(3)]
    ref_means = [row(13 + j) for j in range(3)]
    centre = [sum(m) * (1.0 / parts) for m in means]
    ref_centre = [sum(r) * (1.0 / parts) for r in ref_means]
    off = [[m - centre[i] for m in means[i]] for i in range(3)]
    ref_off = [[r - ref_centre[j] for r in ref_means[j]] for j in range(3)]
    spread = sum(row(3)) + local * sum(o * o for i in range(3) for o in off[i])
    ref_spread = sum(row(16)) + local * sum(o * o for j in range(3) for o in ref_off[j])
    scale = 1.0 / jnp.sqrt(spread * ref_spread + 1e-06)
    now = [
        [
            (sum(row(4 + 3 * i + j)) + local * sum(o * r for o, r in zip(off[i], ref_off[j])))
            * scale
            for j in range(3)
        ]
        for i in range(3)
    ]
    for _ in range(POLAR):
        gram = {}
        for i in range(3):
            for j in range(i, 3):
                gram[i, j] = sum(now[k][i] * now[k][j] for k in range(3))
                gram[j, i] = gram[i, j]
        left = [
            [(1.5 if k == j else 0.0) - 0.5 * gram[k, j] for j in range(3)] for k in range(3)
        ]
        now = [
            [sum(now[i][k] * left[k][j] for k in range(3)) for j in range(3)]
            for i in range(3)
        ]
    for k, value in enumerate(sum(now, []) + centre + ref_centre):
        turn[k : k + 1, :rows] = value
    turned = turn[...].T
    column = [turned[:rows, k : k + 1] for k in range(12)]
    for copy in copies:
        copy.wait()
    centred = [x_ref[j] - column[9 + j] for j in range(3)]
    for i in range(3):
        target = ref_ref[i : i + 1, :] - turned[0:1, 12 + i : 13 + i]
        moved = sum(column[3 * j + i] * centred[j] for j in range(3)) - target
        flat_ref[i] = moved.astype(jnp.bfloat16)
        run = first_ref.shape[1]
        for at, piece in enumerate((first_ref, second_ref)):
            pair = [moved[:, (2 * at + k) * run : (2 * at + k + 1) * run] for k in range(2)]
            piece[i] = jnp.concatenate(pair, axis=0).T.astype(jnp.bfloat16)


def cut_kernel(pieces, half_ref, *refs):
    sources, cols_ref, sem = refs[:pieces], refs[pieces], refs[pieces + 1]
    for half in range(2):

        @pl.when(half_ref[0] == half)
        def _(half=half):
            run_copies(
                [
                    pltpu.make_async_copy(source, cols_ref.at[k], sem.at[k])
                    for k, source in enumerate(sources[half::2])
                ]
            )


def side_by_side(first, second):
    middle = first.shape[1] // 2
    left = jnp.concatenate([first[:, :middle], second[:, :middle]], axis=1)
    right = jnp.concatenate([first[:, middle:], second[:, middle:]], axis=1)
    return left, right


def covariance_kernel(slots, roles, lots, scale, *refs):
    role_ref, pieces = refs[0], refs[1 : 1 + 2 * slots]
    at = 1 + 2 * slots
    groups = [refs[at + k * roles : at + (k + 1) * roles] for k in range(len(lots))]
    at += len(lots) * roles
    out_ref, rows_in, cols_in, left, right, done, sem, out_sem = refs[at:]
    copies = [
        pltpu.make_async_copy(piece, rows_in.at[k % 2, k // 2], sem.at[k])
        for k, piece in enumerate(pieces)
    ]
    for copy in copies:
        copy.start()
    for role in range(roles):

        @pl.when(role_ref[0] == role)
        def _(role=role):
            to = 0
            wanted = []
            for k, count in enumerate(lots):
                wanted.append(
                    pltpu.make_async_copy(
                        groups[k][role], cols_in.at[pl.ds(to, count)], sem.at[2 * slots + k]
                    )
                )
                to += count
            run_copies(wanted)

    run = rows_in.shape[3]
    for d in range(3):
        for q in range(slots // 2):
            low, high = side_by_side(cols_in[2 * q, d], cols_in[2 * q + 1, d])
            right[d, :run, q * LANES : (q + 1) * LANES] = low
            right[d, run:, q * LANES : (q + 1) * LANES] = high
    for copy in copies:
        copy.wait()

    def assemble(i, slot):
        c = lax.div(i, 2)
        at = lax.rem(i, 2)
        for q in range(slots // 2):
            low, high = side_by_side(rows_in[at, 2 * q, c], rows_in[at, 2 * q + 1, c])
            left[slot, :run, q * LANES : (q + 1) * LANES] = low
            left[slot, run:, q * LANES : (q + 1) * LANES] = high

    def write(i):
        start = pl.multiple_of(lax.rem(i, 2) * 2 * run, 2 * run)
        slot = lax.rem(i, 2)
        return pltpu.make_async_copy(
            done.at[slot],
            out_ref.at[lax.div(i, 2), :, pl.ds(start, 2 * run), :],
            out_sem.at[slot],
        )

    assemble(0, 0)

    @pl.loop(0, 6)
    def _(i):
        slot = lax.rem(i, 2)

        @pl.when(i >= 2)
        def _():
            write(i - 2).wait()

        assemble(jnp.minimum(i + 1, 5), 1 - slot)
        for d in range(3):
            done[slot, d] = scale * lax.dot_general(
                left[slot],
                right[d],
                (((1,), (1,)), ((), ())),
                preferred_element_type=jnp.float32,
            )
        write(i).start()

    write(4).wait()
    write(5).wait()


def project(flat, eigvecs, me_a, atom_axis):
    proj = jnp.einsum("cfa,cak->fk", flat, eigvecs, preferred_element_type=jnp.float32)
    width = proj.shape[1] // atom_axis

    def share(to):
        return lax.dynamic_slice_in_dim(proj, to * width, width, axis=1)

    total = share(me_a)
    for d in range(1, atom_axis):
        total = total + lax.ppermute(
            share(lax.bitwise_xor(me_a, jnp.int32(d))),
            "atoms",
            [(a, a ^ d) for a in range(atom_axis)],
        )
    return total


def ring_order(count):
    return list(range(0, count, 2)) + list(range(1, count, 2))[::-1]


def long_axis_covariance(flat, half, role, block, spread_pairs, scale):
    rows = lax.all_gather(flat, "frames", axis=1, tiled=True)
    cut = lax.dynamic_slice_in_dim(rows, half * block, block, axis=2)
    cols = jnp.where(role == 0, cut, jnp.zeros_like(cut))
    for d, pairs in enumerate(spread_pairs):
        sent = lax.ppermute(cut, ("frames", "atoms"), pairs)
        cols = jnp.where(role == d + 1, sent, cols)
    return scale * jnp.einsum(
        "cfp,dfq->cpdq", rows, cols, preferred_element_type=jnp.float32
    )


def per_device(frames, mean_structure, eigvecs):
    local_frames, _, local_atoms = frames.shape
    frame_axis = lax.axis_size("frames")
    atom_axis = lax.axis_size("atoms")
    total_frames = local_frames * frame_axis
    block = local_atoms * atom_axis // frame_axis
    blocks = frame_axis // atom_axis
    me_f = lax.axis_index("frames")
    me_a = lax.axis_index("atoms")
    half = lax.rem(me_f, blocks).astype(jnp.int32).reshape(1)
    owner = lax.div(me_f, blocks)
    role = lax.bitwise_xor(me_a, owner).astype(jnp.int32).reshape(1)
    x = jnp.transpose(frames, (1, 0, 2))
    x_copy = [
        pltpu.VMEM(x.shape, jnp.float32),
        pltpu.VMEM(mean_structure.shape, jnp.float32),
    ]

    stats = pl.pallas_call(
        stats_kernel,
        out_shape=jax.ShapeDtypeStruct((STATS, local_frames), jnp.float32),
        in_specs=[HBM, HBM],
        out_specs=VMEM,
        scratch_shapes=x_copy + [pltpu.SemaphoreType.DMA((2,))],
        compiler_params=params(8),
        name="local_moments",
    )(x, mean_structure)
    others = [
        lax.ppermute(stats, "atoms", [(a, a ^ d) for a in range(atom_axis)])
        for d in range(1, atom_axis)
    ]
    run = local_atoms // 4
    piece = jax.ShapeDtypeStruct((3, run, 2 * local_frames), jnp.bfloat16)
    first, second, flat = pl.pallas_call(
        functools.partial(align_kernel, atom_axis, local_atoms * atom_axis),
        out_shape=(piece, piece, jax.ShapeDtypeStruct(x.shape, jnp.bfloat16)),
        in_specs=[VMEM] * atom_axis + [HBM, HBM],
        out_specs=(VMEM, VMEM, VMEM),
        scratch_shapes=x_copy
        + [pltpu.VMEM((LANES, LANES), jnp.float32), pltpu.SemaphoreType.DMA((2,))],
        compiler_params=params(8),
        name="polar_align",
    )(stats, *others, x, mean_structure)
    projections = project(flat, eigvecs, me_a, atom_axis)

    def pairs(source, target):
        return [
            (
                f * atom_axis + ((f // blocks) ^ source),
                f * atom_axis + ((f // blocks) ^ target),
            )
            for f in range(frame_axis)
        ]

    if blocks != 2 or frame_axis != 8:
        spread_pairs = [pairs(0, d) for d in range(1, atom_axis)]
        covariance = long_axis_covariance(
            flat, half[0], role[0], block, spread_pairs, 1.0 / total_frames
        )
        return covariance, projections

    def spread(pieces):
        cut = pl.pallas_call(
            functools.partial(cut_kernel, len(pieces)),
            out_shape=jax.ShapeDtypeStruct((len(pieces) // 2,) + piece.shape, jnp.bfloat16),
            in_specs=[SMEM] + [ANY] * len(pieces),
            out_specs=ANY,
            scratch_shapes=[pltpu.SemaphoreType.DMA((len(pieces) // 2,))],
            compiler_params=params(8),
            name="cut_columns",
        )(half, *pieces)
        axes = ("frames", "atoms")
        across = lax.ppermute(cut, axes, pairs(0, 2))
        beside = lax.ppermute(cut, axes, pairs(0, 1))
        last = lax.ppermute(across, axes, pairs(2, 3))
        return [cut, beside, across, last]

    order = ring_order(frame_axis)
    forward = [(order[i], order[(i + 1) % frame_axis]) for i in range(frame_axis)]
    backward = [(b, a) for a, b in forward]

    def hop(arrays, way):
        return [lax.ppermute(a, "frames", way) for a in arrays]

    own = [first, second]
    up, down = own, own
    ups, downs = [], []
    for _ in range(1, frame_axis // 2):
        up, down = hop(up, forward), hop(down, backward)
        ups.append(up)
        downs.append(down)
    far = hop(up[:1], forward) + hop(down[1:], backward)
    lots = [own + ups[0] + downs[0] + ups[1] + downs[1], ups[2] + downs[2], far]
    cuts = sum([spread(lot) for lot in lots], [])
    pieces = sum(lots, [])
    counts = [len(lot) // 2 for lot in lots]
    covariance = pl.pallas_call(
        functools.partial(
            covariance_kernel, frame_axis, atom_axis, counts, 1.0 / total_frames
        ),
        out_shape=jax.ShapeDtypeStruct((3, 3, local_atoms, block), jnp.float32),
        in_specs=[SMEM] + [ANY] * (len(pieces) + len(cuts)),
        out_specs=ANY,
        scratch_shapes=[
            pltpu.VMEM((2, frame_axis) + piece.shape, jnp.bfloat16),
            pltpu.VMEM((frame_axis,) + piece.shape, jnp.bfloat16),
            pltpu.VMEM((2, 2 * run, total_frames), jnp.bfloat16),
            pltpu.VMEM((3, block, total_frames), jnp.bfloat16),
            pltpu.VMEM((2, 3, 2 * run, block), jnp.float32),
            pltpu.SemaphoreType.DMA((len(pieces) + len(lots),)),
            pltpu.SemaphoreType.DMA((2,)),
        ],
        compiler_params=params(24),
        cost_estimate=pl.CostEstimate(
            flops=18 * local_atoms * block * total_frames,
            bytes_accessed=24 * MIB,
            transcendentals=0,
        ),
        name="covariance_tile",
    )(role, *pieces, *cuts)
    return jnp.transpose(covariance, (0, 2, 1, 3)), projections


def solution(mesh):
    placed = (P("frames", None, "atoms"), P(None, "atoms"), P(None, "atoms", None))
    return jax.shard_map(
        per_device,
        mesh=mesh,
        in_specs=placed,
        out_specs=(P(None, "atoms", None, "frames"), P("frames", "atoms")),
        check_vma=False,
    )
```

time: 129 us -> 111 us (0.86)
  the two profiles are of different devices: /device:TPU:0 before, /device:TPU:9 now
where the time goes in v3:
time: 111 us; the launch traced here: 110 us
  starting transfers between devices  39 us (35%)
  Pallas kernels  25.1 us (23%)
  waiting for transfers between devices  24.1 us (22%)
  local copies, waits for them, and re-layouts  19 us (17%)
  other arithmetic  1.51 us (1%)
    unnamed x62, local copies, waits for them, and re-layouts  18.9 us
    ppermute x14, waiting for transfers between devices, hop(): return [lax.ppermute(a, 'frames', way) for a in arrays]  15.2 us
    pallas_call x1, Pallas kernels, per_device(): pl.pallas_call(functools.partial(covariance_kernel, frame_axis, atom_axis...  14.6 us
    ppermute x3, starting transfers between devices, spread(): beside = lax.ppermute(cut, axes, pairs(0, 1))  12.8 us
    ppermute x14, starting transfers between devices, hop(): return [lax.ppermute(a, 'frames', way) for a in arrays]  10.3 us
    ppermute x3, starting transfers between devices, spread(): across = lax.ppermute(cut, axes, pairs(0, 2))  9.37 us
    pallas_call x3, Pallas kernels, spread(): pl.pallas_call(functools.partial(cut_kernel, len(pieces)), out_shape=jax....  9.35 us
    ppermute x3, waiting for transfers between devices, project(): lax.ppermute(share(lax.bitwise_xor(me_a, jnp.int32(d))), 'atoms', [(a, a...  6.82 us
  transfers between devices with their start and end apart: 29, of which 11 were waited for; matrix products, arithmetic and copies ran while one was open for 2% of the time, Pallas kernels for 7%

profile of v3, /device:TPU:9, one launch (start us, length us, event | category | flops | bytes accessed | tf_op | source)
XLA Modules:
  0.0 110.0 jit_solution(1205530408950356212)
XLA Ops:
  0.7 1.2 %copy-done.1 = f32[64,3,1024]{2,0,1:T(8,128)S(1)} copy-done((f32[64,3,1024]{2,0,1:T(8,128)S(1)}, f32[64,3,1024]{2,0,1:T(8,128)}, u32[]{:S(2)}) %copy-start.1) | copy-done | bytes 786456
  1.9 0.7 copy-done.25
  2.6 0.6 local_moments.1.refs_0_
  3.2 1.8 %collective-permute-start.2 = (f32[24,64]{1,0:T(8,128)S(1)}, f32[24,64]{1,0:T(8,128)S(1)}, u32[]{:S(2)}, u32[]{:S(2)}) collective-permute-start(f32[24,64]{1,0:T(8,128)S(1)} %local_moments.1.refs_0_), channel_id=1, source_target_pairs={{0,3},{1,2},{2,1},{3,0},{4,7},{5,6},{6,5},{7,4},{8,11},{9,10},{10,... | collective-permute-start | bytes 18440 | tf_op jit(solution)/shard_map/ppermute | solution.py:286
  5.0 0.3 collective-permute-start.1
  5.3 0.2 collective-permute-start
  5.5 1.2 %collective-permute-done.2.refs_3_ = f32[24,64]{1,0:T(8,128)S(1)} collective-permute-done((f32[24,64]{1,0:T(8,128)S(1)}, f32[24,64]{1,0:T(8,128)S(1)}, u32[]{:S(2)}, u32[]{:S(2)}) %collective-permute-start.2) | collective-permute-done | bytes 6176 | tf_op jit(solution)/shard_map/ppermute | solution.py:286
  6.7 0.8 collective-permute-done.1.refs_2_
  7.6 0.7 copy-done.26
  8.3 0.7 polar_align.1
  9.0 0.7 copy-done.21
  9.7 0.2 collective-permute-start.5
  9.9 1.3 %collective-permute-start.3 = (bf16[3,256,128]{2,1,0:T(8,128)(2,1)S(1)}, bf16[3,256,128]{2,1,0:T(8,128)(2,1)S(1)}, u32[]{:S(2)}, u32[]{:S(2)}) collective-permute-start(bf16[3,256,128]{2,1,0:T(8,128)(2,1)S(1)} %get-tuple-element.5.refs_0_.refs_1_), channel_id=1, source_target_pairs={{0,8},{8,16},{16,24},{24,28},{28,20},{20,12},{12,4},{4,0},{1,9},{9... | collective-permute-start | bytes 589832 | tf_op jit(solution)/shard_map/ppermute | solution.py:340
  11.2 0.2 collective-permute-start.6
  11.4 1.3 %collective-permute-start.4 = (bf16[3,256,128]{2,1,0:T(8,128)(2,1)S(1)}, bf16[3,256,128]{2,1,0:T(8,128)(2,1)S(1)}, u32[]{:S(2)}, u32[]{:S(2)}) collective-permute-start(bf16[3,256,128]{2,1,0:T(8,128)(2,1)S(1)} %get-tuple-element.6.refs_1_.refs_2_), channel_id=1, source_target_pairs={{0,8},{8,16},{16,24},{24,28},{28,20},{20,12},{12,4},{4,0},{1,9},{9... | collective-permute-start | bytes 589832 | tf_op jit(solution)/shard_map/ppermute | solution.py:340
  12.7 2.5 %collective-permute-done.5.refs_4_.refs_5_ = bf16[3,256,128]{2,1,0:T(8,128)(2,1)S(1)} collective-permute-done((bf16[3,256,128]{2,1,0:T(8,128)(2,1)S(1)}, bf16[3,256,128]{2,1,0:T(8,128)(2,1)S(1)}, u32[]{:S(2)}, u32[]{:S(2)}) %collective-permute-start.5) | collective-permute-done | bytes 196640 | tf_op jit(solution)/shard_map/ppermute | solution.py:340
  15.1 0.2 collective-permute-start.9
  15.3 1.3 %collective-permute-start.7 = (bf16[3,256,128]{2,1,0:T(8,128)(2,1)S(1)}, bf16[3,256,128]{2,1,0:T(8,128)(2,1)S(1)}, u32[]{:S(2)}, u32[]{:S(2)}) collective-permute-start(bf16[3,256,128]{2,1,0:T(8,128)(2,1)S(1)} %collective-permute-done.3.refs_2_.refs_3_), channel_id=1, source_target_pairs={{0,8},{8,16},{16,24},{24,28},{28,20},{20,12},{12,4},{4,0},{1,9},{9... | collective-permute-start | bytes 589832 | tf_op jit(solution)/shard_map/ppermute | solution.py:340
  16.6 2.7 %collective-permute-done.6.refs_5_.refs_6_ = bf16[3,256,128]{2,1,0:T(8,128)(2,1)S(1)} collective-permute-done((bf16[3,256,128]{2,1,0:T(8,128)(2,1)S(1)}, bf16[3,256,128]{2,1,0:T(8,128)(2,1)S(1)}, u32[]{:S(2)}, u32[]{:S(2)}) %collective-permute-start.6) | collective-permute-done | bytes 196640 | tf_op jit(solution)/shard_map/ppermute | solution.py:340
  19.5 1.3 %collective-permute-start.8 = (bf16[3,256,128]{2,1,0:T(8,128)(2,1)S(1)}, bf16[3,256,128]{2,1,0:T(8,128)(2,1)}, u32[]{:S(2)}, u32[]{:S(2)}) collective-permute-start(bf16[3,256,128]{2,1,0:T(8,128)(2,1)S(1)} %collective-permute-done.4.refs_3_.refs_4_), channel_id=1, source_target_pairs={{0,8},{8,16},{16,24},{24,28},{28,20},{20,12},{12,4},{4,0},{1,9},{9... | collective-permute-start | bytes 589832 | tf_op jit(solution)/shard_map/ppermute | solution.py:340
  20.8 0.7 copy-done.6
  21.5 2.0 %collective-permute-done.9.refs_8_.refs_9_ = bf16[3,256,128]{2,1,0:T(8,128)(2,1)S(1)} collective-permute-done((bf16[3,256,128]{2,1,0:T(8,128)(2,1)S(1)}, bf16[3,256,128]{2,1,0:T(8,128)(2,1)S(1)}, u32[]{:S(2)}, u32[]{:S(2)}) %collective-permute-start.9) | collective-permute-done | bytes 196640 | tf_op jit(solution)/shard_map/ppermute | solution.py:340
  23.6 0.7 copy-done.9
  24.3 0.7 copy-done.12
  24.9 2.9 %collective-permute-done.10.refs_9_.refs_10_ = bf16[3,256,128]{2,1,0:T(8,128)(2,1)S(1)} collective-permute-done((bf16[3,256,128]{2,1,0:T(8,128)(2,1)S(1)}, bf16[3,256,128]{2,1,0:T(8,128)(2,1)S(1)}, u32[]{:S(2)}, u32[]{:S(2)}) %collective-permute-start.10) | collective-permute-done | bytes 196640 | tf_op jit(solution)/shard_map/ppermute | solution.py:340
  27.9 0.7 copy-done.15
  28.6 0.9 copy-done.7
  29.5 0.9 copy-done.10
  30.4 0.9 copy-done.13
  31.3 0.9 copy-done.16
  32.3 1.3 %cut_columns.3.refs_17_ = bf16[5,3,256,128]{3,2,1,0:T(8,128)(2,1)S(1)} custom-call(s32[1]{0:T(128)} %bitcast.2.half_ref, bf16[3,256,128]{2,1,0:T(8,128)(2,1)S(1)} %get-tuple-element.5.refs_0_.refs_1_, bf16[3,256,128]{2,1,0:T(8,128)(2,1)S(1)} %get-tuple-element.6.refs_1_.refs_2_, bf16[3,256,128]{2,1,0:T(8,128)(2,1)S(1)} %collective-permute-done.3.refs_2_.refs_3_, ...), custom_call_target="tpu_custom_call" | custom-call | tf_op jit(solution)/shard_map/cut_columns/pallas_call | solution.py:320
  33.6 3.4 %collective-permute-start.18 = (bf16[5,3,256,128]{3,2,1,0:T(8,128)(2,1)S(1)}, bf16[5,3,256,128]{3,2,1,0:T(8,128)(2,1)}, u32[]{:S(2)}, u32[]{:S(2)}) collective-permute-start(bf16[5,3,256,128]{3,2,1,0:T(8,128)(2,1)S(1)} %cut_columns.3.refs_17_), channel_id=1, source_target_pairs={{0,2},{4,6},{9,11},{13,15},{18,16},{22,20},{27,25},{31,29}} | collective-permute-start | bytes 2949128 | tf_op jit(solution)/shard_map/ppermute | solution.py:330
  36.9 1.5 %collective-permute-start.14 = (bf16[3,256,128]{2,1,0:T(8,128)(2,1)S(1)}, bf16[3,256,128]{2,1,0:T(8,128)(2,1)}, u32[]{:S(2)}, u32[]{:S(2)}) collective-permute-start(bf16[3,256,128]{2,1,0:T(8,128)(2,1)S(1)} %copy-done.16), channel_id=1, source_target_pairs={{8,0},{16,8},{24,16},{28,24},{20,28},{12,20},{4,12},{0,4},{9,1},{1... | collective-permute-start | bytes 589832 | tf_op jit(solution)/shard_map/ppermute | solution.py:340
  38.5 1.4 %collective-permute-start.12 = (bf16[3,256,128]{2,1,0:T(8,128)(2,1)}, bf16[3,256,128]{2,1,0:T(8,128)(2,1)}, u32[]{:S(2)}, u32[]{:S(2)}) collective-permute-start(bf16[3,256,128]{2,1,0:T(8,128)(2,1)} %collective-permute-done.8.refs_7_.refs_8_), channel_id=1, source_target_pairs={{0,8},{8,16},{16,24},{24,28},{28,20},{20,12},{12,4},{4,0},{1,9},{9... | collective-permute-start | bytes 589832 | tf_op jit(solution)/shard_map/ppermute | solution.py:340
  39.9 2.5 %collective-permute-done.11.refs_0_.refs_11_ = bf16[3,256,128]{2,1,0:T(8,128)(2,1)} collective-permute-done((bf16[3,256,128]{2,1,0:T(8,128)(2,1)S(1)}, bf16[3,256,128]{2,1,0:T(8,128)(2,1)}, u32[]{:S(2)}, u32[]{:S(2)}) %collective-permute-start.11) | collective-permute-done | bytes 196640 | tf_op jit(solution)/shard_map/ppermute | solution.py:340
  42.4 1.5 %collective-permute-start.16 = (bf16[3,256,128]{2,1,0:T(8,128)(2,1)}, bf16[3,256,128]{2,1,0:T(8,128)(2,1)}, u32[]{:S(2)}, u32[]{:S(2)}) collective-permute-start(bf16[3,256,128]{2,1,0:T(8,128)(2,1)} %collective-permute-done.14.refs_3_.refs_14_), channel_id=1, source_target_pairs={{8,0},{16,8},{24,16},{28,24},{20,28},{12,20},{4,12},{0,4},{9,1},{1... | collective-permute-start | bytes 589832 | tf_op jit(solution)/shard_map/ppermute | solution.py:340
  43.8 2.5 %collective-permute-done.13.refs_2_.refs_13_ = bf16[3,256,128]{2,1,0:T(8,128)(2,1)S(1)} collective-permute-done((bf16[3,256,128]{2,1,0:T(8,128)(2,1)S(1)}, bf16[3,256,128]{2,1,0:T(8,128)(2,1)S(1)}, u32[]{:S(2)}, u32[]{:S(2)}) %collective-permute-start.13) | collective-permute-done | bytes 196640 | tf_op jit(solution)/shard_map/ppermute | solution.py:340
  46.3 0.7 copy-done.18
  47.0 6.9 %collective-permute-start.17 = (bf16[5,3,256,128]{3,2,1,0:T(8,128)(2,1)S(1)}, bf16[5,3,256,128]{3,2,1,0:T(8,128)(2,1)}, u32[]{:S(2)}, u32[]{:S(2)}) collective-permute-start(bf16[5,3,256,128]{3,2,1,0:T(8,128)(2,1)S(1)} %cut_columns.3.refs_17_), channel_id=1, source_target_pairs={{0,1},{4,5},{9,8},{13,12},{18,19},{22,23},{27,26},{31,30}} | collective-permute-start | bytes 2949128 | tf_op jit(solution)/shard_map/ppermute | solution.py:331
  53.9 1.6 %collective-permute-start.19 = (bf16[5,3,256,128]{3,2,1,0:T(8,128)(2,1)}, bf16[5,3,256,128]{3,2,1,0:T(8,128)(2,1)}, u32[]{:S(2)}, u32[]{:S(2)}) collective-permute-start(bf16[5,3,256,128]{3,2,1,0:T(8,128)(2,1)} %collective-permute-done.18.refs_19_), channel_id=1, source_target_pairs={{2,3},{6,7},{11,10},{15,14},{16,17},{20,21},{25,24},{29,28}} | collective-permute-start | bytes 2949128 | tf_op jit(solution)/shard_map/ppermute | solution.py:332
  55.5 0.9 copy-done.19
  56.4 1.0 cut_columns.4.refs_21_
  57.4 4.7 %collective-permute-start.21 = (bf16[2,3,256,128]{3,2,1,0:T(8,128)(2,1)S(1)}, bf16[2,3,256,128]{3,2,1,0:T(8,128)(2,1)}, u32[]{:S(2)}, u32[]{:S(2)}) collective-permute-start(bf16[2,3,256,128]{3,2,1,0:T(8,128)(2,1)S(1)} %cut_columns.4.refs_21_), channel_id=1, source_target_pairs={{0,2},{4,6},{9,11},{13,15},{18,16},{22,20},{27,25},{31,29}} | collective-permute-start | bytes 1179656 | tf_op jit(solution)/shard_map/ppermute | solution.py:330
  62.1 7.1 %cut_columns.5.refs_25_ = bf16[1,3,256,128]{3,2,1,0:T(8,128)(2,1)} custom-call(s32[1]{0:T(128)} %bitcast.2.half_ref, bf16[3,256,128]{2,1,0:T(8,128)(2,1)} %collective-permute-done.15.refs_0_.refs_15_, bf16[3,256,128]{2,1,0:T(8,128)(2,1)} %collective-permute-done.16.refs_1_.refs_16_), custom_call_target="tpu_custom_call" | custom-call | tf_op jit(solution)/shard_map/cut_columns/pallas_call | solution.py:320
  69.2 1.3 %collective-permute-start.24 = (bf16[1,3,256,128]{3,2,1,0:T(8,128)(2,1)}, bf16[1,3,256,128]{3,2,1,0:T(8,128)(2,1)S(1)}, u32[]{:S(2)}, u32[]{:S(2)}) collective-permute-start(bf16[1,3,256,128]{3,2,1,0:T(8,128)(2,1)} %cut_columns.5.refs_25_), channel_id=1, source_target_pairs={{0,2},{4,6},{9,11},{13,15},{18,16},{22,20},{27,25},{31,29}} | collective-permute-start | bytes 589832 | tf_op jit(solution)/shard_map/ppermute | solution.py:330
  70.5 0.4 convolution_bitcast_fusion
  71.1 1.2 %collective-permute-done.26 = f32[64,64]{1,0:T(8,128)S(1)} collective-permute-done((f32[64,64]{1,0:T(8,128)S(1)}, f32[64,64]{1,0:T(8,128)S(1)}, u32[]{:S(2)}, u32[]{:S(2)}) %collective-permute-start.26) | collective-permute-done | bytes 16416 | tf_op jit(solution)/shard_map/ppermute | solution.py:234
  72.3 3.3 %collective-permute-done.28 = f32[64,64]{1,0:T(8,128)S(1)} collective-permute-done((f32[64,64]{1,0:T(8,128)S(1)}, f32[64,64]{1,0:T(8,128)S(1)}, u32[]{:S(2)}, u32[]{:S(2)}) %collective-permute-start.28) | collective-permute-done | bytes 16416 | tf_op jit(solution)/shard_map/ppermute | solution.py:234
  75.7 0.5 collective-permute-start.27
  76.1 2.3 %collective-permute-done.27 = f32[64,64]{1,0:T(8,128)S(1)} collective-permute-done((f32[64,64]{1,0:T(8,128)S(1)}, f32[64,64]{1,0:T(8,128)S(1)}, u32[]{:S(2)}, u32[]{:S(2)}) %collective-permute-start.27) | collective-permute-done | bytes 16416 | tf_op jit(solution)/shard_map/ppermute | solution.py:234
  78.4 3.9 %collective-permute-start.23 = (bf16[1,3,256,128]{3,2,1,0:T(8,128)(2,1)}, bf16[1,3,256,128]{3,2,1,0:T(8,128)(2,1)}, u32[]{:S(2)}, u32[]{:S(2)}) collective-permute-start(bf16[1,3,256,128]{3,2,1,0:T(8,128)(2,1)} %cut_columns.5.refs_25_), channel_id=1, source_target_pairs={{0,1},{4,5},{9,8},{13,12},{18,19},{22,23},{27,26},{31,30}} | collective-permute-start | bytes 589832 | tf_op jit(solution)/shard_map/ppermute | solution.py:331
  82.3 2.0 %collective-permute-start.20 = (bf16[2,3,256,128]{3,2,1,0:T(8,128)(2,1)S(1)}, bf16[2,3,256,128]{3,2,1,0:T(8,128)(2,1)}, u32[]{:S(2)}, u32[]{:S(2)}) collective-permute-start(bf16[2,3,256,128]{3,2,1,0:T(8,128)(2,1)S(1)} %cut_columns.4.refs_21_), channel_id=1, source_target_pairs={{0,1},{4,5},{9,8},{13,12},{18,19},{22,23},{27,26},{31,30}} | collective-permute-start | bytes 1179656 | tf_op jit(solution)/shard_map/ppermute | solution.py:331
  84.4 1.4 %collective-permute-start.22 = (bf16[2,3,256,128]{3,2,1,0:T(8,128)(2,1)}, bf16[2,3,256,128]{3,2,1,0:T(8,128)(2,1)}, u32[]{:S(2)}, u32[]{:S(2)}) collective-permute-start(bf16[2,3,256,128]{3,2,1,0:T(8,128)(2,1)} %collective-permute-done.21.refs_23_), channel_id=1, source_target_pairs={{2,3},{6,7},{11,10},{15,14},{16,17},{20,21},{25,24},{29,28}} | collective-permute-start | bytes 1179656 | tf_op jit(solution)/shard_map/ppermute | solution.py:332
  85.8 0.7 collective-permute-start.25
  86.5 1.5 %add_add_fusion = f32[64,64]{1,0:T(8,128)} fusion(f32[64,64]{1,0:T(8,128)} %copy-done.29, f32[64,64]{1,0:T(8,128)} %copy-done.30, f32[64,64]{1,0:T(8,128)} %copy-done.28, f32[64,256]{1,0:T(8,128)} %copy-done.27, s32[]{:T(128)S(6)} %select_n.12), kind=kLoop, calls=%fused_computation.1 | loop fusion | flops 12288 | bytes 81924 | tf_op jit(solution)/shard_map/add | solution.py:234
  88.0 0.9 copy-done.3
  89.0 0.9 copy-done.5
  89.9 0.9 copy-done.8
  90.8 0.9 copy-done.11
  91.7 0.9 copy-done.14
  92.7 0.9 copy-done.17
  93.6 0.9 copy-done.20
  94.5 0.9 copy-done.24
  95.4 14.6 %covariance_tile.1 = f32[3,3,1024,512]{3,2,1,0:T(8,128)} custom-call(s32[1]{0:T(128)} %bitcast.refs_0_, bf16[3,256,128]{2,1,0:T(8,128)(2,1)S(1)} %get-tuple-element.5.refs_0_.refs_1_, bf16[3,256,128]{2,1,0:T(8,128)(2,1)S(1)} %get-tuple-element.6.refs_1_.refs_2_, bf16[3,256,128]{2,1,0:T(8,128)(2,1)S(1)} %copy-done.3, bf16[3,256,128]{2,1,0:T(8,128)(2,1)S(1)} %copy-done.8, ...), custom_call_target="tpu_custom_call" | custom-call | flops 4831838208 | bytes 25165824 | tf_op jit(solution)/shard_map/covariance_tile/pallas_call | solution.py:354
  (65 shorter events, 0.5 us)
Async XLA Ops:
  0.6 69.9 %copy-start = (bf16[3,1024,256]{2,1,0:T(8,128)(2,1)S(1)}, bf16[3,1024,256]{2,1,0:T(8,128)(2,1)}, u32[]{:S(2)}) copy-start(bf16[3,1024,256]{2,1,0:T(8,128)(2,1)} %param.5) | copy-start | bytes 4718596
  0.6 1.3 %copy-start.1 = (f32[64,3,1024]{2,0,1:T(8,128)S(1)}, f32[64,3,1024]{2,0,1:T(8,128)}, u32[]{:S(2)}) copy-start(f32[64,3,1024]{2,0,1:T(8,128)} %param.3) | copy-start | bytes 2359300
  1.9 0.7 copy-start.25
  3.2 3.5 %collective-permute-start.2 = (f32[24,64]{1,0:T(8,128)S(1)}, f32[24,64]{1,0:T(8,128)S(1)}, u32[]{:S(2)}, u32[]{:S(2)}) collective-permute-start(f32[24,64]{1,0:T(8,128)S(1)} %local_moments.1.refs_0_), channel_id=1, source_target_pairs={{0,3},{1,2},{2,1},{3,0},{4,7},{5,6},{6,5},{7,4},{8,11},{9,10},{10,... | collective-permute-start | bytes 18440 | tf_op jit(solution)/shard_map/ppermute | solution.py:286
  5.0 2.5 %collective-permute-start.1 = (f32[24,64]{1,0:T(8,128)S(1)}, f32[24,64]{1,0:T(8,128)S(1)}, u32[]{:S(2)}, u32[]{:S(2)}) collective-permute-start(f32[24,64]{1,0:T(8,128)S(1)} %local_moments.1.refs_0_), channel_id=1, source_target_pairs={{0,2},{1,3},{2,0},{3,1},{4,6},{5,7},{6,4},{7,5},{8,10},{9,11},{10,... | collective-permute-start | bytes 18440 | tf_op jit(solution)/shard_map/ppermute | solution.py:286
  5.3 2.3 %collective-permute-start = (f32[24,64]{1,0:T(8,128)S(1)}, f32[24,64]{1,0:T(8,128)S(1)}, u32[]{:S(2)}, u32[]{:S(2)}) collective-permute-start(f32[24,64]{1,0:T(8,128)S(1)} %local_moments.1.refs_0_), channel_id=1, source_target_pairs={{0,1},{1,0},{2,3},{3,2},{4,5},{5,4},{6,7},{7,6},{8,9},{9,8},{10,11... | collective-permute-start | bytes 18440 | tf_op jit(solution)/shard_map/ppermute | solution.py:286
  7.6 0.7 copy-start.26
  9.0 0.7 copy-start.21
  9.7 5.4 %collective-permute-start.5 = (bf16[3,256,128]{2,1,0:T(8,128)(2,1)S(1)}, bf16[3,256,128]{2,1,0:T(8,128)(2,1)S(1)}, u32[]{:S(2)}, u32[]{:S(2)}) collective-permute-start(bf16[3,256,128]{2,1,0:T(8,128)(2,1)S(1)} %get-tuple-element.5.refs_0_.refs_1_), channel_id=1, source_target_pairs={{8,0},{16,8},{24,16},{28,24},{20,28},{12,20},{4,12},{0,4},{9,1},{1... | collective-permute-start | bytes 589832 | tf_op jit(solution)/shard_map/ppermute | solution.py:340
  9.9 5.4 %collective-permute-start.3 = (bf16[3,256,128]{2,1,0:T(8,128)(2,1)S(1)}, bf16[3,256,128]{2,1,0:T(8,128)(2,1)S(1)}, u32[]{:S(2)}, u32[]{:S(2)}) collective-permute-start(bf16[3,256,128]{2,1,0:T(8,128)(2,1)S(1)} %get-tuple-element.5.refs_0_.refs_1_), channel_id=1, source_target_pairs={{0,8},{8,16},{16,24},{24,28},{28,20},{20,12},{12,4},{4,0},{1,9},{9... | collective-permute-start | bytes 589832 | tf_op jit(solution)/shard_map/ppermute | solution.py:340
  11.2 8.2 %collective-permute-start.6 = (bf16[3,256,128]{2,1,0:T(8,128)(2,1)S(1)}, bf16[3,256,128]{2,1,0:T(8,128)(2,1)S(1)}, u32[]{:S(2)}, u32[]{:S(2)}) collective-permute-start(bf16[3,256,128]{2,1,0:T(8,128)(2,1)S(1)} %get-tuple-element.6.refs_1_.refs_2_), channel_id=1, source_target_pairs={{8,0},{16,8},{24,16},{28,24},{20,28},{12,20},{4,12},{0,4},{9,1},{1... | collective-permute-start | bytes 589832 | tf_op jit(solution)/shard_map/ppermute | solution.py:340
  11.4 8.2 %collective-permute-start.4 = (bf16[3,256,128]{2,1,0:T(8,128)(2,1)S(1)}, bf16[3,256,128]{2,1,0:T(8,128)(2,1)S(1)}, u32[]{:S(2)}, u32[]{:S(2)}) collective-permute-start(bf16[3,256,128]{2,1,0:T(8,128)(2,1)S(1)} %get-tuple-element.6.refs_1_.refs_2_), channel_id=1, source_target_pairs={{0,8},{8,16},{16,24},{24,28},{28,20},{20,12},{12,4},{4,0},{1,9},{9... | collective-permute-start | bytes 589832 | tf_op jit(solution)/shard_map/ppermute | solution.py:340
  15.1 8.4 %collective-permute-start.9 = (bf16[3,256,128]{2,1,0:T(8,128)(2,1)S(1)}, bf16[3,256,128]{2,1,0:T(8,128)(2,1)S(1)}, u32[]{:S(2)}, u32[]{:S(2)}) collective-permute-start(bf16[3,256,128]{2,1,0:T(8,128)(2,1)S(1)} %collective-permute-done.5.refs_4_.refs_5_), channel_id=1, source_target_pairs={{8,0},{16,8},{24,16},{28,24},{20,28},{12,20},{4,12},{0,4},{9,1},{1... | collective-permute-start | bytes 589832 | tf_op jit(solution)/shard_map/ppermute | solution.py:340
  15.3 40.2 %copy-start.2 = (bf16[3,256,128]{2,1,0:T(8,128)(2,1)}, bf16[3,256,128]{2,1,0:T(8,128)(2,1)S(1)}, u32[]{:S(2)}) copy-start(bf16[3,256,128]{2,1,0:T(8,128)(2,1)S(1)} %collective-permute-done.3.refs_2_.refs_3_) | copy-start | bytes 589828
  15.3 8.9 %collective-permute-start.7 = (bf16[3,256,128]{2,1,0:T(8,128)(2,1)S(1)}, bf16[3,256,128]{2,1,0:T(8,128)(2,1)S(1)}, u32[]{:S(2)}, u32[]{:S(2)}) collective-permute-start(bf16[3,256,128]{2,1,0:T(8,128)(2,1)S(1)} %collective-permute-done.3.refs_2_.refs_3_), channel_id=1, source_target_pairs={{0,8},{8,16},{16,24},{24,28},{28,20},{20,12},{12,4},{4,0},{1,9},{9... | collective-permute-start | bytes 589832 | tf_op jit(solution)/shard_map/ppermute | solution.py:340
  19.3 36.1 %copy-start.4 = (bf16[3,256,128]{2,1,0:T(8,128)(2,1)}, bf16[3,256,128]{2,1,0:T(8,128)(2,1)S(1)}, u32[]{:S(2)}) copy-start(bf16[3,256,128]{2,1,0:T(8,128)(2,1)S(1)} %collective-permute-done.6.refs_5_.refs_6_) | copy-start | bytes 589828
  19.3 8.5 %collective-permute-start.10 = (bf16[3,256,128]{2,1,0:T(8,128)(2,1)S(1)}, bf16[3,256,128]{2,1,0:T(8,128)(2,1)S(1)}, u32[]{:S(2)}, u32[]{:S(2)}) collective-permute-start(bf16[3,256,128]{2,1,0:T(8,128)(2,1)S(1)} %collective-permute-done.6.refs_5_.refs_6_), channel_id=1, source_target_pairs={{8,0},{16,8},{24,16},{28,24},{20,28},{12,20},{4,12},{0,4},{9,1},{1... | collective-permute-start | bytes 589832 | tf_op jit(solution)/shard_map/ppermute | solution.py:340
  19.5 9.0 %collective-permute-start.8 = (bf16[3,256,128]{2,1,0:T(8,128)(2,1)S(1)}, bf16[3,256,128]{2,1,0:T(8,128)(2,1)}, u32[]{:S(2)}, u32[]{:S(2)}) collective-permute-start(bf16[3,256,128]{2,1,0:T(8,128)(2,1)S(1)} %collective-permute-done.4.refs_3_.refs_4_), channel_id=1, source_target_pairs={{0,8},{8,16},{16,24},{24,28},{28,20},{20,12},{12,4},{4,0},{1,9},{9... | collective-permute-start | bytes 589832 | tf_op jit(solution)/shard_map/ppermute | solution.py:340
  20.8 0.7 copy-start.6
  23.6 0.7 copy-start.9
  24.2 0.7 copy-start.12
  27.9 0.7 copy-start.15
  28.6 0.9 copy-start.7
  29.5 0.9 copy-start.10
  30.4 0.9 copy-start.13
  31.3 0.9 copy-start.16
  33.6 20.3 %collective-permute-start.18 = (bf16[5,3,256,128]{3,2,1,0:T(8,128)(2,1)S(1)}, bf16[5,3,256,128]{3,2,1,0:T(8,128)(2,1)}, u32[]{:S(2)}, u32[]{:S(2)}) collective-permute-start(bf16[5,3,256,128]{3,2,1,0:T(8,128)(2,1)S(1)} %cut_columns.3.refs_17_), channel_id=1, source_target_pairs={{0,2},{4,6},{9,11},{13,15},{18,16},{22,20},{27,25},{31,29}} | collective-permute-start | bytes 2949128 | tf_op jit(solution)/shard_map/ppermute | solution.py:330
  36.9 5.4 %collective-permute-start.11 = (bf16[3,256,128]{2,1,0:T(8,128)(2,1)S(1)}, bf16[3,256,128]{2,1,0:T(8,128)(2,1)}, u32[]{:S(2)}, u32[]{:S(2)}) collective-permute-start(bf16[3,256,128]{2,1,0:T(8,128)(2,1)S(1)} %copy-done.13), channel_id=1, source_target_pairs={{0,8},{8,16},{16,24},{24,28},{28,20},{20,12},{12,4},{4,0},{1,9},{9... | collective-permute-start | bytes 589832 | tf_op jit(solution)/shard_map/ppermute | solution.py:340
  36.9 5.4 %collective-permute-start.14 = (bf16[3,256,128]{2,1,0:T(8,128)(2,1)S(1)}, bf16[3,256,128]{2,1,0:T(8,128)(2,1)}, u32[]{:S(2)}, u32[]{:S(2)}) collective-permute-start(bf16[3,256,128]{2,1,0:T(8,128)(2,1)S(1)} %copy-done.16), channel_id=1, source_target_pairs={{8,0},{16,8},{24,16},{28,24},{20,28},{12,20},{4,12},{0,4},{9,1},{1... | collective-permute-start | bytes 589832 | tf_op jit(solution)/shard_map/ppermute | solution.py:340
  38.4 7.9 %collective-permute-start.13 = (bf16[3,256,128]{2,1,0:T(8,128)(2,1)S(1)}, bf16[3,256,128]{2,1,0:T(8,128)(2,1)S(1)}, u32[]{:S(2)}, u32[]{:S(2)}) collective-permute-start(bf16[3,256,128]{2,1,0:T(8,128)(2,1)S(1)} %copy-done.10), channel_id=1, source_target_pairs={{8,0},{16,8},{24,16},{28,24},{20,28},{12,20},{4,12},{0,4},{9,1},{1... | collective-permute-start | bytes 589832 | tf_op jit(solution)/shard_map/ppermute | solution.py:340
  38.5 17.0 %collective-permute-start.12 = (bf16[3,256,128]{2,1,0:T(8,128)(2,1)}, bf16[3,256,128]{2,1,0:T(8,128)(2,1)}, u32[]{:S(2)}, u32[]{:S(2)}) collective-permute-start(bf16[3,256,128]{2,1,0:T(8,128)(2,1)} %collective-permute-done.8.refs_7_.refs_8_), channel_id=1, source_target_pairs={{0,8},{8,16},{16,24},{24,28},{28,20},{20,12},{12,4},{4,0},{1,9},{9... | collective-permute-start | bytes 589832 | tf_op jit(solution)/shard_map/ppermute | solution.py:340
  42.4 19.8 %collective-permute-start.15 = (bf16[3,256,128]{2,1,0:T(8,128)(2,1)}, bf16[3,256,128]{2,1,0:T(8,128)(2,1)}, u32[]{:S(2)}, u32[]{:S(2)}) collective-permute-start(bf16[3,256,128]{2,1,0:T(8,128)(2,1)} %collective-permute-done.11.refs_0_.refs_11_), channel_id=1, source_target_pairs={{0,8},{8,16},{16,24},{24,28},{28,20},{20,12},{12,4},{4,0},{1,9},{9... | collective-permute-start | bytes 589832 | tf_op jit(solution)/shard_map/ppermute | solution.py:340
  42.4 19.8 %collective-permute-start.16 = (bf16[3,256,128]{2,1,0:T(8,128)(2,1)}, bf16[3,256,128]{2,1,0:T(8,128)(2,1)}, u32[]{:S(2)}, u32[]{:S(2)}) collective-permute-start(bf16[3,256,128]{2,1,0:T(8,128)(2,1)} %collective-permute-done.14.refs_3_.refs_14_), channel_id=1, source_target_pairs={{8,0},{16,8},{24,16},{28,24},{20,28},{12,20},{4,12},{0,4},{9,1},{1... | collective-permute-start | bytes 589832 | tf_op jit(solution)/shard_map/ppermute | solution.py:340
  46.3 0.7 copy-start.18
  47.0 41.0 %collective-permute-start.17 = (bf16[5,3,256,128]{3,2,1,0:T(8,128)(2,1)S(1)}, bf16[5,3,256,128]{3,2,1,0:T(8,128)(2,1)}, u32[]{:S(2)}, u32[]{:S(2)}) collective-permute-start(bf16[5,3,256,128]{3,2,1,0:T(8,128)(2,1)S(1)} %cut_columns.3.refs_17_), channel_id=1, source_target_pairs={{0,1},{4,5},{9,8},{13,12},{18,19},{22,23},{27,26},{31,30}} | collective-permute-start | bytes 2949128 | tf_op jit(solution)/shard_map/ppermute | solution.py:331
  53.9 34.1 %collective-permute-start.19 = (bf16[5,3,256,128]{3,2,1,0:T(8,128)(2,1)}, bf16[5,3,256,128]{3,2,1,0:T(8,128)(2,1)}, u32[]{:S(2)}, u32[]{:S(2)}) collective-permute-start(bf16[5,3,256,128]{3,2,1,0:T(8,128)(2,1)} %collective-permute-done.18.refs_19_), channel_id=1, source_target_pairs={{2,3},{6,7},{11,10},{15,14},{16,17},{20,21},{25,24},{29,28}} | collective-permute-start | bytes 2949128 | tf_op jit(solution)/shard_map/ppermute | solution.py:332
  55.5 0.9 copy-start.19
  56.4 14.1 %copy-start.22 = (bf16[3,64,1024]{2,1,0:T(8,128)(2,1)S(1)}, bf16[3,64,1024]{2,1,0:T(8,128)(2,1)}, u32[]{:S(2)}) copy-start(bf16[3,64,1024]{2,1,0:T(8,128)(2,1)} %copy-done.21) | copy-start | bytes 1179652
  57.4 26.9 %collective-permute-start.21 = (bf16[2,3,256,128]{3,2,1,0:T(8,128)(2,1)S(1)}, bf16[2,3,256,128]{3,2,1,0:T(8,128)(2,1)}, u32[]{:S(2)}, u32[]{:S(2)}) collective-permute-start(bf16[2,3,256,128]{3,2,1,0:T(8,128)(2,1)S(1)} %cut_columns.4.refs_21_), channel_id=1, source_target_pairs={{0,2},{4,6},{9,11},{13,15},{18,16},{22,20},{27,25},{31,29}} | collective-permute-start | bytes 1179656 | tf_op jit(solution)/shard_map/ppermute | solution.py:330
  69.2 13.1 %collective-permute-start.24 = (bf16[1,3,256,128]{3,2,1,0:T(8,128)(2,1)}, bf16[1,3,256,128]{3,2,1,0:T(8,128)(2,1)S(1)}, u32[]{:S(2)}, u32[]{:S(2)}) collective-permute-start(bf16[1,3,256,128]{3,2,1,0:T(8,128)(2,1)} %cut_columns.5.refs_25_), channel_id=1, source_target_pairs={{0,2},{4,6},{9,11},{13,15},{18,16},{22,20},{27,25},{31,29}} | collective-permute-start | bytes 589832 | tf_op jit(solution)/shard_map/ppermute | solution.py:330
  70.9 13.4 %copy-start.27 = (f32[64,256]{1,0:T(8,128)}, f32[64,256]{1,0:T(8,128)S(1)}, u32[]{:S(2)}) copy-start(f32[64,256]{1,0:T(8,128)S(1)} %convolution_bitcast_fusion) | copy-start | bytes 196612
  71.0 1.3 %collective-permute-start.26 = (f32[64,64]{1,0:T(8,128)S(1)}, f32[64,64]{1,0:T(8,128)S(1)}, u32[]{:S(2)}, u32[]{:S(2)}) collective-permute-start(f32[64,64]{1,0:T(8,128)S(1)} %get-tuple-element.8), channel_id=1, source_target_pairs={{0,1},{1,0},{2,3},{3,2},{4,5},{5,4},{6,7},{7,6},{8,9},{9,8},{10,11... | collective-permute-start | bytes 49160 | tf_op jit(solution)/shard_map/ppermute | solution.py:234
  72.3 12.1 %copy-start.28 = (f32[64,64]{1,0:T(8,128)}, f32[64,64]{1,0:T(8,128)S(1)}, u32[]{:S(2)}) copy-start(f32[64,64]{1,0:T(8,128)S(1)} %collective-permute-done.26) | copy-start | bytes 49156
  72.3 3.3 %collective-permute-start.28 = (f32[64,64]{1,0:T(8,128)S(1)}, f32[64,64]{1,0:T(8,128)S(1)}, u32[]{:S(2)}, u32[]{:S(2)}) collective-permute-start(f32[64,64]{1,0:T(8,128)S(1)} %get-tuple-element.9), channel_id=1, source_target_pairs={{0,3},{1,2},{2,1},{3,0},{4,7},{5,6},{6,5},{7,4},{8,11},{9,10},{10,... | collective-permute-start | bytes 49160 | tf_op jit(solution)/shard_map/ppermute | solution.py:234
  75.7 8.7 %copy-start.29 = (f32[64,64]{1,0:T(8,128)}, f32[64,64]{1,0:T(8,128)S(1)}, u32[]{:S(2)}) copy-start(f32[64,64]{1,0:T(8,128)S(1)} %collective-permute-done.28) | copy-start | bytes 49156
  75.7 2.8 %collective-permute-start.27 = (f32[64,64]{1,0:T(8,128)S(1)}, f32[64,64]{1,0:T(8,128)S(1)}, u32[]{:S(2)}, u32[]{:S(2)}) collective-permute-start(f32[64,64]{1,0:T(8,128)S(1)} %get-tuple-element.10), channel_id=1, source_target_pairs={{0,2},{1,3},{2,0},{3,1},{4,6},{5,7},{6,4},{7,5},{8,10},{9,11},{10,... | collective-permute-start | bytes 49160 | tf_op jit(solution)/shard_map/ppermute | solution.py:234
  78.4 5.9 %copy-start.30 = (f32[64,64]{1,0:T(8,128)}, f32[64,64]{1,0:T(8,128)S(1)}, u32[]{:S(2)}) copy-start(f32[64,64]{1,0:T(8,128)S(1)} %collective-permute-done.27) | copy-start | bytes 49156
  78.4 7.4 %collective-permute-start.23 = (bf16[1,3,256,128]{3,2,1,0:T(8,128)(2,1)}, bf16[1,3,256,128]{3,2,1,0:T(8,128)(2,1)}, u32[]{:S(2)}, u32[]{:S(2)}) collective-permute-start(bf16[1,3,256,128]{3,2,1,0:T(8,128)(2,1)} %cut_columns.5.refs_25_), channel_id=1, source_target_pairs={{0,1},{4,5},{9,8},{13,12},{18,19},{22,23},{27,26},{31,30}} | collective-permute-start | bytes 589832 | tf_op jit(solution)/shard_map/ppermute | solution.py:331
  82.3 2.1 %copy-start.23 = (bf16[1,3,256,128]{3,2,1,0:T(8,128)(2,1)}, bf16[1,3,256,128]{3,2,1,0:T(8,128)(2,1)S(1)}, u32[]{:S(2)}) copy-start(bf16[1,3,256,128]{3,2,1,0:T(8,128)(2,1)S(1)} %collective-permute-done.24.refs_27_) | copy-start | bytes 589828
  82.3 5.7 %collective-permute-start.20 = (bf16[2,3,256,128]{3,2,1,0:T(8,128)(2,1)S(1)}, bf16[2,3,256,128]{3,2,1,0:T(8,128)(2,1)}, u32[]{:S(2)}, u32[]{:S(2)}) collective-permute-start(bf16[2,3,256,128]{3,2,1,0:T(8,128)(2,1)S(1)} %cut_columns.4.refs_21_), channel_id=1, source_target_pairs={{0,1},{4,5},{9,8},{13,12},{18,19},{22,23},{27,26},{31,30}} | collective-permute-start | bytes 1179656 | tf_op jit(solution)/shard_map/ppermute | solution.py:331
  84.4 3.6 %collective-permute-start.22 = (bf16[2,3,256,128]{3,2,1,0:T(8,128)(2,1)}, bf16[2,3,256,128]{3,2,1,0:T(8,128)(2,1)}, u32[]{:S(2)}, u32[]{:S(2)}) collective-permute-start(bf16[2,3,256,128]{3,2,1,0:T(8,128)(2,1)} %collective-permute-done.21.refs_23_), channel_id=1, source_target_pairs={{2,3},{6,7},{11,10},{15,14},{16,17},{20,21},{25,24},{29,28}} | collective-permute-start | bytes 1179656 | tf_op jit(solution)/shard_map/ppermute | solution.py:332
  85.8 2.2 %collective-permute-start.25 = (bf16[1,3,256,128]{3,2,1,0:T(8,128)(2,1)}, bf16[1,3,256,128]{3,2,1,0:T(8,128)(2,1)S(1)}, u32[]{:S(2)}, u32[]{:S(2)}) collective-permute-start(bf16[1,3,256,128]{3,2,1,0:T(8,128)(2,1)} %copy-done.23), channel_id=1, source_target_pairs={{2,3},{6,7},{11,10},{15,14},{16,17},{20,21},{25,24},{29,28}} | collective-permute-start | bytes 589832 | tf_op jit(solution)/shard_map/ppermute | solution.py:332
  88.0 0.9 copy-start.3
  89.0 0.9 copy-start.5
  89.9 0.9 copy-start.8
  90.8 0.9 copy-start.11
  91.7 0.9 copy-start.14
  92.7 0.9 copy-start.17
  93.6 0.9 copy-start.20
  94.5 0.9 copy-start.24

commit v4 on v3

--- a/solution.py
+++ b/solution.py
@@ -124,18 +124,37 @@
             piece[i] = jnp.concatenate(pair, axis=0).T.astype(jnp.bfloat16)
 
 
-def cut_kernel(pieces, half_ref, *refs):
-    sources, cols_ref, sem = refs[:pieces], refs[pieces], refs[pieces + 1]
+def project_kernel(me_ref, flat_ref, eig_ref, *refs):
+    shares, cut = refs[:-1], refs[-1]
+    total = sum(
+        jnp.dot(flat_ref[c], eig_ref[c], preferred_element_type=jnp.float32) for c in range(3)
+    )
+    width = cut.shape[2]
+    for k in range(len(shares)):
+        cut[k] = total[:, k * width : (k + 1) * width]
+    for k, share in enumerate(shares):
+        share[...] = cut[lax.bitwise_xor(me_ref[0], k)]
+
+
+def cut_kernel(slots, half_ref, *refs):
+    sources, (cols_ref, held, sem) = refs[: 2 * slots], refs[2 * slots :]
     for half in range(2):
 
         @pl.when(half_ref[0] == half)
         def _(half=half):
             run_copies(
                 [
-                    pltpu.make_async_copy(source, cols_ref.at[k], sem.at[k])
+                    pltpu.make_async_copy(source, held.at[k], sem.at[k])
                     for k, source in enumerate(sources[half::2])
                 ]
             )
+
+    run, lanes = held.shape[2:]
+    for k in range(slots):
+        for c in range(3):
+            turned = held[k, c].astype(jnp.float32).T.astype(jnp.bfloat16)
+            cols_ref[k, c, :, :run] = turned[: lanes // 2]
+            cols_ref[k, c, :, run:] = turned[lanes // 2 :]
 
 
 def side_by_side(first, second):
@@ -150,36 +169,34 @@
     at = 1 + 2 * slots
     groups = [refs[at + k * roles : at + (k + 1) * roles] for k in range(len(lots))]
     at += len(lots) * roles
-    out_ref, rows_in, cols_in, left, right, done, sem, out_sem = refs[at:]
+    out_ref, rows_in, left, right, done, sem, out_sem = refs[at:]
     copies = [
         pltpu.make_async_copy(piece, rows_in.at[k % 2, k // 2], sem.at[k])
         for k, piece in enumerate(pieces)
     ]
-    for copy in copies:
-        copy.start()
+    depth = right.shape[1] // slots
     for role in range(roles):
 
         @pl.when(role_ref[0] == role)
         def _(role=role):
             to = 0
-            wanted = []
             for k, count in enumerate(lots):
-                wanted.append(
+                for n in range(count):
                     pltpu.make_async_copy(
-                        groups[k][role], cols_in.at[pl.ds(to, count)], sem.at[2 * slots + k]
-                    )
-                )
-                to += count
-            run_copies(wanted)
-
+                        groups[k][role].at[n],
+                        right.at[:, pl.ds(to * depth, depth), :],
+                        sem.at[2 * slots + to],
+                    ).start()
+                    to += 1
+
+    for copy in copies:
+        copy.start()
+    for k in range(slots):
+        part = right.at[:, pl.ds(k * depth, depth), :]
+        pltpu.make_async_copy(part, part, sem.at[2 * slots + k]).wait()
+    for copy in copies:
+        copy.wait()
     run = rows_in.shape[3]
-    for d in range(3):
-        for q in range(slots // 2):
-            low, high = side_by_side(cols_in[2 * q, d], cols_in[2 * q + 1, d])
-            right[d, :run, q * LANES : (q + 1) * LANES] = low
-            right[d, run:, q * LANES : (q + 1) * LANES] = high
-    for copy in copies:
-        copy.wait()
 
     def assemble(i, slot):
         c = lax.div(i, 2)
@@ -189,13 +206,13 @@
             left[slot, :run, q * LANES : (q + 1) * LANES] = low
             left[slot, run:, q * LANES : (q + 1) * LANES] = high
 
-    def write(i):
+    def write(i, d):
         start = pl.multiple_of(lax.rem(i, 2) * 2 * run, 2 * run)
         slot = lax.rem(i, 2)
         return pltpu.make_async_copy(
-            done.at[slot],
-            out_ref.at[lax.div(i, 2), :, pl.ds(start, 2 * run), :],
-            out_sem.at[slot],
+            done.at[slot, d],
+            out_ref.at[lax.div(i, 2), d, pl.ds(start, 2 * run), :],
+            out_sem.at[slot, d],
         )
 
     assemble(0, 0)
@@ -206,37 +223,23 @@
 
         @pl.when(i >= 2)
         def _():
-            write(i - 2).wait()
+            for d in range(3):
+                write(i - 2, d).wait()
 
         assemble(jnp.minimum(i + 1, 5), 1 - slot)
         for d in range(3):
-            done[slot, d] = scale * lax.dot_general(
-                left[slot],
-                right[d],
-                (((1,), (1,)), ((), ())),
-                preferred_element_type=jnp.float32,
+            done[slot, d] = scale * jnp.dot(
+                left[slot], right[d], preferred_element_type=jnp.float32
             )
-        write(i).start()
-
-    write(4).wait()
-    write(5).wait()
-
-
-def project(flat, eigvecs, me_a, atom_axis):
-    proj = jnp.einsum("cfa,cak->fk", flat, eigvecs, preferred_element_type=jnp.float32)
-    width = proj.shape[1] // atom_axis
-
-    def share(to):
-        return lax.dynamic_slice_in_dim(proj, to * width, width, axis=1)
-
-    total = share(me_a)
-    for d in range(1, atom_axis):
-        total = total + lax.ppermute(
-            share(lax.bitwise_xor(me_a, jnp.int32(d))),
-            "atoms",
-            [(a, a ^ d) for a in range(atom_axis)],
-        )
-    return total
+            write(i, d).start()
+
+    for d in range(3):
+        write(4, d).wait()
+        write(5, d).wait()
+
+
+def after(value, *others):
+    return lax.optimization_barrier((value,) + others)[0]
 
 
 def ring_order(count):
@@ -298,7 +301,21 @@
         compiler_params=params(8),
         name="polar_align",
     )(stats, *others, x, mean_structure)
-    projections = project(flat, eigvecs, me_a, atom_axis)
+    share = jax.ShapeDtypeStruct((local_frames, eigvecs.shape[2] // atom_axis), jnp.float32)
+    shares = pl.pallas_call(
+        project_kernel,
+        out_shape=(share,) * atom_axis,
+        in_specs=[SMEM, VMEM, VMEM],
+        out_specs=(VMEM,) * atom_axis,
+        scratch_shapes=[pltpu.VMEM((atom_axis,) + share.shape, jnp.float32)],
+        compiler_params=params(8),
+        name="project",
+    )(me_a.astype(jnp.int32).reshape(1), flat, eigvecs)
+    parts = [shares[0]] + [
+        lax.ppermute(shares[d], "atoms", [(a, a ^ d) for a in range(atom_axis)])
+        for d in range(1, atom_axis)
+    ]
+    projections = sum(parts)
 
     def pairs(source, target):
         return [
@@ -317,12 +334,16 @@
         return covariance, projections
 
     def spread(pieces):
+        slots = len(pieces) // 2
         cut = pl.pallas_call(
-            functools.partial(cut_kernel, len(pieces)),
-            out_shape=jax.ShapeDtypeStruct((len(pieces) // 2,) + piece.shape, jnp.bfloat16),
+            functools.partial(cut_kernel, slots),
+            out_shape=jax.ShapeDtypeStruct((slots, 3, local_frames, block), jnp.bfloat16),
             in_specs=[SMEM] + [ANY] * len(pieces),
-            out_specs=ANY,
-            scratch_shapes=[pltpu.SemaphoreType.DMA((len(pieces) // 2,))],
+            out_specs=VMEM,
+            scratch_shapes=[
+                pltpu.VMEM((slots,) + piece.shape, jnp.bfloat16),
+                pltpu.SemaphoreType.DMA((slots,)),
+            ],
             compiler_params=params(8),
             name="cut_columns",
         )(half, *pieces)
@@ -336,19 +357,31 @@
     forward = [(order[i], order[(i + 1) % frame_axis]) for i in range(frame_axis)]
     backward = [(b, a) for a, b in forward]
 
-    def hop(arrays, way):
-        return [lax.ppermute(a, "frames", way) for a in arrays]
+    def hop(up, down):
+        up_a = lax.ppermute(up[0], "frames", forward)
+        down_a = lax.ppermute(down[0], "frames", backward)
+        up_b = lax.ppermute(up[1], "frames", forward)
+        down_b = lax.ppermute(down[1], "frames", backward)
+        return [up_a, up_b], [down_a, down_b]
 
     own = [first, second]
-    up, down = own, own
-    ups, downs = [], []
-    for _ in range(1, frame_axis // 2):
-        up, down = hop(up, forward), hop(down, backward)
-        ups.append(up)
-        downs.append(down)
-    far = hop(up[:1], forward) + hop(down[1:], backward)
-    lots = [own + ups[0] + downs[0] + ups[1] + downs[1], ups[2] + downs[2], far]
-    cuts = sum([spread(lot) for lot in lots], [])
+    up1, down1 = hop(own, own)
+    up1[0] = after(up1[0], *shares)
+    up2, down2 = hop(up1, down1)
+    up2[1] = after(up2[1], *parts)
+    up3, down3 = hop(up2, down2)
+    lots = [own + up1 + down1 + up2 + down2, up3 + down3]
+    cuts = [spread(lots[0])]
+    down3[1] = after(down3[1], cuts[0][0])
+    far = [
+        lax.ppermute(up3[0], "frames", forward),
+        lax.ppermute(down3[1], "frames", backward),
+    ]
+    cuts.append(spread(lots[1]))
+    far[0] = after(far[0], cuts[1][0], cuts[0][2])
+    lots.append(far)
+    cuts.append(spread(far))
+    cuts = sum(cuts, [])
     pieces = sum(lots, [])
     counts = [len(lot) // 2 for lot in lots]
     covariance = pl.pallas_call(
@@ -360,12 +393,11 @@
         out_specs=ANY,
         scratch_shapes=[
             pltpu.VMEM((2, frame_axis) + piece.shape, jnp.bfloat16),
-            pltpu.VMEM((frame_axis,) + piece.shape, jnp.bfloat16),
             pltpu.VMEM((2, 2 * run, total_frames), jnp.bfloat16),
-            pltpu.VMEM((3, block, total_frames), jnp.bfloat16),
+            pltpu.VMEM((3, total_frames, block), jnp.bfloat16),
             pltpu.VMEM((2, 3, 2 * run, block), jnp.float32),
-            pltpu.SemaphoreType.DMA((len(pieces) + len(lots),)),
-            pltpu.SemaphoreType.DMA((2,)),
+            pltpu.SemaphoreType.DMA((len(pieces) + frame_axis,)),
+            pltpu.SemaphoreType.DMA((2, 3)),
         ],
         compiler_params=params(24),
         cost_estimate=pl.CostEstimate(

time: 111 us -> 99.4 us (0.90)
  the two profiles are of different devices: /device:TPU:9 before, /device:TPU:0 now
where the time goes in v4:
time: 99.4 us; the launch traced here: 98.2 us
  starting transfers between devices  37.7 us (38%)
  waiting for transfers between devices  23.5 us (24%)
  Pallas kernels  18.2 us (18%)
  local copies, waits for them, and re-layouts  16.5 us (17%)
  other arithmetic  1.44 us (1%)
    unnamed x56, local copies, waits for them, and re-layouts  16.5 us
    pallas_call x1, Pallas kernels, per_device(): pl.pallas_call(functools.partial(covariance_kernel, frame_axis, atom_axis...  12.7 us
    ppermute x3, starting transfers between devices, spread(): across = lax.ppermute(cut, axes, pairs(0, 2))  11.2 us
    ppermute x3, waiting for transfers between devices, per_device(): lax.ppermute(shares[d], 'atoms', [(a, a ^ d) for a in range(atom_axis)])  8.1 us
    ppermute x3, starting transfers between devices, spread(): beside = lax.ppermute(cut, axes, pairs(0, 1))  4.67 us
    pallas_call x3, Pallas kernels, spread(): pl.pallas_call(functools.partial(cut_kernel, slots), out_shape=jax.ShapeD...  3.85 us
    ppermute x3, waiting for transfers between devices, hop(): down_a = lax.ppermute(down[0], 'frames', backward)  3.78 us
    ppermute x3, starting transfers between devices, spread(): last = lax.ppermute(across, axes, pairs(2, 3))  3.72 us
  transfers between devices with their start and end apart: 29, of which 10 were waited for; matrix products, arithmetic and copies ran while one was open for 1% of the time, Pallas kernels for 2%

profile of v4, /device:TPU:0, one launch (start us, length us, event | category | flops | bytes accessed | tf_op | source)
XLA Modules:
  0.0 98.2 jit_solution(15030327524169496323)
XLA Ops:
  0.6 1.1 %copy-done = f32[64,3,1024]{2,0,1:T(8,128)S(1)} copy-done((f32[64,3,1024]{2,0,1:T(8,128)S(1)}, f32[64,3,1024]{2,0,1:T(8,128)}, u32[]{:S(2)}) %copy-start) | copy-done | bytes 786456
  1.8 0.7 copy-done.26
  2.5 0.6 local_moments.1.refs_0_
  3.0 2.4 %collective-permute-start.2 = (f32[24,64]{1,0:T(8,128)S(1)}, f32[24,64]{1,0:T(8,128)S(1)}, u32[]{:S(2)}, u32[]{:S(2)}) collective-permute-start(f32[24,64]{1,0:T(8,128)S(1)} %local_moments.1.refs_0_), channel_id=1, source_target_pairs={{0,3},{1,2},{2,1},{3,0},{4,7},{5,6},{6,5},{7,4},{8,11},{9,10},{10,... | collective-permute-start | bytes 18440 | tf_op jit(solution)/shard_map/ppermute | solution.py:289
  5.5 0.6 collective-permute-start.1
  6.1 0.0 collective-permute-start
  6.2 0.7 collective-permute-done.2.refs_3_
  6.9 2.3 %collective-permute-done.1.refs_2_ = f32[24,64]{1,0:T(8,128)S(1)} collective-permute-done((f32[24,64]{1,0:T(8,128)S(1)}, f32[24,64]{1,0:T(8,128)S(1)}, u32[]{:S(2)}, u32[]{:S(2)}) %collective-permute-start.1) | collective-permute-done | bytes 6176 | tf_op jit(solution)/shard_map/ppermute | solution.py:289
  9.2 0.7 polar_align.1
  9.9 1.6 %collective-permute-start.3 = (bf16[3,256,128]{2,1,0:T(8,128)(2,1)S(1)}, bf16[3,256,128]{2,1,0:T(8,128)(2,1)S(1)}, u32[]{:S(2)}, u32[]{:S(2)}) collective-permute-start(bf16[3,256,128]{2,1,0:T(8,128)(2,1)S(1)} %get-tuple-element.13.refs_0_.refs_1_), channel_id=1, source_target_pairs={{0,8},{8,16},{16,24},{24,28},{28,20},{20,12},{12,4},{4,0},{1,9},{9... | collective-permute-start | bytes 589832 | tf_op jit(solution)/shard_map/ppermute | solution.py:361
  11.5 1.6 %collective-permute-start.4 = (bf16[3,256,128]{2,1,0:T(8,128)(2,1)S(1)}, bf16[3,256,128]{2,1,0:T(8,128)(2,1)S(1)}, u32[]{:S(2)}, u32[]{:S(2)}) collective-permute-start(bf16[3,256,128]{2,1,0:T(8,128)(2,1)S(1)} %get-tuple-element.14.refs_1_.refs_2_), channel_id=1, source_target_pairs={{0,8},{8,16},{16,24},{24,28},{28,20},{20,12},{12,4},{4,0},{1,9},{9... | collective-permute-start | bytes 589832 | tf_op jit(solution)/shard_map/ppermute | solution.py:363
  13.1 0.4 collective-permute-start.5
  13.5 0.4 collective-permute-start.6
  14.0 1.4 %copy-done.1 = bf16[3,1024,256]{2,1,0:T(8,128)(2,1)S(1)} copy-done((bf16[3,1024,256]{2,1,0:T(8,128)(2,1)S(1)}, bf16[3,1024,256]{2,1,0:T(8,128)(2,1)}, u32[]{:S(2)}) %copy-start.1) | copy-done | bytes 1572888
  15.4 0.5 project.1
  15.9 1.9 %collective-permute-done.3.refs_2_.refs_3_ = bf16[3,256,128]{2,1,0:T(8,128)(2,1)S(1)} collective-permute-done((bf16[3,256,128]{2,1,0:T(8,128)(2,1)S(1)}, bf16[3,256,128]{2,1,0:T(8,128)(2,1)S(1)}, u32[]{:S(2)}, u32[]{:S(2)}) %collective-permute-start.3) | collective-permute-done | bytes 196640 | tf_op jit(solution)/shard_map/ppermute | solution.py:361
  17.8 2.7 %collective-permute-done.4.refs_3_.refs_4_ = bf16[3,256,128]{2,1,0:T(8,128)(2,1)S(1)} collective-permute-done((bf16[3,256,128]{2,1,0:T(8,128)(2,1)S(1)}, bf16[3,256,128]{2,1,0:T(8,128)(2,1)S(1)}, u32[]{:S(2)}, u32[]{:S(2)}) %collective-permute-start.4) | collective-permute-done | bytes 196640 | tf_op jit(solution)/shard_map/ppermute | solution.py:363
  20.5 1.6 %collective-permute-start.8 = (bf16[3,256,128]{2,1,0:T(8,128)(2,1)S(1)}, bf16[3,256,128]{2,1,0:T(8,128)(2,1)}, u32[]{:S(2)}, u32[]{:S(2)}) collective-permute-start(bf16[3,256,128]{2,1,0:T(8,128)(2,1)S(1)} %collective-permute-done.4.refs_3_.refs_4_), channel_id=1, source_target_pairs={{0,8},{8,16},{16,24},{24,28},{28,20},{20,12},{12,4},{4,0},{1,9},{9... | collective-permute-start | bytes 589832 | tf_op jit(solution)/shard_map/ppermute | solution.py:363
  22.1 1.6 %collective-permute-start.7 = (bf16[3,256,128]{2,1,0:T(8,128)(2,1)S(1)}, bf16[3,256,128]{2,1,0:T(8,128)(2,1)}, u32[]{:S(2)}, u32[]{:S(2)}) collective-permute-start(bf16[3,256,128]{2,1,0:T(8,128)(2,1)S(1)} %collective-permute-done.3.refs_2_.refs_3_), channel_id=1, source_target_pairs={{0,8},{8,16},{16,24},{24,28},{28,20},{20,12},{12,4},{4,0},{1,9},{9... | collective-permute-start | bytes 589832 | tf_op jit(solution)/shard_map/ppermute | solution.py:361
  23.6 0.4 collective-permute-start.12
  24.1 0.5 collective-permute-start.13
  24.6 1.3 %collective-permute-done.9 = f32[64,64]{1,0:T(8,128)} collective-permute-done((f32[64,64]{1,0:T(8,128)S(1)}, f32[64,64]{1,0:T(8,128)}, u32[]{:S(2)}, u32[]{:S(2)}) %collective-permute-start.9) | collective-permute-done | bytes 16416 | tf_op jit(solution)/shard_map/ppermute | solution.py:315
  25.9 0.7 collective-permute-start.10
  26.6 3.3 %collective-permute-done.10 = f32[64,64]{1,0:T(8,128)} collective-permute-done((f32[64,64]{1,0:T(8,128)S(1)}, f32[64,64]{1,0:T(8,128)}, u32[]{:S(2)}, u32[]{:S(2)}) %collective-permute-start.10) | collective-permute-done | bytes 16416 | tf_op jit(solution)/shard_map/ppermute | solution.py:315
  29.9 3.4 %collective-permute-done.11 = f32[64,64]{1,0:T(8,128)} collective-permute-done((f32[64,64]{1,0:T(8,128)S(1)}, f32[64,64]{1,0:T(8,128)}, u32[]{:S(2)}, u32[]{:S(2)}) %collective-permute-start.11) | collective-permute-done | bytes 16416 | tf_op jit(solution)/shard_map/ppermute | solution.py:315
  33.4 2.1 %cut_columns.4.refs_17_ = bf16[5,3,64,512]{3,2,1,0:T(8,128)(2,1)S(1)} custom-call(s32[1]{0:T(128)} %bitcast.3.half_ref, bf16[3,256,128]{2,1,0:T(8,128)(2,1)S(1)} %get-tuple-element.13.refs_0_.refs_1_, bf16[3,256,128]{2,1,0:T(8,128)(2,1)S(1)} %get-tuple-element.14.refs_1_.refs_2_, bf16[3,256,128]{2,1,0:T(8,128)(2,1)S(1)} %collective-permute-done.3.refs_2_.refs_3_, ...), custom_call_target="tpu_custom_call" | custom-call | tf_op jit(solution)/shard_map/cut_columns/pallas_call | solution.py:338
  35.5 0.7 copy-done.6
  36.2 0.7 copy-done.8
  36.8 0.7 copy-done.10
  37.5 2.9 %collective-permute-start.19 = (bf16[5,3,64,512]{3,2,1,0:T(8,128)(2,1)S(1)}, bf16[5,3,64,512]{3,2,1,0:T(8,128)(2,1)S(1)}, u32[]{:S(2)}, u32[]{:S(2)}) collective-permute-start(bf16[5,3,64,512]{3,2,1,0:T(8,128)(2,1)S(1)} %cut_columns.4.refs_17_), channel_id=1, source_target_pairs={{0,2},{4,6},{9,11},{13,15},{18,16},{22,20},{27,25},{31,29}} | collective-permute-start | bytes 2949128 | tf_op jit(solution)/shard_map/ppermute | solution.py:351
  40.4 1.7 %collective-permute-start.16 = (bf16[3,256,128]{2,1,0:T(8,128)(2,1)S(1)}, bf16[3,256,128]{2,1,0:T(8,128)(2,1)S(1)}, u32[]{:S(2)}, u32[]{:S(2)}) collective-permute-start(bf16[3,256,128]{2,1,0:T(8,128)(2,1)S(1)} %collective-permute-done.12.refs_8_.refs_9_), channel_id=1, source_target_pairs={{8,0},{16,8},{24,16},{28,24},{20,28},{12,20},{4,12},{0,4},{9,1},{1... | collective-permute-start | bytes 589832 | tf_op jit(solution)/shard_map/ppermute | solution.py:362
  42.1 0.4 collective-permute-start.14
  42.5 1.6 %collective-permute-start.17 = (bf16[3,256,128]{2,1,0:T(8,128)(2,1)}, bf16[3,256,128]{2,1,0:T(8,128)(2,1)S(1)}, u32[]{:S(2)}, u32[]{:S(2)}) collective-permute-start(bf16[3,256,128]{2,1,0:T(8,128)(2,1)} %collective-permute-done.13.refs_9_.refs_10_), channel_id=1, source_target_pairs={{8,0},{16,8},{24,16},{28,24},{20,28},{12,20},{4,12},{0,4},{9,1},{1... | collective-permute-start | bytes 589832 | tf_op jit(solution)/shard_map/ppermute | solution.py:364
  44.1 0.4 collective-permute-start.15
  44.5 3.8 %collective-permute-done.16.refs_2_.refs_13_ = bf16[3,256,128]{2,1,0:T(8,128)(2,1)S(1)} collective-permute-done((bf16[3,256,128]{2,1,0:T(8,128)(2,1)S(1)}, bf16[3,256,128]{2,1,0:T(8,128)(2,1)S(1)}, u32[]{:S(2)}, u32[]{:S(2)}) %collective-permute-start.16) | collective-permute-done | bytes 196640 | tf_op jit(solution)/shard_map/ppermute | solution.py:362
  48.3 1.3 %collective-permute-start.21 = (bf16[5,3,64,512]{3,2,1,0:T(8,128)(2,1)S(1)}, bf16[5,3,64,512]{3,2,1,0:T(8,128)(2,1)S(1)}, u32[]{:S(2)}, u32[]{:S(2)}) collective-permute-start(bf16[5,3,64,512]{3,2,1,0:T(8,128)(2,1)S(1)} %cut_columns.4.refs_17_), channel_id=1, source_target_pairs={{0,1},{4,5},{9,8},{13,12},{18,19},{22,23},{27,26},{31,30}} | collective-permute-start | bytes 2949128 | tf_op jit(solution)/shard_map/ppermute | solution.py:352
  49.7 2.3 %collective-permute-done.19.refs_19_ = bf16[5,3,64,512]{3,2,1,0:T(8,128)(2,1)S(1)} collective-permute-done((bf16[5,3,64,512]{3,2,1,0:T(8,128)(2,1)S(1)}, bf16[5,3,64,512]{3,2,1,0:T(8,128)(2,1)S(1)}, u32[]{:S(2)}, u32[]{:S(2)}) %collective-permute-start.19) | collective-permute-done | bytes 983072 | tf_op jit(solution)/shard_map/ppermute | solution.py:351
  52.0 1.6 %collective-permute-start.22 = (bf16[5,3,64,512]{3,2,1,0:T(8,128)(2,1)S(1)}, bf16[5,3,64,512]{3,2,1,0:T(8,128)(2,1)}, u32[]{:S(2)}, u32[]{:S(2)}) collective-permute-start(bf16[5,3,64,512]{3,2,1,0:T(8,128)(2,1)S(1)} %collective-permute-done.19.refs_19_), channel_id=1, source_target_pairs={{2,3},{6,7},{11,10},{15,14},{16,17},{20,21},{25,24},{29,28}} | collective-permute-start | bytes 2949128 | tf_op jit(solution)/shard_map/ppermute | solution.py:353
  53.7 0.7 cut_columns.3.refs_21_
  54.4 0.1 copy-done.24
  54.4 5.8 %collective-permute-start.24 = (bf16[2,3,64,512]{3,2,1,0:T(8,128)(2,1)S(1)}, bf16[2,3,64,512]{3,2,1,0:T(8,128)(2,1)}, u32[]{:S(2)}, u32[]{:S(2)}) collective-permute-start(bf16[2,3,64,512]{3,2,1,0:T(8,128)(2,1)S(1)} %cut_columns.3.refs_21_), channel_id=1, source_target_pairs={{0,2},{4,6},{9,11},{13,15},{18,16},{22,20},{27,25},{31,29}} | collective-permute-start | bytes 1179656 | tf_op jit(solution)/shard_map/ppermute | solution.py:351
  60.2 2.0 %collective-permute-start.20 = (bf16[3,256,128]{2,1,0:T(8,128)(2,1)S(1)}, bf16[3,256,128]{2,1,0:T(8,128)(2,1)S(1)}, u32[]{:S(2)}, u32[]{:S(2)}) collective-permute-start(bf16[3,256,128]{2,1,0:T(8,128)(2,1)S(1)} %collective-permute-done.17.refs_3_.refs_14_), channel_id=1, source_target_pairs={{8,0},{16,8},{24,16},{28,24},{20,28},{12,20},{4,12},{0,4},{9,1},{1... | collective-permute-start | bytes 589832 | tf_op jit(solution)/shard_map/ppermute | solution.py:378
  62.2 2.0 %collective-permute-start.23 = (bf16[2,3,64,512]{3,2,1,0:T(8,128)(2,1)S(1)}, bf16[2,3,64,512]{3,2,1,0:T(8,128)(2,1)}, u32[]{:S(2)}, u32[]{:S(2)}) collective-permute-start(bf16[2,3,64,512]{3,2,1,0:T(8,128)(2,1)S(1)} %cut_columns.3.refs_21_), channel_id=1, source_target_pairs={{0,1},{4,5},{9,8},{13,12},{18,19},{22,23},{27,26},{31,30}} | collective-permute-start | bytes 1179656 | tf_op jit(solution)/shard_map/ppermute | solution.py:352
  64.2 1.6 %collective-permute-done.20.refs_1_.refs_16_ = bf16[3,256,128]{2,1,0:T(8,128)(2,1)S(1)} collective-permute-done((bf16[3,256,128]{2,1,0:T(8,128)(2,1)S(1)}, bf16[3,256,128]{2,1,0:T(8,128)(2,1)S(1)}, u32[]{:S(2)}, u32[]{:S(2)}) %collective-permute-start.20) | collective-permute-done | bytes 196640 | tf_op jit(solution)/shard_map/ppermute | solution.py:378
  65.9 1.1 %cut_columns.5.refs_25_ = bf16[1,3,64,512]{3,2,1,0:T(8,128)(2,1)} custom-call(s32[1]{0:T(128)} %bitcast.3.half_ref, bf16[3,256,128]{2,1,0:T(8,128)(2,1)S(1)} %collective-permute-done.18.refs_0_.refs_15_, bf16[3,256,128]{2,1,0:T(8,128)(2,1)S(1)} %collective-permute-done.20.refs_1_.refs_16_), custom_call_target="tpu_custom_call" | custom-call | tf_op jit(solution)/shard_map/cut_columns/pallas_call | solution.py:338
  66.9 2.6 %collective-permute-start.27 = (bf16[1,3,64,512]{3,2,1,0:T(8,128)(2,1)}, bf16[1,3,64,512]{3,2,1,0:T(8,128)(2,1)}, u32[]{:S(2)}, u32[]{:S(2)}) collective-permute-start(bf16[1,3,64,512]{3,2,1,0:T(8,128)(2,1)} %cut_columns.5.refs_25_), channel_id=1, source_target_pairs={{0,2},{4,6},{9,11},{13,15},{18,16},{22,20},{27,25},{31,29}} | collective-permute-start | bytes 589832 | tf_op jit(solution)/shard_map/ppermute | solution.py:351
  69.5 1.4 %collective-permute-start.25 = (bf16[2,3,64,512]{3,2,1,0:T(8,128)(2,1)}, bf16[2,3,64,512]{3,2,1,0:T(8,128)(2,1)}, u32[]{:S(2)}, u32[]{:S(2)}) collective-permute-start(bf16[2,3,64,512]{3,2,1,0:T(8,128)(2,1)} %collective-permute-done.24.refs_23_), channel_id=1, source_target_pairs={{2,3},{6,7},{11,10},{15,14},{16,17},{20,21},{25,24},{29,28}} | collective-permute-start | bytes 1179656 | tf_op jit(solution)/shard_map/ppermute | solution.py:353
  71.0 1.3 %collective-permute-start.26 = (bf16[1,3,64,512]{3,2,1,0:T(8,128)(2,1)}, bf16[1,3,64,512]{3,2,1,0:T(8,128)(2,1)S(1)}, u32[]{:S(2)}, u32[]{:S(2)}) collective-permute-start(bf16[1,3,64,512]{3,2,1,0:T(8,128)(2,1)} %cut_columns.5.refs_25_), channel_id=1, source_target_pairs={{0,1},{4,5},{9,8},{13,12},{18,19},{22,23},{27,26},{31,30}} | collective-permute-start | bytes 589832 | tf_op jit(solution)/shard_map/ppermute | solution.py:352
  72.3 0.0 collective-permute-done.27.refs_27_
  72.3 0.7 collective-permute-start.28
  73.0 1.4 %add_add_fusion = f32[64,64]{1,0:T(8,128)} fusion(f32[64,64]{1,0:T(8,128)} %collective-permute-done.11, f32[64,64]{1,0:T(8,128)} %collective-permute-done.10, f32[64,64]{1,0:T(8,128)} %copy-done.27, f32[64,64]{1,0:T(8,128)} %collective-permute-done.9), kind=kLoop, calls=%fused_computation | loop fusion | flops 12288 | bytes 81920 | tf_op jit(solution)/shard_map/add | solution.py:318
  74.5 0.9 copy-done.3
  75.4 0.9 copy-done.5
  76.3 0.9 copy-done.7
  77.2 0.9 copy-done.9
  78.2 0.9 copy-done.11
  79.1 0.9 copy-done.13
  80.0 0.9 copy-done.15
  81.0 0.9 copy-done.17
  81.9 0.9 copy-done.19
  82.8 0.9 copy-done.21
  83.7 0.9 copy-done.23
  84.7 0.9 copy-done.25
  85.6 12.7 %covariance_tile.1 = f32[3,3,1024,512]{3,2,1,0:T(8,128)} custom-call(s32[1]{0:T(128)} %bitcast.refs_0_, bf16[3,256,128]{2,1,0:T(8,128)(2,1)S(1)} %get-tuple-element.13.refs_0_.refs_1_, bf16[3,256,128]{2,1,0:T(8,128)(2,1)S(1)} %copy-done.3, bf16[3,256,128]{2,1,0:T(8,128)(2,1)S(1)} %copy-done.5, bf16[3,256,128]{2,1,0:T(8,128)(2,1)S(1)} %copy-done.7, ...), custom_call_target="tpu_custom_call" | custom-call | flops 4831838208 | bytes 25165824 | tf_op jit(solution)/shard_map/covariance_tile/pallas_call | solution.py:387
  (58 shorter events, 0.1 us)
Async XLA Ops:
  0.6 1.1 %copy-start = (f32[64,3,1024]{2,0,1:T(8,128)S(1)}, f32[64,3,1024]{2,0,1:T(8,128)}, u32[]{:S(2)}) copy-start(f32[64,3,1024]{2,0,1:T(8,128)} %param.3) | copy-start | bytes 2359300
  1.8 0.7 copy-start.26
  3.0 3.8 %collective-permute-start.2 = (f32[24,64]{1,0:T(8,128)S(1)}, f32[24,64]{1,0:T(8,128)S(1)}, u32[]{:S(2)}, u32[]{:S(2)}) collective-permute-start(f32[24,64]{1,0:T(8,128)S(1)} %local_moments.1.refs_0_), channel_id=1, source_target_pairs={{0,3},{1,2},{2,1},{3,0},{4,7},{5,6},{6,5},{7,4},{8,11},{9,10},{10,... | collective-permute-start | bytes 18440 | tf_op jit(solution)/shard_map/ppermute | solution.py:289
  5.5 3.7 %collective-permute-start.1 = (f32[24,64]{1,0:T(8,128)S(1)}, f32[24,64]{1,0:T(8,128)S(1)}, u32[]{:S(2)}, u32[]{:S(2)}) collective-permute-start(f32[24,64]{1,0:T(8,128)S(1)} %local_moments.1.refs_0_), channel_id=1, source_target_pairs={{0,2},{1,3},{2,0},{3,1},{4,6},{5,7},{6,4},{7,5},{8,10},{9,11},{10,... | collective-permute-start | bytes 18440 | tf_op jit(solution)/shard_map/ppermute | solution.py:289
  6.1 3.1 %collective-permute-start = (f32[24,64]{1,0:T(8,128)S(1)}, f32[24,64]{1,0:T(8,128)S(1)}, u32[]{:S(2)}, u32[]{:S(2)}) collective-permute-start(f32[24,64]{1,0:T(8,128)S(1)} %local_moments.1.refs_0_), channel_id=1, source_target_pairs={{0,1},{1,0},{2,3},{3,2},{4,5},{5,4},{6,7},{7,6},{8,9},{9,8},{10,11... | collective-permute-start | bytes 18440 | tf_op jit(solution)/shard_map/ppermute | solution.py:289
  9.9 43.7 %copy-start.2 = (bf16[3,256,128]{2,1,0:T(8,128)(2,1)}, bf16[3,256,128]{2,1,0:T(8,128)(2,1)S(1)}, u32[]{:S(2)}) copy-start(bf16[3,256,128]{2,1,0:T(8,128)(2,1)S(1)} %get-tuple-element.14.refs_1_.refs_2_) | copy-start | bytes 589828
  9.9 7.9 %collective-permute-start.3 = (bf16[3,256,128]{2,1,0:T(8,128)(2,1)S(1)}, bf16[3,256,128]{2,1,0:T(8,128)(2,1)S(1)}, u32[]{:S(2)}, u32[]{:S(2)}) collective-permute-start(bf16[3,256,128]{2,1,0:T(8,128)(2,1)S(1)} %get-tuple-element.13.refs_0_.refs_1_), channel_id=1, source_target_pairs={{0,8},{8,16},{16,24},{24,28},{28,20},{20,12},{12,4},{4,0},{1,9},{9... | collective-permute-start | bytes 589832 | tf_op jit(solution)/shard_map/ppermute | solution.py:361
  11.5 9.0 %collective-permute-start.4 = (bf16[3,256,128]{2,1,0:T(8,128)(2,1)S(1)}, bf16[3,256,128]{2,1,0:T(8,128)(2,1)S(1)}, u32[]{:S(2)}, u32[]{:S(2)}) collective-permute-start(bf16[3,256,128]{2,1,0:T(8,128)(2,1)S(1)} %get-tuple-element.14.refs_1_.refs_2_), channel_id=1, source_target_pairs={{0,8},{8,16},{16,24},{24,28},{28,20},{20,12},{12,4},{4,0},{1,9},{9... | collective-permute-start | bytes 589832 | tf_op jit(solution)/shard_map/ppermute | solution.py:363
  13.1 10.5 %collective-permute-start.5 = (bf16[3,256,128]{2,1,0:T(8,128)(2,1)S(1)}, bf16[3,256,128]{2,1,0:T(8,128)(2,1)S(1)}, u32[]{:S(2)}, u32[]{:S(2)}) collective-permute-start(bf16[3,256,128]{2,1,0:T(8,128)(2,1)S(1)} %get-tuple-element.13.refs_0_.refs_1_), channel_id=1, source_target_pairs={{8,0},{16,8},{24,16},{28,24},{20,28},{12,20},{4,12},{0,4},{9,1},{1... | collective-permute-start | bytes 589832 | tf_op jit(solution)/shard_map/ppermute | solution.py:362
  13.5 10.6 %collective-permute-start.6 = (bf16[3,256,128]{2,1,0:T(8,128)(2,1)S(1)}, bf16[3,256,128]{2,1,0:T(8,128)(2,1)S(1)}, u32[]{:S(2)}, u32[]{:S(2)}) collective-permute-start(bf16[3,256,128]{2,1,0:T(8,128)(2,1)S(1)} %get-tuple-element.14.refs_1_.refs_2_), channel_id=1, source_target_pairs={{8,0},{16,8},{24,16},{28,24},{20,28},{12,20},{4,12},{0,4},{9,1},{1... | collective-permute-start | bytes 589832 | tf_op jit(solution)/shard_map/ppermute | solution.py:364
  14.0 1.4 %copy-start.1 = (bf16[3,1024,256]{2,1,0:T(8,128)(2,1)S(1)}, bf16[3,1024,256]{2,1,0:T(8,128)(2,1)}, u32[]{:S(2)}) copy-start(bf16[3,1024,256]{2,1,0:T(8,128)(2,1)} %eig_ref.1) | copy-start | bytes 4718596
  15.9 8.2 %copy-start.27 = (f32[64,64]{1,0:T(8,128)}, f32[64,64]{1,0:T(8,128)S(1)}, u32[]{:S(2)}) copy-start(f32[64,64]{1,0:T(8,128)S(1)} %get-tuple-element.16) | copy-start | bytes 49156
  17.8 35.8 %copy-start.4 = (bf16[3,256,128]{2,1,0:T(8,128)(2,1)}, bf16[3,256,128]{2,1,0:T(8,128)(2,1)S(1)}, u32[]{:S(2)}) copy-start(bf16[3,256,128]{2,1,0:T(8,128)(2,1)S(1)} %collective-permute-done.3.refs_2_.refs_3_) | copy-start | bytes 589828
  20.5 12.9 %collective-permute-start.8 = (bf16[3,256,128]{2,1,0:T(8,128)(2,1)S(1)}, bf16[3,256,128]{2,1,0:T(8,128)(2,1)}, u32[]{:S(2)}, u32[]{:S(2)}) collective-permute-start(bf16[3,256,128]{2,1,0:T(8,128)(2,1)S(1)} %collective-permute-done.4.refs_3_.refs_4_), channel_id=1, source_target_pairs={{0,8},{8,16},{16,24},{24,28},{28,20},{20,12},{12,4},{4,0},{1,9},{9... | collective-permute-start | bytes 589832 | tf_op jit(solution)/shard_map/ppermute | solution.py:363
  22.1 11.3 %collective-permute-start.7 = (bf16[3,256,128]{2,1,0:T(8,128)(2,1)S(1)}, bf16[3,256,128]{2,1,0:T(8,128)(2,1)}, u32[]{:S(2)}, u32[]{:S(2)}) collective-permute-start(bf16[3,256,128]{2,1,0:T(8,128)(2,1)S(1)} %collective-permute-done.3.refs_2_.refs_3_), channel_id=1, source_target_pairs={{0,8},{8,16},{16,24},{24,28},{28,20},{20,12},{12,4},{4,0},{1,9},{9... | collective-permute-start | bytes 589832 | tf_op jit(solution)/shard_map/ppermute | solution.py:361
  23.6 9.7 %collective-permute-start.12 = (bf16[3,256,128]{2,1,0:T(8,128)(2,1)S(1)}, bf16[3,256,128]{2,1,0:T(8,128)(2,1)S(1)}, u32[]{:S(2)}, u32[]{:S(2)}) collective-permute-start(bf16[3,256,128]{2,1,0:T(8,128)(2,1)S(1)} %collective-permute-done.5.refs_4_.refs_5_), channel_id=1, source_target_pairs={{8,0},{16,8},{24,16},{28,24},{20,28},{12,20},{4,12},{0,4},{9,1},{1... | collective-permute-start | bytes 589832 | tf_op jit(solution)/shard_map/ppermute | solution.py:362
  24.1 9.3 %collective-permute-start.13 = (bf16[3,256,128]{2,1,0:T(8,128)(2,1)S(1)}, bf16[3,256,128]{2,1,0:T(8,128)(2,1)}, u32[]{:S(2)}, u32[]{:S(2)}) collective-permute-start(bf16[3,256,128]{2,1,0:T(8,128)(2,1)S(1)} %collective-permute-done.6.refs_5_.refs_6_), channel_id=1, source_target_pairs={{8,0},{16,8},{24,16},{28,24},{20,28},{12,20},{4,12},{0,4},{9,1},{1... | collective-permute-start | bytes 589832 | tf_op jit(solution)/shard_map/ppermute | solution.py:364
  24.6 1.3 %collective-permute-start.9 = (f32[64,64]{1,0:T(8,128)S(1)}, f32[64,64]{1,0:T(8,128)}, u32[]{:S(2)}, u32[]{:S(2)}) collective-permute-start(f32[64,64]{1,0:T(8,128)S(1)} %get-tuple-element.17), channel_id=1, source_target_pairs={{0,1},{1,0},{2,3},{3,2},{4,5},{5,4},{6,7},{7,6},{8,9},{9,8},{10,11... | collective-permute-start | bytes 49160 | tf_op jit(solution)/shard_map/ppermute | solution.py:315
  25.9 4.0 %collective-permute-start.10 = (f32[64,64]{1,0:T(8,128)S(1)}, f32[64,64]{1,0:T(8,128)}, u32[]{:S(2)}, u32[]{:S(2)}) collective-permute-start(f32[64,64]{1,0:T(8,128)S(1)} %get-tuple-element.18), channel_id=1, source_target_pairs={{0,2},{1,3},{2,0},{3,1},{4,6},{5,7},{6,4},{7,5},{8,10},{9,11},{10,... | collective-permute-start | bytes 49160 | tf_op jit(solution)/shard_map/ppermute | solution.py:315
  29.9 3.4 %collective-permute-start.11 = (f32[64,64]{1,0:T(8,128)S(1)}, f32[64,64]{1,0:T(8,128)}, u32[]{:S(2)}, u32[]{:S(2)}) collective-permute-start(f32[64,64]{1,0:T(8,128)S(1)} %get-tuple-element.19), channel_id=1, source_target_pairs={{0,3},{1,2},{2,1},{3,0},{4,7},{5,6},{6,5},{7,4},{8,11},{9,10},{10,... | collective-permute-start | bytes 49160 | tf_op jit(solution)/shard_map/ppermute | solution.py:315
  33.4 11.2 %copy-start.12 = (bf16[3,256,128]{2,1,0:T(8,128)(2,1)}, bf16[3,256,128]{2,1,0:T(8,128)(2,1)S(1)}, u32[]{:S(2)}) copy-start(bf16[3,256,128]{2,1,0:T(8,128)(2,1)S(1)} %collective-permute-done.12.refs_8_.refs_9_) | copy-start | bytes 589828
  35.5 0.7 copy-start.6
  36.2 0.7 copy-start.8
  36.8 0.7 copy-start.10
  37.5 14.4 %collective-permute-start.19 = (bf16[5,3,64,512]{3,2,1,0:T(8,128)(2,1)S(1)}, bf16[5,3,64,512]{3,2,1,0:T(8,128)(2,1)S(1)}, u32[]{:S(2)}, u32[]{:S(2)}) collective-permute-start(bf16[5,3,64,512]{3,2,1,0:T(8,128)(2,1)S(1)} %cut_columns.4.refs_17_), channel_id=1, source_target_pairs={{0,2},{4,6},{9,11},{13,15},{18,16},{22,20},{27,25},{31,29}} | collective-permute-start | bytes 2949128 | tf_op jit(solution)/shard_map/ppermute | solution.py:351
  40.4 7.9 %collective-permute-start.16 = (bf16[3,256,128]{2,1,0:T(8,128)(2,1)S(1)}, bf16[3,256,128]{2,1,0:T(8,128)(2,1)S(1)}, u32[]{:S(2)}, u32[]{:S(2)}) collective-permute-start(bf16[3,256,128]{2,1,0:T(8,128)(2,1)S(1)} %collective-permute-done.12.refs_8_.refs_9_), channel_id=1, source_target_pairs={{8,0},{16,8},{24,16},{28,24},{20,28},{12,20},{4,12},{0,4},{9,1},{1... | collective-permute-start | bytes 589832 | tf_op jit(solution)/shard_map/ppermute | solution.py:362
  42.1 11.5 %collective-permute-start.14 = (bf16[3,256,128]{2,1,0:T(8,128)(2,1)}, bf16[3,256,128]{2,1,0:T(8,128)(2,1)S(1)}, u32[]{:S(2)}, u32[]{:S(2)}) collective-permute-start(bf16[3,256,128]{2,1,0:T(8,128)(2,1)} %collective-permute-done.7.refs_6_.refs_7_), channel_id=1, source_target_pairs={{0,8},{8,16},{16,24},{24,28},{28,20},{20,12},{12,4},{4,0},{1,9},{9... | collective-permute-start | bytes 589832 | tf_op jit(solution)/shard_map/ppermute | solution.py:361
  42.5 11.1 %collective-permute-start.17 = (bf16[3,256,128]{2,1,0:T(8,128)(2,1)}, bf16[3,256,128]{2,1,0:T(8,128)(2,1)S(1)}, u32[]{:S(2)}, u32[]{:S(2)}) collective-permute-start(bf16[3,256,128]{2,1,0:T(8,128)(2,1)} %collective-permute-done.13.refs_9_.refs_10_), channel_id=1, source_target_pairs={{8,0},{16,8},{24,16},{28,24},{20,28},{12,20},{4,12},{0,4},{9,1},{1... | collective-permute-start | bytes 589832 | tf_op jit(solution)/shard_map/ppermute | solution.py:364
  44.1 9.5 %collective-permute-start.15 = (bf16[3,256,128]{2,1,0:T(8,128)(2,1)}, bf16[3,256,128]{2,1,0:T(8,128)(2,1)S(1)}, u32[]{:S(2)}, u32[]{:S(2)}) collective-permute-start(bf16[3,256,128]{2,1,0:T(8,128)(2,1)} %collective-permute-done.8.refs_7_.refs_8_), channel_id=1, source_target_pairs={{0,8},{8,16},{16,24},{24,28},{28,20},{20,12},{12,4},{4,0},{1,9},{9... | collective-permute-start | bytes 589832 | tf_op jit(solution)/shard_map/ppermute | solution.py:363
  48.3 21.2 %copy-start.18 = (bf16[3,256,128]{2,1,0:T(8,128)(2,1)}, bf16[3,256,128]{2,1,0:T(8,128)(2,1)S(1)}, u32[]{:S(2)}) copy-start(bf16[3,256,128]{2,1,0:T(8,128)(2,1)S(1)} %collective-permute-done.16.refs_2_.refs_13_) | copy-start | bytes 589828
  48.3 26.1 %collective-permute-start.21 = (bf16[5,3,64,512]{3,2,1,0:T(8,128)(2,1)S(1)}, bf16[5,3,64,512]{3,2,1,0:T(8,128)(2,1)S(1)}, u32[]{:S(2)}, u32[]{:S(2)}) collective-permute-start(bf16[5,3,64,512]{3,2,1,0:T(8,128)(2,1)S(1)} %cut_columns.4.refs_17_), channel_id=1, source_target_pairs={{0,1},{4,5},{9,8},{13,12},{18,19},{22,23},{27,26},{31,30}} | collective-permute-start | bytes 2949128 | tf_op jit(solution)/shard_map/ppermute | solution.py:352
  52.0 22.5 %collective-permute-start.22 = (bf16[5,3,64,512]{3,2,1,0:T(8,128)(2,1)S(1)}, bf16[5,3,64,512]{3,2,1,0:T(8,128)(2,1)}, u32[]{:S(2)}, u32[]{:S(2)}) collective-permute-start(bf16[5,3,64,512]{3,2,1,0:T(8,128)(2,1)S(1)} %collective-permute-done.19.refs_19_), channel_id=1, source_target_pairs={{2,3},{6,7},{11,10},{15,14},{16,17},{20,21},{25,24},{29,28}} | collective-permute-start | bytes 2949128 | tf_op jit(solution)/shard_map/ppermute | solution.py:353
  53.6 8.6 %copy-start.20 = (bf16[3,256,128]{2,1,0:T(8,128)(2,1)}, bf16[3,256,128]{2,1,0:T(8,128)(2,1)S(1)}, u32[]{:S(2)}) copy-start(bf16[3,256,128]{2,1,0:T(8,128)(2,1)S(1)} %collective-permute-done.14.refs_0_.refs_11_) | copy-start | bytes 589828
  53.6 8.6 %collective-permute-start.18 = (bf16[3,256,128]{2,1,0:T(8,128)(2,1)S(1)}, bf16[3,256,128]{2,1,0:T(8,128)(2,1)S(1)}, u32[]{:S(2)}, u32[]{:S(2)}) collective-permute-start(bf16[3,256,128]{2,1,0:T(8,128)(2,1)S(1)} %collective-permute-done.14.refs_0_.refs_11_), channel_id=1, source_target_pairs={{0,8},{8,16},{16,24},{24,28},{28,20},{20,12},{12,4},{4,0},{1,9},{9... | collective-permute-start | bytes 589832 | tf_op jit(solution)/shard_map/ppermute | solution.py:377
  53.6 15.9 %copy-start.22 = (bf16[3,256,128]{2,1,0:T(8,128)(2,1)}, bf16[3,256,128]{2,1,0:T(8,128)(2,1)S(1)}, u32[]{:S(2)}) copy-start(bf16[3,256,128]{2,1,0:T(8,128)(2,1)S(1)} %collective-permute-done.17.refs_3_.refs_14_) | copy-start | bytes 589828
  53.6 0.8 copy-start.24
  54.4 15.1 %collective-permute-start.24 = (bf16[2,3,64,512]{3,2,1,0:T(8,128)(2,1)S(1)}, bf16[2,3,64,512]{3,2,1,0:T(8,128)(2,1)}, u32[]{:S(2)}, u32[]{:S(2)}) collective-permute-start(bf16[2,3,64,512]{3,2,1,0:T(8,128)(2,1)S(1)} %cut_columns.3.refs_21_), channel_id=1, source_target_pairs={{0,2},{4,6},{9,11},{13,15},{18,16},{22,20},{27,25},{31,29}} | collective-permute-start | bytes 1179656 | tf_op jit(solution)/shard_map/ppermute | solution.py:351
  60.2 5.7 %collective-permute-start.20 = (bf16[3,256,128]{2,1,0:T(8,128)(2,1)S(1)}, bf16[3,256,128]{2,1,0:T(8,128)(2,1)S(1)}, u32[]{:S(2)}, u32[]{:S(2)}) collective-permute-start(bf16[3,256,128]{2,1,0:T(8,128)(2,1)S(1)} %collective-permute-done.17.refs_3_.refs_14_), channel_id=1, source_target_pairs={{8,0},{16,8},{24,16},{28,24},{20,28},{12,20},{4,12},{0,4},{9,1},{1... | collective-permute-start | bytes 589832 | tf_op jit(solution)/shard_map/ppermute | solution.py:378
  62.2 7.3 %copy-start.14 = (bf16[3,256,128]{2,1,0:T(8,128)(2,1)}, bf16[3,256,128]{2,1,0:T(8,128)(2,1)S(1)}, u32[]{:S(2)}) copy-start(bf16[3,256,128]{2,1,0:T(8,128)(2,1)S(1)} %collective-permute-done.18.refs_0_.refs_15_) | copy-start | bytes 589828
  62.2 8.8 %collective-permute-start.23 = (bf16[2,3,64,512]{3,2,1,0:T(8,128)(2,1)S(1)}, bf16[2,3,64,512]{3,2,1,0:T(8,128)(2,1)}, u32[]{:S(2)}, u32[]{:S(2)}) collective-permute-start(bf16[2,3,64,512]{3,2,1,0:T(8,128)(2,1)S(1)} %cut_columns.3.refs_21_), channel_id=1, source_target_pairs={{0,1},{4,5},{9,8},{13,12},{18,19},{22,23},{27,26},{31,30}} | collective-permute-start | bytes 1179656 | tf_op jit(solution)/shard_map/ppermute | solution.py:352
  65.9 3.7 %copy-start.16 = (bf16[3,256,128]{2,1,0:T(8,128)(2,1)}, bf16[3,256,128]{2,1,0:T(8,128)(2,1)S(1)}, u32[]{:S(2)}) copy-start(bf16[3,256,128]{2,1,0:T(8,128)(2,1)S(1)} %collective-permute-done.20.refs_1_.refs_16_) | copy-start | bytes 589828
  66.9 5.4 %collective-permute-start.27 = (bf16[1,3,64,512]{3,2,1,0:T(8,128)(2,1)}, bf16[1,3,64,512]{3,2,1,0:T(8,128)(2,1)}, u32[]{:S(2)}, u32[]{:S(2)}) collective-permute-start(bf16[1,3,64,512]{3,2,1,0:T(8,128)(2,1)} %cut_columns.5.refs_25_), channel_id=1, source_target_pairs={{0,2},{4,6},{9,11},{13,15},{18,16},{22,20},{27,25},{31,29}} | collective-permute-start | bytes 589832 | tf_op jit(solution)/shard_map/ppermute | solution.py:351
  69.5 4.9 %collective-permute-start.25 = (bf16[2,3,64,512]{3,2,1,0:T(8,128)(2,1)}, bf16[2,3,64,512]{3,2,1,0:T(8,128)(2,1)}, u32[]{:S(2)}, u32[]{:S(2)}) collective-permute-start(bf16[2,3,64,512]{3,2,1,0:T(8,128)(2,1)} %collective-permute-done.24.refs_23_), channel_id=1, source_target_pairs={{2,3},{6,7},{11,10},{15,14},{16,17},{20,21},{25,24},{29,28}} | collective-permute-start | bytes 1179656 | tf_op jit(solution)/shard_map/ppermute | solution.py:353
  71.0 3.5 %collective-permute-start.26 = (bf16[1,3,64,512]{3,2,1,0:T(8,128)(2,1)}, bf16[1,3,64,512]{3,2,1,0:T(8,128)(2,1)S(1)}, u32[]{:S(2)}, u32[]{:S(2)}) collective-permute-start(bf16[1,3,64,512]{3,2,1,0:T(8,128)(2,1)} %cut_columns.5.refs_25_), channel_id=1, source_target_pairs={{0,1},{4,5},{9,8},{13,12},{18,19},{22,23},{27,26},{31,30}} | collective-permute-start | bytes 589832 | tf_op jit(solution)/shard_map/ppermute | solution.py:352
  72.3 2.1 %collective-permute-start.28 = (bf16[1,3,64,512]{3,2,1,0:T(8,128)(2,1)}, bf16[1,3,64,512]{3,2,1,0:T(8,128)(2,1)S(1)}, u32[]{:S(2)}, u32[]{:S(2)}) collective-permute-start(bf16[1,3,64,512]{3,2,1,0:T(8,128)(2,1)} %collective-permute-done.27.refs_27_), channel_id=1, source_target_pairs={{2,3},{6,7},{11,10},{15,14},{16,17},{20,21},{25,24},{29,28}} | collective-permute-start | bytes 589832 | tf_op jit(solution)/shard_map/ppermute | solution.py:353
  74.5 0.9 copy-start.3
  75.4 0.9 copy-start.5
  76.3 0.9 copy-start.7
  77.2 0.9 copy-start.9
  78.2 0.9 copy-start.11
  79.1 0.9 copy-start.13
  80.0 0.9 copy-start.15
  81.0 0.9 copy-start.17
  81.9 0.9 copy-start.19
  82.8 0.9 copy-start.21
  83.7 0.9 copy-start.23
  84.7 0.9 copy-start.25

commit v5 on v4

--- a/solution.py
+++ b/solution.py
@@ -137,24 +137,17 @@
 
 
 def cut_kernel(slots, half_ref, *refs):
-    sources, (cols_ref, held, sem) = refs[: 2 * slots], refs[2 * slots :]
+    sources, cols_ref = refs[: 2 * slots], refs[2 * slots]
+    run, lanes = sources[0].shape[1:]
     for half in range(2):
 
         @pl.when(half_ref[0] == half)
         def _(half=half):
-            run_copies(
-                [
-                    pltpu.make_async_copy(source, held.at[k], sem.at[k])
-                    for k, source in enumerate(sources[half::2])
-                ]
-            )
-
-    run, lanes = held.shape[2:]
-    for k in range(slots):
-        for c in range(3):
-            turned = held[k, c].astype(jnp.float32).T.astype(jnp.bfloat16)
-            cols_ref[k, c, :, :run] = turned[: lanes // 2]
-            cols_ref[k, c, :, run:] = turned[lanes // 2 :]
+            for k, source in enumerate(sources[half::2]):
+                for c in range(3):
+                    turned = source[c].astype(jnp.float32).T.astype(jnp.bfloat16)
+                    cols_ref[k, c, :, :run] = turned[: lanes // 2]
+                    cols_ref[k, c, :, run:] = turned[lanes // 2 :]
 
 
 def side_by_side(first, second):
@@ -169,12 +162,9 @@
     at = 1 + 2 * slots
     groups = [refs[at + k * roles : at + (k + 1) * roles] for k in range(len(lots))]
     at += len(lots) * roles
-    out_ref, rows_in, left, right, done, sem, out_sem = refs[at:]
-    copies = [
-        pltpu.make_async_copy(piece, rows_in.at[k % 2, k // 2], sem.at[k])
-        for k, piece in enumerate(pieces)
-    ]
+    out_ref, left, right, done, out_sem = refs[at:]
     depth = right.shape[1] // slots
+    run = pieces[0].shape[1]
     for role in range(roles):
 
         @pl.when(role_ref[0] == role)
@@ -182,64 +172,51 @@
             to = 0
             for k, count in enumerate(lots):
                 for n in range(count):
-                    pltpu.make_async_copy(
-                        groups[k][role].at[n],
-                        right.at[:, pl.ds(to * depth, depth), :],
-                        sem.at[2 * slots + to],
-                    ).start()
-                    to += 1
-
-    for copy in copies:
-        copy.start()
-    for k in range(slots):
-        part = right.at[:, pl.ds(k * depth, depth), :]
-        pltpu.make_async_copy(part, part, sem.at[2 * slots + k]).wait()
-    for copy in copies:
-        copy.wait()
-    run = rows_in.shape[3]
-
-    def assemble(i, slot):
-        c = lax.div(i, 2)
-        at = lax.rem(i, 2)
+                    for d in range(3):
+                        right[d, to : to + depth, :] = groups[k][role][n, d]
+                    to += depth
+
+    def assemble(c, at):
         for q in range(slots // 2):
-            low, high = side_by_side(rows_in[at, 2 * q, c], rows_in[at, 2 * q + 1, c])
-            left[slot, :run, q * LANES : (q + 1) * LANES] = low
-            left[slot, run:, q * LANES : (q + 1) * LANES] = high
-
-    def write(i, d):
-        start = pl.multiple_of(lax.rem(i, 2) * 2 * run, 2 * run)
-        slot = lax.rem(i, 2)
+            low, high = side_by_side(pieces[4 * q + at][c], pieces[4 * q + 2 + at][c])
+            left[at, :run, q * LANES : (q + 1) * LANES] = low
+            left[at, run:, q * LANES : (q + 1) * LANES] = high
+
+    def write(c, at, d):
         return pltpu.make_async_copy(
-            done.at[slot, d],
-            out_ref.at[lax.div(i, 2), d, pl.ds(start, 2 * run), :],
-            out_sem.at[slot, d],
+            done.at[at, d],
+            out_ref.at[c, d, pl.ds(at * 2 * run, 2 * run), :],
+            out_sem.at[at, d],
         )
 
     assemble(0, 0)
 
-    @pl.loop(0, 6)
-    def _(i):
-        slot = lax.rem(i, 2)
-
-        @pl.when(i >= 2)
-        def _():
+    @pl.loop(0, 3)
+    def _(c):
+        for at in range(2):
+
+            @pl.when(c > 0)
+            def _():
+                for d in range(3):
+                    write(c - 1, at, d).wait()
+
+            assemble(jnp.minimum(c + at, 2), 1 - at)
             for d in range(3):
-                write(i - 2, d).wait()
-
-        assemble(jnp.minimum(i + 1, 5), 1 - slot)
+                done[at, d] = scale * jnp.dot(
+                    left[at], right[d], preferred_element_type=jnp.float32
+                )
+                write(c, at, d).start()
+
+    for at in range(2):
         for d in range(3):
-            done[slot, d] = scale * jnp.dot(
-                left[slot], right[d], preferred_element_type=jnp.float32
-            )
-            write(i, d).start()
-
-    for d in range(3):
-        write(4, d).wait()
-        write(5, d).wait()
+            write(2, at, d).wait()
+
+
+pinned = pltpu.with_memory_space_constraint
 
 
 def after(value, *others):
-    return lax.optimization_barrier((value,) + others)[0]
+    return lax.optimization_barrier((value,) + others)[0] if others else value
 
 
 def ring_order(count):
@@ -270,7 +247,8 @@
     half = lax.rem(me_f, blocks).astype(jnp.int32).reshape(1)
     owner = lax.div(me_f, blocks)
     role = lax.bitwise_xor(me_a, owner).astype(jnp.int32).reshape(1)
-    x = jnp.transpose(frames, (1, 0, 2))
+    x = pinned(jnp.transpose(frames, (1, 0, 2)), pltpu.HBM)
+    mean_structure = pinned(mean_structure, pltpu.HBM)
     x_copy = [
         pltpu.VMEM(x.shape, jnp.float32),
         pltpu.VMEM(mean_structure.shape, jnp.float32),
@@ -311,11 +289,11 @@
         compiler_params=params(8),
         name="project",
     )(me_a.astype(jnp.int32).reshape(1), flat, eigvecs)
-    parts = [shares[0]] + [
-        lax.ppermute(shares[d], "atoms", [(a, a ^ d) for a in range(atom_axis)])
-        for d in range(1, atom_axis)
-    ]
-    projections = sum(parts)
+    def exchange(values):
+        return values[0] + sum(
+            lax.ppermute(values[d], "atoms", [(a, a ^ d) for a in range(atom_axis)])
+            for d in range(1, atom_axis)
+        )
 
     def pairs(source, target):
         return [
@@ -328,29 +306,26 @@
 
     if blocks != 2 or frame_axis != 8:
         spread_pairs = [pairs(0, d) for d in range(1, atom_axis)]
+        projections = exchange(shares)
         covariance = long_axis_covariance(
             flat, half[0], role[0], block, spread_pairs, 1.0 / total_frames
         )
         return covariance, projections
 
-    def spread(pieces):
+    def spread(pieces, earlier, before_last=()):
         slots = len(pieces) // 2
         cut = pl.pallas_call(
             functools.partial(cut_kernel, slots),
-            out_shape=jax.ShapeDtypeStruct((slots, 3, local_frames, block), jnp.bfloat16),
-            in_specs=[SMEM] + [ANY] * len(pieces),
+            out_shape=pltpu.VMEM((slots, 3, local_frames, block), jnp.bfloat16),
+            in_specs=[SMEM] + [VMEM] * len(pieces),
             out_specs=VMEM,
-            scratch_shapes=[
-                pltpu.VMEM((slots,) + piece.shape, jnp.bfloat16),
-                pltpu.SemaphoreType.DMA((slots,)),
-            ],
-            compiler_params=params(8),
+            compiler_params=params(4),
             name="cut_columns",
-        )(half, *pieces)
+        )(after(half, *earlier), *[pinned(piece, pltpu.VMEM) for piece in pieces])
         axes = ("frames", "atoms")
         across = lax.ppermute(cut, axes, pairs(0, 2))
         beside = lax.ppermute(cut, axes, pairs(0, 1))
-        last = lax.ppermute(across, axes, pairs(2, 3))
+        last = lax.ppermute(after(across, *before_last), axes, pairs(2, 3))
         return [cut, beside, across, last]
 
     order = ring_order(frame_axis)
@@ -366,22 +341,17 @@
 
     own = [first, second]
     up1, down1 = hop(own, own)
-    up1[0] = after(up1[0], *shares)
     up2, down2 = hop(up1, down1)
-    up2[1] = after(up2[1], *parts)
     up3, down3 = hop(up2, down2)
-    lots = [own + up1 + down1 + up2 + down2, up3 + down3]
-    cuts = [spread(lots[0])]
-    down3[1] = after(down3[1], cuts[0][0])
     far = [
         lax.ppermute(up3[0], "frames", forward),
         lax.ppermute(down3[1], "frames", backward),
     ]
-    cuts.append(spread(lots[1]))
-    far[0] = after(far[0], cuts[1][0], cuts[0][2])
-    lots.append(far)
-    cuts.append(spread(far))
+    lots = [own + up1 + down1, up2 + down2, up3 + down3, far]
+    cuts = [spread(lots[0], shares), spread(lots[1], []), spread(lots[2], [])]
+    cuts.append(spread(far, [], cuts[0][1:]))
     cuts = sum(cuts, [])
+    projections = exchange([after(value, cuts[-4]) for value in shares])
     pieces = sum(lots, [])
     counts = [len(lot) // 2 for lot in lots]
     covariance = pl.pallas_call(
@@ -389,14 +359,12 @@
             covariance_kernel, frame_axis, atom_axis, counts, 1.0 / total_frames
         ),
         out_shape=jax.ShapeDtypeStruct((3, 3, local_atoms, block), jnp.float32),
-        in_specs=[SMEM] + [ANY] * (len(pieces) + len(cuts)),
+        in_specs=[SMEM] + [VMEM] * (len(pieces) + len(cuts)),
         out_specs=ANY,
         scratch_shapes=[
-            pltpu.VMEM((2, frame_axis) + piece.shape, jnp.bfloat16),
             pltpu.VMEM((2, 2 * run, total_frames), jnp.bfloat16),
             pltpu.VMEM((3, total_frames, block), jnp.bfloat16),
             pltpu.VMEM((2, 3, 2 * run, block), jnp.float32),
-            pltpu.SemaphoreType.DMA((len(pieces) + frame_axis,)),
             pltpu.SemaphoreType.DMA((2, 3)),
         ],
         compiler_params=params(24),
@@ -406,7 +374,7 @@
             transcendentals=0,
         ),
         name="covariance_tile",
-    )(role, *pieces, *cuts)
+    )(role, *[pinned(value, pltpu.VMEM) for value in pieces + cuts])
     return jnp.transpose(covariance, (0, 2, 1, 3)), projections
 
 

time: 99.4 us -> 93.3 us (0.939)
  waiting for transfers between devices: 23.5 us -> 19.4 us
  Pallas kernels: 18.2 us -> 14.1 us
  starting transfers between devices: 37.7 us -> 40.9 us
    ppermute x3, waiting for transfers between devices: 1.89 us -> 7.29 us  [hop(): up_a = lax.ppermute(up[0], 'frames', forward)]
    ppermute x6 -> x7, waiting for transfers between devices: 8.1 us -> 2.74 us  [the longest x3 2.73 us: exchange(): lax.ppermute(values[d], 'atoms', [(a, a ^ d) for a in range(atom_axis)])]
    ppermute x3, waiting for transfers between devices: 0.01 us -> 3.83 us  [hop(): down_b = lax.ppermute(down[1], 'frames', backward)]
    pallas_call x1, Pallas kernels: 12.7 us -> 9.04 us  [per_device(): pl.pallas_call(functools.partial(covariance_kernel, frame_axis, atom_axis...]
    pallas_call x3 -> x4, Pallas kernels: 3.85 us -> 0.74 us  [spread(): pl.pallas_call(functools.partial(cut_kernel, slots), out_shape=pltpu.VMEM...]
    ppermute x3, starting transfers between devices: 3.61 us -> 0.57 us  [hop(): up_a = lax.ppermute(up[0], 'frames', forward)]
    ppermute x3, waiting for transfers between devices: 3.78 us -> 0.79 us  [hop(): down_a = lax.ppermute(down[0], 'frames', backward)]
    ppermute x3, starting transfers between devices: 2.57 us -> 5.48 us  [hop(): down_a = lax.ppermute(down[0], 'frames', backward)]
  transfers between devices with their start and end apart: 29 -> 32, of which waited for: 10 -> 14; matrix products, arithmetic and copies ran while one was open for 1% -> 2% of each run, Pallas kernels for 2% -> 2%
where the time goes in v5:
time: 93.3 us; the launch traced here: 92.5 us
  starting transfers between devices  40.9 us (44%)
  waiting for transfers between devices  19.4 us (21%)
  local copies, waits for them, and re-layouts  15.7 us (17%)
  Pallas kernels  14.1 us (15%)
  other arithmetic  1.43 us (2%)
    unnamed x50, local copies, waits for them, and re-layouts  15.7 us
    ppermute x4, starting transfers between devices, spread(): across = lax.ppermute(cut, axes, pairs(0, 2))  12.6 us
    pallas_call x1, Pallas kernels, per_device(): pl.pallas_call(functools.partial(covariance_kernel, frame_axis, atom_axis...  9.04 us
    ppermute x3, waiting for transfers between devices, hop(): up_a = lax.ppermute(up[0], 'frames', forward)  7.29 us
    ppermute x4, starting transfers between devices, spread(): beside = lax.ppermute(cut, axes, pairs(0, 1))  7.1 us
    ppermute x3, starting transfers between devices, hop(): down_a = lax.ppermute(down[0], 'frames', backward)  5.48 us
    ppermute x3, starting transfers between devices, hop(): down_b = lax.ppermute(down[1], 'frames', backward)  4.23 us
    ppermute x4, starting transfers between devices, spread(): last = lax.ppermute(after(across, *before_last), axes, pairs(2, 3))  4.19 us
  transfers between devices with their start and end apart: 32, of which 14 were waited for; matrix products, arithmetic and copies ran while one was open for 2% of the time, Pallas kernels for 2%

profile of v5, /device:TPU:0, one launch (start us, length us, event | category | flops | bytes accessed | tf_op | source)
XLA Modules:
  0.0 92.5 jit_solution(17679113753933992707)
XLA Ops:
  0.6 1.6 %local_moments.1.refs_0_ = f32[24,64]{1,0:T(8,128)S(1)} custom-call(f32[3,64,1024]{2,1,0:T(8,128)} %bitcast.6, f32[3,1024]{1,0:T(4,128)} %refs_5_.1), custom_call_target="tpu_custom_call" | custom-call | tf_op jit(solution)/shard_map/local_moments/pallas_call | solution.py:257
  2.3 2.4 %collective-permute-start.2 = (f32[24,64]{1,0:T(8,128)S(1)}, f32[24,64]{1,0:T(8,128)S(1)}, u32[]{:S(2)}, u32[]{:S(2)}) collective-permute-start(f32[24,64]{1,0:T(8,128)S(1)} %local_moments.1.refs_0_), channel_id=1, source_target_pairs={{0,3},{1,2},{2,1},{3,0},{4,7},{5,6},{6,5},{7,4},{8,11},{9,10},{10,... | collective-permute-start | bytes 18440 | tf_op jit(solution)/shard_map/ppermute | solution.py:267
  4.7 0.6 collective-permute-start.1
  5.4 0.7 collective-permute-done.2.refs_3_
  6.1 2.3 %collective-permute-done.1.refs_2_ = f32[24,64]{1,0:T(8,128)S(1)} collective-permute-done((f32[24,64]{1,0:T(8,128)S(1)}, f32[24,64]{1,0:T(8,128)S(1)}, u32[]{:S(2)}, u32[]{:S(2)}) %collective-permute-start.1) | collective-permute-done | bytes 6176 | tf_op jit(solution)/shard_map/ppermute | solution.py:267
  8.4 1.6 %polar_align.1 = (bf16[3,256,128]{2,1,0:T(8,128)(2,1)S(1)}, bf16[3,256,128]{2,1,0:T(8,128)(2,1)S(1)}, bf16[3,64,1024]{2,1,0:T(8,128)(2,1)S(1)}) custom-call(f32[24,64]{1,0:T(8,128)S(1)} %local_moments.1.refs_0_, f32[24,64]{1,0:T(8,128)S(1)} %collective-permute-done.refs_1_, f32[24,64]{1,0:T(8,128)S(1)} %collective-permute-done.1.refs_2_, ...), custom_call_target="tpu_custom_call" | custom-call | tf_op jit(solution)/shard_map/polar_align/pallas_call | solution.py:272
  10.0 1.6 %collective-permute-start.5 = (bf16[3,256,128]{2,1,0:T(8,128)(2,1)S(1)}, bf16[3,256,128]{2,1,0:T(8,128)(2,1)S(1)}, u32[]{:S(2)}, u32[]{:S(2)}) collective-permute-start(bf16[3,256,128]{2,1,0:T(8,128)(2,1)S(1)} %get-tuple-element.15.refs_0_.refs_1_), channel_id=1, source_target_pairs={{8,0},{16,8},{24,16},{28,24},{20,28},{12,20},{4,12},{0,4},{9,1},{1... | collective-permute-start | bytes 589832 | tf_op jit(solution)/shard_map/ppermute | solution.py:337
  11.6 0.5 collective-permute-start.3
  12.1 1.5 %collective-permute-start.6 = (bf16[3,256,128]{2,1,0:T(8,128)(2,1)S(1)}, bf16[3,256,128]{2,1,0:T(8,128)(2,1)S(1)}, u32[]{:S(2)}, u32[]{:S(2)}) collective-permute-start(bf16[3,256,128]{2,1,0:T(8,128)(2,1)S(1)} %get-tuple-element.16.refs_1_.refs_2_), channel_id=1, source_target_pairs={{8,0},{16,8},{24,16},{28,24},{20,28},{12,20},{4,12},{0,4},{9,1},{1... | collective-permute-start | bytes 589832 | tf_op jit(solution)/shard_map/ppermute | solution.py:339
  13.6 0.5 collective-permute-start.4
  14.1 1.4 %copy-done = bf16[3,1024,256]{2,1,0:T(8,128)(2,1)S(1)} copy-done((bf16[3,1024,256]{2,1,0:T(8,128)(2,1)S(1)}, bf16[3,1024,256]{2,1,0:T(8,128)(2,1)}, u32[]{:S(2)}) %copy-start) | copy-done | bytes 1572888
  15.5 1.1 %project.1 = (f32[64,64]{1,0:T(8,128)S(1)}, f32[64,64]{1,0:T(8,128)S(1)}, f32[64,64]{1,0:T(8,128)}, f32[64,64]{1,0:T(8,128)}) custom-call(s32[1]{0:T(128)} %bitcast.3.me_ref, bf16[3,64,1024]{2,1,0:T(8,128)(2,1)S(1)} %get-tuple-element.17.flat_ref, bf16[3,1024,256]{2,1,0:T(8,128)(2,1)S(1)} %copy-done), custom_call_target="tpu_custom_call" | custom-call | tf_op jit(solution)/shard_map/project/pallas_call | solution.py:283
  16.6 0.6 copy-done.23
  17.3 0.7 collective-permute-done.5.refs_4_.refs_5_
  17.9 1.5 %collective-permute-done.3.refs_2_.refs_3_ = bf16[3,256,128]{2,1,0:T(8,128)(2,1)S(1)} collective-permute-done((bf16[3,256,128]{2,1,0:T(8,128)(2,1)S(1)}, bf16[3,256,128]{2,1,0:T(8,128)(2,1)S(1)}, u32[]{:S(2)}, u32[]{:S(2)}) %collective-permute-start.3) | collective-permute-done | bytes 196640 | tf_op jit(solution)/shard_map/ppermute | solution.py:336
  19.4 1.2 %collective-permute-done.6.refs_5_.refs_6_ = bf16[3,256,128]{2,1,0:T(8,128)(2,1)S(1)} collective-permute-done((bf16[3,256,128]{2,1,0:T(8,128)(2,1)S(1)}, bf16[3,256,128]{2,1,0:T(8,128)(2,1)S(1)}, u32[]{:S(2)}, u32[]{:S(2)}) %collective-permute-start.6) | collective-permute-done | bytes 196640 | tf_op jit(solution)/shard_map/ppermute | solution.py:339
  20.6 1.2 %collective-permute-done.4.refs_3_.refs_4_ = bf16[3,256,128]{2,1,0:T(8,128)(2,1)S(1)} collective-permute-done((bf16[3,256,128]{2,1,0:T(8,128)(2,1)S(1)}, bf16[3,256,128]{2,1,0:T(8,128)(2,1)S(1)}, u32[]{:S(2)}, u32[]{:S(2)}) %collective-permute-start.4) | collective-permute-done | bytes 196640 | tf_op jit(solution)/shard_map/ppermute | solution.py:338
  21.9 0.2 cut_columns.4.refs_17_
  22.1 2.6 %collective-permute-start.18 = (bf16[3,3,64,512]{3,2,1,0:T(8,128)(2,1)S(1)}, bf16[3,3,64,512]{3,2,1,0:T(8,128)(2,1)S(1)}, u32[]{:S(2)}, u32[]{:S(2)}) collective-permute-start(bf16[3,3,64,512]{3,2,1,0:T(8,128)(2,1)S(1)} %cut_columns.4.refs_17_), channel_id=1, source_target_pairs={{0,2},{4,6},{9,11},{13,15},{18,16},{22,20},{27,25},{31,29}} | collective-permute-start | bytes 1769480 | tf_op jit(solution)/shard_map/ppermute | solution.py:326
  24.8 2.0 %collective-permute-start.9 = (bf16[3,256,128]{2,1,0:T(8,128)(2,1)S(1)}, bf16[3,256,128]{2,1,0:T(8,128)(2,1)S(1)}, u32[]{:S(2)}, u32[]{:S(2)}) collective-permute-start(bf16[3,256,128]{2,1,0:T(8,128)(2,1)S(1)} %collective-permute-done.5.refs_4_.refs_5_), channel_id=1, source_target_pairs={{8,0},{16,8},{24,16},{28,24},{20,28},{12,20},{4,12},{0,4},{9,1},{1... | collective-permute-start | bytes 589832 | tf_op jit(solution)/shard_map/ppermute | solution.py:337
  26.8 1.6 %collective-permute-start.10 = (bf16[3,256,128]{2,1,0:T(8,128)(2,1)S(1)}, bf16[3,256,128]{2,1,0:T(8,128)(2,1)S(1)}, u32[]{:S(2)}, u32[]{:S(2)}) collective-permute-start(bf16[3,256,128]{2,1,0:T(8,128)(2,1)S(1)} %collective-permute-done.6.refs_5_.refs_6_), channel_id=1, source_target_pairs={{8,0},{16,8},{24,16},{28,24},{20,28},{12,20},{4,12},{0,4},{9,1},{1... | collective-permute-start | bytes 589832 | tf_op jit(solution)/shard_map/ppermute | solution.py:339
  28.4 0.5 collective-permute-start.8
  28.9 3.7 %collective-permute-done.7.refs_0_.refs_7_ = bf16[3,256,128]{2,1,0:T(8,128)(2,1)S(1)} collective-permute-done((bf16[3,256,128]{2,1,0:T(8,128)(2,1)S(1)}, bf16[3,256,128]{2,1,0:T(8,128)(2,1)S(1)}, u32[]{:S(2)}, u32[]{:S(2)}) %collective-permute-start.7) | collective-permute-done | bytes 196640 | tf_op jit(solution)/shard_map/ppermute | solution.py:336
  32.6 0.1 collective-permute-done.9.refs_2_.refs_9_
  32.7 1.9 %collective-permute-start.13 = (bf16[3,256,128]{2,1,0:T(8,128)(2,1)S(1)}, bf16[3,256,128]{2,1,0:T(8,128)(2,1)S(1)}, u32[]{:S(2)}, u32[]{:S(2)}) collective-permute-start(bf16[3,256,128]{2,1,0:T(8,128)(2,1)S(1)} %collective-permute-done.9.refs_2_.refs_9_), channel_id=1, source_target_pairs={{8,0},{16,8},{24,16},{28,24},{20,28},{12,20},{4,12},{0,4},{9,1},{1... | collective-permute-start | bytes 589832 | tf_op jit(solution)/shard_map/ppermute | solution.py:337
  34.6 2.3 %collective-permute-done.10.refs_3_.refs_10_ = bf16[3,256,128]{2,1,0:T(8,128)(2,1)S(1)} collective-permute-done((bf16[3,256,128]{2,1,0:T(8,128)(2,1)S(1)}, bf16[3,256,128]{2,1,0:T(8,128)(2,1)S(1)}, u32[]{:S(2)}, u32[]{:S(2)}) %collective-permute-start.10) | collective-permute-done | bytes 196640 | tf_op jit(solution)/shard_map/ppermute | solution.py:339
  36.9 1.1 %collective-permute-start.14 = (bf16[3,256,128]{2,1,0:T(8,128)(2,1)S(1)}, bf16[3,256,128]{2,1,0:T(8,128)(2,1)S(1)}, u32[]{:S(2)}, u32[]{:S(2)}) collective-permute-start(bf16[3,256,128]{2,1,0:T(8,128)(2,1)S(1)} %collective-permute-done.10.refs_3_.refs_10_), channel_id=1, source_target_pairs={{8,0},{16,8},{24,16},{28,24},{20,28},{12,20},{4,12},{0,4},{9,1},{1... | collective-permute-start | bytes 589832 | tf_op jit(solution)/shard_map/ppermute | solution.py:339
  38.1 0.9 collective-permute-start.12
  39.0 2.0 %collective-permute-done.11.refs_0_.refs_11_ = bf16[3,256,128]{2,1,0:T(8,128)(2,1)S(1)} collective-permute-done((bf16[3,256,128]{2,1,0:T(8,128)(2,1)S(1)}, bf16[3,256,128]{2,1,0:T(8,128)(2,1)S(1)}, u32[]{:S(2)}, u32[]{:S(2)}) %collective-permute-start.11) | collective-permute-done | bytes 196640 | tf_op jit(solution)/shard_map/ppermute | solution.py:336
  41.0 1.3 %collective-permute-start.17 = (bf16[3,3,64,512]{3,2,1,0:T(8,128)(2,1)S(1)}, bf16[3,3,64,512]{3,2,1,0:T(8,128)(2,1)S(1)}, u32[]{:S(2)}, u32[]{:S(2)}) collective-permute-start(bf16[3,3,64,512]{3,2,1,0:T(8,128)(2,1)S(1)} %cut_columns.4.refs_17_), channel_id=1, source_target_pairs={{0,1},{4,5},{9,8},{13,12},{18,19},{22,23},{27,26},{31,30}} | collective-permute-start | bytes 1769480 | tf_op jit(solution)/shard_map/ppermute | solution.py:327
  42.4 0.3 collective-permute-done.14.refs_3_.refs_14_
  42.7 1.7 %collective-permute-start.16 = (bf16[3,256,128]{2,1,0:T(8,128)(2,1)S(1)}, bf16[3,256,128]{2,1,0:T(8,128)(2,1)S(1)}, u32[]{:S(2)}, u32[]{:S(2)}) collective-permute-start(bf16[3,256,128]{2,1,0:T(8,128)(2,1)S(1)} %collective-permute-done.14.refs_3_.refs_14_), channel_id=1, source_target_pairs={{8,0},{16,8},{24,16},{28,24},{20,28},{12,20},{4,12},{0,4},{9,1},{1... | collective-permute-start | bytes 589832 | tf_op jit(solution)/shard_map/ppermute | solution.py:348
  44.4 0.2 cut_columns.5.refs_21_
  44.6 0.4 collective-permute-done.12.refs_1_.refs_12_
  45.0 3.4 %collective-permute-start.21 = (bf16[2,3,64,512]{3,2,1,0:T(8,128)(2,1)S(1)}, bf16[2,3,64,512]{3,2,1,0:T(8,128)(2,1)}, u32[]{:S(2)}, u32[]{:S(2)}) collective-permute-start(bf16[2,3,64,512]{3,2,1,0:T(8,128)(2,1)S(1)} %cut_columns.5.refs_21_), channel_id=1, source_target_pairs={{0,2},{4,6},{9,11},{13,15},{18,16},{22,20},{27,25},{31,29}} | collective-permute-start | bytes 1179656 | tf_op jit(solution)/shard_map/ppermute | solution.py:326
  48.5 0.7 collective-permute-start.19
  49.2 1.3 %collective-permute-start.20 = (bf16[2,3,64,512]{3,2,1,0:T(8,128)(2,1)S(1)}, bf16[2,3,64,512]{3,2,1,0:T(8,128)(2,1)S(1)}, u32[]{:S(2)}, u32[]{:S(2)}) collective-permute-start(bf16[2,3,64,512]{3,2,1,0:T(8,128)(2,1)S(1)} %cut_columns.5.refs_21_), channel_id=1, source_target_pairs={{0,1},{4,5},{9,8},{13,12},{18,19},{22,23},{27,26},{31,30}} | collective-permute-start | bytes 1179656 | tf_op jit(solution)/shard_map/ppermute | solution.py:327
  50.5 0.2 cut_columns.6.refs_25_
  50.7 2.0 %collective-permute-start.24 = (bf16[2,3,64,512]{3,2,1,0:T(8,128)(2,1)S(1)}, bf16[2,3,64,512]{3,2,1,0:T(8,128)(2,1)}, u32[]{:S(2)}, u32[]{:S(2)}) collective-permute-start(bf16[2,3,64,512]{3,2,1,0:T(8,128)(2,1)S(1)} %cut_columns.6.refs_25_), channel_id=1, source_target_pairs={{0,2},{4,6},{9,11},{13,15},{18,16},{22,20},{27,25},{31,29}} | collective-permute-start | bytes 1179656 | tf_op jit(solution)/shard_map/ppermute | solution.py:326
  52.7 0.1 cut_columns.7.refs_29_
  53.0 4.5 %collective-permute-start.27 = (bf16[1,3,64,512]{3,2,1,0:T(8,128)(2,1)S(1)}, bf16[1,3,64,512]{3,2,1,0:T(8,128)(2,1)S(1)}, u32[]{:S(2)}, u32[]{:S(2)}) collective-permute-start(bf16[1,3,64,512]{3,2,1,0:T(8,128)(2,1)S(1)} %cut_columns.7.refs_29_), channel_id=1, source_target_pairs={{0,2},{4,6},{9,11},{13,15},{18,16},{22,20},{27,25},{31,29}} | collective-permute-start | bytes 589832 | tf_op jit(solution)/shard_map/ppermute | solution.py:326
  57.5 0.7 copy-done.19
  58.2 0.8 copy-done.15
  59.0 3.2 %collective-permute-start.23 = (bf16[2,3,64,512]{3,2,1,0:T(8,128)(2,1)S(1)}, bf16[2,3,64,512]{3,2,1,0:T(8,128)(2,1)}, u32[]{:S(2)}, u32[]{:S(2)}) collective-permute-start(bf16[2,3,64,512]{3,2,1,0:T(8,128)(2,1)S(1)} %cut_columns.6.refs_25_), channel_id=1, source_target_pairs={{0,1},{4,5},{9,8},{13,12},{18,19},{22,23},{27,26},{31,30}} | collective-permute-start | bytes 1179656 | tf_op jit(solution)/shard_map/ppermute | solution.py:327
  62.2 1.4 %collective-permute-start.22 = (bf16[2,3,64,512]{3,2,1,0:T(8,128)(2,1)}, bf16[2,3,64,512]{3,2,1,0:T(8,128)(2,1)}, u32[]{:S(2)}, u32[]{:S(2)}) collective-permute-start(bf16[2,3,64,512]{3,2,1,0:T(8,128)(2,1)} %collective-permute-done.21.refs_23_), channel_id=1, source_target_pairs={{2,3},{6,7},{11,10},{15,14},{16,17},{20,21},{25,24},{29,28}} | collective-permute-start | bytes 1179656 | tf_op jit(solution)/shard_map/ppermute | solution.py:328
  63.6 1.4 %collective-permute-start.25 = (bf16[2,3,64,512]{3,2,1,0:T(8,128)(2,1)}, bf16[2,3,64,512]{3,2,1,0:T(8,128)(2,1)}, u32[]{:S(2)}, u32[]{:S(2)}) collective-permute-start(bf16[2,3,64,512]{3,2,1,0:T(8,128)(2,1)} %collective-permute-done.24.refs_27_), channel_id=1, source_target_pairs={{2,3},{6,7},{11,10},{15,14},{16,17},{20,21},{25,24},{29,28}} | collective-permute-start | bytes 1179656 | tf_op jit(solution)/shard_map/ppermute | solution.py:328
  65.1 0.6 copy-done.21
  65.8 0.8 copy-done.17
  66.6 2.7 %collective-permute-done.30 = f32[64,64]{1,0:T(8,128)} collective-permute-done((f32[64,64]{1,0:T(8,128)}, f32[64,64]{1,0:T(8,128)}, u32[]{:S(2)}, u32[]{:S(2)}) %collective-permute-start.30) | collective-permute-done | bytes 16416 | tf_op jit(solution)/shard_map/ppermute | solution.py:294
  69.3 1.3 %collective-permute-start.26 = (bf16[1,3,64,512]{3,2,1,0:T(8,128)(2,1)S(1)}, bf16[1,3,64,512]{3,2,1,0:T(8,128)(2,1)S(1)}, u32[]{:S(2)}, u32[]{:S(2)}) collective-permute-start(bf16[1,3,64,512]{3,2,1,0:T(8,128)(2,1)S(1)} %cut_columns.7.refs_29_), channel_id=1, source_target_pairs={{0,1},{4,5},{9,8},{13,12},{18,19},{22,23},{27,26},{31,30}} | collective-permute-start | bytes 589832 | tf_op jit(solution)/shard_map/ppermute | solution.py:327
  70.6 0.7 collective-permute-start.28
  71.3 1.4 %add_add_fusion = f32[64,64]{1,0:T(8,128)} fusion(f32[64,64]{1,0:T(8,128)} %copy-done.23, f32[64,64]{1,0:T(8,128)} %collective-permute-done.31, f32[64,64]{1,0:T(8,128)} %copy-done.24, f32[64,64]{1,0:T(8,128)} %collective-permute-done.30), kind=kLoop, calls=%fused_computation | loop fusion | flops 12288 | bytes 81920 | tf_op jit(solution)/shard_map/add | solution.py:293
  72.8 0.9 copy-done.2
  73.7 0.9 copy-done.4
  74.6 0.9 copy-done.6
  75.5 0.9 copy-done.8
  76.5 0.9 copy-done.10
  77.4 0.9 copy-done.12
  78.3 1.1 %copy-done.14 = bf16[3,3,64,512]{3,2,1,0:T(8,128)(2,1)S(1)} copy-done((bf16[3,3,64,512]{3,2,1,0:T(8,128)(2,1)S(1)}, bf16[3,3,64,512]{3,2,1,0:T(8,128)(2,1)}, u32[]{:S(2)}) %copy-start.14) | copy-done | bytes 589848
  79.4 1.1 %copy-done.16 = bf16[3,3,64,512]{3,2,1,0:T(8,128)(2,1)S(1)} copy-done((bf16[3,3,64,512]{3,2,1,0:T(8,128)(2,1)S(1)}, bf16[3,3,64,512]{3,2,1,0:T(8,128)(2,1)}, u32[]{:S(2)}) %copy-start.16) | copy-done | bytes 589848
  80.5 1.1 %copy-done.18 = bf16[3,3,64,512]{3,2,1,0:T(8,128)(2,1)S(1)} copy-done((bf16[3,3,64,512]{3,2,1,0:T(8,128)(2,1)S(1)}, bf16[3,3,64,512]{3,2,1,0:T(8,128)(2,1)}, u32[]{:S(2)}) %copy-start.18) | copy-done | bytes 589848
  81.5 1.0 %copy-done.20 = bf16[2,3,64,512]{3,2,1,0:T(8,128)(2,1)S(1)} copy-done((bf16[2,3,64,512]{3,2,1,0:T(8,128)(2,1)S(1)}, bf16[2,3,64,512]{3,2,1,0:T(8,128)(2,1)}, u32[]{:S(2)}) %copy-start.20) | copy-done | bytes 393240
  82.5 0.9 copy-done.22
  83.4 9.0 %covariance_tile.1 = f32[3,3,1024,512]{3,2,1,0:T(8,128)} custom-call(s32[1]{0:T(128)} %bitcast.refs_0_, bf16[3,256,128]{2,1,0:T(8,128)(2,1)S(1)} %get-tuple-element.15.refs_0_.refs_1_, bf16[3,256,128]{2,1,0:T(8,128)(2,1)S(1)} %get-tuple-element.16.refs_1_.refs_2_, bf16[3,256,128]{2,1,0:T(8,128)(2,1)S(1)} %collective-permute-done.3.refs_2_.refs_3_, ...), custom_call_target="tpu_custom_call" | custom-call | flops 4831838208 | bytes 25165824 | tf_op jit(solution)/shard_map/covariance_tile/pallas_call | solution.py:357
  (59 shorter events, 0.3 us)
Async XLA Ops:
  2.3 3.8 %collective-permute-start.2 = (f32[24,64]{1,0:T(8,128)S(1)}, f32[24,64]{1,0:T(8,128)S(1)}, u32[]{:S(2)}, u32[]{:S(2)}) collective-permute-start(f32[24,64]{1,0:T(8,128)S(1)} %local_moments.1.refs_0_), channel_id=1, source_target_pairs={{0,3},{1,2},{2,1},{3,0},{4,7},{5,6},{6,5},{7,4},{8,11},{9,10},{10,... | collective-permute-start | bytes 18440 | tf_op jit(solution)/shard_map/ppermute | solution.py:267
  4.7 3.7 %collective-permute-start.1 = (f32[24,64]{1,0:T(8,128)S(1)}, f32[24,64]{1,0:T(8,128)S(1)}, u32[]{:S(2)}, u32[]{:S(2)}) collective-permute-start(f32[24,64]{1,0:T(8,128)S(1)} %local_moments.1.refs_0_), channel_id=1, source_target_pairs={{0,2},{1,3},{2,0},{3,1},{4,6},{5,7},{6,4},{7,5},{8,10},{9,11},{10,... | collective-permute-start | bytes 18440 | tf_op jit(solution)/shard_map/ppermute | solution.py:267
  5.4 3.1 %collective-permute-start = (f32[24,64]{1,0:T(8,128)S(1)}, f32[24,64]{1,0:T(8,128)S(1)}, u32[]{:S(2)}, u32[]{:S(2)}) collective-permute-start(f32[24,64]{1,0:T(8,128)S(1)} %local_moments.1.refs_0_), channel_id=1, source_target_pairs={{0,1},{1,0},{2,3},{3,2},{4,5},{5,4},{6,7},{7,6},{8,9},{9,8},{10,11... | collective-permute-start | bytes 18440 | tf_op jit(solution)/shard_map/ppermute | solution.py:267
  10.0 7.9 %collective-permute-start.5 = (bf16[3,256,128]{2,1,0:T(8,128)(2,1)S(1)}, bf16[3,256,128]{2,1,0:T(8,128)(2,1)S(1)}, u32[]{:S(2)}, u32[]{:S(2)}) collective-permute-start(bf16[3,256,128]{2,1,0:T(8,128)(2,1)S(1)} %get-tuple-element.15.refs_0_.refs_1_), channel_id=1, source_target_pairs={{8,0},{16,8},{24,16},{28,24},{20,28},{12,20},{4,12},{0,4},{9,1},{1... | collective-permute-start | bytes 589832 | tf_op jit(solution)/shard_map/ppermute | solution.py:337
  11.6 7.8 %collective-permute-start.3 = (bf16[3,256,128]{2,1,0:T(8,128)(2,1)S(1)}, bf16[3,256,128]{2,1,0:T(8,128)(2,1)S(1)}, u32[]{:S(2)}, u32[]{:S(2)}) collective-permute-start(bf16[3,256,128]{2,1,0:T(8,128)(2,1)S(1)} %get-tuple-element.15.refs_0_.refs_1_), channel_id=1, source_target_pairs={{0,8},{8,16},{16,24},{24,28},{28,20},{20,12},{12,4},{4,0},{1,9},{9... | collective-permute-start | bytes 589832 | tf_op jit(solution)/shard_map/ppermute | solution.py:336
  12.1 8.5 %collective-permute-start.6 = (bf16[3,256,128]{2,1,0:T(8,128)(2,1)S(1)}, bf16[3,256,128]{2,1,0:T(8,128)(2,1)S(1)}, u32[]{:S(2)}, u32[]{:S(2)}) collective-permute-start(bf16[3,256,128]{2,1,0:T(8,128)(2,1)S(1)} %get-tuple-element.16.refs_1_.refs_2_), channel_id=1, source_target_pairs={{8,0},{16,8},{24,16},{28,24},{20,28},{12,20},{4,12},{0,4},{9,1},{1... | collective-permute-start | bytes 589832 | tf_op jit(solution)/shard_map/ppermute | solution.py:339
  13.6 8.2 %collective-permute-start.4 = (bf16[3,256,128]{2,1,0:T(8,128)(2,1)S(1)}, bf16[3,256,128]{2,1,0:T(8,128)(2,1)S(1)}, u32[]{:S(2)}, u32[]{:S(2)}) collective-permute-start(bf16[3,256,128]{2,1,0:T(8,128)(2,1)S(1)} %get-tuple-element.16.refs_1_.refs_2_), channel_id=1, source_target_pairs={{0,8},{8,16},{16,24},{24,28},{28,20},{20,12},{12,4},{4,0},{1,9},{9... | collective-permute-start | bytes 589832 | tf_op jit(solution)/shard_map/ppermute | solution.py:338
  14.1 1.4 %copy-start = (bf16[3,1024,256]{2,1,0:T(8,128)(2,1)S(1)}, bf16[3,1024,256]{2,1,0:T(8,128)(2,1)}, u32[]{:S(2)}) copy-start(bf16[3,1024,256]{2,1,0:T(8,128)(2,1)} %eig_ref.1) | copy-start | bytes 4718596
  16.6 0.6 copy-start.23
  22.1 26.3 %collective-permute-start.18 = (bf16[3,3,64,512]{3,2,1,0:T(8,128)(2,1)S(1)}, bf16[3,3,64,512]{3,2,1,0:T(8,128)(2,1)S(1)}, u32[]{:S(2)}, u32[]{:S(2)}) collective-permute-start(bf16[3,3,64,512]{3,2,1,0:T(8,128)(2,1)S(1)} %cut_columns.4.refs_17_), channel_id=1, source_target_pairs={{0,2},{4,6},{9,11},{13,15},{18,16},{22,20},{27,25},{31,29}} | collective-permute-start | bytes 1769480 | tf_op jit(solution)/shard_map/ppermute | solution.py:326
  24.8 7.8 %collective-permute-start.7 = (bf16[3,256,128]{2,1,0:T(8,128)(2,1)S(1)}, bf16[3,256,128]{2,1,0:T(8,128)(2,1)S(1)}, u32[]{:S(2)}, u32[]{:S(2)}) collective-permute-start(bf16[3,256,128]{2,1,0:T(8,128)(2,1)S(1)} %collective-permute-done.3.refs_2_.refs_3_), channel_id=1, source_target_pairs={{0,8},{8,16},{16,24},{24,28},{28,20},{20,12},{12,4},{4,0},{1,9},{9... | collective-permute-start | bytes 589832 | tf_op jit(solution)/shard_map/ppermute | solution.py:336
  24.8 7.9 %collective-permute-start.9 = (bf16[3,256,128]{2,1,0:T(8,128)(2,1)S(1)}, bf16[3,256,128]{2,1,0:T(8,128)(2,1)S(1)}, u32[]{:S(2)}, u32[]{:S(2)}) collective-permute-start(bf16[3,256,128]{2,1,0:T(8,128)(2,1)S(1)} %collective-permute-done.5.refs_4_.refs_5_), channel_id=1, source_target_pairs={{8,0},{16,8},{24,16},{28,24},{20,28},{12,20},{4,12},{0,4},{9,1},{1... | collective-permute-start | bytes 589832 | tf_op jit(solution)/shard_map/ppermute | solution.py:337
  26.8 10.1 %collective-permute-start.10 = (bf16[3,256,128]{2,1,0:T(8,128)(2,1)S(1)}, bf16[3,256,128]{2,1,0:T(8,128)(2,1)S(1)}, u32[]{:S(2)}, u32[]{:S(2)}) collective-permute-start(bf16[3,256,128]{2,1,0:T(8,128)(2,1)S(1)} %collective-permute-done.6.refs_5_.refs_6_), channel_id=1, source_target_pairs={{8,0},{16,8},{24,16},{28,24},{20,28},{12,20},{4,12},{0,4},{9,1},{1... | collective-permute-start | bytes 589832 | tf_op jit(solution)/shard_map/ppermute | solution.py:339
  28.4 9.7 %collective-permute-start.8 = (bf16[3,256,128]{2,1,0:T(8,128)(2,1)S(1)}, bf16[3,256,128]{2,1,0:T(8,128)(2,1)S(1)}, u32[]{:S(2)}, u32[]{:S(2)}) collective-permute-start(bf16[3,256,128]{2,1,0:T(8,128)(2,1)S(1)} %collective-permute-done.4.refs_3_.refs_4_), channel_id=1, source_target_pairs={{0,8},{8,16},{16,24},{24,28},{28,20},{20,12},{12,4},{4,0},{1,9},{9... | collective-permute-start | bytes 589832 | tf_op jit(solution)/shard_map/ppermute | solution.py:338
  32.6 8.4 %collective-permute-start.11 = (bf16[3,256,128]{2,1,0:T(8,128)(2,1)S(1)}, bf16[3,256,128]{2,1,0:T(8,128)(2,1)S(1)}, u32[]{:S(2)}, u32[]{:S(2)}) collective-permute-start(bf16[3,256,128]{2,1,0:T(8,128)(2,1)S(1)} %collective-permute-done.7.refs_0_.refs_7_), channel_id=1, source_target_pairs={{0,8},{8,16},{16,24},{24,28},{28,20},{20,12},{12,4},{4,0},{1,9},{9... | collective-permute-start | bytes 589832 | tf_op jit(solution)/shard_map/ppermute | solution.py:336
  32.7 8.3 %collective-permute-start.13 = (bf16[3,256,128]{2,1,0:T(8,128)(2,1)S(1)}, bf16[3,256,128]{2,1,0:T(8,128)(2,1)S(1)}, u32[]{:S(2)}, u32[]{:S(2)}) collective-permute-start(bf16[3,256,128]{2,1,0:T(8,128)(2,1)S(1)} %collective-permute-done.9.refs_2_.refs_9_), channel_id=1, source_target_pairs={{8,0},{16,8},{24,16},{28,24},{20,28},{12,20},{4,12},{0,4},{9,1},{1... | collective-permute-start | bytes 589832 | tf_op jit(solution)/shard_map/ppermute | solution.py:337
  36.9 12.2 %copy-start.1 = (bf16[3,256,128]{2,1,0:T(8,128)(2,1)}, bf16[3,256,128]{2,1,0:T(8,128)(2,1)S(1)}, u32[]{:S(2)}) copy-start(bf16[3,256,128]{2,1,0:T(8,128)(2,1)S(1)} %collective-permute-done.10.refs_3_.refs_10_) | copy-start | bytes 589828
  36.9 5.8 %collective-permute-start.14 = (bf16[3,256,128]{2,1,0:T(8,128)(2,1)S(1)}, bf16[3,256,128]{2,1,0:T(8,128)(2,1)S(1)}, u32[]{:S(2)}, u32[]{:S(2)}) collective-permute-start(bf16[3,256,128]{2,1,0:T(8,128)(2,1)S(1)} %collective-permute-done.10.refs_3_.refs_10_), channel_id=1, source_target_pairs={{8,0},{16,8},{24,16},{28,24},{20,28},{12,20},{4,12},{0,4},{9,1},{1... | collective-permute-start | bytes 589832 | tf_op jit(solution)/shard_map/ppermute | solution.py:339
  38.1 12.6 %copy-start.3 = (bf16[3,256,128]{2,1,0:T(8,128)(2,1)}, bf16[3,256,128]{2,1,0:T(8,128)(2,1)S(1)}, u32[]{:S(2)}) copy-start(bf16[3,256,128]{2,1,0:T(8,128)(2,1)S(1)} %collective-permute-done.8.refs_1_.refs_8_) | copy-start | bytes 589828
  38.1 6.9 %collective-permute-start.12 = (bf16[3,256,128]{2,1,0:T(8,128)(2,1)S(1)}, bf16[3,256,128]{2,1,0:T(8,128)(2,1)S(1)}, u32[]{:S(2)}, u32[]{:S(2)}) collective-permute-start(bf16[3,256,128]{2,1,0:T(8,128)(2,1)S(1)} %collective-permute-done.8.refs_1_.refs_8_), channel_id=1, source_target_pairs={{0,8},{8,16},{16,24},{24,28},{28,20},{20,12},{12,4},{4,0},{1,9},{9... | collective-permute-start | bytes 589832 | tf_op jit(solution)/shard_map/ppermute | solution.py:338
  41.0 24.0 %copy-start.5 = (bf16[3,256,128]{2,1,0:T(8,128)(2,1)}, bf16[3,256,128]{2,1,0:T(8,128)(2,1)S(1)}, u32[]{:S(2)}) copy-start(bf16[3,256,128]{2,1,0:T(8,128)(2,1)S(1)} %collective-permute-done.11.refs_0_.refs_11_) | copy-start | bytes 589828
  41.0 8.1 %collective-permute-start.15 = (bf16[3,256,128]{2,1,0:T(8,128)(2,1)S(1)}, bf16[3,256,128]{2,1,0:T(8,128)(2,1)S(1)}, u32[]{:S(2)}, u32[]{:S(2)}) collective-permute-start(bf16[3,256,128]{2,1,0:T(8,128)(2,1)S(1)} %collective-permute-done.11.refs_0_.refs_11_), channel_id=1, source_target_pairs={{0,8},{8,16},{16,24},{24,28},{28,20},{20,12},{12,4},{4,0},{1,9},{9... | collective-permute-start | bytes 589832 | tf_op jit(solution)/shard_map/ppermute | solution.py:347
  41.0 24.1 %copy-start.7 = (bf16[3,256,128]{2,1,0:T(8,128)(2,1)}, bf16[3,256,128]{2,1,0:T(8,128)(2,1)S(1)}, u32[]{:S(2)}) copy-start(bf16[3,256,128]{2,1,0:T(8,128)(2,1)S(1)} %collective-permute-done.13.refs_2_.refs_13_) | copy-start | bytes 589828
  41.0 17.2 %collective-permute-start.17 = (bf16[3,3,64,512]{3,2,1,0:T(8,128)(2,1)S(1)}, bf16[3,3,64,512]{3,2,1,0:T(8,128)(2,1)S(1)}, u32[]{:S(2)}, u32[]{:S(2)}) collective-permute-start(bf16[3,3,64,512]{3,2,1,0:T(8,128)(2,1)S(1)} %cut_columns.4.refs_17_), channel_id=1, source_target_pairs={{0,1},{4,5},{9,8},{13,12},{18,19},{22,23},{27,26},{31,30}} | collective-permute-start | bytes 1769480 | tf_op jit(solution)/shard_map/ppermute | solution.py:327
  42.7 22.4 %copy-start.9 = (bf16[3,256,128]{2,1,0:T(8,128)(2,1)}, bf16[3,256,128]{2,1,0:T(8,128)(2,1)S(1)}, u32[]{:S(2)}) copy-start(bf16[3,256,128]{2,1,0:T(8,128)(2,1)S(1)} %collective-permute-done.14.refs_3_.refs_14_) | copy-start | bytes 589828
  42.7 8.0 %collective-permute-start.16 = (bf16[3,256,128]{2,1,0:T(8,128)(2,1)S(1)}, bf16[3,256,128]{2,1,0:T(8,128)(2,1)S(1)}, u32[]{:S(2)}, u32[]{:S(2)}) collective-permute-start(bf16[3,256,128]{2,1,0:T(8,128)(2,1)S(1)} %collective-permute-done.14.refs_3_.refs_14_), channel_id=1, source_target_pairs={{8,0},{16,8},{24,16},{28,24},{20,28},{12,20},{4,12},{0,4},{9,1},{1... | collective-permute-start | bytes 589832 | tf_op jit(solution)/shard_map/ppermute | solution.py:348
  45.0 20.1 %copy-start.11 = (bf16[3,256,128]{2,1,0:T(8,128)(2,1)}, bf16[3,256,128]{2,1,0:T(8,128)(2,1)S(1)}, u32[]{:S(2)}) copy-start(bf16[3,256,128]{2,1,0:T(8,128)(2,1)S(1)} %collective-permute-done.12.refs_1_.refs_12_) | copy-start | bytes 589828
  45.0 8.0 %collective-permute-start.21 = (bf16[2,3,64,512]{3,2,1,0:T(8,128)(2,1)S(1)}, bf16[2,3,64,512]{3,2,1,0:T(8,128)(2,1)}, u32[]{:S(2)}, u32[]{:S(2)}) collective-permute-start(bf16[2,3,64,512]{3,2,1,0:T(8,128)(2,1)S(1)} %cut_columns.5.refs_21_), channel_id=1, source_target_pairs={{0,2},{4,6},{9,11},{13,15},{18,16},{22,20},{27,25},{31,29}} | collective-permute-start | bytes 1179656 | tf_op jit(solution)/shard_map/ppermute | solution.py:326
  48.4 16.7 %copy-start.13 = (bf16[3,3,64,512]{3,2,1,0:T(8,128)(2,1)}, bf16[3,3,64,512]{3,2,1,0:T(8,128)(2,1)S(1)}, u32[]{:S(2)}) copy-start(bf16[3,3,64,512]{3,2,1,0:T(8,128)(2,1)S(1)} %collective-permute-done.18.refs_19_) | copy-start | bytes 1769476
  48.5 16.6 %collective-permute-start.19 = (bf16[3,3,64,512]{3,2,1,0:T(8,128)(2,1)S(1)}, bf16[3,3,64,512]{3,2,1,0:T(8,128)(2,1)S(1)}, u32[]{:S(2)}, u32[]{:S(2)}) collective-permute-start(bf16[3,3,64,512]{3,2,1,0:T(8,128)(2,1)S(1)} %collective-permute-done.18.refs_19_), channel_id=1, source_target_pairs={{2,3},{6,7},{11,10},{15,14},{16,17},{20,21},{25,24},{29,28}} | collective-permute-start | bytes 1769480 | tf_op jit(solution)/shard_map/ppermute | solution.py:328
  49.2 8.3 %collective-permute-start.20 = (bf16[2,3,64,512]{3,2,1,0:T(8,128)(2,1)S(1)}, bf16[2,3,64,512]{3,2,1,0:T(8,128)(2,1)S(1)}, u32[]{:S(2)}, u32[]{:S(2)}) collective-permute-start(bf16[2,3,64,512]{3,2,1,0:T(8,128)(2,1)S(1)} %cut_columns.5.refs_21_), channel_id=1, source_target_pairs={{0,1},{4,5},{9,8},{13,12},{18,19},{22,23},{27,26},{31,30}} | collective-permute-start | bytes 1179656 | tf_op jit(solution)/shard_map/ppermute | solution.py:327
  50.7 12.9 %collective-permute-start.24 = (bf16[2,3,64,512]{3,2,1,0:T(8,128)(2,1)S(1)}, bf16[2,3,64,512]{3,2,1,0:T(8,128)(2,1)}, u32[]{:S(2)}, u32[]{:S(2)}) collective-permute-start(bf16[2,3,64,512]{3,2,1,0:T(8,128)(2,1)S(1)} %cut_columns.6.refs_25_), channel_id=1, source_target_pairs={{0,2},{4,6},{9,11},{13,15},{18,16},{22,20},{27,25},{31,29}} | collective-permute-start | bytes 1179656 | tf_op jit(solution)/shard_map/ppermute | solution.py:326
  53.0 12.1 %collective-permute-start.27 = (bf16[1,3,64,512]{3,2,1,0:T(8,128)(2,1)S(1)}, bf16[1,3,64,512]{3,2,1,0:T(8,128)(2,1)S(1)}, u32[]{:S(2)}, u32[]{:S(2)}) collective-permute-start(bf16[1,3,64,512]{3,2,1,0:T(8,128)(2,1)S(1)} %cut_columns.7.refs_29_), channel_id=1, source_target_pairs={{0,2},{4,6},{9,11},{13,15},{18,16},{22,20},{27,25},{31,29}} | collective-permute-start | bytes 589832 | tf_op jit(solution)/shard_map/ppermute | solution.py:326
  57.5 0.7 copy-start.19
  58.2 4.0 %collective-permute-start.29 = (f32[64,64]{1,0:T(8,128)S(1)}, f32[64,64]{1,0:T(8,128)S(1)}, u32[]{:S(2)}, u32[]{:S(2)}) collective-permute-start(f32[64,64]{1,0:T(8,128)S(1)} %get-tuple-element.25), channel_id=1, source_target_pairs={{0,1},{1,0},{2,3},{3,2},{4,5},{5,4},{6,7},{7,6},{8,9},{9,8},{10,11... | collective-permute-start | bytes 49160 | tf_op jit(solution)/shard_map/ppermute | solution.py:294
  58.2 0.8 copy-start.15
  59.0 13.7 %collective-permute-start.23 = (bf16[2,3,64,512]{3,2,1,0:T(8,128)(2,1)S(1)}, bf16[2,3,64,512]{3,2,1,0:T(8,128)(2,1)}, u32[]{:S(2)}, u32[]{:S(2)}) collective-permute-start(bf16[2,3,64,512]{3,2,1,0:T(8,128)(2,1)S(1)} %cut_columns.6.refs_25_), channel_id=1, source_target_pairs={{0,1},{4,5},{9,8},{13,12},{18,19},{22,23},{27,26},{31,30}} | collective-permute-start | bytes 1179656 | tf_op jit(solution)/shard_map/ppermute | solution.py:327
  62.2 2.9 %copy-start.24 = (f32[64,64]{1,0:T(8,128)}, f32[64,64]{1,0:T(8,128)S(1)}, u32[]{:S(2)}) copy-start(f32[64,64]{1,0:T(8,128)S(1)} %collective-permute-done.29) | copy-start | bytes 49156
  62.2 10.5 %collective-permute-start.22 = (bf16[2,3,64,512]{3,2,1,0:T(8,128)(2,1)}, bf16[2,3,64,512]{3,2,1,0:T(8,128)(2,1)}, u32[]{:S(2)}, u32[]{:S(2)}) collective-permute-start(bf16[2,3,64,512]{3,2,1,0:T(8,128)(2,1)} %collective-permute-done.21.refs_23_), channel_id=1, source_target_pairs={{2,3},{6,7},{11,10},{15,14},{16,17},{20,21},{25,24},{29,28}} | collective-permute-start | bytes 1179656 | tf_op jit(solution)/shard_map/ppermute | solution.py:328
  63.6 9.1 %collective-permute-start.25 = (bf16[2,3,64,512]{3,2,1,0:T(8,128)(2,1)}, bf16[2,3,64,512]{3,2,1,0:T(8,128)(2,1)}, u32[]{:S(2)}, u32[]{:S(2)}) collective-permute-start(bf16[2,3,64,512]{3,2,1,0:T(8,128)(2,1)} %collective-permute-done.24.refs_27_), channel_id=1, source_target_pairs={{2,3},{6,7},{11,10},{15,14},{16,17},{20,21},{25,24},{29,28}} | collective-permute-start | bytes 1179656 | tf_op jit(solution)/shard_map/ppermute | solution.py:328
  65.1 0.7 copy-start.21
  65.1 4.2 %collective-permute-start.30 = (f32[64,64]{1,0:T(8,128)}, f32[64,64]{1,0:T(8,128)}, u32[]{:S(2)}, u32[]{:S(2)}) collective-permute-start(f32[64,64]{1,0:T(8,128)} %get-tuple-element.26), channel_id=1, source_target_pairs={{0,2},{1,3},{2,0},{3,1},{4,6},{5,7},{6,4},{7,5},{8,10},{9,11},{10,... | collective-permute-start | bytes 49160 | tf_op jit(solution)/shard_map/ppermute | solution.py:294
  65.8 0.8 copy-start.17
  66.6 4.0 %collective-permute-start.31 = (f32[64,64]{1,0:T(8,128)}, f32[64,64]{1,0:T(8,128)}, u32[]{:S(2)}, u32[]{:S(2)}) collective-permute-start(f32[64,64]{1,0:T(8,128)} %get-tuple-element.27), channel_id=1, source_target_pairs={{0,3},{1,2},{2,1},{3,0},{4,7},{5,6},{6,5},{7,4},{8,11},{9,10},{10,... | collective-permute-start | bytes 49160 | tf_op jit(solution)/shard_map/ppermute | solution.py:294
  69.3 3.4 %collective-permute-start.26 = (bf16[1,3,64,512]{3,2,1,0:T(8,128)(2,1)S(1)}, bf16[1,3,64,512]{3,2,1,0:T(8,128)(2,1)S(1)}, u32[]{:S(2)}, u32[]{:S(2)}) collective-permute-start(bf16[1,3,64,512]{3,2,1,0:T(8,128)(2,1)S(1)} %cut_columns.7.refs_29_), channel_id=1, source_target_pairs={{0,1},{4,5},{9,8},{13,12},{18,19},{22,23},{27,26},{31,30}} | collective-permute-start | bytes 589832 | tf_op jit(solution)/shard_map/ppermute | solution.py:327
  70.6 2.1 %collective-permute-start.28 = (bf16[1,3,64,512]{3,2,1,0:T(8,128)(2,1)}, bf16[1,3,64,512]{3,2,1,0:T(8,128)(2,1)S(1)}, u32[]{:S(2)}, u32[]{:S(2)}) collective-permute-start(bf16[1,3,64,512]{3,2,1,0:T(8,128)(2,1)} %copy-done.21), channel_id=1, source_target_pairs={{2,3},{6,7},{11,10},{15,14},{16,17},{20,21},{25,24},{29,28}} | collective-permute-start | bytes 589832 | tf_op jit(solution)/shard_map/ppermute | solution.py:328
  72.8 0.9 %copy-start.2 = (bf16[3,256,128]{2,1,0:T(8,128)(2,1)S(1)}, bf16[3,256,128]{2,1,0:T(8,128)(2,1)}, u32[]{:S(2)}) copy-start(bf16[3,256,128]{2,1,0:T(8,128)(2,1)} %copy-done.1) | copy-start | bytes 589828
  73.7 0.9 %copy-start.4 = (bf16[3,256,128]{2,1,0:T(8,128)(2,1)S(1)}, bf16[3,256,128]{2,1,0:T(8,128)(2,1)}, u32[]{:S(2)}) copy-start(bf16[3,256,128]{2,1,0:T(8,128)(2,1)} %copy-done.3) | copy-start | bytes 589828
  74.6 0.9 %copy-start.6 = (bf16[3,256,128]{2,1,0:T(8,128)(2,1)S(1)}, bf16[3,256,128]{2,1,0:T(8,128)(2,1)}, u32[]{:S(2)}) copy-start(bf16[3,256,128]{2,1,0:T(8,128)(2,1)} %copy-done.5) | copy-start | bytes 589828
  75.5 0.9 %copy-start.8 = (bf16[3,256,128]{2,1,0:T(8,128)(2,1)S(1)}, bf16[3,256,128]{2,1,0:T(8,128)(2,1)}, u32[]{:S(2)}) copy-start(bf16[3,256,128]{2,1,0:T(8,128)(2,1)} %copy-done.7) | copy-start | bytes 589828
  76.5 0.9 %copy-start.10 = (bf16[3,256,128]{2,1,0:T(8,128)(2,1)S(1)}, bf16[3,256,128]{2,1,0:T(8,128)(2,1)}, u32[]{:S(2)}) copy-start(bf16[3,256,128]{2,1,0:T(8,128)(2,1)} %copy-done.9) | copy-start | bytes 589828
  77.4 0.9 %copy-start.12 = (bf16[3,256,128]{2,1,0:T(8,128)(2,1)S(1)}, bf16[3,256,128]{2,1,0:T(8,128)(2,1)}, u32[]{:S(2)}) copy-start(bf16[3,256,128]{2,1,0:T(8,128)(2,1)} %copy-done.11) | copy-start | bytes 589828
  78.3 1.1 %copy-start.14 = (bf16[3,3,64,512]{3,2,1,0:T(8,128)(2,1)S(1)}, bf16[3,3,64,512]{3,2,1,0:T(8,128)(2,1)}, u32[]{:S(2)}) copy-start(bf16[3,3,64,512]{3,2,1,0:T(8,128)(2,1)} %copy-done.13) | copy-start | bytes 1769476
  79.4 1.1 %copy-start.16 = (bf16[3,3,64,512]{3,2,1,0:T(8,128)(2,1)S(1)}, bf16[3,3,64,512]{3,2,1,0:T(8,128)(2,1)}, u32[]{:S(2)}) copy-start(bf16[3,3,64,512]{3,2,1,0:T(8,128)(2,1)} %copy-done.15) | copy-start | bytes 1769476
  80.5 1.1 %copy-start.18 = (bf16[3,3,64,512]{3,2,1,0:T(8,128)(2,1)S(1)}, bf16[3,3,64,512]{3,2,1,0:T(8,128)(2,1)}, u32[]{:S(2)}) copy-start(bf16[3,3,64,512]{3,2,1,0:T(8,128)(2,1)} %copy-done.17) | copy-start | bytes 1769476
  81.5 1.0 %copy-start.20 = (bf16[2,3,64,512]{3,2,1,0:T(8,128)(2,1)S(1)}, bf16[2,3,64,512]{3,2,1,0:T(8,128)(2,1)}, u32[]{:S(2)}) copy-start(bf16[2,3,64,512]{3,2,1,0:T(8,128)(2,1)} %copy-done.19) | copy-start | bytes 1179652
  82.5 0.9 %copy-start.22 = (bf16[1,3,64,512]{3,2,1,0:T(8,128)(2,1)S(1)}, bf16[1,3,64,512]{3,2,1,0:T(8,128)(2,1)}, u32[]{:S(2)}) copy-start(bf16[1,3,64,512]{3,2,1,0:T(8,128)(2,1)} %copy-done.21) | copy-start | bytes 589828

commit v6 on v5

--- a/solution.py
+++ b/solution.py
@@ -59,23 +59,18 @@
     out = jnp.zeros(shape, jnp.float32)
     for k, value in enumerate(values):
         out = jnp.where(lane == k, jnp.broadcast_to(value, shape), out)
-    out_ref[...] = out.T[:STATS]
-
-
-def align_kernel(parts, atoms, *refs):
-    stats = refs[:parts]
-    x_hbm, ref_hbm, first_ref, second_ref, flat_ref, x_ref, ref_ref, turn, sem = refs[parts:]
-    copies = [
-        pltpu.make_async_copy(ref_hbm, ref_ref, sem.at[0]),
-        pltpu.make_async_copy(x_hbm, x_ref, sem.at[1]),
-    ]
-    for copy in copies:
-        copy.start()
+    turned = out.T[:STATS]
+    for k in range(out_ref.shape[0]):
+        out_ref[k] = jnp.concatenate([turned, jnp.zeros_like(turned)], axis=1)
+
+
+def align_kernel(parts, *refs):
+    stats, x_ref, ref_ref, first_ref, second_ref, flat_ref, turn = refs
     local = x_ref.shape[2]
     rows = x_ref.shape[1]
 
     def row(at):
-        return [s[at : at + 1, :] for s in stats]
+        return [stats[p, at : at + 1, :] for p in range(parts)]
 
     means = [row(i) for i in range(3)]
     ref_means = [row(13 + j) for j in range(3)]
@@ -108,11 +103,9 @@
             for i in range(3)
         ]
     for k, value in enumerate(sum(now, []) + centre + ref_centre):
-        turn[k : k + 1, :rows] = value
+        turn[k : k + 1, :] = value
     turned = turn[...].T
     column = [turned[:rows, k : k + 1] for k in range(12)]
-    for copy in copies:
-        copy.wait()
     centred = [x_ref[j] - column[9 + j] for j in range(3)]
     for i in range(3):
         target = ref_ref[i : i + 1, :] - turned[0:1, 12 + i : 13 + i]
@@ -124,16 +117,21 @@
             piece[i] = jnp.concatenate(pair, axis=0).T.astype(jnp.bfloat16)
 
 
-def project_kernel(me_ref, flat_ref, eig_ref, *refs):
-    shares, cut = refs[:-1], refs[-1]
+def project_kernel(flat_ref, eig_ref, out_ref):
     total = sum(
         jnp.dot(flat_ref[c], eig_ref[c], preferred_element_type=jnp.float32) for c in range(3)
     )
-    width = cut.shape[2]
-    for k in range(len(shares)):
-        cut[k] = total[:, k * width : (k + 1) * width]
-    for k, share in enumerate(shares):
-        share[...] = cut[lax.bitwise_xor(me_ref[0], k)]
+    middle, width = out_ref.shape[1], out_ref.shape[2] // 2
+    for k in range(out_ref.shape[0]):
+        part = total[:, k * width : (k + 1) * width]
+        out_ref[k] = jnp.concatenate([part[:middle], part[middle:]], axis=1)
+
+
+def sum_kernel(parts_ref, out_ref):
+    middle, width = parts_ref.shape[1], parts_ref.shape[2] // 2
+    total = sum(parts_ref[k] for k in range(parts_ref.shape[0]))
+    out_ref[:middle] = total[:, :width]
+    out_ref[middle:] = total[:, width:]
 
 
 def cut_kernel(slots, half_ref, *refs):
@@ -249,51 +247,50 @@
     role = lax.bitwise_xor(me_a, owner).astype(jnp.int32).reshape(1)
     x = pinned(jnp.transpose(frames, (1, 0, 2)), pltpu.HBM)
     mean_structure = pinned(mean_structure, pltpu.HBM)
-    x_copy = [
-        pltpu.VMEM(x.shape, jnp.float32),
-        pltpu.VMEM(mean_structure.shape, jnp.float32),
-    ]
-
-    stats = pl.pallas_call(
+    stats, x, mean_structure = pl.pallas_call(
         stats_kernel,
-        out_shape=jax.ShapeDtypeStruct((STATS, local_frames), jnp.float32),
+        out_shape=(
+            pltpu.VMEM((atom_axis, STATS, LANES), jnp.float32),
+            pltpu.VMEM(x.shape, jnp.float32),
+            pltpu.VMEM(mean_structure.shape, jnp.float32),
+        ),
         in_specs=[HBM, HBM],
-        out_specs=VMEM,
-        scratch_shapes=x_copy + [pltpu.SemaphoreType.DMA((2,))],
+        out_specs=(VMEM, VMEM, VMEM),
+        scratch_shapes=[pltpu.SemaphoreType.DMA((2,))],
         compiler_params=params(8),
         name="local_moments",
     )(x, mean_structure)
-    others = [
-        lax.ppermute(stats, "atoms", [(a, a ^ d) for a in range(atom_axis)])
-        for d in range(1, atom_axis)
-    ]
+    stats = lax.all_to_all(stats, "atoms", split_axis=0, concat_axis=0, tiled=True)
     run = local_atoms // 4
     piece = jax.ShapeDtypeStruct((3, run, 2 * local_frames), jnp.bfloat16)
     first, second, flat = pl.pallas_call(
-        functools.partial(align_kernel, atom_axis, local_atoms * atom_axis),
+        functools.partial(align_kernel, atom_axis),
         out_shape=(piece, piece, jax.ShapeDtypeStruct(x.shape, jnp.bfloat16)),
-        in_specs=[VMEM] * atom_axis + [HBM, HBM],
+        in_specs=[VMEM, VMEM, VMEM],
         out_specs=(VMEM, VMEM, VMEM),
-        scratch_shapes=x_copy
-        + [pltpu.VMEM((LANES, LANES), jnp.float32), pltpu.SemaphoreType.DMA((2,))],
+        scratch_shapes=[pltpu.VMEM((LANES, LANES), jnp.float32)],
         compiler_params=params(8),
         name="polar_align",
-    )(stats, *others, x, mean_structure)
-    share = jax.ShapeDtypeStruct((local_frames, eigvecs.shape[2] // atom_axis), jnp.float32)
+    )(stats, x, mean_structure)
+    share = (local_frames, eigvecs.shape[2] // atom_axis)
     shares = pl.pallas_call(
         project_kernel,
-        out_shape=(share,) * atom_axis,
-        in_specs=[SMEM, VMEM, VMEM],
-        out_specs=(VMEM,) * atom_axis,
-        scratch_shapes=[pltpu.VMEM((atom_axis,) + share.shape, jnp.float32)],
+        out_shape=jax.ShapeDtypeStruct(
+            (atom_axis, local_frames // 2, 2 * share[1]), jnp.float32
+        ),
+        in_specs=[VMEM, VMEM],
+        out_specs=VMEM,
         compiler_params=params(8),
         name="project",
-    )(me_a.astype(jnp.int32).reshape(1), flat, eigvecs)
-    def exchange(values):
-        return values[0] + sum(
-            lax.ppermute(values[d], "atoms", [(a, a ^ d) for a in range(atom_axis)])
-            for d in range(1, atom_axis)
-        )
+    )(flat, eigvecs)
+    projections = pl.pallas_call(
+        sum_kernel,
+        out_shape=jax.ShapeDtypeStruct(share, jnp.float32),
+        in_specs=[VMEM],
+        out_specs=VMEM,
+        compiler_params=params(4),
+        name="sum_shares",
+    )(lax.all_to_all(shares, "atoms", split_axis=0, concat_axis=0, tiled=True))
 
     def pairs(source, target):
         return [
@@ -306,7 +303,6 @@
 
     if blocks != 2 or frame_axis != 8:
         spread_pairs = [pairs(0, d) for d in range(1, atom_axis)]
-        projections = exchange(shares)
         covariance = long_axis_covariance(
             flat, half[0], role[0], block, spread_pairs, 1.0 / total_frames
         )
@@ -348,10 +344,9 @@
         lax.ppermute(down3[1], "frames", backward),
     ]
     lots = [own + up1 + down1, up2 + down2, up3 + down3, far]
-    cuts = [spread(lots[0], shares), spread(lots[1], []), spread(lots[2], [])]
+    cuts = [spread(lots[0], [shares]), spread(lots[1], []), spread(lots[2], [])]
     cuts.append(spread(far, [], cuts[0][1:]))
     cuts = sum(cuts, [])
-    projections = exchange([after(value, cuts[-4]) for value in shares])
     pieces = sum(lots, [])
     counts = [len(lot) // 2 for lot in lots]
     covariance = pl.pallas_call(

time: 93.3 us -> 98.3 us (1.054)
  blocking collectives: 0 us -> 8.04 us
  waiting for transfers between devices: 19.4 us -> 15.7 us
  starting transfers between devices: 40.9 us -> 44.4 us
  local copies, waits for them, and re-layouts: 15.7 us -> 14.2 us
  other arithmetic: 1.43 us -> 0 us
    all_to_all x0 -> x1, blocking collectives: none -> 8.04 us  [per_device(): lax.all_to_all(stats, 'atoms', split_axis=0, concat_axis=0, tiled=True)]
    ppermute x6 -> x0, waiting for transfers between devices: 5.75 us -> none  [the longest x3 3.02 us: per_device(): lax.ppermute(stats, 'atoms', [(a, a ^ d) for a in range(atom_axis)])]
    all_to_all x0 -> x1, waiting for transfers between devices: none -> 4.31 us  [per_device(): lax.all_to_all(shares, 'atoms', split_axis=0, concat_axis=0, tiled=True)]
    all_to_all x0 -> x1, starting transfers between devices: none -> 3.89 us  [per_device(): lax.all_to_all(shares, 'atoms', split_axis=0, concat_axis=0, tiled=True)]
    ppermute x6 -> x0, starting transfers between devices: 3.13 us -> none  [the longest x3 3.12 us: per_device(): lax.ppermute(stats, 'atoms', [(a, a ^ d) for a in range(atom_axis)])]
    ppermute x3, waiting for transfers between devices: 7.29 us -> 4.41 us  [hop(): up_a = lax.ppermute(up[0], 'frames', forward)]
    ppermute x1, starting transfers between devices: 1.73 us -> 3.5 us  [per_device(): lax.ppermute(down3[1], 'frames', backward)]
    unnamed x50 -> x44, local copies, waits for them, and re-layouts: 15.7 us -> 14.2 us
  transfers between devices with their start and end apart: 32 -> 27, of which waited for: 14 -> 10; matrix products, arithmetic and copies ran while one was open for 2% -> 0% of each run, Pallas kernels for 2% -> 3%
where the time goes in v6:
time: 98.3 us; the launch traced here: 97.4 us
  starting transfers between devices  44.4 us (45%)
  waiting for transfers between devices  15.7 us (16%)
  Pallas kernels  14.2 us (14%)
  local copies, waits for them, and re-layouts  14.2 us (14%)
  blocking collectives  8.04 us (8%)
    unnamed x44, local copies, waits for them, and re-layouts  14.2 us
    ppermute x4, starting transfers between devices, spread(): across = lax.ppermute(cut, axes, pairs(0, 2))  12 us
    pallas_call x1, Pallas kernels, per_device(): pl.pallas_call(functools.partial(covariance_kernel, frame_axis, atom_axis...  9.2 us
    all_to_all x1, blocking collectives, per_device(): lax.all_to_all(stats, 'atoms', split_axis=0, concat_axis=0, tiled=True)  8.04 us
    ppermute x4, starting transfers between devices, spread(): beside = lax.ppermute(cut, axes, pairs(0, 1))  6.65 us
    ppermute x3, starting transfers between devices, hop(): down_b = lax.ppermute(down[1], 'frames', backward)  4.91 us
    ppermute x4, starting transfers between devices, spread(): last = lax.ppermute(after(across, *before_last), axes, pairs(2, 3))  4.85 us
    ppermute x3, starting transfers between devices, hop(): down_a = lax.ppermute(down[0], 'frames', backward)  4.71 us
  transfers between devices with their start and end apart: 27, of which 10 were waited for; matrix products, arithmetic and copies ran while one was open for 0% of the time, Pallas kernels for 3%

profile of v6, /device:TPU:0, one launch (start us, length us, event | category | flops | bytes accessed | tf_op | source)
XLA Modules:
  0.0 97.4 jit_solution(9428691396407506823)
XLA Ops:
  0.6 1.7 %local_moments.1 = (f32[4,24,128]{2,1,0:T(8,128)S(1)}, f32[3,64,1024]{2,1,0:T(8,128)S(1)}, f32[3,1024]{1,0:T(4,128)S(1)}) custom-call(f32[3,64,1024]{2,1,0:T(8,128)} %bitcast.5, f32[3,1024]{1,0:T(4,128)} %ref_hbm.1), custom_call_target="tpu_custom_call" | custom-call | tf_op jit(solution)/shard_map/local_moments/pallas_call | solution.py:250
  2.3 8.0 %all_to_all.10.refs_0_ = f32[4,24,128]{2,1,0:T(8,128)S(1)} all-to-all(f32[4,24,128]{2,1,0:T(8,128)S(1)} %get-tuple-element.10), channel_id=1, replica_groups=mesh['frames'=8,'atoms'=4] {'atoms'}, dimensions={0} | all-to-all | bytes 98304 | tf_op jit(solution)/shard_map/all_to_all | solution.py:263
  10.3 0.6 polar_align.1
  10.9 1.6 %collective-permute-start.2 = (bf16[3,256,128]{2,1,0:T(8,128)(2,1)S(1)}, bf16[3,256,128]{2,1,0:T(8,128)(2,1)S(1)}, u32[]{:S(2)}, u32[]{:S(2)}) collective-permute-start(bf16[3,256,128]{2,1,0:T(8,128)(2,1)S(1)} %get-tuple-element.13.refs_0_.refs_1_), channel_id=1, source_target_pairs={{8,0},{16,8},{24,16},{28,24},{20,28},{12,20},{4,12},{0,4},{9,1},{1... | collective-permute-start | bytes 589832 | tf_op jit(solution)/shard_map/ppermute | solution.py:333
  12.5 0.5 collective-permute-start
  13.0 1.5 %collective-permute-start.3 = (bf16[3,256,128]{2,1,0:T(8,128)(2,1)S(1)}, bf16[3,256,128]{2,1,0:T(8,128)(2,1)S(1)}, u32[]{:S(2)}, u32[]{:S(2)}) collective-permute-start(bf16[3,256,128]{2,1,0:T(8,128)(2,1)S(1)} %get-tuple-element.14.refs_1_.refs_2_), channel_id=1, source_target_pairs={{8,0},{16,8},{24,16},{28,24},{20,28},{12,20},{4,12},{0,4},{9,1},{1... | collective-permute-start | bytes 589832 | tf_op jit(solution)/shard_map/ppermute | solution.py:335
  14.5 0.5 collective-permute-start.1
  15.0 1.4 %copy-done = bf16[3,1024,256]{2,1,0:T(8,128)(2,1)S(1)} copy-done((bf16[3,1024,256]{2,1,0:T(8,128)(2,1)S(1)}, bf16[3,1024,256]{2,1,0:T(8,128)(2,1)}, u32[]{:S(2)}) %copy-start) | copy-done | bytes 1572888
  16.5 0.5 project.1
  16.9 0.6 copy-done.21
  17.5 1.3 %collective-permute-done.2.refs_4_.refs_5_ = bf16[3,256,128]{2,1,0:T(8,128)(2,1)S(1)} collective-permute-done((bf16[3,256,128]{2,1,0:T(8,128)(2,1)S(1)}, bf16[3,256,128]{2,1,0:T(8,128)(2,1)S(1)}, u32[]{:S(2)}, u32[]{:S(2)}) %collective-permute-start.2) | collective-permute-done | bytes 196640 | tf_op jit(solution)/shard_map/ppermute | solution.py:333
  18.8 1.5 %collective-permute-start.6 = (bf16[3,256,128]{2,1,0:T(8,128)(2,1)S(1)}, bf16[3,256,128]{2,1,0:T(8,128)(2,1)S(1)}, u32[]{:S(2)}, u32[]{:S(2)}) collective-permute-start(bf16[3,256,128]{2,1,0:T(8,128)(2,1)S(1)} %collective-permute-done.2.refs_4_.refs_5_), channel_id=1, source_target_pairs={{8,0},{16,8},{24,16},{28,24},{20,28},{12,20},{4,12},{0,4},{9,1},{1... | collective-permute-start | bytes 589832 | tf_op jit(solution)/shard_map/ppermute | solution.py:333
  20.3 0.0 collective-permute-done.refs_2_.refs_3_
  20.4 2.7 %collective-permute-done.3.refs_5_.refs_6_ = bf16[3,256,128]{2,1,0:T(8,128)(2,1)S(1)} collective-permute-done((bf16[3,256,128]{2,1,0:T(8,128)(2,1)S(1)}, bf16[3,256,128]{2,1,0:T(8,128)(2,1)S(1)}, u32[]{:S(2)}, u32[]{:S(2)}) %collective-permute-start.3) | collective-permute-done | bytes 196640 | tf_op jit(solution)/shard_map/ppermute | solution.py:335
  23.0 0.2 cut_columns.4.refs_17_
  23.3 2.0 %collective-permute-start.15 = (bf16[3,3,64,512]{3,2,1,0:T(8,128)(2,1)S(1)}, bf16[3,3,64,512]{3,2,1,0:T(8,128)(2,1)S(1)}, u32[]{:S(2)}, u32[]{:S(2)}) collective-permute-start(bf16[3,3,64,512]{3,2,1,0:T(8,128)(2,1)S(1)} %cut_columns.4.refs_17_), channel_id=1, source_target_pairs={{0,2},{4,6},{9,11},{13,15},{18,16},{22,20},{27,25},{31,29}} | collective-permute-start | bytes 1769480 | tf_op jit(solution)/shard_map/ppermute | solution.py:322
  25.3 0.3 collective-permute-start.4
  25.6 1.8 %collective-permute-start.7 = (bf16[3,256,128]{2,1,0:T(8,128)(2,1)S(1)}, bf16[3,256,128]{2,1,0:T(8,128)(2,1)S(1)}, u32[]{:S(2)}, u32[]{:S(2)}) collective-permute-start(bf16[3,256,128]{2,1,0:T(8,128)(2,1)S(1)} %collective-permute-done.3.refs_5_.refs_6_), channel_id=1, source_target_pairs={{8,0},{16,8},{24,16},{28,24},{20,28},{12,20},{4,12},{0,4},{9,1},{1... | collective-permute-start | bytes 589832 | tf_op jit(solution)/shard_map/ppermute | solution.py:335
  27.4 0.4 collective-permute-start.5
  27.8 1.6 %collective-permute-start.10 = (bf16[3,256,128]{2,1,0:T(8,128)(2,1)S(1)}, bf16[3,256,128]{2,1,0:T(8,128)(2,1)S(1)}, u32[]{:S(2)}, u32[]{:S(2)}) collective-permute-start(bf16[3,256,128]{2,1,0:T(8,128)(2,1)S(1)} %collective-permute-done.6.refs_2_.refs_9_), channel_id=1, source_target_pairs={{8,0},{16,8},{24,16},{28,24},{20,28},{12,20},{4,12},{0,4},{9,1},{1... | collective-permute-start | bytes 589832 | tf_op jit(solution)/shard_map/ppermute | solution.py:333
  29.4 3.3 %collective-permute-done.4.refs_0_.refs_7_ = bf16[3,256,128]{2,1,0:T(8,128)(2,1)S(1)} collective-permute-done((bf16[3,256,128]{2,1,0:T(8,128)(2,1)S(1)}, bf16[3,256,128]{2,1,0:T(8,128)(2,1)S(1)}, u32[]{:S(2)}, u32[]{:S(2)}) %collective-permute-start.4) | collective-permute-done | bytes 196640 | tf_op jit(solution)/shard_map/ppermute | solution.py:332
  32.7 0.7 collective-permute-start.8
  33.4 0.1 collective-permute-done.7.refs_3_.refs_10_
  33.6 1.6 %collective-permute-start.11 = (bf16[3,256,128]{2,1,0:T(8,128)(2,1)S(1)}, bf16[3,256,128]{2,1,0:T(8,128)(2,1)S(1)}, u32[]{:S(2)}, u32[]{:S(2)}) collective-permute-start(bf16[3,256,128]{2,1,0:T(8,128)(2,1)S(1)} %collective-permute-done.7.refs_3_.refs_10_), channel_id=1, source_target_pairs={{8,0},{16,8},{24,16},{28,24},{20,28},{12,20},{4,12},{0,4},{9,1},{1... | collective-permute-start | bytes 589832 | tf_op jit(solution)/shard_map/ppermute | solution.py:335
  35.2 0.7 collective-permute-done.5.refs_1_.refs_8_
  35.9 1.3 %collective-permute-start.14 = (bf16[3,3,64,512]{3,2,1,0:T(8,128)(2,1)S(1)}, bf16[3,3,64,512]{3,2,1,0:T(8,128)(2,1)S(1)}, u32[]{:S(2)}, u32[]{:S(2)}) collective-permute-start(bf16[3,3,64,512]{3,2,1,0:T(8,128)(2,1)S(1)} %cut_columns.4.refs_17_), channel_id=1, source_target_pairs={{0,1},{4,5},{9,8},{13,12},{18,19},{22,23},{27,26},{31,30}} | collective-permute-start | bytes 1769480 | tf_op jit(solution)/shard_map/ppermute | solution.py:323
  37.2 0.2 cut_columns.5.refs_21_
  37.4 1.4 %collective-permute-start.9 = (bf16[3,256,128]{2,1,0:T(8,128)(2,1)S(1)}, bf16[3,256,128]{2,1,0:T(8,128)(2,1)S(1)}, u32[]{:S(2)}, u32[]{:S(2)}) collective-permute-start(bf16[3,256,128]{2,1,0:T(8,128)(2,1)S(1)} %collective-permute-done.5.refs_1_.refs_8_), channel_id=1, source_target_pairs={{0,8},{8,16},{16,24},{24,28},{28,20},{20,12},{12,4},{4,0},{1,9},{9... | collective-permute-start | bytes 589832 | tf_op jit(solution)/shard_map/ppermute | solution.py:334
  38.9 1.1 %collective-permute-done.8.refs_0_.refs_11_ = bf16[3,256,128]{2,1,0:T(8,128)(2,1)S(1)} collective-permute-done((bf16[3,256,128]{2,1,0:T(8,128)(2,1)S(1)}, bf16[3,256,128]{2,1,0:T(8,128)(2,1)S(1)}, u32[]{:S(2)}, u32[]{:S(2)}) %collective-permute-start.8) | collective-permute-done | bytes 196640 | tf_op jit(solution)/shard_map/ppermute | solution.py:332
  40.0 3.1 %collective-permute-start.18 = (bf16[2,3,64,512]{3,2,1,0:T(8,128)(2,1)S(1)}, bf16[2,3,64,512]{3,2,1,0:T(8,128)(2,1)}, u32[]{:S(2)}, u32[]{:S(2)}) collective-permute-start(bf16[2,3,64,512]{3,2,1,0:T(8,128)(2,1)S(1)} %cut_columns.5.refs_21_), channel_id=1, source_target_pairs={{0,2},{4,6},{9,11},{13,15},{18,16},{22,20},{27,25},{31,29}} | collective-permute-start | bytes 1179656 | tf_op jit(solution)/shard_map/ppermute | solution.py:322
  43.0 0.0 collective-permute-done.11.refs_3_.refs_14_
  43.1 0.7 collective-permute-start.16
  43.8 0.2 collective-permute-done.9.refs_1_.refs_12_
  44.0 3.5 %collective-permute-start.13 = (bf16[3,256,128]{2,1,0:T(8,128)(2,1)S(1)}, bf16[3,256,128]{2,1,0:T(8,128)(2,1)S(1)}, u32[]{:S(2)}, u32[]{:S(2)}) collective-permute-start(bf16[3,256,128]{2,1,0:T(8,128)(2,1)S(1)} %collective-permute-done.11.refs_3_.refs_14_), channel_id=1, source_target_pairs={{8,0},{16,8},{24,16},{28,24},{20,28},{12,20},{4,12},{0,4},{9,1},{1... | collective-permute-start | bytes 589832 | tf_op jit(solution)/shard_map/ppermute | solution.py:344
  47.5 0.2 cut_columns.6.refs_25_
  47.7 1.1 %collective-permute-done.12.refs_0_.refs_15_ = bf16[3,256,128]{2,1,0:T(8,128)(2,1)S(1)} collective-permute-done((bf16[3,256,128]{2,1,0:T(8,128)(2,1)S(1)}, bf16[3,256,128]{2,1,0:T(8,128)(2,1)S(1)}, u32[]{:S(2)}, u32[]{:S(2)}) %collective-permute-start.12) | collective-permute-done | bytes 196640 | tf_op jit(solution)/shard_map/ppermute | solution.py:343
  48.8 2.0 %collective-permute-start.21 = (bf16[2,3,64,512]{3,2,1,0:T(8,128)(2,1)S(1)}, bf16[2,3,64,512]{3,2,1,0:T(8,128)(2,1)}, u32[]{:S(2)}, u32[]{:S(2)}) collective-permute-start(bf16[2,3,64,512]{3,2,1,0:T(8,128)(2,1)S(1)} %cut_columns.6.refs_25_), channel_id=1, source_target_pairs={{0,2},{4,6},{9,11},{13,15},{18,16},{22,20},{27,25},{31,29}} | collective-permute-start | bytes 1179656 | tf_op jit(solution)/shard_map/ppermute | solution.py:322
  50.9 0.8 collective-permute-done.13.refs_1_.refs_16_
  51.7 0.1 cut_columns.7.refs_29_
  51.8 4.9 %collective-permute-start.24 = (bf16[1,3,64,512]{3,2,1,0:T(8,128)(2,1)S(1)}, bf16[1,3,64,512]{3,2,1,0:T(8,128)(2,1)}, u32[]{:S(2)}, u32[]{:S(2)}) collective-permute-start(bf16[1,3,64,512]{3,2,1,0:T(8,128)(2,1)S(1)} %cut_columns.7.refs_29_), channel_id=1, source_target_pairs={{0,2},{4,6},{9,11},{13,15},{18,16},{22,20},{27,25},{31,29}} | collective-permute-start | bytes 589832 | tf_op jit(solution)/shard_map/ppermute | solution.py:322
  56.8 1.3 %collective-permute-start.17 = (bf16[2,3,64,512]{3,2,1,0:T(8,128)(2,1)S(1)}, bf16[2,3,64,512]{3,2,1,0:T(8,128)(2,1)S(1)}, u32[]{:S(2)}, u32[]{:S(2)}) collective-permute-start(bf16[2,3,64,512]{3,2,1,0:T(8,128)(2,1)S(1)} %cut_columns.5.refs_21_), channel_id=1, source_target_pairs={{0,1},{4,5},{9,8},{13,12},{18,19},{22,23},{27,26},{31,30}} | collective-permute-start | bytes 1179656 | tf_op jit(solution)/shard_map/ppermute | solution.py:323
  58.1 0.0 copy-start.15
  58.1 0.8 copy-done.15
  58.9 2.1 %collective-permute-start.20 = (bf16[2,3,64,512]{3,2,1,0:T(8,128)(2,1)S(1)}, bf16[2,3,64,512]{3,2,1,0:T(8,128)(2,1)}, u32[]{:S(2)}, u32[]{:S(2)}) collective-permute-start(bf16[2,3,64,512]{3,2,1,0:T(8,128)(2,1)S(1)} %cut_columns.6.refs_25_), channel_id=1, source_target_pairs={{0,1},{4,5},{9,8},{13,12},{18,19},{22,23},{27,26},{31,30}} | collective-permute-start | bytes 1179656 | tf_op jit(solution)/shard_map/ppermute | solution.py:323
  61.0 1.4 %collective-permute-start.19 = (bf16[2,3,64,512]{3,2,1,0:T(8,128)(2,1)}, bf16[2,3,64,512]{3,2,1,0:T(8,128)(2,1)}, u32[]{:S(2)}, u32[]{:S(2)}) collective-permute-start(bf16[2,3,64,512]{3,2,1,0:T(8,128)(2,1)} %collective-permute-done.18.refs_23_), channel_id=1, source_target_pairs={{2,3},{6,7},{11,10},{15,14},{16,17},{20,21},{25,24},{29,28}} | collective-permute-start | bytes 1179656 | tf_op jit(solution)/shard_map/ppermute | solution.py:324
  62.4 1.4 %collective-permute-start.22 = (bf16[2,3,64,512]{3,2,1,0:T(8,128)(2,1)}, bf16[2,3,64,512]{3,2,1,0:T(8,128)(2,1)}, u32[]{:S(2)}, u32[]{:S(2)}) collective-permute-start(bf16[2,3,64,512]{3,2,1,0:T(8,128)(2,1)} %collective-permute-done.21.refs_27_), channel_id=1, source_target_pairs={{2,3},{6,7},{11,10},{15,14},{16,17},{20,21},{25,24},{29,28}} | collective-permute-start | bytes 1179656 | tf_op jit(solution)/shard_map/ppermute | solution.py:324
  63.8 0.8 copy-done.17
  64.6 2.0 %collective-permute-start.23 = (bf16[1,3,64,512]{3,2,1,0:T(8,128)(2,1)S(1)}, bf16[1,3,64,512]{3,2,1,0:T(8,128)(2,1)}, u32[]{:S(2)}, u32[]{:S(2)}) collective-permute-start(bf16[1,3,64,512]{3,2,1,0:T(8,128)(2,1)S(1)} %cut_columns.7.refs_29_), channel_id=1, source_target_pairs={{0,1},{4,5},{9,8},{13,12},{18,19},{22,23},{27,26},{31,30}} | collective-permute-start | bytes 589832 | tf_op jit(solution)/shard_map/ppermute | solution.py:323
  66.6 0.8 copy-done.19
  67.4 1.3 %collective-permute-start.25 = (bf16[1,3,64,512]{3,2,1,0:T(8,128)(2,1)}, bf16[1,3,64,512]{3,2,1,0:T(8,128)(2,1)}, u32[]{:S(2)}, u32[]{:S(2)}) collective-permute-start(bf16[1,3,64,512]{3,2,1,0:T(8,128)(2,1)} %collective-permute-done.24.refs_31_), channel_id=1, source_target_pairs={{2,3},{6,7},{11,10},{15,14},{16,17},{20,21},{25,24},{29,28}} | collective-permute-start | bytes 589832 | tf_op jit(solution)/shard_map/ppermute | solution.py:324
  68.7 3.9 %all-to-all-start.1 = ((f32[4,32,128]{2,1,0:T(8,128)}), f32[4,32,128]{2,1,0:T(8,128)}, u32[]{:S(2)}, u32[]{:S(2)}) async-start(f32[4,32,128]{2,1,0:T(8,128)} %copy-done.21), calls=%async_computation.1 | async-start | bytes 131072 | tf_op jit(solution)/shard_map/all_to_all | solution.py:293
  72.6 4.3 %all-to-all-done.1.parts_ref = f32[4,32,128]{2,1,0:T(8,128)} async-done(((f32[4,32,128]{2,1,0:T(8,128)}), f32[4,32,128]{2,1,0:T(8,128)}, u32[]{:S(2)}, u32[]{:S(2)}) %all-to-all-start.1) | async-done | bytes 65568 | tf_op jit(solution)/shard_map/all_to_all | solution.py:293
  76.9 1.5 %sum_shares.1 = f32[64,64]{1,0:T(8,128)} custom-call(f32[4,32,128]{2,1,0:T(8,128)} %all-to-all-done.1.parts_ref), custom_call_target="tpu_custom_call" | custom-call | tf_op jit(solution)/shard_map/sum_shares/pallas_call | solution.py:286
  78.5 0.9 copy-done.2
  79.4 0.9 copy-done.4
  80.3 0.9 copy-done.6
  81.3 0.9 copy-done.8
  82.2 0.9 copy-done.10
  83.1 0.9 copy-done.12
  84.1 1.1 %copy-done.14 = bf16[3,3,64,512]{3,2,1,0:T(8,128)(2,1)S(1)} copy-done((bf16[3,3,64,512]{3,2,1,0:T(8,128)(2,1)S(1)}, bf16[3,3,64,512]{3,2,1,0:T(8,128)(2,1)}, u32[]{:S(2)}) %copy-start.14) | copy-done | bytes 589848
  85.1 1.1 %copy-done.16 = bf16[3,3,64,512]{3,2,1,0:T(8,128)(2,1)S(1)} copy-done((bf16[3,3,64,512]{3,2,1,0:T(8,128)(2,1)S(1)}, bf16[3,3,64,512]{3,2,1,0:T(8,128)(2,1)}, u32[]{:S(2)}) %copy-start.16) | copy-done | bytes 589848
  86.2 1.1 %copy-done.18 = bf16[3,3,64,512]{3,2,1,0:T(8,128)(2,1)S(1)} copy-done((bf16[3,3,64,512]{3,2,1,0:T(8,128)(2,1)S(1)}, bf16[3,3,64,512]{3,2,1,0:T(8,128)(2,1)}, u32[]{:S(2)}) %copy-start.18) | copy-done | bytes 589848
  87.2 1.0 %copy-done.20 = bf16[2,3,64,512]{3,2,1,0:T(8,128)(2,1)S(1)} copy-done((bf16[2,3,64,512]{3,2,1,0:T(8,128)(2,1)S(1)}, bf16[2,3,64,512]{3,2,1,0:T(8,128)(2,1)}, u32[]{:S(2)}) %copy-start.20) | copy-done | bytes 393240
  88.2 9.2 %covariance_tile.1 = f32[3,3,1024,512]{3,2,1,0:T(8,128)} custom-call(s32[1]{0:T(128)} %bitcast.refs_0_, bf16[3,256,128]{2,1,0:T(8,128)(2,1)S(1)} %get-tuple-element.13.refs_0_.refs_1_, bf16[3,256,128]{2,1,0:T(8,128)(2,1)S(1)} %get-tuple-element.14.refs_1_.refs_2_, bf16[3,256,128]{2,1,0:T(8,128)(2,1)S(1)} %collective-permute-done.refs_2_.refs_3_, ...), custom_call_target="tpu_custom_call" | custom-call | flops 4831838208 | bytes 25165824 | tf_op jit(solution)/shard_map/covariance_tile/pallas_call | solution.py:352
  (44 shorter events, 0.1 us)
Async XLA Ops:
  10.9 7.9 %collective-permute-start.2 = (bf16[3,256,128]{2,1,0:T(8,128)(2,1)S(1)}, bf16[3,256,128]{2,1,0:T(8,128)(2,1)S(1)}, u32[]{:S(2)}, u32[]{:S(2)}) collective-permute-start(bf16[3,256,128]{2,1,0:T(8,128)(2,1)S(1)} %get-tuple-element.13.refs_0_.refs_1_), channel_id=1, source_target_pairs={{8,0},{16,8},{24,16},{28,24},{20,28},{12,20},{4,12},{0,4},{9,1},{1... | collective-permute-start | bytes 589832 | tf_op jit(solution)/shard_map/ppermute | solution.py:333
  12.5 7.8 %collective-permute-start = (bf16[3,256,128]{2,1,0:T(8,128)(2,1)S(1)}, bf16[3,256,128]{2,1,0:T(8,128)(2,1)S(1)}, u32[]{:S(2)}, u32[]{:S(2)}) collective-permute-start(bf16[3,256,128]{2,1,0:T(8,128)(2,1)S(1)} %get-tuple-element.13.refs_0_.refs_1_), channel_id=1, source_target_pairs={{0,8},{8,16},{16,24},{24,28},{28,20},{20,12},{12,4},{4,0},{1,9},{9... | collective-permute-start | bytes 589832 | tf_op jit(solution)/shard_map/ppermute | solution.py:332
  13.0 10.0 %collective-permute-start.3 = (bf16[3,256,128]{2,1,0:T(8,128)(2,1)S(1)}, bf16[3,256,128]{2,1,0:T(8,128)(2,1)S(1)}, u32[]{:S(2)}, u32[]{:S(2)}) collective-permute-start(bf16[3,256,128]{2,1,0:T(8,128)(2,1)S(1)} %get-tuple-element.14.refs_1_.refs_2_), channel_id=1, source_target_pairs={{8,0},{16,8},{24,16},{28,24},{20,28},{12,20},{4,12},{0,4},{9,1},{1... | collective-permute-start | bytes 589832 | tf_op jit(solution)/shard_map/ppermute | solution.py:335
  14.5 8.5 %collective-permute-start.1 = (bf16[3,256,128]{2,1,0:T(8,128)(2,1)S(1)}, bf16[3,256,128]{2,1,0:T(8,128)(2,1)S(1)}, u32[]{:S(2)}, u32[]{:S(2)}) collective-permute-start(bf16[3,256,128]{2,1,0:T(8,128)(2,1)S(1)} %get-tuple-element.14.refs_1_.refs_2_), channel_id=1, source_target_pairs={{0,8},{8,16},{16,24},{24,28},{28,20},{20,12},{12,4},{4,0},{1,9},{9... | collective-permute-start | bytes 589832 | tf_op jit(solution)/shard_map/ppermute | solution.py:334
  15.0 1.4 %copy-start = (bf16[3,1024,256]{2,1,0:T(8,128)(2,1)S(1)}, bf16[3,1024,256]{2,1,0:T(8,128)(2,1)}, u32[]{:S(2)}) copy-start(bf16[3,1024,256]{2,1,0:T(8,128)(2,1)} %eig_ref.1) | copy-start | bytes 4718596
  16.9 0.6 copy-start.21
  18.8 9.0 %collective-permute-start.6 = (bf16[3,256,128]{2,1,0:T(8,128)(2,1)S(1)}, bf16[3,256,128]{2,1,0:T(8,128)(2,1)S(1)}, u32[]{:S(2)}, u32[]{:S(2)}) collective-permute-start(bf16[3,256,128]{2,1,0:T(8,128)(2,1)S(1)} %collective-permute-done.2.refs_4_.refs_5_), channel_id=1, source_target_pairs={{8,0},{16,8},{24,16},{28,24},{20,28},{12,20},{4,12},{0,4},{9,1},{1... | collective-permute-start | bytes 589832 | tf_op jit(solution)/shard_map/ppermute | solution.py:333
  23.3 19.8 %collective-permute-start.15 = (bf16[3,3,64,512]{3,2,1,0:T(8,128)(2,1)S(1)}, bf16[3,3,64,512]{3,2,1,0:T(8,128)(2,1)S(1)}, u32[]{:S(2)}, u32[]{:S(2)}) collective-permute-start(bf16[3,3,64,512]{3,2,1,0:T(8,128)(2,1)S(1)} %cut_columns.4.refs_17_), channel_id=1, source_target_pairs={{0,2},{4,6},{9,11},{13,15},{18,16},{22,20},{27,25},{31,29}} | collective-permute-start | bytes 1769480 | tf_op jit(solution)/shard_map/ppermute | solution.py:322
  25.3 7.4 %collective-permute-start.4 = (bf16[3,256,128]{2,1,0:T(8,128)(2,1)S(1)}, bf16[3,256,128]{2,1,0:T(8,128)(2,1)S(1)}, u32[]{:S(2)}, u32[]{:S(2)}) collective-permute-start(bf16[3,256,128]{2,1,0:T(8,128)(2,1)S(1)} %collective-permute-done.refs_2_.refs_3_), channel_id=1, source_target_pairs={{0,8},{8,16},{16,24},{24,28},{28,20},{20,12},{12,4},{4,0},{1,9},{9... | collective-permute-start | bytes 589832 | tf_op jit(solution)/shard_map/ppermute | solution.py:332
  25.6 8.0 %collective-permute-start.7 = (bf16[3,256,128]{2,1,0:T(8,128)(2,1)S(1)}, bf16[3,256,128]{2,1,0:T(8,128)(2,1)S(1)}, u32[]{:S(2)}, u32[]{:S(2)}) collective-permute-start(bf16[3,256,128]{2,1,0:T(8,128)(2,1)S(1)} %collective-permute-done.3.refs_5_.refs_6_), channel_id=1, source_target_pairs={{8,0},{16,8},{24,16},{28,24},{20,28},{12,20},{4,12},{0,4},{9,1},{1... | collective-permute-start | bytes 589832 | tf_op jit(solution)/shard_map/ppermute | solution.py:335
  27.4 8.5 %collective-permute-start.5 = (bf16[3,256,128]{2,1,0:T(8,128)(2,1)S(1)}, bf16[3,256,128]{2,1,0:T(8,128)(2,1)S(1)}, u32[]{:S(2)}, u32[]{:S(2)}) collective-permute-start(bf16[3,256,128]{2,1,0:T(8,128)(2,1)S(1)} %collective-permute-done.1.refs_3_.refs_4_), channel_id=1, source_target_pairs={{0,8},{8,16},{16,24},{24,28},{28,20},{20,12},{12,4},{4,0},{1,9},{9... | collective-permute-start | bytes 589832 | tf_op jit(solution)/shard_map/ppermute | solution.py:334
  27.8 9.6 %collective-permute-start.10 = (bf16[3,256,128]{2,1,0:T(8,128)(2,1)S(1)}, bf16[3,256,128]{2,1,0:T(8,128)(2,1)S(1)}, u32[]{:S(2)}, u32[]{:S(2)}) collective-permute-start(bf16[3,256,128]{2,1,0:T(8,128)(2,1)S(1)} %collective-permute-done.6.refs_2_.refs_9_), channel_id=1, source_target_pairs={{8,0},{16,8},{24,16},{28,24},{20,28},{12,20},{4,12},{0,4},{9,1},{1... | collective-permute-start | bytes 589832 | tf_op jit(solution)/shard_map/ppermute | solution.py:333
  32.7 7.3 %collective-permute-start.8 = (bf16[3,256,128]{2,1,0:T(8,128)(2,1)S(1)}, bf16[3,256,128]{2,1,0:T(8,128)(2,1)S(1)}, u32[]{:S(2)}, u32[]{:S(2)}) collective-permute-start(bf16[3,256,128]{2,1,0:T(8,128)(2,1)S(1)} %collective-permute-done.4.refs_0_.refs_7_), channel_id=1, source_target_pairs={{0,8},{8,16},{16,24},{24,28},{28,20},{20,12},{12,4},{4,0},{1,9},{9... | collective-permute-start | bytes 589832 | tf_op jit(solution)/shard_map/ppermute | solution.py:332
  33.6 10.4 %copy-start.1 = (bf16[3,256,128]{2,1,0:T(8,128)(2,1)}, bf16[3,256,128]{2,1,0:T(8,128)(2,1)S(1)}, u32[]{:S(2)}) copy-start(bf16[3,256,128]{2,1,0:T(8,128)(2,1)S(1)} %collective-permute-done.7.refs_3_.refs_10_) | copy-start | bytes 589828
  33.6 9.4 %collective-permute-start.11 = (bf16[3,256,128]{2,1,0:T(8,128)(2,1)S(1)}, bf16[3,256,128]{2,1,0:T(8,128)(2,1)S(1)}, u32[]{:S(2)}, u32[]{:S(2)}) collective-permute-start(bf16[3,256,128]{2,1,0:T(8,128)(2,1)S(1)} %collective-permute-done.7.refs_3_.refs_10_), channel_id=1, source_target_pairs={{8,0},{16,8},{24,16},{28,24},{20,28},{12,20},{4,12},{0,4},{9,1},{1... | collective-permute-start | bytes 589832 | tf_op jit(solution)/shard_map/ppermute | solution.py:335
  35.9 8.1 %copy-start.3 = (bf16[3,256,128]{2,1,0:T(8,128)(2,1)}, bf16[3,256,128]{2,1,0:T(8,128)(2,1)S(1)}, u32[]{:S(2)}) copy-start(bf16[3,256,128]{2,1,0:T(8,128)(2,1)S(1)} %collective-permute-done.5.refs_1_.refs_8_) | copy-start | bytes 589828
  35.9 22.2 %collective-permute-start.14 = (bf16[3,3,64,512]{3,2,1,0:T(8,128)(2,1)S(1)}, bf16[3,3,64,512]{3,2,1,0:T(8,128)(2,1)S(1)}, u32[]{:S(2)}, u32[]{:S(2)}) collective-permute-start(bf16[3,3,64,512]{3,2,1,0:T(8,128)(2,1)S(1)} %cut_columns.4.refs_17_), channel_id=1, source_target_pairs={{0,1},{4,5},{9,8},{13,12},{18,19},{22,23},{27,26},{31,30}} | collective-permute-start | bytes 1769480 | tf_op jit(solution)/shard_map/ppermute | solution.py:323
  37.4 13.4 %copy-start.5 = (bf16[3,256,128]{2,1,0:T(8,128)(2,1)}, bf16[3,256,128]{2,1,0:T(8,128)(2,1)S(1)}, u32[]{:S(2)}) copy-start(bf16[3,256,128]{2,1,0:T(8,128)(2,1)S(1)} %collective-permute-done.10.refs_2_.refs_13_) | copy-start | bytes 589828
  37.4 6.5 %collective-permute-start.9 = (bf16[3,256,128]{2,1,0:T(8,128)(2,1)S(1)}, bf16[3,256,128]{2,1,0:T(8,128)(2,1)S(1)}, u32[]{:S(2)}, u32[]{:S(2)}) collective-permute-start(bf16[3,256,128]{2,1,0:T(8,128)(2,1)S(1)} %collective-permute-done.5.refs_1_.refs_8_), channel_id=1, source_target_pairs={{0,8},{8,16},{16,24},{24,28},{28,20},{20,12},{12,4},{4,0},{1,9},{9... | collective-permute-start | bytes 589832 | tf_op jit(solution)/shard_map/ppermute | solution.py:334
  40.0 26.6 %copy-start.7 = (bf16[3,256,128]{2,1,0:T(8,128)(2,1)}, bf16[3,256,128]{2,1,0:T(8,128)(2,1)S(1)}, u32[]{:S(2)}) copy-start(bf16[3,256,128]{2,1,0:T(8,128)(2,1)S(1)} %collective-permute-done.8.refs_0_.refs_11_) | copy-start | bytes 589828
  40.0 16.8 %collective-permute-start.18 = (bf16[2,3,64,512]{3,2,1,0:T(8,128)(2,1)S(1)}, bf16[2,3,64,512]{3,2,1,0:T(8,128)(2,1)}, u32[]{:S(2)}, u32[]{:S(2)}) collective-permute-start(bf16[2,3,64,512]{3,2,1,0:T(8,128)(2,1)S(1)} %cut_columns.5.refs_21_), channel_id=1, source_target_pairs={{0,2},{4,6},{9,11},{13,15},{18,16},{22,20},{27,25},{31,29}} | collective-permute-start | bytes 1179656 | tf_op jit(solution)/shard_map/ppermute | solution.py:322
  43.0 23.5 %copy-start.9 = (bf16[3,256,128]{2,1,0:T(8,128)(2,1)}, bf16[3,256,128]{2,1,0:T(8,128)(2,1)S(1)}, u32[]{:S(2)}) copy-start(bf16[3,256,128]{2,1,0:T(8,128)(2,1)S(1)} %collective-permute-done.11.refs_3_.refs_14_) | copy-start | bytes 589828
  43.0 5.8 %collective-permute-start.12 = (bf16[3,256,128]{2,1,0:T(8,128)(2,1)S(1)}, bf16[3,256,128]{2,1,0:T(8,128)(2,1)S(1)}, u32[]{:S(2)}, u32[]{:S(2)}) collective-permute-start(bf16[3,256,128]{2,1,0:T(8,128)(2,1)S(1)} %collective-permute-done.8.refs_0_.refs_11_), channel_id=1, source_target_pairs={{0,8},{8,16},{16,24},{24,28},{28,20},{20,12},{12,4},{4,0},{1,9},{9... | collective-permute-start | bytes 589832 | tf_op jit(solution)/shard_map/ppermute | solution.py:343
  43.0 23.5 %copy-start.13 = (bf16[3,3,64,512]{3,2,1,0:T(8,128)(2,1)}, bf16[3,3,64,512]{3,2,1,0:T(8,128)(2,1)S(1)}, u32[]{:S(2)}) copy-start(bf16[3,3,64,512]{3,2,1,0:T(8,128)(2,1)S(1)} %collective-permute-done.15.refs_19_) | copy-start | bytes 1769476
  43.1 20.7 %collective-permute-start.16 = (bf16[3,3,64,512]{3,2,1,0:T(8,128)(2,1)S(1)}, bf16[3,3,64,512]{3,2,1,0:T(8,128)(2,1)S(1)}, u32[]{:S(2)}, u32[]{:S(2)}) collective-permute-start(bf16[3,3,64,512]{3,2,1,0:T(8,128)(2,1)S(1)} %collective-permute-done.15.refs_19_), channel_id=1, source_target_pairs={{2,3},{6,7},{11,10},{15,14},{16,17},{20,21},{25,24},{29,28}} | collective-permute-start | bytes 1769480 | tf_op jit(solution)/shard_map/ppermute | solution.py:324
  44.0 22.6 %copy-start.11 = (bf16[3,256,128]{2,1,0:T(8,128)(2,1)}, bf16[3,256,128]{2,1,0:T(8,128)(2,1)S(1)}, u32[]{:S(2)}) copy-start(bf16[3,256,128]{2,1,0:T(8,128)(2,1)S(1)} %collective-permute-done.9.refs_1_.refs_12_) | copy-start | bytes 589828
  44.0 7.7 %collective-permute-start.13 = (bf16[3,256,128]{2,1,0:T(8,128)(2,1)S(1)}, bf16[3,256,128]{2,1,0:T(8,128)(2,1)S(1)}, u32[]{:S(2)}, u32[]{:S(2)}) collective-permute-start(bf16[3,256,128]{2,1,0:T(8,128)(2,1)S(1)} %collective-permute-done.11.refs_3_.refs_14_), channel_id=1, source_target_pairs={{8,0},{16,8},{24,16},{28,24},{20,28},{12,20},{4,12},{0,4},{9,1},{1... | collective-permute-start | bytes 589832 | tf_op jit(solution)/shard_map/ppermute | solution.py:344
  48.8 13.5 %collective-permute-start.21 = (bf16[2,3,64,512]{3,2,1,0:T(8,128)(2,1)S(1)}, bf16[2,3,64,512]{3,2,1,0:T(8,128)(2,1)}, u32[]{:S(2)}, u32[]{:S(2)}) collective-permute-start(bf16[2,3,64,512]{3,2,1,0:T(8,128)(2,1)S(1)} %cut_columns.6.refs_25_), channel_id=1, source_target_pairs={{0,2},{4,6},{9,11},{13,15},{18,16},{22,20},{27,25},{31,29}} | collective-permute-start | bytes 1179656 | tf_op jit(solution)/shard_map/ppermute | solution.py:322
  51.8 9.1 %collective-permute-start.24 = (bf16[1,3,64,512]{3,2,1,0:T(8,128)(2,1)S(1)}, bf16[1,3,64,512]{3,2,1,0:T(8,128)(2,1)}, u32[]{:S(2)}, u32[]{:S(2)}) collective-permute-start(bf16[1,3,64,512]{3,2,1,0:T(8,128)(2,1)S(1)} %cut_columns.7.refs_29_), channel_id=1, source_target_pairs={{0,2},{4,6},{9,11},{13,15},{18,16},{22,20},{27,25},{31,29}} | collective-permute-start | bytes 589832 | tf_op jit(solution)/shard_map/ppermute | solution.py:322
  56.8 9.8 %collective-permute-start.17 = (bf16[2,3,64,512]{3,2,1,0:T(8,128)(2,1)S(1)}, bf16[2,3,64,512]{3,2,1,0:T(8,128)(2,1)S(1)}, u32[]{:S(2)}, u32[]{:S(2)}) collective-permute-start(bf16[2,3,64,512]{3,2,1,0:T(8,128)(2,1)S(1)} %cut_columns.5.refs_21_), channel_id=1, source_target_pairs={{0,1},{4,5},{9,8},{13,12},{18,19},{22,23},{27,26},{31,30}} | collective-permute-start | bytes 1179656 | tf_op jit(solution)/shard_map/ppermute | solution.py:323
  58.1 0.8 copy-start.15
  58.9 19.6 %collective-permute-start.20 = (bf16[2,3,64,512]{3,2,1,0:T(8,128)(2,1)S(1)}, bf16[2,3,64,512]{3,2,1,0:T(8,128)(2,1)}, u32[]{:S(2)}, u32[]{:S(2)}) collective-permute-start(bf16[2,3,64,512]{3,2,1,0:T(8,128)(2,1)S(1)} %cut_columns.6.refs_25_), channel_id=1, source_target_pairs={{0,1},{4,5},{9,8},{13,12},{18,19},{22,23},{27,26},{31,30}} | collective-permute-start | bytes 1179656 | tf_op jit(solution)/shard_map/ppermute | solution.py:323
  61.0 17.5 %collective-permute-start.19 = (bf16[2,3,64,512]{3,2,1,0:T(8,128)(2,1)}, bf16[2,3,64,512]{3,2,1,0:T(8,128)(2,1)}, u32[]{:S(2)}, u32[]{:S(2)}) collective-permute-start(bf16[2,3,64,512]{3,2,1,0:T(8,128)(2,1)} %collective-permute-done.18.refs_23_), channel_id=1, source_target_pairs={{2,3},{6,7},{11,10},{15,14},{16,17},{20,21},{25,24},{29,28}} | collective-permute-start | bytes 1179656 | tf_op jit(solution)/shard_map/ppermute | solution.py:324
  62.4 16.1 %collective-permute-start.22 = (bf16[2,3,64,512]{3,2,1,0:T(8,128)(2,1)}, bf16[2,3,64,512]{3,2,1,0:T(8,128)(2,1)}, u32[]{:S(2)}, u32[]{:S(2)}) collective-permute-start(bf16[2,3,64,512]{3,2,1,0:T(8,128)(2,1)} %collective-permute-done.21.refs_27_), channel_id=1, source_target_pairs={{2,3},{6,7},{11,10},{15,14},{16,17},{20,21},{25,24},{29,28}} | collective-permute-start | bytes 1179656 | tf_op jit(solution)/shard_map/ppermute | solution.py:324
  63.8 0.8 copy-start.17
  64.6 13.9 %collective-permute-start.23 = (bf16[1,3,64,512]{3,2,1,0:T(8,128)(2,1)S(1)}, bf16[1,3,64,512]{3,2,1,0:T(8,128)(2,1)}, u32[]{:S(2)}, u32[]{:S(2)}) collective-permute-start(bf16[1,3,64,512]{3,2,1,0:T(8,128)(2,1)S(1)} %cut_columns.7.refs_29_), channel_id=1, source_target_pairs={{0,1},{4,5},{9,8},{13,12},{18,19},{22,23},{27,26},{31,30}} | collective-permute-start | bytes 589832 | tf_op jit(solution)/shard_map/ppermute | solution.py:323
  66.6 0.8 copy-start.19
  67.4 11.1 %collective-permute-start.25 = (bf16[1,3,64,512]{3,2,1,0:T(8,128)(2,1)}, bf16[1,3,64,512]{3,2,1,0:T(8,128)(2,1)}, u32[]{:S(2)}, u32[]{:S(2)}) collective-permute-start(bf16[1,3,64,512]{3,2,1,0:T(8,128)(2,1)} %collective-permute-done.24.refs_31_), channel_id=1, source_target_pairs={{2,3},{6,7},{11,10},{15,14},{16,17},{20,21},{25,24},{29,28}} | collective-permute-start | bytes 589832 | tf_op jit(solution)/shard_map/ppermute | solution.py:324
  68.7 8.2 %all-to-all-start.1 = ((f32[4,32,128]{2,1,0:T(8,128)}), f32[4,32,128]{2,1,0:T(8,128)}, u32[]{:S(2)}, u32[]{:S(2)}) async-start(f32[4,32,128]{2,1,0:T(8,128)} %copy-done.21), calls=%async_computation.1 | async-start | bytes 131072 | tf_op jit(solution)/shard_map/all_to_all | solution.py:293
  78.5 0.9 copy-start.2
  79.4 0.9 copy-start.4
  80.3 0.9 copy-start.6
  81.3 0.9 copy-start.8
  82.2 0.9 copy-start.10
  83.1 0.9 copy-start.12
  84.1 1.1 %copy-start.14 = (bf16[3,3,64,512]{3,2,1,0:T(8,128)(2,1)S(1)}, bf16[3,3,64,512]{3,2,1,0:T(8,128)(2,1)}, u32[]{:S(2)}) copy-start(bf16[3,3,64,512]{3,2,1,0:T(8,128)(2,1)} %copy-done.13) | copy-start | bytes 1769476
  85.1 1.1 %copy-start.16 = (bf16[3,3,64,512]{3,2,1,0:T(8,128)(2,1)S(1)}, bf16[3,3,64,512]{3,2,1,0:T(8,128)(2,1)}, u32[]{:S(2)}) copy-start(bf16[3,3,64,512]{3,2,1,0:T(8,128)(2,1)} %copy-done.15) | copy-start | bytes 1769476
  86.2 1.1 %copy-start.18 = (bf16[3,3,64,512]{3,2,1,0:T(8,128)(2,1)S(1)}, bf16[3,3,64,512]{3,2,1,0:T(8,128)(2,1)}, u32[]{:S(2)}) copy-start(bf16[3,3,64,512]{3,2,1,0:T(8,128)(2,1)} %copy-done.17) | copy-start | bytes 1769476
  87.2 1.0 %copy-start.20 = (bf16[2,3,64,512]{3,2,1,0:T(8,128)(2,1)S(1)}, bf16[2,3,64,512]{3,2,1,0:T(8,128)(2,1)}, u32[]{:S(2)}) copy-start(bf16[2,3,64,512]{3,2,1,0:T(8,128)(2,1)} %copy-done.19) | copy-start | bytes 1179652

commit v7 on v6

--- a/solution.py
+++ b/solution.py
@@ -59,18 +59,17 @@
     out = jnp.zeros(shape, jnp.float32)
     for k, value in enumerate(values):
         out = jnp.where(lane == k, jnp.broadcast_to(value, shape), out)
-    turned = out.T[:STATS]
-    for k in range(out_ref.shape[0]):
-        out_ref[k] = jnp.concatenate([turned, jnp.zeros_like(turned)], axis=1)
+    out_ref[...] = out.T[:STATS]
 
 
 def align_kernel(parts, *refs):
-    stats, x_ref, ref_ref, first_ref, second_ref, flat_ref, turn = refs
+    stats = refs[:parts]
+    x_ref, ref_ref, piece_ref, flat_ref, turn = refs[parts:]
     local = x_ref.shape[2]
     rows = x_ref.shape[1]
 
     def row(at):
-        return [stats[p, at : at + 1, :] for p in range(parts)]
+        return [s[at : at + 1, :] for s in stats]
 
     means = [row(i) for i in range(3)]
     ref_means = [row(13 + j) for j in range(3)]
@@ -103,7 +102,7 @@
             for i in range(3)
         ]
     for k, value in enumerate(sum(now, []) + centre + ref_centre):
-        turn[k : k + 1, :] = value
+        turn[k : k + 1, :rows] = value
     turned = turn[...].T
     column = [turned[:rows, k : k + 1] for k in range(12)]
     centred = [x_ref[j] - column[9 + j] for j in range(3)]
@@ -111,41 +110,63 @@
         target = ref_ref[i : i + 1, :] - turned[0:1, 12 + i : 13 + i]
         moved = sum(column[3 * j + i] * centred[j] for j in range(3)) - target
         flat_ref[i] = moved.astype(jnp.bfloat16)
-        run = first_ref.shape[1]
-        for at, piece in enumerate((first_ref, second_ref)):
+        run = piece_ref.shape[2]
+        for at in range(2):
             pair = [moved[:, (2 * at + k) * run : (2 * at + k + 1) * run] for k in range(2)]
-            piece[i] = jnp.concatenate(pair, axis=0).T.astype(jnp.bfloat16)
-
-
-def project_kernel(flat_ref, eig_ref, out_ref):
+            piece_ref[at, i] = jnp.concatenate(pair, axis=0).T.astype(jnp.bfloat16)
+
+
+def project_kernel(me_ref, flat_ref, eig_ref, *refs):
+    shares, cut = refs[:-1], refs[-1]
     total = sum(
         jnp.dot(flat_ref[c], eig_ref[c], preferred_element_type=jnp.float32) for c in range(3)
     )
-    middle, width = out_ref.shape[1], out_ref.shape[2] // 2
-    for k in range(out_ref.shape[0]):
-        part = total[:, k * width : (k + 1) * width]
-        out_ref[k] = jnp.concatenate([part[:middle], part[middle:]], axis=1)
-
-
-def sum_kernel(parts_ref, out_ref):
-    middle, width = parts_ref.shape[1], parts_ref.shape[2] // 2
-    total = sum(parts_ref[k] for k in range(parts_ref.shape[0]))
-    out_ref[:middle] = total[:, :width]
-    out_ref[middle:] = total[:, width:]
-
-
-def cut_kernel(slots, half_ref, *refs):
-    sources, cols_ref = refs[: 2 * slots], refs[2 * slots]
-    run, lanes = sources[0].shape[1:]
+    width = cut.shape[2]
+    for k in range(len(shares)):
+        cut[k] = total[:, k * width : (k + 1) * width]
+    for k, share in enumerate(shares):
+        share[...] = cut[lax.bitwise_xor(me_ref[0], k)]
+
+
+def sum_kernel(*refs):
+    refs[-1][...] = sum(ref[...] for ref in refs[:-1])
+
+
+def cut_columns(half_ref, halves, cols_ref):
     for half in range(2):
 
         @pl.when(half_ref[0] == half)
         def _(half=half):
-            for k, source in enumerate(sources[half::2]):
+            for k, pair in enumerate(halves):
+                run, lanes = pair[half].shape[1:]
                 for c in range(3):
-                    turned = source[c].astype(jnp.float32).T.astype(jnp.bfloat16)
+                    turned = pair[half][c].astype(jnp.float32).T.astype(jnp.bfloat16)
                     cols_ref[k, c, :, :run] = turned[: lanes // 2]
                     cols_ref[k, c, :, run:] = turned[lanes // 2 :]
+
+
+def cut_kernel(half_ref, *refs):
+    cut_columns(half_ref, [(r.at[0], r.at[1]) for r in refs[:-1]], refs[-1])
+
+
+def cut_last_kernel(half_ref, up_ref, down_ref, cols_ref, up_half, down_half):
+    up_half[...] = up_ref[0]
+    down_half[...] = down_ref[1]
+    cut_columns(half_ref, [(r.at[0], r.at[1]) for r in (up_ref, down_ref)], cols_ref)
+
+
+def cut_far_kernel(half_ref, up_half, down_half, cols_ref):
+    cut_columns(half_ref, [(up_half, down_half)], cols_ref)
+
+
+def pass_on_kernel(role_ref, cut_ref, across_ref, out_ref):
+    @pl.when(role_ref[0] == 0)
+    def _():
+        out_ref[...] = cut_ref[...]
+
+    @pl.when(role_ref[0] != 0)
+    def _():
+        out_ref[...] = across_ref[...]
 
 
 def side_by_side(first, second):
@@ -155,30 +176,69 @@
     return left, right
 
 
-def covariance_kernel(slots, roles, lots, scale, *refs):
-    role_ref, pieces = refs[0], refs[1 : 1 + 2 * slots]
-    at = 1 + 2 * slots
-    groups = [refs[at + k * roles : at + (k + 1) * roles] for k in range(len(lots))]
-    at += len(lots) * roles
-    out_ref, left, right, done, out_sem = refs[at:]
+def covariance_kernel(slots, roles, groups, scale, role_ref, *refs):
+    shards, up_half, down_half = refs[: slots - 1], refs[slots - 1], refs[slots]
+    refs = refs[slots + 1 :]
+    arrays = []
+    for _, _, holder in groups:
+        count = max(holder) + 1
+        arrays.append(refs[:count])
+        refs = refs[count:]
+    out_ref, left, right, done, col_sem, out_sem = refs
     depth = right.shape[1] // slots
-    run = pieces[0].shape[1]
-    for role in range(roles):
-
-        @pl.when(role_ref[0] == role)
-        def _(role=role):
-            to = 0
-            for k, count in enumerate(lots):
-                for n in range(count):
-                    for d in range(3):
-                        right[d, to : to + depth, :] = groups[k][role][n, d]
-                    to += depth
+    run = up_half.shape[1]
+
+    def fetches(k, role, to):
+        source = arrays[k][groups[k][2][role]]
+        return [
+            pltpu.make_async_copy(
+                source.at[n],
+                right.at[:, pl.ds(to + n * depth, depth), :],
+                col_sem.at[to // depth + n],
+            )
+            for n in range(groups[k][0])
+        ]
+
+    def for_each_group(from_hbm, act):
+        for role in range(roles):
+
+            @pl.when(role_ref[0] == role)
+            def _(role=role):
+                to = 0
+                for k, (count, in_hbm, _) in enumerate(groups):
+                    if in_hbm == from_hbm:
+                        act(k, role, to)
+                    to += count * depth
+
+    def start(k, role, to):
+        for copy in fetches(k, role, to):
+            copy.start()
+
+    def wait(k, role, to):
+        for copy in fetches(k, role, to):
+            copy.wait()
+
+    def load(k, role, to):
+        source = arrays[k][groups[k][2][role]]
+        for n in range(groups[k][0]):
+            for d in range(3):
+                right[d, to + n * depth : to + (n + 1) * depth, :] = source[n, d]
+
+    def piece(slot, at, c):
+        if slot < slots - 1:
+            return shards[slot][at, c]
+        return (up_half, down_half)[at][c]
 
     def assemble(c, at):
         for q in range(slots // 2):
-            low, high = side_by_side(pieces[4 * q + at][c], pieces[4 * q + 2 + at][c])
+            low, high = side_by_side(piece(2 * q, at, c), piece(2 * q + 1, at, c))
             left[at, :run, q * LANES : (q + 1) * LANES] = low
             left[at, run:, q * LANES : (q + 1) * LANES] = high
+
+    for_each_group(True, start)
+    for_each_group(False, load)
+    assemble(0, 0)
+    for_each_group(True, wait)
 
     def write(c, at, d):
         return pltpu.make_async_copy(
@@ -186,8 +246,6 @@
             out_ref.at[c, d, pl.ds(at * 2 * run, 2 * run), :],
             out_sem.at[at, d],
         )
-
-    assemble(0, 0)
 
     @pl.loop(0, 3)
     def _(c):
@@ -250,7 +308,7 @@
     stats, x, mean_structure = pl.pallas_call(
         stats_kernel,
         out_shape=(
-            pltpu.VMEM((atom_axis, STATS, LANES), jnp.float32),
+            pltpu.VMEM((STATS, local_frames), jnp.float32),
             pltpu.VMEM(x.shape, jnp.float32),
             pltpu.VMEM(mean_structure.shape, jnp.float32),
         ),
@@ -260,37 +318,43 @@
         compiler_params=params(8),
         name="local_moments",
     )(x, mean_structure)
-    stats = lax.all_to_all(stats, "atoms", split_axis=0, concat_axis=0, tiled=True)
+    def swap(value, distance):
+        return lax.ppermute(value, "atoms", [(a, a ^ distance) for a in range(atom_axis)])
+
+    others = [swap(stats, d) for d in range(1, atom_axis)]
     run = local_atoms // 4
-    piece = jax.ShapeDtypeStruct((3, run, 2 * local_frames), jnp.bfloat16)
-    first, second, flat = pl.pallas_call(
+    piece = (3, run, 2 * local_frames)
+    own, flat = pl.pallas_call(
         functools.partial(align_kernel, atom_axis),
-        out_shape=(piece, piece, jax.ShapeDtypeStruct(x.shape, jnp.bfloat16)),
-        in_specs=[VMEM, VMEM, VMEM],
-        out_specs=(VMEM, VMEM, VMEM),
+        out_shape=(
+            jax.ShapeDtypeStruct((2,) + piece, jnp.bfloat16),
+            jax.ShapeDtypeStruct(x.shape, jnp.bfloat16),
+        ),
+        in_specs=[VMEM] * (atom_axis + 2),
+        out_specs=(VMEM, VMEM),
         scratch_shapes=[pltpu.VMEM((LANES, LANES), jnp.float32)],
         compiler_params=params(8),
         name="polar_align",
-    )(stats, x, mean_structure)
-    share = (local_frames, eigvecs.shape[2] // atom_axis)
+    )(stats, *others, x, mean_structure)
+    share = jax.ShapeDtypeStruct((local_frames, eigvecs.shape[2] // atom_axis), jnp.float32)
     shares = pl.pallas_call(
         project_kernel,
-        out_shape=jax.ShapeDtypeStruct(
-            (atom_axis, local_frames // 2, 2 * share[1]), jnp.float32
-        ),
-        in_specs=[VMEM, VMEM],
-        out_specs=VMEM,
+        out_shape=(share,) * atom_axis,
+        in_specs=[SMEM, VMEM, VMEM],
+        out_specs=(VMEM,) * atom_axis,
+        scratch_shapes=[pltpu.VMEM((atom_axis,) + share.shape, jnp.float32)],
         compiler_params=params(8),
         name="project",
-    )(flat, eigvecs)
+    )(me_a.astype(jnp.int32).reshape(1), flat, eigvecs)
+    parts = [shares[0]] + [swap(shares[d], d) for d in range(1, atom_axis)]
     projections = pl.pallas_call(
         sum_kernel,
-        out_shape=jax.ShapeDtypeStruct(share, jnp.float32),
-        in_specs=[VMEM],
+        out_shape=share,
+        in_specs=[VMEM] * atom_axis,
         out_specs=VMEM,
         compiler_params=params(4),
         name="sum_shares",
-    )(lax.all_to_all(shares, "atoms", split_axis=0, concat_axis=0, tiled=True))
+    )(*parts)
 
     def pairs(source, target):
         return [
@@ -308,68 +372,95 @@
         )
         return covariance, projections
 
-    def spread(pieces, earlier, before_last=()):
-        slots = len(pieces) // 2
-        cut = pl.pallas_call(
-            functools.partial(cut_kernel, slots),
-            out_shape=pltpu.VMEM((slots, 3, local_frames, block), jnp.bfloat16),
-            in_specs=[SMEM] + [VMEM] * len(pieces),
-            out_specs=VMEM,
+    axes = ("frames", "atoms")
+
+    def columns(slots):
+        return pltpu.VMEM((slots, 3, local_frames, block), jnp.bfloat16)
+
+    def kernel(body, out_shape, scalar, values, name):
+        single = not isinstance(out_shape, tuple)
+        return pl.pallas_call(
+            body,
+            out_shape=out_shape,
+            in_specs=[SMEM] + [VMEM] * len(values),
+            out_specs=VMEM if single else (VMEM,) * len(out_shape),
             compiler_params=params(4),
-            name="cut_columns",
-        )(after(half, *earlier), *[pinned(piece, pltpu.VMEM) for piece in pieces])
-        axes = ("frames", "atoms")
+            name=name,
+        )(scalar, *[pinned(value, pltpu.VMEM) for value in values])
+
+    def spread_paired(cut):
         across = lax.ppermute(cut, axes, pairs(0, 2))
-        beside = lax.ppermute(cut, axes, pairs(0, 1))
-        last = lax.ppermute(after(across, *before_last), axes, pairs(2, 3))
-        return [cut, beside, across, last]
+        held = kernel(pass_on_kernel, columns(cut.shape[0]), role, [cut, across], "pass_on")
+        return [held, lax.ppermute(held, axes, pairs(0, 1) + pairs(2, 3))]
 
     order = ring_order(frame_axis)
     forward = [(order[i], order[(i + 1) % frame_axis]) for i in range(frame_axis)]
     backward = [(b, a) for a, b in forward]
 
     def hop(up, down):
-        up_a = lax.ppermute(up[0], "frames", forward)
-        down_a = lax.ppermute(down[0], "frames", backward)
-        up_b = lax.ppermute(up[1], "frames", forward)
-        down_b = lax.ppermute(down[1], "frames", backward)
-        return [up_a, up_b], [down_a, down_b]
-
-    own = [first, second]
-    up1, down1 = hop(own, own)
-    up2, down2 = hop(up1, down1)
-    up3, down3 = hop(up2, down2)
-    far = [
-        lax.ppermute(up3[0], "frames", forward),
-        lax.ppermute(down3[1], "frames", backward),
-    ]
-    lots = [own + up1 + down1, up2 + down2, up3 + down3, far]
-    cuts = [spread(lots[0], [shares]), spread(lots[1], []), spread(lots[2], [])]
-    cuts.append(spread(far, [], cuts[0][1:]))
-    cuts = sum(cuts, [])
-    pieces = sum(lots, [])
-    counts = [len(lot) // 2 for lot in lots]
+        return lax.ppermute(up, "frames", forward), lax.ppermute(down, "frames", backward)
+
+    one = hop(own, own)
+    cut_one = kernel(cut_kernel, columns(3), after(half, *shares), [own, *one], "cut_columns")
+    in_hbm = spread_paired(cut_one)
+    two = hop(*one)
+    cut_two = kernel(cut_kernel, columns(2), after(half, *parts), list(two), "cut_columns")
+    three = hop(*two)
+    half_shard = pltpu.VMEM(piece, jnp.bfloat16)
+    cut_three, *halves = kernel(
+        cut_last_kernel,
+        (columns(2), half_shard, half_shard),
+        after(half, projections, in_hbm[0]),
+        list(three),
+        "cut_columns",
+    )
+    far = hop(*halves)
+    cut_four = kernel(cut_far_kernel, columns(1), half, list(far), "cut_columns")
+
+    direct = [cut_three] + [lax.ppermute(cut_three, axes, pairs(0, d)) for d in (1, 2, 3)]
+    across = lax.ppermute(cut_four, axes, pairs(0, 2))
+    beside = lax.ppermute(cut_four, axes, pairs(0, 1))
+    last = lax.ppermute(across, axes, pairs(2, 3))
+
+    groups = (
+        (3, True, (0, 1, 0, 1)),
+        (2, True, (0, 1, 0, 1)),
+        (2, False, (0, 1, 2, 3)),
+        (1, False, (0, 1, 2, 3)),
+    )
+    in_hbm += spread_paired(cut_two)
+    in_vmem = direct + [cut_four, beside, across, last]
+    rows = [own, *one, *two, *three, *far]
     covariance = pl.pallas_call(
         functools.partial(
-            covariance_kernel, frame_axis, atom_axis, counts, 1.0 / total_frames
+            covariance_kernel, frame_axis, atom_axis, groups, 1.0 / total_frames
         ),
         out_shape=jax.ShapeDtypeStruct((3, 3, local_atoms, block), jnp.float32),
-        in_specs=[SMEM] + [VMEM] * (len(pieces) + len(cuts)),
+        in_specs=[SMEM]
+        + [VMEM] * len(rows)
+        + [HBM] * len(in_hbm)
+        + [VMEM] * len(in_vmem),
         out_specs=ANY,
         scratch_shapes=[
             pltpu.VMEM((2, 2 * run, total_frames), jnp.bfloat16),
             pltpu.VMEM((3, total_frames, block), jnp.bfloat16),
             pltpu.VMEM((2, 3, 2 * run, block), jnp.float32),
+            pltpu.SemaphoreType.DMA((frame_axis,)),
             pltpu.SemaphoreType.DMA((2, 3)),
         ],
-        compiler_params=params(24),
+        compiler_params=params(16),
         cost_estimate=pl.CostEstimate(
             flops=18 * local_atoms * block * total_frames,
             bytes_accessed=24 * MIB,
             transcendentals=0,
         ),
         name="covariance_tile",
-    )(role, *[pinned(value, pltpu.VMEM) for value in pieces + cuts])
+    )(
+        role,
+        *[pinned(value, pltpu.VMEM) for value in rows],
+        *[pinned(value, pltpu.HBM) for value in in_hbm],
+        *[pinned(value, pltpu.VMEM) for value in in_vmem],
+    )
     return jnp.transpose(covariance, (0, 2, 1, 3)), projections
 
 

time: 98.3 us -> 83.3 us (0.85)
  waiting for transfers between devices: 15.7 us -> 31.8 us
  starting transfers between devices: 44.4 us -> 31.8 us
  local copies, waits for them, and re-layouts: 14.2 us -> 3.24 us
  blocking collectives: 8.04 us -> 0 us
    ppermute x26 -> x24, waiting for transfers between devices: 11.4 us -> 31.8 us  [the longest x4 10.8 us: hop(): lax.ppermute(down, 'frames', backward)]
    unnamed x44 -> x14, local copies, waits for them, and re-layouts: 14.2 us -> 3.24 us
    ppermute x26 -> x24, starting transfers between devices: 40.6 us -> 31.8 us  [the longest x2 8.24 us: spread_paired(): across = lax.ppermute(cut, axes, pairs(0, 2))]
    all_to_all x1 -> x0, blocking collectives: 8.04 us -> none  [per_device(): lax.all_to_all(stats, 'atoms', split_axis=0, concat_axis=0, tiled=True)]
    all_to_all x1 -> x0, waiting for transfers between devices: 4.31 us -> none  [per_device(): lax.all_to_all(shares, 'atoms', split_axis=0, concat_axis=0, tiled=True)]
    all_to_all x1 -> x0, starting transfers between devices: 3.89 us -> none  [per_device(): lax.all_to_all(shares, 'atoms', split_axis=0, concat_axis=0, tiled=True)]
    pallas_call x8 -> x10, Pallas kernels: 4.98 us -> 6.26 us  [the longest x6 2.9 us: kernel(): pl.pallas_call(body, out_shape=out_shape, in_specs=[SMEM] + [VMEM] * len(...]
  transfers between devices with their start and end apart: 27 -> 24, of which waited for: 10 -> 13; matrix products, arithmetic and copies ran while one was open for 0% -> 0% of each run, Pallas kernels for 3% -> 5%
where the time goes in v7:
time: 83.3 us; the launch traced here: 82.5 us
  starting transfers between devices  31.8 us (38%)
  waiting for transfers between devices  31.8 us (38%)
  Pallas kernels  14.8 us (18%)
  local copies, waits for them, and re-layouts  3.24 us (4%)
  between operations  0.86 us (1%)
    ppermute x4, waiting for transfers between devices, hop(): lax.ppermute(down, 'frames', backward)  10.8 us
    ppermute x6, waiting for transfers between devices, swap(): lax.ppermute(value, 'atoms', [(a, a ^ distance) for a in range(atom_axis)])  10.3 us
    pallas_call x1, Pallas kernels, per_device(): pl.pallas_call(functools.partial(covariance_kernel, frame_axis, atom_axis...  8.58 us
    ppermute x2, starting transfers between devices, spread_paired(): across = lax.ppermute(cut, axes, pairs(0, 2))  8.24 us
    ppermute x4, starting transfers between devices, hop(): lax.ppermute(down, 'frames', backward)  5.9 us
    ppermute x4, waiting for transfers between devices, hop(): lax.ppermute(up, 'frames', forward)  5.11 us
    ppermute x3, starting transfers between devices, per_device(): lax.ppermute(cut_three, axes, pairs(0, d))  3.94 us
    ppermute x6, starting transfers between devices, swap(): lax.ppermute(value, 'atoms', [(a, a ^ distance) for a in range(atom_axis)])  3.78 us
  transfers between devices with their start and end apart: 24, of which 13 were waited for; matrix products, arithmetic and copies ran while one was open for 0% of the time, Pallas kernels for 5%

profile of v7, /device:TPU:0, one launch (start us, length us, event | category | flops | bytes accessed | tf_op | source)
XLA Modules:
  0.0 82.5 jit_solution(9327062324728068924)
XLA Ops:
  0.6 1.7 %local_moments.1 = (f32[24,64]{1,0:T(8,128)S(1)}, f32[3,64,1024]{2,1,0:T(8,128)S(1)}, f32[3,1024]{1,0:T(4,128)S(1)}) custom-call(f32[3,64,1024]{2,1,0:T(8,128)} %bitcast.6, f32[3,1024]{1,0:T(4,128)} %ref_hbm.1), custom_call_target="tpu_custom_call" | custom-call | tf_op jit(solution)/shard_map/local_moments/pallas_call | solution.py:308
  2.3 2.4 %collective-permute-start.2 = (f32[24,64]{1,0:T(8,128)S(1)}, f32[24,64]{1,0:T(8,128)S(1)}, u32[]{:S(2)}, u32[]{:S(2)}) collective-permute-start(f32[24,64]{1,0:T(8,128)S(1)} %get-tuple-element.17.refs_0_), channel_id=1, source_target_pairs={{0,3},{1,2},{2,1},{3,0},{4,7},{5,6},{6,5},{7,4},{8,11},{9,10},{10,... | collective-permute-start | bytes 18440 | tf_op jit(solution)/shard_map/ppermute | solution.py:322
  4.7 0.6 collective-permute-start.1
  5.4 0.0 collective-permute-start
  5.4 0.7 collective-permute-done.2.refs_3_
  6.1 2.3 %collective-permute-done.1.refs_2_ = f32[24,64]{1,0:T(8,128)S(1)} collective-permute-done((f32[24,64]{1,0:T(8,128)S(1)}, f32[24,64]{1,0:T(8,128)S(1)}, u32[]{:S(2)}, u32[]{:S(2)}) %collective-permute-start.1) | collective-permute-done | bytes 6176 | tf_op jit(solution)/shard_map/ppermute | solution.py:322
  8.4 0.0 collective-permute-done.refs_1_
  8.4 0.6 polar_align.1
  9.0 1.6 %collective-permute-start.4 = (bf16[2,3,256,128]{3,2,1,0:T(8,128)(2,1)S(1)}, bf16[2,3,256,128]{3,2,1,0:T(8,128)(2,1)S(1)}, u32[]{:S(2)}, u32[]{:S(2)}) collective-permute-start(bf16[2,3,256,128]{3,2,1,0:T(8,128)(2,1)S(1)} %get-tuple-element.20.refs_0_), channel_id=1, source_target_pairs={{8,0},{16,8},{24,16},{28,24},{20,28},{12,20},{4,12},{0,4},{9,1},{1... | collective-permute-start | bytes 1179656 | tf_op jit(solution)/shard_map/ppermute | solution.py:401
  10.6 0.5 collective-permute-start.3
  11.1 8.5 %collective-permute-done.4.refs_2_ = bf16[2,3,256,128]{3,2,1,0:T(8,128)(2,1)S(1)} collective-permute-done((bf16[2,3,256,128]{3,2,1,0:T(8,128)(2,1)S(1)}, bf16[2,3,256,128]{3,2,1,0:T(8,128)(2,1)S(1)}, u32[]{:S(2)}, u32[]{:S(2)}) %collective-permute-start.4) | collective-permute-done | bytes 393248 | tf_op jit(solution)/shard_map/ppermute | solution.py:401
  19.6 1.5 %collective-permute-start.6 = (bf16[2,3,256,128]{3,2,1,0:T(8,128)(2,1)S(1)}, bf16[2,3,256,128]{3,2,1,0:T(8,128)(2,1)S(1)}, u32[]{:S(2)}, u32[]{:S(2)}) collective-permute-start(bf16[2,3,256,128]{3,2,1,0:T(8,128)(2,1)S(1)} %collective-permute-done.4.refs_2_), channel_id=1, source_target_pairs={{8,0},{16,8},{24,16},{28,24},{20,28},{12,20},{4,12},{0,4},{9,1},{1... | collective-permute-start | bytes 1179656 | tf_op jit(solution)/shard_map/ppermute | solution.py:401
  21.2 0.0 collective-permute-done.3.refs_1_
  21.2 0.5 collective-permute-start.5
  21.7 1.4 %copy-done.1 = bf16[3,1024,256]{2,1,0:T(8,128)(2,1)S(1)} copy-done((bf16[3,1024,256]{2,1,0:T(8,128)(2,1)S(1)}, bf16[3,1024,256]{2,1,0:T(8,128)(2,1)}, u32[]{:S(2)}) %copy-start.1) | copy-done | bytes 1572888
  23.1 0.5 project.1
  23.6 0.2 cut_columns.4.cut_ref
  23.8 3.4 %collective-permute-start.12 = (bf16[3,3,64,512]{3,2,1,0:T(8,128)(2,1)S(1)}, bf16[3,3,64,512]{3,2,1,0:T(8,128)(2,1)}, u32[]{:S(2)}, u32[]{:S(2)}) collective-permute-start(bf16[3,3,64,512]{3,2,1,0:T(8,128)(2,1)S(1)} %cut_columns.4.cut_ref), channel_id=1, source_target_pairs={{0,2},{4,6},{9,11},{13,15},{18,16},{22,20},{27,25},{31,29}} | collective-permute-start | bytes 1769480 | tf_op jit(solution)/shard_map/ppermute | solution.py:392
  27.2 0.0 collective-permute-start.9
  27.2 0.0 collective-permute-start.10
  27.3 1.2 %collective-permute-done.9.refs_1_ = f32[64,64]{1,0:T(8,128)S(1)} collective-permute-done((f32[64,64]{1,0:T(8,128)S(1)}, f32[64,64]{1,0:T(8,128)S(1)}, u32[]{:S(2)}, u32[]{:S(2)}) %collective-permute-start.9) | collective-permute-done | bytes 16416 | tf_op jit(solution)/shard_map/ppermute | solution.py:322
  28.5 0.7 collective-permute-start.11
  29.1 5.8 %collective-permute-done.10.refs_2_ = f32[64,64]{1,0:T(8,128)S(1)} collective-permute-done((f32[64,64]{1,0:T(8,128)S(1)}, f32[64,64]{1,0:T(8,128)S(1)}, u32[]{:S(2)}, u32[]{:S(2)}) %collective-permute-start.10) | collective-permute-done | bytes 16416 | tf_op jit(solution)/shard_map/ppermute | solution.py:322
  34.9 0.4 collective-permute-done.11.refs_3_
  35.2 0.0 collective-permute-done.6.refs_1_.refs_4_
  35.2 0.0 copy-done.3
  35.2 0.0 collective-permute-done.5.refs_0_.refs_3_
  35.2 0.2 cut_columns.6.cut_ref
  35.4 4.8 %collective-permute-start.16 = (bf16[2,3,64,512]{3,2,1,0:T(8,128)(2,1)S(1)}, bf16[2,3,64,512]{3,2,1,0:T(8,128)(2,1)}, u32[]{:S(2)}, u32[]{:S(2)}) collective-permute-start(bf16[2,3,64,512]{3,2,1,0:T(8,128)(2,1)S(1)} %cut_columns.6.cut_ref), channel_id=1, source_target_pairs={{0,2},{4,6},{9,11},{13,15},{18,16},{22,20},{27,25},{31,29}} | collective-permute-start | bytes 1179656 | tf_op jit(solution)/shard_map/ppermute | solution.py:392
  40.2 1.5 %collective-permute-start.8 = (bf16[2,3,256,128]{3,2,1,0:T(8,128)(2,1)S(1)}, bf16[2,3,256,128]{3,2,1,0:T(8,128)(2,1)S(1)}, u32[]{:S(2)}, u32[]{:S(2)}) collective-permute-start(bf16[2,3,256,128]{3,2,1,0:T(8,128)(2,1)S(1)} %collective-permute-done.6.refs_1_.refs_4_), channel_id=1, source_target_pairs={{8,0},{16,8},{24,16},{28,24},{20,28},{12,20},{4,12},{0,4},{9,1},{1... | collective-permute-start | bytes 1179656 | tf_op jit(solution)/shard_map/ppermute | solution.py:401
  41.8 0.5 collective-permute-start.7
  42.3 0.6 sum_shares.1
  42.9 0.0 collective-permute-done.12.across_ref
  42.9 1.1 %pass_on.2.refs_9_ = bf16[3,3,64,512]{3,2,1,0:T(8,128)(2,1)S(1)} custom-call(s32[1]{0:T(128)} %bitcast.role_ref, bf16[3,3,64,512]{3,2,1,0:T(8,128)(2,1)S(1)} %cut_columns.4.cut_ref, bf16[3,3,64,512]{3,2,1,0:T(8,128)(2,1)} %collective-permute-done.12.across_ref), custom_call_target="tpu_custom_call" | custom-call | tf_op jit(solution)/shard_map/pass_on/pallas_call | solution.py:382
  44.0 0.7 collective-permute-done.16.across_ref
  44.7 1.0 %pass_on.3.refs_11_ = bf16[2,3,64,512]{3,2,1,0:T(8,128)(2,1)S(1)} custom-call(s32[1]{0:T(128)} %bitcast.role_ref, bf16[2,3,64,512]{3,2,1,0:T(8,128)(2,1)S(1)} %cut_columns.6.cut_ref, bf16[2,3,64,512]{3,2,1,0:T(8,128)(2,1)} %collective-permute-done.16.across_ref), custom_call_target="tpu_custom_call" | custom-call | tf_op jit(solution)/shard_map/pass_on/pallas_call | solution.py:382
  45.8 1.3 %collective-permute-start.17 = (bf16[2,3,64,512]{3,2,1,0:T(8,128)(2,1)S(1)}, bf16[2,3,64,512]{3,2,1,0:T(8,128)(2,1)S(1)}, u32[]{:S(2)}, u32[]{:S(2)}) collective-permute-start(bf16[2,3,64,512]{3,2,1,0:T(8,128)(2,1)S(1)} %pass_on.3.refs_11_), channel_id=1, source_target_pairs={{0,1},{4,5},{9,8},{13,12},{18,19},{22,23},{27,26},{31,30},{2,3},{6... | collective-permute-start | bytes 1179656 | tf_op jit(solution)/shard_map/ppermute | solution.py:394
  47.1 0.9 %collective-permute-done.8.down_ref.refs_6_ = bf16[2,3,256,128]{3,2,1,0:T(8,128)(2,1)S(1)} collective-permute-done((bf16[2,3,256,128]{3,2,1,0:T(8,128)(2,1)S(1)}, bf16[2,3,256,128]{3,2,1,0:T(8,128)(2,1)S(1)}, u32[]{:S(2)}, u32[]{:S(2)}) %collective-permute-start.8) | collective-permute-done | bytes 393248 | tf_op jit(solution)/shard_map/ppermute | solution.py:401
  48.0 1.5 %collective-permute-done.7.up_ref.refs_5_ = bf16[2,3,256,128]{3,2,1,0:T(8,128)(2,1)S(1)} collective-permute-done((bf16[2,3,256,128]{3,2,1,0:T(8,128)(2,1)S(1)}, bf16[2,3,256,128]{3,2,1,0:T(8,128)(2,1)S(1)}, u32[]{:S(2)}, u32[]{:S(2)}) %collective-permute-start.7) | collective-permute-done | bytes 393248 | tf_op jit(solution)/shard_map/ppermute | solution.py:401
  49.5 0.2 cut_columns.5
  49.7 1.4 %collective-permute-start.13 = (bf16[3,256,128]{2,1,0:T(8,128)(2,1)S(1)}, bf16[3,256,128]{2,1,0:T(8,128)(2,1)S(1)}, u32[]{:S(2)}, u32[]{:S(2)}) collective-permute-start(bf16[3,256,128]{2,1,0:T(8,128)(2,1)S(1)} %get-tuple-element.28), channel_id=1, source_target_pairs={{0,8},{8,16},{16,24},{24,28},{28,20},{20,12},{12,4},{4,0},{1,9},{9... | collective-permute-start | bytes 589832 | tf_op jit(solution)/shard_map/ppermute | solution.py:401
  51.2 1.3 %collective-permute-start.14 = (bf16[3,256,128]{2,1,0:T(8,128)(2,1)S(1)}, bf16[3,256,128]{2,1,0:T(8,128)(2,1)S(1)}, u32[]{:S(2)}, u32[]{:S(2)}) collective-permute-start(bf16[3,256,128]{2,1,0:T(8,128)(2,1)S(1)} %get-tuple-element.29), channel_id=1, source_target_pairs={{8,0},{16,8},{24,16},{28,24},{20,28},{12,20},{4,12},{0,4},{9,1},{1... | collective-permute-start | bytes 589832 | tf_op jit(solution)/shard_map/ppermute | solution.py:401
  52.4 3.6 %collective-permute-done.13.up_half.refs_7_ = bf16[3,256,128]{2,1,0:T(8,128)(2,1)S(1)} collective-permute-done((bf16[3,256,128]{2,1,0:T(8,128)(2,1)S(1)}, bf16[3,256,128]{2,1,0:T(8,128)(2,1)S(1)}, u32[]{:S(2)}, u32[]{:S(2)}) %collective-permute-start.13) | collective-permute-done | bytes 196640 | tf_op jit(solution)/shard_map/ppermute | solution.py:401
  56.0 1.4 %collective-permute-done.14.down_half.refs_8_ = bf16[3,256,128]{2,1,0:T(8,128)(2,1)S(1)} collective-permute-done((bf16[3,256,128]{2,1,0:T(8,128)(2,1)S(1)}, bf16[3,256,128]{2,1,0:T(8,128)(2,1)S(1)}, u32[]{:S(2)}, u32[]{:S(2)}) %collective-permute-start.14) | collective-permute-done | bytes 196640 | tf_op jit(solution)/shard_map/ppermute | solution.py:401
  57.4 0.1 cut_columns.7.refs_17_
  57.6 2.3 %collective-permute-start.22 = (bf16[1,3,64,512]{3,2,1,0:T(8,128)(2,1)S(1)}, bf16[1,3,64,512]{3,2,1,0:T(8,128)(2,1)S(1)}, u32[]{:S(2)}, u32[]{:S(2)}) collective-permute-start(bf16[1,3,64,512]{3,2,1,0:T(8,128)(2,1)S(1)} %cut_columns.7.refs_17_), channel_id=1, source_target_pairs={{0,2},{4,6},{9,11},{13,15},{18,16},{22,20},{27,25},{31,29}} | collective-permute-start | bytes 589832 | tf_op jit(solution)/shard_map/ppermute | solution.py:421
  59.9 1.3 %collective-permute-start.15 = (bf16[3,3,64,512]{3,2,1,0:T(8,128)(2,1)S(1)}, bf16[3,3,64,512]{3,2,1,0:T(8,128)(2,1)S(1)}, u32[]{:S(2)}, u32[]{:S(2)}) collective-permute-start(bf16[3,3,64,512]{3,2,1,0:T(8,128)(2,1)S(1)} %pass_on.2.refs_9_), channel_id=1, source_target_pairs={{0,1},{4,5},{9,8},{13,12},{18,19},{22,23},{27,26},{31,30},{2,3},{6... | collective-permute-start | bytes 1769480 | tf_op jit(solution)/shard_map/ppermute | solution.py:394
  61.3 1.3 %collective-permute-start.20 = (bf16[2,3,64,512]{3,2,1,0:T(8,128)(2,1)S(1)}, bf16[2,3,64,512]{3,2,1,0:T(8,128)(2,1)S(1)}, u32[]{:S(2)}, u32[]{:S(2)}) collective-permute-start(bf16[2,3,64,512]{3,2,1,0:T(8,128)(2,1)S(1)} %get-tuple-element.31.refs_13_), channel_id=1, source_target_pairs={{0,3},{4,7},{9,10},{13,14},{18,17},{22,21},{27,24},{31,28}} | collective-permute-start | bytes 1179656 | tf_op jit(solution)/shard_map/ppermute | solution.py:420
  62.6 1.3 %collective-permute-start.19 = (bf16[2,3,64,512]{3,2,1,0:T(8,128)(2,1)S(1)}, bf16[2,3,64,512]{3,2,1,0:T(8,128)(2,1)S(1)}, u32[]{:S(2)}, u32[]{:S(2)}) collective-permute-start(bf16[2,3,64,512]{3,2,1,0:T(8,128)(2,1)S(1)} %get-tuple-element.31.refs_13_), channel_id=1, source_target_pairs={{0,2},{4,6},{9,11},{13,15},{18,16},{22,20},{27,25},{31,29}} | collective-permute-start | bytes 1179656 | tf_op jit(solution)/shard_map/ppermute | solution.py:420
  63.9 0.0 collective-permute-done.17.refs_12_
  63.9 0.0 copy-start.6
  63.9 1.3 %collective-permute-start.18 = (bf16[2,3,64,512]{3,2,1,0:T(8,128)(2,1)S(1)}, bf16[2,3,64,512]{3,2,1,0:T(8,128)(2,1)S(1)}, u32[]{:S(2)}, u32[]{:S(2)}) collective-permute-start(bf16[2,3,64,512]{3,2,1,0:T(8,128)(2,1)S(1)} %get-tuple-element.31.refs_13_), channel_id=1, source_target_pairs={{0,1},{4,5},{9,8},{13,12},{18,19},{22,23},{27,26},{31,30}} | collective-permute-start | bytes 1179656 | tf_op jit(solution)/shard_map/ppermute | solution.py:420
  65.2 0.0 collective-permute-done.22.refs_19_
  65.3 1.3 %collective-permute-start.21 = (bf16[1,3,64,512]{3,2,1,0:T(8,128)(2,1)S(1)}, bf16[1,3,64,512]{3,2,1,0:T(8,128)(2,1)S(1)}, u32[]{:S(2)}, u32[]{:S(2)}) collective-permute-start(bf16[1,3,64,512]{3,2,1,0:T(8,128)(2,1)S(1)} %cut_columns.7.refs_17_), channel_id=1, source_target_pairs={{0,1},{4,5},{9,8},{13,12},{18,19},{22,23},{27,26},{31,30}} | collective-permute-start | bytes 589832 | tf_op jit(solution)/shard_map/ppermute | solution.py:422
  66.6 1.0 %collective-permute-done.21.refs_18_ = bf16[1,3,64,512]{3,2,1,0:T(8,128)(2,1)S(1)} collective-permute-done((bf16[1,3,64,512]{3,2,1,0:T(8,128)(2,1)S(1)}, bf16[1,3,64,512]{3,2,1,0:T(8,128)(2,1)S(1)}, u32[]{:S(2)}, u32[]{:S(2)}) %collective-permute-start.21) | collective-permute-done | bytes 196640 | tf_op jit(solution)/shard_map/ppermute | solution.py:422
  67.6 0.7 collective-permute-start.23
  68.3 0.0 collective-permute-done.20.refs_16_
  68.3 3.8 %collective-permute-done.19.refs_15_ = bf16[2,3,64,512]{3,2,1,0:T(8,128)(2,1)S(1)} collective-permute-done((bf16[2,3,64,512]{3,2,1,0:T(8,128)(2,1)S(1)}, bf16[2,3,64,512]{3,2,1,0:T(8,128)(2,1)S(1)}, u32[]{:S(2)}, u32[]{:S(2)}) %collective-permute-start.19) | collective-permute-done | bytes 393248 | tf_op jit(solution)/shard_map/ppermute | solution.py:420
  72.0 0.0 collective-permute-done.18.refs_14_
  72.0 0.0 collective-permute-done.15.refs_10_
  72.1 0.0 collective-permute-done.23.refs_20_
  72.1 0.8 copy-done.5
  72.9 1.0 %copy-done.4 = bf16[2,3,256,128]{3,2,1,0:T(8,128)(2,1)S(1)} copy-done((bf16[2,3,256,128]{3,2,1,0:T(8,128)(2,1)S(1)}, bf16[2,3,256,128]{3,2,1,0:T(8,128)(2,1)}, u32[]{:S(2)}) %copy-start.4) | copy-done | bytes 393240
  73.9 8.6 %covariance_tile.1 = f32[3,3,1024,512]{3,2,1,0:T(8,128)} custom-call(s32[1]{0:T(128)} %bitcast.role_ref, bf16[2,3,256,128]{3,2,1,0:T(8,128)(2,1)S(1)} %get-tuple-element.20.refs_0_, bf16[2,3,256,128]{3,2,1,0:T(8,128)(2,1)S(1)} %copy-done.4, bf16[2,3,256,128]{3,2,1,0:T(8,128)(2,1)S(1)} %collective-permute-done.4.refs_2_, ...), custom_call_target="tpu_custom_call" | custom-call | flops 4831838208 | bytes 25165824 | tf_op jit(solution)/shard_map/covariance_tile/pallas_call | solution.py:434
  (9 shorter events, 0.0 us)
Async XLA Ops:
  2.3 3.8 %collective-permute-start.2 = (f32[24,64]{1,0:T(8,128)S(1)}, f32[24,64]{1,0:T(8,128)S(1)}, u32[]{:S(2)}, u32[]{:S(2)}) collective-permute-start(f32[24,64]{1,0:T(8,128)S(1)} %get-tuple-element.17.refs_0_), channel_id=1, source_target_pairs={{0,3},{1,2},{2,1},{3,0},{4,7},{5,6},{6,5},{7,4},{8,11},{9,10},{10,... | collective-permute-start | bytes 18440 | tf_op jit(solution)/shard_map/ppermute | solution.py:322
  4.7 3.7 %collective-permute-start.1 = (f32[24,64]{1,0:T(8,128)S(1)}, f32[24,64]{1,0:T(8,128)S(1)}, u32[]{:S(2)}, u32[]{:S(2)}) collective-permute-start(f32[24,64]{1,0:T(8,128)S(1)} %get-tuple-element.17.refs_0_), channel_id=1, source_target_pairs={{0,2},{1,3},{2,0},{3,1},{4,6},{5,7},{6,4},{7,5},{8,10},{9,11},{10,... | collective-permute-start | bytes 18440 | tf_op jit(solution)/shard_map/ppermute | solution.py:322
  5.4 3.1 %collective-permute-start = (f32[24,64]{1,0:T(8,128)S(1)}, f32[24,64]{1,0:T(8,128)S(1)}, u32[]{:S(2)}, u32[]{:S(2)}) collective-permute-start(f32[24,64]{1,0:T(8,128)S(1)} %get-tuple-element.17.refs_0_), channel_id=1, source_target_pairs={{0,1},{1,0},{2,3},{3,2},{4,5},{5,4},{6,7},{7,6},{8,9},{9,8},{10,11... | collective-permute-start | bytes 18440 | tf_op jit(solution)/shard_map/ppermute | solution.py:322
  9.0 10.6 %collective-permute-start.4 = (bf16[2,3,256,128]{3,2,1,0:T(8,128)(2,1)S(1)}, bf16[2,3,256,128]{3,2,1,0:T(8,128)(2,1)S(1)}, u32[]{:S(2)}, u32[]{:S(2)}) collective-permute-start(bf16[2,3,256,128]{3,2,1,0:T(8,128)(2,1)S(1)} %get-tuple-element.20.refs_0_), channel_id=1, source_target_pairs={{8,0},{16,8},{24,16},{28,24},{20,28},{12,20},{4,12},{0,4},{9,1},{1... | collective-permute-start | bytes 1179656 | tf_op jit(solution)/shard_map/ppermute | solution.py:401
  10.6 10.5 %collective-permute-start.3 = (bf16[2,3,256,128]{3,2,1,0:T(8,128)(2,1)S(1)}, bf16[2,3,256,128]{3,2,1,0:T(8,128)(2,1)S(1)}, u32[]{:S(2)}, u32[]{:S(2)}) collective-permute-start(bf16[2,3,256,128]{3,2,1,0:T(8,128)(2,1)S(1)} %get-tuple-element.20.refs_0_), channel_id=1, source_target_pairs={{0,8},{8,16},{16,24},{24,28},{28,20},{20,12},{12,4},{4,0},{1,9},{9... | collective-permute-start | bytes 1179656 | tf_op jit(solution)/shard_map/ppermute | solution.py:401
  19.6 15.6 %collective-permute-start.6 = (bf16[2,3,256,128]{3,2,1,0:T(8,128)(2,1)S(1)}, bf16[2,3,256,128]{3,2,1,0:T(8,128)(2,1)S(1)}, u32[]{:S(2)}, u32[]{:S(2)}) collective-permute-start(bf16[2,3,256,128]{3,2,1,0:T(8,128)(2,1)S(1)} %collective-permute-done.4.refs_2_), channel_id=1, source_target_pairs={{8,0},{16,8},{24,16},{28,24},{20,28},{12,20},{4,12},{0,4},{9,1},{1... | collective-permute-start | bytes 1179656 | tf_op jit(solution)/shard_map/ppermute | solution.py:401
  21.2 14.1 %copy-start.3 = (bf16[2,3,256,128]{3,2,1,0:T(8,128)(2,1)}, bf16[2,3,256,128]{3,2,1,0:T(8,128)(2,1)S(1)}, u32[]{:S(2)}) copy-start(bf16[2,3,256,128]{3,2,1,0:T(8,128)(2,1)S(1)} %collective-permute-done.3.refs_1_) | copy-start | bytes 1179652
  21.2 14.1 %collective-permute-start.5 = (bf16[2,3,256,128]{3,2,1,0:T(8,128)(2,1)S(1)}, bf16[2,3,256,128]{3,2,1,0:T(8,128)(2,1)S(1)}, u32[]{:S(2)}, u32[]{:S(2)}) collective-permute-start(bf16[2,3,256,128]{3,2,1,0:T(8,128)(2,1)S(1)} %collective-permute-done.3.refs_1_), channel_id=1, source_target_pairs={{0,8},{8,16},{16,24},{24,28},{28,20},{20,12},{12,4},{4,0},{1,9},{9... | collective-permute-start | bytes 1179656 | tf_op jit(solution)/shard_map/ppermute | solution.py:401
  21.7 1.4 %copy-start.1 = (bf16[3,1024,256]{2,1,0:T(8,128)(2,1)S(1)}, bf16[3,1024,256]{2,1,0:T(8,128)(2,1)}, u32[]{:S(2)}) copy-start(bf16[3,1024,256]{2,1,0:T(8,128)(2,1)} %eig_ref.1) | copy-start | bytes 4718596
  23.8 19.1 %collective-permute-start.12 = (bf16[3,3,64,512]{3,2,1,0:T(8,128)(2,1)S(1)}, bf16[3,3,64,512]{3,2,1,0:T(8,128)(2,1)}, u32[]{:S(2)}, u32[]{:S(2)}) collective-permute-start(bf16[3,3,64,512]{3,2,1,0:T(8,128)(2,1)S(1)} %cut_columns.4.cut_ref), channel_id=1, source_target_pairs={{0,2},{4,6},{9,11},{13,15},{18,16},{22,20},{27,25},{31,29}} | collective-permute-start | bytes 1769480 | tf_op jit(solution)/shard_map/ppermute | solution.py:392
  27.2 1.2 %collective-permute-start.9 = (f32[64,64]{1,0:T(8,128)S(1)}, f32[64,64]{1,0:T(8,128)S(1)}, u32[]{:S(2)}, u32[]{:S(2)}) collective-permute-start(f32[64,64]{1,0:T(8,128)S(1)} %get-tuple-element.23), channel_id=1, source_target_pairs={{0,1},{1,0},{2,3},{3,2},{4,5},{5,4},{6,7},{7,6},{8,9},{9,8},{10,11... | collective-permute-start | bytes 49160 | tf_op jit(solution)/shard_map/ppermute | solution.py:322
  27.2 7.6 %collective-permute-start.10 = (f32[64,64]{1,0:T(8,128)S(1)}, f32[64,64]{1,0:T(8,128)S(1)}, u32[]{:S(2)}, u32[]{:S(2)}) collective-permute-start(f32[64,64]{1,0:T(8,128)S(1)} %get-tuple-element.24), channel_id=1, source_target_pairs={{0,2},{1,3},{2,0},{3,1},{4,6},{5,7},{6,4},{7,5},{8,10},{9,11},{10,... | collective-permute-start | bytes 49160 | tf_op jit(solution)/shard_map/ppermute | solution.py:322
  28.5 6.8 %collective-permute-start.11 = (f32[64,64]{1,0:T(8,128)S(1)}, f32[64,64]{1,0:T(8,128)S(1)}, u32[]{:S(2)}, u32[]{:S(2)}) collective-permute-start(f32[64,64]{1,0:T(8,128)S(1)} %get-tuple-element.25), channel_id=1, source_target_pairs={{0,3},{1,2},{2,1},{3,0},{4,7},{5,6},{6,5},{7,4},{8,11},{9,10},{10,... | collective-permute-start | bytes 49160 | tf_op jit(solution)/shard_map/ppermute | solution.py:322
  35.4 9.3 %collective-permute-start.16 = (bf16[2,3,64,512]{3,2,1,0:T(8,128)(2,1)S(1)}, bf16[2,3,64,512]{3,2,1,0:T(8,128)(2,1)}, u32[]{:S(2)}, u32[]{:S(2)}) collective-permute-start(bf16[2,3,64,512]{3,2,1,0:T(8,128)(2,1)S(1)} %cut_columns.6.cut_ref), channel_id=1, source_target_pairs={{0,2},{4,6},{9,11},{13,15},{18,16},{22,20},{27,25},{31,29}} | collective-permute-start | bytes 1179656 | tf_op jit(solution)/shard_map/ppermute | solution.py:392
  40.2 7.8 %collective-permute-start.8 = (bf16[2,3,256,128]{3,2,1,0:T(8,128)(2,1)S(1)}, bf16[2,3,256,128]{3,2,1,0:T(8,128)(2,1)S(1)}, u32[]{:S(2)}, u32[]{:S(2)}) collective-permute-start(bf16[2,3,256,128]{3,2,1,0:T(8,128)(2,1)S(1)} %collective-permute-done.6.refs_1_.refs_4_), channel_id=1, source_target_pairs={{8,0},{16,8},{24,16},{28,24},{20,28},{12,20},{4,12},{0,4},{9,1},{1... | collective-permute-start | bytes 1179656 | tf_op jit(solution)/shard_map/ppermute | solution.py:401
  41.8 7.8 %collective-permute-start.7 = (bf16[2,3,256,128]{3,2,1,0:T(8,128)(2,1)S(1)}, bf16[2,3,256,128]{3,2,1,0:T(8,128)(2,1)S(1)}, u32[]{:S(2)}, u32[]{:S(2)}) collective-permute-start(bf16[2,3,256,128]{3,2,1,0:T(8,128)(2,1)S(1)} %collective-permute-done.5.refs_0_.refs_3_), channel_id=1, source_target_pairs={{0,8},{8,16},{16,24},{24,28},{28,20},{20,12},{12,4},{4,0},{1,9},{9... | collective-permute-start | bytes 1179656 | tf_op jit(solution)/shard_map/ppermute | solution.py:401
  44.0 28.1 %copy-start = (bf16[3,3,64,512]{3,2,1,0:T(8,128)(2,1)}, bf16[3,3,64,512]{3,2,1,0:T(8,128)(2,1)S(1)}, u32[]{:S(2)}) copy-start(bf16[3,3,64,512]{3,2,1,0:T(8,128)(2,1)S(1)} %pass_on.2.refs_9_) | copy-start | bytes 1769476
  45.8 26.3 %copy-start.2 = (bf16[2,3,64,512]{3,2,1,0:T(8,128)(2,1)}, bf16[2,3,64,512]{3,2,1,0:T(8,128)(2,1)S(1)}, u32[]{:S(2)}) copy-start(bf16[2,3,64,512]{3,2,1,0:T(8,128)(2,1)S(1)} %pass_on.3.refs_11_) | copy-start | bytes 1179652
  45.8 18.1 %collective-permute-start.17 = (bf16[2,3,64,512]{3,2,1,0:T(8,128)(2,1)S(1)}, bf16[2,3,64,512]{3,2,1,0:T(8,128)(2,1)S(1)}, u32[]{:S(2)}, u32[]{:S(2)}) collective-permute-start(bf16[2,3,64,512]{3,2,1,0:T(8,128)(2,1)S(1)} %pass_on.3.refs_11_), channel_id=1, source_target_pairs={{0,1},{4,5},{9,8},{13,12},{18,19},{22,23},{27,26},{31,30},{2,3},{6... | collective-permute-start | bytes 1179656 | tf_op jit(solution)/shard_map/ppermute | solution.py:394
  49.7 6.3 %collective-permute-start.13 = (bf16[3,256,128]{2,1,0:T(8,128)(2,1)S(1)}, bf16[3,256,128]{2,1,0:T(8,128)(2,1)S(1)}, u32[]{:S(2)}, u32[]{:S(2)}) collective-permute-start(bf16[3,256,128]{2,1,0:T(8,128)(2,1)S(1)} %get-tuple-element.28), channel_id=1, source_target_pairs={{0,8},{8,16},{16,24},{24,28},{28,20},{20,12},{12,4},{4,0},{1,9},{9... | collective-permute-start | bytes 589832 | tf_op jit(solution)/shard_map/ppermute | solution.py:401
  51.2 6.3 %collective-permute-start.14 = (bf16[3,256,128]{2,1,0:T(8,128)(2,1)S(1)}, bf16[3,256,128]{2,1,0:T(8,128)(2,1)S(1)}, u32[]{:S(2)}, u32[]{:S(2)}) collective-permute-start(bf16[3,256,128]{2,1,0:T(8,128)(2,1)S(1)} %get-tuple-element.29), channel_id=1, source_target_pairs={{8,0},{16,8},{24,16},{28,24},{20,28},{12,20},{4,12},{0,4},{9,1},{1... | collective-permute-start | bytes 589832 | tf_op jit(solution)/shard_map/ppermute | solution.py:401
  57.6 7.7 %collective-permute-start.22 = (bf16[1,3,64,512]{3,2,1,0:T(8,128)(2,1)S(1)}, bf16[1,3,64,512]{3,2,1,0:T(8,128)(2,1)S(1)}, u32[]{:S(2)}, u32[]{:S(2)}) collective-permute-start(bf16[1,3,64,512]{3,2,1,0:T(8,128)(2,1)S(1)} %cut_columns.7.refs_17_), channel_id=1, source_target_pairs={{0,2},{4,6},{9,11},{13,15},{18,16},{22,20},{27,25},{31,29}} | collective-permute-start | bytes 589832 | tf_op jit(solution)/shard_map/ppermute | solution.py:421
  59.9 12.1 %collective-permute-start.15 = (bf16[3,3,64,512]{3,2,1,0:T(8,128)(2,1)S(1)}, bf16[3,3,64,512]{3,2,1,0:T(8,128)(2,1)S(1)}, u32[]{:S(2)}, u32[]{:S(2)}) collective-permute-start(bf16[3,3,64,512]{3,2,1,0:T(8,128)(2,1)S(1)} %pass_on.2.refs_9_), channel_id=1, source_target_pairs={{0,1},{4,5},{9,8},{13,12},{18,19},{22,23},{27,26},{31,30},{2,3},{6... | collective-permute-start | bytes 1769480 | tf_op jit(solution)/shard_map/ppermute | solution.py:394
  61.3 7.0 %collective-permute-start.20 = (bf16[2,3,64,512]{3,2,1,0:T(8,128)(2,1)S(1)}, bf16[2,3,64,512]{3,2,1,0:T(8,128)(2,1)S(1)}, u32[]{:S(2)}, u32[]{:S(2)}) collective-permute-start(bf16[2,3,64,512]{3,2,1,0:T(8,128)(2,1)S(1)} %get-tuple-element.31.refs_13_), channel_id=1, source_target_pairs={{0,3},{4,7},{9,10},{13,14},{18,17},{22,21},{27,24},{31,28}} | collective-permute-start | bytes 1179656 | tf_op jit(solution)/shard_map/ppermute | solution.py:420
  62.6 9.5 %collective-permute-start.19 = (bf16[2,3,64,512]{3,2,1,0:T(8,128)(2,1)S(1)}, bf16[2,3,64,512]{3,2,1,0:T(8,128)(2,1)S(1)}, u32[]{:S(2)}, u32[]{:S(2)}) collective-permute-start(bf16[2,3,64,512]{3,2,1,0:T(8,128)(2,1)S(1)} %get-tuple-element.31.refs_13_), channel_id=1, source_target_pairs={{0,2},{4,6},{9,11},{13,15},{18,16},{22,20},{27,25},{31,29}} | collective-permute-start | bytes 1179656 | tf_op jit(solution)/shard_map/ppermute | solution.py:420
  63.9 8.2 %copy-start.6 = (bf16[2,3,64,512]{3,2,1,0:T(8,128)(2,1)}, bf16[2,3,64,512]{3,2,1,0:T(8,128)(2,1)S(1)}, u32[]{:S(2)}) copy-start(bf16[2,3,64,512]{3,2,1,0:T(8,128)(2,1)S(1)} %collective-permute-done.17.refs_12_) | copy-start | bytes 1179652
  63.9 8.1 %collective-permute-start.18 = (bf16[2,3,64,512]{3,2,1,0:T(8,128)(2,1)S(1)}, bf16[2,3,64,512]{3,2,1,0:T(8,128)(2,1)S(1)}, u32[]{:S(2)}, u32[]{:S(2)}) collective-permute-start(bf16[2,3,64,512]{3,2,1,0:T(8,128)(2,1)S(1)} %get-tuple-element.31.refs_13_), channel_id=1, source_target_pairs={{0,1},{4,5},{9,8},{13,12},{18,19},{22,23},{27,26},{31,30}} | collective-permute-start | bytes 1179656 | tf_op jit(solution)/shard_map/ppermute | solution.py:420
  65.3 2.4 %collective-permute-start.21 = (bf16[1,3,64,512]{3,2,1,0:T(8,128)(2,1)S(1)}, bf16[1,3,64,512]{3,2,1,0:T(8,128)(2,1)S(1)}, u32[]{:S(2)}, u32[]{:S(2)}) collective-permute-start(bf16[1,3,64,512]{3,2,1,0:T(8,128)(2,1)S(1)} %cut_columns.7.refs_17_), channel_id=1, source_target_pairs={{0,1},{4,5},{9,8},{13,12},{18,19},{22,23},{27,26},{31,30}} | collective-permute-start | bytes 589832 | tf_op jit(solution)/shard_map/ppermute | solution.py:422
  67.6 4.5 %collective-permute-start.23 = (bf16[1,3,64,512]{3,2,1,0:T(8,128)(2,1)S(1)}, bf16[1,3,64,512]{3,2,1,0:T(8,128)(2,1)S(1)}, u32[]{:S(2)}, u32[]{:S(2)}) collective-permute-start(bf16[1,3,64,512]{3,2,1,0:T(8,128)(2,1)S(1)} %collective-permute-done.22.refs_19_), channel_id=1, source_target_pairs={{2,3},{6,7},{11,10},{15,14},{16,17},{20,21},{25,24},{29,28}} | collective-permute-start | bytes 589832 | tf_op jit(solution)/shard_map/ppermute | solution.py:423
  72.1 0.9 %copy-start.5 = (bf16[3,3,64,512]{3,2,1,0:T(8,128)(2,1)}, bf16[3,3,64,512]{3,2,1,0:T(8,128)(2,1)S(1)}, u32[]{:S(2)}) copy-start(bf16[3,3,64,512]{3,2,1,0:T(8,128)(2,1)S(1)} %collective-permute-done.15.refs_10_) | copy-start | bytes 1769476
  72.9 1.0 %copy-start.4 = (bf16[2,3,256,128]{3,2,1,0:T(8,128)(2,1)S(1)}, bf16[2,3,256,128]{3,2,1,0:T(8,128)(2,1)}, u32[]{:S(2)}) copy-start(bf16[2,3,256,128]{3,2,1,0:T(8,128)(2,1)} %copy-done.3) | copy-start | bytes 1179652

commit v8 on v7

--- a/solution.py
+++ b/solution.py
@@ -159,14 +159,16 @@
     cut_columns(half_ref, [(up_half, down_half)], cols_ref)
 
 
-def pass_on_kernel(role_ref, cut_ref, across_ref, out_ref):
-    @pl.when(role_ref[0] == 0)
-    def _():
-        out_ref[...] = cut_ref[...]
-
-    @pl.when(role_ref[0] != 0)
-    def _():
-        out_ref[...] = across_ref[...]
+def pass_on_kernel(role_ref, *refs):
+    sources, out_ref = refs[:-1], refs[-1]
+    for role in range(2):
+
+        @pl.when((role_ref[0] != 0) == bool(role))
+        def _(role=role):
+            to = 0
+            for source in sources[role::2]:
+                out_ref[to : to + source.shape[0]] = source[...]
+                to += source.shape[0]
 
 
 def side_by_side(first, second):
@@ -388,9 +390,12 @@
             name=name,
         )(scalar, *[pinned(value, pltpu.VMEM) for value in values])
 
-    def spread_paired(cut):
-        across = lax.ppermute(cut, axes, pairs(0, 2))
-        held = kernel(pass_on_kernel, columns(cut.shape[0]), role, [cut, across], "pass_on")
+    def cross(cut):
+        return [cut, lax.ppermute(cut, axes, pairs(0, 2))]
+
+    def pass_on(values, role):
+        slots = sum(value.shape[0] for value in values[::2])
+        held = kernel(pass_on_kernel, columns(slots), role, values, "pass_on")
         return [held, lax.ppermute(held, axes, pairs(0, 1) + pairs(2, 3))]
 
     order = ring_order(frame_axis)
@@ -401,11 +406,13 @@
         return lax.ppermute(up, "frames", forward), lax.ppermute(down, "frames", backward)
 
     one = hop(own, own)
-    cut_one = kernel(cut_kernel, columns(3), after(half, *shares), [own, *one], "cut_columns")
-    in_hbm = spread_paired(cut_one)
-    two = hop(*one)
-    cut_two = kernel(cut_kernel, columns(2), after(half, *parts), list(two), "cut_columns")
+    crossed = cross(kernel(cut_kernel, columns(1), half, [own], "cut_columns"))
+    cut_one = kernel(cut_kernel, columns(2), half, list(one), "cut_columns")
+    two = hop(after(one[0], crossed[1], *parts), one[1])
+    in_hbm = pass_on(crossed + cross(cut_one), role)
+    cut_two = kernel(cut_kernel, columns(2), half, list(two), "cut_columns")
     three = hop(*two)
+    crossed = cross(cut_two)
     half_shard = pltpu.VMEM(piece, jnp.bfloat16)
     cut_three, *halves = kernel(
         cut_last_kernel,
@@ -415,21 +422,13 @@
         "cut_columns",
     )
     far = hop(*halves)
-    cut_four = kernel(cut_far_kernel, columns(1), half, list(far), "cut_columns")
-
-    direct = [cut_three] + [lax.ppermute(cut_three, axes, pairs(0, d)) for d in (1, 2, 3)]
-    across = lax.ppermute(cut_four, axes, pairs(0, 2))
-    beside = lax.ppermute(cut_four, axes, pairs(0, 1))
-    last = lax.ppermute(across, axes, pairs(2, 3))
-
-    groups = (
-        (3, True, (0, 1, 0, 1)),
-        (2, True, (0, 1, 0, 1)),
-        (2, False, (0, 1, 2, 3)),
-        (1, False, (0, 1, 2, 3)),
-    )
-    in_hbm += spread_paired(cut_two)
-    in_vmem = direct + [cut_four, beside, across, last]
+    cut_four = kernel(
+        cut_far_kernel, columns(1), after(half, crossed[1]), list(far), "cut_columns"
+    )
+    in_vmem = pass_on(
+        crossed + cross(cut_three) + cross(cut_four), after(role, in_hbm[1])
+    )
+    groups = ((3, True, (0, 1, 0, 1)), (5, False, (0, 1, 0, 1)))
     rows = [own, *one, *two, *three, *far]
     covariance = pl.pallas_call(
         functools.partial(

time: 83.3 us -> 70.7 us (0.85)
  waiting for transfers between devices: 31.8 us -> 19.1 us
  local copies, waits for them, and re-layouts: 3.24 us -> 6.26 us
  starting transfers between devices: 31.8 us -> 29.8 us
  Pallas kernels: 14.8 us -> 13.7 us
    ppermute x4, waiting for transfers between devices: 10.8 us -> 6.53 us  [hop(): lax.ppermute(down, 'frames', backward)]
    ppermute x6, waiting for transfers between devices: 10.3 us -> 6.21 us  [swap(): lax.ppermute(value, 'atoms', [(a, a ^ distance) for a in range(atom_axis)])]
    ppermute x4, waiting for transfers between devices: 5.11 us -> 1.13 us  [hop(): lax.ppermute(up, 'frames', forward)]
    unnamed x14 -> x22, local copies, waits for them, and re-layouts: 3.24 us -> 6.26 us
    ppermute x10 -> x7, starting transfers between devices: 19.1 us -> 17.6 us  [the longest x5 14.9 us: cross(): return [cut, lax.ppermute(cut, axes, pairs(0, 2))]]
    ppermute x4, starting transfers between devices: 5.9 us -> 4.73 us  [hop(): lax.ppermute(down, 'frames', backward)]
    pallas_call x6 -> x7, Pallas kernels: 2.9 us -> 1.95 us  [kernel(): pl.pallas_call(body, out_shape=out_shape, in_specs=[SMEM] + [VMEM] * len(...]
    ppermute x10 -> x7, waiting for transfers between devices: 5.56 us -> 5.26 us  [the longest x5 3.15 us: cross(): return [cut, lax.ppermute(cut, axes, pairs(0, 2))]]
  transfers between devices with their start and end apart: 24 -> 21, of which waited for: 13 -> 11; matrix products, arithmetic and copies ran while one was open for 0% -> 0% of each run, Pallas kernels for 5% -> 4%
where the time goes in v8:
time: 70.7 us; the launch traced here: 69.7 us
  starting transfers between devices  29.8 us (42%)
  waiting for transfers between devices  19.1 us (27%)
  Pallas kernels  13.7 us (19%)
  local copies, waits for them, and re-layouts  6.26 us (9%)
  between operations  0.86 us (1%)
    ppermute x5, starting transfers between devices, cross(): return [cut, lax.ppermute(cut, axes, pairs(0, 2))]  14.9 us
    pallas_call x1, Pallas kernels, per_device(): pl.pallas_call(functools.partial(covariance_kernel, frame_axis, atom_axis...  8.42 us
    ppermute x4, waiting for transfers between devices, hop(): lax.ppermute(down, 'frames', backward)  6.53 us
    unnamed x22, local copies, waits for them, and re-layouts  6.26 us
    ppermute x6, waiting for transfers between devices, swap(): lax.ppermute(value, 'atoms', [(a, a ^ distance) for a in range(atom_axis)])  6.21 us
    ppermute x4, starting transfers between devices, hop(): lax.ppermute(down, 'frames', backward)  4.73 us
    ppermute x6, starting transfers between devices, swap(): lax.ppermute(value, 'atoms', [(a, a ^ distance) for a in range(atom_axis)])  3.93 us
    ppermute x4, starting transfers between devices, hop(): lax.ppermute(up, 'frames', forward)  3.53 us
  transfers between devices with their start and end apart: 21, of which 11 were waited for; matrix products, arithmetic and copies ran while one was open for 0% of the time, Pallas kernels for 4%

profile of v8, /device:TPU:0, one launch (start us, length us, event | category | flops | bytes accessed | tf_op | source)
XLA Modules:
  0.0 69.7 jit_solution(9561860334291500740)
XLA Ops:
  0.6 1.7 %local_moments.1 = (f32[24,64]{1,0:T(8,128)S(1)}, f32[3,64,1024]{2,1,0:T(8,128)S(1)}, f32[3,1024]{1,0:T(4,128)S(1)}) custom-call(f32[3,64,1024]{2,1,0:T(8,128)} %bitcast.6, f32[3,1024]{1,0:T(4,128)} %ref_hbm.1), custom_call_target="tpu_custom_call" | custom-call | tf_op jit(solution)/shard_map/local_moments/pallas_call | solution.py:310
  2.3 2.4 %collective-permute-start.2 = (f32[24,64]{1,0:T(8,128)S(1)}, f32[24,64]{1,0:T(8,128)S(1)}, u32[]{:S(2)}, u32[]{:S(2)}) collective-permute-start(f32[24,64]{1,0:T(8,128)S(1)} %get-tuple-element.18.refs_0_), channel_id=1, source_target_pairs={{0,3},{1,2},{2,1},{3,0},{4,7},{5,6},{6,5},{7,4},{8,11},{9,10},{10,... | collective-permute-start | bytes 18440 | tf_op jit(solution)/shard_map/ppermute | solution.py:324
  4.7 0.6 collective-permute-start.1
  5.4 0.0 collective-permute-start
  5.4 0.7 %collective-permute-done.2.refs_3_ = f32[24,64]{1,0:T(8,128)S(1)} collective-permute-done((f32[24,64]{1,0:T(8,128)S(1)}, f32[24,64]{1,0:T(8,128)S(1)}, u32[]{:S(2)}, u32[]{:S(2)}) %collective-permute-start.2) | collective-permute-done | bytes 6176 | tf_op jit(solution)/shard_map/ppermute | solution.py:324
  6.1 2.3 %collective-permute-done.1.refs_2_ = f32[24,64]{1,0:T(8,128)S(1)} collective-permute-done((f32[24,64]{1,0:T(8,128)S(1)}, f32[24,64]{1,0:T(8,128)S(1)}, u32[]{:S(2)}, u32[]{:S(2)}) %collective-permute-start.1) | collective-permute-done | bytes 6176 | tf_op jit(solution)/shard_map/ppermute | solution.py:324
  8.4 0.0 collective-permute-done.refs_1_
  8.4 0.6 polar_align.1
  9.0 1.6 %collective-permute-start.3 = (bf16[2,3,256,128]{3,2,1,0:T(8,128)(2,1)S(1)}, bf16[2,3,256,128]{3,2,1,0:T(8,128)(2,1)S(1)}, u32[]{:S(2)}, u32[]{:S(2)}) collective-permute-start(bf16[2,3,256,128]{3,2,1,0:T(8,128)(2,1)S(1)} %get-tuple-element.21.refs_0_), channel_id=1, source_target_pairs={{0,8},{8,16},{16,24},{24,28},{28,20},{20,12},{12,4},{4,0},{1,9},{9... | collective-permute-start | bytes 1179656 | tf_op jit(solution)/shard_map/ppermute | solution.py:406
  10.7 0.4 collective-permute-start.4
  11.1 0.1 cut_columns.5.refs_0_
  11.3 2.6 %collective-permute-start.5 = (bf16[1,3,64,512]{3,2,1,0:T(8,128)(2,1)S(1)}, bf16[1,3,64,512]{3,2,1,0:T(8,128)(2,1)S(1)}, u32[]{:S(2)}, u32[]{:S(2)}) collective-permute-start(bf16[1,3,64,512]{3,2,1,0:T(8,128)(2,1)S(1)} %cut_columns.5.refs_0_), channel_id=1, source_target_pairs={{0,2},{4,6},{9,11},{13,15},{18,16},{22,20},{27,25},{31,29}} | collective-permute-start | bytes 589832 | tf_op jit(solution)/shard_map/ppermute | solution.py:394
  13.8 0.0 copy-start.1
  13.8 1.4 %copy-done.1 = bf16[3,1024,256]{2,1,0:T(8,128)(2,1)S(1)} copy-done((bf16[3,1024,256]{2,1,0:T(8,128)(2,1)S(1)}, bf16[3,1024,256]{2,1,0:T(8,128)(2,1)}, u32[]{:S(2)}) %copy-start.1) | copy-done | bytes 1572888
  15.2 0.5 project.1
  15.7 0.0 copy-start.2
  15.7 0.1 collective-permute-start.6
  15.8 0.1 collective-permute-start.7
  15.9 1.1 %collective-permute-done.6.refs_1_ = f32[64,64]{1,0:T(8,128)S(1)} collective-permute-done((f32[64,64]{1,0:T(8,128)S(1)}, f32[64,64]{1,0:T(8,128)S(1)}, u32[]{:S(2)}, u32[]{:S(2)}) %collective-permute-start.6) | collective-permute-done | bytes 16416 | tf_op jit(solution)/shard_map/ppermute | solution.py:324
  17.0 0.6 copy-done.4
  17.6 0.7 collective-permute-start.8
  18.3 1.5 %collective-permute-done.7.refs_2_ = f32[64,64]{1,0:T(8,128)S(1)} collective-permute-done((f32[64,64]{1,0:T(8,128)S(1)}, f32[64,64]{1,0:T(8,128)S(1)}, u32[]{:S(2)}, u32[]{:S(2)}) %collective-permute-start.7) | collective-permute-done | bytes 16416 | tf_op jit(solution)/shard_map/ppermute | solution.py:324
  19.8 0.6 copy-done.6
  20.4 0.6 collective-permute-done.8.refs_3_
  21.0 0.6 copy-done.8
  21.6 0.0 collective-permute-done.5.refs_1_
  21.6 0.0 collective-permute-done.3.refs_0_.refs_1_
  21.6 0.0 collective-permute-done.4.refs_1_.refs_2_
  21.6 1.6 %collective-permute-start.10 = (bf16[2,3,256,128]{3,2,1,0:T(8,128)(2,1)S(1)}, bf16[2,3,256,128]{3,2,1,0:T(8,128)(2,1)S(1)}, u32[]{:S(2)}, u32[]{:S(2)}) collective-permute-start(bf16[2,3,256,128]{3,2,1,0:T(8,128)(2,1)S(1)} %collective-permute-done.4.refs_1_.refs_2_), channel_id=1, source_target_pairs={{8,0},{16,8},{24,16},{28,24},{20,28},{12,20},{4,12},{0,4},{9,1},{1... | collective-permute-start | bytes 1179656 | tf_op jit(solution)/shard_map/ppermute | solution.py:406
  23.2 0.5 collective-permute-start.9
  23.7 0.2 cut_columns.6.refs_2_
  23.9 3.6 %collective-permute-start.13 = (bf16[2,3,64,512]{3,2,1,0:T(8,128)(2,1)S(1)}, bf16[2,3,64,512]{3,2,1,0:T(8,128)(2,1)}, u32[]{:S(2)}, u32[]{:S(2)}) collective-permute-start(bf16[2,3,64,512]{3,2,1,0:T(8,128)(2,1)S(1)} %cut_columns.6.refs_2_), channel_id=1, source_target_pairs={{0,2},{4,6},{9,11},{13,15},{18,16},{22,20},{27,25},{31,29}} | collective-permute-start | bytes 1179656 | tf_op jit(solution)/shard_map/ppermute | solution.py:394
  27.4 5.4 %collective-permute-done.10.refs_1_.refs_4_ = bf16[2,3,256,128]{3,2,1,0:T(8,128)(2,1)S(1)} collective-permute-done((bf16[2,3,256,128]{3,2,1,0:T(8,128)(2,1)S(1)}, bf16[2,3,256,128]{3,2,1,0:T(8,128)(2,1)S(1)}, u32[]{:S(2)}, u32[]{:S(2)}) %collective-permute-start.10) | collective-permute-done | bytes 393248 | tf_op jit(solution)/shard_map/ppermute | solution.py:406
  32.8 1.5 %collective-permute-start.12 = (bf16[2,3,256,128]{3,2,1,0:T(8,128)(2,1)S(1)}, bf16[2,3,256,128]{3,2,1,0:T(8,128)(2,1)S(1)}, u32[]{:S(2)}, u32[]{:S(2)}) collective-permute-start(bf16[2,3,256,128]{3,2,1,0:T(8,128)(2,1)S(1)} %collective-permute-done.10.refs_1_.refs_4_), channel_id=1, source_target_pairs={{8,0},{16,8},{24,16},{28,24},{20,28},{12,20},{4,12},{0,4},{9,1},{1... | collective-permute-start | bytes 1179656 | tf_op jit(solution)/shard_map/ppermute | solution.py:406
  34.3 0.0 collective-permute-done.9.refs_0_.refs_3_
  34.4 0.5 collective-permute-start.11
  34.9 0.2 cut_columns.8.refs_0_
  35.1 2.8 %collective-permute-start.17 = (bf16[2,3,64,512]{3,2,1,0:T(8,128)(2,1)S(1)}, bf16[2,3,64,512]{3,2,1,0:T(8,128)(2,1)S(1)}, u32[]{:S(2)}, u32[]{:S(2)}) collective-permute-start(bf16[2,3,64,512]{3,2,1,0:T(8,128)(2,1)S(1)} %cut_columns.8.refs_0_), channel_id=1, source_target_pairs={{0,2},{4,6},{9,11},{13,15},{18,16},{22,20},{27,25},{31,29}} | collective-permute-start | bytes 1179656 | tf_op jit(solution)/shard_map/ppermute | solution.py:394
  37.9 0.0 collective-permute-done.13.refs_3_
  37.9 1.0 %pass_on.2.refs_9_ = bf16[3,3,64,512]{3,2,1,0:T(8,128)(2,1)S(1)} custom-call(s32[1]{0:T(128)} %bitcast.role_ref, bf16[1,3,64,512]{3,2,1,0:T(8,128)(2,1)S(1)} %cut_columns.5.refs_0_, bf16[1,3,64,512]{3,2,1,0:T(8,128)(2,1)S(1)} %collective-permute-done.5.refs_1_, bf16[2,3,64,512]{3,2,1,0:T(8,128)(2,1)S(1)} %cut_columns.6.refs_2_, ...), custom_call_target="tpu_custom_call" | custom-call | tf_op jit(solution)/shard_map/pass_on/pallas_call | solution.py:384
  39.0 1.3 %collective-permute-start.16 = (bf16[3,3,64,512]{3,2,1,0:T(8,128)(2,1)S(1)}, bf16[3,3,64,512]{3,2,1,0:T(8,128)(2,1)S(1)}, u32[]{:S(2)}, u32[]{:S(2)}) collective-permute-start(bf16[3,3,64,512]{3,2,1,0:T(8,128)(2,1)S(1)} %pass_on.2.refs_9_), channel_id=1, source_target_pairs={{0,1},{4,5},{9,8},{13,12},{18,19},{22,23},{27,26},{31,30},{2,3},{6... | collective-permute-start | bytes 1769480 | tf_op jit(solution)/shard_map/ppermute | solution.py:399
  40.3 0.0 copy-start.3
  40.3 0.7 %copy-done.3 = f32[64,64]{1,0:T(8,128)S(1)} copy-done((f32[64,64]{1,0:T(8,128)S(1)}, f32[64,64]{1,0:T(8,128)}, u32[]{:S(2)}) %copy-start.3) | copy-done | bytes 16408
  41.1 0.8 %copy-done.5 = f32[64,64]{1,0:T(8,128)S(1)} copy-done((f32[64,64]{1,0:T(8,128)S(1)}, f32[64,64]{1,0:T(8,128)}, u32[]{:S(2)}) %copy-start.5) | copy-done | bytes 16408
  41.8 0.8 %copy-done.7 = f32[64,64]{1,0:T(8,128)S(1)} copy-done((f32[64,64]{1,0:T(8,128)S(1)}, f32[64,64]{1,0:T(8,128)}, u32[]{:S(2)}) %copy-start.7) | copy-done | bytes 16408
  42.6 0.8 %copy-done.9 = f32[64,64]{1,0:T(8,128)S(1)} copy-done((f32[64,64]{1,0:T(8,128)S(1)}, f32[64,64]{1,0:T(8,128)}, u32[]{:S(2)}) %copy-start.9) | copy-done | bytes 16408
  43.3 0.6 sum_shares.1
  44.0 0.0 collective-permute-done.12.down_ref.refs_6_
  44.0 0.5 collective-permute-done.11.up_ref.refs_5_
  44.4 0.2 cut_columns.7
  44.6 0.9 %collective-permute-start.14 = (bf16[3,256,128]{2,1,0:T(8,128)(2,1)S(1)}, bf16[3,256,128]{2,1,0:T(8,128)(2,1)S(1)}, u32[]{:S(2)}, u32[]{:S(2)}) collective-permute-start(bf16[3,256,128]{2,1,0:T(8,128)(2,1)S(1)} %get-tuple-element.29), channel_id=1, source_target_pairs={{0,8},{8,16},{16,24},{24,28},{28,20},{20,12},{12,4},{4,0},{1,9},{9... | collective-permute-start | bytes 589832 | tf_op jit(solution)/shard_map/ppermute | solution.py:406
  45.5 1.2 %collective-permute-start.15 = (bf16[3,256,128]{2,1,0:T(8,128)(2,1)S(1)}, bf16[3,256,128]{2,1,0:T(8,128)(2,1)S(1)}, u32[]{:S(2)}, u32[]{:S(2)}) collective-permute-start(bf16[3,256,128]{2,1,0:T(8,128)(2,1)S(1)} %get-tuple-element.30), channel_id=1, source_target_pairs={{8,0},{16,8},{24,16},{28,24},{20,28},{12,20},{4,12},{0,4},{9,1},{1... | collective-permute-start | bytes 589832 | tf_op jit(solution)/shard_map/ppermute | solution.py:406
  46.7 3.0 %collective-permute-start.18 = (bf16[2,3,64,512]{3,2,1,0:T(8,128)(2,1)S(1)}, bf16[2,3,64,512]{3,2,1,0:T(8,128)(2,1)S(1)}, u32[]{:S(2)}, u32[]{:S(2)}) collective-permute-start(bf16[2,3,64,512]{3,2,1,0:T(8,128)(2,1)S(1)} %get-tuple-element.32.refs_2_), channel_id=1, source_target_pairs={{0,2},{4,6},{9,11},{13,15},{18,16},{22,20},{27,25},{31,29}} | collective-permute-start | bytes 1179656 | tf_op jit(solution)/shard_map/ppermute | solution.py:394
  49.7 0.0 collective-permute-done.17.refs_1_
  49.7 0.7 collective-permute-done.14.up_half.refs_7_
  50.4 1.1 %collective-permute-done.15.down_half.refs_8_ = bf16[3,256,128]{2,1,0:T(8,128)(2,1)S(1)} collective-permute-done((bf16[3,256,128]{2,1,0:T(8,128)(2,1)S(1)}, bf16[3,256,128]{2,1,0:T(8,128)(2,1)S(1)}, u32[]{:S(2)}, u32[]{:S(2)}) %collective-permute-start.15) | collective-permute-done | bytes 196640 | tf_op jit(solution)/shard_map/ppermute | solution.py:406
  51.5 0.1 cut_columns.9.refs_4_
  51.6 3.0 %collective-permute-start.19 = (bf16[1,3,64,512]{3,2,1,0:T(8,128)(2,1)S(1)}, bf16[1,3,64,512]{3,2,1,0:T(8,128)(2,1)S(1)}, u32[]{:S(2)}, u32[]{:S(2)}) collective-permute-start(bf16[1,3,64,512]{3,2,1,0:T(8,128)(2,1)S(1)} %cut_columns.9.refs_4_), channel_id=1, source_target_pairs={{0,2},{4,6},{9,11},{13,15},{18,16},{22,20},{27,25},{31,29}} | collective-permute-start | bytes 589832 | tf_op jit(solution)/shard_map/ppermute | solution.py:394
  54.6 0.0 collective-permute-done.16.refs_10_
  54.6 3.1 %collective-permute-done.19.refs_5_ = bf16[1,3,64,512]{3,2,1,0:T(8,128)(2,1)S(1)} collective-permute-done((bf16[1,3,64,512]{3,2,1,0:T(8,128)(2,1)S(1)}, bf16[1,3,64,512]{3,2,1,0:T(8,128)(2,1)S(1)}, u32[]{:S(2)}, u32[]{:S(2)}) %collective-permute-start.19) | collective-permute-done | bytes 196640 | tf_op jit(solution)/shard_map/ppermute | solution.py:394
  57.8 0.1 pass_on.3.refs_11_
  57.8 1.4 %collective-permute-start.20 = (bf16[5,3,64,512]{3,2,1,0:T(8,128)(2,1)S(1)}, bf16[5,3,64,512]{3,2,1,0:T(8,128)(2,1)S(1)}, u32[]{:S(2)}, u32[]{:S(2)}) collective-permute-start(bf16[5,3,64,512]{3,2,1,0:T(8,128)(2,1)S(1)} %pass_on.3.refs_11_), channel_id=1, source_target_pairs={{0,1},{4,5},{9,8},{13,12},{18,19},{22,23},{27,26},{31,30},{2,3},{6... | collective-permute-start | bytes 2949128 | tf_op jit(solution)/shard_map/ppermute | solution.py:399
  59.2 2.1 %collective-permute-done.20.refs_12_ = bf16[5,3,64,512]{3,2,1,0:T(8,128)(2,1)S(1)} collective-permute-done((bf16[5,3,64,512]{3,2,1,0:T(8,128)(2,1)S(1)}, bf16[5,3,64,512]{3,2,1,0:T(8,128)(2,1)S(1)}, u32[]{:S(2)}, u32[]{:S(2)}) %collective-permute-start.20) | collective-permute-done | bytes 983072 | tf_op jit(solution)/shard_map/ppermute | solution.py:399
  61.3 8.4 %covariance_tile.1 = f32[3,3,1024,512]{3,2,1,0:T(8,128)} custom-call(s32[1]{0:T(128)} %bitcast.role_ref, bf16[2,3,256,128]{3,2,1,0:T(8,128)(2,1)S(1)} %get-tuple-element.21.refs_0_, bf16[2,3,256,128]{3,2,1,0:T(8,128)(2,1)S(1)} %collective-permute-done.3.refs_0_.refs_1_, bf16[2,3,256,128]{3,2,1,0:T(8,128)(2,1)S(1)} %collective-permute-done.4.refs_1_.refs_2_, ...), custom_call_target="tpu_custom_call" | custom-call | flops 4831838208 | bytes 25165824 | tf_op jit(solution)/shard_map/covariance_tile/pallas_call | solution.py:433
  (12 shorter events, 0.0 us)
Async XLA Ops:
  2.3 3.8 %collective-permute-start.2 = (f32[24,64]{1,0:T(8,128)S(1)}, f32[24,64]{1,0:T(8,128)S(1)}, u32[]{:S(2)}, u32[]{:S(2)}) collective-permute-start(f32[24,64]{1,0:T(8,128)S(1)} %get-tuple-element.18.refs_0_), channel_id=1, source_target_pairs={{0,3},{1,2},{2,1},{3,0},{4,7},{5,6},{6,5},{7,4},{8,11},{9,10},{10,... | collective-permute-start | bytes 18440 | tf_op jit(solution)/shard_map/ppermute | solution.py:324
  4.7 3.7 %collective-permute-start.1 = (f32[24,64]{1,0:T(8,128)S(1)}, f32[24,64]{1,0:T(8,128)S(1)}, u32[]{:S(2)}, u32[]{:S(2)}) collective-permute-start(f32[24,64]{1,0:T(8,128)S(1)} %get-tuple-element.18.refs_0_), channel_id=1, source_target_pairs={{0,2},{1,3},{2,0},{3,1},{4,6},{5,7},{6,4},{7,5},{8,10},{9,11},{10,... | collective-permute-start | bytes 18440 | tf_op jit(solution)/shard_map/ppermute | solution.py:324
  5.4 3.1 %collective-permute-start = (f32[24,64]{1,0:T(8,128)S(1)}, f32[24,64]{1,0:T(8,128)S(1)}, u32[]{:S(2)}, u32[]{:S(2)}) collective-permute-start(f32[24,64]{1,0:T(8,128)S(1)} %get-tuple-element.18.refs_0_), channel_id=1, source_target_pairs={{0,1},{1,0},{2,3},{3,2},{4,5},{5,4},{6,7},{7,6},{8,9},{9,8},{10,11... | collective-permute-start | bytes 18440 | tf_op jit(solution)/shard_map/ppermute | solution.py:324
  9.0 12.5 %collective-permute-start.3 = (bf16[2,3,256,128]{3,2,1,0:T(8,128)(2,1)S(1)}, bf16[2,3,256,128]{3,2,1,0:T(8,128)(2,1)S(1)}, u32[]{:S(2)}, u32[]{:S(2)}) collective-permute-start(bf16[2,3,256,128]{3,2,1,0:T(8,128)(2,1)S(1)} %get-tuple-element.21.refs_0_), channel_id=1, source_target_pairs={{0,8},{8,16},{16,24},{24,28},{28,20},{20,12},{12,4},{4,0},{1,9},{9... | collective-permute-start | bytes 1179656 | tf_op jit(solution)/shard_map/ppermute | solution.py:406
  10.7 10.9 %collective-permute-start.4 = (bf16[2,3,256,128]{3,2,1,0:T(8,128)(2,1)S(1)}, bf16[2,3,256,128]{3,2,1,0:T(8,128)(2,1)S(1)}, u32[]{:S(2)}, u32[]{:S(2)}) collective-permute-start(bf16[2,3,256,128]{3,2,1,0:T(8,128)(2,1)S(1)} %get-tuple-element.21.refs_0_), channel_id=1, source_target_pairs={{8,0},{16,8},{24,16},{28,24},{20,28},{12,20},{4,12},{0,4},{9,1},{1... | collective-permute-start | bytes 1179656 | tf_op jit(solution)/shard_map/ppermute | solution.py:406
  11.3 10.3 %collective-permute-start.5 = (bf16[1,3,64,512]{3,2,1,0:T(8,128)(2,1)S(1)}, bf16[1,3,64,512]{3,2,1,0:T(8,128)(2,1)S(1)}, u32[]{:S(2)}, u32[]{:S(2)}) collective-permute-start(bf16[1,3,64,512]{3,2,1,0:T(8,128)(2,1)S(1)} %cut_columns.5.refs_0_), channel_id=1, source_target_pairs={{0,2},{4,6},{9,11},{13,15},{18,16},{22,20},{27,25},{31,29}} | collective-permute-start | bytes 589832 | tf_op jit(solution)/shard_map/ppermute | solution.py:394
  13.8 1.4 %copy-start.1 = (bf16[3,1024,256]{2,1,0:T(8,128)(2,1)S(1)}, bf16[3,1024,256]{2,1,0:T(8,128)(2,1)}, u32[]{:S(2)}) copy-start(bf16[3,1024,256]{2,1,0:T(8,128)(2,1)} %eig_ref.1) | copy-start | bytes 4718596
  15.7 18.6 %copy-start.2 = (f32[64,64]{1,0:T(8,128)}, f32[64,64]{1,0:T(8,128)S(1)}, u32[]{:S(2)}) copy-start(f32[64,64]{1,0:T(8,128)S(1)} %get-tuple-element.23.refs_0_) | copy-start | bytes 49156
  15.7 1.3 %collective-permute-start.6 = (f32[64,64]{1,0:T(8,128)S(1)}, f32[64,64]{1,0:T(8,128)S(1)}, u32[]{:S(2)}, u32[]{:S(2)}) collective-permute-start(f32[64,64]{1,0:T(8,128)S(1)} %get-tuple-element.24), channel_id=1, source_target_pairs={{0,1},{1,0},{2,3},{3,2},{4,5},{5,4},{6,7},{7,6},{8,9},{9,8},{10,11... | collective-permute-start | bytes 49160 | tf_op jit(solution)/shard_map/ppermute | solution.py:324
  15.8 4.0 %collective-permute-start.7 = (f32[64,64]{1,0:T(8,128)S(1)}, f32[64,64]{1,0:T(8,128)S(1)}, u32[]{:S(2)}, u32[]{:S(2)}) collective-permute-start(f32[64,64]{1,0:T(8,128)S(1)} %get-tuple-element.25), channel_id=1, source_target_pairs={{0,2},{1,3},{2,0},{3,1},{4,6},{5,7},{6,4},{7,5},{8,10},{9,11},{10,... | collective-permute-start | bytes 49160 | tf_op jit(solution)/shard_map/ppermute | solution.py:324
  17.0 0.6 copy-start.4
  17.6 3.3 %collective-permute-start.8 = (f32[64,64]{1,0:T(8,128)S(1)}, f32[64,64]{1,0:T(8,128)S(1)}, u32[]{:S(2)}, u32[]{:S(2)}) collective-permute-start(f32[64,64]{1,0:T(8,128)S(1)} %get-tuple-element.26), channel_id=1, source_target_pairs={{0,3},{1,2},{2,1},{3,0},{4,7},{5,6},{6,5},{7,4},{8,11},{9,10},{10,... | collective-permute-start | bytes 49160 | tf_op jit(solution)/shard_map/ppermute | solution.py:324
  19.8 0.6 copy-start.6
  21.0 0.6 copy-start.8
  21.6 11.2 %collective-permute-start.10 = (bf16[2,3,256,128]{3,2,1,0:T(8,128)(2,1)S(1)}, bf16[2,3,256,128]{3,2,1,0:T(8,128)(2,1)S(1)}, u32[]{:S(2)}, u32[]{:S(2)}) collective-permute-start(bf16[2,3,256,128]{3,2,1,0:T(8,128)(2,1)S(1)} %collective-permute-done.4.refs_1_.refs_2_), channel_id=1, source_target_pairs={{8,0},{16,8},{24,16},{28,24},{20,28},{12,20},{4,12},{0,4},{9,1},{1... | collective-permute-start | bytes 1179656 | tf_op jit(solution)/shard_map/ppermute | solution.py:406
  23.2 11.2 %collective-permute-start.9 = (bf16[2,3,256,128]{3,2,1,0:T(8,128)(2,1)S(1)}, bf16[2,3,256,128]{3,2,1,0:T(8,128)(2,1)S(1)}, u32[]{:S(2)}, u32[]{:S(2)}) collective-permute-start(bf16[2,3,256,128]{3,2,1,0:T(8,128)(2,1)S(1)} %collective-permute-done.3.refs_0_.refs_1_), channel_id=1, source_target_pairs={{0,8},{8,16},{16,24},{24,28},{28,20},{20,12},{12,4},{4,0},{1,9},{9... | collective-permute-start | bytes 1179656 | tf_op jit(solution)/shard_map/ppermute | solution.py:406
  23.9 14.0 %collective-permute-start.13 = (bf16[2,3,64,512]{3,2,1,0:T(8,128)(2,1)S(1)}, bf16[2,3,64,512]{3,2,1,0:T(8,128)(2,1)}, u32[]{:S(2)}, u32[]{:S(2)}) collective-permute-start(bf16[2,3,64,512]{3,2,1,0:T(8,128)(2,1)S(1)} %cut_columns.6.refs_2_), channel_id=1, source_target_pairs={{0,2},{4,6},{9,11},{13,15},{18,16},{22,20},{27,25},{31,29}} | collective-permute-start | bytes 1179656 | tf_op jit(solution)/shard_map/ppermute | solution.py:394
  32.8 11.1 %collective-permute-start.12 = (bf16[2,3,256,128]{3,2,1,0:T(8,128)(2,1)S(1)}, bf16[2,3,256,128]{3,2,1,0:T(8,128)(2,1)S(1)}, u32[]{:S(2)}, u32[]{:S(2)}) collective-permute-start(bf16[2,3,256,128]{3,2,1,0:T(8,128)(2,1)S(1)} %collective-permute-done.10.refs_1_.refs_4_), channel_id=1, source_target_pairs={{8,0},{16,8},{24,16},{28,24},{20,28},{12,20},{4,12},{0,4},{9,1},{1... | collective-permute-start | bytes 1179656 | tf_op jit(solution)/shard_map/ppermute | solution.py:406
  34.4 10.1 %collective-permute-start.11 = (bf16[2,3,256,128]{3,2,1,0:T(8,128)(2,1)S(1)}, bf16[2,3,256,128]{3,2,1,0:T(8,128)(2,1)S(1)}, u32[]{:S(2)}, u32[]{:S(2)}) collective-permute-start(bf16[2,3,256,128]{3,2,1,0:T(8,128)(2,1)S(1)} %collective-permute-done.9.refs_0_.refs_3_), channel_id=1, source_target_pairs={{0,8},{8,16},{16,24},{24,28},{28,20},{20,12},{12,4},{4,0},{1,9},{9... | collective-permute-start | bytes 1179656 | tf_op jit(solution)/shard_map/ppermute | solution.py:406
  35.1 14.6 %collective-permute-start.17 = (bf16[2,3,64,512]{3,2,1,0:T(8,128)(2,1)S(1)}, bf16[2,3,64,512]{3,2,1,0:T(8,128)(2,1)S(1)}, u32[]{:S(2)}, u32[]{:S(2)}) collective-permute-start(bf16[2,3,64,512]{3,2,1,0:T(8,128)(2,1)S(1)} %cut_columns.8.refs_0_), channel_id=1, source_target_pairs={{0,2},{4,6},{9,11},{13,15},{18,16},{22,20},{27,25},{31,29}} | collective-permute-start | bytes 1179656 | tf_op jit(solution)/shard_map/ppermute | solution.py:394
  39.0 22.4 %copy-start = (bf16[3,3,64,512]{3,2,1,0:T(8,128)(2,1)}, bf16[3,3,64,512]{3,2,1,0:T(8,128)(2,1)S(1)}, u32[]{:S(2)}) copy-start(bf16[3,3,64,512]{3,2,1,0:T(8,128)(2,1)S(1)} %pass_on.2.refs_9_) | copy-start | bytes 1769476
  39.0 15.6 %collective-permute-start.16 = (bf16[3,3,64,512]{3,2,1,0:T(8,128)(2,1)S(1)}, bf16[3,3,64,512]{3,2,1,0:T(8,128)(2,1)S(1)}, u32[]{:S(2)}, u32[]{:S(2)}) collective-permute-start(bf16[3,3,64,512]{3,2,1,0:T(8,128)(2,1)S(1)} %pass_on.2.refs_9_), channel_id=1, source_target_pairs={{0,1},{4,5},{9,8},{13,12},{18,19},{22,23},{27,26},{31,30},{2,3},{6... | collective-permute-start | bytes 1769480 | tf_op jit(solution)/shard_map/ppermute | solution.py:399
  40.3 0.8 %copy-start.3 = (f32[64,64]{1,0:T(8,128)S(1)}, f32[64,64]{1,0:T(8,128)}, u32[]{:S(2)}) copy-start(f32[64,64]{1,0:T(8,128)} %copy-done.2) | copy-start | bytes 49156
  41.1 0.8 %copy-start.5 = (f32[64,64]{1,0:T(8,128)S(1)}, f32[64,64]{1,0:T(8,128)}, u32[]{:S(2)}) copy-start(f32[64,64]{1,0:T(8,128)} %copy-done.4) | copy-start | bytes 49156
  41.8 0.8 %copy-start.7 = (f32[64,64]{1,0:T(8,128)S(1)}, f32[64,64]{1,0:T(8,128)}, u32[]{:S(2)}) copy-start(f32[64,64]{1,0:T(8,128)} %copy-done.6) | copy-start | bytes 49156
  42.6 0.8 %copy-start.9 = (f32[64,64]{1,0:T(8,128)S(1)}, f32[64,64]{1,0:T(8,128)}, u32[]{:S(2)}) copy-start(f32[64,64]{1,0:T(8,128)} %copy-done.8) | copy-start | bytes 49156
  44.6 5.7 %collective-permute-start.14 = (bf16[3,256,128]{2,1,0:T(8,128)(2,1)S(1)}, bf16[3,256,128]{2,1,0:T(8,128)(2,1)S(1)}, u32[]{:S(2)}, u32[]{:S(2)}) collective-permute-start(bf16[3,256,128]{2,1,0:T(8,128)(2,1)S(1)} %get-tuple-element.29), channel_id=1, source_target_pairs={{0,8},{8,16},{16,24},{24,28},{28,20},{20,12},{12,4},{4,0},{1,9},{9... | collective-permute-start | bytes 589832 | tf_op jit(solution)/shard_map/ppermute | solution.py:406
  45.5 6.0 %collective-permute-start.15 = (bf16[3,256,128]{2,1,0:T(8,128)(2,1)S(1)}, bf16[3,256,128]{2,1,0:T(8,128)(2,1)S(1)}, u32[]{:S(2)}, u32[]{:S(2)}) collective-permute-start(bf16[3,256,128]{2,1,0:T(8,128)(2,1)S(1)} %get-tuple-element.30), channel_id=1, source_target_pairs={{8,0},{16,8},{24,16},{28,24},{20,28},{12,20},{4,12},{0,4},{9,1},{1... | collective-permute-start | bytes 589832 | tf_op jit(solution)/shard_map/ppermute | solution.py:406
  46.7 11.0 %collective-permute-start.18 = (bf16[2,3,64,512]{3,2,1,0:T(8,128)(2,1)S(1)}, bf16[2,3,64,512]{3,2,1,0:T(8,128)(2,1)S(1)}, u32[]{:S(2)}, u32[]{:S(2)}) collective-permute-start(bf16[2,3,64,512]{3,2,1,0:T(8,128)(2,1)S(1)} %get-tuple-element.32.refs_2_), channel_id=1, source_target_pairs={{0,2},{4,6},{9,11},{13,15},{18,16},{22,20},{27,25},{31,29}} | collective-permute-start | bytes 1179656 | tf_op jit(solution)/shard_map/ppermute | solution.py:394
  51.6 6.1 %collective-permute-start.19 = (bf16[1,3,64,512]{3,2,1,0:T(8,128)(2,1)S(1)}, bf16[1,3,64,512]{3,2,1,0:T(8,128)(2,1)S(1)}, u32[]{:S(2)}, u32[]{:S(2)}) collective-permute-start(bf16[1,3,64,512]{3,2,1,0:T(8,128)(2,1)S(1)} %cut_columns.9.refs_4_), channel_id=1, source_target_pairs={{0,2},{4,6},{9,11},{13,15},{18,16},{22,20},{27,25},{31,29}} | collective-permute-start | bytes 589832 | tf_op jit(solution)/shard_map/ppermute | solution.py:394
  54.6 6.7 %copy-start.10 = (bf16[3,3,64,512]{3,2,1,0:T(8,128)(2,1)}, bf16[3,3,64,512]{3,2,1,0:T(8,128)(2,1)S(1)}, u32[]{:S(2)}) copy-start(bf16[3,3,64,512]{3,2,1,0:T(8,128)(2,1)S(1)} %collective-permute-done.16.refs_10_) | copy-start | bytes 1769476
  57.8 3.5 %collective-permute-start.20 = (bf16[5,3,64,512]{3,2,1,0:T(8,128)(2,1)S(1)}, bf16[5,3,64,512]{3,2,1,0:T(8,128)(2,1)S(1)}, u32[]{:S(2)}, u32[]{:S(2)}) collective-permute-start(bf16[5,3,64,512]{3,2,1,0:T(8,128)(2,1)S(1)} %pass_on.3.refs_11_), channel_id=1, source_target_pairs={{0,1},{4,5},{9,8},{13,12},{18,19},{22,23},{27,26},{31,30},{2,3},{6... | collective-permute-start | bytes 2949128 | tf_op jit(solution)/shard_map/ppermute | solution.py:399

commit v9 on v8

--- a/solution.py
+++ b/solution.py
@@ -15,6 +15,7 @@
 HBM = pl.BlockSpec(memory_space=pltpu.HBM)
 ANY = pl.BlockSpec(memory_space=pl.ANY)
 MIB = 1024 * 1024
+LONG = 40 * 10**9
 
 
 def params(mib):
@@ -64,7 +65,7 @@
 
 def align_kernel(parts, *refs):
     stats = refs[:parts]
-    x_ref, ref_ref, piece_ref, flat_ref, turn = refs[parts:]
+    x_ref, ref_ref, first_ref, second_ref, flat_ref, turn = refs[parts:]
     local = x_ref.shape[2]
     rows = x_ref.shape[1]
 
@@ -110,10 +111,10 @@
         target = ref_ref[i : i + 1, :] - turned[0:1, 12 + i : 13 + i]
         moved = sum(column[3 * j + i] * centred[j] for j in range(3)) - target
         flat_ref[i] = moved.astype(jnp.bfloat16)
-        run = piece_ref.shape[2]
-        for at in range(2):
+        run = first_ref.shape[1]
+        for at, piece in enumerate((first_ref, second_ref)):
             pair = [moved[:, (2 * at + k) * run : (2 * at + k + 1) * run] for k in range(2)]
-            piece_ref[at, i] = jnp.concatenate(pair, axis=0).T.astype(jnp.bfloat16)
+            piece[i] = jnp.concatenate(pair, axis=0).T.astype(jnp.bfloat16)
 
 
 def project_kernel(me_ref, flat_ref, eig_ref, *refs):
@@ -132,31 +133,18 @@
     refs[-1][...] = sum(ref[...] for ref in refs[:-1])
 
 
-def cut_columns(half_ref, halves, cols_ref):
+def cut_kernel(half_ref, *refs):
+    pieces, cols_ref = refs[:-1], refs[-1]
     for half in range(2):
 
         @pl.when(half_ref[0] == half)
         def _(half=half):
-            for k, pair in enumerate(halves):
-                run, lanes = pair[half].shape[1:]
+            for k, piece in enumerate(pieces[half::2]):
+                run, lanes = piece.shape[1:]
                 for c in range(3):
-                    turned = pair[half][c].astype(jnp.float32).T.astype(jnp.bfloat16)
+                    turned = piece[c].astype(jnp.float32).T.astype(jnp.bfloat16)
                     cols_ref[k, c, :, :run] = turned[: lanes // 2]
                     cols_ref[k, c, :, run:] = turned[lanes // 2 :]
-
-
-def cut_kernel(half_ref, *refs):
-    cut_columns(half_ref, [(r.at[0], r.at[1]) for r in refs[:-1]], refs[-1])
-
-
-def cut_last_kernel(half_ref, up_ref, down_ref, cols_ref, up_half, down_half):
-    up_half[...] = up_ref[0]
-    down_half[...] = down_ref[1]
-    cut_columns(half_ref, [(r.at[0], r.at[1]) for r in (up_ref, down_ref)], cols_ref)
-
-
-def cut_far_kernel(half_ref, up_half, down_half, cols_ref):
-    cut_columns(half_ref, [(up_half, down_half)], cols_ref)
 
 
 def pass_on_kernel(role_ref, *refs):
@@ -179,8 +167,7 @@
 
 
 def covariance_kernel(slots, roles, groups, scale, role_ref, *refs):
-    shards, up_half, down_half = refs[: slots - 1], refs[slots - 1], refs[slots]
-    refs = refs[slots + 1 :]
+    pieces, refs = refs[: 2 * slots], refs[2 * slots :]
     arrays = []
     for _, _, holder in groups:
         count = max(holder) + 1
@@ -188,7 +175,7 @@
         refs = refs[count:]
     out_ref, left, right, done, col_sem, out_sem = refs
     depth = right.shape[1] // slots
-    run = up_half.shape[1]
+    run = pieces[0].shape[1]
 
     def fetches(k, role, to):
         source = arrays[k][groups[k][2][role]]
@@ -226,14 +213,9 @@
             for d in range(3):
                 right[d, to + n * depth : to + (n + 1) * depth, :] = source[n, d]
 
-    def piece(slot, at, c):
-        if slot < slots - 1:
-            return shards[slot][at, c]
-        return (up_half, down_half)[at][c]
-
     def assemble(c, at):
         for q in range(slots // 2):
-            low, high = side_by_side(piece(2 * q, at, c), piece(2 * q + 1, at, c))
+            low, high = side_by_side(pieces[4 * q + at][c], pieces[4 * q + 2 + at][c])
             left[at, :run, q * LANES : (q + 1) * LANES] = low
             left[at, run:, q * LANES : (q + 1) * LANES] = high
 
@@ -325,15 +307,12 @@
 
     others = [swap(stats, d) for d in range(1, atom_axis)]
     run = local_atoms // 4
-    piece = (3, run, 2 * local_frames)
-    own, flat = pl.pallas_call(
+    piece = jax.ShapeDtypeStruct((3, run, 2 * local_frames), jnp.bfloat16)
+    *own, flat = pl.pallas_call(
         functools.partial(align_kernel, atom_axis),
-        out_shape=(
-            jax.ShapeDtypeStruct((2,) + piece, jnp.bfloat16),
-            jax.ShapeDtypeStruct(x.shape, jnp.bfloat16),
-        ),
+        out_shape=(piece, piece, jax.ShapeDtypeStruct(x.shape, jnp.bfloat16)),
         in_specs=[VMEM] * (atom_axis + 2),
-        out_specs=(VMEM, VMEM),
+        out_specs=(VMEM, VMEM, VMEM),
         scratch_shapes=[pltpu.VMEM((LANES, LANES), jnp.float32)],
         compiler_params=params(8),
         name="polar_align",
@@ -348,15 +327,15 @@
         compiler_params=params(8),
         name="project",
     )(me_a.astype(jnp.int32).reshape(1), flat, eigvecs)
-    parts = [shares[0]] + [swap(shares[d], d) for d in range(1, atom_axis)]
-    projections = pl.pallas_call(
-        sum_kernel,
-        out_shape=share,
-        in_specs=[VMEM] * atom_axis,
-        out_specs=VMEM,
-        compiler_params=params(4),
-        name="sum_shares",
-    )(*parts)
+    def sum_shares(shares):
+        return pl.pallas_call(
+            sum_kernel,
+            out_shape=share,
+            in_specs=[VMEM] * atom_axis,
+            out_specs=VMEM,
+            compiler_params=params(4),
+            name="sum_shares",
+        )(shares[0], *[swap(shares[d], d) for d in range(1, atom_axis)])
 
     def pairs(source, target):
         return [
@@ -368,6 +347,7 @@
         ]
 
     if blocks != 2 or frame_axis != 8:
+        projections = sum_shares(shares)
         spread_pairs = [pairs(0, d) for d in range(1, atom_axis)]
         covariance = long_axis_covariance(
             flat, half[0], role[0], block, spread_pairs, 1.0 / total_frames
@@ -379,7 +359,7 @@
     def columns(slots):
         return pltpu.VMEM((slots, 3, local_frames, block), jnp.bfloat16)
 
-    def kernel(body, out_shape, scalar, values, name):
+    def kernel(body, out_shape, scalar, values, name, cost=None):
         single = not isinstance(out_shape, tuple)
         return pl.pallas_call(
             body,
@@ -387,6 +367,7 @@
             in_specs=[SMEM] + [VMEM] * len(values),
             out_specs=VMEM if single else (VMEM,) * len(out_shape),
             compiler_params=params(4),
+            cost_estimate=cost,
             name=name,
         )(scalar, *[pinned(value, pltpu.VMEM) for value in values])
 
@@ -403,33 +384,34 @@
     backward = [(b, a) for a, b in forward]
 
     def hop(up, down):
-        return lax.ppermute(up, "frames", forward), lax.ppermute(down, "frames", backward)
-
+        up_a = lax.ppermute(up[0], "frames", forward)
+        down_a = lax.ppermute(down[0], "frames", backward)
+        up_b = lax.ppermute(up[1], "frames", forward)
+        down_b = lax.ppermute(down[1], "frames", backward)
+        return [up_a, up_b], [down_a, down_b]
+
+    def cut(slots, *earlier, cost=None):
+        pieces = sum(slots, [])
+        return kernel(
+            cut_kernel, columns(len(slots)), after(half, *earlier), pieces, "cut_columns", cost
+        )
+
+    long = pl.CostEstimate(flops=LONG, bytes_accessed=0, transcendentals=0)
     one = hop(own, own)
-    crossed = cross(kernel(cut_kernel, columns(1), half, [own], "cut_columns"))
-    cut_one = kernel(cut_kernel, columns(2), half, list(one), "cut_columns")
-    two = hop(after(one[0], crossed[1], *parts), one[1])
-    in_hbm = pass_on(crossed + cross(cut_one), role)
-    cut_two = kernel(cut_kernel, columns(2), half, list(two), "cut_columns")
+    two = hop(*one)
+    in_hbm = pass_on(cross(cut([own] + list(one))), role)
     three = hop(*two)
-    crossed = cross(cut_two)
-    half_shard = pltpu.VMEM(piece, jnp.bfloat16)
-    cut_three, *halves = kernel(
-        cut_last_kernel,
-        (columns(2), half_shard, half_shard),
-        after(half, projections, in_hbm[0]),
-        list(three),
-        "cut_columns",
-    )
-    far = hop(*halves)
-    cut_four = kernel(
-        cut_far_kernel, columns(1), after(half, crossed[1]), list(far), "cut_columns"
-    )
-    in_vmem = pass_on(
-        crossed + cross(cut_three) + cross(cut_four), after(role, in_hbm[1])
-    )
+    crossed = cross(cut(two, *shares))
+    far = [
+        lax.ppermute(three[0][0], "frames", forward),
+        lax.ppermute(three[1][1], "frames", backward),
+    ]
+    crossed += cross(cut(three))
+    crossed += cross(cut([far], crossed[1], cost=long))
+    projections = sum_shares([after(value, crossed[-2]) for value in shares])
+    in_vmem = pass_on(crossed, after(role, in_hbm[1]))
     groups = ((3, True, (0, 1, 0, 1)), (5, False, (0, 1, 0, 1)))
-    rows = [own, *one, *two, *three, *far]
+    rows = sum([own, *one, *two, *three, far], [])
     covariance = pl.pallas_call(
         functools.partial(
             covariance_kernel, frame_axis, atom_axis, groups, 1.0 / total_frames

time: 70.7 us -> 74.4 us (1.052)
  local copies, waits for them, and re-layouts: 6.26 us -> 1.46 us
  Pallas kernels: 13.7 us -> 17.8 us
  starting transfers between devices: 29.8 us -> 32.3 us
  waiting for transfers between devices: 19.1 us -> 21.4 us
    ppermute x8 -> x14, starting transfers between devices: 8.26 us -> 13.8 us  [the longest x3 5.06 us: hop(): down_b = lax.ppermute(down[1], 'frames', backward)]
    ppermute x5 -> x4, starting transfers between devices: 14.9 us -> 9.81 us  [cross(): return [cut, lax.ppermute(cut, axes, pairs(0, 2))]]
    unnamed x22, local copies, waits for them, and re-layouts: 6.26 us -> 1.46 us
    ppermute x8 -> x14, waiting for transfers between devices: 7.66 us -> 12 us  [the longest x3 4.4 us: hop(): up_a = lax.ppermute(up[0], 'frames', forward)]
    pallas_call x7 -> x6, Pallas kernels: 1.95 us -> 4.87 us  [kernel(): pl.pallas_call(body, out_shape=out_shape, in_specs=[SMEM] + [VMEM] * len(...]
    ppermute x2, waiting for transfers between devices: 2.12 us -> 0.01 us  [pass_on(): return [held, lax.ppermute(held, axes, pairs(0, 1) + pairs(2, 3))]]
    ppermute x6, starting transfers between devices: 3.93 us -> 5.85 us  [swap(): lax.ppermute(value, 'atoms', [(a, a ^ distance) for a in range(atom_axis)])]
    pallas_call x1, Pallas kernels: 8.42 us -> 9.54 us  [per_device(): pl.pallas_call(functools.partial(covariance_kernel, frame_axis, atom_axis...]
  transfers between devices with their start and end apart: 21 -> 26, of which waited for: 11 -> 10; matrix products, arithmetic and copies ran while one was open for 0% -> 0% of each run, Pallas kernels for 4% -> 7%
where the time goes in v9:
time: 74.4 us; the launch traced here: 73.8 us
  starting transfers between devices  32.3 us (43%)
  waiting for transfers between devices  21.4 us (29%)
  Pallas kernels  17.8 us (24%)
  local copies, waits for them, and re-layouts  1.46 us (2%)
  between operations  0.93 us (1%)
    ppermute x4, starting transfers between devices, cross(): return [cut, lax.ppermute(cut, axes, pairs(0, 2))]  9.81 us
    pallas_call x1, Pallas kernels, per_device(): pl.pallas_call(functools.partial(covariance_kernel, frame_axis, atom_axis...  9.54 us
    ppermute x6, waiting for transfers between devices, swap(): lax.ppermute(value, 'atoms', [(a, a ^ distance) for a in range(atom_axis)])  6.25 us
    ppermute x6, starting transfers between devices, swap(): lax.ppermute(value, 'atoms', [(a, a ^ distance) for a in range(atom_axis)])  5.85 us
    ppermute x3, starting transfers between devices, hop(): down_b = lax.ppermute(down[1], 'frames', backward)  5.06 us
    pallas_call x6, Pallas kernels, kernel(): pl.pallas_call(body, out_shape=out_shape, in_specs=[SMEM] + [VMEM] * len(...  4.87 us
    ppermute x3, starting transfers between devices, hop(): down_a = lax.ppermute(down[0], 'frames', backward)  4.65 us
    ppermute x3, waiting for transfers between devices, hop(): up_a = lax.ppermute(up[0], 'frames', forward)  4.4 us
  transfers between devices with their start and end apart: 26, of which 10 were waited for; matrix products, arithmetic and copies ran while one was open for 0% of the time, Pallas kernels for 7%

profile of v9, /device:TPU:0, one launch (start us, length us, event | category | flops | bytes accessed | tf_op | source)
XLA Modules:
  0.0 73.8 jit_solution(16945358393989201383)
XLA Ops:
  0.6 1.7 %local_moments.1 = (f32[24,64]{1,0:T(8,128)S(1)}, f32[3,64,1024]{2,1,0:T(8,128)S(1)}, f32[3,1024]{1,0:T(4,128)S(1)}) custom-call(f32[3,64,1024]{2,1,0:T(8,128)} %bitcast.6, f32[3,1024]{1,0:T(4,128)} %ref_hbm.1), custom_call_target="tpu_custom_call" | custom-call | tf_op jit(solution)/shard_map/local_moments/pallas_call | solution.py:292
  2.3 2.4 %collective-permute-start.2 = (f32[24,64]{1,0:T(8,128)S(1)}, f32[24,64]{1,0:T(8,128)S(1)}, u32[]{:S(2)}, u32[]{:S(2)}) collective-permute-start(f32[24,64]{1,0:T(8,128)S(1)} %get-tuple-element.19.refs_0_), channel_id=1, source_target_pairs={{0,3},{1,2},{2,1},{3,0},{4,7},{5,6},{6,5},{7,4},{8,11},{9,10},{10,... | collective-permute-start | bytes 18440 | tf_op jit(solution)/shard_map/ppermute | solution.py:306
  4.7 0.6 collective-permute-start.1
  5.4 0.0 collective-permute-start
  5.4 0.7 collective-permute-done.2.refs_3_
  6.1 2.3 %collective-permute-done.1.refs_2_ = f32[24,64]{1,0:T(8,128)S(1)} collective-permute-done((f32[24,64]{1,0:T(8,128)S(1)}, f32[24,64]{1,0:T(8,128)S(1)}, u32[]{:S(2)}, u32[]{:S(2)}) %collective-permute-start.1) | collective-permute-done | bytes 6176 | tf_op jit(solution)/shard_map/ppermute | solution.py:306
  8.4 0.6 polar_align.1
  9.0 1.6 %collective-permute-start.5 = (bf16[3,256,128]{2,1,0:T(8,128)(2,1)S(1)}, bf16[3,256,128]{2,1,0:T(8,128)(2,1)S(1)}, u32[]{:S(2)}, u32[]{:S(2)}) collective-permute-start(bf16[3,256,128]{2,1,0:T(8,128)(2,1)S(1)} %get-tuple-element.22.refs_0_), channel_id=1, source_target_pairs={{8,0},{16,8},{24,16},{28,24},{20,28},{12,20},{4,12},{0,4},{9,1},{1... | collective-permute-start | bytes 589832 | tf_op jit(solution)/shard_map/ppermute | solution.py:388
  10.6 0.5 collective-permute-start.3
  11.1 1.5 %collective-permute-start.6 = (bf16[3,256,128]{2,1,0:T(8,128)(2,1)S(1)}, bf16[3,256,128]{2,1,0:T(8,128)(2,1)S(1)}, u32[]{:S(2)}, u32[]{:S(2)}) collective-permute-start(bf16[3,256,128]{2,1,0:T(8,128)(2,1)S(1)} %get-tuple-element.23.refs_1_), channel_id=1, source_target_pairs={{8,0},{16,8},{24,16},{28,24},{20,28},{12,20},{4,12},{0,4},{9,1},{1... | collective-permute-start | bytes 589832 | tf_op jit(solution)/shard_map/ppermute | solution.py:390
  12.6 0.5 collective-permute-start.4
  13.2 3.8 %collective-permute-done.5.refs_4_ = bf16[3,256,128]{2,1,0:T(8,128)(2,1)S(1)} collective-permute-done((bf16[3,256,128]{2,1,0:T(8,128)(2,1)S(1)}, bf16[3,256,128]{2,1,0:T(8,128)(2,1)S(1)}, u32[]{:S(2)}, u32[]{:S(2)}) %collective-permute-start.5) | collective-permute-done | bytes 196640 | tf_op jit(solution)/shard_map/ppermute | solution.py:388
  16.9 1.5 %collective-permute-start.9 = (bf16[3,256,128]{2,1,0:T(8,128)(2,1)S(1)}, bf16[3,256,128]{2,1,0:T(8,128)(2,1)S(1)}, u32[]{:S(2)}, u32[]{:S(2)}) collective-permute-start(bf16[3,256,128]{2,1,0:T(8,128)(2,1)S(1)} %collective-permute-done.5.refs_4_), channel_id=1, source_target_pairs={{8,0},{16,8},{24,16},{28,24},{20,28},{12,20},{4,12},{0,4},{9,1},{1... | collective-permute-start | bytes 589832 | tf_op jit(solution)/shard_map/ppermute | solution.py:388
  18.5 0.0 collective-permute-done.3.refs_2_
  18.5 0.5 collective-permute-start.7
  19.0 2.2 %collective-permute-done.6.refs_5_ = bf16[3,256,128]{2,1,0:T(8,128)(2,1)S(1)} collective-permute-done((bf16[3,256,128]{2,1,0:T(8,128)(2,1)S(1)}, bf16[3,256,128]{2,1,0:T(8,128)(2,1)S(1)}, u32[]{:S(2)}, u32[]{:S(2)}) %collective-permute-start.6) | collective-permute-done | bytes 196640 | tf_op jit(solution)/shard_map/ppermute | solution.py:390
  21.1 1.5 %collective-permute-start.10 = (bf16[3,256,128]{2,1,0:T(8,128)(2,1)S(1)}, bf16[3,256,128]{2,1,0:T(8,128)(2,1)S(1)}, u32[]{:S(2)}, u32[]{:S(2)}) collective-permute-start(bf16[3,256,128]{2,1,0:T(8,128)(2,1)S(1)} %collective-permute-done.6.refs_5_), channel_id=1, source_target_pairs={{8,0},{16,8},{24,16},{28,24},{20,28},{12,20},{4,12},{0,4},{9,1},{1... | collective-permute-start | bytes 589832 | tf_op jit(solution)/shard_map/ppermute | solution.py:390
  22.7 0.0 collective-permute-done.4.refs_3_
  22.7 0.5 collective-permute-start.8
  23.2 0.2 cut_columns.4.refs_0_
  23.4 3.4 %collective-permute-start.17 = (bf16[3,3,64,512]{3,2,1,0:T(8,128)(2,1)S(1)}, bf16[3,3,64,512]{3,2,1,0:T(8,128)(2,1)}, u32[]{:S(2)}, u32[]{:S(2)}) collective-permute-start(bf16[3,3,64,512]{3,2,1,0:T(8,128)(2,1)S(1)} %cut_columns.4.refs_0_), channel_id=1, source_target_pairs={{0,2},{4,6},{9,11},{13,15},{18,16},{22,20},{27,25},{31,29}} | collective-permute-start | bytes 1769480 | tf_op jit(solution)/shard_map/ppermute | solution.py:375
  26.8 1.4 %copy-done.1 = bf16[3,1024,256]{2,1,0:T(8,128)(2,1)S(1)} copy-done((bf16[3,1024,256]{2,1,0:T(8,128)(2,1)S(1)}, bf16[3,1024,256]{2,1,0:T(8,128)(2,1)}, u32[]{:S(2)}) %copy-start.1) | copy-done | bytes 1572888
  28.2 0.5 project.1
  28.7 0.0 copy-start.2
  28.7 0.0 copy-start.8
  28.7 0.0 collective-permute-done.9.refs_2_.refs_8_
  28.7 1.6 %collective-permute-start.13 = (bf16[3,256,128]{2,1,0:T(8,128)(2,1)S(1)}, bf16[3,256,128]{2,1,0:T(8,128)(2,1)S(1)}, u32[]{:S(2)}, u32[]{:S(2)}) collective-permute-start(bf16[3,256,128]{2,1,0:T(8,128)(2,1)S(1)} %collective-permute-done.9.refs_2_.refs_8_), channel_id=1, source_target_pairs={{8,0},{16,8},{24,16},{28,24},{20,28},{12,20},{4,12},{0,4},{9,1},{1... | collective-permute-start | bytes 589832 | tf_op jit(solution)/shard_map/ppermute | solution.py:388
  30.3 0.0 collective-permute-done.7.refs_0_.refs_6_
  30.3 0.0 collective-permute-done.10.refs_3_.refs_9_
  30.3 0.0 collective-permute-done.8.refs_1_.refs_7_
  30.3 0.2 cut_columns.5.refs_0_
  30.5 2.5 %collective-permute-start.19 = (bf16[2,3,64,512]{3,2,1,0:T(8,128)(2,1)S(1)}, bf16[2,3,64,512]{3,2,1,0:T(8,128)(2,1)}, u32[]{:S(2)}, u32[]{:S(2)}) collective-permute-start(bf16[2,3,64,512]{3,2,1,0:T(8,128)(2,1)S(1)} %cut_columns.5.refs_0_), channel_id=1, source_target_pairs={{0,2},{4,6},{9,11},{13,15},{18,16},{22,20},{27,25},{31,29}} | collective-permute-start | bytes 1179656 | tf_op jit(solution)/shard_map/ppermute | solution.py:375
  33.1 0.0 collective-permute-start.11
  33.1 2.0 %collective-permute-start.14 = (bf16[3,256,128]{2,1,0:T(8,128)(2,1)S(1)}, bf16[3,256,128]{2,1,0:T(8,128)(2,1)S(1)}, u32[]{:S(2)}, u32[]{:S(2)}) collective-permute-start(bf16[3,256,128]{2,1,0:T(8,128)(2,1)S(1)} %collective-permute-done.10.refs_3_.refs_9_), channel_id=1, source_target_pairs={{8,0},{16,8},{24,16},{28,24},{20,28},{12,20},{4,12},{0,4},{9,1},{1... | collective-permute-start | bytes 589832 | tf_op jit(solution)/shard_map/ppermute | solution.py:390
  35.1 0.2 collective-permute-done.13.refs_2_.refs_12_
  35.3 0.0 collective-permute-start.12
  35.3 4.4 %collective-permute-done.11.refs_0_.refs_10_ = bf16[3,256,128]{2,1,0:T(8,128)(2,1)S(1)} collective-permute-done((bf16[3,256,128]{2,1,0:T(8,128)(2,1)S(1)}, bf16[3,256,128]{2,1,0:T(8,128)(2,1)S(1)}, u32[]{:S(2)}, u32[]{:S(2)}) %collective-permute-start.11) | collective-permute-done | bytes 196640 | tf_op jit(solution)/shard_map/ppermute | solution.py:387
  39.7 1.2 %collective-permute-start.15 = (bf16[3,256,128]{2,1,0:T(8,128)(2,1)S(1)}, bf16[3,256,128]{2,1,0:T(8,128)(2,1)}, u32[]{:S(2)}, u32[]{:S(2)}) collective-permute-start(bf16[3,256,128]{2,1,0:T(8,128)(2,1)S(1)} %collective-permute-done.11.refs_0_.refs_10_), channel_id=1, source_target_pairs={{0,8},{8,16},{16,24},{24,28},{28,20},{20,12},{12,4},{4,0},{1,9},{9... | collective-permute-start | bytes 589832 | tf_op jit(solution)/shard_map/ppermute | solution.py:406
  40.9 0.9 %collective-permute-start.16 = (bf16[3,256,128]{2,1,0:T(8,128)(2,1)S(1)}, bf16[3,256,128]{2,1,0:T(8,128)(2,1)}, u32[]{:S(2)}, u32[]{:S(2)}) collective-permute-start(bf16[3,256,128]{2,1,0:T(8,128)(2,1)S(1)} %collective-permute-done.14.refs_3_.refs_13_), channel_id=1, source_target_pairs={{8,0},{16,8},{24,16},{28,24},{20,28},{12,20},{4,12},{0,4},{9,1},{1... | collective-permute-start | bytes 589832 | tf_op jit(solution)/shard_map/ppermute | solution.py:407
  41.8 1.4 %collective-permute-done.12.refs_1_.refs_11_ = bf16[3,256,128]{2,1,0:T(8,128)(2,1)} collective-permute-done((bf16[3,256,128]{2,1,0:T(8,128)(2,1)S(1)}, bf16[3,256,128]{2,1,0:T(8,128)(2,1)}, u32[]{:S(2)}, u32[]{:S(2)}) %collective-permute-start.12) | collective-permute-done | bytes 196640 | tf_op jit(solution)/shard_map/ppermute | solution.py:389
  43.2 1.1 %cut_columns.6.refs_2_ = bf16[2,3,64,512]{3,2,1,0:T(8,128)(2,1)S(1)} custom-call(s32[1]{0:T(128)} %bitcast.2.half_ref, bf16[3,256,128]{2,1,0:T(8,128)(2,1)S(1)} %collective-permute-done.11.refs_0_.refs_10_, bf16[3,256,128]{2,1,0:T(8,128)(2,1)} %collective-permute-done.12.refs_1_.refs_11_, bf16[3,256,128]{2,1,0:T(8,128)(2,1)S(1)} %collective-permute-done.13.refs_2_.refs_12_, ...), custom_call_target="tpu_custom_call" | custom-call | tf_op jit(solution)/shard_map/cut_columns/pallas_call | solution.py:364
  44.3 1.9 %collective-permute-start.20 = (bf16[2,3,64,512]{3,2,1,0:T(8,128)(2,1)S(1)}, bf16[2,3,64,512]{3,2,1,0:T(8,128)(2,1)S(1)}, u32[]{:S(2)}, u32[]{:S(2)}) collective-permute-start(bf16[2,3,64,512]{3,2,1,0:T(8,128)(2,1)S(1)} %cut_columns.6.refs_2_), channel_id=1, source_target_pairs={{0,2},{4,6},{9,11},{13,15},{18,16},{22,20},{27,25},{31,29}} | collective-permute-start | bytes 1179656 | tf_op jit(solution)/shard_map/ppermute | solution.py:375
  46.3 0.0 collective-permute-done.19.refs_1_
  46.3 0.0 collective-permute-done.17.refs_1_
  46.3 1.1 %pass_on.2.refs_16_ = bf16[3,3,64,512]{3,2,1,0:T(8,128)(2,1)S(1)} custom-call(s32[1]{0:T(128)} %bitcast.role_ref, bf16[3,3,64,512]{3,2,1,0:T(8,128)(2,1)S(1)} %cut_columns.4.refs_0_, bf16[3,3,64,512]{3,2,1,0:T(8,128)(2,1)} %collective-permute-done.17.refs_1_), custom_call_target="tpu_custom_call" | custom-call | tf_op jit(solution)/shard_map/pass_on/pallas_call | solution.py:364
  47.4 0.0 copy-start.9
  47.4 0.0 copy-start.3
  47.5 1.5 %collective-permute-start.18 = (bf16[3,3,64,512]{3,2,1,0:T(8,128)(2,1)S(1)}, bf16[3,3,64,512]{3,2,1,0:T(8,128)(2,1)S(1)}, u32[]{:S(2)}, u32[]{:S(2)}) collective-permute-start(bf16[3,3,64,512]{3,2,1,0:T(8,128)(2,1)S(1)} %pass_on.2.refs_16_), channel_id=1, source_target_pairs={{0,1},{4,5},{9,8},{13,12},{18,19},{22,23},{27,26},{31,30},{2,3},{6... | collective-permute-start | bytes 1769480 | tf_op jit(solution)/shard_map/ppermute | solution.py:380
  48.9 0.0 collective-permute-done.15.refs_0_.refs_14_
  48.9 1.2 %cut_columns.7.refs_4_ = bf16[1,3,64,512]{3,2,1,0:T(8,128)(2,1)S(1)} custom-call(s32[1]{0:T(128)} %bitcast.2.half_ref, bf16[3,256,128]{2,1,0:T(8,128)(2,1)} %collective-permute-done.15.refs_0_.refs_14_, bf16[3,256,128]{2,1,0:T(8,128)(2,1)} %collective-permute-done.16.refs_1_.refs_15_), custom_call_target="tpu_custom_call" | custom-call | flops 40000000000 | tf_op jit(solution)/shard_map/cut_columns/pallas_call | solution.py:364
  50.1 2.0 %collective-permute-start.21 = (bf16[1,3,64,512]{3,2,1,0:T(8,128)(2,1)S(1)}, bf16[1,3,64,512]{3,2,1,0:T(8,128)(2,1)S(1)}, u32[]{:S(2)}, u32[]{:S(2)}) collective-permute-start(bf16[1,3,64,512]{3,2,1,0:T(8,128)(2,1)S(1)} %cut_columns.7.refs_4_), channel_id=1, source_target_pairs={{0,2},{4,6},{9,11},{13,15},{18,16},{22,20},{27,25},{31,29}} | collective-permute-start | bytes 589832 | tf_op jit(solution)/shard_map/ppermute | solution.py:375
  52.1 0.0 collective-permute-done.18.refs_17_
  52.1 3.1 %collective-permute-done.21.refs_5_ = bf16[1,3,64,512]{3,2,1,0:T(8,128)(2,1)S(1)} collective-permute-done((bf16[1,3,64,512]{3,2,1,0:T(8,128)(2,1)S(1)}, bf16[1,3,64,512]{3,2,1,0:T(8,128)(2,1)S(1)}, u32[]{:S(2)}, u32[]{:S(2)}) %collective-permute-start.21) | collective-permute-done | bytes 196640 | tf_op jit(solution)/shard_map/ppermute | solution.py:375
  55.2 0.0 collective-permute-done.20.refs_3_
  55.2 1.1 %pass_on.3.refs_18_ = bf16[5,3,64,512]{3,2,1,0:T(8,128)(2,1)S(1)} custom-call(s32[1]{0:T(128)} %bitcast.role_ref, bf16[2,3,64,512]{3,2,1,0:T(8,128)(2,1)S(1)} %cut_columns.5.refs_0_, bf16[2,3,64,512]{3,2,1,0:T(8,128)(2,1)} %collective-permute-done.19.refs_1_, bf16[2,3,64,512]{3,2,1,0:T(8,128)(2,1)S(1)} %cut_columns.6.refs_2_, ...), custom_call_target="tpu_custom_call" | custom-call | tf_op jit(solution)/shard_map/pass_on/pallas_call | solution.py:364
  56.3 1.4 %collective-permute-start.22 = (bf16[5,3,64,512]{3,2,1,0:T(8,128)(2,1)S(1)}, bf16[5,3,64,512]{3,2,1,0:T(8,128)(2,1)S(1)}, u32[]{:S(2)}, u32[]{:S(2)}) collective-permute-start(bf16[5,3,64,512]{3,2,1,0:T(8,128)(2,1)S(1)} %pass_on.3.refs_18_), channel_id=1, source_target_pairs={{0,1},{4,5},{9,8},{13,12},{18,19},{22,23},{27,26},{31,30},{2,3},{6... | collective-permute-start | bytes 2949128 | tf_op jit(solution)/shard_map/ppermute | solution.py:380
  57.7 0.1 collective-permute-start.23
  57.8 2.5 %collective-permute-start.24 = (f32[64,64]{1,0:T(8,128)S(1)}, f32[64,64]{1,0:T(8,128)S(1)}, u32[]{:S(2)}, u32[]{:S(2)}) collective-permute-start(f32[64,64]{1,0:T(8,128)S(1)} %copy-done.7), channel_id=1, source_target_pairs={{0,2},{1,3},{2,0},{3,1},{4,6},{5,7},{6,4},{7,5},{8,10},{9,11},{10,... | collective-permute-start | bytes 49160 | tf_op jit(solution)/shard_map/ppermute | solution.py:306
  60.3 0.1 collective-permute-start.25
  60.4 0.0 collective-permute-done.23.refs_1_
  60.4 1.9 %collective-permute-done.24.refs_2_ = f32[64,64]{1,0:T(8,128)S(1)} collective-permute-done((f32[64,64]{1,0:T(8,128)S(1)}, f32[64,64]{1,0:T(8,128)S(1)}, u32[]{:S(2)}, u32[]{:S(2)}) %collective-permute-start.24) | collective-permute-done | bytes 16416 | tf_op jit(solution)/shard_map/ppermute | solution.py:306
  62.3 1.4 %collective-permute-done.25.refs_3_ = f32[64,64]{1,0:T(8,128)S(1)} collective-permute-done((f32[64,64]{1,0:T(8,128)S(1)}, f32[64,64]{1,0:T(8,128)S(1)}, u32[]{:S(2)}, u32[]{:S(2)}) %collective-permute-start.25) | collective-permute-done | bytes 16416 | tf_op jit(solution)/shard_map/ppermute | solution.py:306
  63.7 0.6 sum_shares.1
  64.3 9.5 %covariance_tile.1 = f32[3,3,1024,512]{3,2,1,0:T(8,128)} custom-call(s32[1]{0:T(128)} %bitcast.role_ref, bf16[3,256,128]{2,1,0:T(8,128)(2,1)S(1)} %get-tuple-element.22.refs_0_, bf16[3,256,128]{2,1,0:T(8,128)(2,1)S(1)} %get-tuple-element.23.refs_1_, bf16[3,256,128]{2,1,0:T(8,128)(2,1)S(1)} %collective-permute-done.3.refs_2_, ...), custom_call_target="tpu_custom_call" | custom-call | flops 4831838208 | bytes 25165824 | tf_op jit(solution)/shard_map/covariance_tile/pallas_call | solution.py:415
  (21 shorter events, 0.0 us)
Async XLA Ops:
  2.3 3.8 %collective-permute-start.2 = (f32[24,64]{1,0:T(8,128)S(1)}, f32[24,64]{1,0:T(8,128)S(1)}, u32[]{:S(2)}, u32[]{:S(2)}) collective-permute-start(f32[24,64]{1,0:T(8,128)S(1)} %get-tuple-element.19.refs_0_), channel_id=1, source_target_pairs={{0,3},{1,2},{2,1},{3,0},{4,7},{5,6},{6,5},{7,4},{8,11},{9,10},{10,... | collective-permute-start | bytes 18440 | tf_op jit(solution)/shard_map/ppermute | solution.py:306
  4.7 3.7 %collective-permute-start.1 = (f32[24,64]{1,0:T(8,128)S(1)}, f32[24,64]{1,0:T(8,128)S(1)}, u32[]{:S(2)}, u32[]{:S(2)}) collective-permute-start(f32[24,64]{1,0:T(8,128)S(1)} %get-tuple-element.19.refs_0_), channel_id=1, source_target_pairs={{0,2},{1,3},{2,0},{3,1},{4,6},{5,7},{6,4},{7,5},{8,10},{9,11},{10,... | collective-permute-start | bytes 18440 | tf_op jit(solution)/shard_map/ppermute | solution.py:306
  5.4 3.1 %collective-permute-start = (f32[24,64]{1,0:T(8,128)S(1)}, f32[24,64]{1,0:T(8,128)S(1)}, u32[]{:S(2)}, u32[]{:S(2)}) collective-permute-start(f32[24,64]{1,0:T(8,128)S(1)} %get-tuple-element.19.refs_0_), channel_id=1, source_target_pairs={{0,1},{1,0},{2,3},{3,2},{4,5},{5,4},{6,7},{7,6},{8,9},{9,8},{10,11... | collective-permute-start | bytes 18440 | tf_op jit(solution)/shard_map/ppermute | solution.py:306
  9.0 7.9 %collective-permute-start.5 = (bf16[3,256,128]{2,1,0:T(8,128)(2,1)S(1)}, bf16[3,256,128]{2,1,0:T(8,128)(2,1)S(1)}, u32[]{:S(2)}, u32[]{:S(2)}) collective-permute-start(bf16[3,256,128]{2,1,0:T(8,128)(2,1)S(1)} %get-tuple-element.22.refs_0_), channel_id=1, source_target_pairs={{8,0},{16,8},{24,16},{28,24},{20,28},{12,20},{4,12},{0,4},{9,1},{1... | collective-permute-start | bytes 589832 | tf_op jit(solution)/shard_map/ppermute | solution.py:388
  10.6 7.8 %collective-permute-start.3 = (bf16[3,256,128]{2,1,0:T(8,128)(2,1)S(1)}, bf16[3,256,128]{2,1,0:T(8,128)(2,1)S(1)}, u32[]{:S(2)}, u32[]{:S(2)}) collective-permute-start(bf16[3,256,128]{2,1,0:T(8,128)(2,1)S(1)} %get-tuple-element.22.refs_0_), channel_id=1, source_target_pairs={{0,8},{8,16},{16,24},{24,28},{28,20},{20,12},{12,4},{4,0},{1,9},{9... | collective-permute-start | bytes 589832 | tf_op jit(solution)/shard_map/ppermute | solution.py:387
  11.1 10.0 %collective-permute-start.6 = (bf16[3,256,128]{2,1,0:T(8,128)(2,1)S(1)}, bf16[3,256,128]{2,1,0:T(8,128)(2,1)S(1)}, u32[]{:S(2)}, u32[]{:S(2)}) collective-permute-start(bf16[3,256,128]{2,1,0:T(8,128)(2,1)S(1)} %get-tuple-element.23.refs_1_), channel_id=1, source_target_pairs={{8,0},{16,8},{24,16},{28,24},{20,28},{12,20},{4,12},{0,4},{9,1},{1... | collective-permute-start | bytes 589832 | tf_op jit(solution)/shard_map/ppermute | solution.py:390
  12.6 10.0 %collective-permute-start.4 = (bf16[3,256,128]{2,1,0:T(8,128)(2,1)S(1)}, bf16[3,256,128]{2,1,0:T(8,128)(2,1)S(1)}, u32[]{:S(2)}, u32[]{:S(2)}) collective-permute-start(bf16[3,256,128]{2,1,0:T(8,128)(2,1)S(1)} %get-tuple-element.23.refs_1_), channel_id=1, source_target_pairs={{0,8},{8,16},{16,24},{24,28},{28,20},{20,12},{12,4},{4,0},{1,9},{9... | collective-permute-start | bytes 589832 | tf_op jit(solution)/shard_map/ppermute | solution.py:389
  16.9 11.8 %collective-permute-start.9 = (bf16[3,256,128]{2,1,0:T(8,128)(2,1)S(1)}, bf16[3,256,128]{2,1,0:T(8,128)(2,1)S(1)}, u32[]{:S(2)}, u32[]{:S(2)}) collective-permute-start(bf16[3,256,128]{2,1,0:T(8,128)(2,1)S(1)} %collective-permute-done.5.refs_4_), channel_id=1, source_target_pairs={{8,0},{16,8},{24,16},{28,24},{20,28},{12,20},{4,12},{0,4},{9,1},{1... | collective-permute-start | bytes 589832 | tf_op jit(solution)/shard_map/ppermute | solution.py:388
  18.5 11.8 %collective-permute-start.7 = (bf16[3,256,128]{2,1,0:T(8,128)(2,1)S(1)}, bf16[3,256,128]{2,1,0:T(8,128)(2,1)S(1)}, u32[]{:S(2)}, u32[]{:S(2)}) collective-permute-start(bf16[3,256,128]{2,1,0:T(8,128)(2,1)S(1)} %collective-permute-done.3.refs_2_), channel_id=1, source_target_pairs={{0,8},{8,16},{16,24},{24,28},{28,20},{20,12},{12,4},{4,0},{1,9},{9... | collective-permute-start | bytes 589832 | tf_op jit(solution)/shard_map/ppermute | solution.py:387
  21.1 9.2 %collective-permute-start.10 = (bf16[3,256,128]{2,1,0:T(8,128)(2,1)S(1)}, bf16[3,256,128]{2,1,0:T(8,128)(2,1)S(1)}, u32[]{:S(2)}, u32[]{:S(2)}) collective-permute-start(bf16[3,256,128]{2,1,0:T(8,128)(2,1)S(1)} %collective-permute-done.6.refs_5_), channel_id=1, source_target_pairs={{8,0},{16,8},{24,16},{28,24},{20,28},{12,20},{4,12},{0,4},{9,1},{1... | collective-permute-start | bytes 589832 | tf_op jit(solution)/shard_map/ppermute | solution.py:390
  22.7 7.6 %collective-permute-start.8 = (bf16[3,256,128]{2,1,0:T(8,128)(2,1)S(1)}, bf16[3,256,128]{2,1,0:T(8,128)(2,1)S(1)}, u32[]{:S(2)}, u32[]{:S(2)}) collective-permute-start(bf16[3,256,128]{2,1,0:T(8,128)(2,1)S(1)} %collective-permute-done.4.refs_3_), channel_id=1, source_target_pairs={{0,8},{8,16},{16,24},{24,28},{28,20},{20,12},{12,4},{4,0},{1,9},{9... | collective-permute-start | bytes 589832 | tf_op jit(solution)/shard_map/ppermute | solution.py:389
  23.4 22.8 %collective-permute-start.17 = (bf16[3,3,64,512]{3,2,1,0:T(8,128)(2,1)S(1)}, bf16[3,3,64,512]{3,2,1,0:T(8,128)(2,1)}, u32[]{:S(2)}, u32[]{:S(2)}) collective-permute-start(bf16[3,3,64,512]{3,2,1,0:T(8,128)(2,1)S(1)} %cut_columns.4.refs_0_), channel_id=1, source_target_pairs={{0,2},{4,6},{9,11},{13,15},{18,16},{22,20},{27,25},{31,29}} | collective-permute-start | bytes 1769480 | tf_op jit(solution)/shard_map/ppermute | solution.py:375
  26.8 1.4 %copy-start.1 = (bf16[3,1024,256]{2,1,0:T(8,128)(2,1)S(1)}, bf16[3,1024,256]{2,1,0:T(8,128)(2,1)}, u32[]{:S(2)}) copy-start(bf16[3,1024,256]{2,1,0:T(8,128)(2,1)} %eig_ref.1) | copy-start | bytes 4718596
  28.7 12.2 %copy-start.2 = (f32[64,64]{1,0:T(8,128)}, f32[64,64]{1,0:T(8,128)S(1)}, u32[]{:S(2)}) copy-start(f32[64,64]{1,0:T(8,128)S(1)} %get-tuple-element.32.refs_0_) | copy-start | bytes 49156
  28.7 12.2 %copy-start.4 = (f32[64,64]{1,0:T(8,128)}, f32[64,64]{1,0:T(8,128)S(1)}, u32[]{:S(2)}) copy-start(f32[64,64]{1,0:T(8,128)S(1)} %get-tuple-element.35) | copy-start | bytes 49156
  28.7 12.2 %copy-start.6 = (f32[64,64]{1,0:T(8,128)}, f32[64,64]{1,0:T(8,128)S(1)}, u32[]{:S(2)}) copy-start(f32[64,64]{1,0:T(8,128)S(1)} %get-tuple-element.34) | copy-start | bytes 49156
  28.7 12.2 %copy-start.8 = (f32[64,64]{1,0:T(8,128)}, f32[64,64]{1,0:T(8,128)S(1)}, u32[]{:S(2)}) copy-start(f32[64,64]{1,0:T(8,128)S(1)} %get-tuple-element.33) | copy-start | bytes 49156
  28.7 6.6 %collective-permute-start.13 = (bf16[3,256,128]{2,1,0:T(8,128)(2,1)S(1)}, bf16[3,256,128]{2,1,0:T(8,128)(2,1)S(1)}, u32[]{:S(2)}, u32[]{:S(2)}) collective-permute-start(bf16[3,256,128]{2,1,0:T(8,128)(2,1)S(1)} %collective-permute-done.9.refs_2_.refs_8_), channel_id=1, source_target_pairs={{8,0},{16,8},{24,16},{28,24},{20,28},{12,20},{4,12},{0,4},{9,1},{1... | collective-permute-start | bytes 589832 | tf_op jit(solution)/shard_map/ppermute | solution.py:388
  30.5 15.8 %collective-permute-start.19 = (bf16[2,3,64,512]{3,2,1,0:T(8,128)(2,1)S(1)}, bf16[2,3,64,512]{3,2,1,0:T(8,128)(2,1)}, u32[]{:S(2)}, u32[]{:S(2)}) collective-permute-start(bf16[2,3,64,512]{3,2,1,0:T(8,128)(2,1)S(1)} %cut_columns.5.refs_0_), channel_id=1, source_target_pairs={{0,2},{4,6},{9,11},{13,15},{18,16},{22,20},{27,25},{31,29}} | collective-permute-start | bytes 1179656 | tf_op jit(solution)/shard_map/ppermute | solution.py:375
  33.1 6.6 %collective-permute-start.11 = (bf16[3,256,128]{2,1,0:T(8,128)(2,1)S(1)}, bf16[3,256,128]{2,1,0:T(8,128)(2,1)S(1)}, u32[]{:S(2)}, u32[]{:S(2)}) collective-permute-start(bf16[3,256,128]{2,1,0:T(8,128)(2,1)S(1)} %collective-permute-done.7.refs_0_.refs_6_), channel_id=1, source_target_pairs={{0,8},{8,16},{16,24},{24,28},{28,20},{20,12},{12,4},{4,0},{1,9},{9... | collective-permute-start | bytes 589832 | tf_op jit(solution)/shard_map/ppermute | solution.py:387
  33.1 7.8 %collective-permute-start.14 = (bf16[3,256,128]{2,1,0:T(8,128)(2,1)S(1)}, bf16[3,256,128]{2,1,0:T(8,128)(2,1)S(1)}, u32[]{:S(2)}, u32[]{:S(2)}) collective-permute-start(bf16[3,256,128]{2,1,0:T(8,128)(2,1)S(1)} %collective-permute-done.10.refs_3_.refs_9_), channel_id=1, source_target_pairs={{8,0},{16,8},{24,16},{28,24},{20,28},{12,20},{4,12},{0,4},{9,1},{1... | collective-permute-start | bytes 589832 | tf_op jit(solution)/shard_map/ppermute | solution.py:390
  35.3 7.9 %collective-permute-start.12 = (bf16[3,256,128]{2,1,0:T(8,128)(2,1)S(1)}, bf16[3,256,128]{2,1,0:T(8,128)(2,1)}, u32[]{:S(2)}, u32[]{:S(2)}) collective-permute-start(bf16[3,256,128]{2,1,0:T(8,128)(2,1)S(1)} %collective-permute-done.8.refs_1_.refs_7_), channel_id=1, source_target_pairs={{0,8},{8,16},{16,24},{24,28},{28,20},{20,12},{12,4},{4,0},{1,9},{9... | collective-permute-start | bytes 589832 | tf_op jit(solution)/shard_map/ppermute | solution.py:389
  39.7 9.2 %collective-permute-start.15 = (bf16[3,256,128]{2,1,0:T(8,128)(2,1)S(1)}, bf16[3,256,128]{2,1,0:T(8,128)(2,1)}, u32[]{:S(2)}, u32[]{:S(2)}) collective-permute-start(bf16[3,256,128]{2,1,0:T(8,128)(2,1)S(1)} %collective-permute-done.11.refs_0_.refs_10_), channel_id=1, source_target_pairs={{0,8},{8,16},{16,24},{24,28},{28,20},{20,12},{12,4},{4,0},{1,9},{9... | collective-permute-start | bytes 589832 | tf_op jit(solution)/shard_map/ppermute | solution.py:406
  40.9 8.0 %collective-permute-start.16 = (bf16[3,256,128]{2,1,0:T(8,128)(2,1)S(1)}, bf16[3,256,128]{2,1,0:T(8,128)(2,1)}, u32[]{:S(2)}, u32[]{:S(2)}) collective-permute-start(bf16[3,256,128]{2,1,0:T(8,128)(2,1)S(1)} %collective-permute-done.14.refs_3_.refs_13_), channel_id=1, source_target_pairs={{8,0},{16,8},{24,16},{28,24},{20,28},{12,20},{4,12},{0,4},{9,1},{1... | collective-permute-start | bytes 589832 | tf_op jit(solution)/shard_map/ppermute | solution.py:407
  44.3 10.9 %collective-permute-start.20 = (bf16[2,3,64,512]{3,2,1,0:T(8,128)(2,1)S(1)}, bf16[2,3,64,512]{3,2,1,0:T(8,128)(2,1)S(1)}, u32[]{:S(2)}, u32[]{:S(2)}) collective-permute-start(bf16[2,3,64,512]{3,2,1,0:T(8,128)(2,1)S(1)} %cut_columns.6.refs_2_), channel_id=1, source_target_pairs={{0,2},{4,6},{9,11},{13,15},{18,16},{22,20},{27,25},{31,29}} | collective-permute-start | bytes 1179656 | tf_op jit(solution)/shard_map/ppermute | solution.py:375
  47.4 2.7 %copy-start = (bf16[3,3,64,512]{3,2,1,0:T(8,128)(2,1)}, bf16[3,3,64,512]{3,2,1,0:T(8,128)(2,1)S(1)}, u32[]{:S(2)}) copy-start(bf16[3,3,64,512]{3,2,1,0:T(8,128)(2,1)S(1)} %pass_on.2.refs_16_) | copy-start | bytes 1769476
  47.4 10.3 %copy-start.9 = (f32[64,64]{1,0:T(8,128)S(1)}, f32[64,64]{1,0:T(8,128)}, u32[]{:S(2)}) copy-start(f32[64,64]{1,0:T(8,128)} %copy-done.8) | copy-start | bytes 49156
  47.4 10.3 %copy-start.7 = (f32[64,64]{1,0:T(8,128)S(1)}, f32[64,64]{1,0:T(8,128)}, u32[]{:S(2)}) copy-start(f32[64,64]{1,0:T(8,128)} %copy-done.6) | copy-start | bytes 49156
  47.4 12.9 %copy-start.5 = (f32[64,64]{1,0:T(8,128)S(1)}, f32[64,64]{1,0:T(8,128)}, u32[]{:S(2)}) copy-start(f32[64,64]{1,0:T(8,128)} %copy-done.4) | copy-start | bytes 49156
  47.4 16.2 %copy-start.3 = (f32[64,64]{1,0:T(8,128)S(1)}, f32[64,64]{1,0:T(8,128)}, u32[]{:S(2)}) copy-start(f32[64,64]{1,0:T(8,128)} %copy-done.2) | copy-start | bytes 49156
  47.5 4.6 %collective-permute-start.18 = (bf16[3,3,64,512]{3,2,1,0:T(8,128)(2,1)S(1)}, bf16[3,3,64,512]{3,2,1,0:T(8,128)(2,1)S(1)}, u32[]{:S(2)}, u32[]{:S(2)}) collective-permute-start(bf16[3,3,64,512]{3,2,1,0:T(8,128)(2,1)S(1)} %pass_on.2.refs_16_), channel_id=1, source_target_pairs={{0,1},{4,5},{9,8},{13,12},{18,19},{22,23},{27,26},{31,30},{2,3},{6... | collective-permute-start | bytes 1769480 | tf_op jit(solution)/shard_map/ppermute | solution.py:380
  50.1 5.1 %collective-permute-start.21 = (bf16[1,3,64,512]{3,2,1,0:T(8,128)(2,1)S(1)}, bf16[1,3,64,512]{3,2,1,0:T(8,128)(2,1)S(1)}, u32[]{:S(2)}, u32[]{:S(2)}) collective-permute-start(bf16[1,3,64,512]{3,2,1,0:T(8,128)(2,1)S(1)} %cut_columns.7.refs_4_), channel_id=1, source_target_pairs={{0,2},{4,6},{9,11},{13,15},{18,16},{22,20},{27,25},{31,29}} | collective-permute-start | bytes 589832 | tf_op jit(solution)/shard_map/ppermute | solution.py:375
  52.1 12.2 %copy-start.10 = (bf16[3,3,64,512]{3,2,1,0:T(8,128)(2,1)}, bf16[3,3,64,512]{3,2,1,0:T(8,128)(2,1)S(1)}, u32[]{:S(2)}) copy-start(bf16[3,3,64,512]{3,2,1,0:T(8,128)(2,1)S(1)} %collective-permute-done.18.refs_17_) | copy-start | bytes 1769476
  56.3 8.0 %collective-permute-start.22 = (bf16[5,3,64,512]{3,2,1,0:T(8,128)(2,1)S(1)}, bf16[5,3,64,512]{3,2,1,0:T(8,128)(2,1)S(1)}, u32[]{:S(2)}, u32[]{:S(2)}) collective-permute-start(bf16[5,3,64,512]{3,2,1,0:T(8,128)(2,1)S(1)} %pass_on.3.refs_18_), channel_id=1, source_target_pairs={{0,1},{4,5},{9,8},{13,12},{18,19},{22,23},{27,26},{31,30},{2,3},{6... | collective-permute-start | bytes 2949128 | tf_op jit(solution)/shard_map/ppermute | solution.py:380
  57.7 2.8 %collective-permute-start.23 = (f32[64,64]{1,0:T(8,128)S(1)}, f32[64,64]{1,0:T(8,128)S(1)}, u32[]{:S(2)}, u32[]{:S(2)}) collective-permute-start(f32[64,64]{1,0:T(8,128)S(1)} %copy-done.9), channel_id=1, source_target_pairs={{0,1},{1,0},{2,3},{3,2},{4,5},{5,4},{6,7},{7,6},{8,9},{9,8},{10,11... | collective-permute-start | bytes 49160 | tf_op jit(solution)/shard_map/ppermute | solution.py:306
  57.8 4.5 %collective-permute-start.24 = (f32[64,64]{1,0:T(8,128)S(1)}, f32[64,64]{1,0:T(8,128)S(1)}, u32[]{:S(2)}, u32[]{:S(2)}) collective-permute-start(f32[64,64]{1,0:T(8,128)S(1)} %copy-done.7), channel_id=1, source_target_pairs={{0,2},{1,3},{2,0},{3,1},{4,6},{5,7},{6,4},{7,5},{8,10},{9,11},{10,... | collective-permute-start | bytes 49160 | tf_op jit(solution)/shard_map/ppermute | solution.py:306
  60.3 3.4 %collective-permute-start.25 = (f32[64,64]{1,0:T(8,128)S(1)}, f32[64,64]{1,0:T(8,128)S(1)}, u32[]{:S(2)}, u32[]{:S(2)}) collective-permute-start(f32[64,64]{1,0:T(8,128)S(1)} %copy-done.5), channel_id=1, source_target_pairs={{0,3},{1,2},{2,1},{3,0},{4,7},{5,6},{6,5},{7,4},{8,11},{9,10},{10,... | collective-permute-start | bytes 49160 | tf_op jit(solution)/shard_map/ppermute | solution.py:306

commit v10 on v8

--- a/solution.py
+++ b/solution.py
@@ -15,6 +15,7 @@
 HBM = pl.BlockSpec(memory_space=pltpu.HBM)
 ANY = pl.BlockSpec(memory_space=pl.ANY)
 MIB = 1024 * 1024
+LONG = 4 * 10**9
 
 
 def params(mib):
@@ -149,14 +150,15 @@
     cut_columns(half_ref, [(r.at[0], r.at[1]) for r in refs[:-1]], refs[-1])
 
 
-def cut_last_kernel(half_ref, up_ref, down_ref, cols_ref, up_half, down_half):
-    up_half[...] = up_ref[0]
-    down_half[...] = down_ref[1]
+def cut_split_kernel(half_ref, up_ref, down_ref, cols_ref, *refs):
+    for k, shard in enumerate((up_ref, down_ref)):
+        for at in range(2):
+            refs[2 * k + at][...] = shard[at]
     cut_columns(half_ref, [(r.at[0], r.at[1]) for r in (up_ref, down_ref)], cols_ref)
 
 
-def cut_far_kernel(half_ref, up_half, down_half, cols_ref):
-    cut_columns(half_ref, [(up_half, down_half)], cols_ref)
+def cut_pieces_kernel(half_ref, *refs):
+    cut_columns(half_ref, list(zip(refs[:-1:2], refs[1:-1:2])), refs[-1])
 
 
 def pass_on_kernel(role_ref, *refs):
@@ -178,9 +180,8 @@
     return left, right
 
 
-def covariance_kernel(slots, roles, groups, scale, role_ref, *refs):
-    shards, up_half, down_half = refs[: slots - 1], refs[slots - 1], refs[slots]
-    refs = refs[slots + 1 :]
+def covariance_kernel(slots, whole, roles, groups, scale, role_ref, *refs):
+    shards, pieces, refs = refs[:whole], refs[whole : 2 * slots - whole], refs[2 * slots - whole :]
     arrays = []
     for _, _, holder in groups:
         count = max(holder) + 1
@@ -188,7 +189,7 @@
         refs = refs[count:]
     out_ref, left, right, done, col_sem, out_sem = refs
     depth = right.shape[1] // slots
-    run = up_half.shape[1]
+    run = pieces[0].shape[1]
 
     def fetches(k, role, to):
         source = arrays[k][groups[k][2][role]]
@@ -227,9 +228,9 @@
                 right[d, to + n * depth : to + (n + 1) * depth, :] = source[n, d]
 
     def piece(slot, at, c):
-        if slot < slots - 1:
+        if slot < whole:
             return shards[slot][at, c]
-        return (up_half, down_half)[at][c]
+        return pieces[2 * (slot - whole) + at][c]
 
     def assemble(c, at):
         for q in range(slots // 2):
@@ -379,7 +380,7 @@
     def columns(slots):
         return pltpu.VMEM((slots, 3, local_frames, block), jnp.bfloat16)
 
-    def kernel(body, out_shape, scalar, values, name):
+    def kernel(body, out_shape, scalar, values, name, cost=None):
         single = not isinstance(out_shape, tuple)
         return pl.pallas_call(
             body,
@@ -387,6 +388,7 @@
             in_specs=[SMEM] + [VMEM] * len(values),
             out_specs=VMEM if single else (VMEM,) * len(out_shape),
             compiler_params=params(4),
+            cost_estimate=cost,
             name=name,
         )(scalar, *[pinned(value, pltpu.VMEM) for value in values])
 
@@ -408,31 +410,41 @@
     one = hop(own, own)
     crossed = cross(kernel(cut_kernel, columns(1), half, [own], "cut_columns"))
     cut_one = kernel(cut_kernel, columns(2), half, list(one), "cut_columns")
-    two = hop(after(one[0], crossed[1], *parts), one[1])
+    two = hop(after(one[0], crossed[1]), one[1])
     in_hbm = pass_on(crossed + cross(cut_one), role)
-    cut_two = kernel(cut_kernel, columns(2), half, list(two), "cut_columns")
-    three = hop(*two)
+    split = pltpu.VMEM(piece, jnp.bfloat16)
+    cut_two, *pieces = kernel(
+        cut_split_kernel,
+        (columns(2),) + (split,) * 4,
+        after(half, *parts),
+        list(two),
+        "cut_columns",
+    )
     crossed = cross(cut_two)
-    half_shard = pltpu.VMEM(piece, jnp.bfloat16)
-    cut_three, *halves = kernel(
-        cut_last_kernel,
-        (columns(2), half_shard, half_shard),
+    up_a, down_b = hop(pieces[0], pieces[3])
+    up_b, down_a = hop(pieces[1], pieces[2])
+    far = hop(up_a, down_b)
+    three = [up_a, up_b, down_a, down_b]
+    cut_three = kernel(
+        cut_pieces_kernel,
+        columns(2),
         after(half, projections, in_hbm[0]),
-        list(three),
+        three,
         "cut_columns",
     )
-    far = hop(*halves)
+    long = pl.CostEstimate(flops=LONG, bytes_accessed=0, transcendentals=0)
     cut_four = kernel(
-        cut_far_kernel, columns(1), after(half, crossed[1]), list(far), "cut_columns"
+        cut_pieces_kernel, columns(1), after(half, crossed[1]), list(far), "cut_columns", long
     )
     in_vmem = pass_on(
         crossed + cross(cut_three) + cross(cut_four), after(role, in_hbm[1])
     )
     groups = ((3, True, (0, 1, 0, 1)), (5, False, (0, 1, 0, 1)))
     rows = [own, *one, *two, *three, *far]
+    whole = 5
     covariance = pl.pallas_call(
         functools.partial(
-            covariance_kernel, frame_axis, atom_axis, groups, 1.0 / total_frames
+            covariance_kernel, frame_axis, whole, atom_axis, groups, 1.0 / total_frames
         ),
         out_shape=jax.ShapeDtypeStruct((3, 3, local_atoms, block), jnp.float32),
         in_specs=[SMEM]

time: 70.7 us -> 80 us (1.13)
  waiting for transfers between devices: 19.1 us -> 24.7 us
  Pallas kernels: 13.7 us -> 17.6 us
  local copies, waits for them, and re-layouts: 6.26 us -> 5.39 us
    ppermute x4 -> x5, waiting for transfers between devices: 1.13 us -> 6.37 us  [hop(): lax.ppermute(up, 'frames', forward)]
    ppermute x4 -> x5, waiting for transfers between devices: 6.53 us -> 1.31 us  [hop(): lax.ppermute(down, 'frames', backward)]
    ppermute x5, waiting for transfers between devices: 3.15 us -> 8.08 us  [cross(): return [cut, lax.ppermute(cut, axes, pairs(0, 2))]]
    pallas_call x7, Pallas kernels: 1.95 us -> 4.91 us  [kernel(): pl.pallas_call(body, out_shape=out_shape, in_specs=[SMEM] + [VMEM] * len(...]
    ppermute x4 -> x5, starting transfers between devices: 4.73 us -> 7 us  [hop(): lax.ppermute(down, 'frames', backward)]
    ppermute x5, starting transfers between devices: 14.9 us -> 13.3 us  [cross(): return [cut, lax.ppermute(cut, axes, pairs(0, 2))]]
    pallas_call x1, Pallas kernels: 8.42 us -> 9.35 us  [per_device(): pl.pallas_call(functools.partial(covariance_kernel, frame_axis, whole, at...]
    unnamed x22 -> x26, local copies, waits for them, and re-layouts: 6.26 us -> 5.39 us
  transfers between devices with their start and end apart: 21 -> 23, of which waited for: 11 -> 12; matrix products, arithmetic and copies ran while one was open for 0% -> 0% of each run, Pallas kernels for 4% -> 6%
where the time goes in v10:
time: 80 us; the launch traced here: 78.7 us
  starting transfers between devices  30.2 us (38%)
  waiting for transfers between devices  24.7 us (31%)
  Pallas kernels  17.6 us (22%)
  local copies, waits for them, and re-layouts  5.39 us (7%)
  between operations  0.88 us (1%)
    ppermute x5, starting transfers between devices, cross(): return [cut, lax.ppermute(cut, axes, pairs(0, 2))]  13.3 us
    pallas_call x1, Pallas kernels, per_device(): pl.pallas_call(functools.partial(covariance_kernel, frame_axis, whole, at...  9.35 us
    ppermute x5, waiting for transfers between devices, cross(): return [cut, lax.ppermute(cut, axes, pairs(0, 2))]  8.08 us
    ppermute x5, starting transfers between devices, hop(): lax.ppermute(down, 'frames', backward)  7 us
    ppermute x6, waiting for transfers between devices, swap(): lax.ppermute(value, 'atoms', [(a, a ^ distance) for a in range(atom_axis)])  6.8 us
    ppermute x5, waiting for transfers between devices, hop(): lax.ppermute(up, 'frames', forward)  6.37 us
    unnamed x26, local copies, waits for them, and re-layouts  5.39 us
    pallas_call x7, Pallas kernels, kernel(): pl.pallas_call(body, out_shape=out_shape, in_specs=[SMEM] + [VMEM] * len(...  4.91 us
  transfers between devices with their start and end apart: 23, of which 12 were waited for; matrix products, arithmetic and copies ran while one was open for 0% of the time, Pallas kernels for 6%

profile of v10, /device:TPU:0, one launch (start us, length us, event | category | flops | bytes accessed | tf_op | source)
XLA Modules:
  0.0 78.7 jit_solution(8533753457073022484)
XLA Ops:
  0.6 1.7 %local_moments.1 = (f32[24,64]{1,0:T(8,128)S(1)}, f32[3,64,1024]{2,1,0:T(8,128)S(1)}, f32[3,1024]{1,0:T(4,128)S(1)}) custom-call(f32[3,64,1024]{2,1,0:T(8,128)} %bitcast.6, f32[3,1024]{1,0:T(4,128)} %ref_hbm.1), custom_call_target="tpu_custom_call" | custom-call | tf_op jit(solution)/shard_map/local_moments/pallas_call | solution.py:311
  2.3 2.4 %collective-permute-start.2 = (f32[24,64]{1,0:T(8,128)S(1)}, f32[24,64]{1,0:T(8,128)S(1)}, u32[]{:S(2)}, u32[]{:S(2)}) collective-permute-start(f32[24,64]{1,0:T(8,128)S(1)} %get-tuple-element.21.refs_0_), channel_id=1, source_target_pairs={{0,3},{1,2},{2,1},{3,0},{4,7},{5,6},{6,5},{7,4},{8,11},{9,10},{10,... | collective-permute-start | bytes 18440 | tf_op jit(solution)/shard_map/ppermute | solution.py:325
  4.7 0.6 collective-permute-start.1
  5.4 0.0 collective-permute-start
  5.4 0.7 collective-permute-done.2.refs_3_
  6.1 2.3 %collective-permute-done.1.refs_2_ = f32[24,64]{1,0:T(8,128)S(1)} collective-permute-done((f32[24,64]{1,0:T(8,128)S(1)}, f32[24,64]{1,0:T(8,128)S(1)}, u32[]{:S(2)}, u32[]{:S(2)}) %collective-permute-start.1) | collective-permute-done | bytes 6176 | tf_op jit(solution)/shard_map/ppermute | solution.py:325
  8.4 0.0 collective-permute-done.refs_1_
  8.4 0.6 polar_align.1
  9.0 1.6 %collective-permute-start.3 = (bf16[2,3,256,128]{3,2,1,0:T(8,128)(2,1)S(1)}, bf16[2,3,256,128]{3,2,1,0:T(8,128)(2,1)S(1)}, u32[]{:S(2)}, u32[]{:S(2)}) collective-permute-start(bf16[2,3,256,128]{3,2,1,0:T(8,128)(2,1)S(1)} %get-tuple-element.24.refs_0_), channel_id=1, source_target_pairs={{0,8},{8,16},{16,24},{24,28},{28,20},{20,12},{12,4},{4,0},{1,9},{9... | collective-permute-start | bytes 1179656 | tf_op jit(solution)/shard_map/ppermute | solution.py:408
  10.7 0.4 collective-permute-start.4
  11.1 0.1 cut_columns.5.refs_0_
  11.3 2.6 %collective-permute-start.5 = (bf16[1,3,64,512]{3,2,1,0:T(8,128)(2,1)S(1)}, bf16[1,3,64,512]{3,2,1,0:T(8,128)(2,1)S(1)}, u32[]{:S(2)}, u32[]{:S(2)}) collective-permute-start(bf16[1,3,64,512]{3,2,1,0:T(8,128)(2,1)S(1)} %cut_columns.5.refs_0_), channel_id=1, source_target_pairs={{0,2},{4,6},{9,11},{13,15},{18,16},{22,20},{27,25},{31,29}} | collective-permute-start | bytes 589832 | tf_op jit(solution)/shard_map/ppermute | solution.py:396
  13.8 3.2 %collective-permute-done.5.refs_1_ = bf16[1,3,64,512]{3,2,1,0:T(8,128)(2,1)S(1)} collective-permute-done((bf16[1,3,64,512]{3,2,1,0:T(8,128)(2,1)S(1)}, bf16[1,3,64,512]{3,2,1,0:T(8,128)(2,1)S(1)}, u32[]{:S(2)}, u32[]{:S(2)}) %collective-permute-start.5) | collective-permute-done | bytes 196640 | tf_op jit(solution)/shard_map/ppermute | solution.py:396
  17.0 2.6 %collective-permute-done.3.refs_0_.refs_1_ = bf16[2,3,256,128]{3,2,1,0:T(8,128)(2,1)S(1)} collective-permute-done((bf16[2,3,256,128]{3,2,1,0:T(8,128)(2,1)S(1)}, bf16[2,3,256,128]{3,2,1,0:T(8,128)(2,1)S(1)}, u32[]{:S(2)}, u32[]{:S(2)}) %collective-permute-start.3) | collective-permute-done | bytes 393248 | tf_op jit(solution)/shard_map/ppermute | solution.py:408
  19.6 1.3 %collective-permute-done.4.refs_1_.refs_2_ = bf16[2,3,256,128]{3,2,1,0:T(8,128)(2,1)S(1)} collective-permute-done((bf16[2,3,256,128]{3,2,1,0:T(8,128)(2,1)S(1)}, bf16[2,3,256,128]{3,2,1,0:T(8,128)(2,1)S(1)}, u32[]{:S(2)}, u32[]{:S(2)}) %collective-permute-start.4) | collective-permute-done | bytes 393248 | tf_op jit(solution)/shard_map/ppermute | solution.py:408
  20.9 0.4 collective-permute-start.7
  21.4 1.6 %collective-permute-start.6 = (bf16[2,3,256,128]{3,2,1,0:T(8,128)(2,1)S(1)}, bf16[2,3,256,128]{3,2,1,0:T(8,128)(2,1)S(1)}, u32[]{:S(2)}, u32[]{:S(2)}) collective-permute-start(bf16[2,3,256,128]{3,2,1,0:T(8,128)(2,1)S(1)} %collective-permute-done.3.refs_0_.refs_1_), channel_id=1, source_target_pairs={{0,8},{8,16},{16,24},{24,28},{28,20},{20,12},{12,4},{4,0},{1,9},{9... | collective-permute-start | bytes 1179656 | tf_op jit(solution)/shard_map/ppermute | solution.py:408
  23.0 0.2 cut_columns.7.refs_2_
  23.2 3.4 %collective-permute-start.17 = (bf16[2,3,64,512]{3,2,1,0:T(8,128)(2,1)S(1)}, bf16[2,3,64,512]{3,2,1,0:T(8,128)(2,1)}, u32[]{:S(2)}, u32[]{:S(2)}) collective-permute-start(bf16[2,3,64,512]{3,2,1,0:T(8,128)(2,1)S(1)} %cut_columns.7.refs_2_), channel_id=1, source_target_pairs={{0,2},{4,6},{9,11},{13,15},{18,16},{22,20},{27,25},{31,29}} | collective-permute-start | bytes 1179656 | tf_op jit(solution)/shard_map/ppermute | solution.py:396
  26.5 1.4 %copy-done.1 = bf16[3,1024,256]{2,1,0:T(8,128)(2,1)S(1)} copy-done((bf16[3,1024,256]{2,1,0:T(8,128)(2,1)S(1)}, bf16[3,1024,256]{2,1,0:T(8,128)(2,1)}, u32[]{:S(2)}) %copy-start.1) | copy-done | bytes 1572888
  27.9 0.5 project.1
  28.4 0.0 copy-start.4
  28.4 0.1 collective-permute-start.8
  28.5 0.1 collective-permute-start.9
  28.6 1.1 %collective-permute-done.8.refs_1_ = f32[64,64]{1,0:T(8,128)S(1)} collective-permute-done((f32[64,64]{1,0:T(8,128)S(1)}, f32[64,64]{1,0:T(8,128)S(1)}, u32[]{:S(2)}, u32[]{:S(2)}) %collective-permute-start.8) | collective-permute-done | bytes 16416 | tf_op jit(solution)/shard_map/ppermute | solution.py:325
  29.7 0.7 collective-permute-start.10
  30.4 2.1 %collective-permute-done.9.refs_2_ = f32[64,64]{1,0:T(8,128)S(1)} collective-permute-done((f32[64,64]{1,0:T(8,128)S(1)}, f32[64,64]{1,0:T(8,128)S(1)}, u32[]{:S(2)}, u32[]{:S(2)}) %collective-permute-start.9) | collective-permute-done | bytes 16416 | tf_op jit(solution)/shard_map/ppermute | solution.py:325
  32.5 0.6 collective-permute-done.10.refs_3_
  33.0 0.0 collective-permute-done.7.down_ref.refs_4_
  33.0 0.0 collective-permute-done.6.up_ref.refs_3_
  33.0 1.1 %cut_columns.6 = (bf16[2,3,64,512]{3,2,1,0:T(8,128)(2,1)}, bf16[3,256,128]{2,1,0:T(8,128)(2,1)S(1)}, bf16[3,256,128]{2,1,0:T(8,128)(2,1)}, bf16[3,256,128]{2,1,0:T(8,128)(2,1)}, bf16[3,256,128]{2,1,0:T(8,128)(2,1)S(1)}) custom-call(s32[1]{0:T(128)} %bitcast.2.half_ref, bf16[2,3,256,128]{3,2,1,0:T(8,128)(2,1)S(1)} %collective-permute-done.6.up_ref.refs_3_, ...), custom_call_target="tpu_custom_call" | custom-call | tf_op jit(solution)/shard_map/cut_columns/pallas_call | solution.py:385
  34.2 4.2 %collective-permute-start.19 = (bf16[2,3,64,512]{3,2,1,0:T(8,128)(2,1)}, bf16[2,3,64,512]{3,2,1,0:T(8,128)(2,1)}, u32[]{:S(2)}, u32[]{:S(2)}) collective-permute-start(bf16[2,3,64,512]{3,2,1,0:T(8,128)(2,1)} %get-tuple-element.37.refs_0_), channel_id=1, source_target_pairs={{0,2},{4,6},{9,11},{13,15},{18,16},{22,20},{27,25},{31,29}} | collective-permute-start | bytes 1179656 | tf_op jit(solution)/shard_map/ppermute | solution.py:396
  38.4 0.0 collective-permute-start.11
  38.4 2.0 %collective-permute-start.14 = (bf16[3,256,128]{2,1,0:T(8,128)(2,1)S(1)}, bf16[3,256,128]{2,1,0:T(8,128)(2,1)S(1)}, u32[]{:S(2)}, u32[]{:S(2)}) collective-permute-start(bf16[3,256,128]{2,1,0:T(8,128)(2,1)S(1)} %get-tuple-element.35), channel_id=1, source_target_pairs={{8,0},{16,8},{24,16},{28,24},{20,28},{12,20},{4,12},{0,4},{9,1},{1... | collective-permute-start | bytes 589832 | tf_op jit(solution)/shard_map/ppermute | solution.py:408
  40.4 0.0 collective-permute-start.12
  40.4 0.0 collective-permute-done.17.refs_3_
  40.4 2.1 %collective-permute-start.13 = (bf16[3,256,128]{2,1,0:T(8,128)(2,1)}, bf16[3,256,128]{2,1,0:T(8,128)(2,1)S(1)}, u32[]{:S(2)}, u32[]{:S(2)}) collective-permute-start(bf16[3,256,128]{2,1,0:T(8,128)(2,1)} %get-tuple-element.34), channel_id=1, source_target_pairs={{8,0},{16,8},{24,16},{28,24},{20,28},{12,20},{4,12},{0,4},{9,1},{1... | collective-permute-start | bytes 589832 | tf_op jit(solution)/shard_map/ppermute | solution.py:408
  42.5 3.7 %collective-permute-done.11.refs_0_.refs_5_ = bf16[3,256,128]{2,1,0:T(8,128)(2,1)S(1)} collective-permute-done((bf16[3,256,128]{2,1,0:T(8,128)(2,1)S(1)}, bf16[3,256,128]{2,1,0:T(8,128)(2,1)S(1)}, u32[]{:S(2)}, u32[]{:S(2)}) %collective-permute-start.11) | collective-permute-done | bytes 196640 | tf_op jit(solution)/shard_map/ppermute | solution.py:408
  46.2 0.0 collective-permute-start.15
  46.2 0.0 collective-permute-done.14.refs_3_.refs_8_
  46.2 2.0 %collective-permute-start.16 = (bf16[3,256,128]{2,1,0:T(8,128)(2,1)S(1)}, bf16[3,256,128]{2,1,0:T(8,128)(2,1)}, u32[]{:S(2)}, u32[]{:S(2)}) collective-permute-start(bf16[3,256,128]{2,1,0:T(8,128)(2,1)S(1)} %collective-permute-done.14.refs_3_.refs_8_), channel_id=1, source_target_pairs={{8,0},{16,8},{24,16},{28,24},{20,28},{12,20},{4,12},{0,4},{9,1},{1... | collective-permute-start | bytes 589832 | tf_op jit(solution)/shard_map/ppermute | solution.py:408
  48.2 0.9 %copy-done.3 = bf16[1,3,64,512]{3,2,1,0:T(8,128)(2,1)S(1)} copy-done((bf16[1,3,64,512]{3,2,1,0:T(8,128)(2,1)S(1)}, bf16[1,3,64,512]{3,2,1,0:T(8,128)(2,1)}, u32[]{:S(2)}) %copy-start.3) | copy-done | bytes 196632
  49.2 1.0 %pass_on.2.refs_11_ = bf16[3,3,64,512]{3,2,1,0:T(8,128)(2,1)S(1)} custom-call(s32[1]{0:T(128)} %bitcast.role_ref, bf16[1,3,64,512]{3,2,1,0:T(8,128)(2,1)S(1)} %cut_columns.5.refs_0_, bf16[1,3,64,512]{3,2,1,0:T(8,128)(2,1)S(1)} %copy-done.3, bf16[2,3,64,512]{3,2,1,0:T(8,128)(2,1)S(1)} %cut_columns.7.refs_2_, ...), custom_call_target="tpu_custom_call" | custom-call | tf_op jit(solution)/shard_map/pass_on/pallas_call | solution.py:385
  50.2 0.0 collective-permute-done.12.refs_1_.refs_6_
  50.2 1.3 %collective-permute-start.18 = (bf16[3,3,64,512]{3,2,1,0:T(8,128)(2,1)S(1)}, bf16[3,3,64,512]{3,2,1,0:T(8,128)(2,1)S(1)}, u32[]{:S(2)}, u32[]{:S(2)}) collective-permute-start(bf16[3,3,64,512]{3,2,1,0:T(8,128)(2,1)S(1)} %pass_on.2.refs_11_), channel_id=1, source_target_pairs={{0,1},{4,5},{9,8},{13,12},{18,19},{22,23},{27,26},{31,30},{2,3},{6... | collective-permute-start | bytes 1769480 | tf_op jit(solution)/shard_map/ppermute | solution.py:401
  51.6 0.0 copy-start.5
  51.6 0.7 copy-done.5
  52.3 0.8 copy-done.7
  53.1 0.8 copy-done.9
  53.8 0.8 copy-done.11
  54.6 0.6 sum_shares.1
  55.2 0.0 collective-permute-done.13.refs_2_.refs_7_
  55.2 0.2 cut_columns.8.refs_2_
  55.4 1.9 %collective-permute-start.20 = (bf16[2,3,64,512]{3,2,1,0:T(8,128)(2,1)S(1)}, bf16[2,3,64,512]{3,2,1,0:T(8,128)(2,1)S(1)}, u32[]{:S(2)}, u32[]{:S(2)}) collective-permute-start(bf16[2,3,64,512]{3,2,1,0:T(8,128)(2,1)S(1)} %cut_columns.8.refs_2_), channel_id=1, source_target_pairs={{0,2},{4,6},{9,11},{13,15},{18,16},{22,20},{27,25},{31,29}} | collective-permute-start | bytes 1179656 | tf_op jit(solution)/shard_map/ppermute | solution.py:396
  57.3 0.0 collective-permute-done.19.refs_1_
  57.4 0.0 collective-permute-done.16.refs_1_.refs_10_
  57.4 1.1 %cut_columns.9.refs_4_ = bf16[1,3,64,512]{3,2,1,0:T(8,128)(2,1)S(1)} custom-call(s32[1]{0:T(128)} %bitcast.2.half_ref, bf16[3,256,128]{2,1,0:T(8,128)(2,1)S(1)} %collective-permute-done.15.refs_0_.refs_9_, bf16[3,256,128]{2,1,0:T(8,128)(2,1)} %collective-permute-done.16.refs_1_.refs_10_), custom_call_target="tpu_custom_call" | custom-call | flops 4000000000 | tf_op jit(solution)/shard_map/cut_columns/pallas_call | solution.py:385
  58.4 1.3 %collective-permute-start.21 = (bf16[1,3,64,512]{3,2,1,0:T(8,128)(2,1)S(1)}, bf16[1,3,64,512]{3,2,1,0:T(8,128)(2,1)S(1)}, u32[]{:S(2)}, u32[]{:S(2)}) collective-permute-start(bf16[1,3,64,512]{3,2,1,0:T(8,128)(2,1)S(1)} %cut_columns.9.refs_4_), channel_id=1, source_target_pairs={{0,2},{4,6},{9,11},{13,15},{18,16},{22,20},{27,25},{31,29}} | collective-permute-start | bytes 589832 | tf_op jit(solution)/shard_map/ppermute | solution.py:396
  59.8 2.8 %collective-permute-done.20.refs_3_ = bf16[2,3,64,512]{3,2,1,0:T(8,128)(2,1)S(1)} collective-permute-done((bf16[2,3,64,512]{3,2,1,0:T(8,128)(2,1)S(1)}, bf16[2,3,64,512]{3,2,1,0:T(8,128)(2,1)S(1)}, u32[]{:S(2)}, u32[]{:S(2)}) %collective-permute-start.20) | collective-permute-done | bytes 393248 | tf_op jit(solution)/shard_map/ppermute | solution.py:396
  62.6 2.1 %collective-permute-done.21.refs_5_ = bf16[1,3,64,512]{3,2,1,0:T(8,128)(2,1)S(1)} collective-permute-done((bf16[1,3,64,512]{3,2,1,0:T(8,128)(2,1)S(1)}, bf16[1,3,64,512]{3,2,1,0:T(8,128)(2,1)S(1)}, u32[]{:S(2)}, u32[]{:S(2)}) %collective-permute-start.21) | collective-permute-done | bytes 196640 | tf_op jit(solution)/shard_map/ppermute | solution.py:396
  64.7 1.2 %pass_on.3.refs_13_ = bf16[5,3,64,512]{3,2,1,0:T(8,128)(2,1)S(1)} custom-call(s32[1]{0:T(128)} %bitcast.role_ref, bf16[2,3,64,512]{3,2,1,0:T(8,128)(2,1)} %get-tuple-element.37.refs_0_, bf16[2,3,64,512]{3,2,1,0:T(8,128)(2,1)} %collective-permute-done.19.refs_1_, bf16[2,3,64,512]{3,2,1,0:T(8,128)(2,1)S(1)} %cut_columns.8.refs_2_, ...), custom_call_target="tpu_custom_call" | custom-call | tf_op jit(solution)/shard_map/pass_on/pallas_call | solution.py:385
  65.9 1.4 %collective-permute-start.22 = (bf16[5,3,64,512]{3,2,1,0:T(8,128)(2,1)S(1)}, bf16[5,3,64,512]{3,2,1,0:T(8,128)(2,1)S(1)}, u32[]{:S(2)}, u32[]{:S(2)}) collective-permute-start(bf16[5,3,64,512]{3,2,1,0:T(8,128)(2,1)S(1)} %pass_on.3.refs_13_), channel_id=1, source_target_pairs={{0,1},{4,5},{9,8},{13,12},{18,19},{22,23},{27,26},{31,30},{2,3},{6... | collective-permute-start | bytes 2949128 | tf_op jit(solution)/shard_map/ppermute | solution.py:401
  67.2 2.1 %collective-permute-done.22.refs_14_ = bf16[5,3,64,512]{3,2,1,0:T(8,128)(2,1)S(1)} collective-permute-done((bf16[5,3,64,512]{3,2,1,0:T(8,128)(2,1)S(1)}, bf16[5,3,64,512]{3,2,1,0:T(8,128)(2,1)S(1)}, u32[]{:S(2)}, u32[]{:S(2)}) %collective-permute-start.22) | collective-permute-done | bytes 983072 | tf_op jit(solution)/shard_map/ppermute | solution.py:401
  69.4 9.4 %covariance_tile.1 = f32[3,3,1024,512]{3,2,1,0:T(8,128)} custom-call(s32[1]{0:T(128)} %bitcast.role_ref, bf16[2,3,256,128]{3,2,1,0:T(8,128)(2,1)S(1)} %get-tuple-element.24.refs_0_, bf16[2,3,256,128]{3,2,1,0:T(8,128)(2,1)S(1)} %collective-permute-done.3.refs_0_.refs_1_, bf16[2,3,256,128]{3,2,1,0:T(8,128)(2,1)S(1)} %collective-permute-done.4.refs_1_.refs_2_, ...), custom_call_target="tpu_custom_call" | custom-call | flops 4831838208 | bytes 25165824 | tf_op jit(solution)/shard_map/covariance_tile/pallas_call | solution.py:445
  (20 shorter events, 0.0 us)
Async XLA Ops:
  2.3 3.8 %collective-permute-start.2 = (f32[24,64]{1,0:T(8,128)S(1)}, f32[24,64]{1,0:T(8,128)S(1)}, u32[]{:S(2)}, u32[]{:S(2)}) collective-permute-start(f32[24,64]{1,0:T(8,128)S(1)} %get-tuple-element.21.refs_0_), channel_id=1, source_target_pairs={{0,3},{1,2},{2,1},{3,0},{4,7},{5,6},{6,5},{7,4},{8,11},{9,10},{10,... | collective-permute-start | bytes 18440 | tf_op jit(solution)/shard_map/ppermute | solution.py:325
  4.7 3.7 %collective-permute-start.1 = (f32[24,64]{1,0:T(8,128)S(1)}, f32[24,64]{1,0:T(8,128)S(1)}, u32[]{:S(2)}, u32[]{:S(2)}) collective-permute-start(f32[24,64]{1,0:T(8,128)S(1)} %get-tuple-element.21.refs_0_), channel_id=1, source_target_pairs={{0,2},{1,3},{2,0},{3,1},{4,6},{5,7},{6,4},{7,5},{8,10},{9,11},{10,... | collective-permute-start | bytes 18440 | tf_op jit(solution)/shard_map/ppermute | solution.py:325
  5.4 3.1 %collective-permute-start = (f32[24,64]{1,0:T(8,128)S(1)}, f32[24,64]{1,0:T(8,128)S(1)}, u32[]{:S(2)}, u32[]{:S(2)}) collective-permute-start(f32[24,64]{1,0:T(8,128)S(1)} %get-tuple-element.21.refs_0_), channel_id=1, source_target_pairs={{0,1},{1,0},{2,3},{3,2},{4,5},{5,4},{6,7},{7,6},{8,9},{9,8},{10,11... | collective-permute-start | bytes 18440 | tf_op jit(solution)/shard_map/ppermute | solution.py:325
  9.0 10.6 %collective-permute-start.3 = (bf16[2,3,256,128]{3,2,1,0:T(8,128)(2,1)S(1)}, bf16[2,3,256,128]{3,2,1,0:T(8,128)(2,1)S(1)}, u32[]{:S(2)}, u32[]{:S(2)}) collective-permute-start(bf16[2,3,256,128]{3,2,1,0:T(8,128)(2,1)S(1)} %get-tuple-element.24.refs_0_), channel_id=1, source_target_pairs={{0,8},{8,16},{16,24},{24,28},{28,20},{20,12},{12,4},{4,0},{1,9},{9... | collective-permute-start | bytes 1179656 | tf_op jit(solution)/shard_map/ppermute | solution.py:408
  10.7 10.3 %collective-permute-start.4 = (bf16[2,3,256,128]{3,2,1,0:T(8,128)(2,1)S(1)}, bf16[2,3,256,128]{3,2,1,0:T(8,128)(2,1)S(1)}, u32[]{:S(2)}, u32[]{:S(2)}) collective-permute-start(bf16[2,3,256,128]{3,2,1,0:T(8,128)(2,1)S(1)} %get-tuple-element.24.refs_0_), channel_id=1, source_target_pairs={{8,0},{16,8},{24,16},{28,24},{20,28},{12,20},{4,12},{0,4},{9,1},{1... | collective-permute-start | bytes 1179656 | tf_op jit(solution)/shard_map/ppermute | solution.py:408
  11.3 5.7 %collective-permute-start.5 = (bf16[1,3,64,512]{3,2,1,0:T(8,128)(2,1)S(1)}, bf16[1,3,64,512]{3,2,1,0:T(8,128)(2,1)S(1)}, u32[]{:S(2)}, u32[]{:S(2)}) collective-permute-start(bf16[1,3,64,512]{3,2,1,0:T(8,128)(2,1)S(1)} %cut_columns.5.refs_0_), channel_id=1, source_target_pairs={{0,2},{4,6},{9,11},{13,15},{18,16},{22,20},{27,25},{31,29}} | collective-permute-start | bytes 589832 | tf_op jit(solution)/shard_map/ppermute | solution.py:396
  17.0 23.4 %copy-start.2 = (bf16[1,3,64,512]{3,2,1,0:T(8,128)(2,1)}, bf16[1,3,64,512]{3,2,1,0:T(8,128)(2,1)S(1)}, u32[]{:S(2)}) copy-start(bf16[1,3,64,512]{3,2,1,0:T(8,128)(2,1)S(1)} %collective-permute-done.5.refs_1_) | copy-start | bytes 589828
  20.9 12.1 %collective-permute-start.7 = (bf16[2,3,256,128]{3,2,1,0:T(8,128)(2,1)S(1)}, bf16[2,3,256,128]{3,2,1,0:T(8,128)(2,1)S(1)}, u32[]{:S(2)}, u32[]{:S(2)}) collective-permute-start(bf16[2,3,256,128]{3,2,1,0:T(8,128)(2,1)S(1)} %collective-permute-done.4.refs_1_.refs_2_), channel_id=1, source_target_pairs={{8,0},{16,8},{24,16},{28,24},{20,28},{12,20},{4,12},{0,4},{9,1},{1... | collective-permute-start | bytes 1179656 | tf_op jit(solution)/shard_map/ppermute | solution.py:408
  21.4 11.7 %collective-permute-start.6 = (bf16[2,3,256,128]{3,2,1,0:T(8,128)(2,1)S(1)}, bf16[2,3,256,128]{3,2,1,0:T(8,128)(2,1)S(1)}, u32[]{:S(2)}, u32[]{:S(2)}) collective-permute-start(bf16[2,3,256,128]{3,2,1,0:T(8,128)(2,1)S(1)} %collective-permute-done.3.refs_0_.refs_1_), channel_id=1, source_target_pairs={{0,8},{8,16},{16,24},{24,28},{28,20},{20,12},{12,4},{4,0},{1,9},{9... | collective-permute-start | bytes 1179656 | tf_op jit(solution)/shard_map/ppermute | solution.py:408
  23.2 17.2 %collective-permute-start.17 = (bf16[2,3,64,512]{3,2,1,0:T(8,128)(2,1)S(1)}, bf16[2,3,64,512]{3,2,1,0:T(8,128)(2,1)}, u32[]{:S(2)}, u32[]{:S(2)}) collective-permute-start(bf16[2,3,64,512]{3,2,1,0:T(8,128)(2,1)S(1)} %cut_columns.7.refs_2_), channel_id=1, source_target_pairs={{0,2},{4,6},{9,11},{13,15},{18,16},{22,20},{27,25},{31,29}} | collective-permute-start | bytes 1179656 | tf_op jit(solution)/shard_map/ppermute | solution.py:396
  26.5 1.4 %copy-start.1 = (bf16[3,1024,256]{2,1,0:T(8,128)(2,1)S(1)}, bf16[3,1024,256]{2,1,0:T(8,128)(2,1)}, u32[]{:S(2)}) copy-start(bf16[3,1024,256]{2,1,0:T(8,128)(2,1)} %eig_ref.1) | copy-start | bytes 4718596
  28.4 17.8 %copy-start.4 = (f32[64,64]{1,0:T(8,128)}, f32[64,64]{1,0:T(8,128)S(1)}, u32[]{:S(2)}) copy-start(f32[64,64]{1,0:T(8,128)S(1)} %get-tuple-element.27.refs_0_) | copy-start | bytes 49156
  28.4 1.3 %collective-permute-start.8 = (f32[64,64]{1,0:T(8,128)S(1)}, f32[64,64]{1,0:T(8,128)S(1)}, u32[]{:S(2)}, u32[]{:S(2)}) collective-permute-start(f32[64,64]{1,0:T(8,128)S(1)} %get-tuple-element.28), channel_id=1, source_target_pairs={{0,1},{1,0},{2,3},{3,2},{4,5},{5,4},{6,7},{7,6},{8,9},{9,8},{10,11... | collective-permute-start | bytes 49160 | tf_op jit(solution)/shard_map/ppermute | solution.py:325
  28.5 4.0 %collective-permute-start.9 = (f32[64,64]{1,0:T(8,128)S(1)}, f32[64,64]{1,0:T(8,128)S(1)}, u32[]{:S(2)}, u32[]{:S(2)}) collective-permute-start(f32[64,64]{1,0:T(8,128)S(1)} %get-tuple-element.29), channel_id=1, source_target_pairs={{0,2},{1,3},{2,0},{3,1},{4,6},{5,7},{6,4},{7,5},{8,10},{9,11},{10,... | collective-permute-start | bytes 49160 | tf_op jit(solution)/shard_map/ppermute | solution.py:325
  29.7 10.7 %copy-start.6 = (f32[64,64]{1,0:T(8,128)}, f32[64,64]{1,0:T(8,128)S(1)}, u32[]{:S(2)}) copy-start(f32[64,64]{1,0:T(8,128)S(1)} %collective-permute-done.8.refs_1_) | copy-start | bytes 49156
  29.7 3.3 %collective-permute-start.10 = (f32[64,64]{1,0:T(8,128)S(1)}, f32[64,64]{1,0:T(8,128)S(1)}, u32[]{:S(2)}, u32[]{:S(2)}) collective-permute-start(f32[64,64]{1,0:T(8,128)S(1)} %get-tuple-element.30), channel_id=1, source_target_pairs={{0,3},{1,2},{2,1},{3,0},{4,7},{5,6},{6,5},{7,4},{8,11},{9,10},{10,... | collective-permute-start | bytes 49160 | tf_op jit(solution)/shard_map/ppermute | solution.py:325
  32.5 7.9 %copy-start.8 = (f32[64,64]{1,0:T(8,128)}, f32[64,64]{1,0:T(8,128)S(1)}, u32[]{:S(2)}) copy-start(f32[64,64]{1,0:T(8,128)S(1)} %collective-permute-done.9.refs_2_) | copy-start | bytes 49156
  33.0 7.4 %copy-start.10 = (f32[64,64]{1,0:T(8,128)}, f32[64,64]{1,0:T(8,128)S(1)}, u32[]{:S(2)}) copy-start(f32[64,64]{1,0:T(8,128)S(1)} %collective-permute-done.10.refs_3_) | copy-start | bytes 49156
  34.2 23.2 %collective-permute-start.19 = (bf16[2,3,64,512]{3,2,1,0:T(8,128)(2,1)}, bf16[2,3,64,512]{3,2,1,0:T(8,128)(2,1)}, u32[]{:S(2)}, u32[]{:S(2)}) collective-permute-start(bf16[2,3,64,512]{3,2,1,0:T(8,128)(2,1)} %get-tuple-element.37.refs_0_), channel_id=1, source_target_pairs={{0,2},{4,6},{9,11},{13,15},{18,16},{22,20},{27,25},{31,29}} | collective-permute-start | bytes 1179656 | tf_op jit(solution)/shard_map/ppermute | solution.py:396
  38.4 7.8 %collective-permute-start.11 = (bf16[3,256,128]{2,1,0:T(8,128)(2,1)S(1)}, bf16[3,256,128]{2,1,0:T(8,128)(2,1)S(1)}, u32[]{:S(2)}, u32[]{:S(2)}) collective-permute-start(bf16[3,256,128]{2,1,0:T(8,128)(2,1)S(1)} %get-tuple-element.32), channel_id=1, source_target_pairs={{0,8},{8,16},{16,24},{24,28},{28,20},{20,12},{12,4},{4,0},{1,9},{9... | collective-permute-start | bytes 589832 | tf_op jit(solution)/shard_map/ppermute | solution.py:408
  38.4 7.8 %collective-permute-start.14 = (bf16[3,256,128]{2,1,0:T(8,128)(2,1)S(1)}, bf16[3,256,128]{2,1,0:T(8,128)(2,1)S(1)}, u32[]{:S(2)}, u32[]{:S(2)}) collective-permute-start(bf16[3,256,128]{2,1,0:T(8,128)(2,1)S(1)} %get-tuple-element.35), channel_id=1, source_target_pairs={{8,0},{16,8},{24,16},{28,24},{20,28},{12,20},{4,12},{0,4},{9,1},{1... | collective-permute-start | bytes 589832 | tf_op jit(solution)/shard_map/ppermute | solution.py:408
  40.4 9.8 %collective-permute-start.12 = (bf16[3,256,128]{2,1,0:T(8,128)(2,1)}, bf16[3,256,128]{2,1,0:T(8,128)(2,1)S(1)}, u32[]{:S(2)}, u32[]{:S(2)}) collective-permute-start(bf16[3,256,128]{2,1,0:T(8,128)(2,1)} %get-tuple-element.33), channel_id=1, source_target_pairs={{0,8},{8,16},{16,24},{24,28},{28,20},{20,12},{12,4},{4,0},{1,9},{9... | collective-permute-start | bytes 589832 | tf_op jit(solution)/shard_map/ppermute | solution.py:408
  40.4 14.8 %collective-permute-start.13 = (bf16[3,256,128]{2,1,0:T(8,128)(2,1)}, bf16[3,256,128]{2,1,0:T(8,128)(2,1)S(1)}, u32[]{:S(2)}, u32[]{:S(2)}) collective-permute-start(bf16[3,256,128]{2,1,0:T(8,128)(2,1)} %get-tuple-element.34), channel_id=1, source_target_pairs={{8,0},{16,8},{24,16},{28,24},{20,28},{12,20},{4,12},{0,4},{9,1},{1... | collective-permute-start | bytes 589832 | tf_op jit(solution)/shard_map/ppermute | solution.py:408
  46.2 11.1 %collective-permute-start.15 = (bf16[3,256,128]{2,1,0:T(8,128)(2,1)S(1)}, bf16[3,256,128]{2,1,0:T(8,128)(2,1)S(1)}, u32[]{:S(2)}, u32[]{:S(2)}) collective-permute-start(bf16[3,256,128]{2,1,0:T(8,128)(2,1)S(1)} %collective-permute-done.11.refs_0_.refs_5_), channel_id=1, source_target_pairs={{0,8},{8,16},{16,24},{24,28},{28,20},{20,12},{12,4},{4,0},{1,9},{9... | collective-permute-start | bytes 589832 | tf_op jit(solution)/shard_map/ppermute | solution.py:408
  46.2 11.1 %collective-permute-start.16 = (bf16[3,256,128]{2,1,0:T(8,128)(2,1)S(1)}, bf16[3,256,128]{2,1,0:T(8,128)(2,1)}, u32[]{:S(2)}, u32[]{:S(2)}) collective-permute-start(bf16[3,256,128]{2,1,0:T(8,128)(2,1)S(1)} %collective-permute-done.14.refs_3_.refs_8_), channel_id=1, source_target_pairs={{8,0},{16,8},{24,16},{28,24},{20,28},{12,20},{4,12},{0,4},{9,1},{1... | collective-permute-start | bytes 589832 | tf_op jit(solution)/shard_map/ppermute | solution.py:408
  48.2 0.9 %copy-start.3 = (bf16[1,3,64,512]{3,2,1,0:T(8,128)(2,1)S(1)}, bf16[1,3,64,512]{3,2,1,0:T(8,128)(2,1)}, u32[]{:S(2)}) copy-start(bf16[1,3,64,512]{3,2,1,0:T(8,128)(2,1)} %copy-done.2) | copy-start | bytes 589828
  50.2 19.2 %copy-start = (bf16[3,3,64,512]{3,2,1,0:T(8,128)(2,1)}, bf16[3,3,64,512]{3,2,1,0:T(8,128)(2,1)S(1)}, u32[]{:S(2)}) copy-start(bf16[3,3,64,512]{3,2,1,0:T(8,128)(2,1)S(1)} %pass_on.2.refs_11_) | copy-start | bytes 1769476
  50.2 9.5 %collective-permute-start.18 = (bf16[3,3,64,512]{3,2,1,0:T(8,128)(2,1)S(1)}, bf16[3,3,64,512]{3,2,1,0:T(8,128)(2,1)S(1)}, u32[]{:S(2)}, u32[]{:S(2)}) collective-permute-start(bf16[3,3,64,512]{3,2,1,0:T(8,128)(2,1)S(1)} %pass_on.2.refs_11_), channel_id=1, source_target_pairs={{0,1},{4,5},{9,8},{13,12},{18,19},{22,23},{27,26},{31,30},{2,3},{6... | collective-permute-start | bytes 1769480 | tf_op jit(solution)/shard_map/ppermute | solution.py:401
  51.6 0.8 copy-start.5
  52.3 0.8 copy-start.7
  53.1 0.8 copy-start.9
  53.8 0.8 copy-start.11
  55.4 7.2 %collective-permute-start.20 = (bf16[2,3,64,512]{3,2,1,0:T(8,128)(2,1)S(1)}, bf16[2,3,64,512]{3,2,1,0:T(8,128)(2,1)S(1)}, u32[]{:S(2)}, u32[]{:S(2)}) collective-permute-start(bf16[2,3,64,512]{3,2,1,0:T(8,128)(2,1)S(1)} %cut_columns.8.refs_2_), channel_id=1, source_target_pairs={{0,2},{4,6},{9,11},{13,15},{18,16},{22,20},{27,25},{31,29}} | collective-permute-start | bytes 1179656 | tf_op jit(solution)/shard_map/ppermute | solution.py:396
  58.4 6.2 %collective-permute-start.21 = (bf16[1,3,64,512]{3,2,1,0:T(8,128)(2,1)S(1)}, bf16[1,3,64,512]{3,2,1,0:T(8,128)(2,1)S(1)}, u32[]{:S(2)}, u32[]{:S(2)}) collective-permute-start(bf16[1,3,64,512]{3,2,1,0:T(8,128)(2,1)S(1)} %cut_columns.9.refs_4_), channel_id=1, source_target_pairs={{0,2},{4,6},{9,11},{13,15},{18,16},{22,20},{27,25},{31,29}} | collective-permute-start | bytes 589832 | tf_op jit(solution)/shard_map/ppermute | solution.py:396
  59.8 9.6 %copy-start.12 = (bf16[3,3,64,512]{3,2,1,0:T(8,128)(2,1)}, bf16[3,3,64,512]{3,2,1,0:T(8,128)(2,1)S(1)}, u32[]{:S(2)}) copy-start(bf16[3,3,64,512]{3,2,1,0:T(8,128)(2,1)S(1)} %collective-permute-done.18.refs_12_) | copy-start | bytes 1769476
  65.9 3.5 %collective-permute-start.22 = (bf16[5,3,64,512]{3,2,1,0:T(8,128)(2,1)S(1)}, bf16[5,3,64,512]{3,2,1,0:T(8,128)(2,1)S(1)}, u32[]{:S(2)}, u32[]{:S(2)}) collective-permute-start(bf16[5,3,64,512]{3,2,1,0:T(8,128)(2,1)S(1)} %pass_on.3.refs_13_), channel_id=1, source_target_pairs={{0,1},{4,5},{9,8},{13,12},{18,19},{22,23},{27,26},{31,30},{2,3},{6... | collective-permute-start | bytes 2949128 | tf_op jit(solution)/shard_map/ppermute | solution.py:401

commit v11 on v10

--- a/solution.py
+++ b/solution.py
@@ -129,10 +129,6 @@
         share[...] = cut[lax.bitwise_xor(me_ref[0], k)]
 
 
-def sum_kernel(*refs):
-    refs[-1][...] = sum(ref[...] for ref in refs[:-1])
-
-
 def cut_columns(half_ref, halves, cols_ref):
     for half in range(2):
 
@@ -187,7 +183,13 @@
         count = max(holder) + 1
         arrays.append(refs[:count])
         refs = refs[count:]
-    out_ref, left, right, done, col_sem, out_sem = refs
+    shares, refs = refs[:roles], refs[roles:]
+    out_ref, proj_ref, left, right, done, held, col_sem, out_sem, share_sem = refs
+    sums = [
+        pltpu.make_async_copy(part, held.at[k], share_sem.at[k]) for k, part in enumerate(shares)
+    ]
+    for copy in sums:
+        copy.start()
     depth = right.shape[1] // slots
     run = pieces[0].shape[1]
 
@@ -242,6 +244,9 @@
     for_each_group(False, load)
     assemble(0, 0)
     for_each_group(True, wait)
+    for copy in sums:
+        copy.wait()
+    proj_ref[...] = sum(held[k] for k in range(roles))
 
     def write(c, at, d):
         return pltpu.make_async_copy(
@@ -350,15 +355,6 @@
         name="project",
     )(me_a.astype(jnp.int32).reshape(1), flat, eigvecs)
     parts = [shares[0]] + [swap(shares[d], d) for d in range(1, atom_axis)]
-    projections = pl.pallas_call(
-        sum_kernel,
-        out_shape=share,
-        in_specs=[VMEM] * atom_axis,
-        out_specs=VMEM,
-        compiler_params=params(4),
-        name="sum_shares",
-    )(*parts)
-
     def pairs(source, target):
         return [
             (
@@ -369,6 +365,7 @@
         ]
 
     if blocks != 2 or frame_axis != 8:
+        projections = sum(parts)
         spread_pairs = [pairs(0, d) for d in range(1, atom_axis)]
         covariance = long_axis_covariance(
             flat, half[0], role[0], block, spread_pairs, 1.0 / total_frames
@@ -410,13 +407,13 @@
     one = hop(own, own)
     crossed = cross(kernel(cut_kernel, columns(1), half, [own], "cut_columns"))
     cut_one = kernel(cut_kernel, columns(2), half, list(one), "cut_columns")
-    two = hop(after(one[0], crossed[1]), one[1])
+    two = hop(after(one[0], crossed[1], *parts), one[1])
     in_hbm = pass_on(crossed + cross(cut_one), role)
     split = pltpu.VMEM(piece, jnp.bfloat16)
     cut_two, *pieces = kernel(
         cut_split_kernel,
         (columns(2),) + (split,) * 4,
-        after(half, *parts),
+        half,
         list(two),
         "cut_columns",
     )
@@ -428,7 +425,7 @@
     cut_three = kernel(
         cut_pieces_kernel,
         columns(2),
-        after(half, projections, in_hbm[0]),
+        after(half, in_hbm[1]),
         three,
         "cut_columns",
     )
@@ -442,22 +439,25 @@
     groups = ((3, True, (0, 1, 0, 1)), (5, False, (0, 1, 0, 1)))
     rows = [own, *one, *two, *three, *far]
     whole = 5
-    covariance = pl.pallas_call(
+    covariance, projections = pl.pallas_call(
         functools.partial(
             covariance_kernel, frame_axis, whole, atom_axis, groups, 1.0 / total_frames
         ),
-        out_shape=jax.ShapeDtypeStruct((3, 3, local_atoms, block), jnp.float32),
+        out_shape=(jax.ShapeDtypeStruct((3, 3, local_atoms, block), jnp.float32), share),
         in_specs=[SMEM]
         + [VMEM] * len(rows)
         + [HBM] * len(in_hbm)
-        + [VMEM] * len(in_vmem),
-        out_specs=ANY,
+        + [VMEM] * len(in_vmem)
+        + [HBM] * len(parts),
+        out_specs=(ANY, VMEM),
         scratch_shapes=[
             pltpu.VMEM((2, 2 * run, total_frames), jnp.bfloat16),
             pltpu.VMEM((3, total_frames, block), jnp.bfloat16),
             pltpu.VMEM((2, 3, 2 * run, block), jnp.float32),
+            pltpu.VMEM((atom_axis,) + share.shape, jnp.float32),
             pltpu.SemaphoreType.DMA((frame_axis,)),
             pltpu.SemaphoreType.DMA((2, 3)),
+            pltpu.SemaphoreType.DMA((atom_axis,)),
         ],
         compiler_params=params(16),
         cost_estimate=pl.CostEstimate(
@@ -471,6 +471,7 @@
         *[pinned(value, pltpu.VMEM) for value in rows],
         *[pinned(value, pltpu.HBM) for value in in_hbm],
         *[pinned(value, pltpu.VMEM) for value in in_vmem],
+        *[pinned(value, pltpu.HBM) for value in parts],
     )
     return jnp.transpose(covariance, (0, 2, 1, 3)), projections
 

time: 80 us -> 74.8 us (0.935)
  Pallas kernels: 17.6 us -> 12.8 us
  waiting for transfers between devices: 24.7 us -> 29.1 us
  local copies, waits for them, and re-layouts: 5.39 us -> 1.43 us
    ppermute x5, waiting for transfers between devices: 1.31 us -> 9.91 us  [hop(): lax.ppermute(down, 'frames', backward)]
    unnamed x26 -> x14, local copies, waits for them, and re-layouts: 5.39 us -> 1.43 us
    pallas_call x7, Pallas kernels: 4.91 us -> 0.98 us  [kernel(): pl.pallas_call(body, out_shape=out_shape, in_specs=[SMEM] + [VMEM] * len(...]
    ppermute x6, waiting for transfers between devices: 6.8 us -> 3.03 us  [swap(): lax.ppermute(value, 'atoms', [(a, a ^ distance) for a in range(atom_axis)])]
    ppermute x5, starting transfers between devices: 3.21 us -> 1.37 us  [hop(): lax.ppermute(up, 'frames', forward)]
    ppermute x5, starting transfers between devices: 7 us -> 8.69 us  [hop(): lax.ppermute(down, 'frames', backward)]
    ppermute x5, waiting for transfers between devices: 8.08 us -> 6.7 us  [cross(): return [cut, lax.ppermute(cut, axes, pairs(0, 2))]]
    ppermute x5, waiting for transfers between devices: 6.37 us -> 7.34 us  [hop(): lax.ppermute(up, 'frames', forward)]
  transfers between devices with their start and end apart: 23 -> 23, of which waited for: 12 -> 11; matrix products, arithmetic and copies ran while one was open for 0% -> 0% of each run, Pallas kernels for 6% -> 2%
where the time goes in v11:
time: 74.8 us; the launch traced here: 74.1 us
  starting transfers between devices  29.9 us (40%)
  waiting for transfers between devices  29.1 us (39%)
  Pallas kernels  12.8 us (17%)
  local copies, waits for them, and re-layouts  1.43 us (2%)
  between operations  0.92 us (1%)
    ppermute x5, starting transfers between devices, cross(): return [cut, lax.ppermute(cut, axes, pairs(0, 2))]  13.9 us
    ppermute x5, waiting for transfers between devices, hop(): lax.ppermute(down, 'frames', backward)  9.91 us
    pallas_call x1, Pallas kernels, per_device(): pl.pallas_call(functools.partial(covariance_kernel, frame_axis, whole, at...  9.11 us
    ppermute x5, starting transfers between devices, hop(): lax.ppermute(down, 'frames', backward)  8.69 us
    ppermute x5, waiting for transfers between devices, hop(): lax.ppermute(up, 'frames', forward)  7.34 us
    ppermute x5, waiting for transfers between devices, cross(): return [cut, lax.ppermute(cut, axes, pairs(0, 2))]  6.7 us
    ppermute x6, starting transfers between devices, swap(): lax.ppermute(value, 'atoms', [(a, a ^ distance) for a in range(atom_axis)])  3.27 us
    ppermute x6, waiting for transfers between devices, swap(): lax.ppermute(value, 'atoms', [(a, a ^ distance) for a in range(atom_axis)])  3.03 us
  transfers between devices with their start and end apart: 23, of which 11 were waited for; matrix products, arithmetic and copies ran while one was open for 0% of the time, Pallas kernels for 2%

profile of v11, /device:TPU:0, one launch (start us, length us, event | category | flops | bytes accessed | tf_op | source)
XLA Modules:
  0.0 74.1 jit_solution(16453845699079718935)
XLA Ops:
  0.6 1.7 %local_moments.1 = (f32[24,64]{1,0:T(8,128)S(1)}, f32[3,64,1024]{2,1,0:T(8,128)S(1)}, f32[3,1024]{1,0:T(4,128)S(1)}) custom-call(f32[3,64,1024]{2,1,0:T(8,128)} %bitcast.5, f32[3,1024]{1,0:T(4,128)} %ref_hbm.1), custom_call_target="tpu_custom_call" | custom-call | tf_op jit(solution)/shard_map/local_moments/pallas_call | solution.py:316
  2.3 2.4 %collective-permute-start.2 = (f32[24,64]{1,0:T(8,128)S(1)}, f32[24,64]{1,0:T(8,128)S(1)}, u32[]{:S(2)}, u32[]{:S(2)}) collective-permute-start(f32[24,64]{1,0:T(8,128)S(1)} %get-tuple-element.22.refs_0_), channel_id=1, source_target_pairs={{0,3},{1,2},{2,1},{3,0},{4,7},{5,6},{6,5},{7,4},{8,11},{9,10},{10,... | collective-permute-start | bytes 18440 | tf_op jit(solution)/shard_map/ppermute | solution.py:330
  4.7 0.6 collective-permute-start.1
  5.4 0.0 collective-permute-start
  5.4 0.7 collective-permute-done.2.refs_3_
  6.1 2.3 %collective-permute-done.1.refs_2_ = f32[24,64]{1,0:T(8,128)S(1)} collective-permute-done((f32[24,64]{1,0:T(8,128)S(1)}, f32[24,64]{1,0:T(8,128)S(1)}, u32[]{:S(2)}, u32[]{:S(2)}) %collective-permute-start.1) | collective-permute-done | bytes 6176 | tf_op jit(solution)/shard_map/ppermute | solution.py:330
  8.4 0.0 collective-permute-done.refs_1_
  8.4 0.6 polar_align.1
  9.0 1.6 %collective-permute-start.4 = (bf16[2,3,256,128]{3,2,1,0:T(8,128)(2,1)S(1)}, bf16[2,3,256,128]{3,2,1,0:T(8,128)(2,1)S(1)}, u32[]{:S(2)}, u32[]{:S(2)}) collective-permute-start(bf16[2,3,256,128]{3,2,1,0:T(8,128)(2,1)S(1)} %get-tuple-element.25.refs_0_), channel_id=1, source_target_pairs={{8,0},{16,8},{24,16},{28,24},{20,28},{12,20},{4,12},{0,4},{9,1},{1... | collective-permute-start | bytes 1179656 | tf_op jit(solution)/shard_map/ppermute | solution.py:405
  10.6 0.5 collective-permute-start.3
  11.1 0.1 cut_columns.5.refs_0_
  11.3 2.6 %collective-permute-start.5 = (bf16[1,3,64,512]{3,2,1,0:T(8,128)(2,1)S(1)}, bf16[1,3,64,512]{3,2,1,0:T(8,128)(2,1)S(1)}, u32[]{:S(2)}, u32[]{:S(2)}) collective-permute-start(bf16[1,3,64,512]{3,2,1,0:T(8,128)(2,1)S(1)} %cut_columns.5.refs_0_), channel_id=1, source_target_pairs={{0,2},{4,6},{9,11},{13,15},{18,16},{22,20},{27,25},{31,29}} | collective-permute-start | bytes 589832 | tf_op jit(solution)/shard_map/ppermute | solution.py:393
  13.8 0.0 copy-start
  13.8 1.4 %copy-done = bf16[3,1024,256]{2,1,0:T(8,128)(2,1)S(1)} copy-done((bf16[3,1024,256]{2,1,0:T(8,128)(2,1)S(1)}, bf16[3,1024,256]{2,1,0:T(8,128)(2,1)}, u32[]{:S(2)}) %copy-start) | copy-done | bytes 1572888
  15.2 0.5 project.1
  15.7 0.0 copy-start.2
  15.7 0.1 collective-permute-start.6
  15.8 0.1 collective-permute-start.7
  15.9 3.8 %collective-permute-done.4.refs_1_.refs_2_ = bf16[2,3,256,128]{3,2,1,0:T(8,128)(2,1)S(1)} collective-permute-done((bf16[2,3,256,128]{3,2,1,0:T(8,128)(2,1)S(1)}, bf16[2,3,256,128]{3,2,1,0:T(8,128)(2,1)S(1)}, u32[]{:S(2)}, u32[]{:S(2)}) %collective-permute-start.4) | collective-permute-done | bytes 393248 | tf_op jit(solution)/shard_map/ppermute | solution.py:405
  19.6 0.0 collective-permute-start.8
  19.6 1.2 %collective-permute-done.3.refs_0_.refs_1_ = bf16[2,3,256,128]{3,2,1,0:T(8,128)(2,1)S(1)} collective-permute-done((bf16[2,3,256,128]{3,2,1,0:T(8,128)(2,1)S(1)}, bf16[2,3,256,128]{3,2,1,0:T(8,128)(2,1)S(1)}, u32[]{:S(2)}, u32[]{:S(2)}) %collective-permute-start.3) | collective-permute-done | bytes 393248 | tf_op jit(solution)/shard_map/ppermute | solution.py:405
  20.9 0.2 cut_columns.7.refs_2_
  21.1 2.6 %collective-permute-start.17 = (bf16[2,3,64,512]{3,2,1,0:T(8,128)(2,1)S(1)}, bf16[2,3,64,512]{3,2,1,0:T(8,128)(2,1)S(1)}, u32[]{:S(2)}, u32[]{:S(2)}) collective-permute-start(bf16[2,3,64,512]{3,2,1,0:T(8,128)(2,1)S(1)} %cut_columns.7.refs_2_), channel_id=1, source_target_pairs={{0,2},{4,6},{9,11},{13,15},{18,16},{22,20},{27,25},{31,29}} | collective-permute-start | bytes 1179656 | tf_op jit(solution)/shard_map/ppermute | solution.py:393
  23.7 0.0 collective-permute-done.6.refs_16_
  23.7 0.0 copy-start.4
  23.7 0.0 collective-permute-done.7.refs_17_
  23.7 0.0 copy-start.5
  23.7 0.0 collective-permute-done.8.refs_18_
  23.8 0.0 copy-start.6
  23.8 0.0 collective-permute-done.5.refs_1_
  23.8 0.0 copy-done.2
  23.8 1.6 %collective-permute-start.10 = (bf16[2,3,256,128]{3,2,1,0:T(8,128)(2,1)S(1)}, bf16[2,3,256,128]{3,2,1,0:T(8,128)(2,1)S(1)}, u32[]{:S(2)}, u32[]{:S(2)}) collective-permute-start(bf16[2,3,256,128]{3,2,1,0:T(8,128)(2,1)S(1)} %collective-permute-done.4.refs_1_.refs_2_), channel_id=1, source_target_pairs={{8,0},{16,8},{24,16},{28,24},{20,28},{12,20},{4,12},{0,4},{9,1},{1... | collective-permute-start | bytes 1179656 | tf_op jit(solution)/shard_map/ppermute | solution.py:405
  25.4 0.5 collective-permute-start.9
  25.9 3.1 %collective-permute-done.17.refs_3_ = bf16[2,3,64,512]{3,2,1,0:T(8,128)(2,1)S(1)} collective-permute-done((bf16[2,3,64,512]{3,2,1,0:T(8,128)(2,1)S(1)}, bf16[2,3,64,512]{3,2,1,0:T(8,128)(2,1)S(1)}, u32[]{:S(2)}, u32[]{:S(2)}) %collective-permute-start.17) | collective-permute-done | bytes 393248 | tf_op jit(solution)/shard_map/ppermute | solution.py:393
  29.0 1.3 %collective-permute-start.18 = (bf16[3,3,64,512]{3,2,1,0:T(8,128)(2,1)S(1)}, bf16[3,3,64,512]{3,2,1,0:T(8,128)(2,1)S(1)}, u32[]{:S(2)}, u32[]{:S(2)}) collective-permute-start(bf16[3,3,64,512]{3,2,1,0:T(8,128)(2,1)S(1)} %pass_on.2.refs_11_), channel_id=1, source_target_pairs={{0,1},{4,5},{9,8},{13,12},{18,19},{22,23},{27,26},{31,30},{2,3},{6... | collective-permute-start | bytes 1769480 | tf_op jit(solution)/shard_map/ppermute | solution.py:398
  30.4 4.3 %collective-permute-done.10.down_ref.refs_4_ = bf16[2,3,256,128]{3,2,1,0:T(8,128)(2,1)S(1)} collective-permute-done((bf16[2,3,256,128]{3,2,1,0:T(8,128)(2,1)S(1)}, bf16[2,3,256,128]{3,2,1,0:T(8,128)(2,1)S(1)}, u32[]{:S(2)}, u32[]{:S(2)}) %collective-permute-start.10) | collective-permute-done | bytes 393248 | tf_op jit(solution)/shard_map/ppermute | solution.py:405
  34.6 1.2 %collective-permute-done.9.up_ref.refs_3_ = bf16[2,3,256,128]{3,2,1,0:T(8,128)(2,1)S(1)} collective-permute-done((bf16[2,3,256,128]{3,2,1,0:T(8,128)(2,1)S(1)}, bf16[2,3,256,128]{3,2,1,0:T(8,128)(2,1)S(1)}, u32[]{:S(2)}, u32[]{:S(2)}) %collective-permute-start.9) | collective-permute-done | bytes 393248 | tf_op jit(solution)/shard_map/ppermute | solution.py:405
  35.9 0.2 cut_columns.6
  36.1 2.3 %collective-permute-start.19 = (bf16[2,3,64,512]{3,2,1,0:T(8,128)(2,1)S(1)}, bf16[2,3,64,512]{3,2,1,0:T(8,128)(2,1)S(1)}, u32[]{:S(2)}, u32[]{:S(2)}) collective-permute-start(bf16[2,3,64,512]{3,2,1,0:T(8,128)(2,1)S(1)} %get-tuple-element.37.refs_0_), channel_id=1, source_target_pairs={{0,2},{4,6},{9,11},{13,15},{18,16},{22,20},{27,25},{31,29}} | collective-permute-start | bytes 1179656 | tf_op jit(solution)/shard_map/ppermute | solution.py:393
  38.4 0.1 collective-permute-start.11
  38.5 2.0 %collective-permute-start.14 = (bf16[3,256,128]{2,1,0:T(8,128)(2,1)S(1)}, bf16[3,256,128]{2,1,0:T(8,128)(2,1)S(1)}, u32[]{:S(2)}, u32[]{:S(2)}) collective-permute-start(bf16[3,256,128]{2,1,0:T(8,128)(2,1)S(1)} %get-tuple-element.35), channel_id=1, source_target_pairs={{8,0},{16,8},{24,16},{28,24},{20,28},{12,20},{4,12},{0,4},{9,1},{1... | collective-permute-start | bytes 589832 | tf_op jit(solution)/shard_map/ppermute | solution.py:405
  40.5 0.1 collective-permute-start.12
  40.5 4.9 %collective-permute-done.11.refs_0_.refs_5_ = bf16[3,256,128]{2,1,0:T(8,128)(2,1)S(1)} collective-permute-done((bf16[3,256,128]{2,1,0:T(8,128)(2,1)S(1)}, bf16[3,256,128]{2,1,0:T(8,128)(2,1)S(1)}, u32[]{:S(2)}, u32[]{:S(2)}) %collective-permute-start.11) | collective-permute-done | bytes 196640 | tf_op jit(solution)/shard_map/ppermute | solution.py:405
  45.4 1.7 %collective-permute-start.13 = (bf16[3,256,128]{2,1,0:T(8,128)(2,1)S(1)}, bf16[3,256,128]{2,1,0:T(8,128)(2,1)S(1)}, u32[]{:S(2)}, u32[]{:S(2)}) collective-permute-start(bf16[3,256,128]{2,1,0:T(8,128)(2,1)S(1)} %get-tuple-element.34), channel_id=1, source_target_pairs={{8,0},{16,8},{24,16},{28,24},{20,28},{12,20},{4,12},{0,4},{9,1},{1... | collective-permute-start | bytes 589832 | tf_op jit(solution)/shard_map/ppermute | solution.py:405
  47.2 0.0 collective-permute-done.14.refs_3_.refs_8_
  47.2 0.3 collective-permute-start.15
  47.4 0.0 collective-permute-done.19.refs_1_
  47.5 1.7 %collective-permute-start.16 = (bf16[3,256,128]{2,1,0:T(8,128)(2,1)S(1)}, bf16[3,256,128]{2,1,0:T(8,128)(2,1)S(1)}, u32[]{:S(2)}, u32[]{:S(2)}) collective-permute-start(bf16[3,256,128]{2,1,0:T(8,128)(2,1)S(1)} %collective-permute-done.14.refs_3_.refs_8_), channel_id=1, source_target_pairs={{8,0},{16,8},{24,16},{28,24},{20,28},{12,20},{4,12},{0,4},{9,1},{1... | collective-permute-start | bytes 589832 | tf_op jit(solution)/shard_map/ppermute | solution.py:405
  49.2 0.0 collective-permute-done.18.refs_12_
  49.2 0.0 collective-permute-done.12.refs_1_.refs_6_
  49.2 1.9 %collective-permute-done.13.refs_2_.refs_7_ = bf16[3,256,128]{2,1,0:T(8,128)(2,1)S(1)} collective-permute-done((bf16[3,256,128]{2,1,0:T(8,128)(2,1)S(1)}, bf16[3,256,128]{2,1,0:T(8,128)(2,1)S(1)}, u32[]{:S(2)}, u32[]{:S(2)}) %collective-permute-start.13) | collective-permute-done | bytes 196640 | tf_op jit(solution)/shard_map/ppermute | solution.py:405
  51.1 0.2 cut_columns.8.refs_2_
  51.3 2.8 %collective-permute-start.20 = (bf16[2,3,64,512]{3,2,1,0:T(8,128)(2,1)S(1)}, bf16[2,3,64,512]{3,2,1,0:T(8,128)(2,1)S(1)}, u32[]{:S(2)}, u32[]{:S(2)}) collective-permute-start(bf16[2,3,64,512]{3,2,1,0:T(8,128)(2,1)S(1)} %cut_columns.8.refs_2_), channel_id=1, source_target_pairs={{0,2},{4,6},{9,11},{13,15},{18,16},{22,20},{27,25},{31,29}} | collective-permute-start | bytes 1179656 | tf_op jit(solution)/shard_map/ppermute | solution.py:393
  54.1 0.0 collective-permute-done.15.refs_0_.refs_9_
  54.1 0.0 collective-permute-done.16.refs_1_.refs_10_
  54.1 0.1 cut_columns.9.refs_4_
  54.2 3.6 %collective-permute-start.21 = (bf16[1,3,64,512]{3,2,1,0:T(8,128)(2,1)S(1)}, bf16[1,3,64,512]{3,2,1,0:T(8,128)(2,1)S(1)}, u32[]{:S(2)}, u32[]{:S(2)}) collective-permute-start(bf16[1,3,64,512]{3,2,1,0:T(8,128)(2,1)S(1)} %cut_columns.9.refs_4_), channel_id=1, source_target_pairs={{0,2},{4,6},{9,11},{13,15},{18,16},{22,20},{27,25},{31,29}} | collective-permute-start | bytes 589832 | tf_op jit(solution)/shard_map/ppermute | solution.py:393
  57.8 3.6 %collective-permute-done.21.refs_5_ = bf16[1,3,64,512]{3,2,1,0:T(8,128)(2,1)S(1)} collective-permute-done((bf16[1,3,64,512]{3,2,1,0:T(8,128)(2,1)S(1)}, bf16[1,3,64,512]{3,2,1,0:T(8,128)(2,1)S(1)}, u32[]{:S(2)}, u32[]{:S(2)}) %collective-permute-start.21) | collective-permute-done | bytes 196640 | tf_op jit(solution)/shard_map/ppermute | solution.py:393
  61.4 0.0 collective-permute-done.20.refs_3_
  61.4 0.1 pass_on.3.refs_13_
  61.5 1.4 %collective-permute-start.22 = (bf16[5,3,64,512]{3,2,1,0:T(8,128)(2,1)S(1)}, bf16[5,3,64,512]{3,2,1,0:T(8,128)(2,1)S(1)}, u32[]{:S(2)}, u32[]{:S(2)}) collective-permute-start(bf16[5,3,64,512]{3,2,1,0:T(8,128)(2,1)S(1)} %pass_on.3.refs_13_), channel_id=1, source_target_pairs={{0,1},{4,5},{9,8},{13,12},{18,19},{22,23},{27,26},{31,30},{2,3},{6... | collective-permute-start | bytes 2949128 | tf_op jit(solution)/shard_map/ppermute | solution.py:398
  62.9 2.1 %collective-permute-done.22.refs_14_ = bf16[5,3,64,512]{3,2,1,0:T(8,128)(2,1)S(1)} collective-permute-done((bf16[5,3,64,512]{3,2,1,0:T(8,128)(2,1)S(1)}, bf16[5,3,64,512]{3,2,1,0:T(8,128)(2,1)S(1)}, u32[]{:S(2)}, u32[]{:S(2)}) %collective-permute-start.22) | collective-permute-done | bytes 983072 | tf_op jit(solution)/shard_map/ppermute | solution.py:398
  65.0 0.0 copy-done.6
  65.0 9.1 %covariance_tile.1 = (f32[3,3,1024,512]{3,2,1,0:T(8,128)}, f32[64,64]{1,0:T(8,128)}) custom-call(s32[1]{0:T(128)} %bitcast.role_ref, bf16[2,3,256,128]{3,2,1,0:T(8,128)(2,1)S(1)} %get-tuple-element.25.refs_0_, bf16[2,3,256,128]{3,2,1,0:T(8,128)(2,1)S(1)} %collective-permute-done.3.refs_0_.refs_1_, ...), custom_call_target="tpu_custom_call" | custom-call | flops 4831838208 | bytes 25165824 | tf_op jit(solution)/shard_map/covariance_tile/pallas_call | solution.py:442
  (7 shorter events, 0.1 us)
Async XLA Ops:
  2.3 3.8 %collective-permute-start.2 = (f32[24,64]{1,0:T(8,128)S(1)}, f32[24,64]{1,0:T(8,128)S(1)}, u32[]{:S(2)}, u32[]{:S(2)}) collective-permute-start(f32[24,64]{1,0:T(8,128)S(1)} %get-tuple-element.22.refs_0_), channel_id=1, source_target_pairs={{0,3},{1,2},{2,1},{3,0},{4,7},{5,6},{6,5},{7,4},{8,11},{9,10},{10,... | collective-permute-start | bytes 18440 | tf_op jit(solution)/shard_map/ppermute | solution.py:330
  4.7 3.7 %collective-permute-start.1 = (f32[24,64]{1,0:T(8,128)S(1)}, f32[24,64]{1,0:T(8,128)S(1)}, u32[]{:S(2)}, u32[]{:S(2)}) collective-permute-start(f32[24,64]{1,0:T(8,128)S(1)} %get-tuple-element.22.refs_0_), channel_id=1, source_target_pairs={{0,2},{1,3},{2,0},{3,1},{4,6},{5,7},{6,4},{7,5},{8,10},{9,11},{10,... | collective-permute-start | bytes 18440 | tf_op jit(solution)/shard_map/ppermute | solution.py:330
  5.4 3.1 %collective-permute-start = (f32[24,64]{1,0:T(8,128)S(1)}, f32[24,64]{1,0:T(8,128)S(1)}, u32[]{:S(2)}, u32[]{:S(2)}) collective-permute-start(f32[24,64]{1,0:T(8,128)S(1)} %get-tuple-element.22.refs_0_), channel_id=1, source_target_pairs={{0,1},{1,0},{2,3},{3,2},{4,5},{5,4},{6,7},{7,6},{8,9},{9,8},{10,11... | collective-permute-start | bytes 18440 | tf_op jit(solution)/shard_map/ppermute | solution.py:330
  9.0 10.6 %collective-permute-start.4 = (bf16[2,3,256,128]{3,2,1,0:T(8,128)(2,1)S(1)}, bf16[2,3,256,128]{3,2,1,0:T(8,128)(2,1)S(1)}, u32[]{:S(2)}, u32[]{:S(2)}) collective-permute-start(bf16[2,3,256,128]{3,2,1,0:T(8,128)(2,1)S(1)} %get-tuple-element.25.refs_0_), channel_id=1, source_target_pairs={{8,0},{16,8},{24,16},{28,24},{20,28},{12,20},{4,12},{0,4},{9,1},{1... | collective-permute-start | bytes 1179656 | tf_op jit(solution)/shard_map/ppermute | solution.py:405
  10.6 10.3 %collective-permute-start.3 = (bf16[2,3,256,128]{3,2,1,0:T(8,128)(2,1)S(1)}, bf16[2,3,256,128]{3,2,1,0:T(8,128)(2,1)S(1)}, u32[]{:S(2)}, u32[]{:S(2)}) collective-permute-start(bf16[2,3,256,128]{3,2,1,0:T(8,128)(2,1)S(1)} %get-tuple-element.25.refs_0_), channel_id=1, source_target_pairs={{0,8},{8,16},{16,24},{24,28},{28,20},{20,12},{12,4},{4,0},{1,9},{9... | collective-permute-start | bytes 1179656 | tf_op jit(solution)/shard_map/ppermute | solution.py:405
  11.3 12.5 %collective-permute-start.5 = (bf16[1,3,64,512]{3,2,1,0:T(8,128)(2,1)S(1)}, bf16[1,3,64,512]{3,2,1,0:T(8,128)(2,1)S(1)}, u32[]{:S(2)}, u32[]{:S(2)}) collective-permute-start(bf16[1,3,64,512]{3,2,1,0:T(8,128)(2,1)S(1)} %cut_columns.5.refs_0_), channel_id=1, source_target_pairs={{0,2},{4,6},{9,11},{13,15},{18,16},{22,20},{27,25},{31,29}} | collective-permute-start | bytes 589832 | tf_op jit(solution)/shard_map/ppermute | solution.py:393
  13.8 1.4 %copy-start = (bf16[3,1024,256]{2,1,0:T(8,128)(2,1)S(1)}, bf16[3,1024,256]{2,1,0:T(8,128)(2,1)}, u32[]{:S(2)}) copy-start(bf16[3,1024,256]{2,1,0:T(8,128)(2,1)} %eig_ref.1) | copy-start | bytes 4718596
  15.7 8.0 %copy-start.2 = (f32[64,64]{1,0:T(8,128)}, f32[64,64]{1,0:T(8,128)S(1)}, u32[]{:S(2)}) copy-start(f32[64,64]{1,0:T(8,128)S(1)} %get-tuple-element.27.refs_15_) | copy-start | bytes 49156
  15.7 8.0 %collective-permute-start.6 = (f32[64,64]{1,0:T(8,128)S(1)}, f32[64,64]{1,0:T(8,128)S(1)}, u32[]{:S(2)}, u32[]{:S(2)}) collective-permute-start(f32[64,64]{1,0:T(8,128)S(1)} %get-tuple-element.28), channel_id=1, source_target_pairs={{0,1},{1,0},{2,3},{3,2},{4,5},{5,4},{6,7},{7,6},{8,9},{9,8},{10,11... | collective-permute-start | bytes 49160 | tf_op jit(solution)/shard_map/ppermute | solution.py:330
  15.8 7.9 %collective-permute-start.7 = (f32[64,64]{1,0:T(8,128)S(1)}, f32[64,64]{1,0:T(8,128)S(1)}, u32[]{:S(2)}, u32[]{:S(2)}) collective-permute-start(f32[64,64]{1,0:T(8,128)S(1)} %get-tuple-element.29), channel_id=1, source_target_pairs={{0,2},{1,3},{2,0},{3,1},{4,6},{5,7},{6,4},{7,5},{8,10},{9,11},{10,... | collective-permute-start | bytes 49160 | tf_op jit(solution)/shard_map/ppermute | solution.py:330
  19.6 4.1 %collective-permute-start.8 = (f32[64,64]{1,0:T(8,128)S(1)}, f32[64,64]{1,0:T(8,128)S(1)}, u32[]{:S(2)}, u32[]{:S(2)}) collective-permute-start(f32[64,64]{1,0:T(8,128)S(1)} %get-tuple-element.30), channel_id=1, source_target_pairs={{0,3},{1,2},{2,1},{3,0},{4,7},{5,6},{6,5},{7,4},{8,11},{9,10},{10,... | collective-permute-start | bytes 49160 | tf_op jit(solution)/shard_map/ppermute | solution.py:330
  21.1 7.9 %collective-permute-start.17 = (bf16[2,3,64,512]{3,2,1,0:T(8,128)(2,1)S(1)}, bf16[2,3,64,512]{3,2,1,0:T(8,128)(2,1)S(1)}, u32[]{:S(2)}, u32[]{:S(2)}) collective-permute-start(bf16[2,3,64,512]{3,2,1,0:T(8,128)(2,1)S(1)} %cut_columns.7.refs_2_), channel_id=1, source_target_pairs={{0,2},{4,6},{9,11},{13,15},{18,16},{22,20},{27,25},{31,29}} | collective-permute-start | bytes 1179656 | tf_op jit(solution)/shard_map/ppermute | solution.py:393
  23.7 41.3 %copy-start.4 = (f32[64,64]{1,0:T(8,128)}, f32[64,64]{1,0:T(8,128)S(1)}, u32[]{:S(2)}) copy-start(f32[64,64]{1,0:T(8,128)S(1)} %collective-permute-done.6.refs_16_) | copy-start | bytes 49156
  23.7 41.3 %copy-start.5 = (f32[64,64]{1,0:T(8,128)}, f32[64,64]{1,0:T(8,128)S(1)}, u32[]{:S(2)}) copy-start(f32[64,64]{1,0:T(8,128)S(1)} %collective-permute-done.7.refs_17_) | copy-start | bytes 49156
  23.8 41.2 %copy-start.6 = (f32[64,64]{1,0:T(8,128)}, f32[64,64]{1,0:T(8,128)S(1)}, u32[]{:S(2)}) copy-start(f32[64,64]{1,0:T(8,128)S(1)} %collective-permute-done.8.refs_18_) | copy-start | bytes 49156
  23.8 10.8 %collective-permute-start.10 = (bf16[2,3,256,128]{3,2,1,0:T(8,128)(2,1)S(1)}, bf16[2,3,256,128]{3,2,1,0:T(8,128)(2,1)S(1)}, u32[]{:S(2)}, u32[]{:S(2)}) collective-permute-start(bf16[2,3,256,128]{3,2,1,0:T(8,128)(2,1)S(1)} %collective-permute-done.4.refs_1_.refs_2_), channel_id=1, source_target_pairs={{8,0},{16,8},{24,16},{28,24},{20,28},{12,20},{4,12},{0,4},{9,1},{1... | collective-permute-start | bytes 1179656 | tf_op jit(solution)/shard_map/ppermute | solution.py:405
  25.4 10.4 %collective-permute-start.9 = (bf16[2,3,256,128]{3,2,1,0:T(8,128)(2,1)S(1)}, bf16[2,3,256,128]{3,2,1,0:T(8,128)(2,1)S(1)}, u32[]{:S(2)}, u32[]{:S(2)}) collective-permute-start(bf16[2,3,256,128]{3,2,1,0:T(8,128)(2,1)S(1)} %collective-permute-done.3.refs_0_.refs_1_), channel_id=1, source_target_pairs={{0,8},{8,16},{16,24},{24,28},{28,20},{20,12},{12,4},{4,0},{1,9},{9... | collective-permute-start | bytes 1179656 | tf_op jit(solution)/shard_map/ppermute | solution.py:405
  29.0 36.0 %copy-start.1 = (bf16[3,3,64,512]{3,2,1,0:T(8,128)(2,1)}, bf16[3,3,64,512]{3,2,1,0:T(8,128)(2,1)S(1)}, u32[]{:S(2)}) copy-start(bf16[3,3,64,512]{3,2,1,0:T(8,128)(2,1)S(1)} %pass_on.2.refs_11_) | copy-start | bytes 1769476
  29.0 20.2 %collective-permute-start.18 = (bf16[3,3,64,512]{3,2,1,0:T(8,128)(2,1)S(1)}, bf16[3,3,64,512]{3,2,1,0:T(8,128)(2,1)S(1)}, u32[]{:S(2)}, u32[]{:S(2)}) collective-permute-start(bf16[3,3,64,512]{3,2,1,0:T(8,128)(2,1)S(1)} %pass_on.2.refs_11_), channel_id=1, source_target_pairs={{0,1},{4,5},{9,8},{13,12},{18,19},{22,23},{27,26},{31,30},{2,3},{6... | collective-permute-start | bytes 1769480 | tf_op jit(solution)/shard_map/ppermute | solution.py:398
  36.1 11.4 %collective-permute-start.19 = (bf16[2,3,64,512]{3,2,1,0:T(8,128)(2,1)S(1)}, bf16[2,3,64,512]{3,2,1,0:T(8,128)(2,1)S(1)}, u32[]{:S(2)}, u32[]{:S(2)}) collective-permute-start(bf16[2,3,64,512]{3,2,1,0:T(8,128)(2,1)S(1)} %get-tuple-element.37.refs_0_), channel_id=1, source_target_pairs={{0,2},{4,6},{9,11},{13,15},{18,16},{22,20},{27,25},{31,29}} | collective-permute-start | bytes 1179656 | tf_op jit(solution)/shard_map/ppermute | solution.py:393
  38.4 7.0 %collective-permute-start.11 = (bf16[3,256,128]{2,1,0:T(8,128)(2,1)S(1)}, bf16[3,256,128]{2,1,0:T(8,128)(2,1)S(1)}, u32[]{:S(2)}, u32[]{:S(2)}) collective-permute-start(bf16[3,256,128]{2,1,0:T(8,128)(2,1)S(1)} %get-tuple-element.32), channel_id=1, source_target_pairs={{0,8},{8,16},{16,24},{24,28},{28,20},{20,12},{12,4},{4,0},{1,9},{9... | collective-permute-start | bytes 589832 | tf_op jit(solution)/shard_map/ppermute | solution.py:405
  38.5 8.7 %collective-permute-start.14 = (bf16[3,256,128]{2,1,0:T(8,128)(2,1)S(1)}, bf16[3,256,128]{2,1,0:T(8,128)(2,1)S(1)}, u32[]{:S(2)}, u32[]{:S(2)}) collective-permute-start(bf16[3,256,128]{2,1,0:T(8,128)(2,1)S(1)} %get-tuple-element.35), channel_id=1, source_target_pairs={{8,0},{16,8},{24,16},{28,24},{20,28},{12,20},{4,12},{0,4},{9,1},{1... | collective-permute-start | bytes 589832 | tf_op jit(solution)/shard_map/ppermute | solution.py:405
  40.5 8.7 %collective-permute-start.12 = (bf16[3,256,128]{2,1,0:T(8,128)(2,1)S(1)}, bf16[3,256,128]{2,1,0:T(8,128)(2,1)S(1)}, u32[]{:S(2)}, u32[]{:S(2)}) collective-permute-start(bf16[3,256,128]{2,1,0:T(8,128)(2,1)S(1)} %get-tuple-element.33), channel_id=1, source_target_pairs={{0,8},{8,16},{16,24},{24,28},{28,20},{20,12},{12,4},{4,0},{1,9},{9... | collective-permute-start | bytes 589832 | tf_op jit(solution)/shard_map/ppermute | solution.py:405
  45.4 5.7 %collective-permute-start.13 = (bf16[3,256,128]{2,1,0:T(8,128)(2,1)S(1)}, bf16[3,256,128]{2,1,0:T(8,128)(2,1)S(1)}, u32[]{:S(2)}, u32[]{:S(2)}) collective-permute-start(bf16[3,256,128]{2,1,0:T(8,128)(2,1)S(1)} %get-tuple-element.34), channel_id=1, source_target_pairs={{8,0},{16,8},{24,16},{28,24},{20,28},{12,20},{4,12},{0,4},{9,1},{1... | collective-permute-start | bytes 589832 | tf_op jit(solution)/shard_map/ppermute | solution.py:405
  47.2 6.9 %collective-permute-start.15 = (bf16[3,256,128]{2,1,0:T(8,128)(2,1)S(1)}, bf16[3,256,128]{2,1,0:T(8,128)(2,1)S(1)}, u32[]{:S(2)}, u32[]{:S(2)}) collective-permute-start(bf16[3,256,128]{2,1,0:T(8,128)(2,1)S(1)} %collective-permute-done.11.refs_0_.refs_5_), channel_id=1, source_target_pairs={{0,8},{8,16},{16,24},{24,28},{28,20},{20,12},{12,4},{4,0},{1,9},{9... | collective-permute-start | bytes 589832 | tf_op jit(solution)/shard_map/ppermute | solution.py:405
  47.5 6.6 %collective-permute-start.16 = (bf16[3,256,128]{2,1,0:T(8,128)(2,1)S(1)}, bf16[3,256,128]{2,1,0:T(8,128)(2,1)S(1)}, u32[]{:S(2)}, u32[]{:S(2)}) collective-permute-start(bf16[3,256,128]{2,1,0:T(8,128)(2,1)S(1)} %collective-permute-done.14.refs_3_.refs_8_), channel_id=1, source_target_pairs={{8,0},{16,8},{24,16},{28,24},{20,28},{12,20},{4,12},{0,4},{9,1},{1... | collective-permute-start | bytes 589832 | tf_op jit(solution)/shard_map/ppermute | solution.py:405
  49.2 15.8 %copy-start.3 = (bf16[3,3,64,512]{3,2,1,0:T(8,128)(2,1)}, bf16[3,3,64,512]{3,2,1,0:T(8,128)(2,1)S(1)}, u32[]{:S(2)}) copy-start(bf16[3,3,64,512]{3,2,1,0:T(8,128)(2,1)S(1)} %collective-permute-done.18.refs_12_) | copy-start | bytes 1769476
  51.3 10.2 %collective-permute-start.20 = (bf16[2,3,64,512]{3,2,1,0:T(8,128)(2,1)S(1)}, bf16[2,3,64,512]{3,2,1,0:T(8,128)(2,1)S(1)}, u32[]{:S(2)}, u32[]{:S(2)}) collective-permute-start(bf16[2,3,64,512]{3,2,1,0:T(8,128)(2,1)S(1)} %cut_columns.8.refs_2_), channel_id=1, source_target_pairs={{0,2},{4,6},{9,11},{13,15},{18,16},{22,20},{27,25},{31,29}} | collective-permute-start | bytes 1179656 | tf_op jit(solution)/shard_map/ppermute | solution.py:393
  54.2 7.2 %collective-permute-start.21 = (bf16[1,3,64,512]{3,2,1,0:T(8,128)(2,1)S(1)}, bf16[1,3,64,512]{3,2,1,0:T(8,128)(2,1)S(1)}, u32[]{:S(2)}, u32[]{:S(2)}) collective-permute-start(bf16[1,3,64,512]{3,2,1,0:T(8,128)(2,1)S(1)} %cut_columns.9.refs_4_), channel_id=1, source_target_pairs={{0,2},{4,6},{9,11},{13,15},{18,16},{22,20},{27,25},{31,29}} | collective-permute-start | bytes 589832 | tf_op jit(solution)/shard_map/ppermute | solution.py:393
  61.5 3.5 %collective-permute-start.22 = (bf16[5,3,64,512]{3,2,1,0:T(8,128)(2,1)S(1)}, bf16[5,3,64,512]{3,2,1,0:T(8,128)(2,1)S(1)}, u32[]{:S(2)}, u32[]{:S(2)}) collective-permute-start(bf16[5,3,64,512]{3,2,1,0:T(8,128)(2,1)S(1)} %pass_on.3.refs_13_), channel_id=1, source_target_pairs={{0,1},{4,5},{9,8},{13,12},{18,19},{22,23},{27,26},{31,30},{2,3},{6... | collective-permute-start | bytes 2949128 | tf_op jit(solution)/shard_map/ppermute | solution.py:398

commit v12 on v11

--- a/solution.py
+++ b/solution.py
@@ -406,37 +406,30 @@
 
     one = hop(own, own)
     crossed = cross(kernel(cut_kernel, columns(1), half, [own], "cut_columns"))
+    in_hbm = pass_on(crossed, role)
     cut_one = kernel(cut_kernel, columns(2), half, list(one), "cut_columns")
-    two = hop(after(one[0], crossed[1], *parts), one[1])
-    in_hbm = pass_on(crossed + cross(cut_one), role)
+    two = hop(after(one[0], crossed[1]), one[1])
+    crossed = cross(cut_one)
     split = pltpu.VMEM(piece, jnp.bfloat16)
     cut_two, *pieces = kernel(
         cut_split_kernel,
         (columns(2),) + (split,) * 4,
-        half,
+        after(half, in_hbm[1], *parts),
         list(two),
         "cut_columns",
     )
-    crossed = cross(cut_two)
+    crossed += cross(cut_two)
     up_a, down_b = hop(pieces[0], pieces[3])
     up_b, down_a = hop(pieces[1], pieces[2])
     far = hop(up_a, down_b)
     three = [up_a, up_b, down_a, down_b]
-    cut_three = kernel(
-        cut_pieces_kernel,
-        columns(2),
-        after(half, in_hbm[1]),
-        three,
-        "cut_columns",
-    )
+    cut_three = kernel(cut_pieces_kernel, columns(2), after(half, crossed[1]), three, "cut_columns")
     long = pl.CostEstimate(flops=LONG, bytes_accessed=0, transcendentals=0)
     cut_four = kernel(
-        cut_pieces_kernel, columns(1), after(half, crossed[1]), list(far), "cut_columns", long
-    )
-    in_vmem = pass_on(
-        crossed + cross(cut_three) + cross(cut_four), after(role, in_hbm[1])
-    )
-    groups = ((3, True, (0, 1, 0, 1)), (5, False, (0, 1, 0, 1)))
+        cut_pieces_kernel, columns(1), half, list(far), "cut_columns", long
+    )
+    in_vmem = pass_on(crossed + cross(cut_three) + cross(cut_four), role)
+    groups = ((1, True, (0, 1, 0, 1)), (7, False, (0, 1, 0, 1)))
     rows = [own, *one, *two, *three, *far]
     whole = 5
     covariance, projections = pl.pallas_call(

time: 74.8 us -> 73.1 us (0.977)
  waiting for transfers between devices: 29.1 us -> 24.4 us
  Pallas kernels: 12.8 us -> 14.8 us
  starting transfers between devices: 29.9 us -> 30.7 us
    ppermute x5, waiting for transfers between devices: 9.91 us -> 2.26 us  [hop(): lax.ppermute(down, 'frames', backward)]
    ppermute x5, starting transfers between devices: 1.37 us -> 5.8 us  [hop(): lax.ppermute(up, 'frames', forward)]
    ppermute x5, starting transfers between devices: 8.69 us -> 4.77 us  [hop(): lax.ppermute(down, 'frames', backward)]
    ppermute x6, waiting for transfers between devices: 3.03 us -> 5.38 us  [swap(): lax.ppermute(value, 'atoms', [(a, a ^ distance) for a in range(atom_axis)])]
    ppermute x5, waiting for transfers between devices: 6.7 us -> 8.06 us  [cross(): return [cut, lax.ppermute(cut, axes, pairs(0, 2))]]
    ppermute x6, starting transfers between devices: 3.27 us -> 4.61 us  [swap(): lax.ppermute(value, 'atoms', [(a, a ^ distance) for a in range(atom_axis)])]
    ppermute x5, waiting for transfers between devices: 7.34 us -> 6.04 us  [hop(): lax.ppermute(up, 'frames', forward)]
    pallas_call x7, Pallas kernels: 0.98 us -> 2.03 us  [kernel(): pl.pallas_call(body, out_shape=out_shape, in_specs=[SMEM] + [VMEM] * len(...]
  transfers between devices with their start and end apart: 23 -> 23, of which waited for: 11 -> 12; matrix products, arithmetic and copies ran while one was open for 0% -> 0% of each run, Pallas kernels for 2% -> 3%
where the time goes in v12:
time: 73.1 us; the launch traced here: 72.6 us
  starting transfers between devices  30.7 us (42%)
  waiting for transfers between devices  24.4 us (33%)
  Pallas kernels  14.8 us (20%)
  local copies, waits for them, and re-layouts  1.76 us (2%)
  between operations  0.95 us (1%)
    ppermute x5, starting transfers between devices, cross(): return [cut, lax.ppermute(cut, axes, pairs(0, 2))]  12.8 us
    pallas_call x1, Pallas kernels, per_device(): pl.pallas_call(functools.partial(covariance_kernel, frame_axis, whole, at...  9.93 us
    ppermute x5, waiting for transfers between devices, cross(): return [cut, lax.ppermute(cut, axes, pairs(0, 2))]  8.06 us
    ppermute x5, waiting for transfers between devices, hop(): lax.ppermute(up, 'frames', forward)  6.04 us
    ppermute x5, starting transfers between devices, hop(): lax.ppermute(up, 'frames', forward)  5.8 us
    ppermute x6, waiting for transfers between devices, swap(): lax.ppermute(value, 'atoms', [(a, a ^ distance) for a in range(atom_axis)])  5.38 us
    ppermute x5, starting transfers between devices, hop(): lax.ppermute(down, 'frames', backward)  4.77 us
    ppermute x6, starting transfers between devices, swap(): lax.ppermute(value, 'atoms', [(a, a ^ distance) for a in range(atom_axis)])  4.61 us
  transfers between devices with their start and end apart: 23, of which 12 were waited for; matrix products, arithmetic and copies ran while one was open for 0% of the time, Pallas kernels for 3%

profile of v12, /device:TPU:0, one launch (start us, length us, event | category | flops | bytes accessed | tf_op | source)
XLA Modules:
  0.0 72.6 jit_solution(5674113162708847936)
XLA Ops:
  0.6 1.8 %local_moments.1 = (f32[24,64]{1,0:T(8,128)S(1)}, f32[3,64,1024]{2,1,0:T(8,128)S(1)}, f32[3,1024]{1,0:T(4,128)S(1)}) custom-call(f32[3,64,1024]{2,1,0:T(8,128)} %bitcast.5, f32[3,1024]{1,0:T(4,128)} %ref_hbm.1), custom_call_target="tpu_custom_call" | custom-call | tf_op jit(solution)/shard_map/local_moments/pallas_call | solution.py:316
  2.4 2.4 %collective-permute-start.2 = (f32[24,64]{1,0:T(8,128)S(1)}, f32[24,64]{1,0:T(8,128)S(1)}, u32[]{:S(2)}, u32[]{:S(2)}) collective-permute-start(f32[24,64]{1,0:T(8,128)S(1)} %get-tuple-element.21.refs_0_), channel_id=1, source_target_pairs={{0,3},{1,2},{2,1},{3,0},{4,7},{5,6},{6,5},{7,4},{8,11},{9,10},{10,... | collective-permute-start | bytes 18440 | tf_op jit(solution)/shard_map/ppermute | solution.py:330
  4.9 0.6 collective-permute-start.1
  5.5 0.0 collective-permute-start
  5.5 0.7 collective-permute-done.2.refs_3_
  6.3 2.3 %collective-permute-done.1.refs_2_ = f32[24,64]{1,0:T(8,128)S(1)} collective-permute-done((f32[24,64]{1,0:T(8,128)S(1)}, f32[24,64]{1,0:T(8,128)S(1)}, u32[]{:S(2)}, u32[]{:S(2)}) %collective-permute-start.1) | collective-permute-done | bytes 6176 | tf_op jit(solution)/shard_map/ppermute | solution.py:330
  8.6 0.0 collective-permute-done.refs_1_
  8.6 0.6 polar_align.1
  9.2 0.0 copy-start.1
  9.2 0.7 %copy-done.1 = bf16[3,64,1024]{2,1,0:T(8,128)(2,1)} copy-done((bf16[3,64,1024]{2,1,0:T(8,128)(2,1)}, bf16[3,64,1024]{2,1,0:T(8,128)(2,1)S(1)}, u32[]{:S(2)}) %copy-start.1) | copy-done | bytes 393240
  9.9 1.6 %collective-permute-start.3 = (bf16[2,3,256,128]{3,2,1,0:T(8,128)(2,1)S(1)}, bf16[2,3,256,128]{3,2,1,0:T(8,128)(2,1)S(1)}, u32[]{:S(2)}, u32[]{:S(2)}) collective-permute-start(bf16[2,3,256,128]{3,2,1,0:T(8,128)(2,1)S(1)} %get-tuple-element.24.refs_0_), channel_id=1, source_target_pairs={{0,8},{8,16},{16,24},{24,28},{28,20},{20,12},{12,4},{4,0},{1,9},{9... | collective-permute-start | bytes 1179656 | tf_op jit(solution)/shard_map/ppermute | solution.py:405
  11.5 0.4 collective-permute-start.4
  12.0 0.1 cut_columns.5.refs_0_
  12.1 2.6 %collective-permute-start.5 = (bf16[1,3,64,512]{3,2,1,0:T(8,128)(2,1)S(1)}, bf16[1,3,64,512]{3,2,1,0:T(8,128)(2,1)S(1)}, u32[]{:S(2)}, u32[]{:S(2)}) collective-permute-start(bf16[1,3,64,512]{3,2,1,0:T(8,128)(2,1)S(1)} %cut_columns.5.refs_0_), channel_id=1, source_target_pairs={{0,2},{4,6},{9,11},{13,15},{18,16},{22,20},{27,25},{31,29}} | collective-permute-start | bytes 589832 | tf_op jit(solution)/shard_map/ppermute | solution.py:393
  14.7 3.2 %collective-permute-done.5.refs_1_ = bf16[1,3,64,512]{3,2,1,0:T(8,128)(2,1)S(1)} collective-permute-done((bf16[1,3,64,512]{3,2,1,0:T(8,128)(2,1)S(1)}, bf16[1,3,64,512]{3,2,1,0:T(8,128)(2,1)S(1)}, u32[]{:S(2)}, u32[]{:S(2)}) %collective-permute-start.5) | collective-permute-done | bytes 196640 | tf_op jit(solution)/shard_map/ppermute | solution.py:393
  17.8 2.7 %collective-permute-done.3.refs_0_.refs_1_ = bf16[2,3,256,128]{3,2,1,0:T(8,128)(2,1)S(1)} collective-permute-done((bf16[2,3,256,128]{3,2,1,0:T(8,128)(2,1)S(1)}, bf16[2,3,256,128]{3,2,1,0:T(8,128)(2,1)S(1)}, u32[]{:S(2)}, u32[]{:S(2)}) %collective-permute-start.3) | collective-permute-done | bytes 393248 | tf_op jit(solution)/shard_map/ppermute | solution.py:405
  20.5 1.3 %collective-permute-done.4.refs_1_.refs_2_ = bf16[2,3,256,128]{3,2,1,0:T(8,128)(2,1)S(1)} collective-permute-done((bf16[2,3,256,128]{3,2,1,0:T(8,128)(2,1)S(1)}, bf16[2,3,256,128]{3,2,1,0:T(8,128)(2,1)S(1)}, u32[]{:S(2)}, u32[]{:S(2)}) %collective-permute-start.4) | collective-permute-done | bytes 393248 | tf_op jit(solution)/shard_map/ppermute | solution.py:405
  21.8 0.4 collective-permute-start.7
  22.2 1.6 %collective-permute-start.6 = (bf16[2,3,256,128]{3,2,1,0:T(8,128)(2,1)S(1)}, bf16[2,3,256,128]{3,2,1,0:T(8,128)(2,1)}, u32[]{:S(2)}, u32[]{:S(2)}) collective-permute-start(bf16[2,3,256,128]{3,2,1,0:T(8,128)(2,1)S(1)} %collective-permute-done.3.refs_0_.refs_1_), channel_id=1, source_target_pairs={{0,8},{8,16},{16,24},{24,28},{28,20},{20,12},{12,4},{4,0},{1,9},{9... | collective-permute-start | bytes 1179656 | tf_op jit(solution)/shard_map/ppermute | solution.py:405
  23.8 1.3 %collective-permute-start.8 = (bf16[1,3,64,512]{3,2,1,0:T(8,128)(2,1)S(1)}, bf16[1,3,64,512]{3,2,1,0:T(8,128)(2,1)S(1)}, u32[]{:S(2)}, u32[]{:S(2)}) collective-permute-start(bf16[1,3,64,512]{3,2,1,0:T(8,128)(2,1)S(1)} %pass_on.2.refs_11_), channel_id=1, source_target_pairs={{0,1},{4,5},{9,8},{13,12},{18,19},{22,23},{27,26},{31,30},{2,3},{6... | collective-permute-start | bytes 589832 | tf_op jit(solution)/shard_map/ppermute | solution.py:398
  25.1 0.0 copy-done
  25.1 0.0 copy-start.2
  25.2 1.0 %copy-done.2 = bf16[3,64,1024]{2,1,0:T(8,128)(2,1)S(1)} copy-done((bf16[3,64,1024]{2,1,0:T(8,128)(2,1)S(1)}, bf16[3,64,1024]{2,1,0:T(8,128)(2,1)}, u32[]{:S(2)}) %copy-start.2) | copy-done | bytes 393240
  26.1 0.5 project.1
  26.6 0.1 collective-permute-start.9
  26.7 0.8 %collective-permute-start.10 = (f32[64,64]{1,0:T(8,128)S(1)}, f32[64,64]{1,0:T(8,128)S(1)}, u32[]{:S(2)}, u32[]{:S(2)}) collective-permute-start(f32[64,64]{1,0:T(8,128)S(1)} %get-tuple-element.29), channel_id=1, source_target_pairs={{0,2},{1,3},{2,0},{3,1},{4,6},{5,7},{6,4},{7,5},{8,10},{9,11},{10,... | collective-permute-start | bytes 49160 | tf_op jit(solution)/shard_map/ppermute | solution.py:330
  27.5 0.4 collective-permute-done.9.refs_16_
  27.9 0.7 collective-permute-start.11
  28.6 0.2 cut_columns.7.refs_0_
  28.8 0.0 copy-done.3
  28.8 1.9 %collective-permute-done.10.refs_17_ = f32[64,64]{1,0:T(8,128)S(1)} collective-permute-done((f32[64,64]{1,0:T(8,128)S(1)}, f32[64,64]{1,0:T(8,128)S(1)}, u32[]{:S(2)}, u32[]{:S(2)}) %collective-permute-start.10) | collective-permute-done | bytes 16416 | tf_op jit(solution)/shard_map/ppermute | solution.py:330
  30.7 2.6 %collective-permute-start.18 = (bf16[2,3,64,512]{3,2,1,0:T(8,128)(2,1)S(1)}, bf16[2,3,64,512]{3,2,1,0:T(8,128)(2,1)S(1)}, u32[]{:S(2)}, u32[]{:S(2)}) collective-permute-start(bf16[2,3,64,512]{3,2,1,0:T(8,128)(2,1)S(1)} %cut_columns.7.refs_0_), channel_id=1, source_target_pairs={{0,2},{4,6},{9,11},{13,15},{18,16},{22,20},{27,25},{31,29}} | collective-permute-start | bytes 1179656 | tf_op jit(solution)/shard_map/ppermute | solution.py:393
  33.3 0.0 collective-permute-done.11.refs_18_
  33.3 0.0 copy-start.8
  33.3 0.0 collective-permute-done.8.refs_12_
  33.3 0.0 collective-permute-done.7.down_ref.refs_4_
  33.4 0.0 collective-permute-done.6.up_ref.refs_3_
  33.4 1.3 %cut_columns.6 = (bf16[2,3,64,512]{3,2,1,0:T(8,128)(2,1)S(1)}, bf16[3,256,128]{2,1,0:T(8,128)(2,1)S(1)}, bf16[3,256,128]{2,1,0:T(8,128)(2,1)S(1)}, bf16[3,256,12...) custom-call(s32[1]{0:T(128)} %bitcast.2.half_ref, bf16[2,3,256,128]{3,2,1,0:T(8,128)(2,1)} %collective-permute-done.6.up_ref.refs_3_, ...), custom_call_target="tpu_custom_call" | custom-call | tf_op jit(solution)/shard_map/cut_columns/pallas_call | solution.py:382
  34.7 0.8 %collective-permute-start.12 = (bf16[3,256,128]{2,1,0:T(8,128)(2,1)S(1)}, bf16[3,256,128]{2,1,0:T(8,128)(2,1)S(1)}, u32[]{:S(2)}, u32[]{:S(2)}) collective-permute-start(bf16[3,256,128]{2,1,0:T(8,128)(2,1)S(1)} %get-tuple-element.32), channel_id=1, source_target_pairs={{0,8},{8,16},{16,24},{24,28},{28,20},{20,12},{12,4},{4,0},{1,9},{9... | collective-permute-start | bytes 589832 | tf_op jit(solution)/shard_map/ppermute | solution.py:405
  35.5 1.3 %collective-permute-start.15 = (bf16[3,256,128]{2,1,0:T(8,128)(2,1)S(1)}, bf16[3,256,128]{2,1,0:T(8,128)(2,1)S(1)}, u32[]{:S(2)}, u32[]{:S(2)}) collective-permute-start(bf16[3,256,128]{2,1,0:T(8,128)(2,1)S(1)} %get-tuple-element.35), channel_id=1, source_target_pairs={{8,0},{16,8},{24,16},{28,24},{20,28},{12,20},{4,12},{0,4},{9,1},{1... | collective-permute-start | bytes 589832 | tf_op jit(solution)/shard_map/ppermute | solution.py:405
  36.7 0.8 %collective-permute-start.13 = (bf16[3,256,128]{2,1,0:T(8,128)(2,1)S(1)}, bf16[3,256,128]{2,1,0:T(8,128)(2,1)S(1)}, u32[]{:S(2)}, u32[]{:S(2)}) collective-permute-start(bf16[3,256,128]{2,1,0:T(8,128)(2,1)S(1)} %get-tuple-element.33), channel_id=1, source_target_pairs={{0,8},{8,16},{16,24},{24,28},{28,20},{20,12},{12,4},{4,0},{1,9},{9... | collective-permute-start | bytes 589832 | tf_op jit(solution)/shard_map/ppermute | solution.py:405
  37.5 1.3 %collective-permute-start.14 = (bf16[3,256,128]{2,1,0:T(8,128)(2,1)S(1)}, bf16[3,256,128]{2,1,0:T(8,128)(2,1)S(1)}, u32[]{:S(2)}, u32[]{:S(2)}) collective-permute-start(bf16[3,256,128]{2,1,0:T(8,128)(2,1)S(1)} %get-tuple-element.34), channel_id=1, source_target_pairs={{8,0},{16,8},{24,16},{28,24},{20,28},{12,20},{4,12},{0,4},{9,1},{1... | collective-permute-start | bytes 589832 | tf_op jit(solution)/shard_map/ppermute | solution.py:405
  38.8 3.4 %collective-permute-done.12.refs_0_.refs_5_ = bf16[3,256,128]{2,1,0:T(8,128)(2,1)S(1)} collective-permute-done((bf16[3,256,128]{2,1,0:T(8,128)(2,1)S(1)}, bf16[3,256,128]{2,1,0:T(8,128)(2,1)S(1)}, u32[]{:S(2)}, u32[]{:S(2)}) %collective-permute-start.12) | collective-permute-done | bytes 196640 | tf_op jit(solution)/shard_map/ppermute | solution.py:405
  42.1 1.1 %collective-permute-start.16 = (bf16[3,256,128]{2,1,0:T(8,128)(2,1)S(1)}, bf16[3,256,128]{2,1,0:T(8,128)(2,1)S(1)}, u32[]{:S(2)}, u32[]{:S(2)}) collective-permute-start(bf16[3,256,128]{2,1,0:T(8,128)(2,1)S(1)} %collective-permute-done.12.refs_0_.refs_5_), channel_id=1, source_target_pairs={{0,8},{8,16},{16,24},{24,28},{28,20},{20,12},{12,4},{4,0},{1,9},{9... | collective-permute-start | bytes 589832 | tf_op jit(solution)/shard_map/ppermute | solution.py:405
  43.2 0.0 collective-permute-done.15.refs_3_.refs_8_
  43.2 1.3 %collective-permute-start.17 = (bf16[3,256,128]{2,1,0:T(8,128)(2,1)S(1)}, bf16[3,256,128]{2,1,0:T(8,128)(2,1)S(1)}, u32[]{:S(2)}, u32[]{:S(2)}) collective-permute-start(bf16[3,256,128]{2,1,0:T(8,128)(2,1)S(1)} %collective-permute-done.15.refs_3_.refs_8_), channel_id=1, source_target_pairs={{8,0},{16,8},{24,16},{28,24},{20,28},{12,20},{4,12},{0,4},{9,1},{1... | collective-permute-start | bytes 589832 | tf_op jit(solution)/shard_map/ppermute | solution.py:405
  44.6 0.0 collective-permute-done.18.refs_1_
  44.6 2.4 %collective-permute-start.19 = (bf16[2,3,64,512]{3,2,1,0:T(8,128)(2,1)S(1)}, bf16[2,3,64,512]{3,2,1,0:T(8,128)(2,1)S(1)}, u32[]{:S(2)}, u32[]{:S(2)}) collective-permute-start(bf16[2,3,64,512]{3,2,1,0:T(8,128)(2,1)S(1)} %get-tuple-element.36.refs_2_), channel_id=1, source_target_pairs={{0,2},{4,6},{9,11},{13,15},{18,16},{22,20},{27,25},{31,29}} | collective-permute-start | bytes 1179656 | tf_op jit(solution)/shard_map/ppermute | solution.py:393
  46.9 0.0 collective-permute-done.13.refs_1_.refs_6_
  47.0 0.5 collective-permute-done.14.refs_2_.refs_7_
  47.4 0.2 cut_columns.8.refs_4_
  47.6 0.0 copy-done.4
  47.6 3.2 %collective-permute-start.20 = (bf16[2,3,64,512]{3,2,1,0:T(8,128)(2,1)S(1)}, bf16[2,3,64,512]{3,2,1,0:T(8,128)(2,1)S(1)}, u32[]{:S(2)}, u32[]{:S(2)}) collective-permute-start(bf16[2,3,64,512]{3,2,1,0:T(8,128)(2,1)S(1)} %cut_columns.8.refs_4_), channel_id=1, source_target_pairs={{0,2},{4,6},{9,11},{13,15},{18,16},{22,20},{27,25},{31,29}} | collective-permute-start | bytes 1179656 | tf_op jit(solution)/shard_map/ppermute | solution.py:393
  50.8 0.0 collective-permute-done.16.refs_0_.refs_9_
  50.9 0.5 collective-permute-done.17.refs_1_.refs_10_
  51.3 0.1 cut_columns.9.refs_6_
  51.5 2.1 %collective-permute-start.21 = (bf16[1,3,64,512]{3,2,1,0:T(8,128)(2,1)S(1)}, bf16[1,3,64,512]{3,2,1,0:T(8,128)(2,1)S(1)}, u32[]{:S(2)}, u32[]{:S(2)}) collective-permute-start(bf16[1,3,64,512]{3,2,1,0:T(8,128)(2,1)S(1)} %cut_columns.9.refs_6_), channel_id=1, source_target_pairs={{0,2},{4,6},{9,11},{13,15},{18,16},{22,20},{27,25},{31,29}} | collective-permute-start | bytes 589832 | tf_op jit(solution)/shard_map/ppermute | solution.py:393
  53.6 0.0 collective-permute-done.19.refs_3_
  53.6 4.9 %collective-permute-done.21.refs_7_ = bf16[1,3,64,512]{3,2,1,0:T(8,128)(2,1)S(1)} collective-permute-done((bf16[1,3,64,512]{3,2,1,0:T(8,128)(2,1)S(1)}, bf16[1,3,64,512]{3,2,1,0:T(8,128)(2,1)S(1)}, u32[]{:S(2)}, u32[]{:S(2)}) %collective-permute-start.21) | collective-permute-done | bytes 196640 | tf_op jit(solution)/shard_map/ppermute | solution.py:393
  58.5 0.0 collective-permute-done.20.refs_5_
  58.5 0.1 pass_on.3.refs_13_
  58.6 1.4 %collective-permute-start.22 = (bf16[7,3,64,512]{3,2,1,0:T(8,128)(2,1)S(1)}, bf16[7,3,64,512]{3,2,1,0:T(8,128)(2,1)S(1)}, u32[]{:S(2)}, u32[]{:S(2)}) collective-permute-start(bf16[7,3,64,512]{3,2,1,0:T(8,128)(2,1)S(1)} %pass_on.3.refs_13_), channel_id=1, source_target_pairs={{0,1},{4,5},{9,8},{13,12},{18,19},{22,23},{27,26},{31,30},{2,3},{6... | collective-permute-start | bytes 4128776 | tf_op jit(solution)/shard_map/ppermute | solution.py:398
  60.0 2.6 %collective-permute-done.22.refs_14_ = bf16[7,3,64,512]{3,2,1,0:T(8,128)(2,1)S(1)} collective-permute-done((bf16[7,3,64,512]{3,2,1,0:T(8,128)(2,1)S(1)}, bf16[7,3,64,512]{3,2,1,0:T(8,128)(2,1)S(1)}, u32[]{:S(2)}, u32[]{:S(2)}) %collective-permute-start.22) | collective-permute-done | bytes 1376288 | tf_op jit(solution)/shard_map/ppermute | solution.py:398
  62.7 9.9 %covariance_tile.1 = (f32[3,3,1024,512]{3,2,1,0:T(8,128)}, f32[64,64]{1,0:T(8,128)}) custom-call(s32[1]{0:T(128)} %bitcast.role_ref, bf16[2,3,256,128]{3,2,1,0:T(8,128)(2,1)S(1)} %get-tuple-element.24.refs_0_, bf16[2,3,256,128]{3,2,1,0:T(8,128)(2,1)S(1)} %collective-permute-done.3.refs_0_.refs_1_, ...), custom_call_target="tpu_custom_call" | custom-call | flops 4831838208 | bytes 25165824 | tf_op jit(solution)/shard_map/covariance_tile/pallas_call | solution.py:435
  (11 shorter events, 0.0 us)
Async XLA Ops:
  0.6 24.5 %copy-start = (bf16[3,1024,256]{2,1,0:T(8,128)(2,1)S(1)}, bf16[3,1024,256]{2,1,0:T(8,128)(2,1)}, u32[]{:S(2)}) copy-start(bf16[3,1024,256]{2,1,0:T(8,128)(2,1)} %eig_ref.1) | copy-start | bytes 4718596
  2.4 3.8 %collective-permute-start.2 = (f32[24,64]{1,0:T(8,128)S(1)}, f32[24,64]{1,0:T(8,128)S(1)}, u32[]{:S(2)}, u32[]{:S(2)}) collective-permute-start(f32[24,64]{1,0:T(8,128)S(1)} %get-tuple-element.21.refs_0_), channel_id=1, source_target_pairs={{0,3},{1,2},{2,1},{3,0},{4,7},{5,6},{6,5},{7,4},{8,11},{9,10},{10,... | collective-permute-start | bytes 18440 | tf_op jit(solution)/shard_map/ppermute | solution.py:330
  4.9 3.7 %collective-permute-start.1 = (f32[24,64]{1,0:T(8,128)S(1)}, f32[24,64]{1,0:T(8,128)S(1)}, u32[]{:S(2)}, u32[]{:S(2)}) collective-permute-start(f32[24,64]{1,0:T(8,128)S(1)} %get-tuple-element.21.refs_0_), channel_id=1, source_target_pairs={{0,2},{1,3},{2,0},{3,1},{4,6},{5,7},{6,4},{7,5},{8,10},{9,11},{10,... | collective-permute-start | bytes 18440 | tf_op jit(solution)/shard_map/ppermute | solution.py:330
  5.5 3.1 %collective-permute-start = (f32[24,64]{1,0:T(8,128)S(1)}, f32[24,64]{1,0:T(8,128)S(1)}, u32[]{:S(2)}, u32[]{:S(2)}) collective-permute-start(f32[24,64]{1,0:T(8,128)S(1)} %get-tuple-element.21.refs_0_), channel_id=1, source_target_pairs={{0,1},{1,0},{2,3},{3,2},{4,5},{5,4},{6,7},{7,6},{8,9},{9,8},{10,11... | collective-permute-start | bytes 18440 | tf_op jit(solution)/shard_map/ppermute | solution.py:330
  9.2 0.7 %copy-start.1 = (bf16[3,64,1024]{2,1,0:T(8,128)(2,1)}, bf16[3,64,1024]{2,1,0:T(8,128)(2,1)S(1)}, u32[]{:S(2)}) copy-start(bf16[3,64,1024]{2,1,0:T(8,128)(2,1)S(1)} %get-tuple-element.26.flat_ref) | copy-start | bytes 1179652
  9.9 10.5 %collective-permute-start.3 = (bf16[2,3,256,128]{3,2,1,0:T(8,128)(2,1)S(1)}, bf16[2,3,256,128]{3,2,1,0:T(8,128)(2,1)S(1)}, u32[]{:S(2)}, u32[]{:S(2)}) collective-permute-start(bf16[2,3,256,128]{3,2,1,0:T(8,128)(2,1)S(1)} %get-tuple-element.24.refs_0_), channel_id=1, source_target_pairs={{0,8},{8,16},{16,24},{24,28},{28,20},{20,12},{12,4},{4,0},{1,9},{9... | collective-permute-start | bytes 1179656 | tf_op jit(solution)/shard_map/ppermute | solution.py:405
  11.5 10.3 %collective-permute-start.4 = (bf16[2,3,256,128]{3,2,1,0:T(8,128)(2,1)S(1)}, bf16[2,3,256,128]{3,2,1,0:T(8,128)(2,1)S(1)}, u32[]{:S(2)}, u32[]{:S(2)}) collective-permute-start(bf16[2,3,256,128]{3,2,1,0:T(8,128)(2,1)S(1)} %get-tuple-element.24.refs_0_), channel_id=1, source_target_pairs={{8,0},{16,8},{24,16},{28,24},{20,28},{12,20},{4,12},{0,4},{9,1},{1... | collective-permute-start | bytes 1179656 | tf_op jit(solution)/shard_map/ppermute | solution.py:405
  12.1 5.7 %collective-permute-start.5 = (bf16[1,3,64,512]{3,2,1,0:T(8,128)(2,1)S(1)}, bf16[1,3,64,512]{3,2,1,0:T(8,128)(2,1)S(1)}, u32[]{:S(2)}, u32[]{:S(2)}) collective-permute-start(bf16[1,3,64,512]{3,2,1,0:T(8,128)(2,1)S(1)} %cut_columns.5.refs_0_), channel_id=1, source_target_pairs={{0,2},{4,6},{9,11},{13,15},{18,16},{22,20},{27,25},{31,29}} | collective-permute-start | bytes 589832 | tf_op jit(solution)/shard_map/ppermute | solution.py:393
  21.8 11.6 %collective-permute-start.7 = (bf16[2,3,256,128]{3,2,1,0:T(8,128)(2,1)S(1)}, bf16[2,3,256,128]{3,2,1,0:T(8,128)(2,1)S(1)}, u32[]{:S(2)}, u32[]{:S(2)}) collective-permute-start(bf16[2,3,256,128]{3,2,1,0:T(8,128)(2,1)S(1)} %collective-permute-done.4.refs_1_.refs_2_), channel_id=1, source_target_pairs={{8,0},{16,8},{24,16},{28,24},{20,28},{12,20},{4,12},{0,4},{9,1},{1... | collective-permute-start | bytes 1179656 | tf_op jit(solution)/shard_map/ppermute | solution.py:405
  22.2 11.1 %collective-permute-start.6 = (bf16[2,3,256,128]{3,2,1,0:T(8,128)(2,1)S(1)}, bf16[2,3,256,128]{3,2,1,0:T(8,128)(2,1)}, u32[]{:S(2)}, u32[]{:S(2)}) collective-permute-start(bf16[2,3,256,128]{3,2,1,0:T(8,128)(2,1)S(1)} %collective-permute-done.3.refs_0_.refs_1_), channel_id=1, source_target_pairs={{0,8},{8,16},{16,24},{24,28},{28,20},{20,12},{12,4},{4,0},{1,9},{9... | collective-permute-start | bytes 1179656 | tf_op jit(solution)/shard_map/ppermute | solution.py:405
  23.8 4.9 %copy-start.3 = (bf16[1,3,64,512]{3,2,1,0:T(8,128)(2,1)}, bf16[1,3,64,512]{3,2,1,0:T(8,128)(2,1)S(1)}, u32[]{:S(2)}) copy-start(bf16[1,3,64,512]{3,2,1,0:T(8,128)(2,1)S(1)} %pass_on.2.refs_11_) | copy-start | bytes 589828
  23.8 9.5 %collective-permute-start.8 = (bf16[1,3,64,512]{3,2,1,0:T(8,128)(2,1)S(1)}, bf16[1,3,64,512]{3,2,1,0:T(8,128)(2,1)S(1)}, u32[]{:S(2)}, u32[]{:S(2)}) collective-permute-start(bf16[1,3,64,512]{3,2,1,0:T(8,128)(2,1)S(1)} %pass_on.2.refs_11_), channel_id=1, source_target_pairs={{0,1},{4,5},{9,8},{13,12},{18,19},{22,23},{27,26},{31,30},{2,3},{6... | collective-permute-start | bytes 589832 | tf_op jit(solution)/shard_map/ppermute | solution.py:398
  25.1 1.0 %copy-start.2 = (bf16[3,64,1024]{2,1,0:T(8,128)(2,1)S(1)}, bf16[3,64,1024]{2,1,0:T(8,128)(2,1)}, u32[]{:S(2)}) copy-start(bf16[3,64,1024]{2,1,0:T(8,128)(2,1)} %copy-done.1) | copy-start | bytes 1179652
  26.6 21.0 %copy-start.4 = (f32[64,64]{1,0:T(8,128)}, f32[64,64]{1,0:T(8,128)S(1)}, u32[]{:S(2)}) copy-start(f32[64,64]{1,0:T(8,128)S(1)} %get-tuple-element.27.refs_15_) | copy-start | bytes 49156
  26.6 1.3 %collective-permute-start.9 = (f32[64,64]{1,0:T(8,128)S(1)}, f32[64,64]{1,0:T(8,128)S(1)}, u32[]{:S(2)}, u32[]{:S(2)}) collective-permute-start(f32[64,64]{1,0:T(8,128)S(1)} %get-tuple-element.28), channel_id=1, source_target_pairs={{0,1},{1,0},{2,3},{3,2},{4,5},{5,4},{6,7},{7,6},{8,9},{9,8},{10,11... | collective-permute-start | bytes 49160 | tf_op jit(solution)/shard_map/ppermute | solution.py:330
  26.7 4.0 %collective-permute-start.10 = (f32[64,64]{1,0:T(8,128)S(1)}, f32[64,64]{1,0:T(8,128)S(1)}, u32[]{:S(2)}, u32[]{:S(2)}) collective-permute-start(f32[64,64]{1,0:T(8,128)S(1)} %get-tuple-element.29), channel_id=1, source_target_pairs={{0,2},{1,3},{2,0},{3,1},{4,6},{5,7},{6,4},{7,5},{8,10},{9,11},{10,... | collective-permute-start | bytes 49160 | tf_op jit(solution)/shard_map/ppermute | solution.py:330
  27.9 19.7 %copy-start.6 = (f32[64,64]{1,0:T(8,128)}, f32[64,64]{1,0:T(8,128)S(1)}, u32[]{:S(2)}) copy-start(f32[64,64]{1,0:T(8,128)S(1)} %collective-permute-done.9.refs_16_) | copy-start | bytes 49156
  27.9 5.4 %collective-permute-start.11 = (f32[64,64]{1,0:T(8,128)S(1)}, f32[64,64]{1,0:T(8,128)S(1)}, u32[]{:S(2)}, u32[]{:S(2)}) collective-permute-start(f32[64,64]{1,0:T(8,128)S(1)} %get-tuple-element.30), channel_id=1, source_target_pairs={{0,3},{1,2},{2,1},{3,0},{4,7},{5,6},{6,5},{7,4},{8,11},{9,10},{10,... | collective-permute-start | bytes 49160 | tf_op jit(solution)/shard_map/ppermute | solution.py:330
  30.7 20.8 %copy-start.7 = (f32[64,64]{1,0:T(8,128)}, f32[64,64]{1,0:T(8,128)S(1)}, u32[]{:S(2)}) copy-start(f32[64,64]{1,0:T(8,128)S(1)} %collective-permute-done.10.refs_17_) | copy-start | bytes 49156
  30.7 13.9 %collective-permute-start.18 = (bf16[2,3,64,512]{3,2,1,0:T(8,128)(2,1)S(1)}, bf16[2,3,64,512]{3,2,1,0:T(8,128)(2,1)S(1)}, u32[]{:S(2)}, u32[]{:S(2)}) collective-permute-start(bf16[2,3,64,512]{3,2,1,0:T(8,128)(2,1)S(1)} %cut_columns.7.refs_0_), channel_id=1, source_target_pairs={{0,2},{4,6},{9,11},{13,15},{18,16},{22,20},{27,25},{31,29}} | collective-permute-start | bytes 1179656 | tf_op jit(solution)/shard_map/ppermute | solution.py:393
  33.3 18.2 %copy-start.8 = (f32[64,64]{1,0:T(8,128)}, f32[64,64]{1,0:T(8,128)S(1)}, u32[]{:S(2)}) copy-start(f32[64,64]{1,0:T(8,128)S(1)} %collective-permute-done.11.refs_18_) | copy-start | bytes 49156
  33.3 18.2 %copy-start.5 = (bf16[1,3,64,512]{3,2,1,0:T(8,128)(2,1)}, bf16[1,3,64,512]{3,2,1,0:T(8,128)(2,1)S(1)}, u32[]{:S(2)}) copy-start(bf16[1,3,64,512]{3,2,1,0:T(8,128)(2,1)S(1)} %collective-permute-done.8.refs_12_) | copy-start | bytes 589828
  34.7 7.5 %collective-permute-start.12 = (bf16[3,256,128]{2,1,0:T(8,128)(2,1)S(1)}, bf16[3,256,128]{2,1,0:T(8,128)(2,1)S(1)}, u32[]{:S(2)}, u32[]{:S(2)}) collective-permute-start(bf16[3,256,128]{2,1,0:T(8,128)(2,1)S(1)} %get-tuple-element.32), channel_id=1, source_target_pairs={{0,8},{8,16},{16,24},{24,28},{28,20},{20,12},{12,4},{4,0},{1,9},{9... | collective-permute-start | bytes 589832 | tf_op jit(solution)/shard_map/ppermute | solution.py:405
  35.5 7.8 %collective-permute-start.15 = (bf16[3,256,128]{2,1,0:T(8,128)(2,1)S(1)}, bf16[3,256,128]{2,1,0:T(8,128)(2,1)S(1)}, u32[]{:S(2)}, u32[]{:S(2)}) collective-permute-start(bf16[3,256,128]{2,1,0:T(8,128)(2,1)S(1)} %get-tuple-element.35), channel_id=1, source_target_pairs={{8,0},{16,8},{24,16},{28,24},{20,28},{12,20},{4,12},{0,4},{9,1},{1... | collective-permute-start | bytes 589832 | tf_op jit(solution)/shard_map/ppermute | solution.py:405
  36.7 10.2 %collective-permute-start.13 = (bf16[3,256,128]{2,1,0:T(8,128)(2,1)S(1)}, bf16[3,256,128]{2,1,0:T(8,128)(2,1)S(1)}, u32[]{:S(2)}, u32[]{:S(2)}) collective-permute-start(bf16[3,256,128]{2,1,0:T(8,128)(2,1)S(1)} %get-tuple-element.33), channel_id=1, source_target_pairs={{0,8},{8,16},{16,24},{24,28},{28,20},{20,12},{12,4},{4,0},{1,9},{9... | collective-permute-start | bytes 589832 | tf_op jit(solution)/shard_map/ppermute | solution.py:405
  37.5 9.9 %collective-permute-start.14 = (bf16[3,256,128]{2,1,0:T(8,128)(2,1)S(1)}, bf16[3,256,128]{2,1,0:T(8,128)(2,1)S(1)}, u32[]{:S(2)}, u32[]{:S(2)}) collective-permute-start(bf16[3,256,128]{2,1,0:T(8,128)(2,1)S(1)} %get-tuple-element.34), channel_id=1, source_target_pairs={{8,0},{16,8},{24,16},{28,24},{20,28},{12,20},{4,12},{0,4},{9,1},{1... | collective-permute-start | bytes 589832 | tf_op jit(solution)/shard_map/ppermute | solution.py:405
  42.1 8.7 %collective-permute-start.16 = (bf16[3,256,128]{2,1,0:T(8,128)(2,1)S(1)}, bf16[3,256,128]{2,1,0:T(8,128)(2,1)S(1)}, u32[]{:S(2)}, u32[]{:S(2)}) collective-permute-start(bf16[3,256,128]{2,1,0:T(8,128)(2,1)S(1)} %collective-permute-done.12.refs_0_.refs_5_), channel_id=1, source_target_pairs={{0,8},{8,16},{16,24},{24,28},{28,20},{20,12},{12,4},{4,0},{1,9},{9... | collective-permute-start | bytes 589832 | tf_op jit(solution)/shard_map/ppermute | solution.py:405
  43.2 8.1 %collective-permute-start.17 = (bf16[3,256,128]{2,1,0:T(8,128)(2,1)S(1)}, bf16[3,256,128]{2,1,0:T(8,128)(2,1)S(1)}, u32[]{:S(2)}, u32[]{:S(2)}) collective-permute-start(bf16[3,256,128]{2,1,0:T(8,128)(2,1)S(1)} %collective-permute-done.15.refs_3_.refs_8_), channel_id=1, source_target_pairs={{8,0},{16,8},{24,16},{28,24},{20,28},{12,20},{4,12},{0,4},{9,1},{1... | collective-permute-start | bytes 589832 | tf_op jit(solution)/shard_map/ppermute | solution.py:405
  44.6 9.1 %collective-permute-start.19 = (bf16[2,3,64,512]{3,2,1,0:T(8,128)(2,1)S(1)}, bf16[2,3,64,512]{3,2,1,0:T(8,128)(2,1)S(1)}, u32[]{:S(2)}, u32[]{:S(2)}) collective-permute-start(bf16[2,3,64,512]{3,2,1,0:T(8,128)(2,1)S(1)} %get-tuple-element.36.refs_2_), channel_id=1, source_target_pairs={{0,2},{4,6},{9,11},{13,15},{18,16},{22,20},{27,25},{31,29}} | collective-permute-start | bytes 1179656 | tf_op jit(solution)/shard_map/ppermute | solution.py:393
  47.6 10.9 %collective-permute-start.20 = (bf16[2,3,64,512]{3,2,1,0:T(8,128)(2,1)S(1)}, bf16[2,3,64,512]{3,2,1,0:T(8,128)(2,1)S(1)}, u32[]{:S(2)}, u32[]{:S(2)}) collective-permute-start(bf16[2,3,64,512]{3,2,1,0:T(8,128)(2,1)S(1)} %cut_columns.8.refs_4_), channel_id=1, source_target_pairs={{0,2},{4,6},{9,11},{13,15},{18,16},{22,20},{27,25},{31,29}} | collective-permute-start | bytes 1179656 | tf_op jit(solution)/shard_map/ppermute | solution.py:393
  51.5 7.0 %collective-permute-start.21 = (bf16[1,3,64,512]{3,2,1,0:T(8,128)(2,1)S(1)}, bf16[1,3,64,512]{3,2,1,0:T(8,128)(2,1)S(1)}, u32[]{:S(2)}, u32[]{:S(2)}) collective-permute-start(bf16[1,3,64,512]{3,2,1,0:T(8,128)(2,1)S(1)} %cut_columns.9.refs_6_), channel_id=1, source_target_pairs={{0,2},{4,6},{9,11},{13,15},{18,16},{22,20},{27,25},{31,29}} | collective-permute-start | bytes 589832 | tf_op jit(solution)/shard_map/ppermute | solution.py:393
  58.6 4.0 %collective-permute-start.22 = (bf16[7,3,64,512]{3,2,1,0:T(8,128)(2,1)S(1)}, bf16[7,3,64,512]{3,2,1,0:T(8,128)(2,1)S(1)}, u32[]{:S(2)}, u32[]{:S(2)}) collective-permute-start(bf16[7,3,64,512]{3,2,1,0:T(8,128)(2,1)S(1)} %pass_on.3.refs_13_), channel_id=1, source_target_pairs={{0,1},{4,5},{9,8},{13,12},{18,19},{22,23},{27,26},{31,30},{2,3},{6... | collective-permute-start | bytes 4128776 | tf_op jit(solution)/shard_map/ppermute | solution.py:398

commit v13 on v8

--- a/solution.py
+++ b/solution.py
@@ -391,12 +391,12 @@
         )(scalar, *[pinned(value, pltpu.VMEM) for value in values])
 
     def cross(cut):
-        return [cut, lax.ppermute(cut, axes, pairs(0, 2))]
+        return [cut, lax.ppermute(cut, axes, pairs(0, 2) + pairs(2, 0))]
 
     def pass_on(values, role):
         slots = sum(value.shape[0] for value in values[::2])
         held = kernel(pass_on_kernel, columns(slots), role, values, "pass_on")
-        return [held, lax.ppermute(held, axes, pairs(0, 1) + pairs(2, 3))]
+        return [held, swap(held, 1)]
 
     order = ring_order(frame_axis)
     forward = [(order[i], order[(i + 1) % frame_axis]) for i in range(frame_axis)]
@@ -410,14 +410,16 @@
     cut_one = kernel(cut_kernel, columns(2), half, list(one), "cut_columns")
     two = hop(after(one[0], crossed[1], *parts), one[1])
     in_hbm = pass_on(crossed + cross(cut_one), role)
-    cut_two = kernel(cut_kernel, columns(2), half, list(two), "cut_columns")
+    cut_two = kernel(
+        cut_kernel, columns(2), after(half, projections), list(two), "cut_columns"
+    )
     three = hop(*two)
     crossed = cross(cut_two)
     half_shard = pltpu.VMEM(piece, jnp.bfloat16)
     cut_three, *halves = kernel(
         cut_last_kernel,
         (columns(2), half_shard, half_shard),
-        after(half, projections, in_hbm[0]),
+        after(half, in_hbm[0]),
         list(three),
         "cut_columns",
     )

time: 70.7 us -> 71.3 us (level)
  waiting for transfers between devices: 19.1 us -> 21.4 us
  starting transfers between devices: 29.8 us -> 28.4 us
    ppermute x7 -> x5, starting transfers between devices: 17.6 us -> 14.5 us  [cross(): return [cut, lax.ppermute(cut, axes, pairs(0, 2) + pairs(2, 0))]]
    ppermute x6 -> x8, starting transfers between devices: 3.93 us -> 5.68 us  [swap(): lax.ppermute(value, 'atoms', [(a, a ^ distance) for a in range(atom_axis)])]
    ppermute x6 -> x8, waiting for transfers between devices: 6.21 us -> 7.41 us  [swap(): lax.ppermute(value, 'atoms', [(a, a ^ distance) for a in range(atom_axis)])]
    ppermute x4, waiting for transfers between devices: 6.53 us -> 7.45 us  [hop(): lax.ppermute(down, 'frames', backward)]
    ppermute x4, waiting for transfers between devices: 1.13 us -> 1.86 us  [hop(): lax.ppermute(up, 'frames', forward)]
    ppermute x7 -> x5, waiting for transfers between devices: 5.26 us -> 4.73 us  [cross(): return [cut, lax.ppermute(cut, axes, pairs(0, 2) + pairs(2, 0))]]
where the time goes in v13:
time: 71.3 us; the launch traced here: 70.7 us
  starting transfers between devices  28.4 us (40%)
  waiting for transfers between devices  21.4 us (30%)
  Pallas kernels  13.7 us (19%)
  local copies, waits for them, and re-layouts  6.28 us (9%)
  between operations  0.85 us (1%)
    ppermute x5, starting transfers between devices, cross(): return [cut, lax.ppermute(cut, axes, pairs(0, 2) + pairs(2, 0))]  14.5 us
    pallas_call x1, Pallas kernels, per_device(): pl.pallas_call(functools.partial(covariance_kernel, frame_axis, atom_axis...  8.42 us
    ppermute x4, waiting for transfers between devices, hop(): lax.ppermute(down, 'frames', backward)  7.45 us
    ppermute x8, waiting for transfers between devices, swap(): lax.ppermute(value, 'atoms', [(a, a ^ distance) for a in range(atom_axis)])  7.41 us
    unnamed x22, local copies, waits for them, and re-layouts  6.28 us
    ppermute x8, starting transfers between devices, swap(): lax.ppermute(value, 'atoms', [(a, a ^ distance) for a in range(atom_axis)])  5.68 us
    ppermute x4, starting transfers between devices, hop(): lax.ppermute(down, 'frames', backward)  5.04 us
    ppermute x5, waiting for transfers between devices, cross(): return [cut, lax.ppermute(cut, axes, pairs(0, 2) + pairs(2, 0))]  4.73 us
  transfers between devices with their start and end apart: 21, of which 11 were waited for; matrix products, arithmetic and copies ran while one was open for 0% of the time, Pallas kernels for 4%

profile of v13, /device:TPU:0, one launch (start us, length us, event | category | flops | bytes accessed | tf_op | source)
XLA Modules:
  0.0 70.7 jit_solution(429667218653216720)
XLA Ops:
  0.6 1.7 %local_moments.1 = (f32[24,64]{1,0:T(8,128)S(1)}, f32[3,64,1024]{2,1,0:T(8,128)S(1)}, f32[3,1024]{1,0:T(4,128)S(1)}) custom-call(f32[3,64,1024]{2,1,0:T(8,128)} %bitcast.6, f32[3,1024]{1,0:T(4,128)} %ref_hbm.1), custom_call_target="tpu_custom_call" | custom-call | tf_op jit(solution)/shard_map/local_moments/pallas_call | solution.py:310
  2.3 2.4 %collective-permute-start.2 = (f32[24,64]{1,0:T(8,128)S(1)}, f32[24,64]{1,0:T(8,128)S(1)}, u32[]{:S(2)}, u32[]{:S(2)}) collective-permute-start(f32[24,64]{1,0:T(8,128)S(1)} %get-tuple-element.19.refs_0_), channel_id=1, source_target_pairs={{0,3},{1,2},{2,1},{3,0},{4,7},{5,6},{6,5},{7,4},{8,11},{9,10},{10,... | collective-permute-start | bytes 18440 | tf_op jit(solution)/shard_map/ppermute | solution.py:324
  4.7 0.6 collective-permute-start.1
  5.4 0.0 collective-permute-start
  5.4 0.7 %collective-permute-done.2.refs_3_ = f32[24,64]{1,0:T(8,128)S(1)} collective-permute-done((f32[24,64]{1,0:T(8,128)S(1)}, f32[24,64]{1,0:T(8,128)S(1)}, u32[]{:S(2)}, u32[]{:S(2)}) %collective-permute-start.2) | collective-permute-done | bytes 6176 | tf_op jit(solution)/shard_map/ppermute | solution.py:324
  6.1 2.3 %collective-permute-done.1.refs_2_ = f32[24,64]{1,0:T(8,128)S(1)} collective-permute-done((f32[24,64]{1,0:T(8,128)S(1)}, f32[24,64]{1,0:T(8,128)S(1)}, u32[]{:S(2)}, u32[]{:S(2)}) %collective-permute-start.1) | collective-permute-done | bytes 6176 | tf_op jit(solution)/shard_map/ppermute | solution.py:324
  8.4 0.0 collective-permute-done.refs_1_
  8.4 0.6 polar_align.1
  9.0 1.6 %collective-permute-start.3 = (bf16[2,3,256,128]{3,2,1,0:T(8,128)(2,1)S(1)}, bf16[2,3,256,128]{3,2,1,0:T(8,128)(2,1)S(1)}, u32[]{:S(2)}, u32[]{:S(2)}) collective-permute-start(bf16[2,3,256,128]{3,2,1,0:T(8,128)(2,1)S(1)} %get-tuple-element.22.refs_0_), channel_id=1, source_target_pairs={{0,8},{8,16},{16,24},{24,28},{28,20},{20,12},{12,4},{4,0},{1,9},{9... | collective-permute-start | bytes 1179656 | tf_op jit(solution)/shard_map/ppermute | solution.py:406
  10.7 0.4 collective-permute-start.4
  11.1 0.1 cut_columns.5.refs_0_
  11.3 2.5 %collective-permute-start.5 = (bf16[1,3,64,512]{3,2,1,0:T(8,128)(2,1)S(1)}, bf16[1,3,64,512]{3,2,1,0:T(8,128)(2,1)S(1)}, u32[]{:S(2)}, u32[]{:S(2)}) collective-permute-start(bf16[1,3,64,512]{3,2,1,0:T(8,128)(2,1)S(1)} %cut_columns.5.refs_0_), channel_id=1, source_target_pairs={{0,2},{4,6},{9,11},{13,15},{18,16},{22,20},{27,25},{31,29},{2,0},{... | collective-permute-start | bytes 589832 | tf_op jit(solution)/shard_map/ppermute | solution.py:394
  13.8 0.0 copy-start.1
  13.8 1.4 %copy-done.1 = bf16[3,1024,256]{2,1,0:T(8,128)(2,1)S(1)} copy-done((bf16[3,1024,256]{2,1,0:T(8,128)(2,1)S(1)}, bf16[3,1024,256]{2,1,0:T(8,128)(2,1)}, u32[]{:S(2)}) %copy-start.1) | copy-done | bytes 1572888
  15.2 0.5 project.1
  15.7 0.0 copy-start.2
  15.7 0.1 collective-permute-start.6
  15.8 1.5 %collective-permute-start.7 = (f32[64,64]{1,0:T(8,128)S(1)}, f32[64,64]{1,0:T(8,128)S(1)}, u32[]{:S(2)}, u32[]{:S(2)}) collective-permute-start(f32[64,64]{1,0:T(8,128)S(1)} %get-tuple-element.26), channel_id=1, source_target_pairs={{0,2},{1,3},{2,0},{3,1},{4,6},{5,7},{6,4},{7,5},{8,10},{9,11},{10,... | collective-permute-start | bytes 49160 | tf_op jit(solution)/shard_map/ppermute | solution.py:324
  17.3 0.0 collective-permute-done.6.refs_1_
  17.3 0.6 copy-done.4
  17.9 0.9 %collective-permute-start.8 = (f32[64,64]{1,0:T(8,128)S(1)}, f32[64,64]{1,0:T(8,128)S(1)}, u32[]{:S(2)}, u32[]{:S(2)}) collective-permute-start(f32[64,64]{1,0:T(8,128)S(1)} %get-tuple-element.27), channel_id=1, source_target_pairs={{0,3},{1,2},{2,1},{3,0},{4,7},{5,6},{6,5},{7,4},{8,11},{9,10},{10,... | collective-permute-start | bytes 49160 | tf_op jit(solution)/shard_map/ppermute | solution.py:324
  18.8 1.0 %collective-permute-done.7.refs_2_ = f32[64,64]{1,0:T(8,128)S(1)} collective-permute-done((f32[64,64]{1,0:T(8,128)S(1)}, f32[64,64]{1,0:T(8,128)S(1)}, u32[]{:S(2)}, u32[]{:S(2)}) %collective-permute-start.7) | collective-permute-done | bytes 16416 | tf_op jit(solution)/shard_map/ppermute | solution.py:324
  19.8 0.6 copy-done.6
  20.4 0.8 %collective-permute-done.8.refs_3_ = f32[64,64]{1,0:T(8,128)S(1)} collective-permute-done((f32[64,64]{1,0:T(8,128)S(1)}, f32[64,64]{1,0:T(8,128)S(1)}, u32[]{:S(2)}, u32[]{:S(2)}) %collective-permute-start.8) | collective-permute-done | bytes 16416 | tf_op jit(solution)/shard_map/ppermute | solution.py:324
  21.2 0.6 copy-done.8
  21.8 0.0 collective-permute-done.5.refs_1_
  21.8 0.0 collective-permute-done.3.refs_0_.refs_1_
  21.8 0.0 collective-permute-done.4.refs_1_.refs_2_
  21.8 1.6 %collective-permute-start.10 = (bf16[2,3,256,128]{3,2,1,0:T(8,128)(2,1)S(1)}, bf16[2,3,256,128]{3,2,1,0:T(8,128)(2,1)S(1)}, u32[]{:S(2)}, u32[]{:S(2)}) collective-permute-start(bf16[2,3,256,128]{3,2,1,0:T(8,128)(2,1)S(1)} %collective-permute-done.4.refs_1_.refs_2_), channel_id=1, source_target_pairs={{8,0},{16,8},{24,16},{28,24},{20,28},{12,20},{4,12},{0,4},{9,1},{1... | collective-permute-start | bytes 1179656 | tf_op jit(solution)/shard_map/ppermute | solution.py:406
  23.4 0.5 collective-permute-start.9
  23.9 0.2 cut_columns.6.refs_2_
  24.1 3.0 %collective-permute-start.13 = (bf16[2,3,64,512]{3,2,1,0:T(8,128)(2,1)S(1)}, bf16[2,3,64,512]{3,2,1,0:T(8,128)(2,1)}, u32[]{:S(2)}, u32[]{:S(2)}) collective-permute-start(bf16[2,3,64,512]{3,2,1,0:T(8,128)(2,1)S(1)} %cut_columns.6.refs_2_), channel_id=1, source_target_pairs={{0,2},{4,6},{9,11},{13,15},{18,16},{22,20},{27,25},{31,29},{2,0},{... | collective-permute-start | bytes 1179656 | tf_op jit(solution)/shard_map/ppermute | solution.py:394
  27.2 5.9 %collective-permute-done.10.refs_1_.refs_4_ = bf16[2,3,256,128]{3,2,1,0:T(8,128)(2,1)S(1)} collective-permute-done((bf16[2,3,256,128]{3,2,1,0:T(8,128)(2,1)S(1)}, bf16[2,3,256,128]{3,2,1,0:T(8,128)(2,1)S(1)}, u32[]{:S(2)}, u32[]{:S(2)}) %collective-permute-start.10) | collective-permute-done | bytes 393248 | tf_op jit(solution)/shard_map/ppermute | solution.py:406
  33.1 1.5 %collective-permute-start.12 = (bf16[2,3,256,128]{3,2,1,0:T(8,128)(2,1)S(1)}, bf16[2,3,256,128]{3,2,1,0:T(8,128)(2,1)S(1)}, u32[]{:S(2)}, u32[]{:S(2)}) collective-permute-start(bf16[2,3,256,128]{3,2,1,0:T(8,128)(2,1)S(1)} %collective-permute-done.10.refs_1_.refs_4_), channel_id=1, source_target_pairs={{8,0},{16,8},{24,16},{28,24},{20,28},{12,20},{4,12},{0,4},{9,1},{1... | collective-permute-start | bytes 1179656 | tf_op jit(solution)/shard_map/ppermute | solution.py:406
  34.6 0.0 collective-permute-done.9.refs_0_.refs_3_
  34.6 0.5 collective-permute-start.11
  35.1 0.8 %copy-done.3 = f32[64,64]{1,0:T(8,128)S(1)} copy-done((f32[64,64]{1,0:T(8,128)S(1)}, f32[64,64]{1,0:T(8,128)}, u32[]{:S(2)}) %copy-start.3) | copy-done | bytes 16408
  35.9 0.8 %copy-done.5 = f32[64,64]{1,0:T(8,128)S(1)} copy-done((f32[64,64]{1,0:T(8,128)S(1)}, f32[64,64]{1,0:T(8,128)}, u32[]{:S(2)}) %copy-start.5) | copy-done | bytes 16408
  36.6 0.8 %copy-done.7 = f32[64,64]{1,0:T(8,128)S(1)} copy-done((f32[64,64]{1,0:T(8,128)S(1)}, f32[64,64]{1,0:T(8,128)}, u32[]{:S(2)}) %copy-start.7) | copy-done | bytes 16408
  37.4 0.8 %copy-done.9 = f32[64,64]{1,0:T(8,128)S(1)} copy-done((f32[64,64]{1,0:T(8,128)S(1)}, f32[64,64]{1,0:T(8,128)}, u32[]{:S(2)}) %copy-start.9) | copy-done | bytes 16408
  38.2 0.6 sum_shares.1
  38.8 0.2 cut_columns.8.refs_0_
  39.0 3.0 %collective-permute-start.17 = (bf16[2,3,64,512]{3,2,1,0:T(8,128)(2,1)S(1)}, bf16[2,3,64,512]{3,2,1,0:T(8,128)(2,1)S(1)}, u32[]{:S(2)}, u32[]{:S(2)}) collective-permute-start(bf16[2,3,64,512]{3,2,1,0:T(8,128)(2,1)S(1)} %cut_columns.8.refs_0_), channel_id=1, source_target_pairs={{0,2},{4,6},{9,11},{13,15},{18,16},{22,20},{27,25},{31,29},{2,0},{... | collective-permute-start | bytes 1179656 | tf_op jit(solution)/shard_map/ppermute | solution.py:394
  42.0 0.0 collective-permute-done.13.refs_3_
  42.0 1.0 %pass_on.2.refs_9_ = bf16[3,3,64,512]{3,2,1,0:T(8,128)(2,1)S(1)} custom-call(s32[1]{0:T(128)} %bitcast.role_ref, bf16[1,3,64,512]{3,2,1,0:T(8,128)(2,1)S(1)} %cut_columns.5.refs_0_, bf16[1,3,64,512]{3,2,1,0:T(8,128)(2,1)S(1)} %collective-permute-done.5.refs_1_, bf16[2,3,64,512]{3,2,1,0:T(8,128)(2,1)S(1)} %cut_columns.6.refs_2_, ...), custom_call_target="tpu_custom_call" | custom-call | tf_op jit(solution)/shard_map/pass_on/pallas_call | solution.py:384
  43.1 0.1 collective-permute-start.16
  43.2 0.4 collective-permute-done.12.down_ref.refs_6_
  43.5 1.2 %collective-permute-done.11.up_ref.refs_5_ = bf16[2,3,256,128]{3,2,1,0:T(8,128)(2,1)S(1)} collective-permute-done((bf16[2,3,256,128]{3,2,1,0:T(8,128)(2,1)S(1)}, bf16[2,3,256,128]{3,2,1,0:T(8,128)(2,1)S(1)}, u32[]{:S(2)}, u32[]{:S(2)}) %collective-permute-start.11) | collective-permute-done | bytes 393248 | tf_op jit(solution)/shard_map/ppermute | solution.py:406
  44.8 0.2 cut_columns.7
  45.0 0.6 collective-permute-start.14
  45.6 1.5 %collective-permute-start.15 = (bf16[3,256,128]{2,1,0:T(8,128)(2,1)S(1)}, bf16[3,256,128]{2,1,0:T(8,128)(2,1)S(1)}, u32[]{:S(2)}, u32[]{:S(2)}) collective-permute-start(bf16[3,256,128]{2,1,0:T(8,128)(2,1)S(1)} %get-tuple-element.31), channel_id=1, source_target_pairs={{8,0},{16,8},{24,16},{28,24},{20,28},{12,20},{4,12},{0,4},{9,1},{1... | collective-permute-start | bytes 589832 | tf_op jit(solution)/shard_map/ppermute | solution.py:406
  47.1 3.0 %collective-permute-start.18 = (bf16[2,3,64,512]{3,2,1,0:T(8,128)(2,1)S(1)}, bf16[2,3,64,512]{3,2,1,0:T(8,128)(2,1)S(1)}, u32[]{:S(2)}, u32[]{:S(2)}) collective-permute-start(bf16[2,3,64,512]{3,2,1,0:T(8,128)(2,1)S(1)} %get-tuple-element.34.refs_2_), channel_id=1, source_target_pairs={{0,2},{4,6},{9,11},{13,15},{18,16},{22,20},{27,25},{31,29},{2,0},{... | collective-permute-start | bytes 1179656 | tf_op jit(solution)/shard_map/ppermute | solution.py:394
  50.1 0.0 collective-permute-done.17.refs_1_
  50.1 0.6 collective-permute-done.14.up_half.refs_7_
  50.7 1.1 %collective-permute-done.15.down_half.refs_8_ = bf16[3,256,128]{2,1,0:T(8,128)(2,1)S(1)} collective-permute-done((bf16[3,256,128]{2,1,0:T(8,128)(2,1)S(1)}, bf16[3,256,128]{2,1,0:T(8,128)(2,1)S(1)}, u32[]{:S(2)}, u32[]{:S(2)}) %collective-permute-start.15) | collective-permute-done | bytes 196640 | tf_op jit(solution)/shard_map/ppermute | solution.py:406
  51.8 0.1 cut_columns.9.refs_4_
  52.0 2.8 %collective-permute-start.19 = (bf16[1,3,64,512]{3,2,1,0:T(8,128)(2,1)S(1)}, bf16[1,3,64,512]{3,2,1,0:T(8,128)(2,1)S(1)}, u32[]{:S(2)}, u32[]{:S(2)}) collective-permute-start(bf16[1,3,64,512]{3,2,1,0:T(8,128)(2,1)S(1)} %cut_columns.9.refs_4_), channel_id=1, source_target_pairs={{0,2},{4,6},{9,11},{13,15},{18,16},{22,20},{27,25},{31,29},{2,0},{... | collective-permute-start | bytes 589832 | tf_op jit(solution)/shard_map/ppermute | solution.py:394
  54.8 0.0 collective-permute-done.16.refs_10_
  54.8 4.7 %collective-permute-done.19.refs_5_ = bf16[1,3,64,512]{3,2,1,0:T(8,128)(2,1)S(1)} collective-permute-done((bf16[1,3,64,512]{3,2,1,0:T(8,128)(2,1)S(1)}, bf16[1,3,64,512]{3,2,1,0:T(8,128)(2,1)S(1)}, u32[]{:S(2)}, u32[]{:S(2)}) %collective-permute-start.19) | collective-permute-done | bytes 196640 | tf_op jit(solution)/shard_map/ppermute | solution.py:394
  59.6 0.0 collective-permute-done.18.refs_3_
  59.6 0.1 pass_on.3.refs_11_
  59.6 0.1 collective-permute-start.20
  59.7 2.6 %collective-permute-done.20.refs_12_ = bf16[5,3,64,512]{3,2,1,0:T(8,128)(2,1)S(1)} collective-permute-done((bf16[5,3,64,512]{3,2,1,0:T(8,128)(2,1)S(1)}, bf16[5,3,64,512]{3,2,1,0:T(8,128)(2,1)S(1)}, u32[]{:S(2)}, u32[]{:S(2)}) %collective-permute-start.20) | collective-permute-done | bytes 983072 | tf_op jit(solution)/shard_map/ppermute | solution.py:324
  62.3 8.4 %covariance_tile.1 = f32[3,3,1024,512]{3,2,1,0:T(8,128)} custom-call(s32[1]{0:T(128)} %bitcast.role_ref, bf16[2,3,256,128]{3,2,1,0:T(8,128)(2,1)S(1)} %get-tuple-element.22.refs_0_, bf16[2,3,256,128]{3,2,1,0:T(8,128)(2,1)S(1)} %collective-permute-done.3.refs_0_.refs_1_, bf16[2,3,256,128]{3,2,1,0:T(8,128)(2,1)S(1)} %collective-permute-done.4.refs_1_.refs_2_, ...), custom_call_target="tpu_custom_call" | custom-call | flops 4831838208 | bytes 25165824 | tf_op jit(solution)/shard_map/covariance_tile/pallas_call | solution.py:435
  (12 shorter events, 0.0 us)
Async XLA Ops:
  2.3 3.8 %collective-permute-start.2 = (f32[24,64]{1,0:T(8,128)S(1)}, f32[24,64]{1,0:T(8,128)S(1)}, u32[]{:S(2)}, u32[]{:S(2)}) collective-permute-start(f32[24,64]{1,0:T(8,128)S(1)} %get-tuple-element.19.refs_0_), channel_id=1, source_target_pairs={{0,3},{1,2},{2,1},{3,0},{4,7},{5,6},{6,5},{7,4},{8,11},{9,10},{10,... | collective-permute-start | bytes 18440 | tf_op jit(solution)/shard_map/ppermute | solution.py:324
  4.7 3.7 %collective-permute-start.1 = (f32[24,64]{1,0:T(8,128)S(1)}, f32[24,64]{1,0:T(8,128)S(1)}, u32[]{:S(2)}, u32[]{:S(2)}) collective-permute-start(f32[24,64]{1,0:T(8,128)S(1)} %get-tuple-element.19.refs_0_), channel_id=1, source_target_pairs={{0,2},{1,3},{2,0},{3,1},{4,6},{5,7},{6,4},{7,5},{8,10},{9,11},{10,... | collective-permute-start | bytes 18440 | tf_op jit(solution)/shard_map/ppermute | solution.py:324
  5.4 3.1 %collective-permute-start = (f32[24,64]{1,0:T(8,128)S(1)}, f32[24,64]{1,0:T(8,128)S(1)}, u32[]{:S(2)}, u32[]{:S(2)}) collective-permute-start(f32[24,64]{1,0:T(8,128)S(1)} %get-tuple-element.19.refs_0_), channel_id=1, source_target_pairs={{0,1},{1,0},{2,3},{3,2},{4,5},{5,4},{6,7},{7,6},{8,9},{9,8},{10,11... | collective-permute-start | bytes 18440 | tf_op jit(solution)/shard_map/ppermute | solution.py:324
  9.0 12.8 %collective-permute-start.3 = (bf16[2,3,256,128]{3,2,1,0:T(8,128)(2,1)S(1)}, bf16[2,3,256,128]{3,2,1,0:T(8,128)(2,1)S(1)}, u32[]{:S(2)}, u32[]{:S(2)}) collective-permute-start(bf16[2,3,256,128]{3,2,1,0:T(8,128)(2,1)S(1)} %get-tuple-element.22.refs_0_), channel_id=1, source_target_pairs={{0,8},{8,16},{16,24},{24,28},{28,20},{20,12},{12,4},{4,0},{1,9},{9... | collective-permute-start | bytes 1179656 | tf_op jit(solution)/shard_map/ppermute | solution.py:406
  10.7 11.2 %collective-permute-start.4 = (bf16[2,3,256,128]{3,2,1,0:T(8,128)(2,1)S(1)}, bf16[2,3,256,128]{3,2,1,0:T(8,128)(2,1)S(1)}, u32[]{:S(2)}, u32[]{:S(2)}) collective-permute-start(bf16[2,3,256,128]{3,2,1,0:T(8,128)(2,1)S(1)} %get-tuple-element.22.refs_0_), channel_id=1, source_target_pairs={{8,0},{16,8},{24,16},{28,24},{20,28},{12,20},{4,12},{0,4},{9,1},{1... | collective-permute-start | bytes 1179656 | tf_op jit(solution)/shard_map/ppermute | solution.py:406
  11.3 10.6 %collective-permute-start.5 = (bf16[1,3,64,512]{3,2,1,0:T(8,128)(2,1)S(1)}, bf16[1,3,64,512]{3,2,1,0:T(8,128)(2,1)S(1)}, u32[]{:S(2)}, u32[]{:S(2)}) collective-permute-start(bf16[1,3,64,512]{3,2,1,0:T(8,128)(2,1)S(1)} %cut_columns.5.refs_0_), channel_id=1, source_target_pairs={{0,2},{4,6},{9,11},{13,15},{18,16},{22,20},{27,25},{31,29},{2,0},{... | collective-permute-start | bytes 589832 | tf_op jit(solution)/shard_map/ppermute | solution.py:394
  13.8 1.4 %copy-start.1 = (bf16[3,1024,256]{2,1,0:T(8,128)(2,1)S(1)}, bf16[3,1024,256]{2,1,0:T(8,128)(2,1)}, u32[]{:S(2)}) copy-start(bf16[3,1024,256]{2,1,0:T(8,128)(2,1)} %eig_ref.1) | copy-start | bytes 4718596
  15.7 18.9 %copy-start.2 = (f32[64,64]{1,0:T(8,128)}, f32[64,64]{1,0:T(8,128)S(1)}, u32[]{:S(2)}) copy-start(f32[64,64]{1,0:T(8,128)S(1)} %get-tuple-element.24.refs_0_) | copy-start | bytes 49156
  15.7 1.5 %collective-permute-start.6 = (f32[64,64]{1,0:T(8,128)S(1)}, f32[64,64]{1,0:T(8,128)S(1)}, u32[]{:S(2)}, u32[]{:S(2)}) collective-permute-start(f32[64,64]{1,0:T(8,128)S(1)} %get-tuple-element.25), channel_id=1, source_target_pairs={{0,1},{1,0},{2,3},{3,2},{4,5},{5,4},{6,7},{7,6},{8,9},{9,8},{10,11... | collective-permute-start | bytes 49160 | tf_op jit(solution)/shard_map/ppermute | solution.py:324
  15.8 4.0 %collective-permute-start.7 = (f32[64,64]{1,0:T(8,128)S(1)}, f32[64,64]{1,0:T(8,128)S(1)}, u32[]{:S(2)}, u32[]{:S(2)}) collective-permute-start(f32[64,64]{1,0:T(8,128)S(1)} %get-tuple-element.26), channel_id=1, source_target_pairs={{0,2},{1,3},{2,0},{3,1},{4,6},{5,7},{6,4},{7,5},{8,10},{9,11},{10,... | collective-permute-start | bytes 49160 | tf_op jit(solution)/shard_map/ppermute | solution.py:324
  17.3 0.6 copy-start.4
  17.9 3.3 %collective-permute-start.8 = (f32[64,64]{1,0:T(8,128)S(1)}, f32[64,64]{1,0:T(8,128)S(1)}, u32[]{:S(2)}, u32[]{:S(2)}) collective-permute-start(f32[64,64]{1,0:T(8,128)S(1)} %get-tuple-element.27), channel_id=1, source_target_pairs={{0,3},{1,2},{2,1},{3,0},{4,7},{5,6},{6,5},{7,4},{8,11},{9,10},{10,... | collective-permute-start | bytes 49160 | tf_op jit(solution)/shard_map/ppermute | solution.py:324
  19.8 0.6 copy-start.6
  21.2 0.6 copy-start.8
  21.8 11.2 %collective-permute-start.10 = (bf16[2,3,256,128]{3,2,1,0:T(8,128)(2,1)S(1)}, bf16[2,3,256,128]{3,2,1,0:T(8,128)(2,1)S(1)}, u32[]{:S(2)}, u32[]{:S(2)}) collective-permute-start(bf16[2,3,256,128]{3,2,1,0:T(8,128)(2,1)S(1)} %collective-permute-done.4.refs_1_.refs_2_), channel_id=1, source_target_pairs={{8,0},{16,8},{24,16},{28,24},{20,28},{12,20},{4,12},{0,4},{9,1},{1... | collective-permute-start | bytes 1179656 | tf_op jit(solution)/shard_map/ppermute | solution.py:406
  23.4 11.2 %collective-permute-start.9 = (bf16[2,3,256,128]{3,2,1,0:T(8,128)(2,1)S(1)}, bf16[2,3,256,128]{3,2,1,0:T(8,128)(2,1)S(1)}, u32[]{:S(2)}, u32[]{:S(2)}) collective-permute-start(bf16[2,3,256,128]{3,2,1,0:T(8,128)(2,1)S(1)} %collective-permute-done.3.refs_0_.refs_1_), channel_id=1, source_target_pairs={{0,8},{8,16},{16,24},{24,28},{28,20},{20,12},{12,4},{4,0},{1,9},{9... | collective-permute-start | bytes 1179656 | tf_op jit(solution)/shard_map/ppermute | solution.py:406
  24.1 17.9 %collective-permute-start.13 = (bf16[2,3,64,512]{3,2,1,0:T(8,128)(2,1)S(1)}, bf16[2,3,64,512]{3,2,1,0:T(8,128)(2,1)}, u32[]{:S(2)}, u32[]{:S(2)}) collective-permute-start(bf16[2,3,64,512]{3,2,1,0:T(8,128)(2,1)S(1)} %cut_columns.6.refs_2_), channel_id=1, source_target_pairs={{0,2},{4,6},{9,11},{13,15},{18,16},{22,20},{27,25},{31,29},{2,0},{... | collective-permute-start | bytes 1179656 | tf_op jit(solution)/shard_map/ppermute | solution.py:394
  33.1 10.5 %collective-permute-start.12 = (bf16[2,3,256,128]{3,2,1,0:T(8,128)(2,1)S(1)}, bf16[2,3,256,128]{3,2,1,0:T(8,128)(2,1)S(1)}, u32[]{:S(2)}, u32[]{:S(2)}) collective-permute-start(bf16[2,3,256,128]{3,2,1,0:T(8,128)(2,1)S(1)} %collective-permute-done.10.refs_1_.refs_4_), channel_id=1, source_target_pairs={{8,0},{16,8},{24,16},{28,24},{20,28},{12,20},{4,12},{0,4},{9,1},{1... | collective-permute-start | bytes 1179656 | tf_op jit(solution)/shard_map/ppermute | solution.py:406
  34.6 10.2 %collective-permute-start.11 = (bf16[2,3,256,128]{3,2,1,0:T(8,128)(2,1)S(1)}, bf16[2,3,256,128]{3,2,1,0:T(8,128)(2,1)S(1)}, u32[]{:S(2)}, u32[]{:S(2)}) collective-permute-start(bf16[2,3,256,128]{3,2,1,0:T(8,128)(2,1)S(1)} %collective-permute-done.9.refs_0_.refs_3_), channel_id=1, source_target_pairs={{0,8},{8,16},{16,24},{24,28},{28,20},{20,12},{12,4},{4,0},{1,9},{9... | collective-permute-start | bytes 1179656 | tf_op jit(solution)/shard_map/ppermute | solution.py:406
  35.1 0.8 %copy-start.3 = (f32[64,64]{1,0:T(8,128)S(1)}, f32[64,64]{1,0:T(8,128)}, u32[]{:S(2)}) copy-start(f32[64,64]{1,0:T(8,128)} %copy-done.2) | copy-start | bytes 49156
  35.9 0.8 %copy-start.5 = (f32[64,64]{1,0:T(8,128)S(1)}, f32[64,64]{1,0:T(8,128)}, u32[]{:S(2)}) copy-start(f32[64,64]{1,0:T(8,128)} %copy-done.4) | copy-start | bytes 49156
  36.6 0.8 %copy-start.7 = (f32[64,64]{1,0:T(8,128)S(1)}, f32[64,64]{1,0:T(8,128)}, u32[]{:S(2)}) copy-start(f32[64,64]{1,0:T(8,128)} %copy-done.6) | copy-start | bytes 49156
  37.4 0.8 %copy-start.9 = (f32[64,64]{1,0:T(8,128)S(1)}, f32[64,64]{1,0:T(8,128)}, u32[]{:S(2)}) copy-start(f32[64,64]{1,0:T(8,128)} %copy-done.8) | copy-start | bytes 49156
  39.0 11.1 %collective-permute-start.17 = (bf16[2,3,64,512]{3,2,1,0:T(8,128)(2,1)S(1)}, bf16[2,3,64,512]{3,2,1,0:T(8,128)(2,1)S(1)}, u32[]{:S(2)}, u32[]{:S(2)}) collective-permute-start(bf16[2,3,64,512]{3,2,1,0:T(8,128)(2,1)S(1)} %cut_columns.8.refs_0_), channel_id=1, source_target_pairs={{0,2},{4,6},{9,11},{13,15},{18,16},{22,20},{27,25},{31,29},{2,0},{... | collective-permute-start | bytes 1179656 | tf_op jit(solution)/shard_map/ppermute | solution.py:394
  43.1 19.2 %copy-start = (bf16[3,3,64,512]{3,2,1,0:T(8,128)(2,1)}, bf16[3,3,64,512]{3,2,1,0:T(8,128)(2,1)S(1)}, u32[]{:S(2)}) copy-start(bf16[3,3,64,512]{3,2,1,0:T(8,128)(2,1)S(1)} %pass_on.2.refs_9_) | copy-start | bytes 1769476
  43.1 11.7 %collective-permute-start.16 = (bf16[3,3,64,512]{3,2,1,0:T(8,128)(2,1)S(1)}, bf16[3,3,64,512]{3,2,1,0:T(8,128)(2,1)S(1)}, u32[]{:S(2)}, u32[]{:S(2)}) collective-permute-start(bf16[3,3,64,512]{3,2,1,0:T(8,128)(2,1)S(1)} %pass_on.2.refs_9_), channel_id=1, source_target_pairs={{0,1},{1,0},{2,3},{3,2},{4,5},{5,4},{6,7},{7,6},{8,9},{9,8},{10,11... | collective-permute-start | bytes 1769480 | tf_op jit(solution)/shard_map/ppermute | solution.py:324
  45.0 5.7 %collective-permute-start.14 = (bf16[3,256,128]{2,1,0:T(8,128)(2,1)S(1)}, bf16[3,256,128]{2,1,0:T(8,128)(2,1)S(1)}, u32[]{:S(2)}, u32[]{:S(2)}) collective-permute-start(bf16[3,256,128]{2,1,0:T(8,128)(2,1)S(1)} %get-tuple-element.30), channel_id=1, source_target_pairs={{0,8},{8,16},{16,24},{24,28},{28,20},{20,12},{12,4},{4,0},{1,9},{9... | collective-permute-start | bytes 589832 | tf_op jit(solution)/shard_map/ppermute | solution.py:406
  45.6 6.3 %collective-permute-start.15 = (bf16[3,256,128]{2,1,0:T(8,128)(2,1)S(1)}, bf16[3,256,128]{2,1,0:T(8,128)(2,1)S(1)}, u32[]{:S(2)}, u32[]{:S(2)}) collective-permute-start(bf16[3,256,128]{2,1,0:T(8,128)(2,1)S(1)} %get-tuple-element.31), channel_id=1, source_target_pairs={{8,0},{16,8},{24,16},{28,24},{20,28},{12,20},{4,12},{0,4},{9,1},{1... | collective-permute-start | bytes 589832 | tf_op jit(solution)/shard_map/ppermute | solution.py:406
  47.1 12.5 %collective-permute-start.18 = (bf16[2,3,64,512]{3,2,1,0:T(8,128)(2,1)S(1)}, bf16[2,3,64,512]{3,2,1,0:T(8,128)(2,1)S(1)}, u32[]{:S(2)}, u32[]{:S(2)}) collective-permute-start(bf16[2,3,64,512]{3,2,1,0:T(8,128)(2,1)S(1)} %get-tuple-element.34.refs_2_), channel_id=1, source_target_pairs={{0,2},{4,6},{9,11},{13,15},{18,16},{22,20},{27,25},{31,29},{2,0},{... | collective-permute-start | bytes 1179656 | tf_op jit(solution)/shard_map/ppermute | solution.py:394
  52.0 7.6 %collective-permute-start.19 = (bf16[1,3,64,512]{3,2,1,0:T(8,128)(2,1)S(1)}, bf16[1,3,64,512]{3,2,1,0:T(8,128)(2,1)S(1)}, u32[]{:S(2)}, u32[]{:S(2)}) collective-permute-start(bf16[1,3,64,512]{3,2,1,0:T(8,128)(2,1)S(1)} %cut_columns.9.refs_4_), channel_id=1, source_target_pairs={{0,2},{4,6},{9,11},{13,15},{18,16},{22,20},{27,25},{31,29},{2,0},{... | collective-permute-start | bytes 589832 | tf_op jit(solution)/shard_map/ppermute | solution.py:394
  54.8 7.4 %copy-start.10 = (bf16[3,3,64,512]{3,2,1,0:T(8,128)(2,1)}, bf16[3,3,64,512]{3,2,1,0:T(8,128)(2,1)S(1)}, u32[]{:S(2)}) copy-start(bf16[3,3,64,512]{3,2,1,0:T(8,128)(2,1)S(1)} %collective-permute-done.16.refs_10_) | copy-start | bytes 1769476
  59.6 2.6 %collective-permute-start.20 = (bf16[5,3,64,512]{3,2,1,0:T(8,128)(2,1)S(1)}, bf16[5,3,64,512]{3,2,1,0:T(8,128)(2,1)S(1)}, u32[]{:S(2)}, u32[]{:S(2)}) collective-permute-start(bf16[5,3,64,512]{3,2,1,0:T(8,128)(2,1)S(1)} %pass_on.3.refs_11_), channel_id=1, source_target_pairs={{0,1},{1,0},{2,3},{3,2},{4,5},{5,4},{6,7},{7,6},{8,9},{9,8},{10,11... | collective-permute-start | bytes 2949128 | tf_op jit(solution)/shard_map/ppermute | solution.py:324

commit v14 on v13

--- a/solution.py
+++ b/solution.py
@@ -391,7 +391,8 @@
         )(scalar, *[pinned(value, pltpu.VMEM) for value in values])
 
     def cross(cut):
-        return [cut, lax.ppermute(cut, axes, pairs(0, 2) + pairs(2, 0))]
+        whole = pairs(0, 2) + pairs(2, 0) + pairs(1, 1) + pairs(3, 3)
+        return [cut, lax.ppermute(cut, axes, whole)]
 
     def pass_on(values, role):
         slots = sum(value.shape[0] for value in values[::2])

time: 71.3 us -> 71.3 us (level)
  no operation moved by 1% of the time
where the time goes in v14:
time: 71.3 us; the launch traced here: 70.7 us
  starting transfers between devices  28.4 us (40%)
  waiting for transfers between devices  21.4 us (30%)
  Pallas kernels  13.7 us (19%)
  local copies, waits for them, and re-layouts  6.28 us (9%)
  between operations  0.85 us (1%)
    ppermute x5, starting transfers between devices, cross(): return [cut, lax.ppermute(cut, axes, whole)]  14.5 us
    pallas_call x1, Pallas kernels, per_device(): pl.pallas_call(functools.partial(covariance_kernel, frame_axis, atom_axis...  8.42 us
    ppermute x4, waiting for transfers between devices, hop(): lax.ppermute(down, 'frames', backward)  7.45 us
    ppermute x8, waiting for transfers between devices, swap(): lax.ppermute(value, 'atoms', [(a, a ^ distance) for a in range(atom_axis)])  7.41 us
    unnamed x22, local copies, waits for them, and re-layouts  6.28 us
    ppermute x8, starting transfers between devices, swap(): lax.ppermute(value, 'atoms', [(a, a ^ distance) for a in range(atom_axis)])  5.68 us
    ppermute x4, starting transfers between devices, hop(): lax.ppermute(down, 'frames', backward)  5.04 us
    ppermute x5, waiting for transfers between devices, cross(): return [cut, lax.ppermute(cut, axes, whole)]  4.73 us
  transfers between devices with their start and end apart: 21, of which 11 were waited for; matrix products, arithmetic and copies ran while one was open for 0% of the time, Pallas kernels for 4%

profile of v14, /device:TPU:0, one launch (start us, length us, event | category | flops | bytes accessed | tf_op | source)
XLA Modules:
  0.0 70.7 jit_solution(16711083253070435336)
XLA Ops:
  0.6 1.7 %local_moments.1 = (f32[24,64]{1,0:T(8,128)S(1)}, f32[3,64,1024]{2,1,0:T(8,128)S(1)}, f32[3,1024]{1,0:T(4,128)S(1)}) custom-call(f32[3,64,1024]{2,1,0:T(8,128)} %bitcast.6, f32[3,1024]{1,0:T(4,128)} %ref_hbm.1), custom_call_target="tpu_custom_call" | custom-call | tf_op jit(solution)/shard_map/local_moments/pallas_call | solution.py:310
  2.3 2.4 %collective-permute-start.2 = (f32[24,64]{1,0:T(8,128)S(1)}, f32[24,64]{1,0:T(8,128)S(1)}, u32[]{:S(2)}, u32[]{:S(2)}) collective-permute-start(f32[24,64]{1,0:T(8,128)S(1)} %get-tuple-element.19.refs_0_), channel_id=1, source_target_pairs={{0,3},{1,2},{2,1},{3,0},{4,7},{5,6},{6,5},{7,4},{8,11},{9,10},{10,... | collective-permute-start | bytes 18440 | tf_op jit(solution)/shard_map/ppermute | solution.py:324
  4.7 0.6 collective-permute-start.1
  5.4 0.0 collective-permute-start
  5.4 0.7 %collective-permute-done.2.refs_3_ = f32[24,64]{1,0:T(8,128)S(1)} collective-permute-done((f32[24,64]{1,0:T(8,128)S(1)}, f32[24,64]{1,0:T(8,128)S(1)}, u32[]{:S(2)}, u32[]{:S(2)}) %collective-permute-start.2) | collective-permute-done | bytes 6176 | tf_op jit(solution)/shard_map/ppermute | solution.py:324
  6.1 2.3 %collective-permute-done.1.refs_2_ = f32[24,64]{1,0:T(8,128)S(1)} collective-permute-done((f32[24,64]{1,0:T(8,128)S(1)}, f32[24,64]{1,0:T(8,128)S(1)}, u32[]{:S(2)}, u32[]{:S(2)}) %collective-permute-start.1) | collective-permute-done | bytes 6176 | tf_op jit(solution)/shard_map/ppermute | solution.py:324
  8.4 0.0 collective-permute-done.refs_1_
  8.4 0.6 polar_align.1
  9.0 1.6 %collective-permute-start.3 = (bf16[2,3,256,128]{3,2,1,0:T(8,128)(2,1)S(1)}, bf16[2,3,256,128]{3,2,1,0:T(8,128)(2,1)S(1)}, u32[]{:S(2)}, u32[]{:S(2)}) collective-permute-start(bf16[2,3,256,128]{3,2,1,0:T(8,128)(2,1)S(1)} %get-tuple-element.22.refs_0_), channel_id=1, source_target_pairs={{0,8},{8,16},{16,24},{24,28},{28,20},{20,12},{12,4},{4,0},{1,9},{9... | collective-permute-start | bytes 1179656 | tf_op jit(solution)/shard_map/ppermute | solution.py:407
  10.7 0.4 collective-permute-start.4
  11.1 0.1 cut_columns.5.refs_0_
  11.3 2.5 %collective-permute-start.5 = (bf16[1,3,64,512]{3,2,1,0:T(8,128)(2,1)S(1)}, bf16[1,3,64,512]{3,2,1,0:T(8,128)(2,1)S(1)}, u32[]{:S(2)}, u32[]{:S(2)}) collective-permute-start(bf16[1,3,64,512]{3,2,1,0:T(8,128)(2,1)S(1)} %cut_columns.5.refs_0_), channel_id=1, source_target_pairs={{0,2},{4,6},{9,11},{13,15},{18,16},{22,20},{27,25},{31,29},{2,0},{... | collective-permute-start | bytes 589832 | tf_op jit(solution)/shard_map/ppermute | solution.py:395
  13.8 0.0 copy-start.1
  13.8 1.4 %copy-done.1 = bf16[3,1024,256]{2,1,0:T(8,128)(2,1)S(1)} copy-done((bf16[3,1024,256]{2,1,0:T(8,128)(2,1)S(1)}, bf16[3,1024,256]{2,1,0:T(8,128)(2,1)}, u32[]{:S(2)}) %copy-start.1) | copy-done | bytes 1572888
  15.2 0.5 project.1
  15.7 0.0 copy-start.2
  15.7 0.1 collective-permute-start.6
  15.8 1.5 %collective-permute-start.7 = (f32[64,64]{1,0:T(8,128)S(1)}, f32[64,64]{1,0:T(8,128)S(1)}, u32[]{:S(2)}, u32[]{:S(2)}) collective-permute-start(f32[64,64]{1,0:T(8,128)S(1)} %get-tuple-element.26), channel_id=1, source_target_pairs={{0,2},{1,3},{2,0},{3,1},{4,6},{5,7},{6,4},{7,5},{8,10},{9,11},{10,... | collective-permute-start | bytes 49160 | tf_op jit(solution)/shard_map/ppermute | solution.py:324
  17.3 0.0 collective-permute-done.6.refs_1_
  17.3 0.6 copy-done.4
  17.9 0.9 %collective-permute-start.8 = (f32[64,64]{1,0:T(8,128)S(1)}, f32[64,64]{1,0:T(8,128)S(1)}, u32[]{:S(2)}, u32[]{:S(2)}) collective-permute-start(f32[64,64]{1,0:T(8,128)S(1)} %get-tuple-element.27), channel_id=1, source_target_pairs={{0,3},{1,2},{2,1},{3,0},{4,7},{5,6},{6,5},{7,4},{8,11},{9,10},{10,... | collective-permute-start | bytes 49160 | tf_op jit(solution)/shard_map/ppermute | solution.py:324
  18.8 1.0 %collective-permute-done.7.refs_2_ = f32[64,64]{1,0:T(8,128)S(1)} collective-permute-done((f32[64,64]{1,0:T(8,128)S(1)}, f32[64,64]{1,0:T(8,128)S(1)}, u32[]{:S(2)}, u32[]{:S(2)}) %collective-permute-start.7) | collective-permute-done | bytes 16416 | tf_op jit(solution)/shard_map/ppermute | solution.py:324
  19.8 0.6 copy-done.6
  20.4 0.8 %collective-permute-done.8.refs_3_ = f32[64,64]{1,0:T(8,128)S(1)} collective-permute-done((f32[64,64]{1,0:T(8,128)S(1)}, f32[64,64]{1,0:T(8,128)S(1)}, u32[]{:S(2)}, u32[]{:S(2)}) %collective-permute-start.8) | collective-permute-done | bytes 16416 | tf_op jit(solution)/shard_map/ppermute | solution.py:324
  21.2 0.6 copy-done.8
  21.8 0.0 collective-permute-done.5.refs_1_
  21.8 0.0 collective-permute-done.3.refs_0_.refs_1_
  21.8 0.0 collective-permute-done.4.refs_1_.refs_2_
  21.8 1.6 %collective-permute-start.10 = (bf16[2,3,256,128]{3,2,1,0:T(8,128)(2,1)S(1)}, bf16[2,3,256,128]{3,2,1,0:T(8,128)(2,1)S(1)}, u32[]{:S(2)}, u32[]{:S(2)}) collective-permute-start(bf16[2,3,256,128]{3,2,1,0:T(8,128)(2,1)S(1)} %collective-permute-done.4.refs_1_.refs_2_), channel_id=1, source_target_pairs={{8,0},{16,8},{24,16},{28,24},{20,28},{12,20},{4,12},{0,4},{9,1},{1... | collective-permute-start | bytes 1179656 | tf_op jit(solution)/shard_map/ppermute | solution.py:407
  23.4 0.5 collective-permute-start.9
  23.9 0.2 cut_columns.6.refs_2_
  24.1 3.0 %collective-permute-start.13 = (bf16[2,3,64,512]{3,2,1,0:T(8,128)(2,1)S(1)}, bf16[2,3,64,512]{3,2,1,0:T(8,128)(2,1)}, u32[]{:S(2)}, u32[]{:S(2)}) collective-permute-start(bf16[2,3,64,512]{3,2,1,0:T(8,128)(2,1)S(1)} %cut_columns.6.refs_2_), channel_id=1, source_target_pairs={{0,2},{4,6},{9,11},{13,15},{18,16},{22,20},{27,25},{31,29},{2,0},{... | collective-permute-start | bytes 1179656 | tf_op jit(solution)/shard_map/ppermute | solution.py:395
  27.2 5.9 %collective-permute-done.10.refs_1_.refs_4_ = bf16[2,3,256,128]{3,2,1,0:T(8,128)(2,1)S(1)} collective-permute-done((bf16[2,3,256,128]{3,2,1,0:T(8,128)(2,1)S(1)}, bf16[2,3,256,128]{3,2,1,0:T(8,128)(2,1)S(1)}, u32[]{:S(2)}, u32[]{:S(2)}) %collective-permute-start.10) | collective-permute-done | bytes 393248 | tf_op jit(solution)/shard_map/ppermute | solution.py:407
  33.1 1.5 %collective-permute-start.12 = (bf16[2,3,256,128]{3,2,1,0:T(8,128)(2,1)S(1)}, bf16[2,3,256,128]{3,2,1,0:T(8,128)(2,1)S(1)}, u32[]{:S(2)}, u32[]{:S(2)}) collective-permute-start(bf16[2,3,256,128]{3,2,1,0:T(8,128)(2,1)S(1)} %collective-permute-done.10.refs_1_.refs_4_), channel_id=1, source_target_pairs={{8,0},{16,8},{24,16},{28,24},{20,28},{12,20},{4,12},{0,4},{9,1},{1... | collective-permute-start | bytes 1179656 | tf_op jit(solution)/shard_map/ppermute | solution.py:407
  34.6 0.0 collective-permute-done.9.refs_0_.refs_3_
  34.6 0.5 collective-permute-start.11
  35.1 0.8 %copy-done.3 = f32[64,64]{1,0:T(8,128)S(1)} copy-done((f32[64,64]{1,0:T(8,128)S(1)}, f32[64,64]{1,0:T(8,128)}, u32[]{:S(2)}) %copy-start.3) | copy-done | bytes 16408
  35.9 0.8 %copy-done.5 = f32[64,64]{1,0:T(8,128)S(1)} copy-done((f32[64,64]{1,0:T(8,128)S(1)}, f32[64,64]{1,0:T(8,128)}, u32[]{:S(2)}) %copy-start.5) | copy-done | bytes 16408
  36.6 0.8 %copy-done.7 = f32[64,64]{1,0:T(8,128)S(1)} copy-done((f32[64,64]{1,0:T(8,128)S(1)}, f32[64,64]{1,0:T(8,128)}, u32[]{:S(2)}) %copy-start.7) | copy-done | bytes 16408
  37.4 0.8 %copy-done.9 = f32[64,64]{1,0:T(8,128)S(1)} copy-done((f32[64,64]{1,0:T(8,128)S(1)}, f32[64,64]{1,0:T(8,128)}, u32[]{:S(2)}) %copy-start.9) | copy-done | bytes 16408
  38.2 0.6 sum_shares.1
  38.8 0.2 cut_columns.8.refs_0_
  39.0 3.0 %collective-permute-start.17 = (bf16[2,3,64,512]{3,2,1,0:T(8,128)(2,1)S(1)}, bf16[2,3,64,512]{3,2,1,0:T(8,128)(2,1)S(1)}, u32[]{:S(2)}, u32[]{:S(2)}) collective-permute-start(bf16[2,3,64,512]{3,2,1,0:T(8,128)(2,1)S(1)} %cut_columns.8.refs_0_), channel_id=1, source_target_pairs={{0,2},{4,6},{9,11},{13,15},{18,16},{22,20},{27,25},{31,29},{2,0},{... | collective-permute-start | bytes 1179656 | tf_op jit(solution)/shard_map/ppermute | solution.py:395
  42.0 0.0 collective-permute-done.13.refs_3_
  42.0 1.0 %pass_on.2.refs_9_ = bf16[3,3,64,512]{3,2,1,0:T(8,128)(2,1)S(1)} custom-call(s32[1]{0:T(128)} %bitcast.role_ref, bf16[1,3,64,512]{3,2,1,0:T(8,128)(2,1)S(1)} %cut_columns.5.refs_0_, bf16[1,3,64,512]{3,2,1,0:T(8,128)(2,1)S(1)} %collective-permute-done.5.refs_1_, bf16[2,3,64,512]{3,2,1,0:T(8,128)(2,1)S(1)} %cut_columns.6.refs_2_, ...), custom_call_target="tpu_custom_call" | custom-call | tf_op jit(solution)/shard_map/pass_on/pallas_call | solution.py:384
  43.1 0.1 collective-permute-start.16
  43.2 0.4 collective-permute-done.12.down_ref.refs_6_
  43.5 1.2 %collective-permute-done.11.up_ref.refs_5_ = bf16[2,3,256,128]{3,2,1,0:T(8,128)(2,1)S(1)} collective-permute-done((bf16[2,3,256,128]{3,2,1,0:T(8,128)(2,1)S(1)}, bf16[2,3,256,128]{3,2,1,0:T(8,128)(2,1)S(1)}, u32[]{:S(2)}, u32[]{:S(2)}) %collective-permute-start.11) | collective-permute-done | bytes 393248 | tf_op jit(solution)/shard_map/ppermute | solution.py:407
  44.8 0.2 cut_columns.7
  45.0 0.6 collective-permute-start.14
  45.6 1.5 %collective-permute-start.15 = (bf16[3,256,128]{2,1,0:T(8,128)(2,1)S(1)}, bf16[3,256,128]{2,1,0:T(8,128)(2,1)S(1)}, u32[]{:S(2)}, u32[]{:S(2)}) collective-permute-start(bf16[3,256,128]{2,1,0:T(8,128)(2,1)S(1)} %get-tuple-element.31), channel_id=1, source_target_pairs={{8,0},{16,8},{24,16},{28,24},{20,28},{12,20},{4,12},{0,4},{9,1},{1... | collective-permute-start | bytes 589832 | tf_op jit(solution)/shard_map/ppermute | solution.py:407
  47.1 3.0 %collective-permute-start.18 = (bf16[2,3,64,512]{3,2,1,0:T(8,128)(2,1)S(1)}, bf16[2,3,64,512]{3,2,1,0:T(8,128)(2,1)S(1)}, u32[]{:S(2)}, u32[]{:S(2)}) collective-permute-start(bf16[2,3,64,512]{3,2,1,0:T(8,128)(2,1)S(1)} %get-tuple-element.34.refs_2_), channel_id=1, source_target_pairs={{0,2},{4,6},{9,11},{13,15},{18,16},{22,20},{27,25},{31,29},{2,0},{... | collective-permute-start | bytes 1179656 | tf_op jit(solution)/shard_map/ppermute | solution.py:395
  50.1 0.0 collective-permute-done.17.refs_1_
  50.1 0.6 collective-permute-done.14.up_half.refs_7_
  50.7 1.1 %collective-permute-done.15.down_half.refs_8_ = bf16[3,256,128]{2,1,0:T(8,128)(2,1)S(1)} collective-permute-done((bf16[3,256,128]{2,1,0:T(8,128)(2,1)S(1)}, bf16[3,256,128]{2,1,0:T(8,128)(2,1)S(1)}, u32[]{:S(2)}, u32[]{:S(2)}) %collective-permute-start.15) | collective-permute-done | bytes 196640 | tf_op jit(solution)/shard_map/ppermute | solution.py:407
  51.8 0.1 cut_columns.9.refs_4_
  52.0 2.8 %collective-permute-start.19 = (bf16[1,3,64,512]{3,2,1,0:T(8,128)(2,1)S(1)}, bf16[1,3,64,512]{3,2,1,0:T(8,128)(2,1)S(1)}, u32[]{:S(2)}, u32[]{:S(2)}) collective-permute-start(bf16[1,3,64,512]{3,2,1,0:T(8,128)(2,1)S(1)} %cut_columns.9.refs_4_), channel_id=1, source_target_pairs={{0,2},{4,6},{9,11},{13,15},{18,16},{22,20},{27,25},{31,29},{2,0},{... | collective-permute-start | bytes 589832 | tf_op jit(solution)/shard_map/ppermute | solution.py:395
  54.8 0.0 collective-permute-done.16.refs_10_
  54.8 4.7 %collective-permute-done.19.refs_5_ = bf16[1,3,64,512]{3,2,1,0:T(8,128)(2,1)S(1)} collective-permute-done((bf16[1,3,64,512]{3,2,1,0:T(8,128)(2,1)S(1)}, bf16[1,3,64,512]{3,2,1,0:T(8,128)(2,1)S(1)}, u32[]{:S(2)}, u32[]{:S(2)}) %collective-permute-start.19) | collective-permute-done | bytes 196640 | tf_op jit(solution)/shard_map/ppermute | solution.py:395
  59.6 0.0 collective-permute-done.18.refs_3_
  59.6 0.1 pass_on.3.refs_11_
  59.6 0.1 collective-permute-start.20
  59.7 2.6 %collective-permute-done.20.refs_12_ = bf16[5,3,64,512]{3,2,1,0:T(8,128)(2,1)S(1)} collective-permute-done((bf16[5,3,64,512]{3,2,1,0:T(8,128)(2,1)S(1)}, bf16[5,3,64,512]{3,2,1,0:T(8,128)(2,1)S(1)}, u32[]{:S(2)}, u32[]{:S(2)}) %collective-permute-start.20) | collective-permute-done | bytes 983072 | tf_op jit(solution)/shard_map/ppermute | solution.py:324
  62.3 8.4 %covariance_tile.1 = f32[3,3,1024,512]{3,2,1,0:T(8,128)} custom-call(s32[1]{0:T(128)} %bitcast.role_ref, bf16[2,3,256,128]{3,2,1,0:T(8,128)(2,1)S(1)} %get-tuple-element.22.refs_0_, bf16[2,3,256,128]{3,2,1,0:T(8,128)(2,1)S(1)} %collective-permute-done.3.refs_0_.refs_1_, bf16[2,3,256,128]{3,2,1,0:T(8,128)(2,1)S(1)} %collective-permute-done.4.refs_1_.refs_2_, ...), custom_call_target="tpu_custom_call" | custom-call | flops 4831838208 | bytes 25165824 | tf_op jit(solution)/shard_map/covariance_tile/pallas_call | solution.py:436
  (12 shorter events, 0.0 us)
Async XLA Ops:
  2.3 3.8 %collective-permute-start.2 = (f32[24,64]{1,0:T(8,128)S(1)}, f32[24,64]{1,0:T(8,128)S(1)}, u32[]{:S(2)}, u32[]{:S(2)}) collective-permute-start(f32[24,64]{1,0:T(8,128)S(1)} %get-tuple-element.19.refs_0_), channel_id=1, source_target_pairs={{0,3},{1,2},{2,1},{3,0},{4,7},{5,6},{6,5},{7,4},{8,11},{9,10},{10,... | collective-permute-start | bytes 18440 | tf_op jit(solution)/shard_map/ppermute | solution.py:324
  4.7 3.7 %collective-permute-start.1 = (f32[24,64]{1,0:T(8,128)S(1)}, f32[24,64]{1,0:T(8,128)S(1)}, u32[]{:S(2)}, u32[]{:S(2)}) collective-permute-start(f32[24,64]{1,0:T(8,128)S(1)} %get-tuple-element.19.refs_0_), channel_id=1, source_target_pairs={{0,2},{1,3},{2,0},{3,1},{4,6},{5,7},{6,4},{7,5},{8,10},{9,11},{10,... | collective-permute-start | bytes 18440 | tf_op jit(solution)/shard_map/ppermute | solution.py:324
  5.4 3.1 %collective-permute-start = (f32[24,64]{1,0:T(8,128)S(1)}, f32[24,64]{1,0:T(8,128)S(1)}, u32[]{:S(2)}, u32[]{:S(2)}) collective-permute-start(f32[24,64]{1,0:T(8,128)S(1)} %get-tuple-element.19.refs_0_), channel_id=1, source_target_pairs={{0,1},{1,0},{2,3},{3,2},{4,5},{5,4},{6,7},{7,6},{8,9},{9,8},{10,11... | collective-permute-start | bytes 18440 | tf_op jit(solution)/shard_map/ppermute | solution.py:324
  9.0 12.8 %collective-permute-start.3 = (bf16[2,3,256,128]{3,2,1,0:T(8,128)(2,1)S(1)}, bf16[2,3,256,128]{3,2,1,0:T(8,128)(2,1)S(1)}, u32[]{:S(2)}, u32[]{:S(2)}) collective-permute-start(bf16[2,3,256,128]{3,2,1,0:T(8,128)(2,1)S(1)} %get-tuple-element.22.refs_0_), channel_id=1, source_target_pairs={{0,8},{8,16},{16,24},{24,28},{28,20},{20,12},{12,4},{4,0},{1,9},{9... | collective-permute-start | bytes 1179656 | tf_op jit(solution)/shard_map/ppermute | solution.py:407
  10.7 11.2 %collective-permute-start.4 = (bf16[2,3,256,128]{3,2,1,0:T(8,128)(2,1)S(1)}, bf16[2,3,256,128]{3,2,1,0:T(8,128)(2,1)S(1)}, u32[]{:S(2)}, u32[]{:S(2)}) collective-permute-start(bf16[2,3,256,128]{3,2,1,0:T(8,128)(2,1)S(1)} %get-tuple-element.22.refs_0_), channel_id=1, source_target_pairs={{8,0},{16,8},{24,16},{28,24},{20,28},{12,20},{4,12},{0,4},{9,1},{1... | collective-permute-start | bytes 1179656 | tf_op jit(solution)/shard_map/ppermute | solution.py:407
  11.3 10.6 %collective-permute-start.5 = (bf16[1,3,64,512]{3,2,1,0:T(8,128)(2,1)S(1)}, bf16[1,3,64,512]{3,2,1,0:T(8,128)(2,1)S(1)}, u32[]{:S(2)}, u32[]{:S(2)}) collective-permute-start(bf16[1,3,64,512]{3,2,1,0:T(8,128)(2,1)S(1)} %cut_columns.5.refs_0_), channel_id=1, source_target_pairs={{0,2},{4,6},{9,11},{13,15},{18,16},{22,20},{27,25},{31,29},{2,0},{... | collective-permute-start | bytes 589832 | tf_op jit(solution)/shard_map/ppermute | solution.py:395
  13.8 1.4 %copy-start.1 = (bf16[3,1024,256]{2,1,0:T(8,128)(2,1)S(1)}, bf16[3,1024,256]{2,1,0:T(8,128)(2,1)}, u32[]{:S(2)}) copy-start(bf16[3,1024,256]{2,1,0:T(8,128)(2,1)} %eig_ref.1) | copy-start | bytes 4718596
  15.7 18.9 %copy-start.2 = (f32[64,64]{1,0:T(8,128)}, f32[64,64]{1,0:T(8,128)S(1)}, u32[]{:S(2)}) copy-start(f32[64,64]{1,0:T(8,128)S(1)} %get-tuple-element.24.refs_0_) | copy-start | bytes 49156
  15.7 1.5 %collective-permute-start.6 = (f32[64,64]{1,0:T(8,128)S(1)}, f32[64,64]{1,0:T(8,128)S(1)}, u32[]{:S(2)}, u32[]{:S(2)}) collective-permute-start(f32[64,64]{1,0:T(8,128)S(1)} %get-tuple-element.25), channel_id=1, source_target_pairs={{0,1},{1,0},{2,3},{3,2},{4,5},{5,4},{6,7},{7,6},{8,9},{9,8},{10,11... | collective-permute-start | bytes 49160 | tf_op jit(solution)/shard_map/ppermute | solution.py:324
  15.8 4.0 %collective-permute-start.7 = (f32[64,64]{1,0:T(8,128)S(1)}, f32[64,64]{1,0:T(8,128)S(1)}, u32[]{:S(2)}, u32[]{:S(2)}) collective-permute-start(f32[64,64]{1,0:T(8,128)S(1)} %get-tuple-element.26), channel_id=1, source_target_pairs={{0,2},{1,3},{2,0},{3,1},{4,6},{5,7},{6,4},{7,5},{8,10},{9,11},{10,... | collective-permute-start | bytes 49160 | tf_op jit(solution)/shard_map/ppermute | solution.py:324
  17.3 0.6 copy-start.4
  17.9 3.3 %collective-permute-start.8 = (f32[64,64]{1,0:T(8,128)S(1)}, f32[64,64]{1,0:T(8,128)S(1)}, u32[]{:S(2)}, u32[]{:S(2)}) collective-permute-start(f32[64,64]{1,0:T(8,128)S(1)} %get-tuple-element.27), channel_id=1, source_target_pairs={{0,3},{1,2},{2,1},{3,0},{4,7},{5,6},{6,5},{7,4},{8,11},{9,10},{10,... | collective-permute-start | bytes 49160 | tf_op jit(solution)/shard_map/ppermute | solution.py:324
  19.8 0.6 copy-start.6
  21.2 0.6 copy-start.8
  21.8 11.2 %collective-permute-start.10 = (bf16[2,3,256,128]{3,2,1,0:T(8,128)(2,1)S(1)}, bf16[2,3,256,128]{3,2,1,0:T(8,128)(2,1)S(1)}, u32[]{:S(2)}, u32[]{:S(2)}) collective-permute-start(bf16[2,3,256,128]{3,2,1,0:T(8,128)(2,1)S(1)} %collective-permute-done.4.refs_1_.refs_2_), channel_id=1, source_target_pairs={{8,0},{16,8},{24,16},{28,24},{20,28},{12,20},{4,12},{0,4},{9,1},{1... | collective-permute-start | bytes 1179656 | tf_op jit(solution)/shard_map/ppermute | solution.py:407
  23.4 11.2 %collective-permute-start.9 = (bf16[2,3,256,128]{3,2,1,0:T(8,128)(2,1)S(1)}, bf16[2,3,256,128]{3,2,1,0:T(8,128)(2,1)S(1)}, u32[]{:S(2)}, u32[]{:S(2)}) collective-permute-start(bf16[2,3,256,128]{3,2,1,0:T(8,128)(2,1)S(1)} %collective-permute-done.3.refs_0_.refs_1_), channel_id=1, source_target_pairs={{0,8},{8,16},{16,24},{24,28},{28,20},{20,12},{12,4},{4,0},{1,9},{9... | collective-permute-start | bytes 1179656 | tf_op jit(solution)/shard_map/ppermute | solution.py:407
  24.1 17.9 %collective-permute-start.13 = (bf16[2,3,64,512]{3,2,1,0:T(8,128)(2,1)S(1)}, bf16[2,3,64,512]{3,2,1,0:T(8,128)(2,1)}, u32[]{:S(2)}, u32[]{:S(2)}) collective-permute-start(bf16[2,3,64,512]{3,2,1,0:T(8,128)(2,1)S(1)} %cut_columns.6.refs_2_), channel_id=1, source_target_pairs={{0,2},{4,6},{9,11},{13,15},{18,16},{22,20},{27,25},{31,29},{2,0},{... | collective-permute-start | bytes 1179656 | tf_op jit(solution)/shard_map/ppermute | solution.py:395
  33.1 10.5 %collective-permute-start.12 = (bf16[2,3,256,128]{3,2,1,0:T(8,128)(2,1)S(1)}, bf16[2,3,256,128]{3,2,1,0:T(8,128)(2,1)S(1)}, u32[]{:S(2)}, u32[]{:S(2)}) collective-permute-start(bf16[2,3,256,128]{3,2,1,0:T(8,128)(2,1)S(1)} %collective-permute-done.10.refs_1_.refs_4_), channel_id=1, source_target_pairs={{8,0},{16,8},{24,16},{28,24},{20,28},{12,20},{4,12},{0,4},{9,1},{1... | collective-permute-start | bytes 1179656 | tf_op jit(solution)/shard_map/ppermute | solution.py:407
  34.6 10.2 %collective-permute-start.11 = (bf16[2,3,256,128]{3,2,1,0:T(8,128)(2,1)S(1)}, bf16[2,3,256,128]{3,2,1,0:T(8,128)(2,1)S(1)}, u32[]{:S(2)}, u32[]{:S(2)}) collective-permute-start(bf16[2,3,256,128]{3,2,1,0:T(8,128)(2,1)S(1)} %collective-permute-done.9.refs_0_.refs_3_), channel_id=1, source_target_pairs={{0,8},{8,16},{16,24},{24,28},{28,20},{20,12},{12,4},{4,0},{1,9},{9... | collective-permute-start | bytes 1179656 | tf_op jit(solution)/shard_map/ppermute | solution.py:407
  35.1 0.8 %copy-start.3 = (f32[64,64]{1,0:T(8,128)S(1)}, f32[64,64]{1,0:T(8,128)}, u32[]{:S(2)}) copy-start(f32[64,64]{1,0:T(8,128)} %copy-done.2) | copy-start | bytes 49156
  35.9 0.8 %copy-start.5 = (f32[64,64]{1,0:T(8,128)S(1)}, f32[64,64]{1,0:T(8,128)}, u32[]{:S(2)}) copy-start(f32[64,64]{1,0:T(8,128)} %copy-done.4) | copy-start | bytes 49156
  36.6 0.8 %copy-start.7 = (f32[64,64]{1,0:T(8,128)S(1)}, f32[64,64]{1,0:T(8,128)}, u32[]{:S(2)}) copy-start(f32[64,64]{1,0:T(8,128)} %copy-done.6) | copy-start | bytes 49156
  37.4 0.8 %copy-start.9 = (f32[64,64]{1,0:T(8,128)S(1)}, f32[64,64]{1,0:T(8,128)}, u32[]{:S(2)}) copy-start(f32[64,64]{1,0:T(8,128)} %copy-done.8) | copy-start | bytes 49156
  39.0 11.1 %collective-permute-start.17 = (bf16[2,3,64,512]{3,2,1,0:T(8,128)(2,1)S(1)}, bf16[2,3,64,512]{3,2,1,0:T(8,128)(2,1)S(1)}, u32[]{:S(2)}, u32[]{:S(2)}) collective-permute-start(bf16[2,3,64,512]{3,2,1,0:T(8,128)(2,1)S(1)} %cut_columns.8.refs_0_), channel_id=1, source_target_pairs={{0,2},{4,6},{9,11},{13,15},{18,16},{22,20},{27,25},{31,29},{2,0},{... | collective-permute-start | bytes 1179656 | tf_op jit(solution)/shard_map/ppermute | solution.py:395
  43.1 19.2 %copy-start = (bf16[3,3,64,512]{3,2,1,0:T(8,128)(2,1)}, bf16[3,3,64,512]{3,2,1,0:T(8,128)(2,1)S(1)}, u32[]{:S(2)}) copy-start(bf16[3,3,64,512]{3,2,1,0:T(8,128)(2,1)S(1)} %pass_on.2.refs_9_) | copy-start | bytes 1769476
  43.1 11.7 %collective-permute-start.16 = (bf16[3,3,64,512]{3,2,1,0:T(8,128)(2,1)S(1)}, bf16[3,3,64,512]{3,2,1,0:T(8,128)(2,1)S(1)}, u32[]{:S(2)}, u32[]{:S(2)}) collective-permute-start(bf16[3,3,64,512]{3,2,1,0:T(8,128)(2,1)S(1)} %pass_on.2.refs_9_), channel_id=1, source_target_pairs={{0,1},{1,0},{2,3},{3,2},{4,5},{5,4},{6,7},{7,6},{8,9},{9,8},{10,11... | collective-permute-start | bytes 1769480 | tf_op jit(solution)/shard_map/ppermute | solution.py:324
  45.0 5.7 %collective-permute-start.14 = (bf16[3,256,128]{2,1,0:T(8,128)(2,1)S(1)}, bf16[3,256,128]{2,1,0:T(8,128)(2,1)S(1)}, u32[]{:S(2)}, u32[]{:S(2)}) collective-permute-start(bf16[3,256,128]{2,1,0:T(8,128)(2,1)S(1)} %get-tuple-element.30), channel_id=1, source_target_pairs={{0,8},{8,16},{16,24},{24,28},{28,20},{20,12},{12,4},{4,0},{1,9},{9... | collective-permute-start | bytes 589832 | tf_op jit(solution)/shard_map/ppermute | solution.py:407
  45.6 6.3 %collective-permute-start.15 = (bf16[3,256,128]{2,1,0:T(8,128)(2,1)S(1)}, bf16[3,256,128]{2,1,0:T(8,128)(2,1)S(1)}, u32[]{:S(2)}, u32[]{:S(2)}) collective-permute-start(bf16[3,256,128]{2,1,0:T(8,128)(2,1)S(1)} %get-tuple-element.31), channel_id=1, source_target_pairs={{8,0},{16,8},{24,16},{28,24},{20,28},{12,20},{4,12},{0,4},{9,1},{1... | collective-permute-start | bytes 589832 | tf_op jit(solution)/shard_map/ppermute | solution.py:407
  47.1 12.5 %collective-permute-start.18 = (bf16[2,3,64,512]{3,2,1,0:T(8,128)(2,1)S(1)}, bf16[2,3,64,512]{3,2,1,0:T(8,128)(2,1)S(1)}, u32[]{:S(2)}, u32[]{:S(2)}) collective-permute-start(bf16[2,3,64,512]{3,2,1,0:T(8,128)(2,1)S(1)} %get-tuple-element.34.refs_2_), channel_id=1, source_target_pairs={{0,2},{4,6},{9,11},{13,15},{18,16},{22,20},{27,25},{31,29},{2,0},{... | collective-permute-start | bytes 1179656 | tf_op jit(solution)/shard_map/ppermute | solution.py:395
  52.0 7.6 %collective-permute-start.19 = (bf16[1,3,64,512]{3,2,1,0:T(8,128)(2,1)S(1)}, bf16[1,3,64,512]{3,2,1,0:T(8,128)(2,1)S(1)}, u32[]{:S(2)}, u32[]{:S(2)}) collective-permute-start(bf16[1,3,64,512]{3,2,1,0:T(8,128)(2,1)S(1)} %cut_columns.9.refs_4_), channel_id=1, source_target_pairs={{0,2},{4,6},{9,11},{13,15},{18,16},{22,20},{27,25},{31,29},{2,0},{... | collective-permute-start | bytes 589832 | tf_op jit(solution)/shard_map/ppermute | solution.py:395
  54.8 7.4 %copy-start.10 = (bf16[3,3,64,512]{3,2,1,0:T(8,128)(2,1)}, bf16[3,3,64,512]{3,2,1,0:T(8,128)(2,1)S(1)}, u32[]{:S(2)}) copy-start(bf16[3,3,64,512]{3,2,1,0:T(8,128)(2,1)S(1)} %collective-permute-done.16.refs_10_) | copy-start | bytes 1769476
  59.6 2.6 %collective-permute-start.20 = (bf16[5,3,64,512]{3,2,1,0:T(8,128)(2,1)S(1)}, bf16[5,3,64,512]{3,2,1,0:T(8,128)(2,1)S(1)}, u32[]{:S(2)}, u32[]{:S(2)}) collective-permute-start(bf16[5,3,64,512]{3,2,1,0:T(8,128)(2,1)S(1)} %pass_on.3.refs_11_), channel_id=1, source_target_pairs={{0,1},{1,0},{2,3},{3,2},{4,5},{5,4},{6,7},{7,6},{8,9},{9,8},{10,11... | collective-permute-start | bytes 2949128 | tf_op jit(solution)/shard_map/ppermute | solution.py:324

commit v15 on v13

--- a/solution.py
+++ b/solution.py
@@ -171,6 +171,18 @@
                 to += source.shape[0]
 
 
+def pick_half_kernel(role_ref, own_ref, beside_ref, out_ref):
+    width = out_ref.shape[3]
+
+    @pl.when(role_ref[0] == 0)
+    def _():
+        out_ref[...] = own_ref[:, :, :, :width]
+
+    @pl.when(role_ref[0] != 0)
+    def _():
+        out_ref[...] = beside_ref[:, :, :, width:]
+
+
 def side_by_side(first, second):
     middle = first.shape[1] // 2
     left = jnp.concatenate([first[:, :middle], second[:, :middle]], axis=1)
@@ -182,22 +194,33 @@
     shards, up_half, down_half = refs[: slots - 1], refs[slots - 1], refs[slots]
     refs = refs[slots + 1 :]
     arrays = []
-    for _, _, holder in groups:
-        count = max(holder) + 1
+    for _, _, count in groups:
         arrays.append(refs[:count])
         refs = refs[count:]
     out_ref, left, right, done, col_sem, out_sem = refs
     depth = right.shape[1] // slots
     run = up_half.shape[1]
 
+    def parts_of(k, role):
+        if len(arrays[k]) == 2:
+            return [(arrays[k][role % 2], 0)]
+        own, beside, across, halves = arrays[k]
+        width = across.shape[3]
+        return {
+            0: [(own, 0)],
+            1: [(beside, 0)],
+            2: [(across, 0), (halves, width)],
+            3: [(halves, 0), (across, width)],
+        }[role]
+
     def fetches(k, role, to):
-        source = arrays[k][groups[k][2][role]]
         return [
             pltpu.make_async_copy(
                 source.at[n],
-                right.at[:, pl.ds(to + n * depth, depth), :],
-                col_sem.at[to // depth + n],
+                right.at[:, pl.ds(to + n * depth, depth), pl.ds(at, source.shape[3])],
+                col_sem.at[2 * (to // depth + n) + p],
             )
+            for p, (source, at) in enumerate(parts_of(k, role))
             for n in range(groups[k][0])
         ]
 
@@ -221,10 +244,12 @@
             copy.wait()
 
     def load(k, role, to):
-        source = arrays[k][groups[k][2][role]]
-        for n in range(groups[k][0]):
-            for d in range(3):
-                right[d, to + n * depth : to + (n + 1) * depth, :] = source[n, d]
+        for source, at in parts_of(k, role):
+            for n in range(groups[k][0]):
+                for d in range(3):
+                    right[
+                        d, to + n * depth : to + (n + 1) * depth, at : at + source.shape[3]
+                    ] = source[n, d]
 
     def piece(slot, at, c):
         if slot < slots - 1:
@@ -391,12 +416,19 @@
         )(scalar, *[pinned(value, pltpu.VMEM) for value in values])
 
     def cross(cut):
-        return [cut, lax.ppermute(cut, axes, pairs(0, 2) + pairs(2, 0))]
+        return [cut, lax.ppermute(cut, axes, pairs(0, 2))]
 
     def pass_on(values, role):
         slots = sum(value.shape[0] for value in values[::2])
         held = kernel(pass_on_kernel, columns(slots), role, values, "pass_on")
         return [held, swap(held, 1)]
+
+    def halves_across(cut):
+        beside = swap(cut, 1)
+        half_shape = pltpu.VMEM(cut.shape[:3] + (block // 2,), jnp.bfloat16)
+        picked = kernel(pick_half_kernel, half_shape, role, [cut, beside], "pick_half")
+        across = swap(picked, 2)
+        return [cut, beside, across, swap(across, 1)], picked
 
     order = ring_order(frame_axis)
     forward = [(order[i], order[(i + 1) % frame_axis]) for i in range(frame_axis)]
@@ -427,10 +459,9 @@
     cut_four = kernel(
         cut_far_kernel, columns(1), after(half, crossed[1]), list(far), "cut_columns"
     )
-    in_vmem = pass_on(
-        crossed + cross(cut_three) + cross(cut_four), after(role, in_hbm[1])
-    )
-    groups = ((3, True, (0, 1, 0, 1)), (5, False, (0, 1, 0, 1)))
+    last, picked = halves_across(cut_four)
+    in_vmem = pass_on(crossed + cross(cut_three), after(role, in_hbm[1], picked)) + last
+    groups = ((3, True, 2), (4, False, 2), (1, False, 4))
     rows = [own, *one, *two, *three, *far]
     covariance = pl.pallas_call(
         functools.partial(
@@ -446,7 +477,7 @@
             pltpu.VMEM((2, 2 * run, total_frames), jnp.bfloat16),
             pltpu.VMEM((3, total_frames, block), jnp.bfloat16),
             pltpu.VMEM((2, 3, 2 * run, block), jnp.float32),
-            pltpu.SemaphoreType.DMA((frame_axis,)),
+            pltpu.SemaphoreType.DMA((2 * frame_axis,)),
             pltpu.SemaphoreType.DMA((2, 3)),
         ],
         compiler_params=params(16),

time: 71.3 us -> 71.6 us (level)
  waiting for transfers between devices: 21.4 us -> 24.1 us
  local copies, waits for them, and re-layouts: 6.28 us -> 3.95 us
  Pallas kernels: 13.7 us -> 14.8 us
  starting transfers between devices: 28.4 us -> 27.5 us
    ppermute x8 -> x11, waiting for transfers between devices: 7.41 us -> 12.9 us  [swap(): lax.ppermute(value, 'atoms', [(a, a ^ distance) for a in range(atom_axis)])]
    ppermute x5 -> x4, waiting for transfers between devices: 4.73 us -> 1.74 us  [cross(): return [cut, lax.ppermute(cut, axes, pairs(0, 2))]]
    unnamed x22 -> x14, local copies, waits for them, and re-layouts: 6.28 us -> 3.95 us
    ppermute x5 -> x4, starting transfers between devices: 14.5 us -> 12.6 us  [cross(): return [cut, lax.ppermute(cut, axes, pairs(0, 2))]]
    ppermute x8 -> x11, starting transfers between devices: 5.68 us -> 6.69 us  [swap(): lax.ppermute(value, 'atoms', [(a, a ^ distance) for a in range(atom_axis)])]
    ppermute x4, starting transfers between devices: 5.04 us -> 4.04 us  [hop(): lax.ppermute(down, 'frames', backward)]
    pallas_call x7 -> x8, Pallas kernels: 1.95 us -> 2.93 us  [kernel(): pl.pallas_call(body, out_shape=out_shape, in_specs=[SMEM] + [VMEM] * len(...]
    ppermute x4, starting transfers between devices: 3.22 us -> 4.17 us  [hop(): lax.ppermute(up, 'frames', forward)]
  transfers between devices with their start and end apart: 21 -> 23, of which waited for: 11 -> 14; matrix products, arithmetic and copies ran while one was open for 0% -> 0% of each run, Pallas kernels for 4% -> 4%
where the time goes in v15:
time: 71.6 us; the launch traced here: 71.2 us
  starting transfers between devices  27.5 us (38%)
  waiting for transfers between devices  24.1 us (34%)
  Pallas kernels  14.8 us (21%)
  local copies, waits for them, and re-layouts  3.95 us (6%)
  between operations  0.84 us (1%)
    ppermute x11, waiting for transfers between devices, swap(): lax.ppermute(value, 'atoms', [(a, a ^ distance) for a in range(atom_axis)])  12.9 us
    ppermute x4, starting transfers between devices, cross(): return [cut, lax.ppermute(cut, axes, pairs(0, 2))]  12.6 us
    pallas_call x1, Pallas kernels, per_device(): pl.pallas_call(functools.partial(covariance_kernel, frame_axis, atom_axis...  8.51 us
    ppermute x4, waiting for transfers between devices, hop(): lax.ppermute(down, 'frames', backward)  8.2 us
    ppermute x11, starting transfers between devices, swap(): lax.ppermute(value, 'atoms', [(a, a ^ distance) for a in range(atom_axis)])  6.69 us
    ppermute x4, starting transfers between devices, hop(): lax.ppermute(up, 'frames', forward)  4.17 us
    ppermute x4, starting transfers between devices, hop(): lax.ppermute(down, 'frames', backward)  4.04 us
    unnamed x14, local copies, waits for them, and re-layouts  3.95 us
  transfers between devices with their start and end apart: 23, of which 14 were waited for; matrix products, arithmetic and copies ran while one was open for 0% of the time, Pallas kernels for 4%

profile of v15, /device:TPU:0, one launch (start us, length us, event | category | flops | bytes accessed | tf_op | source)
XLA Modules:
  0.0 71.2 jit_solution(17639294565051793671)
XLA Ops:
  0.6 1.7 %local_moments.1 = (f32[24,64]{1,0:T(8,128)S(1)}, f32[3,64,1024]{2,1,0:T(8,128)S(1)}, f32[3,1024]{1,0:T(4,128)S(1)}) custom-call(f32[3,64,1024]{2,1,0:T(8,128)} %bitcast.6, f32[3,1024]{1,0:T(4,128)} %ref_hbm.1), custom_call_target="tpu_custom_call" | custom-call | tf_op jit(solution)/shard_map/local_moments/pallas_call | solution.py:335
  2.3 2.4 %collective-permute-start.2 = (f32[24,64]{1,0:T(8,128)S(1)}, f32[24,64]{1,0:T(8,128)S(1)}, u32[]{:S(2)}, u32[]{:S(2)}) collective-permute-start(f32[24,64]{1,0:T(8,128)S(1)} %get-tuple-element.19.refs_0_), channel_id=1, source_target_pairs={{0,3},{1,2},{2,1},{3,0},{4,7},{5,6},{6,5},{7,4},{8,11},{9,10},{10,... | collective-permute-start | bytes 18440 | tf_op jit(solution)/shard_map/ppermute | solution.py:349
  4.7 0.6 collective-permute-start.1
  5.4 0.0 collective-permute-start
  5.4 0.7 %collective-permute-done.2.refs_3_ = f32[24,64]{1,0:T(8,128)S(1)} collective-permute-done((f32[24,64]{1,0:T(8,128)S(1)}, f32[24,64]{1,0:T(8,128)S(1)}, u32[]{:S(2)}, u32[]{:S(2)}) %collective-permute-start.2) | collective-permute-done | bytes 6176 | tf_op jit(solution)/shard_map/ppermute | solution.py:349
  6.1 2.3 %collective-permute-done.1.refs_2_ = f32[24,64]{1,0:T(8,128)S(1)} collective-permute-done((f32[24,64]{1,0:T(8,128)S(1)}, f32[24,64]{1,0:T(8,128)S(1)}, u32[]{:S(2)}, u32[]{:S(2)}) %collective-permute-start.1) | collective-permute-done | bytes 6176 | tf_op jit(solution)/shard_map/ppermute | solution.py:349
  8.4 0.0 collective-permute-done.refs_1_
  8.4 0.6 polar_align.1
  9.0 1.6 %collective-permute-start.3 = (bf16[2,3,256,128]{3,2,1,0:T(8,128)(2,1)S(1)}, bf16[2,3,256,128]{3,2,1,0:T(8,128)(2,1)S(1)}, u32[]{:S(2)}, u32[]{:S(2)}) collective-permute-start(bf16[2,3,256,128]{3,2,1,0:T(8,128)(2,1)S(1)} %get-tuple-element.22.refs_0_), channel_id=1, source_target_pairs={{0,8},{8,16},{16,24},{24,28},{28,20},{20,12},{12,4},{4,0},{1,9},{9... | collective-permute-start | bytes 1179656 | tf_op jit(solution)/shard_map/ppermute | solution.py:438
  10.7 0.4 collective-permute-start.4
  11.1 0.1 cut_columns.5.refs_0_
  11.3 0.0 copy-start.2
  11.3 2.6 %collective-permute-start.5 = (bf16[1,3,64,512]{3,2,1,0:T(8,128)(2,1)S(1)}, bf16[1,3,64,512]{3,2,1,0:T(8,128)(2,1)S(1)}, u32[]{:S(2)}, u32[]{:S(2)}) collective-permute-start(bf16[1,3,64,512]{3,2,1,0:T(8,128)(2,1)S(1)} %cut_columns.5.refs_0_), channel_id=1, source_target_pairs={{0,2},{4,6},{9,11},{13,15},{18,16},{22,20},{27,25},{31,29}} | collective-permute-start | bytes 589832 | tf_op jit(solution)/shard_map/ppermute | solution.py:419
  13.8 0.0 copy-start.1
  13.9 1.4 %copy-done.1 = bf16[3,1024,256]{2,1,0:T(8,128)(2,1)S(1)} copy-done((bf16[3,1024,256]{2,1,0:T(8,128)(2,1)S(1)}, bf16[3,1024,256]{2,1,0:T(8,128)(2,1)}, u32[]{:S(2)}) %copy-start.1) | copy-done | bytes 1572888
  15.3 0.5 project.1
  15.7 0.1 collective-permute-start.6
  15.8 0.1 collective-permute-start.7
  15.9 1.1 %collective-permute-done.6.refs_1_ = f32[64,64]{1,0:T(8,128)S(1)} collective-permute-done((f32[64,64]{1,0:T(8,128)S(1)}, f32[64,64]{1,0:T(8,128)S(1)}, u32[]{:S(2)}, u32[]{:S(2)}) %collective-permute-start.6) | collective-permute-done | bytes 16416 | tf_op jit(solution)/shard_map/ppermute | solution.py:349
  17.0 0.7 collective-permute-start.8
  17.7 2.1 %collective-permute-done.7.refs_2_ = f32[64,64]{1,0:T(8,128)S(1)} collective-permute-done((f32[64,64]{1,0:T(8,128)S(1)}, f32[64,64]{1,0:T(8,128)S(1)}, u32[]{:S(2)}, u32[]{:S(2)}) %collective-permute-start.7) | collective-permute-done | bytes 16416 | tf_op jit(solution)/shard_map/ppermute | solution.py:349
  19.8 0.6 collective-permute-done.8.refs_3_
  20.4 0.0 collective-permute-done.5.refs_1_
  20.4 0.7 copy-done.4
  21.0 0.0 collective-permute-done.3.refs_0_.refs_1_
  21.0 0.0 collective-permute-done.4.refs_1_.refs_2_
  21.1 1.5 %collective-permute-start.10 = (bf16[2,3,256,128]{3,2,1,0:T(8,128)(2,1)S(1)}, bf16[2,3,256,128]{3,2,1,0:T(8,128)(2,1)S(1)}, u32[]{:S(2)}, u32[]{:S(2)}) collective-permute-start(bf16[2,3,256,128]{3,2,1,0:T(8,128)(2,1)S(1)} %collective-permute-done.4.refs_1_.refs_2_), channel_id=1, source_target_pairs={{8,0},{16,8},{24,16},{28,24},{20,28},{12,20},{4,12},{0,4},{9,1},{1... | collective-permute-start | bytes 1179656 | tf_op jit(solution)/shard_map/ppermute | solution.py:438
  22.6 0.5 collective-permute-start.9
  23.1 0.2 cut_columns.6.refs_2_
  23.3 3.6 %collective-permute-start.13 = (bf16[2,3,64,512]{3,2,1,0:T(8,128)(2,1)S(1)}, bf16[2,3,64,512]{3,2,1,0:T(8,128)(2,1)}, u32[]{:S(2)}, u32[]{:S(2)}) collective-permute-start(bf16[2,3,64,512]{3,2,1,0:T(8,128)(2,1)S(1)} %cut_columns.6.refs_2_), channel_id=1, source_target_pairs={{0,2},{4,6},{9,11},{13,15},{18,16},{22,20},{27,25},{31,29}} | collective-permute-start | bytes 1179656 | tf_op jit(solution)/shard_map/ppermute | solution.py:419
  26.8 5.7 %collective-permute-done.10.refs_1_.refs_4_ = bf16[2,3,256,128]{3,2,1,0:T(8,128)(2,1)S(1)} collective-permute-done((bf16[2,3,256,128]{3,2,1,0:T(8,128)(2,1)S(1)}, bf16[2,3,256,128]{3,2,1,0:T(8,128)(2,1)S(1)}, u32[]{:S(2)}, u32[]{:S(2)}) %collective-permute-start.10) | collective-permute-done | bytes 393248 | tf_op jit(solution)/shard_map/ppermute | solution.py:438
  32.5 1.2 %collective-permute-start.12 = (bf16[2,3,256,128]{3,2,1,0:T(8,128)(2,1)S(1)}, bf16[2,3,256,128]{3,2,1,0:T(8,128)(2,1)S(1)}, u32[]{:S(2)}, u32[]{:S(2)}) collective-permute-start(bf16[2,3,256,128]{3,2,1,0:T(8,128)(2,1)S(1)} %collective-permute-done.10.refs_1_.refs_4_), channel_id=1, source_target_pairs={{8,0},{16,8},{24,16},{28,24},{20,28},{12,20},{4,12},{0,4},{9,1},{1... | collective-permute-start | bytes 1179656 | tf_op jit(solution)/shard_map/ppermute | solution.py:438
  33.8 0.0 collective-permute-done.9.refs_0_.refs_3_
  33.8 0.8 %collective-permute-start.11 = (bf16[2,3,256,128]{3,2,1,0:T(8,128)(2,1)S(1)}, bf16[2,3,256,128]{3,2,1,0:T(8,128)(2,1)S(1)}, u32[]{:S(2)}, u32[]{:S(2)}) collective-permute-start(bf16[2,3,256,128]{3,2,1,0:T(8,128)(2,1)S(1)} %collective-permute-done.9.refs_0_.refs_3_), channel_id=1, source_target_pairs={{0,8},{8,16},{16,24},{24,28},{28,20},{20,12},{12,4},{4,0},{1,9},{9... | collective-permute-start | bytes 1179656 | tf_op jit(solution)/shard_map/ppermute | solution.py:438
  34.6 0.6 sum_shares.1
  35.2 0.2 cut_columns.8.refs_0_
  35.4 3.6 %collective-permute-start.17 = (bf16[2,3,64,512]{3,2,1,0:T(8,128)(2,1)S(1)}, bf16[2,3,64,512]{3,2,1,0:T(8,128)(2,1)}, u32[]{:S(2)}, u32[]{:S(2)}) collective-permute-start(bf16[2,3,64,512]{3,2,1,0:T(8,128)(2,1)S(1)} %cut_columns.8.refs_0_), channel_id=1, source_target_pairs={{0,2},{4,6},{9,11},{13,15},{18,16},{22,20},{27,25},{31,29}} | collective-permute-start | bytes 1179656 | tf_op jit(solution)/shard_map/ppermute | solution.py:419
  38.9 0.0 collective-permute-done.13.refs_3_
  38.9 0.9 %copy-done.3 = bf16[1,3,64,512]{3,2,1,0:T(8,128)(2,1)S(1)} copy-done((bf16[1,3,64,512]{3,2,1,0:T(8,128)(2,1)S(1)}, bf16[1,3,64,512]{3,2,1,0:T(8,128)(2,1)}, u32[]{:S(2)}) %copy-start.3) | copy-done | bytes 196632
  39.9 0.9 %copy-done.5 = bf16[1,3,64,512]{3,2,1,0:T(8,128)(2,1)S(1)} copy-done((bf16[1,3,64,512]{3,2,1,0:T(8,128)(2,1)S(1)}, bf16[1,3,64,512]{3,2,1,0:T(8,128)(2,1)}, u32[]{:S(2)}) %copy-start.5) | copy-done | bytes 196632
  40.8 1.0 %pass_on.2.refs_9_ = bf16[3,3,64,512]{3,2,1,0:T(8,128)(2,1)S(1)} custom-call(s32[1]{0:T(128)} %bitcast.role_ref, bf16[1,3,64,512]{3,2,1,0:T(8,128)(2,1)S(1)} %copy-done.3, bf16[1,3,64,512]{3,2,1,0:T(8,128)(2,1)S(1)} %copy-done.5, bf16[2,3,64,512]{3,2,1,0:T(8,128)(2,1)S(1)} %cut_columns.6.refs_2_, bf16[2,3,64,512]{3,2,1,0:T(8,128)(2,1)} %collective-permute-done.13.refs_3_), custom_call_target="tpu_custom_call" | custom-call | tf_op jit(solution)/shard_map/pass_on/pallas_call | solution.py:409
  41.9 0.1 collective-permute-start.16
  41.9 1.3 %collective-permute-done.12.down_ref.refs_6_ = bf16[2,3,256,128]{3,2,1,0:T(8,128)(2,1)S(1)} collective-permute-done((bf16[2,3,256,128]{3,2,1,0:T(8,128)(2,1)S(1)}, bf16[2,3,256,128]{3,2,1,0:T(8,128)(2,1)S(1)}, u32[]{:S(2)}, u32[]{:S(2)}) %collective-permute-start.12) | collective-permute-done | bytes 393248 | tf_op jit(solution)/shard_map/ppermute | solution.py:438
  43.2 0.6 collective-permute-done.11.up_ref.refs_5_
  43.8 0.2 cut_columns.7
  44.0 1.2 %collective-permute-start.14 = (bf16[3,256,128]{2,1,0:T(8,128)(2,1)S(1)}, bf16[3,256,128]{2,1,0:T(8,128)(2,1)S(1)}, u32[]{:S(2)}, u32[]{:S(2)}) collective-permute-start(bf16[3,256,128]{2,1,0:T(8,128)(2,1)S(1)} %get-tuple-element.30), channel_id=1, source_target_pairs={{0,8},{8,16},{16,24},{24,28},{28,20},{20,12},{12,4},{4,0},{1,9},{9... | collective-permute-start | bytes 589832 | tf_op jit(solution)/shard_map/ppermute | solution.py:438
  45.3 0.9 %collective-permute-start.15 = (bf16[3,256,128]{2,1,0:T(8,128)(2,1)S(1)}, bf16[3,256,128]{2,1,0:T(8,128)(2,1)S(1)}, u32[]{:S(2)}, u32[]{:S(2)}) collective-permute-start(bf16[3,256,128]{2,1,0:T(8,128)(2,1)S(1)} %get-tuple-element.31), channel_id=1, source_target_pairs={{8,0},{16,8},{24,16},{28,24},{20,28},{12,20},{4,12},{0,4},{9,1},{1... | collective-permute-start | bytes 589832 | tf_op jit(solution)/shard_map/ppermute | solution.py:438
  46.1 3.0 %collective-permute-start.19 = (bf16[2,3,64,512]{3,2,1,0:T(8,128)(2,1)S(1)}, bf16[2,3,64,512]{3,2,1,0:T(8,128)(2,1)S(1)}, u32[]{:S(2)}, u32[]{:S(2)}) collective-permute-start(bf16[2,3,64,512]{3,2,1,0:T(8,128)(2,1)S(1)} %get-tuple-element.35.refs_2_), channel_id=1, source_target_pairs={{0,2},{4,6},{9,11},{13,15},{18,16},{22,20},{27,25},{31,29}} | collective-permute-start | bytes 1179656 | tf_op jit(solution)/shard_map/ppermute | solution.py:419
  49.1 0.0 collective-permute-done.17.refs_1_
  49.1 0.7 collective-permute-done.14.up_half.refs_7_
  49.8 1.2 %collective-permute-done.15.down_half.refs_8_ = bf16[3,256,128]{2,1,0:T(8,128)(2,1)S(1)} collective-permute-done((bf16[3,256,128]{2,1,0:T(8,128)(2,1)S(1)}, bf16[3,256,128]{2,1,0:T(8,128)(2,1)S(1)}, u32[]{:S(2)}, u32[]{:S(2)}) %collective-permute-start.15) | collective-permute-done | bytes 196640 | tf_op jit(solution)/shard_map/ppermute | solution.py:438
  50.9 0.1 cut_columns.9.own_ref.refs_13_
  51.1 0.1 collective-permute-start.18
  51.2 1.4 %collective-permute-done.18.beside_ref.refs_14_ = bf16[1,3,64,512]{3,2,1,0:T(8,128)(2,1)S(1)} collective-permute-done((bf16[1,3,64,512]{3,2,1,0:T(8,128)(2,1)S(1)}, bf16[1,3,64,512]{3,2,1,0:T(8,128)(2,1)S(1)}, u32[]{:S(2)}, u32[]{:S(2)}) %collective-permute-start.18) | collective-permute-done | bytes 196640 | tf_op jit(solution)/shard_map/ppermute | solution.py:349
  52.6 0.0 collective-permute-done.16.refs_10_
  52.6 1.7 %collective-permute-done.19.refs_3_ = bf16[2,3,64,512]{3,2,1,0:T(8,128)(2,1)S(1)} collective-permute-done((bf16[2,3,64,512]{3,2,1,0:T(8,128)(2,1)S(1)}, bf16[2,3,64,512]{3,2,1,0:T(8,128)(2,1)S(1)}, u32[]{:S(2)}, u32[]{:S(2)}) %collective-permute-start.19) | collective-permute-done | bytes 393248 | tf_op jit(solution)/shard_map/ppermute | solution.py:419
  54.4 1.1 %pass_on.3.refs_11_ = bf16[4,3,64,512]{3,2,1,0:T(8,128)(2,1)S(1)} custom-call(s32[1]{0:T(128)} %bitcast.role_ref, bf16[2,3,64,512]{3,2,1,0:T(8,128)(2,1)S(1)} %cut_columns.8.refs_0_, bf16[2,3,64,512]{3,2,1,0:T(8,128)(2,1)} %collective-permute-done.17.refs_1_, bf16[2,3,64,512]{3,2,1,0:T(8,128)(2,1)S(1)} %get-tuple-element.35.refs_2_, ...), custom_call_target="tpu_custom_call" | custom-call | tf_op jit(solution)/shard_map/pass_on/pallas_call | solution.py:409
  55.4 0.1 collective-permute-start.20
  55.5 2.5 %collective-permute-start.21 = (bf16[1,3,64,256]{3,2,1,0:T(8,128)(2,1)S(1)}, bf16[1,3,64,256]{3,2,1,0:T(8,128)(2,1)S(1)}, u32[]{:S(2)}, u32[]{:S(2)}) collective-permute-start(bf16[1,3,64,256]{3,2,1,0:T(8,128)(2,1)S(1)} %pick_half.1), channel_id=1, source_target_pairs={{0,2},{1,3},{2,0},{3,1},{4,6},{5,7},{6,4},{7,5},{8,10},{9,11},{10,... | collective-permute-start | bytes 294920 | tf_op jit(solution)/shard_map/ppermute | solution.py:349
  58.0 3.4 %collective-permute-done.21.refs_15_ = bf16[1,3,64,256]{3,2,1,0:T(8,128)(2,1)S(1)} collective-permute-done((bf16[1,3,64,256]{3,2,1,0:T(8,128)(2,1)S(1)}, bf16[1,3,64,256]{3,2,1,0:T(8,128)(2,1)S(1)}, u32[]{:S(2)}, u32[]{:S(2)}) %collective-permute-start.21) | collective-permute-done | bytes 98336 | tf_op jit(solution)/shard_map/ppermute | solution.py:349
  61.4 0.0 collective-permute-start.22
  61.4 1.3 %collective-permute-done.22.refs_16_ = bf16[1,3,64,256]{3,2,1,0:T(8,128)(2,1)S(1)} collective-permute-done((bf16[1,3,64,256]{3,2,1,0:T(8,128)(2,1)S(1)}, bf16[1,3,64,256]{3,2,1,0:T(8,128)(2,1)S(1)}, u32[]{:S(2)}, u32[]{:S(2)}) %collective-permute-start.22) | collective-permute-done | bytes 98336 | tf_op jit(solution)/shard_map/ppermute | solution.py:349
  62.7 0.0 collective-permute-done.20.refs_12_
  62.7 8.5 %covariance_tile.1 = f32[3,3,1024,512]{3,2,1,0:T(8,128)} custom-call(s32[1]{0:T(128)} %bitcast.role_ref, bf16[2,3,256,128]{3,2,1,0:T(8,128)(2,1)S(1)} %get-tuple-element.22.refs_0_, bf16[2,3,256,128]{3,2,1,0:T(8,128)(2,1)S(1)} %collective-permute-done.3.refs_0_.refs_1_, bf16[2,3,256,128]{3,2,1,0:T(8,128)(2,1)S(1)} %collective-permute-done.4.refs_1_.refs_2_, ...), custom_call_target="tpu_custom_call" | custom-call | flops 4831838208 | bytes 25165824 | tf_op jit(solution)/shard_map/covariance_tile/pallas_call | solution.py:466
  (9 shorter events, 0.0 us)
Async XLA Ops:
  2.3 3.8 %collective-permute-start.2 = (f32[24,64]{1,0:T(8,128)S(1)}, f32[24,64]{1,0:T(8,128)S(1)}, u32[]{:S(2)}, u32[]{:S(2)}) collective-permute-start(f32[24,64]{1,0:T(8,128)S(1)} %get-tuple-element.19.refs_0_), channel_id=1, source_target_pairs={{0,3},{1,2},{2,1},{3,0},{4,7},{5,6},{6,5},{7,4},{8,11},{9,10},{10,... | collective-permute-start | bytes 18440 | tf_op jit(solution)/shard_map/ppermute | solution.py:349
  4.7 3.7 %collective-permute-start.1 = (f32[24,64]{1,0:T(8,128)S(1)}, f32[24,64]{1,0:T(8,128)S(1)}, u32[]{:S(2)}, u32[]{:S(2)}) collective-permute-start(f32[24,64]{1,0:T(8,128)S(1)} %get-tuple-element.19.refs_0_), channel_id=1, source_target_pairs={{0,2},{1,3},{2,0},{3,1},{4,6},{5,7},{6,4},{7,5},{8,10},{9,11},{10,... | collective-permute-start | bytes 18440 | tf_op jit(solution)/shard_map/ppermute | solution.py:349
  5.4 3.1 %collective-permute-start = (f32[24,64]{1,0:T(8,128)S(1)}, f32[24,64]{1,0:T(8,128)S(1)}, u32[]{:S(2)}, u32[]{:S(2)}) collective-permute-start(f32[24,64]{1,0:T(8,128)S(1)} %get-tuple-element.19.refs_0_), channel_id=1, source_target_pairs={{0,1},{1,0},{2,3},{3,2},{4,5},{5,4},{6,7},{7,6},{8,9},{9,8},{10,11... | collective-permute-start | bytes 18440 | tf_op jit(solution)/shard_map/ppermute | solution.py:349
  9.0 12.0 %collective-permute-start.3 = (bf16[2,3,256,128]{3,2,1,0:T(8,128)(2,1)S(1)}, bf16[2,3,256,128]{3,2,1,0:T(8,128)(2,1)S(1)}, u32[]{:S(2)}, u32[]{:S(2)}) collective-permute-start(bf16[2,3,256,128]{3,2,1,0:T(8,128)(2,1)S(1)} %get-tuple-element.22.refs_0_), channel_id=1, source_target_pairs={{0,8},{8,16},{16,24},{24,28},{28,20},{20,12},{12,4},{4,0},{1,9},{9... | collective-permute-start | bytes 1179656 | tf_op jit(solution)/shard_map/ppermute | solution.py:438
  10.7 10.4 %collective-permute-start.4 = (bf16[2,3,256,128]{3,2,1,0:T(8,128)(2,1)S(1)}, bf16[2,3,256,128]{3,2,1,0:T(8,128)(2,1)S(1)}, u32[]{:S(2)}, u32[]{:S(2)}) collective-permute-start(bf16[2,3,256,128]{3,2,1,0:T(8,128)(2,1)S(1)} %get-tuple-element.22.refs_0_), channel_id=1, source_target_pairs={{8,0},{16,8},{24,16},{28,24},{20,28},{12,20},{4,12},{0,4},{9,1},{1... | collective-permute-start | bytes 1179656 | tf_op jit(solution)/shard_map/ppermute | solution.py:438
  11.3 23.3 %copy-start.2 = (bf16[1,3,64,512]{3,2,1,0:T(8,128)(2,1)}, bf16[1,3,64,512]{3,2,1,0:T(8,128)(2,1)S(1)}, u32[]{:S(2)}) copy-start(bf16[1,3,64,512]{3,2,1,0:T(8,128)(2,1)S(1)} %cut_columns.5.refs_0_) | copy-start | bytes 589828
  11.3 9.1 %collective-permute-start.5 = (bf16[1,3,64,512]{3,2,1,0:T(8,128)(2,1)S(1)}, bf16[1,3,64,512]{3,2,1,0:T(8,128)(2,1)S(1)}, u32[]{:S(2)}, u32[]{:S(2)}) collective-permute-start(bf16[1,3,64,512]{3,2,1,0:T(8,128)(2,1)S(1)} %cut_columns.5.refs_0_), channel_id=1, source_target_pairs={{0,2},{4,6},{9,11},{13,15},{18,16},{22,20},{27,25},{31,29}} | collective-permute-start | bytes 589832 | tf_op jit(solution)/shard_map/ppermute | solution.py:419
  13.8 1.4 %copy-start.1 = (bf16[3,1024,256]{2,1,0:T(8,128)(2,1)S(1)}, bf16[3,1024,256]{2,1,0:T(8,128)(2,1)}, u32[]{:S(2)}) copy-start(bf16[3,1024,256]{2,1,0:T(8,128)(2,1)} %eig_ref.1) | copy-start | bytes 4718596
  15.7 1.3 %collective-permute-start.6 = (f32[64,64]{1,0:T(8,128)S(1)}, f32[64,64]{1,0:T(8,128)S(1)}, u32[]{:S(2)}, u32[]{:S(2)}) collective-permute-start(f32[64,64]{1,0:T(8,128)S(1)} %get-tuple-element.25), channel_id=1, source_target_pairs={{0,1},{1,0},{2,3},{3,2},{4,5},{5,4},{6,7},{7,6},{8,9},{9,8},{10,11... | collective-permute-start | bytes 49160 | tf_op jit(solution)/shard_map/ppermute | solution.py:349
  15.8 4.0 %collective-permute-start.7 = (f32[64,64]{1,0:T(8,128)S(1)}, f32[64,64]{1,0:T(8,128)S(1)}, u32[]{:S(2)}, u32[]{:S(2)}) collective-permute-start(f32[64,64]{1,0:T(8,128)S(1)} %get-tuple-element.26), channel_id=1, source_target_pairs={{0,2},{1,3},{2,0},{3,1},{4,6},{5,7},{6,4},{7,5},{8,10},{9,11},{10,... | collective-permute-start | bytes 49160 | tf_op jit(solution)/shard_map/ppermute | solution.py:349
  17.0 3.3 %collective-permute-start.8 = (f32[64,64]{1,0:T(8,128)S(1)}, f32[64,64]{1,0:T(8,128)S(1)}, u32[]{:S(2)}, u32[]{:S(2)}) collective-permute-start(f32[64,64]{1,0:T(8,128)S(1)} %get-tuple-element.27), channel_id=1, source_target_pairs={{0,3},{1,2},{2,1},{3,0},{4,7},{5,6},{6,5},{7,4},{8,11},{9,10},{10,... | collective-permute-start | bytes 49160 | tf_op jit(solution)/shard_map/ppermute | solution.py:349
  20.4 0.7 copy-start.4
  21.1 11.5 %collective-permute-start.10 = (bf16[2,3,256,128]{3,2,1,0:T(8,128)(2,1)S(1)}, bf16[2,3,256,128]{3,2,1,0:T(8,128)(2,1)S(1)}, u32[]{:S(2)}, u32[]{:S(2)}) collective-permute-start(bf16[2,3,256,128]{3,2,1,0:T(8,128)(2,1)S(1)} %collective-permute-done.4.refs_1_.refs_2_), channel_id=1, source_target_pairs={{8,0},{16,8},{24,16},{28,24},{20,28},{12,20},{4,12},{0,4},{9,1},{1... | collective-permute-start | bytes 1179656 | tf_op jit(solution)/shard_map/ppermute | solution.py:438
  22.6 11.2 %collective-permute-start.9 = (bf16[2,3,256,128]{3,2,1,0:T(8,128)(2,1)S(1)}, bf16[2,3,256,128]{3,2,1,0:T(8,128)(2,1)S(1)}, u32[]{:S(2)}, u32[]{:S(2)}) collective-permute-start(bf16[2,3,256,128]{3,2,1,0:T(8,128)(2,1)S(1)} %collective-permute-done.3.refs_0_.refs_1_), channel_id=1, source_target_pairs={{0,8},{8,16},{16,24},{24,28},{28,20},{20,12},{12,4},{4,0},{1,9},{9... | collective-permute-start | bytes 1179656 | tf_op jit(solution)/shard_map/ppermute | solution.py:438
  23.3 15.7 %collective-permute-start.13 = (bf16[2,3,64,512]{3,2,1,0:T(8,128)(2,1)S(1)}, bf16[2,3,64,512]{3,2,1,0:T(8,128)(2,1)}, u32[]{:S(2)}, u32[]{:S(2)}) collective-permute-start(bf16[2,3,64,512]{3,2,1,0:T(8,128)(2,1)S(1)} %cut_columns.6.refs_2_), channel_id=1, source_target_pairs={{0,2},{4,6},{9,11},{13,15},{18,16},{22,20},{27,25},{31,29}} | collective-permute-start | bytes 1179656 | tf_op jit(solution)/shard_map/ppermute | solution.py:419
  32.5 10.7 %collective-permute-start.12 = (bf16[2,3,256,128]{3,2,1,0:T(8,128)(2,1)S(1)}, bf16[2,3,256,128]{3,2,1,0:T(8,128)(2,1)S(1)}, u32[]{:S(2)}, u32[]{:S(2)}) collective-permute-start(bf16[2,3,256,128]{3,2,1,0:T(8,128)(2,1)S(1)} %collective-permute-done.10.refs_1_.refs_4_), channel_id=1, source_target_pairs={{8,0},{16,8},{24,16},{28,24},{20,28},{12,20},{4,12},{0,4},{9,1},{1... | collective-permute-start | bytes 1179656 | tf_op jit(solution)/shard_map/ppermute | solution.py:438
  33.8 10.1 %collective-permute-start.11 = (bf16[2,3,256,128]{3,2,1,0:T(8,128)(2,1)S(1)}, bf16[2,3,256,128]{3,2,1,0:T(8,128)(2,1)S(1)}, u32[]{:S(2)}, u32[]{:S(2)}) collective-permute-start(bf16[2,3,256,128]{3,2,1,0:T(8,128)(2,1)S(1)} %collective-permute-done.9.refs_0_.refs_3_), channel_id=1, source_target_pairs={{0,8},{8,16},{16,24},{24,28},{28,20},{20,12},{12,4},{4,0},{1,9},{9... | collective-permute-start | bytes 1179656 | tf_op jit(solution)/shard_map/ppermute | solution.py:438
  35.4 13.7 %collective-permute-start.17 = (bf16[2,3,64,512]{3,2,1,0:T(8,128)(2,1)S(1)}, bf16[2,3,64,512]{3,2,1,0:T(8,128)(2,1)}, u32[]{:S(2)}, u32[]{:S(2)}) collective-permute-start(bf16[2,3,64,512]{3,2,1,0:T(8,128)(2,1)S(1)} %cut_columns.8.refs_0_), channel_id=1, source_target_pairs={{0,2},{4,6},{9,11},{13,15},{18,16},{22,20},{27,25},{31,29}} | collective-permute-start | bytes 1179656 | tf_op jit(solution)/shard_map/ppermute | solution.py:419
  38.9 0.9 %copy-start.3 = (bf16[1,3,64,512]{3,2,1,0:T(8,128)(2,1)S(1)}, bf16[1,3,64,512]{3,2,1,0:T(8,128)(2,1)}, u32[]{:S(2)}) copy-start(bf16[1,3,64,512]{3,2,1,0:T(8,128)(2,1)} %copy-done.2) | copy-start | bytes 589828
  39.9 0.9 %copy-start.5 = (bf16[1,3,64,512]{3,2,1,0:T(8,128)(2,1)S(1)}, bf16[1,3,64,512]{3,2,1,0:T(8,128)(2,1)}, u32[]{:S(2)}) copy-start(bf16[1,3,64,512]{3,2,1,0:T(8,128)(2,1)} %copy-done.4) | copy-start | bytes 589828
  41.8 20.9 %copy-start = (bf16[3,3,64,512]{3,2,1,0:T(8,128)(2,1)}, bf16[3,3,64,512]{3,2,1,0:T(8,128)(2,1)S(1)}, u32[]{:S(2)}) copy-start(bf16[3,3,64,512]{3,2,1,0:T(8,128)(2,1)S(1)} %pass_on.2.refs_9_) | copy-start | bytes 1769476
  41.9 10.7 %collective-permute-start.16 = (bf16[3,3,64,512]{3,2,1,0:T(8,128)(2,1)S(1)}, bf16[3,3,64,512]{3,2,1,0:T(8,128)(2,1)S(1)}, u32[]{:S(2)}, u32[]{:S(2)}) collective-permute-start(bf16[3,3,64,512]{3,2,1,0:T(8,128)(2,1)S(1)} %pass_on.2.refs_9_), channel_id=1, source_target_pairs={{0,1},{1,0},{2,3},{3,2},{4,5},{5,4},{6,7},{7,6},{8,9},{9,8},{10,11... | collective-permute-start | bytes 1769480 | tf_op jit(solution)/shard_map/ppermute | solution.py:349
  44.0 5.7 %collective-permute-start.14 = (bf16[3,256,128]{2,1,0:T(8,128)(2,1)S(1)}, bf16[3,256,128]{2,1,0:T(8,128)(2,1)S(1)}, u32[]{:S(2)}, u32[]{:S(2)}) collective-permute-start(bf16[3,256,128]{2,1,0:T(8,128)(2,1)S(1)} %get-tuple-element.30), channel_id=1, source_target_pairs={{0,8},{8,16},{16,24},{24,28},{28,20},{20,12},{12,4},{4,0},{1,9},{9... | collective-permute-start | bytes 589832 | tf_op jit(solution)/shard_map/ppermute | solution.py:438
  45.3 5.7 %collective-permute-start.15 = (bf16[3,256,128]{2,1,0:T(8,128)(2,1)S(1)}, bf16[3,256,128]{2,1,0:T(8,128)(2,1)S(1)}, u32[]{:S(2)}, u32[]{:S(2)}) collective-permute-start(bf16[3,256,128]{2,1,0:T(8,128)(2,1)S(1)} %get-tuple-element.31), channel_id=1, source_target_pairs={{8,0},{16,8},{24,16},{28,24},{20,28},{12,20},{4,12},{0,4},{9,1},{1... | collective-permute-start | bytes 589832 | tf_op jit(solution)/shard_map/ppermute | solution.py:438
  46.1 8.2 %collective-permute-start.19 = (bf16[2,3,64,512]{3,2,1,0:T(8,128)(2,1)S(1)}, bf16[2,3,64,512]{3,2,1,0:T(8,128)(2,1)S(1)}, u32[]{:S(2)}, u32[]{:S(2)}) collective-permute-start(bf16[2,3,64,512]{3,2,1,0:T(8,128)(2,1)S(1)} %get-tuple-element.35.refs_2_), channel_id=1, source_target_pairs={{0,2},{4,6},{9,11},{13,15},{18,16},{22,20},{27,25},{31,29}} | collective-permute-start | bytes 1179656 | tf_op jit(solution)/shard_map/ppermute | solution.py:419
  51.1 1.5 %collective-permute-start.18 = (bf16[1,3,64,512]{3,2,1,0:T(8,128)(2,1)S(1)}, bf16[1,3,64,512]{3,2,1,0:T(8,128)(2,1)S(1)}, u32[]{:S(2)}, u32[]{:S(2)}) collective-permute-start(bf16[1,3,64,512]{3,2,1,0:T(8,128)(2,1)S(1)} %cut_columns.9.own_ref.refs_13_), channel_id=1, source_target_pairs={{0,1},{1,0},{2,3},{3,2},{4,5},{5,4},{6,7},{7,6},{8,9},{9,8},{10,11... | collective-permute-start | bytes 589832 | tf_op jit(solution)/shard_map/ppermute | solution.py:349
  52.6 10.1 %copy-start.6 = (bf16[3,3,64,512]{3,2,1,0:T(8,128)(2,1)}, bf16[3,3,64,512]{3,2,1,0:T(8,128)(2,1)S(1)}, u32[]{:S(2)}) copy-start(bf16[3,3,64,512]{3,2,1,0:T(8,128)(2,1)S(1)} %collective-permute-done.16.refs_10_) | copy-start | bytes 1769476
  55.4 7.3 %collective-permute-start.20 = (bf16[4,3,64,512]{3,2,1,0:T(8,128)(2,1)S(1)}, bf16[4,3,64,512]{3,2,1,0:T(8,128)(2,1)S(1)}, u32[]{:S(2)}, u32[]{:S(2)}) collective-permute-start(bf16[4,3,64,512]{3,2,1,0:T(8,128)(2,1)S(1)} %pass_on.3.refs_11_), channel_id=1, source_target_pairs={{0,1},{1,0},{2,3},{3,2},{4,5},{5,4},{6,7},{7,6},{8,9},{9,8},{10,11... | collective-permute-start | bytes 2359304 | tf_op jit(solution)/shard_map/ppermute | solution.py:349
  55.5 5.9 %collective-permute-start.21 = (bf16[1,3,64,256]{3,2,1,0:T(8,128)(2,1)S(1)}, bf16[1,3,64,256]{3,2,1,0:T(8,128)(2,1)S(1)}, u32[]{:S(2)}, u32[]{:S(2)}) collective-permute-start(bf16[1,3,64,256]{3,2,1,0:T(8,128)(2,1)S(1)} %pick_half.1), channel_id=1, source_target_pairs={{0,2},{1,3},{2,0},{3,1},{4,6},{5,7},{6,4},{7,5},{8,10},{9,11},{10,... | collective-permute-start | bytes 294920 | tf_op jit(solution)/shard_map/ppermute | solution.py:349
  61.4 1.3 %collective-permute-start.22 = (bf16[1,3,64,256]{3,2,1,0:T(8,128)(2,1)S(1)}, bf16[1,3,64,256]{3,2,1,0:T(8,128)(2,1)S(1)}, u32[]{:S(2)}, u32[]{:S(2)}) collective-permute-start(bf16[1,3,64,256]{3,2,1,0:T(8,128)(2,1)S(1)} %collective-permute-done.21.refs_15_), channel_id=1, source_target_pairs={{0,1},{1,0},{2,3},{3,2},{4,5},{5,4},{6,7},{7,6},{8,9},{9,8},{10,11... | collective-permute-start | bytes 294920 | tf_op jit(solution)/shard_map/ppermute | solution.py:349

commit v16 on v15

--- a/solution.py
+++ b/solution.py
@@ -423,10 +423,12 @@
         held = kernel(pass_on_kernel, columns(slots), role, values, "pass_on")
         return [held, swap(held, 1)]
 
-    def halves_across(cut):
+    def halves_across(cut, *earlier):
         beside = swap(cut, 1)
         half_shape = pltpu.VMEM(cut.shape[:3] + (block // 2,), jnp.bfloat16)
-        picked = kernel(pick_half_kernel, half_shape, role, [cut, beside], "pick_half")
+        picked = kernel(
+            pick_half_kernel, half_shape, after(role, *earlier), [cut, beside], "pick_half"
+        )
         across = swap(picked, 2)
         return [cut, beside, across, swap(across, 1)], picked
 
@@ -446,7 +448,7 @@
         cut_kernel, columns(2), after(half, projections), list(two), "cut_columns"
     )
     three = hop(*two)
-    crossed = cross(cut_two)
+    in_hbm += pass_on(cross(cut_two), role)
     half_shard = pltpu.VMEM(piece, jnp.bfloat16)
     cut_three, *halves = kernel(
         cut_last_kernel,
@@ -456,12 +458,12 @@
         "cut_columns",
     )
     far = hop(*halves)
+    in_vmem, picked = halves_across(cut_three)
     cut_four = kernel(
-        cut_far_kernel, columns(1), after(half, crossed[1]), list(far), "cut_columns"
-    )
-    last, picked = halves_across(cut_four)
-    in_vmem = pass_on(crossed + cross(cut_three), after(role, in_hbm[1], picked)) + last
-    groups = ((3, True, 2), (4, False, 2), (1, False, 4))
+        cut_far_kernel, columns(1), after(half, in_hbm[0], in_hbm[2], picked), list(far), "cut_columns"
+    )
+    in_vmem += halves_across(cut_four, in_vmem[2], in_hbm[1])[0]
+    groups = ((3, True, 2), (2, True, 2), (2, False, 4), (1, False, 4))
     rows = [own, *one, *two, *three, *far]
     covariance = pl.pallas_call(
         functools.partial(

time: 71.6 us -> 70.6 us (0.986); the launches traced: 71.2 us -> 69.2 us
  waiting for transfers between devices: 24.1 us -> 21.4 us
  local copies, waits for them, and re-layouts: 3.95 us -> 6.28 us
  Pallas kernels: 14.8 us -> 14 us
  starting transfers between devices: 27.5 us -> 26.7 us
    ppermute x4 -> x3, starting transfers between devices: 12.6 us -> 8.94 us  [cross(): return [cut, lax.ppermute(cut, axes, pairs(0, 2))]]
    ppermute x11 -> x14, starting transfers between devices: 6.69 us -> 9.54 us  [swap(): lax.ppermute(value, 'atoms', [(a, a ^ distance) for a in range(atom_axis)])]
    unnamed x14 -> x26, local copies, waits for them, and re-layouts: 3.95 us -> 6.28 us
    ppermute x11 -> x14, waiting for transfers between devices: 12.9 us -> 11.4 us  [swap(): lax.ppermute(value, 'atoms', [(a, a ^ distance) for a in range(atom_axis)])]
    ppermute x4, waiting for transfers between devices: 8.2 us -> 6.78 us  [hop(): lax.ppermute(down, 'frames', backward)]
    ppermute x4, waiting for transfers between devices: 1.24 us -> 2.63 us  [hop(): lax.ppermute(up, 'frames', forward)]
    ppermute x4 -> x3, waiting for transfers between devices: 1.74 us -> 0.62 us  [cross(): return [cut, lax.ppermute(cut, axes, pairs(0, 2))]]
    pallas_call x8 -> x9, Pallas kernels: 2.93 us -> 1.94 us  [kernel(): pl.pallas_call(body, out_shape=out_shape, in_specs=[SMEM] + [VMEM] * len(...]
  transfers between devices with their start and end apart: 23 -> 25, of which waited for: 14 -> 15; matrix products, arithmetic and copies ran while one was open for 0% -> 0% of each run, Pallas kernels for 4% -> 4%
where the time goes in v16:
time: 70.6 us; the launch traced here: 69.2 us
  starting transfers between devices  26.7 us (38%)
  waiting for transfers between devices  21.4 us (30%)
  Pallas kernels  14 us (20%)
  local copies, waits for them, and re-layouts  6.28 us (9%)
  between operations  0.86 us (1%)
    ppermute x14, waiting for transfers between devices, swap(): lax.ppermute(value, 'atoms', [(a, a ^ distance) for a in range(atom_axis)])  11.4 us
    ppermute x14, starting transfers between devices, swap(): lax.ppermute(value, 'atoms', [(a, a ^ distance) for a in range(atom_axis)])  9.54 us
    ppermute x3, starting transfers between devices, cross(): return [cut, lax.ppermute(cut, axes, pairs(0, 2))]  8.94 us
    pallas_call x1, Pallas kernels, per_device(): pl.pallas_call(functools.partial(covariance_kernel, frame_axis, atom_axis...  8.67 us
    ppermute x4, waiting for transfers between devices, hop(): lax.ppermute(down, 'frames', backward)  6.78 us
    unnamed x26, local copies, waits for them, and re-layouts  6.28 us
    ppermute x4, starting transfers between devices, hop(): lax.ppermute(down, 'frames', backward)  4.73 us
    ppermute x4, starting transfers between devices, hop(): lax.ppermute(up, 'frames', forward)  3.48 us
  transfers between devices with their start and end apart: 25, of which 15 were waited for; matrix products, arithmetic and copies ran while one was open for 0% of the time, Pallas kernels for 4%

profile of v16, /device:TPU:0, one launch (start us, length us, event | category | flops | bytes accessed | tf_op | source)
XLA Modules:
  0.0 69.2 jit_solution(7609534410372833730)
XLA Ops:
  0.6 1.7 %local_moments.1 = (f32[24,64]{1,0:T(8,128)S(1)}, f32[3,64,1024]{2,1,0:T(8,128)S(1)}, f32[3,1024]{1,0:T(4,128)S(1)}) custom-call(f32[3,64,1024]{2,1,0:T(8,128)} %bitcast.6, f32[3,1024]{1,0:T(4,128)} %ref_hbm.1), custom_call_target="tpu_custom_call" | custom-call | tf_op jit(solution)/shard_map/local_moments/pallas_call | solution.py:335
  2.3 2.4 %collective-permute-start.2 = (f32[24,64]{1,0:T(8,128)S(1)}, f32[24,64]{1,0:T(8,128)S(1)}, u32[]{:S(2)}, u32[]{:S(2)}) collective-permute-start(f32[24,64]{1,0:T(8,128)S(1)} %get-tuple-element.19.refs_0_), channel_id=1, source_target_pairs={{0,3},{1,2},{2,1},{3,0},{4,7},{5,6},{6,5},{7,4},{8,11},{9,10},{10,... | collective-permute-start | bytes 18440 | tf_op jit(solution)/shard_map/ppermute | solution.py:349
  4.7 0.6 collective-permute-start.1
  5.4 0.0 collective-permute-start
  5.4 0.7 %collective-permute-done.2.refs_3_ = f32[24,64]{1,0:T(8,128)S(1)} collective-permute-done((f32[24,64]{1,0:T(8,128)S(1)}, f32[24,64]{1,0:T(8,128)S(1)}, u32[]{:S(2)}, u32[]{:S(2)}) %collective-permute-start.2) | collective-permute-done | bytes 6176 | tf_op jit(solution)/shard_map/ppermute | solution.py:349
  6.1 2.3 %collective-permute-done.1.refs_2_ = f32[24,64]{1,0:T(8,128)S(1)} collective-permute-done((f32[24,64]{1,0:T(8,128)S(1)}, f32[24,64]{1,0:T(8,128)S(1)}, u32[]{:S(2)}, u32[]{:S(2)}) %collective-permute-start.1) | collective-permute-done | bytes 6176 | tf_op jit(solution)/shard_map/ppermute | solution.py:349
  8.4 0.0 collective-permute-done.refs_1_
  8.4 0.6 polar_align.1
  9.0 1.6 %collective-permute-start.3 = (bf16[2,3,256,128]{3,2,1,0:T(8,128)(2,1)S(1)}, bf16[2,3,256,128]{3,2,1,0:T(8,128)(2,1)S(1)}, u32[]{:S(2)}, u32[]{:S(2)}) collective-permute-start(bf16[2,3,256,128]{3,2,1,0:T(8,128)(2,1)S(1)} %get-tuple-element.22.refs_0_), channel_id=1, source_target_pairs={{0,8},{8,16},{16,24},{24,28},{28,20},{20,12},{12,4},{4,0},{1,9},{9... | collective-permute-start | bytes 1179656 | tf_op jit(solution)/shard_map/ppermute | solution.py:440
  10.7 0.4 collective-permute-start.4
  11.1 0.1 cut_columns.5.refs_0_
  11.3 2.6 %collective-permute-start.5 = (bf16[1,3,64,512]{3,2,1,0:T(8,128)(2,1)S(1)}, bf16[1,3,64,512]{3,2,1,0:T(8,128)(2,1)S(1)}, u32[]{:S(2)}, u32[]{:S(2)}) collective-permute-start(bf16[1,3,64,512]{3,2,1,0:T(8,128)(2,1)S(1)} %cut_columns.5.refs_0_), channel_id=1, source_target_pairs={{0,2},{4,6},{9,11},{13,15},{18,16},{22,20},{27,25},{31,29}} | collective-permute-start | bytes 589832 | tf_op jit(solution)/shard_map/ppermute | solution.py:419
  13.8 0.0 copy-start.1
  13.8 1.4 %copy-done.1 = bf16[3,1024,256]{2,1,0:T(8,128)(2,1)S(1)} copy-done((bf16[3,1024,256]{2,1,0:T(8,128)(2,1)S(1)}, bf16[3,1024,256]{2,1,0:T(8,128)(2,1)}, u32[]{:S(2)}) %copy-start.1) | copy-done | bytes 1572888
  15.2 0.5 project.1
  15.7 0.0 copy-start.3
  15.7 0.1 collective-permute-start.6
  15.8 0.1 collective-permute-start.7
  15.9 1.1 %collective-permute-done.6.refs_1_ = f32[64,64]{1,0:T(8,128)S(1)} collective-permute-done((f32[64,64]{1,0:T(8,128)S(1)}, f32[64,64]{1,0:T(8,128)S(1)}, u32[]{:S(2)}, u32[]{:S(2)}) %collective-permute-start.6) | collective-permute-done | bytes 16416 | tf_op jit(solution)/shard_map/ppermute | solution.py:349
  17.0 0.6 copy-done.5
  17.6 0.7 collective-permute-start.8
  18.3 1.5 %collective-permute-done.7.refs_2_ = f32[64,64]{1,0:T(8,128)S(1)} collective-permute-done((f32[64,64]{1,0:T(8,128)S(1)}, f32[64,64]{1,0:T(8,128)S(1)}, u32[]{:S(2)}, u32[]{:S(2)}) %collective-permute-start.7) | collective-permute-done | bytes 16416 | tf_op jit(solution)/shard_map/ppermute | solution.py:349
  19.8 0.6 copy-done.7
  20.4 0.6 collective-permute-done.8.refs_3_
  21.0 0.6 copy-done.9
  21.6 1.6 %collective-permute-start.10 = (bf16[2,3,256,128]{3,2,1,0:T(8,128)(2,1)S(1)}, bf16[2,3,256,128]{3,2,1,0:T(8,128)(2,1)S(1)}, u32[]{:S(2)}, u32[]{:S(2)}) collective-permute-start(bf16[2,3,256,128]{3,2,1,0:T(8,128)(2,1)S(1)} %collective-permute-done.4.refs_1_.refs_2_), channel_id=1, source_target_pairs={{8,0},{16,8},{24,16},{28,24},{20,28},{12,20},{4,12},{0,4},{9,1},{1... | collective-permute-start | bytes 1179656 | tf_op jit(solution)/shard_map/ppermute | solution.py:440
  23.2 0.5 collective-permute-start.9
  23.7 0.2 cut_columns.6.refs_2_
  23.9 3.6 %collective-permute-start.13 = (bf16[2,3,64,512]{3,2,1,0:T(8,128)(2,1)S(1)}, bf16[2,3,64,512]{3,2,1,0:T(8,128)(2,1)}, u32[]{:S(2)}, u32[]{:S(2)}) collective-permute-start(bf16[2,3,64,512]{3,2,1,0:T(8,128)(2,1)S(1)} %cut_columns.6.refs_2_), channel_id=1, source_target_pairs={{0,2},{4,6},{9,11},{13,15},{18,16},{22,20},{27,25},{31,29}} | collective-permute-start | bytes 1179656 | tf_op jit(solution)/shard_map/ppermute | solution.py:419
  27.4 5.4 %collective-permute-done.10.refs_1_.refs_4_ = bf16[2,3,256,128]{3,2,1,0:T(8,128)(2,1)S(1)} collective-permute-done((bf16[2,3,256,128]{3,2,1,0:T(8,128)(2,1)S(1)}, bf16[2,3,256,128]{3,2,1,0:T(8,128)(2,1)S(1)}, u32[]{:S(2)}, u32[]{:S(2)}) %collective-permute-start.10) | collective-permute-done | bytes 393248 | tf_op jit(solution)/shard_map/ppermute | solution.py:440
  32.8 1.5 %collective-permute-start.12 = (bf16[2,3,256,128]{3,2,1,0:T(8,128)(2,1)S(1)}, bf16[2,3,256,128]{3,2,1,0:T(8,128)(2,1)S(1)}, u32[]{:S(2)}, u32[]{:S(2)}) collective-permute-start(bf16[2,3,256,128]{3,2,1,0:T(8,128)(2,1)S(1)} %collective-permute-done.10.refs_1_.refs_4_), channel_id=1, source_target_pairs={{8,0},{16,8},{24,16},{28,24},{20,28},{12,20},{4,12},{0,4},{9,1},{1... | collective-permute-start | bytes 1179656 | tf_op jit(solution)/shard_map/ppermute | solution.py:440
  34.4 0.5 collective-permute-start.11
  34.9 0.8 %copy-done.4 = f32[64,64]{1,0:T(8,128)S(1)} copy-done((f32[64,64]{1,0:T(8,128)S(1)}, f32[64,64]{1,0:T(8,128)}, u32[]{:S(2)}) %copy-start.4) | copy-done | bytes 16408
  35.6 0.8 %copy-done.6 = f32[64,64]{1,0:T(8,128)S(1)} copy-done((f32[64,64]{1,0:T(8,128)S(1)}, f32[64,64]{1,0:T(8,128)}, u32[]{:S(2)}) %copy-start.6) | copy-done | bytes 16408
  36.4 0.8 %copy-done.8 = f32[64,64]{1,0:T(8,128)S(1)} copy-done((f32[64,64]{1,0:T(8,128)S(1)}, f32[64,64]{1,0:T(8,128)}, u32[]{:S(2)}) %copy-start.8) | copy-done | bytes 16408
  37.1 0.8 %copy-done.10 = f32[64,64]{1,0:T(8,128)S(1)} copy-done((f32[64,64]{1,0:T(8,128)S(1)}, f32[64,64]{1,0:T(8,128)}, u32[]{:S(2)}) %copy-start.10) | copy-done | bytes 16408
  37.9 0.6 sum_shares.1
  38.5 0.0 collective-permute-done.13.refs_3_
  38.5 1.0 %pass_on.2.refs_9_ = bf16[3,3,64,512]{3,2,1,0:T(8,128)(2,1)S(1)} custom-call(s32[1]{0:T(128)} %bitcast.role_ref, bf16[1,3,64,512]{3,2,1,0:T(8,128)(2,1)S(1)} %cut_columns.5.refs_0_, bf16[1,3,64,512]{3,2,1,0:T(8,128)(2,1)S(1)} %collective-permute-done.5.refs_1_, bf16[2,3,64,512]{3,2,1,0:T(8,128)(2,1)S(1)} %cut_columns.6.refs_2_, ...), custom_call_target="tpu_custom_call" | custom-call | tf_op jit(solution)/shard_map/pass_on/pallas_call | solution.py:409
  39.6 0.2 cut_columns.8.refs_0_
  39.8 2.8 %collective-permute-start.17 = (bf16[2,3,64,512]{3,2,1,0:T(8,128)(2,1)S(1)}, bf16[2,3,64,512]{3,2,1,0:T(8,128)(2,1)S(1)}, u32[]{:S(2)}, u32[]{:S(2)}) collective-permute-start(bf16[2,3,64,512]{3,2,1,0:T(8,128)(2,1)S(1)} %cut_columns.8.refs_0_), channel_id=1, source_target_pairs={{0,2},{4,6},{9,11},{13,15},{18,16},{22,20},{27,25},{31,29}} | collective-permute-start | bytes 1179656 | tf_op jit(solution)/shard_map/ppermute | solution.py:419
  42.6 0.8 %collective-permute-done.12.down_ref.refs_6_ = bf16[2,3,256,128]{3,2,1,0:T(8,128)(2,1)S(1)} collective-permute-done((bf16[2,3,256,128]{3,2,1,0:T(8,128)(2,1)S(1)}, bf16[2,3,256,128]{3,2,1,0:T(8,128)(2,1)S(1)}, u32[]{:S(2)}, u32[]{:S(2)}) %collective-permute-start.12) | collective-permute-done | bytes 393248 | tf_op jit(solution)/shard_map/ppermute | solution.py:440
  43.4 1.0 %collective-permute-done.11.up_ref.refs_5_ = bf16[2,3,256,128]{3,2,1,0:T(8,128)(2,1)S(1)} collective-permute-done((bf16[2,3,256,128]{3,2,1,0:T(8,128)(2,1)S(1)}, bf16[2,3,256,128]{3,2,1,0:T(8,128)(2,1)S(1)}, u32[]{:S(2)}, u32[]{:S(2)}) %collective-permute-start.11) | collective-permute-done | bytes 393248 | tf_op jit(solution)/shard_map/ppermute | solution.py:440
  44.4 0.2 cut_columns.7
  44.6 0.1 collective-permute-start.19
  44.7 0.5 collective-permute-start.16
  45.2 0.8 %collective-permute-start.14 = (bf16[3,256,128]{2,1,0:T(8,128)(2,1)S(1)}, bf16[3,256,128]{2,1,0:T(8,128)(2,1)S(1)}, u32[]{:S(2)}, u32[]{:S(2)}) collective-permute-start(bf16[3,256,128]{2,1,0:T(8,128)(2,1)S(1)} %get-tuple-element.30), channel_id=1, source_target_pairs={{0,8},{8,16},{16,24},{24,28},{28,20},{20,12},{12,4},{4,0},{1,9},{9... | collective-permute-start | bytes 589832 | tf_op jit(solution)/shard_map/ppermute | solution.py:440
  46.0 1.2 %collective-permute-start.15 = (bf16[3,256,128]{2,1,0:T(8,128)(2,1)S(1)}, bf16[3,256,128]{2,1,0:T(8,128)(2,1)S(1)}, u32[]{:S(2)}, u32[]{:S(2)}) collective-permute-start(bf16[3,256,128]{2,1,0:T(8,128)(2,1)S(1)} %get-tuple-element.31), channel_id=1, source_target_pairs={{8,0},{16,8},{24,16},{28,24},{20,28},{12,20},{4,12},{0,4},{9,1},{1... | collective-permute-start | bytes 589832 | tf_op jit(solution)/shard_map/ppermute | solution.py:440
  47.2 0.6 collective-permute-done.17.refs_1_
  47.9 0.0 collective-permute-done.19.beside_ref.refs_14_
  47.9 2.5 %collective-permute-start.20 = (bf16[2,3,64,256]{3,2,1,0:T(8,128)(2,1)S(1)}, bf16[2,3,64,256]{3,2,1,0:T(8,128)(2,1)S(1)}, u32[]{:S(2)}, u32[]{:S(2)}) collective-permute-start(bf16[2,3,64,256]{3,2,1,0:T(8,128)(2,1)S(1)} %pick_half.2), channel_id=1, source_target_pairs={{0,2},{1,3},{2,0},{3,1},{4,6},{5,7},{6,4},{7,5},{8,10},{9,11},{10,... | collective-permute-start | bytes 589832 | tf_op jit(solution)/shard_map/ppermute | solution.py:349
  50.5 1.6 %collective-permute-done.14.up_half.refs_7_ = bf16[3,256,128]{2,1,0:T(8,128)(2,1)S(1)} collective-permute-done((bf16[3,256,128]{2,1,0:T(8,128)(2,1)S(1)}, bf16[3,256,128]{2,1,0:T(8,128)(2,1)S(1)}, u32[]{:S(2)}, u32[]{:S(2)}) %collective-permute-start.14) | collective-permute-done | bytes 196640 | tf_op jit(solution)/shard_map/ppermute | solution.py:440
  52.1 0.5 collective-permute-done.15.down_half.refs_8_
  52.6 0.1 cut_columns.9.own_ref.refs_17_
  52.8 0.1 collective-permute-start.22
  52.9 0.5 collective-permute-start.18
  53.4 0.0 collective-permute-done.16.refs_10_
  53.4 0.8 %collective-permute-done.20.refs_15_ = bf16[2,3,64,256]{3,2,1,0:T(8,128)(2,1)S(1)} collective-permute-done((bf16[2,3,64,256]{3,2,1,0:T(8,128)(2,1)S(1)}, bf16[2,3,64,256]{3,2,1,0:T(8,128)(2,1)S(1)}, u32[]{:S(2)}, u32[]{:S(2)}) %collective-permute-start.20) | collective-permute-done | bytes 196640 | tf_op jit(solution)/shard_map/ppermute | solution.py:349
  54.1 0.2 collective-permute-done.22.beside_ref.refs_18_
  54.3 1.9 %collective-permute-start.23 = (bf16[1,3,64,256]{3,2,1,0:T(8,128)(2,1)S(1)}, bf16[1,3,64,256]{3,2,1,0:T(8,128)(2,1)S(1)}, u32[]{:S(2)}, u32[]{:S(2)}) collective-permute-start(bf16[1,3,64,256]{3,2,1,0:T(8,128)(2,1)S(1)} %pick_half.3), channel_id=1, source_target_pairs={{0,2},{1,3},{2,0},{3,1},{4,6},{5,7},{6,4},{7,5},{8,10},{9,11},{10,... | collective-permute-start | bytes 294920 | tf_op jit(solution)/shard_map/ppermute | solution.py:349
  56.2 0.0 collective-permute-start.21
  56.2 2.9 %collective-permute-done.23.refs_19_ = bf16[1,3,64,256]{3,2,1,0:T(8,128)(2,1)S(1)} collective-permute-done((bf16[1,3,64,256]{3,2,1,0:T(8,128)(2,1)S(1)}, bf16[1,3,64,256]{3,2,1,0:T(8,128)(2,1)S(1)}, u32[]{:S(2)}, u32[]{:S(2)}) %collective-permute-start.23) | collective-permute-done | bytes 98336 | tf_op jit(solution)/shard_map/ppermute | solution.py:349
  59.2 1.3 %collective-permute-done.24.refs_20_ = bf16[1,3,64,256]{3,2,1,0:T(8,128)(2,1)S(1)} collective-permute-done((bf16[1,3,64,256]{3,2,1,0:T(8,128)(2,1)S(1)}, bf16[1,3,64,256]{3,2,1,0:T(8,128)(2,1)S(1)}, u32[]{:S(2)}, u32[]{:S(2)}) %collective-permute-start.24) | collective-permute-done | bytes 98336 | tf_op jit(solution)/shard_map/ppermute | solution.py:349
  60.5 8.7 %covariance_tile.1 = f32[3,3,1024,512]{3,2,1,0:T(8,128)} custom-call(s32[1]{0:T(128)} %bitcast.role_ref, bf16[2,3,256,128]{3,2,1,0:T(8,128)(2,1)S(1)} %get-tuple-element.22.refs_0_, bf16[2,3,256,128]{3,2,1,0:T(8,128)(2,1)S(1)} %collective-permute-done.3.refs_0_.refs_1_, bf16[2,3,256,128]{3,2,1,0:T(8,128)(2,1)S(1)} %collective-permute-done.4.refs_1_.refs_2_, ...), custom_call_target="tpu_custom_call" | custom-call | flops 4831838208 | bytes 25165824 | tf_op jit(solution)/shard_map/covariance_tile/pallas_call | solution.py:468
  (26 shorter events, 0.1 us)
Async XLA Ops:
  2.3 3.8 %collective-permute-start.2 = (f32[24,64]{1,0:T(8,128)S(1)}, f32[24,64]{1,0:T(8,128)S(1)}, u32[]{:S(2)}, u32[]{:S(2)}) collective-permute-start(f32[24,64]{1,0:T(8,128)S(1)} %get-tuple-element.19.refs_0_), channel_id=1, source_target_pairs={{0,3},{1,2},{2,1},{3,0},{4,7},{5,6},{6,5},{7,4},{8,11},{9,10},{10,... | collective-permute-start | bytes 18440 | tf_op jit(solution)/shard_map/ppermute | solution.py:349
  4.7 3.7 %collective-permute-start.1 = (f32[24,64]{1,0:T(8,128)S(1)}, f32[24,64]{1,0:T(8,128)S(1)}, u32[]{:S(2)}, u32[]{:S(2)}) collective-permute-start(f32[24,64]{1,0:T(8,128)S(1)} %get-tuple-element.19.refs_0_), channel_id=1, source_target_pairs={{0,2},{1,3},{2,0},{3,1},{4,6},{5,7},{6,4},{7,5},{8,10},{9,11},{10,... | collective-permute-start | bytes 18440 | tf_op jit(solution)/shard_map/ppermute | solution.py:349
  5.4 3.1 %collective-permute-start = (f32[24,64]{1,0:T(8,128)S(1)}, f32[24,64]{1,0:T(8,128)S(1)}, u32[]{:S(2)}, u32[]{:S(2)}) collective-permute-start(f32[24,64]{1,0:T(8,128)S(1)} %get-tuple-element.19.refs_0_), channel_id=1, source_target_pairs={{0,1},{1,0},{2,3},{3,2},{4,5},{5,4},{6,7},{7,6},{8,9},{9,8},{10,11... | collective-permute-start | bytes 18440 | tf_op jit(solution)/shard_map/ppermute | solution.py:349
  9.0 12.5 %collective-permute-start.3 = (bf16[2,3,256,128]{3,2,1,0:T(8,128)(2,1)S(1)}, bf16[2,3,256,128]{3,2,1,0:T(8,128)(2,1)S(1)}, u32[]{:S(2)}, u32[]{:S(2)}) collective-permute-start(bf16[2,3,256,128]{3,2,1,0:T(8,128)(2,1)S(1)} %get-tuple-element.22.refs_0_), channel_id=1, source_target_pairs={{0,8},{8,16},{16,24},{24,28},{28,20},{20,12},{12,4},{4,0},{1,9},{9... | collective-permute-start | bytes 1179656 | tf_op jit(solution)/shard_map/ppermute | solution.py:440
  10.7 10.9 %collective-permute-start.4 = (bf16[2,3,256,128]{3,2,1,0:T(8,128)(2,1)S(1)}, bf16[2,3,256,128]{3,2,1,0:T(8,128)(2,1)S(1)}, u32[]{:S(2)}, u32[]{:S(2)}) collective-permute-start(bf16[2,3,256,128]{3,2,1,0:T(8,128)(2,1)S(1)} %get-tuple-element.22.refs_0_), channel_id=1, source_target_pairs={{8,0},{16,8},{24,16},{28,24},{20,28},{12,20},{4,12},{0,4},{9,1},{1... | collective-permute-start | bytes 1179656 | tf_op jit(solution)/shard_map/ppermute | solution.py:440
  11.3 10.3 %collective-permute-start.5 = (bf16[1,3,64,512]{3,2,1,0:T(8,128)(2,1)S(1)}, bf16[1,3,64,512]{3,2,1,0:T(8,128)(2,1)S(1)}, u32[]{:S(2)}, u32[]{:S(2)}) collective-permute-start(bf16[1,3,64,512]{3,2,1,0:T(8,128)(2,1)S(1)} %cut_columns.5.refs_0_), channel_id=1, source_target_pairs={{0,2},{4,6},{9,11},{13,15},{18,16},{22,20},{27,25},{31,29}} | collective-permute-start | bytes 589832 | tf_op jit(solution)/shard_map/ppermute | solution.py:419
  13.8 1.4 %copy-start.1 = (bf16[3,1024,256]{2,1,0:T(8,128)(2,1)S(1)}, bf16[3,1024,256]{2,1,0:T(8,128)(2,1)}, u32[]{:S(2)}) copy-start(bf16[3,1024,256]{2,1,0:T(8,128)(2,1)} %eig_ref.1) | copy-start | bytes 4718596
  15.7 18.6 %copy-start.3 = (f32[64,64]{1,0:T(8,128)}, f32[64,64]{1,0:T(8,128)S(1)}, u32[]{:S(2)}) copy-start(f32[64,64]{1,0:T(8,128)S(1)} %get-tuple-element.24.refs_0_) | copy-start | bytes 49156
  15.7 1.3 %collective-permute-start.6 = (f32[64,64]{1,0:T(8,128)S(1)}, f32[64,64]{1,0:T(8,128)S(1)}, u32[]{:S(2)}, u32[]{:S(2)}) collective-permute-start(f32[64,64]{1,0:T(8,128)S(1)} %get-tuple-element.25), channel_id=1, source_target_pairs={{0,1},{1,0},{2,3},{3,2},{4,5},{5,4},{6,7},{7,6},{8,9},{9,8},{10,11... | collective-permute-start | bytes 49160 | tf_op jit(solution)/shard_map/ppermute | solution.py:349
  15.8 4.0 %collective-permute-start.7 = (f32[64,64]{1,0:T(8,128)S(1)}, f32[64,64]{1,0:T(8,128)S(1)}, u32[]{:S(2)}, u32[]{:S(2)}) collective-permute-start(f32[64,64]{1,0:T(8,128)S(1)} %get-tuple-element.26), channel_id=1, source_target_pairs={{0,2},{1,3},{2,0},{3,1},{4,6},{5,7},{6,4},{7,5},{8,10},{9,11},{10,... | collective-permute-start | bytes 49160 | tf_op jit(solution)/shard_map/ppermute | solution.py:349
  17.0 0.6 copy-start.5
  17.6 3.3 %collective-permute-start.8 = (f32[64,64]{1,0:T(8,128)S(1)}, f32[64,64]{1,0:T(8,128)S(1)}, u32[]{:S(2)}, u32[]{:S(2)}) collective-permute-start(f32[64,64]{1,0:T(8,128)S(1)} %get-tuple-element.27), channel_id=1, source_target_pairs={{0,3},{1,2},{2,1},{3,0},{4,7},{5,6},{6,5},{7,4},{8,11},{9,10},{10,... | collective-permute-start | bytes 49160 | tf_op jit(solution)/shard_map/ppermute | solution.py:349
  19.8 0.6 copy-start.7
  21.0 0.6 copy-start.9
  21.6 11.2 %collective-permute-start.10 = (bf16[2,3,256,128]{3,2,1,0:T(8,128)(2,1)S(1)}, bf16[2,3,256,128]{3,2,1,0:T(8,128)(2,1)S(1)}, u32[]{:S(2)}, u32[]{:S(2)}) collective-permute-start(bf16[2,3,256,128]{3,2,1,0:T(8,128)(2,1)S(1)} %collective-permute-done.4.refs_1_.refs_2_), channel_id=1, source_target_pairs={{8,0},{16,8},{24,16},{28,24},{20,28},{12,20},{4,12},{0,4},{9,1},{1... | collective-permute-start | bytes 1179656 | tf_op jit(solution)/shard_map/ppermute | solution.py:440
  23.2 11.2 %collective-permute-start.9 = (bf16[2,3,256,128]{3,2,1,0:T(8,128)(2,1)S(1)}, bf16[2,3,256,128]{3,2,1,0:T(8,128)(2,1)S(1)}, u32[]{:S(2)}, u32[]{:S(2)}) collective-permute-start(bf16[2,3,256,128]{3,2,1,0:T(8,128)(2,1)S(1)} %collective-permute-done.3.refs_0_.refs_1_), channel_id=1, source_target_pairs={{0,8},{8,16},{16,24},{24,28},{28,20},{20,12},{12,4},{4,0},{1,9},{9... | collective-permute-start | bytes 1179656 | tf_op jit(solution)/shard_map/ppermute | solution.py:440
  23.9 14.7 %collective-permute-start.13 = (bf16[2,3,64,512]{3,2,1,0:T(8,128)(2,1)S(1)}, bf16[2,3,64,512]{3,2,1,0:T(8,128)(2,1)}, u32[]{:S(2)}, u32[]{:S(2)}) collective-permute-start(bf16[2,3,64,512]{3,2,1,0:T(8,128)(2,1)S(1)} %cut_columns.6.refs_2_), channel_id=1, source_target_pairs={{0,2},{4,6},{9,11},{13,15},{18,16},{22,20},{27,25},{31,29}} | collective-permute-start | bytes 1179656 | tf_op jit(solution)/shard_map/ppermute | solution.py:419
  32.8 10.6 %collective-permute-start.12 = (bf16[2,3,256,128]{3,2,1,0:T(8,128)(2,1)S(1)}, bf16[2,3,256,128]{3,2,1,0:T(8,128)(2,1)S(1)}, u32[]{:S(2)}, u32[]{:S(2)}) collective-permute-start(bf16[2,3,256,128]{3,2,1,0:T(8,128)(2,1)S(1)} %collective-permute-done.10.refs_1_.refs_4_), channel_id=1, source_target_pairs={{8,0},{16,8},{24,16},{28,24},{20,28},{12,20},{4,12},{0,4},{9,1},{1... | collective-permute-start | bytes 1179656 | tf_op jit(solution)/shard_map/ppermute | solution.py:440
  34.4 10.1 %collective-permute-start.11 = (bf16[2,3,256,128]{3,2,1,0:T(8,128)(2,1)S(1)}, bf16[2,3,256,128]{3,2,1,0:T(8,128)(2,1)S(1)}, u32[]{:S(2)}, u32[]{:S(2)}) collective-permute-start(bf16[2,3,256,128]{3,2,1,0:T(8,128)(2,1)S(1)} %collective-permute-done.9.refs_0_.refs_3_), channel_id=1, source_target_pairs={{0,8},{8,16},{16,24},{24,28},{28,20},{20,12},{12,4},{4,0},{1,9},{9... | collective-permute-start | bytes 1179656 | tf_op jit(solution)/shard_map/ppermute | solution.py:440
  34.9 0.8 %copy-start.4 = (f32[64,64]{1,0:T(8,128)S(1)}, f32[64,64]{1,0:T(8,128)}, u32[]{:S(2)}) copy-start(f32[64,64]{1,0:T(8,128)} %copy-done.3) | copy-start | bytes 49156
  35.6 0.8 %copy-start.6 = (f32[64,64]{1,0:T(8,128)S(1)}, f32[64,64]{1,0:T(8,128)}, u32[]{:S(2)}) copy-start(f32[64,64]{1,0:T(8,128)} %copy-done.5) | copy-start | bytes 49156
  36.4 0.8 %copy-start.8 = (f32[64,64]{1,0:T(8,128)S(1)}, f32[64,64]{1,0:T(8,128)}, u32[]{:S(2)}) copy-start(f32[64,64]{1,0:T(8,128)} %copy-done.7) | copy-start | bytes 49156
  37.1 0.8 %copy-start.10 = (f32[64,64]{1,0:T(8,128)S(1)}, f32[64,64]{1,0:T(8,128)}, u32[]{:S(2)}) copy-start(f32[64,64]{1,0:T(8,128)} %copy-done.9) | copy-start | bytes 49156
  39.6 20.9 %copy-start = (bf16[3,3,64,512]{3,2,1,0:T(8,128)(2,1)}, bf16[3,3,64,512]{3,2,1,0:T(8,128)(2,1)S(1)}, u32[]{:S(2)}) copy-start(bf16[3,3,64,512]{3,2,1,0:T(8,128)(2,1)S(1)} %pass_on.2.refs_9_) | copy-start | bytes 1769476
  39.8 8.1 %collective-permute-start.17 = (bf16[2,3,64,512]{3,2,1,0:T(8,128)(2,1)S(1)}, bf16[2,3,64,512]{3,2,1,0:T(8,128)(2,1)S(1)}, u32[]{:S(2)}, u32[]{:S(2)}) collective-permute-start(bf16[2,3,64,512]{3,2,1,0:T(8,128)(2,1)S(1)} %cut_columns.8.refs_0_), channel_id=1, source_target_pairs={{0,2},{4,6},{9,11},{13,15},{18,16},{22,20},{27,25},{31,29}} | collective-permute-start | bytes 1179656 | tf_op jit(solution)/shard_map/ppermute | solution.py:419
  44.6 3.3 %collective-permute-start.19 = (bf16[2,3,64,512]{3,2,1,0:T(8,128)(2,1)S(1)}, bf16[2,3,64,512]{3,2,1,0:T(8,128)(2,1)S(1)}, u32[]{:S(2)}, u32[]{:S(2)}) collective-permute-start(bf16[2,3,64,512]{3,2,1,0:T(8,128)(2,1)S(1)} %get-tuple-element.33.own_ref.refs_13_), channel_id=1, source_target_pairs={{0,1},{1,0},{2,3},{3,2},{4,5},{5,4},{6,7},{7,6},{8,9},{9,8},{10,11... | collective-permute-start | bytes 1179656 | tf_op jit(solution)/shard_map/ppermute | solution.py:349
  44.7 8.7 %collective-permute-start.16 = (bf16[3,3,64,512]{3,2,1,0:T(8,128)(2,1)S(1)}, bf16[3,3,64,512]{3,2,1,0:T(8,128)(2,1)S(1)}, u32[]{:S(2)}, u32[]{:S(2)}) collective-permute-start(bf16[3,3,64,512]{3,2,1,0:T(8,128)(2,1)S(1)} %pass_on.2.refs_9_), channel_id=1, source_target_pairs={{0,1},{1,0},{2,3},{3,2},{4,5},{5,4},{6,7},{7,6},{8,9},{9,8},{10,11... | collective-permute-start | bytes 1769480 | tf_op jit(solution)/shard_map/ppermute | solution.py:349
  45.2 6.9 %collective-permute-start.14 = (bf16[3,256,128]{2,1,0:T(8,128)(2,1)S(1)}, bf16[3,256,128]{2,1,0:T(8,128)(2,1)S(1)}, u32[]{:S(2)}, u32[]{:S(2)}) collective-permute-start(bf16[3,256,128]{2,1,0:T(8,128)(2,1)S(1)} %get-tuple-element.30), channel_id=1, source_target_pairs={{0,8},{8,16},{16,24},{24,28},{28,20},{20,12},{12,4},{4,0},{1,9},{9... | collective-permute-start | bytes 589832 | tf_op jit(solution)/shard_map/ppermute | solution.py:440
  46.0 6.6 %collective-permute-start.15 = (bf16[3,256,128]{2,1,0:T(8,128)(2,1)S(1)}, bf16[3,256,128]{2,1,0:T(8,128)(2,1)S(1)}, u32[]{:S(2)}, u32[]{:S(2)}) collective-permute-start(bf16[3,256,128]{2,1,0:T(8,128)(2,1)S(1)} %get-tuple-element.31), channel_id=1, source_target_pairs={{8,0},{16,8},{24,16},{28,24},{20,28},{12,20},{4,12},{0,4},{9,1},{1... | collective-permute-start | bytes 589832 | tf_op jit(solution)/shard_map/ppermute | solution.py:440
  47.9 12.6 %copy-start.2 = (bf16[2,3,64,512]{3,2,1,0:T(8,128)(2,1)}, bf16[2,3,64,512]{3,2,1,0:T(8,128)(2,1)S(1)}, u32[]{:S(2)}) copy-start(bf16[2,3,64,512]{3,2,1,0:T(8,128)(2,1)S(1)} %pass_on.3.refs_11_) | copy-start | bytes 1179652
  47.9 6.2 %collective-permute-start.20 = (bf16[2,3,64,256]{3,2,1,0:T(8,128)(2,1)S(1)}, bf16[2,3,64,256]{3,2,1,0:T(8,128)(2,1)S(1)}, u32[]{:S(2)}, u32[]{:S(2)}) collective-permute-start(bf16[2,3,64,256]{3,2,1,0:T(8,128)(2,1)S(1)} %pick_half.2), channel_id=1, source_target_pairs={{0,2},{1,3},{2,0},{3,1},{4,6},{5,7},{6,4},{7,5},{8,10},{9,11},{10,... | collective-permute-start | bytes 589832 | tf_op jit(solution)/shard_map/ppermute | solution.py:349
  52.8 1.5 %collective-permute-start.22 = (bf16[1,3,64,512]{3,2,1,0:T(8,128)(2,1)S(1)}, bf16[1,3,64,512]{3,2,1,0:T(8,128)(2,1)S(1)}, u32[]{:S(2)}, u32[]{:S(2)}) collective-permute-start(bf16[1,3,64,512]{3,2,1,0:T(8,128)(2,1)S(1)} %cut_columns.9.own_ref.refs_17_), channel_id=1, source_target_pairs={{0,1},{1,0},{2,3},{3,2},{4,5},{5,4},{6,7},{7,6},{8,9},{9,8},{10,11... | collective-permute-start | bytes 589832 | tf_op jit(solution)/shard_map/ppermute | solution.py:349
  52.9 6.3 %collective-permute-start.18 = (bf16[2,3,64,512]{3,2,1,0:T(8,128)(2,1)S(1)}, bf16[2,3,64,512]{3,2,1,0:T(8,128)(2,1)S(1)}, u32[]{:S(2)}, u32[]{:S(2)}) collective-permute-start(bf16[2,3,64,512]{3,2,1,0:T(8,128)(2,1)S(1)} %pass_on.3.refs_11_), channel_id=1, source_target_pairs={{0,1},{1,0},{2,3},{3,2},{4,5},{5,4},{6,7},{7,6},{8,9},{9,8},{10,11... | collective-permute-start | bytes 1179656 | tf_op jit(solution)/shard_map/ppermute | solution.py:349
  53.4 7.1 %copy-start.11 = (bf16[3,3,64,512]{3,2,1,0:T(8,128)(2,1)}, bf16[3,3,64,512]{3,2,1,0:T(8,128)(2,1)S(1)}, u32[]{:S(2)}) copy-start(bf16[3,3,64,512]{3,2,1,0:T(8,128)(2,1)S(1)} %collective-permute-done.16.refs_10_) | copy-start | bytes 1769476
  54.3 4.9 %collective-permute-start.23 = (bf16[1,3,64,256]{3,2,1,0:T(8,128)(2,1)S(1)}, bf16[1,3,64,256]{3,2,1,0:T(8,128)(2,1)S(1)}, u32[]{:S(2)}, u32[]{:S(2)}) collective-permute-start(bf16[1,3,64,256]{3,2,1,0:T(8,128)(2,1)S(1)} %pick_half.3), channel_id=1, source_target_pairs={{0,2},{1,3},{2,0},{3,1},{4,6},{5,7},{6,4},{7,5},{8,10},{9,11},{10,... | collective-permute-start | bytes 294920 | tf_op jit(solution)/shard_map/ppermute | solution.py:349
  56.2 4.2 %collective-permute-start.21 = (bf16[2,3,64,256]{3,2,1,0:T(8,128)(2,1)S(1)}, bf16[2,3,64,256]{3,2,1,0:T(8,128)(2,1)S(1)}, u32[]{:S(2)}, u32[]{:S(2)}) collective-permute-start(bf16[2,3,64,256]{3,2,1,0:T(8,128)(2,1)S(1)} %collective-permute-done.20.refs_15_), channel_id=1, source_target_pairs={{0,1},{1,0},{2,3},{3,2},{4,5},{5,4},{6,7},{7,6},{8,9},{9,8},{10,11... | collective-permute-start | bytes 589832 | tf_op jit(solution)/shard_map/ppermute | solution.py:349
  59.2 1.3 %collective-permute-start.24 = (bf16[1,3,64,256]{3,2,1,0:T(8,128)(2,1)S(1)}, bf16[1,3,64,256]{3,2,1,0:T(8,128)(2,1)S(1)}, u32[]{:S(2)}, u32[]{:S(2)}) collective-permute-start(bf16[1,3,64,256]{3,2,1,0:T(8,128)(2,1)S(1)} %collective-permute-done.23.refs_19_), channel_id=1, source_target_pairs={{0,1},{1,0},{2,3},{3,2},{4,5},{5,4},{6,7},{7,6},{8,9},{9,8},{10,11... | collective-permute-start | bytes 294920 | tf_op jit(solution)/shard_map/ppermute | solution.py:349
  59.2 1.3 %copy-start.12 = (bf16[2,3,64,512]{3,2,1,0:T(8,128)(2,1)}, bf16[2,3,64,512]{3,2,1,0:T(8,128)(2,1)S(1)}, u32[]{:S(2)}) copy-start(bf16[2,3,64,512]{3,2,1,0:T(8,128)(2,1)S(1)} %collective-permute-done.18.refs_12_) | copy-start | bytes 1179652

commit v17 on v16

--- a/solution.py
+++ b/solution.py
@@ -128,10 +128,6 @@
         share[...] = cut[lax.bitwise_xor(me_ref[0], k)]
 
 
-def sum_kernel(*refs):
-    refs[-1][...] = sum(ref[...] for ref in refs[:-1])
-
-
 def cut_columns(half_ref, halves, cols_ref):
     for half in range(2):
 
@@ -197,7 +193,13 @@
     for _, _, count in groups:
         arrays.append(refs[:count])
         refs = refs[count:]
-    out_ref, left, right, done, col_sem, out_sem = refs
+    shares, refs = refs[:roles], refs[roles:]
+    out_ref, proj_ref, left, right, done, held, col_sem, out_sem, share_sem = refs
+    sums = [
+        pltpu.make_async_copy(part, held.at[k], share_sem.at[k]) for k, part in enumerate(shares)
+    ]
+    for copy in sums:
+        copy.start()
     depth = right.shape[1] // slots
     run = up_half.shape[1]
 
@@ -266,6 +268,9 @@
     for_each_group(False, load)
     assemble(0, 0)
     for_each_group(True, wait)
+    for copy in sums:
+        copy.wait()
+    proj_ref[...] = sum(held[k] for k in range(roles))
 
     def write(c, at, d):
         return pltpu.make_async_copy(
@@ -374,15 +379,6 @@
         name="project",
     )(me_a.astype(jnp.int32).reshape(1), flat, eigvecs)
     parts = [shares[0]] + [swap(shares[d], d) for d in range(1, atom_axis)]
-    projections = pl.pallas_call(
-        sum_kernel,
-        out_shape=share,
-        in_specs=[VMEM] * atom_axis,
-        out_specs=VMEM,
-        compiler_params=params(4),
-        name="sum_shares",
-    )(*parts)
-
     def pairs(source, target):
         return [
             (
@@ -393,6 +389,7 @@
         ]
 
     if blocks != 2 or frame_axis != 8:
+        projections = sum(parts)
         spread_pairs = [pairs(0, d) for d in range(1, atom_axis)]
         covariance = long_axis_covariance(
             flat, half[0], role[0], block, spread_pairs, 1.0 / total_frames
@@ -444,9 +441,7 @@
     cut_one = kernel(cut_kernel, columns(2), half, list(one), "cut_columns")
     two = hop(after(one[0], crossed[1], *parts), one[1])
     in_hbm = pass_on(crossed + cross(cut_one), role)
-    cut_two = kernel(
-        cut_kernel, columns(2), after(half, projections), list(two), "cut_columns"
-    )
+    cut_two = kernel(cut_kernel, columns(2), half, list(two), "cut_columns")
     three = hop(*two)
     in_hbm += pass_on(cross(cut_two), role)
     half_shard = pltpu.VMEM(piece, jnp.bfloat16)
@@ -460,27 +455,30 @@
     far = hop(*halves)
     in_vmem, picked = halves_across(cut_three)
     cut_four = kernel(
-        cut_far_kernel, columns(1), after(half, in_hbm[0], in_hbm[2], picked), list(far), "cut_columns"
-    )
-    in_vmem += halves_across(cut_four, in_vmem[2], in_hbm[1])[0]
+        cut_far_kernel, columns(1), after(half, in_hbm[1], in_hbm[2], picked), list(far), "cut_columns"
+    )
+    in_vmem += halves_across(cut_four, in_vmem[2])[0]
     groups = ((3, True, 2), (2, True, 2), (2, False, 4), (1, False, 4))
     rows = [own, *one, *two, *three, *far]
-    covariance = pl.pallas_call(
+    covariance, projections = pl.pallas_call(
         functools.partial(
             covariance_kernel, frame_axis, atom_axis, groups, 1.0 / total_frames
         ),
-        out_shape=jax.ShapeDtypeStruct((3, 3, local_atoms, block), jnp.float32),
+        out_shape=(jax.ShapeDtypeStruct((3, 3, local_atoms, block), jnp.float32), share),
         in_specs=[SMEM]
         + [VMEM] * len(rows)
         + [HBM] * len(in_hbm)
-        + [VMEM] * len(in_vmem),
-        out_specs=ANY,
+        + [VMEM] * len(in_vmem)
+        + [HBM] * len(parts),
+        out_specs=(ANY, VMEM),
         scratch_shapes=[
             pltpu.VMEM((2, 2 * run, total_frames), jnp.bfloat16),
             pltpu.VMEM((3, total_frames, block), jnp.bfloat16),
             pltpu.VMEM((2, 3, 2 * run, block), jnp.float32),
+            pltpu.VMEM((atom_axis,) + share.shape, jnp.float32),
             pltpu.SemaphoreType.DMA((2 * frame_axis,)),
             pltpu.SemaphoreType.DMA((2, 3)),
+            pltpu.SemaphoreType.DMA((atom_axis,)),
         ],
         compiler_params=params(16),
         cost_estimate=pl.CostEstimate(
@@ -494,6 +492,7 @@
         *[pinned(value, pltpu.VMEM) for value in rows],
         *[pinned(value, pltpu.HBM) for value in in_hbm],
         *[pinned(value, pltpu.VMEM) for value in in_vmem],
+        *[pinned(value, pltpu.HBM) for value in parts],
     )
     return jnp.transpose(covariance, (0, 2, 1, 3)), projections
 

time: 70.6 us -> 69.8 us (0.989); the launches traced: 69.2 us -> 69.5 us
  waiting for transfers between devices: 21.4 us -> 28.7 us
  local copies, waits for them, and re-layouts: 6.28 us -> 2.02 us
  starting transfers between devices: 26.7 us -> 23.9 us
    ppermute x4, waiting for transfers between devices: 6.78 us -> 11.2 us  [hop(): lax.ppermute(down, 'frames', backward)]
    unnamed x26 -> x18, local copies, waits for them, and re-layouts: 6.28 us -> 2.02 us
    ppermute x14, starting transfers between devices: 9.54 us -> 6.75 us  [swap(): lax.ppermute(value, 'atoms', [(a, a ^ distance) for a in range(atom_axis)])]
    ppermute x4, waiting for transfers between devices: 2.63 us -> 4.62 us  [hop(): lax.ppermute(up, 'frames', forward)]
    ppermute x14, waiting for transfers between devices: 11.4 us -> 12.9 us  [swap(): lax.ppermute(value, 'atoms', [(a, a ^ distance) for a in range(atom_axis)])]
    ppermute x4, starting transfers between devices: 3.48 us -> 4.23 us  [hop(): lax.ppermute(up, 'frames', forward)]
    ppermute x4, starting transfers between devices: 4.73 us -> 3.97 us  [hop(): lax.ppermute(down, 'frames', backward)]
  transfers between devices with their start and end apart: 25 -> 25, of which waited for: 15 -> 13; matrix products, arithmetic and copies ran while one was open for 0% -> 0% of each run, Pallas kernels for 4% -> 3%
where the time goes in v17:
time: 69.8 us; the launch traced here: 69.5 us
  waiting for transfers between devices  28.7 us (41%)
  starting transfers between devices  23.9 us (34%)
  Pallas kernels  14 us (20%)
  local copies, waits for them, and re-layouts  2.02 us (3%)
  between operations  0.87 us (1%)
    ppermute x14, waiting for transfers between devices, swap(): lax.ppermute(value, 'atoms', [(a, a ^ distance) for a in range(atom_axis)])  12.9 us
    ppermute x4, waiting for transfers between devices, hop(): lax.ppermute(down, 'frames', backward)  11.2 us
    pallas_call x1, Pallas kernels, per_device(): pl.pallas_call(functools.partial(covariance_kernel, frame_axis, atom_axis...  9.35 us
    ppermute x3, starting transfers between devices, cross(): return [cut, lax.ppermute(cut, axes, pairs(0, 2))]  8.95 us
    ppermute x14, starting transfers between devices, swap(): lax.ppermute(value, 'atoms', [(a, a ^ distance) for a in range(atom_axis)])  6.75 us
    ppermute x4, waiting for transfers between devices, hop(): lax.ppermute(up, 'frames', forward)  4.62 us
    ppermute x4, starting transfers between devices, hop(): lax.ppermute(up, 'frames', forward)  4.23 us
    ppermute x4, starting transfers between devices, hop(): lax.ppermute(down, 'frames', backward)  3.97 us
  transfers between devices with their start and end apart: 25, of which 13 were waited for; matrix products, arithmetic and copies ran while one was open for 0% of the time, Pallas kernels for 3%

profile of v17, /device:TPU:0, one launch (start us, length us, event | category | flops | bytes accessed | tf_op | source)
XLA Modules:
  0.0 69.5 jit_solution(10683990577716401350)
XLA Ops:
  0.6 1.7 %local_moments.1 = (f32[24,64]{1,0:T(8,128)S(1)}, f32[3,64,1024]{2,1,0:T(8,128)S(1)}, f32[3,1024]{1,0:T(4,128)S(1)}) custom-call(f32[3,64,1024]{2,1,0:T(8,128)} %bitcast.5, f32[3,1024]{1,0:T(4,128)} %ref_hbm.1), custom_call_target="tpu_custom_call" | custom-call | tf_op jit(solution)/shard_map/local_moments/pallas_call | solution.py:340
  2.3 2.4 %collective-permute-start.2 = (f32[24,64]{1,0:T(8,128)S(1)}, f32[24,64]{1,0:T(8,128)S(1)}, u32[]{:S(2)}, u32[]{:S(2)}) collective-permute-start(f32[24,64]{1,0:T(8,128)S(1)} %get-tuple-element.20.refs_0_), channel_id=1, source_target_pairs={{0,3},{1,2},{2,1},{3,0},{4,7},{5,6},{6,5},{7,4},{8,11},{9,10},{10,... | collective-permute-start | bytes 18440 | tf_op jit(solution)/shard_map/ppermute | solution.py:354
  4.7 0.6 collective-permute-start.1
  5.4 0.0 collective-permute-start
  5.4 0.7 %collective-permute-done.2.refs_3_ = f32[24,64]{1,0:T(8,128)S(1)} collective-permute-done((f32[24,64]{1,0:T(8,128)S(1)}, f32[24,64]{1,0:T(8,128)S(1)}, u32[]{:S(2)}, u32[]{:S(2)}) %collective-permute-start.2) | collective-permute-done | bytes 6176 | tf_op jit(solution)/shard_map/ppermute | solution.py:354
  6.1 2.3 %collective-permute-done.1.refs_2_ = f32[24,64]{1,0:T(8,128)S(1)} collective-permute-done((f32[24,64]{1,0:T(8,128)S(1)}, f32[24,64]{1,0:T(8,128)S(1)}, u32[]{:S(2)}, u32[]{:S(2)}) %collective-permute-start.1) | collective-permute-done | bytes 6176 | tf_op jit(solution)/shard_map/ppermute | solution.py:354
  8.4 0.0 collective-permute-done.refs_1_
  8.4 0.6 polar_align.1
  9.0 1.6 %collective-permute-start.3 = (bf16[2,3,256,128]{3,2,1,0:T(8,128)(2,1)S(1)}, bf16[2,3,256,128]{3,2,1,0:T(8,128)(2,1)S(1)}, u32[]{:S(2)}, u32[]{:S(2)}) collective-permute-start(bf16[2,3,256,128]{3,2,1,0:T(8,128)(2,1)S(1)} %get-tuple-element.23.refs_0_), channel_id=1, source_target_pairs={{0,8},{8,16},{16,24},{24,28},{28,20},{20,12},{12,4},{4,0},{1,9},{9... | collective-permute-start | bytes 1179656 | tf_op jit(solution)/shard_map/ppermute | solution.py:437
  10.7 0.4 collective-permute-start.4
  11.1 0.1 cut_columns.5.refs_0_
  11.3 2.6 %collective-permute-start.5 = (bf16[1,3,64,512]{3,2,1,0:T(8,128)(2,1)S(1)}, bf16[1,3,64,512]{3,2,1,0:T(8,128)(2,1)S(1)}, u32[]{:S(2)}, u32[]{:S(2)}) collective-permute-start(bf16[1,3,64,512]{3,2,1,0:T(8,128)(2,1)S(1)} %cut_columns.5.refs_0_), channel_id=1, source_target_pairs={{0,2},{4,6},{9,11},{13,15},{18,16},{22,20},{27,25},{31,29}} | collective-permute-start | bytes 589832 | tf_op jit(solution)/shard_map/ppermute | solution.py:416
  13.8 0.0 copy-start
  13.8 1.4 %copy-done = bf16[3,1024,256]{2,1,0:T(8,128)(2,1)S(1)} copy-done((bf16[3,1024,256]{2,1,0:T(8,128)(2,1)S(1)}, bf16[3,1024,256]{2,1,0:T(8,128)(2,1)}, u32[]{:S(2)}) %copy-start) | copy-done | bytes 1572888
  15.2 0.5 project.1
  15.7 0.1 collective-permute-start.6
  15.8 0.1 collective-permute-start.7
  15.9 1.1 %collective-permute-done.6.refs_22_ = f32[64,64]{1,0:T(8,128)S(1)} collective-permute-done((f32[64,64]{1,0:T(8,128)S(1)}, f32[64,64]{1,0:T(8,128)S(1)}, u32[]{:S(2)}, u32[]{:S(2)}) %collective-permute-start.6) | collective-permute-done | bytes 16416 | tf_op jit(solution)/shard_map/ppermute | solution.py:354
  17.0 0.7 collective-permute-start.8
  17.7 2.1 %collective-permute-done.7.refs_23_ = f32[64,64]{1,0:T(8,128)S(1)} collective-permute-done((f32[64,64]{1,0:T(8,128)S(1)}, f32[64,64]{1,0:T(8,128)S(1)}, u32[]{:S(2)}, u32[]{:S(2)}) %collective-permute-start.7) | collective-permute-done | bytes 16416 | tf_op jit(solution)/shard_map/ppermute | solution.py:354
  19.8 0.6 collective-permute-done.8.refs_24_
  20.4 0.0 collective-permute-done.5.refs_1_
  20.4 0.0 collective-permute-done.3.refs_0_.refs_1_
  20.4 0.0 copy-done.7
  20.4 0.6 copy-done.8
  21.0 0.0 collective-permute-done.4.refs_1_.refs_2_
  21.0 1.5 %collective-permute-start.10 = (bf16[2,3,256,128]{3,2,1,0:T(8,128)(2,1)S(1)}, bf16[2,3,256,128]{3,2,1,0:T(8,128)(2,1)S(1)}, u32[]{:S(2)}, u32[]{:S(2)}) collective-permute-start(bf16[2,3,256,128]{3,2,1,0:T(8,128)(2,1)S(1)} %collective-permute-done.4.refs_1_.refs_2_), channel_id=1, source_target_pairs={{8,0},{16,8},{24,16},{28,24},{20,28},{12,20},{4,12},{0,4},{9,1},{1... | collective-permute-start | bytes 1179656 | tf_op jit(solution)/shard_map/ppermute | solution.py:437
  22.5 0.5 collective-permute-start.9
  23.0 0.2 cut_columns.6.refs_2_
  23.2 3.6 %collective-permute-start.13 = (bf16[2,3,64,512]{3,2,1,0:T(8,128)(2,1)S(1)}, bf16[2,3,64,512]{3,2,1,0:T(8,128)(2,1)}, u32[]{:S(2)}, u32[]{:S(2)}) collective-permute-start(bf16[2,3,64,512]{3,2,1,0:T(8,128)(2,1)S(1)} %cut_columns.6.refs_2_), channel_id=1, source_target_pairs={{0,2},{4,6},{9,11},{13,15},{18,16},{22,20},{27,25},{31,29}} | collective-permute-start | bytes 1179656 | tf_op jit(solution)/shard_map/ppermute | solution.py:416
  26.8 5.7 %collective-permute-done.10.refs_1_.refs_4_ = bf16[2,3,256,128]{3,2,1,0:T(8,128)(2,1)S(1)} collective-permute-done((bf16[2,3,256,128]{3,2,1,0:T(8,128)(2,1)S(1)}, bf16[2,3,256,128]{3,2,1,0:T(8,128)(2,1)S(1)}, u32[]{:S(2)}, u32[]{:S(2)}) %collective-permute-start.10) | collective-permute-done | bytes 393248 | tf_op jit(solution)/shard_map/ppermute | solution.py:437
  32.5 1.2 %collective-permute-start.12 = (bf16[2,3,256,128]{3,2,1,0:T(8,128)(2,1)S(1)}, bf16[2,3,256,128]{3,2,1,0:T(8,128)(2,1)S(1)}, u32[]{:S(2)}, u32[]{:S(2)}) collective-permute-start(bf16[2,3,256,128]{3,2,1,0:T(8,128)(2,1)S(1)} %collective-permute-done.10.refs_1_.refs_4_), channel_id=1, source_target_pairs={{8,0},{16,8},{24,16},{28,24},{20,28},{12,20},{4,12},{0,4},{9,1},{1... | collective-permute-start | bytes 1179656 | tf_op jit(solution)/shard_map/ppermute | solution.py:437
  33.7 0.0 collective-permute-done.9.refs_0_.refs_3_
  33.7 0.8 %collective-permute-start.11 = (bf16[2,3,256,128]{3,2,1,0:T(8,128)(2,1)S(1)}, bf16[2,3,256,128]{3,2,1,0:T(8,128)(2,1)S(1)}, u32[]{:S(2)}, u32[]{:S(2)}) collective-permute-start(bf16[2,3,256,128]{3,2,1,0:T(8,128)(2,1)S(1)} %collective-permute-done.9.refs_0_.refs_3_), channel_id=1, source_target_pairs={{0,8},{8,16},{16,24},{24,28},{28,20},{20,12},{12,4},{4,0},{1,9},{9... | collective-permute-start | bytes 1179656 | tf_op jit(solution)/shard_map/ppermute | solution.py:437
  34.5 0.0 collective-permute-done.13.refs_3_
  34.5 1.0 %pass_on.2.refs_9_ = bf16[3,3,64,512]{3,2,1,0:T(8,128)(2,1)S(1)} custom-call(s32[1]{0:T(128)} %bitcast.role_ref, bf16[1,3,64,512]{3,2,1,0:T(8,128)(2,1)S(1)} %cut_columns.5.refs_0_, bf16[1,3,64,512]{3,2,1,0:T(8,128)(2,1)S(1)} %collective-permute-done.5.refs_1_, bf16[2,3,64,512]{3,2,1,0:T(8,128)(2,1)S(1)} %cut_columns.6.refs_2_, ...), custom_call_target="tpu_custom_call" | custom-call | tf_op jit(solution)/shard_map/pass_on/pallas_call | solution.py:406
  35.6 0.1 collective-permute-start.16
  35.6 0.2 cut_columns.8.refs_0_
  35.8 2.8 %collective-permute-start.17 = (bf16[2,3,64,512]{3,2,1,0:T(8,128)(2,1)S(1)}, bf16[2,3,64,512]{3,2,1,0:T(8,128)(2,1)S(1)}, u32[]{:S(2)}, u32[]{:S(2)}) collective-permute-start(bf16[2,3,64,512]{3,2,1,0:T(8,128)(2,1)S(1)} %cut_columns.8.refs_0_), channel_id=1, source_target_pairs={{0,2},{4,6},{9,11},{13,15},{18,16},{22,20},{27,25},{31,29}} | collective-permute-start | bytes 1179656 | tf_op jit(solution)/shard_map/ppermute | solution.py:416
  38.6 4.5 %collective-permute-done.12.down_ref.refs_6_ = bf16[2,3,256,128]{3,2,1,0:T(8,128)(2,1)S(1)} collective-permute-done((bf16[2,3,256,128]{3,2,1,0:T(8,128)(2,1)S(1)}, bf16[2,3,256,128]{3,2,1,0:T(8,128)(2,1)S(1)}, u32[]{:S(2)}, u32[]{:S(2)}) %collective-permute-start.12) | collective-permute-done | bytes 393248 | tf_op jit(solution)/shard_map/ppermute | solution.py:437
  43.2 0.6 collective-permute-done.11.up_ref.refs_5_
  43.8 0.2 cut_columns.7
  44.0 0.1 collective-permute-start.19
  44.0 1.3 %collective-permute-start.14 = (bf16[3,256,128]{2,1,0:T(8,128)(2,1)S(1)}, bf16[3,256,128]{2,1,0:T(8,128)(2,1)S(1)}, u32[]{:S(2)}, u32[]{:S(2)}) collective-permute-start(bf16[3,256,128]{2,1,0:T(8,128)(2,1)S(1)} %get-tuple-element.31), channel_id=1, source_target_pairs={{0,8},{8,16},{16,24},{24,28},{28,20},{20,12},{12,4},{4,0},{1,9},{9... | collective-permute-start | bytes 589832 | tf_op jit(solution)/shard_map/ppermute | solution.py:437
  45.3 0.8 %collective-permute-start.15 = (bf16[3,256,128]{2,1,0:T(8,128)(2,1)S(1)}, bf16[3,256,128]{2,1,0:T(8,128)(2,1)S(1)}, u32[]{:S(2)}, u32[]{:S(2)}) collective-permute-start(bf16[3,256,128]{2,1,0:T(8,128)(2,1)S(1)} %get-tuple-element.32), channel_id=1, source_target_pairs={{8,0},{16,8},{24,16},{28,24},{20,28},{12,20},{4,12},{0,4},{9,1},{1... | collective-permute-start | bytes 589832 | tf_op jit(solution)/shard_map/ppermute | solution.py:437
  46.1 0.0 collective-permute-done.17.refs_1_
  46.2 0.0 collective-permute-done.19.beside_ref.refs_14_
  46.2 1.1 %collective-permute-start.20 = (bf16[2,3,64,256]{3,2,1,0:T(8,128)(2,1)S(1)}, bf16[2,3,64,256]{3,2,1,0:T(8,128)(2,1)S(1)}, u32[]{:S(2)}, u32[]{:S(2)}) collective-permute-start(bf16[2,3,64,256]{3,2,1,0:T(8,128)(2,1)S(1)} %pick_half.2), channel_id=1, source_target_pairs={{0,2},{1,3},{2,0},{3,1},{4,6},{5,7},{6,4},{7,5},{8,10},{9,11},{10,... | collective-permute-start | bytes 589832 | tf_op jit(solution)/shard_map/ppermute | solution.py:354
  47.3 0.0 collective-permute-done.16.refs_10_
  47.3 4.0 %collective-permute-done.14.up_half.refs_7_ = bf16[3,256,128]{2,1,0:T(8,128)(2,1)S(1)} collective-permute-done((bf16[3,256,128]{2,1,0:T(8,128)(2,1)S(1)}, bf16[3,256,128]{2,1,0:T(8,128)(2,1)S(1)}, u32[]{:S(2)}, u32[]{:S(2)}) %collective-permute-start.14) | collective-permute-done | bytes 196640 | tf_op jit(solution)/shard_map/ppermute | solution.py:437
  51.4 0.9 %collective-permute-done.15.down_half.refs_8_ = bf16[3,256,128]{2,1,0:T(8,128)(2,1)S(1)} collective-permute-done((bf16[3,256,128]{2,1,0:T(8,128)(2,1)S(1)}, bf16[3,256,128]{2,1,0:T(8,128)(2,1)S(1)}, u32[]{:S(2)}, u32[]{:S(2)}) %collective-permute-start.15) | collective-permute-done | bytes 196640 | tf_op jit(solution)/shard_map/ppermute | solution.py:437
  52.3 0.1 cut_columns.9.own_ref.refs_17_
  52.5 0.1 collective-permute-start.22
  52.5 0.5 collective-permute-start.18
  53.0 0.0 collective-permute-done.20.refs_15_
  53.0 0.9 %collective-permute-done.22.beside_ref.refs_18_ = bf16[1,3,64,512]{3,2,1,0:T(8,128)(2,1)S(1)} collective-permute-done((bf16[1,3,64,512]{3,2,1,0:T(8,128)(2,1)S(1)}, bf16[1,3,64,512]{3,2,1,0:T(8,128)(2,1)S(1)}, u32[]{:S(2)}, u32[]{:S(2)}) %collective-permute-start.22) | collective-permute-done | bytes 196640 | tf_op jit(solution)/shard_map/ppermute | solution.py:354
  54.0 1.0 %collective-permute-start.23 = (bf16[1,3,64,256]{3,2,1,0:T(8,128)(2,1)S(1)}, bf16[1,3,64,256]{3,2,1,0:T(8,128)(2,1)S(1)}, u32[]{:S(2)}, u32[]{:S(2)}) collective-permute-start(bf16[1,3,64,256]{3,2,1,0:T(8,128)(2,1)S(1)} %pick_half.3), channel_id=1, source_target_pairs={{0,2},{1,3},{2,0},{3,1},{4,6},{5,7},{6,4},{7,5},{8,10},{9,11},{10,... | collective-permute-start | bytes 294920 | tf_op jit(solution)/shard_map/ppermute | solution.py:354
  55.0 0.0 collective-permute-start.21
  55.0 3.9 %collective-permute-done.23.refs_19_ = bf16[1,3,64,256]{3,2,1,0:T(8,128)(2,1)S(1)} collective-permute-done((bf16[1,3,64,256]{3,2,1,0:T(8,128)(2,1)S(1)}, bf16[1,3,64,256]{3,2,1,0:T(8,128)(2,1)S(1)}, u32[]{:S(2)}, u32[]{:S(2)}) %collective-permute-start.23) | collective-permute-done | bytes 98336 | tf_op jit(solution)/shard_map/ppermute | solution.py:354
  58.8 0.0 collective-permute-start.24
  58.8 0.0 collective-permute-done.18.refs_12_
  58.8 1.3 %collective-permute-done.24.refs_20_ = bf16[1,3,64,256]{3,2,1,0:T(8,128)(2,1)S(1)} collective-permute-done((bf16[1,3,64,256]{3,2,1,0:T(8,128)(2,1)S(1)}, bf16[1,3,64,256]{3,2,1,0:T(8,128)(2,1)S(1)}, u32[]{:S(2)}, u32[]{:S(2)}) %collective-permute-start.24) | collective-permute-done | bytes 98336 | tf_op jit(solution)/shard_map/ppermute | solution.py:354
  60.1 0.0 collective-permute-done.21.refs_16_
  60.2 9.3 %covariance_tile.1 = (f32[3,3,1024,512]{3,2,1,0:T(8,128)}, f32[64,64]{1,0:T(8,128)}) custom-call(s32[1]{0:T(128)} %bitcast.role_ref, bf16[2,3,256,128]{3,2,1,0:T(8,128)(2,1)S(1)} %get-tuple-element.23.refs_0_, bf16[2,3,256,128]{3,2,1,0:T(8,128)(2,1)S(1)} %collective-permute-done.3.refs_0_.refs_1_, ...), custom_call_target="tpu_custom_call" | custom-call | flops 4831838208 | bytes 25165824 | tf_op jit(solution)/shard_map/covariance_tile/pallas_call | solution.py:463
  (17 shorter events, 0.1 us)
Async XLA Ops:
  2.3 3.8 %collective-permute-start.2 = (f32[24,64]{1,0:T(8,128)S(1)}, f32[24,64]{1,0:T(8,128)S(1)}, u32[]{:S(2)}, u32[]{:S(2)}) collective-permute-start(f32[24,64]{1,0:T(8,128)S(1)} %get-tuple-element.20.refs_0_), channel_id=1, source_target_pairs={{0,3},{1,2},{2,1},{3,0},{4,7},{5,6},{6,5},{7,4},{8,11},{9,10},{10,... | collective-permute-start | bytes 18440 | tf_op jit(solution)/shard_map/ppermute | solution.py:354
  4.7 3.7 %collective-permute-start.1 = (f32[24,64]{1,0:T(8,128)S(1)}, f32[24,64]{1,0:T(8,128)S(1)}, u32[]{:S(2)}, u32[]{:S(2)}) collective-permute-start(f32[24,64]{1,0:T(8,128)S(1)} %get-tuple-element.20.refs_0_), channel_id=1, source_target_pairs={{0,2},{1,3},{2,0},{3,1},{4,6},{5,7},{6,4},{7,5},{8,10},{9,11},{10,... | collective-permute-start | bytes 18440 | tf_op jit(solution)/shard_map/ppermute | solution.py:354
  5.4 3.1 %collective-permute-start = (f32[24,64]{1,0:T(8,128)S(1)}, f32[24,64]{1,0:T(8,128)S(1)}, u32[]{:S(2)}, u32[]{:S(2)}) collective-permute-start(f32[24,64]{1,0:T(8,128)S(1)} %get-tuple-element.20.refs_0_), channel_id=1, source_target_pairs={{0,1},{1,0},{2,3},{3,2},{4,5},{5,4},{6,7},{7,6},{8,9},{9,8},{10,11... | collective-permute-start | bytes 18440 | tf_op jit(solution)/shard_map/ppermute | solution.py:354
  9.0 11.3 %collective-permute-start.3 = (bf16[2,3,256,128]{3,2,1,0:T(8,128)(2,1)S(1)}, bf16[2,3,256,128]{3,2,1,0:T(8,128)(2,1)S(1)}, u32[]{:S(2)}, u32[]{:S(2)}) collective-permute-start(bf16[2,3,256,128]{3,2,1,0:T(8,128)(2,1)S(1)} %get-tuple-element.23.refs_0_), channel_id=1, source_target_pairs={{0,8},{8,16},{16,24},{24,28},{28,20},{20,12},{12,4},{4,0},{1,9},{9... | collective-permute-start | bytes 1179656 | tf_op jit(solution)/shard_map/ppermute | solution.py:437
  10.7 10.3 %collective-permute-start.4 = (bf16[2,3,256,128]{3,2,1,0:T(8,128)(2,1)S(1)}, bf16[2,3,256,128]{3,2,1,0:T(8,128)(2,1)S(1)}, u32[]{:S(2)}, u32[]{:S(2)}) collective-permute-start(bf16[2,3,256,128]{3,2,1,0:T(8,128)(2,1)S(1)} %get-tuple-element.23.refs_0_), channel_id=1, source_target_pairs={{8,0},{16,8},{24,16},{28,24},{20,28},{12,20},{4,12},{0,4},{9,1},{1... | collective-permute-start | bytes 1179656 | tf_op jit(solution)/shard_map/ppermute | solution.py:437
  11.3 9.1 %collective-permute-start.5 = (bf16[1,3,64,512]{3,2,1,0:T(8,128)(2,1)S(1)}, bf16[1,3,64,512]{3,2,1,0:T(8,128)(2,1)S(1)}, u32[]{:S(2)}, u32[]{:S(2)}) collective-permute-start(bf16[1,3,64,512]{3,2,1,0:T(8,128)(2,1)S(1)} %cut_columns.5.refs_0_), channel_id=1, source_target_pairs={{0,2},{4,6},{9,11},{13,15},{18,16},{22,20},{27,25},{31,29}} | collective-permute-start | bytes 589832 | tf_op jit(solution)/shard_map/ppermute | solution.py:416
  13.8 1.4 %copy-start = (bf16[3,1024,256]{2,1,0:T(8,128)(2,1)S(1)}, bf16[3,1024,256]{2,1,0:T(8,128)(2,1)}, u32[]{:S(2)}) copy-start(bf16[3,1024,256]{2,1,0:T(8,128)(2,1)} %eig_ref.1) | copy-start | bytes 4718596
  15.7 18.0 %copy-start.3 = (f32[64,64]{1,0:T(8,128)}, f32[64,64]{1,0:T(8,128)S(1)}, u32[]{:S(2)}) copy-start(f32[64,64]{1,0:T(8,128)S(1)} %get-tuple-element.25.refs_21_) | copy-start | bytes 49156
  15.7 1.3 %collective-permute-start.6 = (f32[64,64]{1,0:T(8,128)S(1)}, f32[64,64]{1,0:T(8,128)S(1)}, u32[]{:S(2)}, u32[]{:S(2)}) collective-permute-start(f32[64,64]{1,0:T(8,128)S(1)} %get-tuple-element.26), channel_id=1, source_target_pairs={{0,1},{1,0},{2,3},{3,2},{4,5},{5,4},{6,7},{7,6},{8,9},{9,8},{10,11... | collective-permute-start | bytes 49160 | tf_op jit(solution)/shard_map/ppermute | solution.py:354
  15.8 4.0 %collective-permute-start.7 = (f32[64,64]{1,0:T(8,128)S(1)}, f32[64,64]{1,0:T(8,128)S(1)}, u32[]{:S(2)}, u32[]{:S(2)}) collective-permute-start(f32[64,64]{1,0:T(8,128)S(1)} %get-tuple-element.27), channel_id=1, source_target_pairs={{0,2},{1,3},{2,0},{3,1},{4,6},{5,7},{6,4},{7,5},{8,10},{9,11},{10,... | collective-permute-start | bytes 49160 | tf_op jit(solution)/shard_map/ppermute | solution.py:354
  17.0 3.4 %copy-start.6 = (f32[64,64]{1,0:T(8,128)}, f32[64,64]{1,0:T(8,128)S(1)}, u32[]{:S(2)}) copy-start(f32[64,64]{1,0:T(8,128)S(1)} %collective-permute-done.6.refs_22_) | copy-start | bytes 49156
  17.0 3.3 %collective-permute-start.8 = (f32[64,64]{1,0:T(8,128)S(1)}, f32[64,64]{1,0:T(8,128)S(1)}, u32[]{:S(2)}, u32[]{:S(2)}) collective-permute-start(f32[64,64]{1,0:T(8,128)S(1)} %get-tuple-element.28), channel_id=1, source_target_pairs={{0,3},{1,2},{2,1},{3,0},{4,7},{5,6},{6,5},{7,4},{8,11},{9,10},{10,... | collective-permute-start | bytes 49160 | tf_op jit(solution)/shard_map/ppermute | solution.py:354
  19.8 0.6 copy-start.7
  20.4 0.6 copy-start.8
  21.0 11.5 %collective-permute-start.10 = (bf16[2,3,256,128]{3,2,1,0:T(8,128)(2,1)S(1)}, bf16[2,3,256,128]{3,2,1,0:T(8,128)(2,1)S(1)}, u32[]{:S(2)}, u32[]{:S(2)}) collective-permute-start(bf16[2,3,256,128]{3,2,1,0:T(8,128)(2,1)S(1)} %collective-permute-done.4.refs_1_.refs_2_), channel_id=1, source_target_pairs={{8,0},{16,8},{24,16},{28,24},{20,28},{12,20},{4,12},{0,4},{9,1},{1... | collective-permute-start | bytes 1179656 | tf_op jit(solution)/shard_map/ppermute | solution.py:437
  22.5 11.2 %collective-permute-start.9 = (bf16[2,3,256,128]{3,2,1,0:T(8,128)(2,1)S(1)}, bf16[2,3,256,128]{3,2,1,0:T(8,128)(2,1)S(1)}, u32[]{:S(2)}, u32[]{:S(2)}) collective-permute-start(bf16[2,3,256,128]{3,2,1,0:T(8,128)(2,1)S(1)} %collective-permute-done.3.refs_0_.refs_1_), channel_id=1, source_target_pairs={{0,8},{8,16},{16,24},{24,28},{28,20},{20,12},{12,4},{4,0},{1,9},{9... | collective-permute-start | bytes 1179656 | tf_op jit(solution)/shard_map/ppermute | solution.py:437
  23.2 11.3 %collective-permute-start.13 = (bf16[2,3,64,512]{3,2,1,0:T(8,128)(2,1)S(1)}, bf16[2,3,64,512]{3,2,1,0:T(8,128)(2,1)}, u32[]{:S(2)}, u32[]{:S(2)}) collective-permute-start(bf16[2,3,64,512]{3,2,1,0:T(8,128)(2,1)S(1)} %cut_columns.6.refs_2_), channel_id=1, source_target_pairs={{0,2},{4,6},{9,11},{13,15},{18,16},{22,20},{27,25},{31,29}} | collective-permute-start | bytes 1179656 | tf_op jit(solution)/shard_map/ppermute | solution.py:416
  32.5 10.7 %collective-permute-start.12 = (bf16[2,3,256,128]{3,2,1,0:T(8,128)(2,1)S(1)}, bf16[2,3,256,128]{3,2,1,0:T(8,128)(2,1)S(1)}, u32[]{:S(2)}, u32[]{:S(2)}) collective-permute-start(bf16[2,3,256,128]{3,2,1,0:T(8,128)(2,1)S(1)} %collective-permute-done.10.refs_1_.refs_4_), channel_id=1, source_target_pairs={{8,0},{16,8},{24,16},{28,24},{20,28},{12,20},{4,12},{0,4},{9,1},{1... | collective-permute-start | bytes 1179656 | tf_op jit(solution)/shard_map/ppermute | solution.py:437
  33.7 10.1 %collective-permute-start.11 = (bf16[2,3,256,128]{3,2,1,0:T(8,128)(2,1)S(1)}, bf16[2,3,256,128]{3,2,1,0:T(8,128)(2,1)S(1)}, u32[]{:S(2)}, u32[]{:S(2)}) collective-permute-start(bf16[2,3,256,128]{3,2,1,0:T(8,128)(2,1)S(1)} %collective-permute-done.9.refs_0_.refs_3_), channel_id=1, source_target_pairs={{0,8},{8,16},{16,24},{24,28},{28,20},{20,12},{12,4},{4,0},{1,9},{9... | collective-permute-start | bytes 1179656 | tf_op jit(solution)/shard_map/ppermute | solution.py:437
  35.5 24.6 %copy-start.1 = (bf16[3,3,64,512]{3,2,1,0:T(8,128)(2,1)}, bf16[3,3,64,512]{3,2,1,0:T(8,128)(2,1)S(1)}, u32[]{:S(2)}) copy-start(bf16[3,3,64,512]{3,2,1,0:T(8,128)(2,1)S(1)} %pass_on.2.refs_9_) | copy-start | bytes 1769476
  35.6 11.8 %collective-permute-start.16 = (bf16[3,3,64,512]{3,2,1,0:T(8,128)(2,1)S(1)}, bf16[3,3,64,512]{3,2,1,0:T(8,128)(2,1)S(1)}, u32[]{:S(2)}, u32[]{:S(2)}) collective-permute-start(bf16[3,3,64,512]{3,2,1,0:T(8,128)(2,1)S(1)} %pass_on.2.refs_9_), channel_id=1, source_target_pairs={{0,1},{1,0},{2,3},{3,2},{4,5},{5,4},{6,7},{7,6},{8,9},{9,8},{10,11... | collective-permute-start | bytes 1769480 | tf_op jit(solution)/shard_map/ppermute | solution.py:354
  35.8 10.3 %collective-permute-start.17 = (bf16[2,3,64,512]{3,2,1,0:T(8,128)(2,1)S(1)}, bf16[2,3,64,512]{3,2,1,0:T(8,128)(2,1)S(1)}, u32[]{:S(2)}, u32[]{:S(2)}) collective-permute-start(bf16[2,3,64,512]{3,2,1,0:T(8,128)(2,1)S(1)} %cut_columns.8.refs_0_), channel_id=1, source_target_pairs={{0,2},{4,6},{9,11},{13,15},{18,16},{22,20},{27,25},{31,29}} | collective-permute-start | bytes 1179656 | tf_op jit(solution)/shard_map/ppermute | solution.py:416
  44.0 2.2 %collective-permute-start.19 = (bf16[2,3,64,512]{3,2,1,0:T(8,128)(2,1)S(1)}, bf16[2,3,64,512]{3,2,1,0:T(8,128)(2,1)S(1)}, u32[]{:S(2)}, u32[]{:S(2)}) collective-permute-start(bf16[2,3,64,512]{3,2,1,0:T(8,128)(2,1)S(1)} %get-tuple-element.33.own_ref.refs_13_), channel_id=1, source_target_pairs={{0,1},{1,0},{2,3},{3,2},{4,5},{5,4},{6,7},{7,6},{8,9},{9,8},{10,11... | collective-permute-start | bytes 1179656 | tf_op jit(solution)/shard_map/ppermute | solution.py:354
  44.0 7.3 %collective-permute-start.14 = (bf16[3,256,128]{2,1,0:T(8,128)(2,1)S(1)}, bf16[3,256,128]{2,1,0:T(8,128)(2,1)S(1)}, u32[]{:S(2)}, u32[]{:S(2)}) collective-permute-start(bf16[3,256,128]{2,1,0:T(8,128)(2,1)S(1)} %get-tuple-element.31), channel_id=1, source_target_pairs={{0,8},{8,16},{16,24},{24,28},{28,20},{20,12},{12,4},{4,0},{1,9},{9... | collective-permute-start | bytes 589832 | tf_op jit(solution)/shard_map/ppermute | solution.py:437
  45.3 7.0 %collective-permute-start.15 = (bf16[3,256,128]{2,1,0:T(8,128)(2,1)S(1)}, bf16[3,256,128]{2,1,0:T(8,128)(2,1)S(1)}, u32[]{:S(2)}, u32[]{:S(2)}) collective-permute-start(bf16[3,256,128]{2,1,0:T(8,128)(2,1)S(1)} %get-tuple-element.32), channel_id=1, source_target_pairs={{8,0},{16,8},{24,16},{28,24},{20,28},{12,20},{4,12},{0,4},{9,1},{1... | collective-permute-start | bytes 589832 | tf_op jit(solution)/shard_map/ppermute | solution.py:437
  46.2 14.0 %copy-start.2 = (bf16[2,3,64,512]{3,2,1,0:T(8,128)(2,1)}, bf16[2,3,64,512]{3,2,1,0:T(8,128)(2,1)S(1)}, u32[]{:S(2)}) copy-start(bf16[2,3,64,512]{3,2,1,0:T(8,128)(2,1)S(1)} %pass_on.3.refs_11_) | copy-start | bytes 1179652
  46.2 6.8 %collective-permute-start.20 = (bf16[2,3,64,256]{3,2,1,0:T(8,128)(2,1)S(1)}, bf16[2,3,64,256]{3,2,1,0:T(8,128)(2,1)S(1)}, u32[]{:S(2)}, u32[]{:S(2)}) collective-permute-start(bf16[2,3,64,256]{3,2,1,0:T(8,128)(2,1)S(1)} %pick_half.2), channel_id=1, source_target_pairs={{0,2},{1,3},{2,0},{3,1},{4,6},{5,7},{6,4},{7,5},{8,10},{9,11},{10,... | collective-permute-start | bytes 589832 | tf_op jit(solution)/shard_map/ppermute | solution.py:354
  47.3 12.8 %copy-start.4 = (bf16[3,3,64,512]{3,2,1,0:T(8,128)(2,1)}, bf16[3,3,64,512]{3,2,1,0:T(8,128)(2,1)S(1)}, u32[]{:S(2)}) copy-start(bf16[3,3,64,512]{3,2,1,0:T(8,128)(2,1)S(1)} %collective-permute-done.16.refs_10_) | copy-start | bytes 1769476
  52.5 1.5 %collective-permute-start.22 = (bf16[1,3,64,512]{3,2,1,0:T(8,128)(2,1)S(1)}, bf16[1,3,64,512]{3,2,1,0:T(8,128)(2,1)S(1)}, u32[]{:S(2)}, u32[]{:S(2)}) collective-permute-start(bf16[1,3,64,512]{3,2,1,0:T(8,128)(2,1)S(1)} %cut_columns.9.own_ref.refs_17_), channel_id=1, source_target_pairs={{0,1},{1,0},{2,3},{3,2},{4,5},{5,4},{6,7},{7,6},{8,9},{9,8},{10,11... | collective-permute-start | bytes 589832 | tf_op jit(solution)/shard_map/ppermute | solution.py:354
  52.5 6.3 %collective-permute-start.18 = (bf16[2,3,64,512]{3,2,1,0:T(8,128)(2,1)S(1)}, bf16[2,3,64,512]{3,2,1,0:T(8,128)(2,1)S(1)}, u32[]{:S(2)}, u32[]{:S(2)}) collective-permute-start(bf16[2,3,64,512]{3,2,1,0:T(8,128)(2,1)S(1)} %pass_on.3.refs_11_), channel_id=1, source_target_pairs={{0,1},{1,0},{2,3},{3,2},{4,5},{5,4},{6,7},{7,6},{8,9},{9,8},{10,11... | collective-permute-start | bytes 1179656 | tf_op jit(solution)/shard_map/ppermute | solution.py:354
  54.0 4.9 %collective-permute-start.23 = (bf16[1,3,64,256]{3,2,1,0:T(8,128)(2,1)S(1)}, bf16[1,3,64,256]{3,2,1,0:T(8,128)(2,1)S(1)}, u32[]{:S(2)}, u32[]{:S(2)}) collective-permute-start(bf16[1,3,64,256]{3,2,1,0:T(8,128)(2,1)S(1)} %pick_half.3), channel_id=1, source_target_pairs={{0,2},{1,3},{2,0},{3,1},{4,6},{5,7},{6,4},{7,5},{8,10},{9,11},{10,... | collective-permute-start | bytes 294920 | tf_op jit(solution)/shard_map/ppermute | solution.py:354
  55.0 5.2 %collective-permute-start.21 = (bf16[2,3,64,256]{3,2,1,0:T(8,128)(2,1)S(1)}, bf16[2,3,64,256]{3,2,1,0:T(8,128)(2,1)S(1)}, u32[]{:S(2)}, u32[]{:S(2)}) collective-permute-start(bf16[2,3,64,256]{3,2,1,0:T(8,128)(2,1)S(1)} %collective-permute-done.20.refs_15_), channel_id=1, source_target_pairs={{0,1},{1,0},{2,3},{3,2},{4,5},{5,4},{6,7},{7,6},{8,9},{9,8},{10,11... | collective-permute-start | bytes 589832 | tf_op jit(solution)/shard_map/ppermute | solution.py:354
  58.8 1.3 %collective-permute-start.24 = (bf16[1,3,64,256]{3,2,1,0:T(8,128)(2,1)S(1)}, bf16[1,3,64,256]{3,2,1,0:T(8,128)(2,1)S(1)}, u32[]{:S(2)}, u32[]{:S(2)}) collective-permute-start(bf16[1,3,64,256]{3,2,1,0:T(8,128)(2,1)S(1)} %collective-permute-done.23.refs_19_), channel_id=1, source_target_pairs={{0,1},{1,0},{2,3},{3,2},{4,5},{5,4},{6,7},{7,6},{8,9},{9,8},{10,11... | collective-permute-start | bytes 294920 | tf_op jit(solution)/shard_map/ppermute | solution.py:354
  58.8 1.3 %copy-start.5 = (bf16[2,3,64,512]{3,2,1,0:T(8,128)(2,1)}, bf16[2,3,64,512]{3,2,1,0:T(8,128)(2,1)S(1)}, u32[]{:S(2)}) copy-start(bf16[2,3,64,512]{3,2,1,0:T(8,128)(2,1)S(1)} %collective-permute-done.18.refs_12_) | copy-start | bytes 1179652

commit v18 on v17

--- a/solution.py
+++ b/solution.py
@@ -439,11 +439,11 @@
     one = hop(own, own)
     crossed = cross(kernel(cut_kernel, columns(1), half, [own], "cut_columns"))
     cut_one = kernel(cut_kernel, columns(2), half, list(one), "cut_columns")
-    two = hop(after(one[0], crossed[1], *parts), one[1])
+    two = hop(after(one[0], crossed[1]), one[1])
     in_hbm = pass_on(crossed + cross(cut_one), role)
     cut_two = kernel(cut_kernel, columns(2), half, list(two), "cut_columns")
-    three = hop(*two)
-    in_hbm += pass_on(cross(cut_two), role)
+    three = hop(after(two[0], *parts), two[1])
+    in_vmem = pass_on(cross(cut_two), role)
     half_shard = pltpu.VMEM(piece, jnp.bfloat16)
     cut_three, *halves = kernel(
         cut_last_kernel,
@@ -453,12 +453,13 @@
         "cut_columns",
     )
     far = hop(*halves)
-    in_vmem, picked = halves_across(cut_three)
+    three_halves, picked = halves_across(cut_three)
+    in_vmem += three_halves
     cut_four = kernel(
-        cut_far_kernel, columns(1), after(half, in_hbm[1], in_hbm[2], picked), list(far), "cut_columns"
-    )
-    in_vmem += halves_across(cut_four, in_vmem[2])[0]
-    groups = ((3, True, 2), (2, True, 2), (2, False, 4), (1, False, 4))
+        cut_far_kernel, columns(1), after(half, in_hbm[1], in_vmem[0], picked), list(far), "cut_columns"
+    )
+    in_vmem += halves_across(cut_four, three_halves[2])[0]
+    groups = ((3, True, 2), (2, False, 2), (2, False, 4), (1, False, 4))
     rows = [own, *one, *two, *three, *far]
     covariance, projections = pl.pallas_call(
         functools.partial(

time: 69.8 us -> 70.5 us (1.010)
    ppermute x4, waiting for transfers between devices: 11.2 us -> 5.01 us  [hop(): lax.ppermute(down, 'frames', backward)]
    ppermute x4, waiting for transfers between devices: 4.62 us -> 7.92 us  [hop(): lax.ppermute(up, 'frames', forward)]
    ppermute x3, waiting for transfers between devices: 0.01 us -> 3.16 us  [cross(): return [cut, lax.ppermute(cut, axes, pairs(0, 2))]]
    unnamed x18 -> x14, local copies, waits for them, and re-layouts: 2.02 us -> 2.62 us
  transfers between devices with their start and end apart: 25 -> 25, of which waited for: 13 -> 15; matrix products, arithmetic and copies ran while one was open for 0% -> 0% of each run, Pallas kernels for 3% -> 3%
where the time goes in v18:
time: 70.5 us; the launch traced here: 70.2 us
  waiting for transfers between devices  29 us (41%)
  starting transfers between devices  23.9 us (34%)
  Pallas kernels  13.9 us (20%)
  local copies, waits for them, and re-layouts  2.62 us (4%)
  between operations  0.82 us (1%)
    ppermute x14, waiting for transfers between devices, swap(): lax.ppermute(value, 'atoms', [(a, a ^ distance) for a in range(atom_axis)])  12.9 us
    pallas_call x1, Pallas kernels, per_device(): pl.pallas_call(functools.partial(covariance_kernel, frame_axis, atom_axis...  9.18 us
    ppermute x3, starting transfers between devices, cross(): return [cut, lax.ppermute(cut, axes, pairs(0, 2))]  8.97 us
    ppermute x4, waiting for transfers between devices, hop(): lax.ppermute(up, 'frames', forward)  7.92 us
    ppermute x14, starting transfers between devices, swap(): lax.ppermute(value, 'atoms', [(a, a ^ distance) for a in range(atom_axis)])  6.74 us
    ppermute x4, waiting for transfers between devices, hop(): lax.ppermute(down, 'frames', backward)  5.01 us
    ppermute x4, starting transfers between devices, hop(): lax.ppermute(up, 'frames', forward)  4.35 us
    ppermute x4, starting transfers between devices, hop(): lax.ppermute(down, 'frames', backward)  3.86 us
  transfers between devices with their start and end apart: 25, of which 15 were waited for; matrix products, arithmetic and copies ran while one was open for 0% of the time, Pallas kernels for 3%

profile of v18, /device:TPU:0, one launch (start us, length us, event | category | flops | bytes accessed | tf_op | source)
XLA Modules:
  0.0 70.2 jit_solution(1588003697719304208)
XLA Ops:
  0.6 1.7 %local_moments.1 = (f32[24,64]{1,0:T(8,128)S(1)}, f32[3,64,1024]{2,1,0:T(8,128)S(1)}, f32[3,1024]{1,0:T(4,128)S(1)}) custom-call(f32[3,64,1024]{2,1,0:T(8,128)} %bitcast.5, f32[3,1024]{1,0:T(4,128)} %ref_hbm.1), custom_call_target="tpu_custom_call" | custom-call | tf_op jit(solution)/shard_map/local_moments/pallas_call | solution.py:340
  2.3 2.4 %collective-permute-start.2 = (f32[24,64]{1,0:T(8,128)S(1)}, f32[24,64]{1,0:T(8,128)S(1)}, u32[]{:S(2)}, u32[]{:S(2)}) collective-permute-start(f32[24,64]{1,0:T(8,128)S(1)} %get-tuple-element.21.refs_0_), channel_id=1, source_target_pairs={{0,3},{1,2},{2,1},{3,0},{4,7},{5,6},{6,5},{7,4},{8,11},{9,10},{10,... | collective-permute-start | bytes 18440 | tf_op jit(solution)/shard_map/ppermute | solution.py:354
  4.7 0.6 collective-permute-start.1
  5.4 0.0 collective-permute-start
  5.4 0.7 %collective-permute-done.2.refs_3_ = f32[24,64]{1,0:T(8,128)S(1)} collective-permute-done((f32[24,64]{1,0:T(8,128)S(1)}, f32[24,64]{1,0:T(8,128)S(1)}, u32[]{:S(2)}, u32[]{:S(2)}) %collective-permute-start.2) | collective-permute-done | bytes 6176 | tf_op jit(solution)/shard_map/ppermute | solution.py:354
  6.1 2.3 %collective-permute-done.1.refs_2_ = f32[24,64]{1,0:T(8,128)S(1)} collective-permute-done((f32[24,64]{1,0:T(8,128)S(1)}, f32[24,64]{1,0:T(8,128)S(1)}, u32[]{:S(2)}, u32[]{:S(2)}) %collective-permute-start.1) | collective-permute-done | bytes 6176 | tf_op jit(solution)/shard_map/ppermute | solution.py:354
  8.4 0.0 collective-permute-done.refs_1_
  8.4 0.6 polar_align.1
  9.0 1.6 %collective-permute-start.3 = (bf16[2,3,256,128]{3,2,1,0:T(8,128)(2,1)S(1)}, bf16[2,3,256,128]{3,2,1,0:T(8,128)(2,1)S(1)}, u32[]{:S(2)}, u32[]{:S(2)}) collective-permute-start(bf16[2,3,256,128]{3,2,1,0:T(8,128)(2,1)S(1)} %get-tuple-element.24.refs_0_), channel_id=1, source_target_pairs={{0,8},{8,16},{16,24},{24,28},{28,20},{20,12},{12,4},{4,0},{1,9},{9... | collective-permute-start | bytes 1179656 | tf_op jit(solution)/shard_map/ppermute | solution.py:437
  10.7 0.4 collective-permute-start.4
  11.1 0.1 cut_columns.5.refs_0_
  11.3 2.6 %collective-permute-start.5 = (bf16[1,3,64,512]{3,2,1,0:T(8,128)(2,1)S(1)}, bf16[1,3,64,512]{3,2,1,0:T(8,128)(2,1)S(1)}, u32[]{:S(2)}, u32[]{:S(2)}) collective-permute-start(bf16[1,3,64,512]{3,2,1,0:T(8,128)(2,1)S(1)} %cut_columns.5.refs_0_), channel_id=1, source_target_pairs={{0,2},{4,6},{9,11},{13,15},{18,16},{22,20},{27,25},{31,29}} | collective-permute-start | bytes 589832 | tf_op jit(solution)/shard_map/ppermute | solution.py:416
  13.8 3.2 %collective-permute-done.5.refs_1_ = bf16[1,3,64,512]{3,2,1,0:T(8,128)(2,1)S(1)} collective-permute-done((bf16[1,3,64,512]{3,2,1,0:T(8,128)(2,1)S(1)}, bf16[1,3,64,512]{3,2,1,0:T(8,128)(2,1)S(1)}, u32[]{:S(2)}, u32[]{:S(2)}) %collective-permute-start.5) | collective-permute-done | bytes 196640 | tf_op jit(solution)/shard_map/ppermute | solution.py:416
  17.0 2.7 %collective-permute-done.3.refs_0_.refs_1_ = bf16[2,3,256,128]{3,2,1,0:T(8,128)(2,1)S(1)} collective-permute-done((bf16[2,3,256,128]{3,2,1,0:T(8,128)(2,1)S(1)}, bf16[2,3,256,128]{3,2,1,0:T(8,128)(2,1)S(1)}, u32[]{:S(2)}, u32[]{:S(2)}) %collective-permute-start.3) | collective-permute-done | bytes 393248 | tf_op jit(solution)/shard_map/ppermute | solution.py:437
  19.6 1.6 %collective-permute-start.6 = (bf16[2,3,256,128]{3,2,1,0:T(8,128)(2,1)S(1)}, bf16[2,3,256,128]{3,2,1,0:T(8,128)(2,1)S(1)}, u32[]{:S(2)}, u32[]{:S(2)}) collective-permute-start(bf16[2,3,256,128]{3,2,1,0:T(8,128)(2,1)S(1)} %collective-permute-done.3.refs_0_.refs_1_), channel_id=1, source_target_pairs={{0,8},{8,16},{16,24},{24,28},{28,20},{20,12},{12,4},{4,0},{1,9},{9... | collective-permute-start | bytes 1179656 | tf_op jit(solution)/shard_map/ppermute | solution.py:437
  21.2 0.0 collective-permute-done.4.refs_1_.refs_2_
  21.2 0.5 collective-permute-start.7
  21.7 0.2 cut_columns.6.refs_2_
  21.9 3.3 %collective-permute-start.13 = (bf16[2,3,64,512]{3,2,1,0:T(8,128)(2,1)S(1)}, bf16[2,3,64,512]{3,2,1,0:T(8,128)(2,1)}, u32[]{:S(2)}, u32[]{:S(2)}) collective-permute-start(bf16[2,3,64,512]{3,2,1,0:T(8,128)(2,1)S(1)} %cut_columns.6.refs_2_), channel_id=1, source_target_pairs={{0,2},{4,6},{9,11},{13,15},{18,16},{22,20},{27,25},{31,29}} | collective-permute-start | bytes 1179656 | tf_op jit(solution)/shard_map/ppermute | solution.py:416
  25.2 1.4 %copy-done = bf16[3,1024,256]{2,1,0:T(8,128)(2,1)S(1)} copy-done((bf16[3,1024,256]{2,1,0:T(8,128)(2,1)S(1)}, bf16[3,1024,256]{2,1,0:T(8,128)(2,1)}, u32[]{:S(2)}) %copy-start) | copy-done | bytes 1572888
  26.6 0.5 project.1
  27.1 0.6 copy-done.2
  27.7 0.0 collective-permute-start.8
  27.7 0.0 collective-permute-start.9
  27.7 1.2 %collective-permute-done.8.refs_22_ = f32[64,64]{1,0:T(8,128)S(1)} collective-permute-done((f32[64,64]{1,0:T(8,128)S(1)}, f32[64,64]{1,0:T(8,128)S(1)}, u32[]{:S(2)}, u32[]{:S(2)}) %collective-permute-start.8) | collective-permute-done | bytes 16416 | tf_op jit(solution)/shard_map/ppermute | solution.py:354
  28.9 0.7 collective-permute-start.10
  29.6 2.0 %collective-permute-done.9.refs_23_ = f32[64,64]{1,0:T(8,128)S(1)} collective-permute-done((f32[64,64]{1,0:T(8,128)S(1)}, f32[64,64]{1,0:T(8,128)S(1)}, u32[]{:S(2)}, u32[]{:S(2)}) %collective-permute-start.9) | collective-permute-done | bytes 16416 | tf_op jit(solution)/shard_map/ppermute | solution.py:354
  31.6 0.6 collective-permute-done.10.refs_24_
  32.3 0.0 collective-permute-done.6.refs_0_.refs_3_
  32.3 0.6 copy-done.6
  32.9 0.0 collective-permute-done.7.refs_1_.refs_4_
  32.9 1.5 %collective-permute-start.12 = (bf16[2,3,256,128]{3,2,1,0:T(8,128)(2,1)S(1)}, bf16[2,3,256,128]{3,2,1,0:T(8,128)(2,1)S(1)}, u32[]{:S(2)}, u32[]{:S(2)}) collective-permute-start(bf16[2,3,256,128]{3,2,1,0:T(8,128)(2,1)S(1)} %collective-permute-done.7.refs_1_.refs_4_), channel_id=1, source_target_pairs={{8,0},{16,8},{24,16},{28,24},{20,28},{12,20},{4,12},{0,4},{9,1},{1... | collective-permute-start | bytes 1179656 | tf_op jit(solution)/shard_map/ppermute | solution.py:437
  34.4 0.5 collective-permute-start.11
  34.9 0.0 collective-permute-done.13.refs_3_
  34.9 1.0 %pass_on.2.refs_9_ = bf16[3,3,64,512]{3,2,1,0:T(8,128)(2,1)S(1)} custom-call(s32[1]{0:T(128)} %bitcast.role_ref, bf16[1,3,64,512]{3,2,1,0:T(8,128)(2,1)S(1)} %cut_columns.5.refs_0_, bf16[1,3,64,512]{3,2,1,0:T(8,128)(2,1)S(1)} %collective-permute-done.5.refs_1_, bf16[2,3,64,512]{3,2,1,0:T(8,128)(2,1)S(1)} %cut_columns.6.refs_2_, ...), custom_call_target="tpu_custom_call" | custom-call | tf_op jit(solution)/shard_map/pass_on/pallas_call | solution.py:406
  36.0 0.1 collective-permute-start.16
  36.0 0.2 cut_columns.8.refs_0_
  36.2 3.1 %collective-permute-start.17 = (bf16[2,3,64,512]{3,2,1,0:T(8,128)(2,1)S(1)}, bf16[2,3,64,512]{3,2,1,0:T(8,128)(2,1)S(1)}, u32[]{:S(2)}, u32[]{:S(2)}) collective-permute-start(bf16[2,3,64,512]{3,2,1,0:T(8,128)(2,1)S(1)} %cut_columns.8.refs_0_), channel_id=1, source_target_pairs={{0,2},{4,6},{9,11},{13,15},{18,16},{22,20},{27,25},{31,29}} | collective-permute-start | bytes 1179656 | tf_op jit(solution)/shard_map/ppermute | solution.py:416
  39.3 4.8 %collective-permute-done.12.down_ref.refs_6_ = bf16[2,3,256,128]{3,2,1,0:T(8,128)(2,1)S(1)} collective-permute-done((bf16[2,3,256,128]{3,2,1,0:T(8,128)(2,1)S(1)}, bf16[2,3,256,128]{3,2,1,0:T(8,128)(2,1)S(1)}, u32[]{:S(2)}, u32[]{:S(2)}) %collective-permute-start.12) | collective-permute-done | bytes 393248 | tf_op jit(solution)/shard_map/ppermute | solution.py:437
  44.1 1.2 %collective-permute-done.11.up_ref.refs_5_ = bf16[2,3,256,128]{3,2,1,0:T(8,128)(2,1)S(1)} collective-permute-done((bf16[2,3,256,128]{3,2,1,0:T(8,128)(2,1)S(1)}, bf16[2,3,256,128]{3,2,1,0:T(8,128)(2,1)S(1)}, u32[]{:S(2)}, u32[]{:S(2)}) %collective-permute-start.11) | collective-permute-done | bytes 393248 | tf_op jit(solution)/shard_map/ppermute | solution.py:437
  45.3 0.2 cut_columns.7
  45.5 0.1 collective-permute-start.19
  45.6 0.6 collective-permute-start.14
  46.2 1.4 %collective-permute-start.15 = (bf16[3,256,128]{2,1,0:T(8,128)(2,1)S(1)}, bf16[3,256,128]{2,1,0:T(8,128)(2,1)S(1)}, u32[]{:S(2)}, u32[]{:S(2)}) collective-permute-start(bf16[3,256,128]{2,1,0:T(8,128)(2,1)S(1)} %get-tuple-element.34), channel_id=1, source_target_pairs={{8,0},{16,8},{24,16},{28,24},{20,28},{12,20},{4,12},{0,4},{9,1},{1... | collective-permute-start | bytes 589832 | tf_op jit(solution)/shard_map/ppermute | solution.py:437
  47.7 0.0 collective-permute-done.17.refs_1_
  47.7 0.0 collective-permute-done.19.beside_ref.refs_14_
  47.8 1.1 %collective-permute-start.20 = (bf16[2,3,64,256]{3,2,1,0:T(8,128)(2,1)S(1)}, bf16[2,3,64,256]{3,2,1,0:T(8,128)(2,1)S(1)}, u32[]{:S(2)}, u32[]{:S(2)}) collective-permute-start(bf16[2,3,64,256]{3,2,1,0:T(8,128)(2,1)S(1)} %pick_half.2), channel_id=1, source_target_pairs={{0,2},{1,3},{2,0},{3,1},{4,6},{5,7},{6,4},{7,5},{8,10},{9,11},{10,... | collective-permute-start | bytes 589832 | tf_op jit(solution)/shard_map/ppermute | solution.py:354
  48.9 0.0 collective-permute-done.16.refs_10_
  48.9 4.0 %collective-permute-done.14.up_half.refs_7_ = bf16[3,256,128]{2,1,0:T(8,128)(2,1)S(1)} collective-permute-done((bf16[3,256,128]{2,1,0:T(8,128)(2,1)S(1)}, bf16[3,256,128]{2,1,0:T(8,128)(2,1)S(1)}, u32[]{:S(2)}, u32[]{:S(2)}) %collective-permute-start.14) | collective-permute-done | bytes 196640 | tf_op jit(solution)/shard_map/ppermute | solution.py:437
  53.0 0.2 collective-permute-done.15.down_half.refs_8_
  53.2 0.1 cut_columns.9.own_ref.refs_17_
  53.3 0.1 collective-permute-start.22
  53.4 0.5 collective-permute-start.18
  53.9 0.6 collective-permute-done.20.refs_15_
  54.6 0.3 collective-permute-done.22.beside_ref.refs_18_
  54.9 1.1 %collective-permute-start.23 = (bf16[1,3,64,256]{3,2,1,0:T(8,128)(2,1)S(1)}, bf16[1,3,64,256]{3,2,1,0:T(8,128)(2,1)S(1)}, u32[]{:S(2)}, u32[]{:S(2)}) collective-permute-start(bf16[1,3,64,256]{3,2,1,0:T(8,128)(2,1)S(1)} %pick_half.3), channel_id=1, source_target_pairs={{0,2},{1,3},{2,0},{3,1},{4,6},{5,7},{6,4},{7,5},{8,10},{9,11},{10,... | collective-permute-start | bytes 294920 | tf_op jit(solution)/shard_map/ppermute | solution.py:354
  56.0 0.0 collective-permute-start.21
  56.0 3.8 %collective-permute-done.23.refs_19_ = bf16[1,3,64,256]{3,2,1,0:T(8,128)(2,1)S(1)} collective-permute-done((bf16[1,3,64,256]{3,2,1,0:T(8,128)(2,1)S(1)}, bf16[1,3,64,256]{3,2,1,0:T(8,128)(2,1)S(1)}, u32[]{:S(2)}, u32[]{:S(2)}) %collective-permute-start.23) | collective-permute-done | bytes 98336 | tf_op jit(solution)/shard_map/ppermute | solution.py:354
  59.7 0.0 collective-permute-start.24
  59.7 0.0 collective-permute-done.18.refs_12_
  59.7 1.3 %collective-permute-done.24.refs_20_ = bf16[1,3,64,256]{3,2,1,0:T(8,128)(2,1)S(1)} collective-permute-done((bf16[1,3,64,256]{3,2,1,0:T(8,128)(2,1)S(1)}, bf16[1,3,64,256]{3,2,1,0:T(8,128)(2,1)S(1)}, u32[]{:S(2)}, u32[]{:S(2)}) %collective-permute-start.24) | collective-permute-done | bytes 98336 | tf_op jit(solution)/shard_map/ppermute | solution.py:354
  61.0 0.0 collective-permute-done.21.refs_16_
  61.0 0.0 copy-done.1
  61.0 9.2 %covariance_tile.1 = (f32[3,3,1024,512]{3,2,1,0:T(8,128)}, f32[64,64]{1,0:T(8,128)}) custom-call(s32[1]{0:T(128)} %bitcast.role_ref, bf16[2,3,256,128]{3,2,1,0:T(8,128)(2,1)S(1)} %get-tuple-element.24.refs_0_, bf16[2,3,256,128]{3,2,1,0:T(8,128)(2,1)S(1)} %collective-permute-done.3.refs_0_.refs_1_, ...), custom_call_target="tpu_custom_call" | custom-call | flops 4831838208 | bytes 25165824 | tf_op jit(solution)/shard_map/covariance_tile/pallas_call | solution.py:464
  (13 shorter events, 0.1 us)
Async XLA Ops:
  2.3 3.8 %collective-permute-start.2 = (f32[24,64]{1,0:T(8,128)S(1)}, f32[24,64]{1,0:T(8,128)S(1)}, u32[]{:S(2)}, u32[]{:S(2)}) collective-permute-start(f32[24,64]{1,0:T(8,128)S(1)} %get-tuple-element.21.refs_0_), channel_id=1, source_target_pairs={{0,3},{1,2},{2,1},{3,0},{4,7},{5,6},{6,5},{7,4},{8,11},{9,10},{10,... | collective-permute-start | bytes 18440 | tf_op jit(solution)/shard_map/ppermute | solution.py:354
  4.7 3.7 %collective-permute-start.1 = (f32[24,64]{1,0:T(8,128)S(1)}, f32[24,64]{1,0:T(8,128)S(1)}, u32[]{:S(2)}, u32[]{:S(2)}) collective-permute-start(f32[24,64]{1,0:T(8,128)S(1)} %get-tuple-element.21.refs_0_), channel_id=1, source_target_pairs={{0,2},{1,3},{2,0},{3,1},{4,6},{5,7},{6,4},{7,5},{8,10},{9,11},{10,... | collective-permute-start | bytes 18440 | tf_op jit(solution)/shard_map/ppermute | solution.py:354
  5.4 3.1 %collective-permute-start = (f32[24,64]{1,0:T(8,128)S(1)}, f32[24,64]{1,0:T(8,128)S(1)}, u32[]{:S(2)}, u32[]{:S(2)}) collective-permute-start(f32[24,64]{1,0:T(8,128)S(1)} %get-tuple-element.21.refs_0_), channel_id=1, source_target_pairs={{0,1},{1,0},{2,3},{3,2},{4,5},{5,4},{6,7},{7,6},{8,9},{9,8},{10,11... | collective-permute-start | bytes 18440 | tf_op jit(solution)/shard_map/ppermute | solution.py:354
  9.0 10.6 %collective-permute-start.3 = (bf16[2,3,256,128]{3,2,1,0:T(8,128)(2,1)S(1)}, bf16[2,3,256,128]{3,2,1,0:T(8,128)(2,1)S(1)}, u32[]{:S(2)}, u32[]{:S(2)}) collective-permute-start(bf16[2,3,256,128]{3,2,1,0:T(8,128)(2,1)S(1)} %get-tuple-element.24.refs_0_), channel_id=1, source_target_pairs={{0,8},{8,16},{16,24},{24,28},{28,20},{20,12},{12,4},{4,0},{1,9},{9... | collective-permute-start | bytes 1179656 | tf_op jit(solution)/shard_map/ppermute | solution.py:437
  10.7 10.5 %collective-permute-start.4 = (bf16[2,3,256,128]{3,2,1,0:T(8,128)(2,1)S(1)}, bf16[2,3,256,128]{3,2,1,0:T(8,128)(2,1)S(1)}, u32[]{:S(2)}, u32[]{:S(2)}) collective-permute-start(bf16[2,3,256,128]{3,2,1,0:T(8,128)(2,1)S(1)} %get-tuple-element.24.refs_0_), channel_id=1, source_target_pairs={{8,0},{16,8},{24,16},{28,24},{20,28},{12,20},{4,12},{0,4},{9,1},{1... | collective-permute-start | bytes 1179656 | tf_op jit(solution)/shard_map/ppermute | solution.py:437
  11.3 5.7 %collective-permute-start.5 = (bf16[1,3,64,512]{3,2,1,0:T(8,128)(2,1)S(1)}, bf16[1,3,64,512]{3,2,1,0:T(8,128)(2,1)S(1)}, u32[]{:S(2)}, u32[]{:S(2)}) collective-permute-start(bf16[1,3,64,512]{3,2,1,0:T(8,128)(2,1)S(1)} %cut_columns.5.refs_0_), channel_id=1, source_target_pairs={{0,2},{4,6},{9,11},{13,15},{18,16},{22,20},{27,25},{31,29}} | collective-permute-start | bytes 589832 | tf_op jit(solution)/shard_map/ppermute | solution.py:416
  19.6 12.6 %collective-permute-start.6 = (bf16[2,3,256,128]{3,2,1,0:T(8,128)(2,1)S(1)}, bf16[2,3,256,128]{3,2,1,0:T(8,128)(2,1)S(1)}, u32[]{:S(2)}, u32[]{:S(2)}) collective-permute-start(bf16[2,3,256,128]{3,2,1,0:T(8,128)(2,1)S(1)} %collective-permute-done.3.refs_0_.refs_1_), channel_id=1, source_target_pairs={{0,8},{8,16},{16,24},{24,28},{28,20},{20,12},{12,4},{4,0},{1,9},{9... | collective-permute-start | bytes 1179656 | tf_op jit(solution)/shard_map/ppermute | solution.py:437
  21.2 11.7 %collective-permute-start.7 = (bf16[2,3,256,128]{3,2,1,0:T(8,128)(2,1)S(1)}, bf16[2,3,256,128]{3,2,1,0:T(8,128)(2,1)S(1)}, u32[]{:S(2)}, u32[]{:S(2)}) collective-permute-start(bf16[2,3,256,128]{3,2,1,0:T(8,128)(2,1)S(1)} %collective-permute-done.4.refs_1_.refs_2_), channel_id=1, source_target_pairs={{8,0},{16,8},{24,16},{28,24},{20,28},{12,20},{4,12},{0,4},{9,1},{1... | collective-permute-start | bytes 1179656 | tf_op jit(solution)/shard_map/ppermute | solution.py:437
  21.9 13.1 %collective-permute-start.13 = (bf16[2,3,64,512]{3,2,1,0:T(8,128)(2,1)S(1)}, bf16[2,3,64,512]{3,2,1,0:T(8,128)(2,1)}, u32[]{:S(2)}, u32[]{:S(2)}) collective-permute-start(bf16[2,3,64,512]{3,2,1,0:T(8,128)(2,1)S(1)} %cut_columns.6.refs_2_), channel_id=1, source_target_pairs={{0,2},{4,6},{9,11},{13,15},{18,16},{22,20},{27,25},{31,29}} | collective-permute-start | bytes 1179656 | tf_op jit(solution)/shard_map/ppermute | solution.py:416
  25.2 1.4 %copy-start = (bf16[3,1024,256]{2,1,0:T(8,128)(2,1)S(1)}, bf16[3,1024,256]{2,1,0:T(8,128)(2,1)}, u32[]{:S(2)}) copy-start(bf16[3,1024,256]{2,1,0:T(8,128)(2,1)} %eig_ref.1) | copy-start | bytes 4718596
  27.1 0.6 copy-start.2
  27.7 1.2 %collective-permute-start.8 = (f32[64,64]{1,0:T(8,128)S(1)}, f32[64,64]{1,0:T(8,128)S(1)}, u32[]{:S(2)}, u32[]{:S(2)}) collective-permute-start(f32[64,64]{1,0:T(8,128)S(1)} %get-tuple-element.28), channel_id=1, source_target_pairs={{0,1},{1,0},{2,3},{3,2},{4,5},{5,4},{6,7},{7,6},{8,9},{9,8},{10,11... | collective-permute-start | bytes 49160 | tf_op jit(solution)/shard_map/ppermute | solution.py:354
  27.7 3.9 %collective-permute-start.9 = (f32[64,64]{1,0:T(8,128)S(1)}, f32[64,64]{1,0:T(8,128)S(1)}, u32[]{:S(2)}, u32[]{:S(2)}) collective-permute-start(f32[64,64]{1,0:T(8,128)S(1)} %get-tuple-element.29), channel_id=1, source_target_pairs={{0,2},{1,3},{2,0},{3,1},{4,6},{5,7},{6,4},{7,5},{8,10},{9,11},{10,... | collective-permute-start | bytes 49160 | tf_op jit(solution)/shard_map/ppermute | solution.py:354
  28.9 3.4 %copy-start.4 = (f32[64,64]{1,0:T(8,128)}, f32[64,64]{1,0:T(8,128)S(1)}, u32[]{:S(2)}) copy-start(f32[64,64]{1,0:T(8,128)S(1)} %collective-permute-done.8.refs_22_) | copy-start | bytes 49156
  28.9 3.3 %collective-permute-start.10 = (f32[64,64]{1,0:T(8,128)S(1)}, f32[64,64]{1,0:T(8,128)S(1)}, u32[]{:S(2)}, u32[]{:S(2)}) collective-permute-start(f32[64,64]{1,0:T(8,128)S(1)} %get-tuple-element.30), channel_id=1, source_target_pairs={{0,3},{1,2},{2,1},{3,0},{4,7},{5,6},{6,5},{7,4},{8,11},{9,10},{10,... | collective-permute-start | bytes 49160 | tf_op jit(solution)/shard_map/ppermute | solution.py:354
  31.6 0.7 copy-start.5
  32.3 0.6 copy-start.6
  32.9 11.2 %collective-permute-start.12 = (bf16[2,3,256,128]{3,2,1,0:T(8,128)(2,1)S(1)}, bf16[2,3,256,128]{3,2,1,0:T(8,128)(2,1)S(1)}, u32[]{:S(2)}, u32[]{:S(2)}) collective-permute-start(bf16[2,3,256,128]{3,2,1,0:T(8,128)(2,1)S(1)} %collective-permute-done.7.refs_1_.refs_4_), channel_id=1, source_target_pairs={{8,0},{16,8},{24,16},{28,24},{20,28},{12,20},{4,12},{0,4},{9,1},{1... | collective-permute-start | bytes 1179656 | tf_op jit(solution)/shard_map/ppermute | solution.py:437
  34.4 10.9 %collective-permute-start.11 = (bf16[2,3,256,128]{3,2,1,0:T(8,128)(2,1)S(1)}, bf16[2,3,256,128]{3,2,1,0:T(8,128)(2,1)S(1)}, u32[]{:S(2)}, u32[]{:S(2)}) collective-permute-start(bf16[2,3,256,128]{3,2,1,0:T(8,128)(2,1)S(1)} %collective-permute-done.6.refs_0_.refs_3_), channel_id=1, source_target_pairs={{0,8},{8,16},{16,24},{24,28},{28,20},{20,12},{12,4},{4,0},{1,9},{9... | collective-permute-start | bytes 1179656 | tf_op jit(solution)/shard_map/ppermute | solution.py:437
  36.0 25.1 %copy-start.1 = (bf16[3,3,64,512]{3,2,1,0:T(8,128)(2,1)}, bf16[3,3,64,512]{3,2,1,0:T(8,128)(2,1)S(1)}, u32[]{:S(2)}) copy-start(bf16[3,3,64,512]{3,2,1,0:T(8,128)(2,1)S(1)} %pass_on.2.refs_9_) | copy-start | bytes 1769476
  36.0 12.9 %collective-permute-start.16 = (bf16[3,3,64,512]{3,2,1,0:T(8,128)(2,1)S(1)}, bf16[3,3,64,512]{3,2,1,0:T(8,128)(2,1)S(1)}, u32[]{:S(2)}, u32[]{:S(2)}) collective-permute-start(bf16[3,3,64,512]{3,2,1,0:T(8,128)(2,1)S(1)} %pass_on.2.refs_9_), channel_id=1, source_target_pairs={{0,1},{1,0},{2,3},{3,2},{4,5},{5,4},{6,7},{7,6},{8,9},{9,8},{10,11... | collective-permute-start | bytes 1769480 | tf_op jit(solution)/shard_map/ppermute | solution.py:354
  36.2 11.4 %collective-permute-start.17 = (bf16[2,3,64,512]{3,2,1,0:T(8,128)(2,1)S(1)}, bf16[2,3,64,512]{3,2,1,0:T(8,128)(2,1)S(1)}, u32[]{:S(2)}, u32[]{:S(2)}) collective-permute-start(bf16[2,3,64,512]{3,2,1,0:T(8,128)(2,1)S(1)} %cut_columns.8.refs_0_), channel_id=1, source_target_pairs={{0,2},{4,6},{9,11},{13,15},{18,16},{22,20},{27,25},{31,29}} | collective-permute-start | bytes 1179656 | tf_op jit(solution)/shard_map/ppermute | solution.py:416
  45.5 2.2 %collective-permute-start.19 = (bf16[2,3,64,512]{3,2,1,0:T(8,128)(2,1)S(1)}, bf16[2,3,64,512]{3,2,1,0:T(8,128)(2,1)S(1)}, u32[]{:S(2)}, u32[]{:S(2)}) collective-permute-start(bf16[2,3,64,512]{3,2,1,0:T(8,128)(2,1)S(1)} %get-tuple-element.35.own_ref.refs_13_), channel_id=1, source_target_pairs={{0,1},{1,0},{2,3},{3,2},{4,5},{5,4},{6,7},{7,6},{8,9},{9,8},{10,11... | collective-permute-start | bytes 1179656 | tf_op jit(solution)/shard_map/ppermute | solution.py:354
  45.6 7.4 %collective-permute-start.14 = (bf16[3,256,128]{2,1,0:T(8,128)(2,1)S(1)}, bf16[3,256,128]{2,1,0:T(8,128)(2,1)S(1)}, u32[]{:S(2)}, u32[]{:S(2)}) collective-permute-start(bf16[3,256,128]{2,1,0:T(8,128)(2,1)S(1)} %get-tuple-element.33), channel_id=1, source_target_pairs={{0,8},{8,16},{16,24},{24,28},{28,20},{20,12},{12,4},{4,0},{1,9},{9... | collective-permute-start | bytes 589832 | tf_op jit(solution)/shard_map/ppermute | solution.py:437
  46.2 7.0 %collective-permute-start.15 = (bf16[3,256,128]{2,1,0:T(8,128)(2,1)S(1)}, bf16[3,256,128]{2,1,0:T(8,128)(2,1)S(1)}, u32[]{:S(2)}, u32[]{:S(2)}) collective-permute-start(bf16[3,256,128]{2,1,0:T(8,128)(2,1)S(1)} %get-tuple-element.34), channel_id=1, source_target_pairs={{8,0},{16,8},{24,16},{28,24},{20,28},{12,20},{4,12},{0,4},{9,1},{1... | collective-permute-start | bytes 589832 | tf_op jit(solution)/shard_map/ppermute | solution.py:437
  47.8 6.8 %collective-permute-start.20 = (bf16[2,3,64,256]{3,2,1,0:T(8,128)(2,1)S(1)}, bf16[2,3,64,256]{3,2,1,0:T(8,128)(2,1)S(1)}, u32[]{:S(2)}, u32[]{:S(2)}) collective-permute-start(bf16[2,3,64,256]{3,2,1,0:T(8,128)(2,1)S(1)} %pick_half.2), channel_id=1, source_target_pairs={{0,2},{1,3},{2,0},{3,1},{4,6},{5,7},{6,4},{7,5},{8,10},{9,11},{10,... | collective-permute-start | bytes 589832 | tf_op jit(solution)/shard_map/ppermute | solution.py:354
  48.9 12.1 %copy-start.3 = (bf16[3,3,64,512]{3,2,1,0:T(8,128)(2,1)}, bf16[3,3,64,512]{3,2,1,0:T(8,128)(2,1)S(1)}, u32[]{:S(2)}) copy-start(bf16[3,3,64,512]{3,2,1,0:T(8,128)(2,1)S(1)} %collective-permute-done.16.refs_10_) | copy-start | bytes 1769476
  53.3 1.5 %collective-permute-start.22 = (bf16[1,3,64,512]{3,2,1,0:T(8,128)(2,1)S(1)}, bf16[1,3,64,512]{3,2,1,0:T(8,128)(2,1)S(1)}, u32[]{:S(2)}, u32[]{:S(2)}) collective-permute-start(bf16[1,3,64,512]{3,2,1,0:T(8,128)(2,1)S(1)} %cut_columns.9.own_ref.refs_17_), channel_id=1, source_target_pairs={{0,1},{1,0},{2,3},{3,2},{4,5},{5,4},{6,7},{7,6},{8,9},{9,8},{10,11... | collective-permute-start | bytes 589832 | tf_op jit(solution)/shard_map/ppermute | solution.py:354
  53.4 6.3 %collective-permute-start.18 = (bf16[2,3,64,512]{3,2,1,0:T(8,128)(2,1)S(1)}, bf16[2,3,64,512]{3,2,1,0:T(8,128)(2,1)S(1)}, u32[]{:S(2)}, u32[]{:S(2)}) collective-permute-start(bf16[2,3,64,512]{3,2,1,0:T(8,128)(2,1)S(1)} %pass_on.3.refs_11_), channel_id=1, source_target_pairs={{0,1},{1,0},{2,3},{3,2},{4,5},{5,4},{6,7},{7,6},{8,9},{9,8},{10,11... | collective-permute-start | bytes 1179656 | tf_op jit(solution)/shard_map/ppermute | solution.py:354
  54.9 4.9 %collective-permute-start.23 = (bf16[1,3,64,256]{3,2,1,0:T(8,128)(2,1)S(1)}, bf16[1,3,64,256]{3,2,1,0:T(8,128)(2,1)S(1)}, u32[]{:S(2)}, u32[]{:S(2)}) collective-permute-start(bf16[1,3,64,256]{3,2,1,0:T(8,128)(2,1)S(1)} %pick_half.3), channel_id=1, source_target_pairs={{0,2},{1,3},{2,0},{3,1},{4,6},{5,7},{6,4},{7,5},{8,10},{9,11},{10,... | collective-permute-start | bytes 294920 | tf_op jit(solution)/shard_map/ppermute | solution.py:354
  56.0 5.1 %collective-permute-start.21 = (bf16[2,3,64,256]{3,2,1,0:T(8,128)(2,1)S(1)}, bf16[2,3,64,256]{3,2,1,0:T(8,128)(2,1)S(1)}, u32[]{:S(2)}, u32[]{:S(2)}) collective-permute-start(bf16[2,3,64,256]{3,2,1,0:T(8,128)(2,1)S(1)} %collective-permute-done.20.refs_15_), channel_id=1, source_target_pairs={{0,1},{1,0},{2,3},{3,2},{4,5},{5,4},{6,7},{7,6},{8,9},{9,8},{10,11... | collective-permute-start | bytes 589832 | tf_op jit(solution)/shard_map/ppermute | solution.py:354
  59.7 1.3 %collective-permute-start.24 = (bf16[1,3,64,256]{3,2,1,0:T(8,128)(2,1)S(1)}, bf16[1,3,64,256]{3,2,1,0:T(8,128)(2,1)S(1)}, u32[]{:S(2)}, u32[]{:S(2)}) collective-permute-start(bf16[1,3,64,256]{3,2,1,0:T(8,128)(2,1)S(1)} %collective-permute-done.23.refs_19_), channel_id=1, source_target_pairs={{0,1},{1,0},{2,3},{3,2},{4,5},{5,4},{6,7},{7,6},{8,9},{9,8},{10,11... | collective-permute-start | bytes 294920 | tf_op jit(solution)/shard_map/ppermute | solution.py:354

commit v19 on v18

--- a/solution.py
+++ b/solution.py
@@ -268,10 +268,6 @@
     for_each_group(False, load)
     assemble(0, 0)
     for_each_group(True, wait)
-    for copy in sums:
-        copy.wait()
-    proj_ref[...] = sum(held[k] for k in range(roles))
-
     def write(c, at, d):
         return pltpu.make_async_copy(
             done.at[at, d],
@@ -295,9 +291,15 @@
                 )
                 write(c, at, d).start()
 
+    for copy in sums:
+        copy.wait()
+    held[0] = sum(held[k] for k in range(roles))
+    leave = pltpu.make_async_copy(held.at[0], proj_ref, share_sem.at[0])
+    leave.start()
     for at in range(2):
         for d in range(3):
             write(2, at, d).wait()
+    leave.wait()
 
 
 pinned = pltpu.with_memory_space_constraint
@@ -439,10 +441,10 @@
     one = hop(own, own)
     crossed = cross(kernel(cut_kernel, columns(1), half, [own], "cut_columns"))
     cut_one = kernel(cut_kernel, columns(2), half, list(one), "cut_columns")
-    two = hop(after(one[0], crossed[1]), one[1])
+    two = hop(after(one[0], crossed[1], *parts), one[1])
     in_hbm = pass_on(crossed + cross(cut_one), role)
     cut_two = kernel(cut_kernel, columns(2), half, list(two), "cut_columns")
-    three = hop(after(two[0], *parts), two[1])
+    three = hop(*two)
     in_vmem = pass_on(cross(cut_two), role)
     half_shard = pltpu.VMEM(piece, jnp.bfloat16)
     cut_three, *halves = kernel(
@@ -471,7 +473,7 @@
         + [HBM] * len(in_hbm)
         + [VMEM] * len(in_vmem)
         + [HBM] * len(parts),
-        out_specs=(ANY, VMEM),
+        out_specs=(ANY, ANY),
         scratch_shapes=[
             pltpu.VMEM((2, 2 * run, total_frames), jnp.bfloat16),
             pltpu.VMEM((3, total_frames, block), jnp.bfloat16),

time: 70.5 us -> 69 us (0.979)
    ppermute x4, waiting for transfers between devices: 5.01 us -> 11.2 us  [hop(): lax.ppermute(down, 'frames', backward)]
    ppermute x4, waiting for transfers between devices: 7.92 us -> 4.64 us  [hop(): lax.ppermute(up, 'frames', forward)]
    ppermute x3, waiting for transfers between devices: 3.16 us -> 0.01 us  [cross(): return [cut, lax.ppermute(cut, axes, pairs(0, 2))]]
  transfers between devices with their start and end apart: 25 -> 25, of which waited for: 15 -> 13; matrix products, arithmetic and copies ran while one was open for 0% -> 0% of each run, Pallas kernels for 3% -> 4%
where the time goes in v19:
time: 69 us; the launch traced here: 68.7 us
  waiting for transfers between devices  28.7 us (42%)
  starting transfers between devices  23.9 us (35%)
  Pallas kernels  13.2 us (19%)
  local copies, waits for them, and re-layouts  2.01 us (3%)
  between operations  0.84 us (1%)
    ppermute x14, waiting for transfers between devices, swap(): lax.ppermute(value, 'atoms', [(a, a ^ distance) for a in range(atom_axis)])  12.9 us
    ppermute x4, waiting for transfers between devices, hop(): lax.ppermute(down, 'frames', backward)  11.2 us
    ppermute x3, starting transfers between devices, cross(): return [cut, lax.ppermute(cut, axes, pairs(0, 2))]  8.93 us
    pallas_call x1, Pallas kernels, per_device(): pl.pallas_call(functools.partial(covariance_kernel, frame_axis, atom_axis...  8.55 us
    ppermute x14, starting transfers between devices, swap(): lax.ppermute(value, 'atoms', [(a, a ^ distance) for a in range(atom_axis)])  6.76 us
    ppermute x4, waiting for transfers between devices, hop(): lax.ppermute(up, 'frames', forward)  4.64 us
    ppermute x4, starting transfers between devices, hop(): lax.ppermute(up, 'frames', forward)  4.22 us
    ppermute x4, starting transfers between devices, hop(): lax.ppermute(down, 'frames', backward)  3.98 us
  transfers between devices with their start and end apart: 25, of which 13 were waited for; matrix products, arithmetic and copies ran while one was open for 0% of the time, Pallas kernels for 4%

profile of v19, /device:TPU:0, one launch (start us, length us, event | category | flops | bytes accessed | tf_op | source)
XLA Modules:
  0.0 68.7 jit_solution(7196304247299557480)
XLA Ops:
  0.6 1.7 %local_moments.1 = (f32[24,64]{1,0:T(8,128)S(1)}, f32[3,64,1024]{2,1,0:T(8,128)S(1)}, f32[3,1024]{1,0:T(4,128)S(1)}) custom-call(f32[3,64,1024]{2,1,0:T(8,128)} %bitcast.5, f32[3,1024]{1,0:T(4,128)} %ref_hbm.1), custom_call_target="tpu_custom_call" | custom-call | tf_op jit(solution)/shard_map/local_moments/pallas_call | solution.py:342
  2.3 2.4 %collective-permute-start.2 = (f32[24,64]{1,0:T(8,128)S(1)}, f32[24,64]{1,0:T(8,128)S(1)}, u32[]{:S(2)}, u32[]{:S(2)}) collective-permute-start(f32[24,64]{1,0:T(8,128)S(1)} %get-tuple-element.20.refs_0_), channel_id=1, source_target_pairs={{0,3},{1,2},{2,1},{3,0},{4,7},{5,6},{6,5},{7,4},{8,11},{9,10},{10,... | collective-permute-start | bytes 18440 | tf_op jit(solution)/shard_map/ppermute | solution.py:356
  4.7 0.6 collective-permute-start.1
  5.4 0.0 collective-permute-start
  5.4 0.7 %collective-permute-done.2.refs_3_ = f32[24,64]{1,0:T(8,128)S(1)} collective-permute-done((f32[24,64]{1,0:T(8,128)S(1)}, f32[24,64]{1,0:T(8,128)S(1)}, u32[]{:S(2)}, u32[]{:S(2)}) %collective-permute-start.2) | collective-permute-done | bytes 6176 | tf_op jit(solution)/shard_map/ppermute | solution.py:356
  6.1 2.3 %collective-permute-done.1.refs_2_ = f32[24,64]{1,0:T(8,128)S(1)} collective-permute-done((f32[24,64]{1,0:T(8,128)S(1)}, f32[24,64]{1,0:T(8,128)S(1)}, u32[]{:S(2)}, u32[]{:S(2)}) %collective-permute-start.1) | collective-permute-done | bytes 6176 | tf_op jit(solution)/shard_map/ppermute | solution.py:356
  8.4 0.0 collective-permute-done.refs_1_
  8.4 0.6 polar_align.1
  9.0 1.6 %collective-permute-start.3 = (bf16[2,3,256,128]{3,2,1,0:T(8,128)(2,1)S(1)}, bf16[2,3,256,128]{3,2,1,0:T(8,128)(2,1)S(1)}, u32[]{:S(2)}, u32[]{:S(2)}) collective-permute-start(bf16[2,3,256,128]{3,2,1,0:T(8,128)(2,1)S(1)} %get-tuple-element.23.refs_0_), channel_id=1, source_target_pairs={{0,8},{8,16},{16,24},{24,28},{28,20},{20,12},{12,4},{4,0},{1,9},{9... | collective-permute-start | bytes 1179656 | tf_op jit(solution)/shard_map/ppermute | solution.py:439
  10.7 0.4 collective-permute-start.4
  11.1 0.1 cut_columns.5.refs_0_
  11.3 2.6 %collective-permute-start.5 = (bf16[1,3,64,512]{3,2,1,0:T(8,128)(2,1)S(1)}, bf16[1,3,64,512]{3,2,1,0:T(8,128)(2,1)S(1)}, u32[]{:S(2)}, u32[]{:S(2)}) collective-permute-start(bf16[1,3,64,512]{3,2,1,0:T(8,128)(2,1)S(1)} %cut_columns.5.refs_0_), channel_id=1, source_target_pairs={{0,2},{4,6},{9,11},{13,15},{18,16},{22,20},{27,25},{31,29}} | collective-permute-start | bytes 589832 | tf_op jit(solution)/shard_map/ppermute | solution.py:418
  13.8 0.0 copy-start
  13.8 1.4 %copy-done = bf16[3,1024,256]{2,1,0:T(8,128)(2,1)S(1)} copy-done((bf16[3,1024,256]{2,1,0:T(8,128)(2,1)S(1)}, bf16[3,1024,256]{2,1,0:T(8,128)(2,1)}, u32[]{:S(2)}) %copy-start) | copy-done | bytes 1572888
  15.2 0.5 project.1
  15.7 0.1 collective-permute-start.6
  15.8 0.1 collective-permute-start.7
  15.9 1.1 %collective-permute-done.6.refs_22_ = f32[64,64]{1,0:T(8,128)S(1)} collective-permute-done((f32[64,64]{1,0:T(8,128)S(1)}, f32[64,64]{1,0:T(8,128)S(1)}, u32[]{:S(2)}, u32[]{:S(2)}) %collective-permute-start.6) | collective-permute-done | bytes 16416 | tf_op jit(solution)/shard_map/ppermute | solution.py:356
  17.0 0.7 collective-permute-start.8
  17.7 2.1 %collective-permute-done.7.refs_23_ = f32[64,64]{1,0:T(8,128)S(1)} collective-permute-done((f32[64,64]{1,0:T(8,128)S(1)}, f32[64,64]{1,0:T(8,128)S(1)}, u32[]{:S(2)}, u32[]{:S(2)}) %collective-permute-start.7) | collective-permute-done | bytes 16416 | tf_op jit(solution)/shard_map/ppermute | solution.py:356
  19.8 0.6 collective-permute-done.8.refs_24_
  20.4 0.0 collective-permute-done.5.refs_1_
  20.4 0.0 collective-permute-done.3.refs_0_.refs_1_
  20.4 0.0 copy-done.5
  20.4 0.6 copy-done.6
  21.0 0.0 collective-permute-done.4.refs_1_.refs_2_
  21.0 1.5 %collective-permute-start.10 = (bf16[2,3,256,128]{3,2,1,0:T(8,128)(2,1)S(1)}, bf16[2,3,256,128]{3,2,1,0:T(8,128)(2,1)S(1)}, u32[]{:S(2)}, u32[]{:S(2)}) collective-permute-start(bf16[2,3,256,128]{3,2,1,0:T(8,128)(2,1)S(1)} %collective-permute-done.4.refs_1_.refs_2_), channel_id=1, source_target_pairs={{8,0},{16,8},{24,16},{28,24},{20,28},{12,20},{4,12},{0,4},{9,1},{1... | collective-permute-start | bytes 1179656 | tf_op jit(solution)/shard_map/ppermute | solution.py:439
  22.5 0.5 collective-permute-start.9
  23.0 0.2 cut_columns.6.refs_2_
  23.2 3.6 %collective-permute-start.13 = (bf16[2,3,64,512]{3,2,1,0:T(8,128)(2,1)S(1)}, bf16[2,3,64,512]{3,2,1,0:T(8,128)(2,1)}, u32[]{:S(2)}, u32[]{:S(2)}) collective-permute-start(bf16[2,3,64,512]{3,2,1,0:T(8,128)(2,1)S(1)} %cut_columns.6.refs_2_), channel_id=1, source_target_pairs={{0,2},{4,6},{9,11},{13,15},{18,16},{22,20},{27,25},{31,29}} | collective-permute-start | bytes 1179656 | tf_op jit(solution)/shard_map/ppermute | solution.py:418
  26.7 5.7 %collective-permute-done.10.refs_1_.refs_4_ = bf16[2,3,256,128]{3,2,1,0:T(8,128)(2,1)S(1)} collective-permute-done((bf16[2,3,256,128]{3,2,1,0:T(8,128)(2,1)S(1)}, bf16[2,3,256,128]{3,2,1,0:T(8,128)(2,1)S(1)}, u32[]{:S(2)}, u32[]{:S(2)}) %collective-permute-start.10) | collective-permute-done | bytes 393248 | tf_op jit(solution)/shard_map/ppermute | solution.py:439
  32.5 1.2 %collective-permute-start.12 = (bf16[2,3,256,128]{3,2,1,0:T(8,128)(2,1)S(1)}, bf16[2,3,256,128]{3,2,1,0:T(8,128)(2,1)S(1)}, u32[]{:S(2)}, u32[]{:S(2)}) collective-permute-start(bf16[2,3,256,128]{3,2,1,0:T(8,128)(2,1)S(1)} %collective-permute-done.10.refs_1_.refs_4_), channel_id=1, source_target_pairs={{8,0},{16,8},{24,16},{28,24},{20,28},{12,20},{4,12},{0,4},{9,1},{1... | collective-permute-start | bytes 1179656 | tf_op jit(solution)/shard_map/ppermute | solution.py:439
  33.7 0.0 collective-permute-done.9.refs_0_.refs_3_
  33.7 0.8 %collective-permute-start.11 = (bf16[2,3,256,128]{3,2,1,0:T(8,128)(2,1)S(1)}, bf16[2,3,256,128]{3,2,1,0:T(8,128)(2,1)S(1)}, u32[]{:S(2)}, u32[]{:S(2)}) collective-permute-start(bf16[2,3,256,128]{3,2,1,0:T(8,128)(2,1)S(1)} %collective-permute-done.9.refs_0_.refs_3_), channel_id=1, source_target_pairs={{0,8},{8,16},{16,24},{24,28},{28,20},{20,12},{12,4},{4,0},{1,9},{9... | collective-permute-start | bytes 1179656 | tf_op jit(solution)/shard_map/ppermute | solution.py:439
  34.5 0.0 collective-permute-done.13.refs_3_
  34.5 1.0 %pass_on.2.refs_9_ = bf16[3,3,64,512]{3,2,1,0:T(8,128)(2,1)S(1)} custom-call(s32[1]{0:T(128)} %bitcast.role_ref, bf16[1,3,64,512]{3,2,1,0:T(8,128)(2,1)S(1)} %cut_columns.5.refs_0_, bf16[1,3,64,512]{3,2,1,0:T(8,128)(2,1)S(1)} %collective-permute-done.5.refs_1_, bf16[2,3,64,512]{3,2,1,0:T(8,128)(2,1)S(1)} %cut_columns.6.refs_2_, ...), custom_call_target="tpu_custom_call" | custom-call | tf_op jit(solution)/shard_map/pass_on/pallas_call | solution.py:408
  35.5 0.1 collective-permute-start.16
  35.6 0.2 cut_columns.8.refs_0_
  35.8 2.8 %collective-permute-start.17 = (bf16[2,3,64,512]{3,2,1,0:T(8,128)(2,1)S(1)}, bf16[2,3,64,512]{3,2,1,0:T(8,128)(2,1)S(1)}, u32[]{:S(2)}, u32[]{:S(2)}) collective-permute-start(bf16[2,3,64,512]{3,2,1,0:T(8,128)(2,1)S(1)} %cut_columns.8.refs_0_), channel_id=1, source_target_pairs={{0,2},{4,6},{9,11},{13,15},{18,16},{22,20},{27,25},{31,29}} | collective-permute-start | bytes 1179656 | tf_op jit(solution)/shard_map/ppermute | solution.py:418
  38.6 4.5 %collective-permute-done.12.down_ref.refs_6_ = bf16[2,3,256,128]{3,2,1,0:T(8,128)(2,1)S(1)} collective-permute-done((bf16[2,3,256,128]{3,2,1,0:T(8,128)(2,1)S(1)}, bf16[2,3,256,128]{3,2,1,0:T(8,128)(2,1)S(1)}, u32[]{:S(2)}, u32[]{:S(2)}) %collective-permute-start.12) | collective-permute-done | bytes 393248 | tf_op jit(solution)/shard_map/ppermute | solution.py:439
  43.2 0.6 collective-permute-done.11.up_ref.refs_5_
  43.8 0.2 cut_columns.7
  44.0 0.1 collective-permute-start.19
  44.0 1.3 %collective-permute-start.14 = (bf16[3,256,128]{2,1,0:T(8,128)(2,1)S(1)}, bf16[3,256,128]{2,1,0:T(8,128)(2,1)S(1)}, u32[]{:S(2)}, u32[]{:S(2)}) collective-permute-start(bf16[3,256,128]{2,1,0:T(8,128)(2,1)S(1)} %get-tuple-element.31), channel_id=1, source_target_pairs={{0,8},{8,16},{16,24},{24,28},{28,20},{20,12},{12,4},{4,0},{1,9},{9... | collective-permute-start | bytes 589832 | tf_op jit(solution)/shard_map/ppermute | solution.py:439
  45.3 0.8 %collective-permute-start.15 = (bf16[3,256,128]{2,1,0:T(8,128)(2,1)S(1)}, bf16[3,256,128]{2,1,0:T(8,128)(2,1)S(1)}, u32[]{:S(2)}, u32[]{:S(2)}) collective-permute-start(bf16[3,256,128]{2,1,0:T(8,128)(2,1)S(1)} %get-tuple-element.32), channel_id=1, source_target_pairs={{8,0},{16,8},{24,16},{28,24},{20,28},{12,20},{4,12},{0,4},{9,1},{1... | collective-permute-start | bytes 589832 | tf_op jit(solution)/shard_map/ppermute | solution.py:439
  46.1 0.0 collective-permute-done.17.refs_1_
  46.2 0.0 collective-permute-done.19.beside_ref.refs_14_
  46.2 1.1 %collective-permute-start.20 = (bf16[2,3,64,256]{3,2,1,0:T(8,128)(2,1)S(1)}, bf16[2,3,64,256]{3,2,1,0:T(8,128)(2,1)S(1)}, u32[]{:S(2)}, u32[]{:S(2)}) collective-permute-start(bf16[2,3,64,256]{3,2,1,0:T(8,128)(2,1)S(1)} %pick_half.2), channel_id=1, source_target_pairs={{0,2},{1,3},{2,0},{3,1},{4,6},{5,7},{6,4},{7,5},{8,10},{9,11},{10,... | collective-permute-start | bytes 589832 | tf_op jit(solution)/shard_map/ppermute | solution.py:356
  47.3 0.0 collective-permute-done.16.refs_10_
  47.3 4.1 %collective-permute-done.14.up_half.refs_7_ = bf16[3,256,128]{2,1,0:T(8,128)(2,1)S(1)} collective-permute-done((bf16[3,256,128]{2,1,0:T(8,128)(2,1)S(1)}, bf16[3,256,128]{2,1,0:T(8,128)(2,1)S(1)}, u32[]{:S(2)}, u32[]{:S(2)}) %collective-permute-start.14) | collective-permute-done | bytes 196640 | tf_op jit(solution)/shard_map/ppermute | solution.py:439
  51.4 0.9 %collective-permute-done.15.down_half.refs_8_ = bf16[3,256,128]{2,1,0:T(8,128)(2,1)S(1)} collective-permute-done((bf16[3,256,128]{2,1,0:T(8,128)(2,1)S(1)}, bf16[3,256,128]{2,1,0:T(8,128)(2,1)S(1)}, u32[]{:S(2)}, u32[]{:S(2)}) %collective-permute-start.15) | collective-permute-done | bytes 196640 | tf_op jit(solution)/shard_map/ppermute | solution.py:439
  52.3 0.1 cut_columns.9.own_ref.refs_17_
  52.4 0.1 collective-permute-start.22
  52.5 0.5 collective-permute-start.18
  53.0 0.0 collective-permute-done.20.refs_15_
  53.0 0.9 %collective-permute-done.22.beside_ref.refs_18_ = bf16[1,3,64,512]{3,2,1,0:T(8,128)(2,1)S(1)} collective-permute-done((bf16[1,3,64,512]{3,2,1,0:T(8,128)(2,1)S(1)}, bf16[1,3,64,512]{3,2,1,0:T(8,128)(2,1)S(1)}, u32[]{:S(2)}, u32[]{:S(2)}) %collective-permute-start.22) | collective-permute-done | bytes 196640 | tf_op jit(solution)/shard_map/ppermute | solution.py:356
  54.0 1.0 %collective-permute-start.23 = (bf16[1,3,64,256]{3,2,1,0:T(8,128)(2,1)S(1)}, bf16[1,3,64,256]{3,2,1,0:T(8,128)(2,1)S(1)}, u32[]{:S(2)}, u32[]{:S(2)}) collective-permute-start(bf16[1,3,64,256]{3,2,1,0:T(8,128)(2,1)S(1)} %pick_half.3), channel_id=1, source_target_pairs={{0,2},{1,3},{2,0},{3,1},{4,6},{5,7},{6,4},{7,5},{8,10},{9,11},{10,... | collective-permute-start | bytes 294920 | tf_op jit(solution)/shard_map/ppermute | solution.py:356
  55.0 0.0 collective-permute-start.21
  55.0 3.9 %collective-permute-done.23.refs_19_ = bf16[1,3,64,256]{3,2,1,0:T(8,128)(2,1)S(1)} collective-permute-done((bf16[1,3,64,256]{3,2,1,0:T(8,128)(2,1)S(1)}, bf16[1,3,64,256]{3,2,1,0:T(8,128)(2,1)S(1)}, u32[]{:S(2)}, u32[]{:S(2)}) %collective-permute-start.23) | collective-permute-done | bytes 98336 | tf_op jit(solution)/shard_map/ppermute | solution.py:356
  58.8 0.0 collective-permute-start.24
  58.8 0.0 collective-permute-done.18.refs_12_
  58.8 1.3 %collective-permute-done.24.refs_20_ = bf16[1,3,64,256]{3,2,1,0:T(8,128)(2,1)S(1)} collective-permute-done((bf16[1,3,64,256]{3,2,1,0:T(8,128)(2,1)S(1)}, bf16[1,3,64,256]{3,2,1,0:T(8,128)(2,1)S(1)}, u32[]{:S(2)}, u32[]{:S(2)}) %collective-permute-start.24) | collective-permute-done | bytes 98336 | tf_op jit(solution)/shard_map/ppermute | solution.py:356
  60.1 0.0 collective-permute-done.21.refs_16_
  60.1 8.6 %covariance_tile.1 = (f32[3,3,1024,512]{3,2,1,0:T(8,128)}, f32[64,64]{1,0:T(8,128)}) custom-call(s32[1]{0:T(128)} %bitcast.role_ref, bf16[2,3,256,128]{3,2,1,0:T(8,128)(2,1)S(1)} %get-tuple-element.23.refs_0_, bf16[2,3,256,128]{3,2,1,0:T(8,128)(2,1)S(1)} %collective-permute-done.3.refs_0_.refs_1_, ...), custom_call_target="tpu_custom_call" | custom-call | flops 4831838208 | bytes 25165824 | tf_op jit(solution)/shard_map/covariance_tile/pallas_call | solution.py:466
  (13 shorter events, 0.1 us)
Async XLA Ops:
  2.3 3.8 %collective-permute-start.2 = (f32[24,64]{1,0:T(8,128)S(1)}, f32[24,64]{1,0:T(8,128)S(1)}, u32[]{:S(2)}, u32[]{:S(2)}) collective-permute-start(f32[24,64]{1,0:T(8,128)S(1)} %get-tuple-element.20.refs_0_), channel_id=1, source_target_pairs={{0,3},{1,2},{2,1},{3,0},{4,7},{5,6},{6,5},{7,4},{8,11},{9,10},{10,... | collective-permute-start | bytes 18440 | tf_op jit(solution)/shard_map/ppermute | solution.py:356
  4.7 3.7 %collective-permute-start.1 = (f32[24,64]{1,0:T(8,128)S(1)}, f32[24,64]{1,0:T(8,128)S(1)}, u32[]{:S(2)}, u32[]{:S(2)}) collective-permute-start(f32[24,64]{1,0:T(8,128)S(1)} %get-tuple-element.20.refs_0_), channel_id=1, source_target_pairs={{0,2},{1,3},{2,0},{3,1},{4,6},{5,7},{6,4},{7,5},{8,10},{9,11},{10,... | collective-permute-start | bytes 18440 | tf_op jit(solution)/shard_map/ppermute | solution.py:356
  5.4 3.1 %collective-permute-start = (f32[24,64]{1,0:T(8,128)S(1)}, f32[24,64]{1,0:T(8,128)S(1)}, u32[]{:S(2)}, u32[]{:S(2)}) collective-permute-start(f32[24,64]{1,0:T(8,128)S(1)} %get-tuple-element.20.refs_0_), channel_id=1, source_target_pairs={{0,1},{1,0},{2,3},{3,2},{4,5},{5,4},{6,7},{7,6},{8,9},{9,8},{10,11... | collective-permute-start | bytes 18440 | tf_op jit(solution)/shard_map/ppermute | solution.py:356
  9.0 11.3 %collective-permute-start.3 = (bf16[2,3,256,128]{3,2,1,0:T(8,128)(2,1)S(1)}, bf16[2,3,256,128]{3,2,1,0:T(8,128)(2,1)S(1)}, u32[]{:S(2)}, u32[]{:S(2)}) collective-permute-start(bf16[2,3,256,128]{3,2,1,0:T(8,128)(2,1)S(1)} %get-tuple-element.23.refs_0_), channel_id=1, source_target_pairs={{0,8},{8,16},{16,24},{24,28},{28,20},{20,12},{12,4},{4,0},{1,9},{9... | collective-permute-start | bytes 1179656 | tf_op jit(solution)/shard_map/ppermute | solution.py:439
  10.7 10.3 %collective-permute-start.4 = (bf16[2,3,256,128]{3,2,1,0:T(8,128)(2,1)S(1)}, bf16[2,3,256,128]{3,2,1,0:T(8,128)(2,1)S(1)}, u32[]{:S(2)}, u32[]{:S(2)}) collective-permute-start(bf16[2,3,256,128]{3,2,1,0:T(8,128)(2,1)S(1)} %get-tuple-element.23.refs_0_), channel_id=1, source_target_pairs={{8,0},{16,8},{24,16},{28,24},{20,28},{12,20},{4,12},{0,4},{9,1},{1... | collective-permute-start | bytes 1179656 | tf_op jit(solution)/shard_map/ppermute | solution.py:439
  11.3 9.1 %collective-permute-start.5 = (bf16[1,3,64,512]{3,2,1,0:T(8,128)(2,1)S(1)}, bf16[1,3,64,512]{3,2,1,0:T(8,128)(2,1)S(1)}, u32[]{:S(2)}, u32[]{:S(2)}) collective-permute-start(bf16[1,3,64,512]{3,2,1,0:T(8,128)(2,1)S(1)} %cut_columns.5.refs_0_), channel_id=1, source_target_pairs={{0,2},{4,6},{9,11},{13,15},{18,16},{22,20},{27,25},{31,29}} | collective-permute-start | bytes 589832 | tf_op jit(solution)/shard_map/ppermute | solution.py:418
  13.8 1.4 %copy-start = (bf16[3,1024,256]{2,1,0:T(8,128)(2,1)S(1)}, bf16[3,1024,256]{2,1,0:T(8,128)(2,1)}, u32[]{:S(2)}) copy-start(bf16[3,1024,256]{2,1,0:T(8,128)(2,1)} %eig_ref.1) | copy-start | bytes 4718596
  15.7 17.9 %copy-start.2 = (f32[64,64]{1,0:T(8,128)}, f32[64,64]{1,0:T(8,128)S(1)}, u32[]{:S(2)}) copy-start(f32[64,64]{1,0:T(8,128)S(1)} %get-tuple-element.25.refs_21_) | copy-start | bytes 49156
  15.7 1.3 %collective-permute-start.6 = (f32[64,64]{1,0:T(8,128)S(1)}, f32[64,64]{1,0:T(8,128)S(1)}, u32[]{:S(2)}, u32[]{:S(2)}) collective-permute-start(f32[64,64]{1,0:T(8,128)S(1)} %get-tuple-element.26), channel_id=1, source_target_pairs={{0,1},{1,0},{2,3},{3,2},{4,5},{5,4},{6,7},{7,6},{8,9},{9,8},{10,11... | collective-permute-start | bytes 49160 | tf_op jit(solution)/shard_map/ppermute | solution.py:356
  15.8 4.0 %collective-permute-start.7 = (f32[64,64]{1,0:T(8,128)S(1)}, f32[64,64]{1,0:T(8,128)S(1)}, u32[]{:S(2)}, u32[]{:S(2)}) collective-permute-start(f32[64,64]{1,0:T(8,128)S(1)} %get-tuple-element.27), channel_id=1, source_target_pairs={{0,2},{1,3},{2,0},{3,1},{4,6},{5,7},{6,4},{7,5},{8,10},{9,11},{10,... | collective-permute-start | bytes 49160 | tf_op jit(solution)/shard_map/ppermute | solution.py:356
  17.0 3.4 %copy-start.4 = (f32[64,64]{1,0:T(8,128)}, f32[64,64]{1,0:T(8,128)S(1)}, u32[]{:S(2)}) copy-start(f32[64,64]{1,0:T(8,128)S(1)} %collective-permute-done.6.refs_22_) | copy-start | bytes 49156
  17.0 3.3 %collective-permute-start.8 = (f32[64,64]{1,0:T(8,128)S(1)}, f32[64,64]{1,0:T(8,128)S(1)}, u32[]{:S(2)}, u32[]{:S(2)}) collective-permute-start(f32[64,64]{1,0:T(8,128)S(1)} %get-tuple-element.28), channel_id=1, source_target_pairs={{0,3},{1,2},{2,1},{3,0},{4,7},{5,6},{6,5},{7,4},{8,11},{9,10},{10,... | collective-permute-start | bytes 49160 | tf_op jit(solution)/shard_map/ppermute | solution.py:356
  19.8 0.6 copy-start.5
  20.4 0.6 copy-start.6
  21.0 11.5 %collective-permute-start.10 = (bf16[2,3,256,128]{3,2,1,0:T(8,128)(2,1)S(1)}, bf16[2,3,256,128]{3,2,1,0:T(8,128)(2,1)S(1)}, u32[]{:S(2)}, u32[]{:S(2)}) collective-permute-start(bf16[2,3,256,128]{3,2,1,0:T(8,128)(2,1)S(1)} %collective-permute-done.4.refs_1_.refs_2_), channel_id=1, source_target_pairs={{8,0},{16,8},{24,16},{28,24},{20,28},{12,20},{4,12},{0,4},{9,1},{1... | collective-permute-start | bytes 1179656 | tf_op jit(solution)/shard_map/ppermute | solution.py:439
  22.5 11.2 %collective-permute-start.9 = (bf16[2,3,256,128]{3,2,1,0:T(8,128)(2,1)S(1)}, bf16[2,3,256,128]{3,2,1,0:T(8,128)(2,1)S(1)}, u32[]{:S(2)}, u32[]{:S(2)}) collective-permute-start(bf16[2,3,256,128]{3,2,1,0:T(8,128)(2,1)S(1)} %collective-permute-done.3.refs_0_.refs_1_), channel_id=1, source_target_pairs={{0,8},{8,16},{16,24},{24,28},{28,20},{20,12},{12,4},{4,0},{1,9},{9... | collective-permute-start | bytes 1179656 | tf_op jit(solution)/shard_map/ppermute | solution.py:439
  23.2 11.3 %collective-permute-start.13 = (bf16[2,3,64,512]{3,2,1,0:T(8,128)(2,1)S(1)}, bf16[2,3,64,512]{3,2,1,0:T(8,128)(2,1)}, u32[]{:S(2)}, u32[]{:S(2)}) collective-permute-start(bf16[2,3,64,512]{3,2,1,0:T(8,128)(2,1)S(1)} %cut_columns.6.refs_2_), channel_id=1, source_target_pairs={{0,2},{4,6},{9,11},{13,15},{18,16},{22,20},{27,25},{31,29}} | collective-permute-start | bytes 1179656 | tf_op jit(solution)/shard_map/ppermute | solution.py:418
  32.5 10.7 %collective-permute-start.12 = (bf16[2,3,256,128]{3,2,1,0:T(8,128)(2,1)S(1)}, bf16[2,3,256,128]{3,2,1,0:T(8,128)(2,1)S(1)}, u32[]{:S(2)}, u32[]{:S(2)}) collective-permute-start(bf16[2,3,256,128]{3,2,1,0:T(8,128)(2,1)S(1)} %collective-permute-done.10.refs_1_.refs_4_), channel_id=1, source_target_pairs={{8,0},{16,8},{24,16},{28,24},{20,28},{12,20},{4,12},{0,4},{9,1},{1... | collective-permute-start | bytes 1179656 | tf_op jit(solution)/shard_map/ppermute | solution.py:439
  33.7 10.1 %collective-permute-start.11 = (bf16[2,3,256,128]{3,2,1,0:T(8,128)(2,1)S(1)}, bf16[2,3,256,128]{3,2,1,0:T(8,128)(2,1)S(1)}, u32[]{:S(2)}, u32[]{:S(2)}) collective-permute-start(bf16[2,3,256,128]{3,2,1,0:T(8,128)(2,1)S(1)} %collective-permute-done.9.refs_0_.refs_3_), channel_id=1, source_target_pairs={{0,8},{8,16},{16,24},{24,28},{28,20},{20,12},{12,4},{4,0},{1,9},{9... | collective-permute-start | bytes 1179656 | tf_op jit(solution)/shard_map/ppermute | solution.py:439
  35.5 24.6 %copy-start.1 = (bf16[3,3,64,512]{3,2,1,0:T(8,128)(2,1)}, bf16[3,3,64,512]{3,2,1,0:T(8,128)(2,1)S(1)}, u32[]{:S(2)}) copy-start(bf16[3,3,64,512]{3,2,1,0:T(8,128)(2,1)S(1)} %pass_on.2.refs_9_) | copy-start | bytes 1769476
  35.5 11.8 %collective-permute-start.16 = (bf16[3,3,64,512]{3,2,1,0:T(8,128)(2,1)S(1)}, bf16[3,3,64,512]{3,2,1,0:T(8,128)(2,1)S(1)}, u32[]{:S(2)}, u32[]{:S(2)}) collective-permute-start(bf16[3,3,64,512]{3,2,1,0:T(8,128)(2,1)S(1)} %pass_on.2.refs_9_), channel_id=1, source_target_pairs={{0,1},{1,0},{2,3},{3,2},{4,5},{5,4},{6,7},{7,6},{8,9},{9,8},{10,11... | collective-permute-start | bytes 1769480 | tf_op jit(solution)/shard_map/ppermute | solution.py:356
  35.8 10.3 %collective-permute-start.17 = (bf16[2,3,64,512]{3,2,1,0:T(8,128)(2,1)S(1)}, bf16[2,3,64,512]{3,2,1,0:T(8,128)(2,1)S(1)}, u32[]{:S(2)}, u32[]{:S(2)}) collective-permute-start(bf16[2,3,64,512]{3,2,1,0:T(8,128)(2,1)S(1)} %cut_columns.8.refs_0_), channel_id=1, source_target_pairs={{0,2},{4,6},{9,11},{13,15},{18,16},{22,20},{27,25},{31,29}} | collective-permute-start | bytes 1179656 | tf_op jit(solution)/shard_map/ppermute | solution.py:418
  44.0 2.2 %collective-permute-start.19 = (bf16[2,3,64,512]{3,2,1,0:T(8,128)(2,1)S(1)}, bf16[2,3,64,512]{3,2,1,0:T(8,128)(2,1)S(1)}, u32[]{:S(2)}, u32[]{:S(2)}) collective-permute-start(bf16[2,3,64,512]{3,2,1,0:T(8,128)(2,1)S(1)} %get-tuple-element.33.own_ref.refs_13_), channel_id=1, source_target_pairs={{0,1},{1,0},{2,3},{3,2},{4,5},{5,4},{6,7},{7,6},{8,9},{9,8},{10,11... | collective-permute-start | bytes 1179656 | tf_op jit(solution)/shard_map/ppermute | solution.py:356
  44.0 7.3 %collective-permute-start.14 = (bf16[3,256,128]{2,1,0:T(8,128)(2,1)S(1)}, bf16[3,256,128]{2,1,0:T(8,128)(2,1)S(1)}, u32[]{:S(2)}, u32[]{:S(2)}) collective-permute-start(bf16[3,256,128]{2,1,0:T(8,128)(2,1)S(1)} %get-tuple-element.31), channel_id=1, source_target_pairs={{0,8},{8,16},{16,24},{24,28},{28,20},{20,12},{12,4},{4,0},{1,9},{9... | collective-permute-start | bytes 589832 | tf_op jit(solution)/shard_map/ppermute | solution.py:439
  45.3 7.0 %collective-permute-start.15 = (bf16[3,256,128]{2,1,0:T(8,128)(2,1)S(1)}, bf16[3,256,128]{2,1,0:T(8,128)(2,1)S(1)}, u32[]{:S(2)}, u32[]{:S(2)}) collective-permute-start(bf16[3,256,128]{2,1,0:T(8,128)(2,1)S(1)} %get-tuple-element.32), channel_id=1, source_target_pairs={{8,0},{16,8},{24,16},{28,24},{20,28},{12,20},{4,12},{0,4},{9,1},{1... | collective-permute-start | bytes 589832 | tf_op jit(solution)/shard_map/ppermute | solution.py:439
  46.2 6.8 %collective-permute-start.20 = (bf16[2,3,64,256]{3,2,1,0:T(8,128)(2,1)S(1)}, bf16[2,3,64,256]{3,2,1,0:T(8,128)(2,1)S(1)}, u32[]{:S(2)}, u32[]{:S(2)}) collective-permute-start(bf16[2,3,64,256]{3,2,1,0:T(8,128)(2,1)S(1)} %pick_half.2), channel_id=1, source_target_pairs={{0,2},{1,3},{2,0},{3,1},{4,6},{5,7},{6,4},{7,5},{8,10},{9,11},{10,... | collective-permute-start | bytes 589832 | tf_op jit(solution)/shard_map/ppermute | solution.py:356
  47.3 12.8 %copy-start.3 = (bf16[3,3,64,512]{3,2,1,0:T(8,128)(2,1)}, bf16[3,3,64,512]{3,2,1,0:T(8,128)(2,1)S(1)}, u32[]{:S(2)}) copy-start(bf16[3,3,64,512]{3,2,1,0:T(8,128)(2,1)S(1)} %collective-permute-done.16.refs_10_) | copy-start | bytes 1769476
  52.4 1.5 %collective-permute-start.22 = (bf16[1,3,64,512]{3,2,1,0:T(8,128)(2,1)S(1)}, bf16[1,3,64,512]{3,2,1,0:T(8,128)(2,1)S(1)}, u32[]{:S(2)}, u32[]{:S(2)}) collective-permute-start(bf16[1,3,64,512]{3,2,1,0:T(8,128)(2,1)S(1)} %cut_columns.9.own_ref.refs_17_), channel_id=1, source_target_pairs={{0,1},{1,0},{2,3},{3,2},{4,5},{5,4},{6,7},{7,6},{8,9},{9,8},{10,11... | collective-permute-start | bytes 589832 | tf_op jit(solution)/shard_map/ppermute | solution.py:356
  52.5 6.3 %collective-permute-start.18 = (bf16[2,3,64,512]{3,2,1,0:T(8,128)(2,1)S(1)}, bf16[2,3,64,512]{3,2,1,0:T(8,128)(2,1)S(1)}, u32[]{:S(2)}, u32[]{:S(2)}) collective-permute-start(bf16[2,3,64,512]{3,2,1,0:T(8,128)(2,1)S(1)} %pass_on.3.refs_11_), channel_id=1, source_target_pairs={{0,1},{1,0},{2,3},{3,2},{4,5},{5,4},{6,7},{7,6},{8,9},{9,8},{10,11... | collective-permute-start | bytes 1179656 | tf_op jit(solution)/shard_map/ppermute | solution.py:356
  54.0 4.9 %collective-permute-start.23 = (bf16[1,3,64,256]{3,2,1,0:T(8,128)(2,1)S(1)}, bf16[1,3,64,256]{3,2,1,0:T(8,128)(2,1)S(1)}, u32[]{:S(2)}, u32[]{:S(2)}) collective-permute-start(bf16[1,3,64,256]{3,2,1,0:T(8,128)(2,1)S(1)} %pick_half.3), channel_id=1, source_target_pairs={{0,2},{1,3},{2,0},{3,1},{4,6},{5,7},{6,4},{7,5},{8,10},{9,11},{10,... | collective-permute-start | bytes 294920 | tf_op jit(solution)/shard_map/ppermute | solution.py:356
  55.0 5.2 %collective-permute-start.21 = (bf16[2,3,64,256]{3,2,1,0:T(8,128)(2,1)S(1)}, bf16[2,3,64,256]{3,2,1,0:T(8,128)(2,1)S(1)}, u32[]{:S(2)}, u32[]{:S(2)}) collective-permute-start(bf16[2,3,64,256]{3,2,1,0:T(8,128)(2,1)S(1)} %collective-permute-done.20.refs_15_), channel_id=1, source_target_pairs={{0,1},{1,0},{2,3},{3,2},{4,5},{5,4},{6,7},{7,6},{8,9},{9,8},{10,11... | collective-permute-start | bytes 589832 | tf_op jit(solution)/shard_map/ppermute | solution.py:356
  58.8 1.3 %collective-permute-start.24 = (bf16[1,3,64,256]{3,2,1,0:T(8,128)(2,1)S(1)}, bf16[1,3,64,256]{3,2,1,0:T(8,128)(2,1)S(1)}, u32[]{:S(2)}, u32[]{:S(2)}) collective-permute-start(bf16[1,3,64,256]{3,2,1,0:T(8,128)(2,1)S(1)} %collective-permute-done.23.refs_19_), channel_id=1, source_target_pairs={{0,1},{1,0},{2,3},{3,2},{4,5},{5,4},{6,7},{7,6},{8,9},{9,8},{10,11... | collective-permute-start | bytes 294920 | tf_op jit(solution)/shard_map/ppermute | solution.py:356

commit v20 on v19

--- a/solution.py
+++ b/solution.py
@@ -439,10 +439,9 @@
         return lax.ppermute(up, "frames", forward), lax.ppermute(down, "frames", backward)
 
     one = hop(own, own)
-    crossed = cross(kernel(cut_kernel, columns(1), half, [own], "cut_columns"))
-    cut_one = kernel(cut_kernel, columns(2), half, list(one), "cut_columns")
-    two = hop(after(one[0], crossed[1], *parts), one[1])
-    in_hbm = pass_on(crossed + cross(cut_one), role)
+    cut_one = kernel(cut_kernel, columns(3), half, [own, *one], "cut_columns")
+    two = hop(after(one[0], *parts), one[1])
+    in_hbm = pass_on(cross(cut_one), role)
     cut_two = kernel(cut_kernel, columns(2), half, list(two), "cut_columns")
     three = hop(*two)
     in_vmem = pass_on(cross(cut_two), role)

time: 69 us -> 67.1 us (0.972); the launches traced: 68.7 us -> 65.9 us
  waiting for transfers between devices: 28.7 us -> 24.3 us
  starting transfers between devices: 23.9 us -> 25.6 us
  Pallas kernels: 13.2 us -> 12.1 us
  local copies, waits for them, and re-layouts: 2.01 us -> 3.02 us
    ppermute x4, waiting for transfers between devices: 11.2 us -> 7.31 us  [hop(): lax.ppermute(down, 'frames', backward)]
    ppermute x14, starting transfers between devices: 6.76 us -> 10.3 us  [swap(): lax.ppermute(value, 'atoms', [(a, a ^ distance) for a in range(atom_axis)])]
    ppermute x3 -> x2, waiting for transfers between devices: 0.01 us -> 2.26 us  [cross(): return [cut, lax.ppermute(cut, axes, pairs(0, 2))]]
    ppermute x3 -> x2, starting transfers between devices: 8.93 us -> 7.04 us  [cross(): return [cut, lax.ppermute(cut, axes, pairs(0, 2))]]
    ppermute x14, waiting for transfers between devices: 12.9 us -> 11.2 us  [swap(): lax.ppermute(value, 'atoms', [(a, a ^ distance) for a in range(atom_axis)])]
    ppermute x4, starting transfers between devices: 4.22 us -> 5.77 us  [hop(): lax.ppermute(up, 'frames', forward)]
    ppermute x4, starting transfers between devices: 3.98 us -> 2.49 us  [hop(): lax.ppermute(down, 'frames', backward)]
    ppermute x4, waiting for transfers between devices: 4.64 us -> 3.56 us  [hop(): lax.ppermute(up, 'frames', forward)]
  transfers between devices with their start and end apart: 25 -> 24, of which waited for: 13 -> 16; matrix products, arithmetic and copies ran while one was open for 0% -> 0% of each run, Pallas kernels for 4% -> 2%
where the time goes in v20:
time: 67.1 us; the launch traced here: 65.9 us
  starting transfers between devices  25.6 us (38%)
  waiting for transfers between devices  24.3 us (36%)
  Pallas kernels  12.1 us (18%)
  local copies, waits for them, and re-layouts  3.02 us (5%)
  between operations  0.82 us (1%)
    ppermute x14, waiting for transfers between devices, swap(): lax.ppermute(value, 'atoms', [(a, a ^ distance) for a in range(atom_axis)])  11.2 us
    ppermute x14, starting transfers between devices, swap(): lax.ppermute(value, 'atoms', [(a, a ^ distance) for a in range(atom_axis)])  10.3 us
    pallas_call x1, Pallas kernels, per_device(): pl.pallas_call(functools.partial(covariance_kernel, frame_axis, atom_axis...  8.53 us
    ppermute x4, waiting for transfers between devices, hop(): lax.ppermute(down, 'frames', backward)  7.31 us
    ppermute x2, starting transfers between devices, cross(): return [cut, lax.ppermute(cut, axes, pairs(0, 2))]  7.04 us
    ppermute x4, starting transfers between devices, hop(): lax.ppermute(up, 'frames', forward)  5.77 us
    ppermute x4, waiting for transfers between devices, hop(): lax.ppermute(up, 'frames', forward)  3.56 us
    unnamed x18, local copies, waits for them, and re-layouts  3.02 us
  transfers between devices with their start and end apart: 24, of which 16 were waited for; matrix products, arithmetic and copies ran while one was open for 0% of the time, Pallas kernels for 2%

profile of v20, /device:TPU:0, one launch (start us, length us, event | category | flops | bytes accessed | tf_op | source)
XLA Modules:
  0.0 65.9 jit_solution(12647679177303026161)
XLA Ops:
  0.6 1.7 %local_moments.1 = (f32[24,64]{1,0:T(8,128)S(1)}, f32[3,64,1024]{2,1,0:T(8,128)S(1)}, f32[3,1024]{1,0:T(4,128)S(1)}) custom-call(f32[3,64,1024]{2,1,0:T(8,128)} %bitcast.5, f32[3,1024]{1,0:T(4,128)} %ref_hbm.1), custom_call_target="tpu_custom_call" | custom-call | tf_op jit(solution)/shard_map/local_moments/pallas_call | solution.py:342
  2.3 2.4 %collective-permute-start.2 = (f32[24,64]{1,0:T(8,128)S(1)}, f32[24,64]{1,0:T(8,128)S(1)}, u32[]{:S(2)}, u32[]{:S(2)}) collective-permute-start(f32[24,64]{1,0:T(8,128)S(1)} %get-tuple-element.20.refs_0_), channel_id=1, source_target_pairs={{0,3},{1,2},{2,1},{3,0},{4,7},{5,6},{6,5},{7,4},{8,11},{9,10},{10,... | collective-permute-start | bytes 18440 | tf_op jit(solution)/shard_map/ppermute | solution.py:356
  4.7 0.6 collective-permute-start.1
  5.4 0.0 collective-permute-start
  5.4 0.7 %collective-permute-done.2.refs_3_ = f32[24,64]{1,0:T(8,128)S(1)} collective-permute-done((f32[24,64]{1,0:T(8,128)S(1)}, f32[24,64]{1,0:T(8,128)S(1)}, u32[]{:S(2)}, u32[]{:S(2)}) %collective-permute-start.2) | collective-permute-done | bytes 6176 | tf_op jit(solution)/shard_map/ppermute | solution.py:356
  6.1 2.3 %collective-permute-done.1.refs_2_ = f32[24,64]{1,0:T(8,128)S(1)} collective-permute-done((f32[24,64]{1,0:T(8,128)S(1)}, f32[24,64]{1,0:T(8,128)S(1)}, u32[]{:S(2)}, u32[]{:S(2)}) %collective-permute-start.1) | collective-permute-done | bytes 6176 | tf_op jit(solution)/shard_map/ppermute | solution.py:356
  8.4 0.0 collective-permute-done.refs_1_
  8.4 0.6 polar_align.1
  9.0 1.6 %collective-permute-start.3 = (bf16[2,3,256,128]{3,2,1,0:T(8,128)(2,1)S(1)}, bf16[2,3,256,128]{3,2,1,0:T(8,128)(2,1)S(1)}, u32[]{:S(2)}, u32[]{:S(2)}) collective-permute-start(bf16[2,3,256,128]{3,2,1,0:T(8,128)(2,1)S(1)} %get-tuple-element.23.refs_0_), channel_id=1, source_target_pairs={{0,8},{8,16},{16,24},{24,28},{28,20},{20,12},{12,4},{4,0},{1,9},{9... | collective-permute-start | bytes 1179656 | tf_op jit(solution)/shard_map/ppermute | solution.py:439
  10.7 0.4 collective-permute-start.4
  11.1 1.4 %copy-done = bf16[3,1024,256]{2,1,0:T(8,128)(2,1)S(1)} copy-done((bf16[3,1024,256]{2,1,0:T(8,128)(2,1)S(1)}, bf16[3,1024,256]{2,1,0:T(8,128)(2,1)}, u32[]{:S(2)}) %copy-start) | copy-done | bytes 1572888
  12.5 0.5 project.1
  13.0 0.0 copy-start.4
  13.0 0.6 copy-done.4
  13.6 0.0 collective-permute-start.5
  13.6 0.6 collective-permute-start.6
  14.3 1.2 %collective-permute-start.7 = (f32[64,64]{1,0:T(8,128)S(1)}, f32[64,64]{1,0:T(8,128)S(1)}, u32[]{:S(2)}, u32[]{:S(2)}) collective-permute-start(f32[64,64]{1,0:T(8,128)S(1)} %get-tuple-element.28), channel_id=1, source_target_pairs={{0,3},{1,2},{2,1},{3,0},{4,7},{5,6},{6,5},{7,4},{8,11},{9,10},{10,... | collective-permute-start | bytes 49160 | tf_op jit(solution)/shard_map/ppermute | solution.py:356
  15.5 0.0 collective-permute-done.5.refs_22_
  15.5 2.3 %collective-permute-done.6.refs_23_ = f32[64,64]{1,0:T(8,128)S(1)} collective-permute-done((f32[64,64]{1,0:T(8,128)S(1)}, f32[64,64]{1,0:T(8,128)S(1)}, u32[]{:S(2)}, u32[]{:S(2)}) %collective-permute-start.6) | collective-permute-done | bytes 16416 | tf_op jit(solution)/shard_map/ppermute | solution.py:356
  17.8 0.1 collective-permute-done.7.refs_24_
  17.9 1.7 %collective-permute-done.3.refs_1_ = bf16[2,3,256,128]{3,2,1,0:T(8,128)(2,1)S(1)} collective-permute-done((bf16[2,3,256,128]{3,2,1,0:T(8,128)(2,1)S(1)}, bf16[2,3,256,128]{3,2,1,0:T(8,128)(2,1)S(1)}, u32[]{:S(2)}, u32[]{:S(2)}) %collective-permute-start.3) | collective-permute-done | bytes 393248 | tf_op jit(solution)/shard_map/ppermute | solution.py:439
  19.6 1.3 %collective-permute-done.4.refs_2_ = bf16[2,3,256,128]{3,2,1,0:T(8,128)(2,1)S(1)} collective-permute-done((bf16[2,3,256,128]{3,2,1,0:T(8,128)(2,1)S(1)}, bf16[2,3,256,128]{3,2,1,0:T(8,128)(2,1)S(1)}, u32[]{:S(2)}, u32[]{:S(2)}) %collective-permute-start.4) | collective-permute-done | bytes 393248 | tf_op jit(solution)/shard_map/ppermute | solution.py:439
  20.9 0.4 collective-permute-start.9
  21.4 1.6 %collective-permute-start.8 = (bf16[2,3,256,128]{3,2,1,0:T(8,128)(2,1)S(1)}, bf16[2,3,256,128]{3,2,1,0:T(8,128)(2,1)S(1)}, u32[]{:S(2)}, u32[]{:S(2)}) collective-permute-start(bf16[2,3,256,128]{3,2,1,0:T(8,128)(2,1)S(1)} %collective-permute-done.3.refs_1_), channel_id=1, source_target_pairs={{0,8},{8,16},{16,24},{24,28},{28,20},{20,12},{12,4},{4,0},{1,9},{9... | collective-permute-start | bytes 1179656 | tf_op jit(solution)/shard_map/ppermute | solution.py:439
  23.0 0.2 cut_columns.4.refs_0_
  23.2 2.6 %collective-permute-start.12 = (bf16[3,3,64,512]{3,2,1,0:T(8,128)(2,1)S(1)}, bf16[3,3,64,512]{3,2,1,0:T(8,128)(2,1)S(1)}, u32[]{:S(2)}, u32[]{:S(2)}) collective-permute-start(bf16[3,3,64,512]{3,2,1,0:T(8,128)(2,1)S(1)} %cut_columns.4.refs_0_), channel_id=1, source_target_pairs={{0,2},{4,6},{9,11},{13,15},{18,16},{22,20},{27,25},{31,29}} | collective-permute-start | bytes 1769480 | tf_op jit(solution)/shard_map/ppermute | solution.py:418
  25.9 0.0 copy-done.2
  25.9 4.4 %collective-permute-done.9.refs_1_.refs_4_ = bf16[2,3,256,128]{3,2,1,0:T(8,128)(2,1)S(1)} collective-permute-done((bf16[2,3,256,128]{3,2,1,0:T(8,128)(2,1)S(1)}, bf16[2,3,256,128]{3,2,1,0:T(8,128)(2,1)S(1)}, u32[]{:S(2)}, u32[]{:S(2)}) %collective-permute-start.9) | collective-permute-done | bytes 393248 | tf_op jit(solution)/shard_map/ppermute | solution.py:439
  30.3 0.7 %collective-permute-start.11 = (bf16[2,3,256,128]{3,2,1,0:T(8,128)(2,1)S(1)}, bf16[2,3,256,128]{3,2,1,0:T(8,128)(2,1)S(1)}, u32[]{:S(2)}, u32[]{:S(2)}) collective-permute-start(bf16[2,3,256,128]{3,2,1,0:T(8,128)(2,1)S(1)} %collective-permute-done.9.refs_1_.refs_4_), channel_id=1, source_target_pairs={{8,0},{16,8},{24,16},{28,24},{20,28},{12,20},{4,12},{0,4},{9,1},{1... | collective-permute-start | bytes 1179656 | tf_op jit(solution)/shard_map/ppermute | solution.py:439
  31.0 0.0 copy-done.6
  31.0 0.0 copy-done.7
  31.0 0.0 copy-done.8
  31.0 0.0 collective-permute-done.8.refs_0_.refs_3_
  31.0 1.4 %collective-permute-start.10 = (bf16[2,3,256,128]{3,2,1,0:T(8,128)(2,1)S(1)}, bf16[2,3,256,128]{3,2,1,0:T(8,128)(2,1)S(1)}, u32[]{:S(2)}, u32[]{:S(2)}) collective-permute-start(bf16[2,3,256,128]{3,2,1,0:T(8,128)(2,1)S(1)} %collective-permute-done.8.refs_0_.refs_3_), channel_id=1, source_target_pairs={{0,8},{8,16},{16,24},{24,28},{28,20},{20,12},{12,4},{4,0},{1,9},{9... | collective-permute-start | bytes 1179656 | tf_op jit(solution)/shard_map/ppermute | solution.py:439
  32.4 0.8 %collective-permute-done.12.refs_1_ = bf16[3,3,64,512]{3,2,1,0:T(8,128)(2,1)S(1)} collective-permute-done((bf16[3,3,64,512]{3,2,1,0:T(8,128)(2,1)S(1)}, bf16[3,3,64,512]{3,2,1,0:T(8,128)(2,1)S(1)}, u32[]{:S(2)}, u32[]{:S(2)}) %collective-permute-start.12) | collective-permute-done | bytes 589856 | tf_op jit(solution)/shard_map/ppermute | solution.py:418
  33.3 0.1 collective-permute-start.15
  33.4 0.2 cut_columns.6.refs_0_
  33.5 4.4 %collective-permute-start.16 = (bf16[2,3,64,512]{3,2,1,0:T(8,128)(2,1)S(1)}, bf16[2,3,64,512]{3,2,1,0:T(8,128)(2,1)S(1)}, u32[]{:S(2)}, u32[]{:S(2)}) collective-permute-start(bf16[2,3,64,512]{3,2,1,0:T(8,128)(2,1)S(1)} %cut_columns.6.refs_0_), channel_id=1, source_target_pairs={{0,2},{4,6},{9,11},{13,15},{18,16},{22,20},{27,25},{31,29}} | collective-permute-start | bytes 1179656 | tf_op jit(solution)/shard_map/ppermute | solution.py:418
  38.0 0.8 %collective-permute-done.11.down_ref.refs_6_ = bf16[2,3,256,128]{3,2,1,0:T(8,128)(2,1)S(1)} collective-permute-done((bf16[2,3,256,128]{3,2,1,0:T(8,128)(2,1)S(1)}, bf16[2,3,256,128]{3,2,1,0:T(8,128)(2,1)S(1)}, u32[]{:S(2)}, u32[]{:S(2)}) %collective-permute-start.11) | collective-permute-done | bytes 393248 | tf_op jit(solution)/shard_map/ppermute | solution.py:439
  38.7 0.7 %collective-permute-done.10.up_ref.refs_5_ = bf16[2,3,256,128]{3,2,1,0:T(8,128)(2,1)S(1)} collective-permute-done((bf16[2,3,256,128]{3,2,1,0:T(8,128)(2,1)S(1)}, bf16[2,3,256,128]{3,2,1,0:T(8,128)(2,1)S(1)}, u32[]{:S(2)}, u32[]{:S(2)}) %collective-permute-start.10) | collective-permute-done | bytes 393248 | tf_op jit(solution)/shard_map/ppermute | solution.py:439
  39.4 0.2 cut_columns.5
  39.6 0.1 collective-permute-start.18
  39.7 1.2 %collective-permute-start.13 = (bf16[3,256,128]{2,1,0:T(8,128)(2,1)S(1)}, bf16[3,256,128]{2,1,0:T(8,128)(2,1)S(1)}, u32[]{:S(2)}, u32[]{:S(2)}) collective-permute-start(bf16[3,256,128]{2,1,0:T(8,128)(2,1)S(1)} %get-tuple-element.31), channel_id=1, source_target_pairs={{0,8},{8,16},{16,24},{24,28},{28,20},{20,12},{12,4},{4,0},{1,9},{9... | collective-permute-start | bytes 589832 | tf_op jit(solution)/shard_map/ppermute | solution.py:439
  40.9 0.9 %collective-permute-start.14 = (bf16[3,256,128]{2,1,0:T(8,128)(2,1)S(1)}, bf16[3,256,128]{2,1,0:T(8,128)(2,1)S(1)}, u32[]{:S(2)}, u32[]{:S(2)}) collective-permute-start(bf16[3,256,128]{2,1,0:T(8,128)(2,1)S(1)} %get-tuple-element.32), channel_id=1, source_target_pairs={{8,0},{16,8},{24,16},{28,24},{20,28},{12,20},{4,12},{0,4},{9,1},{1... | collective-permute-start | bytes 589832 | tf_op jit(solution)/shard_map/ppermute | solution.py:439
  41.8 1.4 %collective-permute-done.16.refs_1_ = bf16[2,3,64,512]{3,2,1,0:T(8,128)(2,1)S(1)} collective-permute-done((bf16[2,3,64,512]{3,2,1,0:T(8,128)(2,1)S(1)}, bf16[2,3,64,512]{3,2,1,0:T(8,128)(2,1)S(1)}, u32[]{:S(2)}, u32[]{:S(2)}) %collective-permute-start.16) | collective-permute-done | bytes 393248 | tf_op jit(solution)/shard_map/ppermute | solution.py:418
  43.2 0.0 collective-permute-done.18.beside_ref.refs_14_
  43.3 2.5 %collective-permute-start.19 = (bf16[2,3,64,256]{3,2,1,0:T(8,128)(2,1)S(1)}, bf16[2,3,64,256]{3,2,1,0:T(8,128)(2,1)S(1)}, u32[]{:S(2)}, u32[]{:S(2)}) collective-permute-start(bf16[2,3,64,256]{3,2,1,0:T(8,128)(2,1)S(1)} %pick_half.2), channel_id=1, source_target_pairs={{0,2},{1,3},{2,0},{3,1},{4,6},{5,7},{6,4},{7,5},{8,10},{9,11},{10,... | collective-permute-start | bytes 589832 | tf_op jit(solution)/shard_map/ppermute | solution.py:356
  45.8 0.0 collective-permute-done.15.refs_10_
  45.8 1.2 %collective-permute-done.13.up_half.refs_7_ = bf16[3,256,128]{2,1,0:T(8,128)(2,1)S(1)} collective-permute-done((bf16[3,256,128]{2,1,0:T(8,128)(2,1)S(1)}, bf16[3,256,128]{2,1,0:T(8,128)(2,1)S(1)}, u32[]{:S(2)}, u32[]{:S(2)}) %collective-permute-start.13) | collective-permute-done | bytes 196640 | tf_op jit(solution)/shard_map/ppermute | solution.py:439
  47.0 0.8 %collective-permute-done.14.down_half.refs_8_ = bf16[3,256,128]{2,1,0:T(8,128)(2,1)S(1)} collective-permute-done((bf16[3,256,128]{2,1,0:T(8,128)(2,1)S(1)}, bf16[3,256,128]{2,1,0:T(8,128)(2,1)S(1)}, u32[]{:S(2)}, u32[]{:S(2)}) %collective-permute-start.14) | collective-permute-done | bytes 196640 | tf_op jit(solution)/shard_map/ppermute | solution.py:439
  47.8 0.1 cut_columns.7.own_ref.refs_17_
  48.0 0.1 collective-permute-start.21
  48.1 0.5 collective-permute-start.17
  48.6 0.9 %collective-permute-done.19.refs_15_ = bf16[2,3,64,256]{3,2,1,0:T(8,128)(2,1)S(1)} collective-permute-done((bf16[2,3,64,256]{3,2,1,0:T(8,128)(2,1)S(1)}, bf16[2,3,64,256]{3,2,1,0:T(8,128)(2,1)S(1)}, u32[]{:S(2)}, u32[]{:S(2)}) %collective-permute-start.19) | collective-permute-done | bytes 196640 | tf_op jit(solution)/shard_map/ppermute | solution.py:356
  49.5 0.0 collective-permute-start.20
  49.5 0.0 collective-permute-done.21.beside_ref.refs_18_
  49.5 2.1 %collective-permute-start.22 = (bf16[1,3,64,256]{3,2,1,0:T(8,128)(2,1)S(1)}, bf16[1,3,64,256]{3,2,1,0:T(8,128)(2,1)S(1)}, u32[]{:S(2)}, u32[]{:S(2)}) collective-permute-start(bf16[1,3,64,256]{3,2,1,0:T(8,128)(2,1)S(1)} %pick_half.3), channel_id=1, source_target_pairs={{0,2},{1,3},{2,0},{3,1},{4,6},{5,7},{6,4},{7,5},{8,10},{9,11},{10,... | collective-permute-start | bytes 294920 | tf_op jit(solution)/shard_map/ppermute | solution.py:356
  51.6 3.5 %collective-permute-done.22.refs_19_ = bf16[1,3,64,256]{3,2,1,0:T(8,128)(2,1)S(1)} collective-permute-done((bf16[1,3,64,256]{3,2,1,0:T(8,128)(2,1)S(1)}, bf16[1,3,64,256]{3,2,1,0:T(8,128)(2,1)S(1)}, u32[]{:S(2)}, u32[]{:S(2)}) %collective-permute-start.22) | collective-permute-done | bytes 98336 | tf_op jit(solution)/shard_map/ppermute | solution.py:356
  55.0 0.0 collective-permute-start.23
  55.0 0.0 collective-permute-done.17.refs_12_
  55.1 0.0 collective-permute-done.20.refs_16_
  55.1 1.3 %collective-permute-done.23.refs_20_ = bf16[1,3,64,256]{3,2,1,0:T(8,128)(2,1)S(1)} collective-permute-done((bf16[1,3,64,256]{3,2,1,0:T(8,128)(2,1)S(1)}, bf16[1,3,64,256]{3,2,1,0:T(8,128)(2,1)S(1)}, u32[]{:S(2)}, u32[]{:S(2)}) %collective-permute-start.23) | collective-permute-done | bytes 98336 | tf_op jit(solution)/shard_map/ppermute | solution.py:356
  56.4 1.0 %copy-done.3 = bf16[2,3,256,128]{3,2,1,0:T(8,128)(2,1)S(1)} copy-done((bf16[2,3,256,128]{3,2,1,0:T(8,128)(2,1)S(1)}, bf16[2,3,256,128]{3,2,1,0:T(8,128)(2,1)}, u32[]{:S(2)}) %copy-start.3) | copy-done | bytes 393240
  57.4 8.5 %covariance_tile.1 = (f32[3,3,1024,512]{3,2,1,0:T(8,128)}, f32[64,64]{1,0:T(8,128)}) custom-call(s32[1]{0:T(128)} %bitcast.role_ref, bf16[2,3,256,128]{3,2,1,0:T(8,128)(2,1)S(1)} %get-tuple-element.23.refs_0_, bf16[2,3,256,128]{3,2,1,0:T(8,128)(2,1)S(1)} %collective-permute-done.3.refs_1_, bf16[2,3,256,128]{3,2,1,0:T(8,128)(2,1)S(1)} %copy-done.3, ...), custom_call_target="tpu_custom_call" | custom-call | flops 4831838208 | bytes 25165824 | tf_op jit(solution)/shard_map/covariance_tile/pallas_call | solution.py:465
  (14 shorter events, 0.1 us)
Async XLA Ops:
  2.3 3.8 %collective-permute-start.2 = (f32[24,64]{1,0:T(8,128)S(1)}, f32[24,64]{1,0:T(8,128)S(1)}, u32[]{:S(2)}, u32[]{:S(2)}) collective-permute-start(f32[24,64]{1,0:T(8,128)S(1)} %get-tuple-element.20.refs_0_), channel_id=1, source_target_pairs={{0,3},{1,2},{2,1},{3,0},{4,7},{5,6},{6,5},{7,4},{8,11},{9,10},{10,... | collective-permute-start | bytes 18440 | tf_op jit(solution)/shard_map/ppermute | solution.py:356
  4.7 3.7 %collective-permute-start.1 = (f32[24,64]{1,0:T(8,128)S(1)}, f32[24,64]{1,0:T(8,128)S(1)}, u32[]{:S(2)}, u32[]{:S(2)}) collective-permute-start(f32[24,64]{1,0:T(8,128)S(1)} %get-tuple-element.20.refs_0_), channel_id=1, source_target_pairs={{0,2},{1,3},{2,0},{3,1},{4,6},{5,7},{6,4},{7,5},{8,10},{9,11},{10,... | collective-permute-start | bytes 18440 | tf_op jit(solution)/shard_map/ppermute | solution.py:356
  5.4 3.1 %collective-permute-start = (f32[24,64]{1,0:T(8,128)S(1)}, f32[24,64]{1,0:T(8,128)S(1)}, u32[]{:S(2)}, u32[]{:S(2)}) collective-permute-start(f32[24,64]{1,0:T(8,128)S(1)} %get-tuple-element.20.refs_0_), channel_id=1, source_target_pairs={{0,1},{1,0},{2,3},{3,2},{4,5},{5,4},{6,7},{7,6},{8,9},{9,8},{10,11... | collective-permute-start | bytes 18440 | tf_op jit(solution)/shard_map/ppermute | solution.py:356
  9.0 10.6 %collective-permute-start.3 = (bf16[2,3,256,128]{3,2,1,0:T(8,128)(2,1)S(1)}, bf16[2,3,256,128]{3,2,1,0:T(8,128)(2,1)S(1)}, u32[]{:S(2)}, u32[]{:S(2)}) collective-permute-start(bf16[2,3,256,128]{3,2,1,0:T(8,128)(2,1)S(1)} %get-tuple-element.23.refs_0_), channel_id=1, source_target_pairs={{0,8},{8,16},{16,24},{24,28},{28,20},{20,12},{12,4},{4,0},{1,9},{9... | collective-permute-start | bytes 1179656 | tf_op jit(solution)/shard_map/ppermute | solution.py:439
  10.7 10.3 %collective-permute-start.4 = (bf16[2,3,256,128]{3,2,1,0:T(8,128)(2,1)S(1)}, bf16[2,3,256,128]{3,2,1,0:T(8,128)(2,1)S(1)}, u32[]{:S(2)}, u32[]{:S(2)}) collective-permute-start(bf16[2,3,256,128]{3,2,1,0:T(8,128)(2,1)S(1)} %get-tuple-element.23.refs_0_), channel_id=1, source_target_pairs={{8,0},{16,8},{24,16},{28,24},{20,28},{12,20},{4,12},{0,4},{9,1},{1... | collective-permute-start | bytes 1179656 | tf_op jit(solution)/shard_map/ppermute | solution.py:439
  11.1 1.4 %copy-start = (bf16[3,1024,256]{2,1,0:T(8,128)(2,1)S(1)}, bf16[3,1024,256]{2,1,0:T(8,128)(2,1)}, u32[]{:S(2)}) copy-start(bf16[3,1024,256]{2,1,0:T(8,128)(2,1)} %eig_ref.1) | copy-start | bytes 4718596
  13.0 0.6 copy-start.4
  13.6 1.9 %collective-permute-start.5 = (f32[64,64]{1,0:T(8,128)S(1)}, f32[64,64]{1,0:T(8,128)S(1)}, u32[]{:S(2)}, u32[]{:S(2)}) collective-permute-start(f32[64,64]{1,0:T(8,128)S(1)} %get-tuple-element.26), channel_id=1, source_target_pairs={{0,1},{1,0},{2,3},{3,2},{4,5},{5,4},{6,7},{7,6},{8,9},{9,8},{10,11... | collective-permute-start | bytes 49160 | tf_op jit(solution)/shard_map/ppermute | solution.py:356
  13.6 4.2 %collective-permute-start.6 = (f32[64,64]{1,0:T(8,128)S(1)}, f32[64,64]{1,0:T(8,128)S(1)}, u32[]{:S(2)}, u32[]{:S(2)}) collective-permute-start(f32[64,64]{1,0:T(8,128)S(1)} %get-tuple-element.27), channel_id=1, source_target_pairs={{0,2},{1,3},{2,0},{3,1},{4,6},{5,7},{6,4},{7,5},{8,10},{9,11},{10,... | collective-permute-start | bytes 49160 | tf_op jit(solution)/shard_map/ppermute | solution.py:356
  14.3 3.7 %collective-permute-start.7 = (f32[64,64]{1,0:T(8,128)S(1)}, f32[64,64]{1,0:T(8,128)S(1)}, u32[]{:S(2)}, u32[]{:S(2)}) collective-permute-start(f32[64,64]{1,0:T(8,128)S(1)} %get-tuple-element.28), channel_id=1, source_target_pairs={{0,3},{1,2},{2,1},{3,0},{4,7},{5,6},{6,5},{7,4},{8,11},{9,10},{10,... | collective-permute-start | bytes 49160 | tf_op jit(solution)/shard_map/ppermute | solution.py:356
  15.5 15.5 %copy-start.6 = (f32[64,64]{1,0:T(8,128)}, f32[64,64]{1,0:T(8,128)S(1)}, u32[]{:S(2)}) copy-start(f32[64,64]{1,0:T(8,128)S(1)} %collective-permute-done.5.refs_22_) | copy-start | bytes 49156
  17.8 13.2 %copy-start.7 = (f32[64,64]{1,0:T(8,128)}, f32[64,64]{1,0:T(8,128)S(1)}, u32[]{:S(2)}) copy-start(f32[64,64]{1,0:T(8,128)S(1)} %collective-permute-done.6.refs_23_) | copy-start | bytes 49156
  17.9 13.0 %copy-start.8 = (f32[64,64]{1,0:T(8,128)}, f32[64,64]{1,0:T(8,128)S(1)}, u32[]{:S(2)}) copy-start(f32[64,64]{1,0:T(8,128)S(1)} %collective-permute-done.7.refs_24_) | copy-start | bytes 49156
  20.9 4.9 %copy-start.2 = (bf16[2,3,256,128]{3,2,1,0:T(8,128)(2,1)}, bf16[2,3,256,128]{3,2,1,0:T(8,128)(2,1)S(1)}, u32[]{:S(2)}) copy-start(bf16[2,3,256,128]{3,2,1,0:T(8,128)(2,1)S(1)} %collective-permute-done.4.refs_2_) | copy-start | bytes 1179652
  20.9 9.3 %collective-permute-start.9 = (bf16[2,3,256,128]{3,2,1,0:T(8,128)(2,1)S(1)}, bf16[2,3,256,128]{3,2,1,0:T(8,128)(2,1)S(1)}, u32[]{:S(2)}, u32[]{:S(2)}) collective-permute-start(bf16[2,3,256,128]{3,2,1,0:T(8,128)(2,1)S(1)} %collective-permute-done.4.refs_2_), channel_id=1, source_target_pairs={{8,0},{16,8},{24,16},{28,24},{20,28},{12,20},{4,12},{0,4},{9,1},{1... | collective-permute-start | bytes 1179656 | tf_op jit(solution)/shard_map/ppermute | solution.py:439
  21.4 9.6 %collective-permute-start.8 = (bf16[2,3,256,128]{3,2,1,0:T(8,128)(2,1)S(1)}, bf16[2,3,256,128]{3,2,1,0:T(8,128)(2,1)S(1)}, u32[]{:S(2)}, u32[]{:S(2)}) collective-permute-start(bf16[2,3,256,128]{3,2,1,0:T(8,128)(2,1)S(1)} %collective-permute-done.3.refs_1_), channel_id=1, source_target_pairs={{0,8},{8,16},{16,24},{24,28},{28,20},{20,12},{12,4},{4,0},{1,9},{9... | collective-permute-start | bytes 1179656 | tf_op jit(solution)/shard_map/ppermute | solution.py:439
  23.2 10.0 %collective-permute-start.12 = (bf16[3,3,64,512]{3,2,1,0:T(8,128)(2,1)S(1)}, bf16[3,3,64,512]{3,2,1,0:T(8,128)(2,1)S(1)}, u32[]{:S(2)}, u32[]{:S(2)}) collective-permute-start(bf16[3,3,64,512]{3,2,1,0:T(8,128)(2,1)S(1)} %cut_columns.4.refs_0_), channel_id=1, source_target_pairs={{0,2},{4,6},{9,11},{13,15},{18,16},{22,20},{27,25},{31,29}} | collective-permute-start | bytes 1769480 | tf_op jit(solution)/shard_map/ppermute | solution.py:418
  30.3 8.4 %collective-permute-start.11 = (bf16[2,3,256,128]{3,2,1,0:T(8,128)(2,1)S(1)}, bf16[2,3,256,128]{3,2,1,0:T(8,128)(2,1)S(1)}, u32[]{:S(2)}, u32[]{:S(2)}) collective-permute-start(bf16[2,3,256,128]{3,2,1,0:T(8,128)(2,1)S(1)} %collective-permute-done.9.refs_1_.refs_4_), channel_id=1, source_target_pairs={{8,0},{16,8},{24,16},{28,24},{20,28},{12,20},{4,12},{0,4},{9,1},{1... | collective-permute-start | bytes 1179656 | tf_op jit(solution)/shard_map/ppermute | solution.py:439
  31.0 8.4 %collective-permute-start.10 = (bf16[2,3,256,128]{3,2,1,0:T(8,128)(2,1)S(1)}, bf16[2,3,256,128]{3,2,1,0:T(8,128)(2,1)S(1)}, u32[]{:S(2)}, u32[]{:S(2)}) collective-permute-start(bf16[2,3,256,128]{3,2,1,0:T(8,128)(2,1)S(1)} %collective-permute-done.8.refs_0_.refs_3_), channel_id=1, source_target_pairs={{0,8},{8,16},{16,24},{24,28},{28,20},{20,12},{12,4},{4,0},{1,9},{9... | collective-permute-start | bytes 1179656 | tf_op jit(solution)/shard_map/ppermute | solution.py:439
  33.3 23.1 %copy-start.1 = (bf16[3,3,64,512]{3,2,1,0:T(8,128)(2,1)}, bf16[3,3,64,512]{3,2,1,0:T(8,128)(2,1)S(1)}, u32[]{:S(2)}) copy-start(bf16[3,3,64,512]{3,2,1,0:T(8,128)(2,1)S(1)} %pass_on.2.refs_9_) | copy-start | bytes 1769476
  33.3 12.6 %collective-permute-start.15 = (bf16[3,3,64,512]{3,2,1,0:T(8,128)(2,1)S(1)}, bf16[3,3,64,512]{3,2,1,0:T(8,128)(2,1)S(1)}, u32[]{:S(2)}, u32[]{:S(2)}) collective-permute-start(bf16[3,3,64,512]{3,2,1,0:T(8,128)(2,1)S(1)} %pass_on.2.refs_9_), channel_id=1, source_target_pairs={{0,1},{1,0},{2,3},{3,2},{4,5},{5,4},{6,7},{7,6},{8,9},{9,8},{10,11... | collective-permute-start | bytes 1769480 | tf_op jit(solution)/shard_map/ppermute | solution.py:356
  33.5 9.7 %collective-permute-start.16 = (bf16[2,3,64,512]{3,2,1,0:T(8,128)(2,1)S(1)}, bf16[2,3,64,512]{3,2,1,0:T(8,128)(2,1)S(1)}, u32[]{:S(2)}, u32[]{:S(2)}) collective-permute-start(bf16[2,3,64,512]{3,2,1,0:T(8,128)(2,1)S(1)} %cut_columns.6.refs_0_), channel_id=1, source_target_pairs={{0,2},{4,6},{9,11},{13,15},{18,16},{22,20},{27,25},{31,29}} | collective-permute-start | bytes 1179656 | tf_op jit(solution)/shard_map/ppermute | solution.py:418
  39.6 3.6 %collective-permute-start.18 = (bf16[2,3,64,512]{3,2,1,0:T(8,128)(2,1)S(1)}, bf16[2,3,64,512]{3,2,1,0:T(8,128)(2,1)S(1)}, u32[]{:S(2)}, u32[]{:S(2)}) collective-permute-start(bf16[2,3,64,512]{3,2,1,0:T(8,128)(2,1)S(1)} %get-tuple-element.33.own_ref.refs_13_), channel_id=1, source_target_pairs={{0,1},{1,0},{2,3},{3,2},{4,5},{5,4},{6,7},{7,6},{8,9},{9,8},{10,11... | collective-permute-start | bytes 1179656 | tf_op jit(solution)/shard_map/ppermute | solution.py:356
  39.7 7.3 %collective-permute-start.13 = (bf16[3,256,128]{2,1,0:T(8,128)(2,1)S(1)}, bf16[3,256,128]{2,1,0:T(8,128)(2,1)S(1)}, u32[]{:S(2)}, u32[]{:S(2)}) collective-permute-start(bf16[3,256,128]{2,1,0:T(8,128)(2,1)S(1)} %get-tuple-element.31), channel_id=1, source_target_pairs={{0,8},{8,16},{16,24},{24,28},{28,20},{20,12},{12,4},{4,0},{1,9},{9... | collective-permute-start | bytes 589832 | tf_op jit(solution)/shard_map/ppermute | solution.py:439
  40.9 7.0 %collective-permute-start.14 = (bf16[3,256,128]{2,1,0:T(8,128)(2,1)S(1)}, bf16[3,256,128]{2,1,0:T(8,128)(2,1)S(1)}, u32[]{:S(2)}, u32[]{:S(2)}) collective-permute-start(bf16[3,256,128]{2,1,0:T(8,128)(2,1)S(1)} %get-tuple-element.32), channel_id=1, source_target_pairs={{8,0},{16,8},{24,16},{28,24},{20,28},{12,20},{4,12},{0,4},{9,1},{1... | collective-permute-start | bytes 589832 | tf_op jit(solution)/shard_map/ppermute | solution.py:439
  43.3 6.2 %collective-permute-start.19 = (bf16[2,3,64,256]{3,2,1,0:T(8,128)(2,1)S(1)}, bf16[2,3,64,256]{3,2,1,0:T(8,128)(2,1)S(1)}, u32[]{:S(2)}, u32[]{:S(2)}) collective-permute-start(bf16[2,3,64,256]{3,2,1,0:T(8,128)(2,1)S(1)} %pick_half.2), channel_id=1, source_target_pairs={{0,2},{1,3},{2,0},{3,1},{4,6},{5,7},{6,4},{7,5},{8,10},{9,11},{10,... | collective-permute-start | bytes 589832 | tf_op jit(solution)/shard_map/ppermute | solution.py:356
  45.8 10.5 %copy-start.5 = (bf16[3,3,64,512]{3,2,1,0:T(8,128)(2,1)}, bf16[3,3,64,512]{3,2,1,0:T(8,128)(2,1)S(1)}, u32[]{:S(2)}) copy-start(bf16[3,3,64,512]{3,2,1,0:T(8,128)(2,1)S(1)} %collective-permute-done.15.refs_10_) | copy-start | bytes 1769476
  48.0 1.5 %collective-permute-start.21 = (bf16[1,3,64,512]{3,2,1,0:T(8,128)(2,1)S(1)}, bf16[1,3,64,512]{3,2,1,0:T(8,128)(2,1)S(1)}, u32[]{:S(2)}, u32[]{:S(2)}) collective-permute-start(bf16[1,3,64,512]{3,2,1,0:T(8,128)(2,1)S(1)} %cut_columns.7.own_ref.refs_17_), channel_id=1, source_target_pairs={{0,1},{1,0},{2,3},{3,2},{4,5},{5,4},{6,7},{7,6},{8,9},{9,8},{10,11... | collective-permute-start | bytes 589832 | tf_op jit(solution)/shard_map/ppermute | solution.py:356
  48.1 7.0 %collective-permute-start.17 = (bf16[2,3,64,512]{3,2,1,0:T(8,128)(2,1)S(1)}, bf16[2,3,64,512]{3,2,1,0:T(8,128)(2,1)S(1)}, u32[]{:S(2)}, u32[]{:S(2)}) collective-permute-start(bf16[2,3,64,512]{3,2,1,0:T(8,128)(2,1)S(1)} %pass_on.3.refs_11_), channel_id=1, source_target_pairs={{0,1},{1,0},{2,3},{3,2},{4,5},{5,4},{6,7},{7,6},{8,9},{9,8},{10,11... | collective-permute-start | bytes 1179656 | tf_op jit(solution)/shard_map/ppermute | solution.py:356
  49.5 5.6 %collective-permute-start.20 = (bf16[2,3,64,256]{3,2,1,0:T(8,128)(2,1)S(1)}, bf16[2,3,64,256]{3,2,1,0:T(8,128)(2,1)S(1)}, u32[]{:S(2)}, u32[]{:S(2)}) collective-permute-start(bf16[2,3,64,256]{3,2,1,0:T(8,128)(2,1)S(1)} %collective-permute-done.19.refs_15_), channel_id=1, source_target_pairs={{0,1},{1,0},{2,3},{3,2},{4,5},{5,4},{6,7},{7,6},{8,9},{9,8},{10,11... | collective-permute-start | bytes 589832 | tf_op jit(solution)/shard_map/ppermute | solution.py:356
  49.5 5.5 %collective-permute-start.22 = (bf16[1,3,64,256]{3,2,1,0:T(8,128)(2,1)S(1)}, bf16[1,3,64,256]{3,2,1,0:T(8,128)(2,1)S(1)}, u32[]{:S(2)}, u32[]{:S(2)}) collective-permute-start(bf16[1,3,64,256]{3,2,1,0:T(8,128)(2,1)S(1)} %pick_half.3), channel_id=1, source_target_pairs={{0,2},{1,3},{2,0},{3,1},{4,6},{5,7},{6,4},{7,5},{8,10},{9,11},{10,... | collective-permute-start | bytes 294920 | tf_op jit(solution)/shard_map/ppermute | solution.py:356
  55.0 1.3 %collective-permute-start.23 = (bf16[1,3,64,256]{3,2,1,0:T(8,128)(2,1)S(1)}, bf16[1,3,64,256]{3,2,1,0:T(8,128)(2,1)S(1)}, u32[]{:S(2)}, u32[]{:S(2)}) collective-permute-start(bf16[1,3,64,256]{3,2,1,0:T(8,128)(2,1)S(1)} %collective-permute-done.22.refs_19_), channel_id=1, source_target_pairs={{0,1},{1,0},{2,3},{3,2},{4,5},{5,4},{6,7},{7,6},{8,9},{9,8},{10,11... | collective-permute-start | bytes 294920 | tf_op jit(solution)/shard_map/ppermute | solution.py:356
  56.4 1.0 %copy-start.3 = (bf16[2,3,256,128]{3,2,1,0:T(8,128)(2,1)S(1)}, bf16[2,3,256,128]{3,2,1,0:T(8,128)(2,1)}, u32[]{:S(2)}) copy-start(bf16[2,3,256,128]{3,2,1,0:T(8,128)(2,1)} %copy-done.2) | copy-start | bytes 1179652

commit v21 on v20

--- a/solution.py
+++ b/solution.py
@@ -444,23 +444,23 @@
     in_hbm = pass_on(cross(cut_one), role)
     cut_two = kernel(cut_kernel, columns(2), half, list(two), "cut_columns")
     three = hop(*two)
-    in_vmem = pass_on(cross(cut_two), role)
+    two_halves = halves_across(cut_two)[0]
+    in_hbm += two_halves
     half_shard = pltpu.VMEM(piece, jnp.bfloat16)
     cut_three, *halves = kernel(
         cut_last_kernel,
         (columns(2), half_shard, half_shard),
-        after(half, in_hbm[0]),
+        after(half, in_hbm[0], two_halves[2]),
         list(three),
         "cut_columns",
     )
     far = hop(*halves)
-    three_halves, picked = halves_across(cut_three)
-    in_vmem += three_halves
+    in_vmem, picked = halves_across(cut_three)
     cut_four = kernel(
-        cut_far_kernel, columns(1), after(half, in_hbm[1], in_vmem[0], picked), list(far), "cut_columns"
-    )
-    in_vmem += halves_across(cut_four, three_halves[2])[0]
-    groups = ((3, True, 2), (2, False, 2), (2, False, 4), (1, False, 4))
+        cut_far_kernel, columns(1), after(half, in_hbm[1], picked), list(far), "cut_columns"
+    )
+    in_vmem += halves_across(cut_four, in_vmem[2], two_halves[3])[0]
+    groups = ((3, True, 2), (2, True, 4), (2, False, 4), (1, False, 4))
     rows = [own, *one, *two, *three, *far]
     covariance, projections = pl.pallas_call(
         functools.partial(

time: 67.1 us -> 71.6 us (1.067); the launches traced: 65.9 us -> 71.3 us
  waiting for transfers between devices: 24.3 us -> 33.3 us
  starting transfers between devices: 25.6 us -> 19.8 us
  local copies, waits for them, and re-layouts: 3.02 us -> 5.04 us
    ppermute x14 -> x16, waiting for transfers between devices: 11.2 us -> 17.4 us  [swap(): lax.ppermute(value, 'atoms', [(a, a ^ distance) for a in range(atom_axis)])]
    ppermute x2 -> x1, starting transfers between devices: 7.04 us -> 2.63 us  [cross(): return [cut, lax.ppermute(cut, axes, pairs(0, 2))]]
    ppermute x4, waiting for transfers between devices: 3.56 us -> 7.36 us  [hop(): lax.ppermute(up, 'frames', forward)]
    ppermute x2 -> x1, waiting for transfers between devices: 2.26 us -> 0.01 us  [cross(): return [cut, lax.ppermute(cut, axes, pairs(0, 2))]]
    unnamed x18 -> x34, local copies, waits for them, and re-layouts: 3.02 us -> 5.04 us
    ppermute x4, starting transfers between devices: 2.49 us -> 4.09 us  [hop(): lax.ppermute(down, 'frames', backward)]
    ppermute x4, starting transfers between devices: 5.77 us -> 4.17 us  [hop(): lax.ppermute(up, 'frames', forward)]
    ppermute x14 -> x16, starting transfers between devices: 10.3 us -> 8.92 us  [swap(): lax.ppermute(value, 'atoms', [(a, a ^ distance) for a in range(atom_axis)])]
  transfers between devices with their start and end apart: 24 -> 25, of which waited for: 16 -> 16; matrix products, arithmetic and copies ran while one was open for 0% -> 0% of each run, Pallas kernels for 2% -> 2%
where the time goes in v21:
time: 71.6 us; the launch traced here: 71.3 us
  waiting for transfers between devices  33.3 us (47%)
  starting transfers between devices  19.8 us (28%)
  Pallas kernels  12.3 us (17%)
  local copies, waits for them, and re-layouts  5.04 us (7%)
  between operations  0.89 us (1%)
    ppermute x16, waiting for transfers between devices, swap(): lax.ppermute(value, 'atoms', [(a, a ^ distance) for a in range(atom_axis)])  17.4 us
    ppermute x16, starting transfers between devices, swap(): lax.ppermute(value, 'atoms', [(a, a ^ distance) for a in range(atom_axis)])  8.92 us
    pallas_call x1, Pallas kernels, per_device(): pl.pallas_call(functools.partial(covariance_kernel, frame_axis, atom_axis...  8.69 us
    ppermute x4, waiting for transfers between devices, hop(): lax.ppermute(down, 'frames', backward)  8.54 us
    ppermute x4, waiting for transfers between devices, hop(): lax.ppermute(up, 'frames', forward)  7.36 us
    unnamed x34, local copies, waits for them, and re-layouts  5.04 us
    ppermute x4, starting transfers between devices, hop(): lax.ppermute(up, 'frames', forward)  4.17 us
    ppermute x4, starting transfers between devices, hop(): lax.ppermute(down, 'frames', backward)  4.09 us
  transfers between devices with their start and end apart: 25, of which 16 were waited for; matrix products, arithmetic and copies ran while one was open for 0% of the time, Pallas kernels for 2%

profile of v21, /device:TPU:0, one launch (start us, length us, event | category | flops | bytes accessed | tf_op | source)
XLA Modules:
  0.0 71.3 jit_solution(4516783447418789308)
XLA Ops:
  0.6 1.7 %local_moments.1 = (f32[24,64]{1,0:T(8,128)S(1)}, f32[3,64,1024]{2,1,0:T(8,128)S(1)}, f32[3,1024]{1,0:T(4,128)S(1)}) custom-call(f32[3,64,1024]{2,1,0:T(8,128)} %bitcast.5, f32[3,1024]{1,0:T(4,128)} %ref_hbm.1), custom_call_target="tpu_custom_call" | custom-call | tf_op jit(solution)/shard_map/local_moments/pallas_call | solution.py:342
  2.3 2.4 %collective-permute-start.2 = (f32[24,64]{1,0:T(8,128)S(1)}, f32[24,64]{1,0:T(8,128)S(1)}, u32[]{:S(2)}, u32[]{:S(2)}) collective-permute-start(f32[24,64]{1,0:T(8,128)S(1)} %get-tuple-element.20.refs_0_), channel_id=1, source_target_pairs={{0,3},{1,2},{2,1},{3,0},{4,7},{5,6},{6,5},{7,4},{8,11},{9,10},{10,... | collective-permute-start | bytes 18440 | tf_op jit(solution)/shard_map/ppermute | solution.py:356
  4.7 0.6 collective-permute-start.1
  5.4 0.0 collective-permute-start
  5.4 0.7 %collective-permute-done.2.refs_3_ = f32[24,64]{1,0:T(8,128)S(1)} collective-permute-done((f32[24,64]{1,0:T(8,128)S(1)}, f32[24,64]{1,0:T(8,128)S(1)}, u32[]{:S(2)}, u32[]{:S(2)}) %collective-permute-start.2) | collective-permute-done | bytes 6176 | tf_op jit(solution)/shard_map/ppermute | solution.py:356
  6.1 2.3 %collective-permute-done.1.refs_2_ = f32[24,64]{1,0:T(8,128)S(1)} collective-permute-done((f32[24,64]{1,0:T(8,128)S(1)}, f32[24,64]{1,0:T(8,128)S(1)}, u32[]{:S(2)}, u32[]{:S(2)}) %collective-permute-start.1) | collective-permute-done | bytes 6176 | tf_op jit(solution)/shard_map/ppermute | solution.py:356
  8.4 0.0 collective-permute-done.refs_1_
  8.4 0.6 polar_align.1
  9.0 0.0 copy-start.4
  9.1 1.6 %collective-permute-start.3 = (bf16[2,3,256,128]{3,2,1,0:T(8,128)(2,1)S(1)}, bf16[2,3,256,128]{3,2,1,0:T(8,128)(2,1)S(1)}, u32[]{:S(2)}, u32[]{:S(2)}) collective-permute-start(bf16[2,3,256,128]{3,2,1,0:T(8,128)(2,1)S(1)} %get-tuple-element.23.refs_0_), channel_id=1, source_target_pairs={{0,8},{8,16},{16,24},{24,28},{28,20},{20,12},{12,4},{4,0},{1,9},{9... | collective-permute-start | bytes 1179656 | tf_op jit(solution)/shard_map/ppermute | solution.py:439
  10.7 0.4 collective-permute-start.4
  11.1 1.4 %copy-done.1 = bf16[3,1024,256]{2,1,0:T(8,128)(2,1)S(1)} copy-done((bf16[3,1024,256]{2,1,0:T(8,128)(2,1)S(1)}, bf16[3,1024,256]{2,1,0:T(8,128)(2,1)}, u32[]{:S(2)}) %copy-start.1) | copy-done | bytes 1572888
  12.5 0.5 project.1
  13.0 0.6 copy-done.10
  13.6 0.0 collective-permute-start.5
  13.6 0.6 collective-permute-start.6
  14.3 1.2 %collective-permute-start.7 = (f32[64,64]{1,0:T(8,128)S(1)}, f32[64,64]{1,0:T(8,128)S(1)}, u32[]{:S(2)}, u32[]{:S(2)}) collective-permute-start(f32[64,64]{1,0:T(8,128)S(1)} %get-tuple-element.28), channel_id=1, source_target_pairs={{0,3},{1,2},{2,1},{3,0},{4,7},{5,6},{6,5},{7,4},{8,11},{9,10},{10,... | collective-permute-start | bytes 49160 | tf_op jit(solution)/shard_map/ppermute | solution.py:356
  15.5 0.0 collective-permute-done.5.refs_24_
  15.5 2.3 %collective-permute-done.6.refs_25_ = f32[64,64]{1,0:T(8,128)S(1)} collective-permute-done((f32[64,64]{1,0:T(8,128)S(1)}, f32[64,64]{1,0:T(8,128)S(1)}, u32[]{:S(2)}, u32[]{:S(2)}) %collective-permute-start.6) | collective-permute-done | bytes 16416 | tf_op jit(solution)/shard_map/ppermute | solution.py:356
  17.8 0.1 collective-permute-done.7.refs_26_
  18.0 1.7 %collective-permute-done.3.refs_1_ = bf16[2,3,256,128]{3,2,1,0:T(8,128)(2,1)S(1)} collective-permute-done((bf16[2,3,256,128]{3,2,1,0:T(8,128)(2,1)S(1)}, bf16[2,3,256,128]{3,2,1,0:T(8,128)(2,1)S(1)}, u32[]{:S(2)}, u32[]{:S(2)}) %collective-permute-start.3) | collective-permute-done | bytes 393248 | tf_op jit(solution)/shard_map/ppermute | solution.py:439
  19.7 1.3 %collective-permute-done.4.refs_2_ = bf16[2,3,256,128]{3,2,1,0:T(8,128)(2,1)S(1)} collective-permute-done((bf16[2,3,256,128]{3,2,1,0:T(8,128)(2,1)S(1)}, bf16[2,3,256,128]{3,2,1,0:T(8,128)(2,1)S(1)}, u32[]{:S(2)}, u32[]{:S(2)}) %collective-permute-start.4) | collective-permute-done | bytes 393248 | tf_op jit(solution)/shard_map/ppermute | solution.py:439
  21.0 0.4 collective-permute-start.9
  21.4 1.6 %collective-permute-start.8 = (bf16[2,3,256,128]{3,2,1,0:T(8,128)(2,1)S(1)}, bf16[2,3,256,128]{3,2,1,0:T(8,128)(2,1)S(1)}, u32[]{:S(2)}, u32[]{:S(2)}) collective-permute-start(bf16[2,3,256,128]{3,2,1,0:T(8,128)(2,1)S(1)} %collective-permute-done.3.refs_1_), channel_id=1, source_target_pairs={{0,8},{8,16},{16,24},{24,28},{28,20},{20,12},{12,4},{4,0},{1,9},{9... | collective-permute-start | bytes 1179656 | tf_op jit(solution)/shard_map/ppermute | solution.py:439
  23.0 0.2 cut_columns.4.refs_0_
  23.2 2.6 %collective-permute-start.12 = (bf16[3,3,64,512]{3,2,1,0:T(8,128)(2,1)S(1)}, bf16[3,3,64,512]{3,2,1,0:T(8,128)(2,1)S(1)}, u32[]{:S(2)}, u32[]{:S(2)}) collective-permute-start(bf16[3,3,64,512]{3,2,1,0:T(8,128)(2,1)S(1)} %cut_columns.4.refs_0_), channel_id=1, source_target_pairs={{0,2},{4,6},{9,11},{13,15},{18,16},{22,20},{27,25},{31,29}} | collective-permute-start | bytes 1769480 | tf_op jit(solution)/shard_map/ppermute | solution.py:418
  25.9 4.4 %collective-permute-done.9.refs_1_.refs_4_ = bf16[2,3,256,128]{3,2,1,0:T(8,128)(2,1)S(1)} collective-permute-done((bf16[2,3,256,128]{3,2,1,0:T(8,128)(2,1)S(1)}, bf16[2,3,256,128]{3,2,1,0:T(8,128)(2,1)S(1)}, u32[]{:S(2)}, u32[]{:S(2)}) %collective-permute-start.9) | collective-permute-done | bytes 393248 | tf_op jit(solution)/shard_map/ppermute | solution.py:439
  30.3 0.4 collective-permute-done.8.refs_0_.refs_3_
  30.7 0.2 cut_columns.5.own_ref.refs_11_
  30.9 0.1 collective-permute-start.13
  31.0 1.6 %collective-permute-start.11 = (bf16[2,3,256,128]{3,2,1,0:T(8,128)(2,1)S(1)}, bf16[2,3,256,128]{3,2,1,0:T(8,128)(2,1)S(1)}, u32[]{:S(2)}, u32[]{:S(2)}) collective-permute-start(bf16[2,3,256,128]{3,2,1,0:T(8,128)(2,1)S(1)} %collective-permute-done.9.refs_1_.refs_4_), channel_id=1, source_target_pairs={{8,0},{16,8},{24,16},{28,24},{20,28},{12,20},{4,12},{0,4},{9,1},{1... | collective-permute-start | bytes 1179656 | tf_op jit(solution)/shard_map/ppermute | solution.py:439
  32.6 0.5 collective-permute-start.10
  33.1 0.0 collective-permute-done.13.beside_ref.refs_12_
  33.1 1.2 %collective-permute-start.14 = (bf16[2,3,64,256]{3,2,1,0:T(8,128)(2,1)S(1)}, bf16[2,3,64,256]{3,2,1,0:T(8,128)(2,1)S(1)}, u32[]{:S(2)}, u32[]{:S(2)}) collective-permute-start(bf16[2,3,64,256]{3,2,1,0:T(8,128)(2,1)S(1)} %pick_half.3), channel_id=1, source_target_pairs={{0,2},{1,3},{2,0},{3,1},{4,6},{5,7},{6,4},{7,5},{8,10},{9,11},{10,... | collective-permute-start | bytes 589832 | tf_op jit(solution)/shard_map/ppermute | solution.py:356
  34.3 0.0 collective-permute-done.12.refs_1_
  34.4 0.1 collective-permute-start.17
  34.5 5.4 %collective-permute-done.14.refs_13_ = bf16[2,3,64,256]{3,2,1,0:T(8,128)(2,1)S(1)} collective-permute-done((bf16[2,3,64,256]{3,2,1,0:T(8,128)(2,1)S(1)}, bf16[2,3,64,256]{3,2,1,0:T(8,128)(2,1)S(1)}, u32[]{:S(2)}, u32[]{:S(2)}) %collective-permute-start.14) | collective-permute-done | bytes 196640 | tf_op jit(solution)/shard_map/ppermute | solution.py:356
  39.9 2.7 %collective-permute-done.11.down_ref.refs_6_ = bf16[2,3,256,128]{3,2,1,0:T(8,128)(2,1)S(1)} collective-permute-done((bf16[2,3,256,128]{3,2,1,0:T(8,128)(2,1)S(1)}, bf16[2,3,256,128]{3,2,1,0:T(8,128)(2,1)S(1)}, u32[]{:S(2)}, u32[]{:S(2)}) %collective-permute-start.11) | collective-permute-done | bytes 393248 | tf_op jit(solution)/shard_map/ppermute | solution.py:439
  42.5 1.3 %collective-permute-done.10.up_ref.refs_5_ = bf16[2,3,256,128]{3,2,1,0:T(8,128)(2,1)S(1)} collective-permute-done((bf16[2,3,256,128]{3,2,1,0:T(8,128)(2,1)S(1)}, bf16[2,3,256,128]{3,2,1,0:T(8,128)(2,1)S(1)}, u32[]{:S(2)}, u32[]{:S(2)}) %collective-permute-start.10) | collective-permute-done | bytes 393248 | tf_op jit(solution)/shard_map/ppermute | solution.py:439
  43.8 0.2 cut_columns.6
  44.0 0.1 collective-permute-start.19
  44.1 0.5 collective-permute-start.15
  44.6 1.6 %collective-permute-start.16 = (bf16[3,256,128]{2,1,0:T(8,128)(2,1)S(1)}, bf16[3,256,128]{2,1,0:T(8,128)(2,1)S(1)}, u32[]{:S(2)}, u32[]{:S(2)}) collective-permute-start(bf16[3,256,128]{2,1,0:T(8,128)(2,1)S(1)} %get-tuple-element.32), channel_id=1, source_target_pairs={{8,0},{16,8},{24,16},{28,24},{20,28},{12,20},{4,12},{0,4},{9,1},{1... | collective-permute-start | bytes 589832 | tf_op jit(solution)/shard_map/ppermute | solution.py:439
  46.2 0.0 collective-permute-start.18
  46.2 0.0 collective-permute-done.19.beside_ref.refs_16_
  46.2 1.2 %collective-permute-start.20 = (bf16[2,3,64,256]{3,2,1,0:T(8,128)(2,1)S(1)}, bf16[2,3,64,256]{3,2,1,0:T(8,128)(2,1)S(1)}, u32[]{:S(2)}, u32[]{:S(2)}) collective-permute-start(bf16[2,3,64,256]{3,2,1,0:T(8,128)(2,1)S(1)} %pick_half.4), channel_id=1, source_target_pairs={{0,2},{1,3},{2,0},{3,1},{4,6},{5,7},{6,4},{7,5},{8,10},{9,11},{10,... | collective-permute-start | bytes 589832 | tf_op jit(solution)/shard_map/ppermute | solution.py:356
  47.4 0.0 collective-permute-done.17.refs_10_
  47.4 4.0 %collective-permute-done.15.up_half.refs_7_ = bf16[3,256,128]{2,1,0:T(8,128)(2,1)S(1)} collective-permute-done((bf16[3,256,128]{2,1,0:T(8,128)(2,1)S(1)}, bf16[3,256,128]{2,1,0:T(8,128)(2,1)S(1)}, u32[]{:S(2)}, u32[]{:S(2)}) %collective-permute-start.15) | collective-permute-done | bytes 196640 | tf_op jit(solution)/shard_map/ppermute | solution.py:439
  51.4 0.2 collective-permute-done.16.down_half.refs_8_
  51.6 0.1 cut_columns.7.own_ref.refs_19_
  51.7 0.1 collective-permute-start.22
  51.8 0.0 collective-permute-done.18.refs_14_
  51.8 1.8 %collective-permute-done.20.refs_17_ = bf16[2,3,64,256]{3,2,1,0:T(8,128)(2,1)S(1)} collective-permute-done((bf16[2,3,64,256]{3,2,1,0:T(8,128)(2,1)S(1)}, bf16[2,3,64,256]{3,2,1,0:T(8,128)(2,1)S(1)}, u32[]{:S(2)}, u32[]{:S(2)}) %collective-permute-start.20) | collective-permute-done | bytes 196640 | tf_op jit(solution)/shard_map/ppermute | solution.py:356
  53.6 0.0 collective-permute-done.22.beside_ref.refs_20_
  53.6 1.2 %collective-permute-start.23 = (bf16[1,3,64,256]{3,2,1,0:T(8,128)(2,1)S(1)}, bf16[1,3,64,256]{3,2,1,0:T(8,128)(2,1)S(1)}, u32[]{:S(2)}, u32[]{:S(2)}) collective-permute-start(bf16[1,3,64,256]{3,2,1,0:T(8,128)(2,1)S(1)} %pick_half.5), channel_id=1, source_target_pairs={{0,2},{1,3},{2,0},{3,1},{4,6},{5,7},{6,4},{7,5},{8,10},{9,11},{10,... | collective-permute-start | bytes 294920 | tf_op jit(solution)/shard_map/ppermute | solution.py:356
  54.8 0.0 collective-permute-start.21
  54.8 3.5 %collective-permute-done.23.refs_21_ = bf16[1,3,64,256]{3,2,1,0:T(8,128)(2,1)S(1)} collective-permute-done((bf16[1,3,64,256]{3,2,1,0:T(8,128)(2,1)S(1)}, bf16[1,3,64,256]{3,2,1,0:T(8,128)(2,1)S(1)}, u32[]{:S(2)}, u32[]{:S(2)}) %collective-permute-start.23) | collective-permute-done | bytes 98336 | tf_op jit(solution)/shard_map/ppermute | solution.py:356
  58.3 0.0 collective-permute-start.24
  58.3 1.3 %collective-permute-done.24.refs_22_ = bf16[1,3,64,256]{3,2,1,0:T(8,128)(2,1)S(1)} collective-permute-done((bf16[1,3,64,256]{3,2,1,0:T(8,128)(2,1)S(1)}, bf16[1,3,64,256]{3,2,1,0:T(8,128)(2,1)S(1)}, u32[]{:S(2)}, u32[]{:S(2)}) %collective-permute-start.24) | collective-permute-done | bytes 98336 | tf_op jit(solution)/shard_map/ppermute | solution.py:356
  59.6 0.0 copy-start.5
  59.6 1.0 %copy-done.5 = bf16[2,3,256,128]{3,2,1,0:T(8,128)(2,1)S(1)} copy-done((bf16[2,3,256,128]{3,2,1,0:T(8,128)(2,1)S(1)}, bf16[2,3,256,128]{3,2,1,0:T(8,128)(2,1)}, u32[]{:S(2)}) %copy-start.5) | copy-done | bytes 393240
  60.6 1.0 %copy-done.7 = bf16[2,3,256,128]{3,2,1,0:T(8,128)(2,1)S(1)} copy-done((bf16[2,3,256,128]{3,2,1,0:T(8,128)(2,1)S(1)}, bf16[2,3,256,128]{3,2,1,0:T(8,128)(2,1)}, u32[]{:S(2)}) %copy-start.7) | copy-done | bytes 393240
  61.6 1.0 %copy-done.9 = bf16[2,3,256,128]{3,2,1,0:T(8,128)(2,1)S(1)} copy-done((bf16[2,3,256,128]{3,2,1,0:T(8,128)(2,1)S(1)}, bf16[2,3,256,128]{3,2,1,0:T(8,128)(2,1)}, u32[]{:S(2)}) %copy-start.9) | copy-done | bytes 393240
  62.6 8.7 %covariance_tile.1 = (f32[3,3,1024,512]{3,2,1,0:T(8,128)}, f32[64,64]{1,0:T(8,128)}) custom-call(s32[1]{0:T(128)} %bitcast.role_ref, bf16[2,3,256,128]{3,2,1,0:T(8,128)(2,1)S(1)} %copy-done.5, bf16[2,3,256,128]{3,2,1,0:T(8,128)(2,1)S(1)} %copy-done.7, bf16[2,3,256,128]{3,2,1,0:T(8,128)(2,1)S(1)} %copy-done.9, ...), custom_call_target="tpu_custom_call" | custom-call | flops 4831838208 | bytes 25165824 | tf_op jit(solution)/shard_map/covariance_tile/pallas_call | solution.py:465
  (32 shorter events, 0.1 us)
Async XLA Ops:
  2.3 3.8 %collective-permute-start.2 = (f32[24,64]{1,0:T(8,128)S(1)}, f32[24,64]{1,0:T(8,128)S(1)}, u32[]{:S(2)}, u32[]{:S(2)}) collective-permute-start(f32[24,64]{1,0:T(8,128)S(1)} %get-tuple-element.20.refs_0_), channel_id=1, source_target_pairs={{0,3},{1,2},{2,1},{3,0},{4,7},{5,6},{6,5},{7,4},{8,11},{9,10},{10,... | collective-permute-start | bytes 18440 | tf_op jit(solution)/shard_map/ppermute | solution.py:356
  4.7 3.7 %collective-permute-start.1 = (f32[24,64]{1,0:T(8,128)S(1)}, f32[24,64]{1,0:T(8,128)S(1)}, u32[]{:S(2)}, u32[]{:S(2)}) collective-permute-start(f32[24,64]{1,0:T(8,128)S(1)} %get-tuple-element.20.refs_0_), channel_id=1, source_target_pairs={{0,2},{1,3},{2,0},{3,1},{4,6},{5,7},{6,4},{7,5},{8,10},{9,11},{10,... | collective-permute-start | bytes 18440 | tf_op jit(solution)/shard_map/ppermute | solution.py:356
  5.4 3.1 %collective-permute-start = (f32[24,64]{1,0:T(8,128)S(1)}, f32[24,64]{1,0:T(8,128)S(1)}, u32[]{:S(2)}, u32[]{:S(2)}) collective-permute-start(f32[24,64]{1,0:T(8,128)S(1)} %get-tuple-element.20.refs_0_), channel_id=1, source_target_pairs={{0,1},{1,0},{2,3},{3,2},{4,5},{5,4},{6,7},{7,6},{8,9},{9,8},{10,11... | collective-permute-start | bytes 18440 | tf_op jit(solution)/shard_map/ppermute | solution.py:356
  9.0 21.3 %copy-start.4 = (bf16[2,3,256,128]{3,2,1,0:T(8,128)(2,1)}, bf16[2,3,256,128]{3,2,1,0:T(8,128)(2,1)S(1)}, u32[]{:S(2)}) copy-start(bf16[2,3,256,128]{3,2,1,0:T(8,128)(2,1)S(1)} %get-tuple-element.23.refs_0_) | copy-start | bytes 1179652
  9.1 10.6 %collective-permute-start.3 = (bf16[2,3,256,128]{3,2,1,0:T(8,128)(2,1)S(1)}, bf16[2,3,256,128]{3,2,1,0:T(8,128)(2,1)S(1)}, u32[]{:S(2)}, u32[]{:S(2)}) collective-permute-start(bf16[2,3,256,128]{3,2,1,0:T(8,128)(2,1)S(1)} %get-tuple-element.23.refs_0_), channel_id=1, source_target_pairs={{0,8},{8,16},{16,24},{24,28},{28,20},{20,12},{12,4},{4,0},{1,9},{9... | collective-permute-start | bytes 1179656 | tf_op jit(solution)/shard_map/ppermute | solution.py:439
  10.7 10.3 %collective-permute-start.4 = (bf16[2,3,256,128]{3,2,1,0:T(8,128)(2,1)S(1)}, bf16[2,3,256,128]{3,2,1,0:T(8,128)(2,1)S(1)}, u32[]{:S(2)}, u32[]{:S(2)}) collective-permute-start(bf16[2,3,256,128]{3,2,1,0:T(8,128)(2,1)S(1)} %get-tuple-element.23.refs_0_), channel_id=1, source_target_pairs={{8,0},{16,8},{24,16},{28,24},{20,28},{12,20},{4,12},{0,4},{9,1},{1... | collective-permute-start | bytes 1179656 | tf_op jit(solution)/shard_map/ppermute | solution.py:439
  11.1 1.4 %copy-start.1 = (bf16[3,1024,256]{2,1,0:T(8,128)(2,1)S(1)}, bf16[3,1024,256]{2,1,0:T(8,128)(2,1)}, u32[]{:S(2)}) copy-start(bf16[3,1024,256]{2,1,0:T(8,128)(2,1)} %eig_ref.1) | copy-start | bytes 4718596
  13.0 0.6 copy-start.10
  13.6 1.9 %collective-permute-start.5 = (f32[64,64]{1,0:T(8,128)S(1)}, f32[64,64]{1,0:T(8,128)S(1)}, u32[]{:S(2)}, u32[]{:S(2)}) collective-permute-start(f32[64,64]{1,0:T(8,128)S(1)} %get-tuple-element.26), channel_id=1, source_target_pairs={{0,1},{1,0},{2,3},{3,2},{4,5},{5,4},{6,7},{7,6},{8,9},{9,8},{10,11... | collective-permute-start | bytes 49160 | tf_op jit(solution)/shard_map/ppermute | solution.py:356
  13.6 4.2 %collective-permute-start.6 = (f32[64,64]{1,0:T(8,128)S(1)}, f32[64,64]{1,0:T(8,128)S(1)}, u32[]{:S(2)}, u32[]{:S(2)}) collective-permute-start(f32[64,64]{1,0:T(8,128)S(1)} %get-tuple-element.27), channel_id=1, source_target_pairs={{0,2},{1,3},{2,0},{3,1},{4,6},{5,7},{6,4},{7,5},{8,10},{9,11},{10,... | collective-permute-start | bytes 49160 | tf_op jit(solution)/shard_map/ppermute | solution.py:356
  14.3 3.7 %collective-permute-start.7 = (f32[64,64]{1,0:T(8,128)S(1)}, f32[64,64]{1,0:T(8,128)S(1)}, u32[]{:S(2)}, u32[]{:S(2)}) collective-permute-start(f32[64,64]{1,0:T(8,128)S(1)} %get-tuple-element.28), channel_id=1, source_target_pairs={{0,3},{1,2},{2,1},{3,0},{4,7},{5,6},{6,5},{7,4},{8,11},{9,10},{10,... | collective-permute-start | bytes 49160 | tf_op jit(solution)/shard_map/ppermute | solution.py:356
  15.5 7.5 %copy-start.14 = (f32[64,64]{1,0:T(8,128)}, f32[64,64]{1,0:T(8,128)S(1)}, u32[]{:S(2)}) copy-start(f32[64,64]{1,0:T(8,128)S(1)} %collective-permute-done.5.refs_24_) | copy-start | bytes 49156
  17.8 5.2 %copy-start.15 = (f32[64,64]{1,0:T(8,128)}, f32[64,64]{1,0:T(8,128)S(1)}, u32[]{:S(2)}) copy-start(f32[64,64]{1,0:T(8,128)S(1)} %collective-permute-done.6.refs_25_) | copy-start | bytes 49156
  18.0 5.0 %copy-start.16 = (f32[64,64]{1,0:T(8,128)}, f32[64,64]{1,0:T(8,128)S(1)}, u32[]{:S(2)}) copy-start(f32[64,64]{1,0:T(8,128)S(1)} %collective-permute-done.7.refs_26_) | copy-start | bytes 49156
  19.7 11.0 %copy-start.6 = (bf16[2,3,256,128]{3,2,1,0:T(8,128)(2,1)}, bf16[2,3,256,128]{3,2,1,0:T(8,128)(2,1)S(1)}, u32[]{:S(2)}) copy-start(bf16[2,3,256,128]{3,2,1,0:T(8,128)(2,1)S(1)} %collective-permute-done.3.refs_1_) | copy-start | bytes 1179652
  21.0 9.9 %copy-start.8 = (bf16[2,3,256,128]{3,2,1,0:T(8,128)(2,1)}, bf16[2,3,256,128]{3,2,1,0:T(8,128)(2,1)S(1)}, u32[]{:S(2)}) copy-start(bf16[2,3,256,128]{3,2,1,0:T(8,128)(2,1)S(1)} %collective-permute-done.4.refs_2_) | copy-start | bytes 1179652
  21.0 9.3 %collective-permute-start.9 = (bf16[2,3,256,128]{3,2,1,0:T(8,128)(2,1)S(1)}, bf16[2,3,256,128]{3,2,1,0:T(8,128)(2,1)S(1)}, u32[]{:S(2)}, u32[]{:S(2)}) collective-permute-start(bf16[2,3,256,128]{3,2,1,0:T(8,128)(2,1)S(1)} %collective-permute-done.4.refs_2_), channel_id=1, source_target_pairs={{8,0},{16,8},{24,16},{28,24},{20,28},{12,20},{4,12},{0,4},{9,1},{1... | collective-permute-start | bytes 1179656 | tf_op jit(solution)/shard_map/ppermute | solution.py:439
  21.4 9.3 %collective-permute-start.8 = (bf16[2,3,256,128]{3,2,1,0:T(8,128)(2,1)S(1)}, bf16[2,3,256,128]{3,2,1,0:T(8,128)(2,1)S(1)}, u32[]{:S(2)}, u32[]{:S(2)}) collective-permute-start(bf16[2,3,256,128]{3,2,1,0:T(8,128)(2,1)S(1)} %collective-permute-done.3.refs_1_), channel_id=1, source_target_pairs={{0,8},{8,16},{16,24},{24,28},{28,20},{20,12},{12,4},{4,0},{1,9},{9... | collective-permute-start | bytes 1179656 | tf_op jit(solution)/shard_map/ppermute | solution.py:439
  23.2 11.1 %collective-permute-start.12 = (bf16[3,3,64,512]{3,2,1,0:T(8,128)(2,1)S(1)}, bf16[3,3,64,512]{3,2,1,0:T(8,128)(2,1)S(1)}, u32[]{:S(2)}, u32[]{:S(2)}) collective-permute-start(bf16[3,3,64,512]{3,2,1,0:T(8,128)(2,1)S(1)} %cut_columns.4.refs_0_), channel_id=1, source_target_pairs={{0,2},{4,6},{9,11},{13,15},{18,16},{22,20},{27,25},{31,29}} | collective-permute-start | bytes 1769480 | tf_op jit(solution)/shard_map/ppermute | solution.py:418
  30.9 28.7 %copy-start = (bf16[2,3,64,512]{3,2,1,0:T(8,128)(2,1)}, bf16[2,3,64,512]{3,2,1,0:T(8,128)(2,1)S(1)}, u32[]{:S(2)}) copy-start(bf16[2,3,64,512]{3,2,1,0:T(8,128)(2,1)S(1)} %cut_columns.5.own_ref.refs_11_) | copy-start | bytes 1179652
  30.9 2.2 %collective-permute-start.13 = (bf16[2,3,64,512]{3,2,1,0:T(8,128)(2,1)S(1)}, bf16[2,3,64,512]{3,2,1,0:T(8,128)(2,1)S(1)}, u32[]{:S(2)}, u32[]{:S(2)}) collective-permute-start(bf16[2,3,64,512]{3,2,1,0:T(8,128)(2,1)S(1)} %cut_columns.5.own_ref.refs_11_), channel_id=1, source_target_pairs={{0,1},{1,0},{2,3},{3,2},{4,5},{5,4},{6,7},{7,6},{8,9},{9,8},{10,11... | collective-permute-start | bytes 1179656 | tf_op jit(solution)/shard_map/ppermute | solution.py:356
  31.0 11.5 %collective-permute-start.11 = (bf16[2,3,256,128]{3,2,1,0:T(8,128)(2,1)S(1)}, bf16[2,3,256,128]{3,2,1,0:T(8,128)(2,1)S(1)}, u32[]{:S(2)}, u32[]{:S(2)}) collective-permute-start(bf16[2,3,256,128]{3,2,1,0:T(8,128)(2,1)S(1)} %collective-permute-done.9.refs_1_.refs_4_), channel_id=1, source_target_pairs={{8,0},{16,8},{24,16},{28,24},{20,28},{12,20},{4,12},{0,4},{9,1},{1... | collective-permute-start | bytes 1179656 | tf_op jit(solution)/shard_map/ppermute | solution.py:439
  32.6 11.2 %collective-permute-start.10 = (bf16[2,3,256,128]{3,2,1,0:T(8,128)(2,1)S(1)}, bf16[2,3,256,128]{3,2,1,0:T(8,128)(2,1)S(1)}, u32[]{:S(2)}, u32[]{:S(2)}) collective-permute-start(bf16[2,3,256,128]{3,2,1,0:T(8,128)(2,1)S(1)} %collective-permute-done.8.refs_0_.refs_3_), channel_id=1, source_target_pairs={{0,8},{8,16},{16,24},{24,28},{28,20},{20,12},{12,4},{4,0},{1,9},{9... | collective-permute-start | bytes 1179656 | tf_op jit(solution)/shard_map/ppermute | solution.py:439
  33.1 26.5 %copy-start.3 = (bf16[2,3,64,512]{3,2,1,0:T(8,128)(2,1)}, bf16[2,3,64,512]{3,2,1,0:T(8,128)(2,1)S(1)}, u32[]{:S(2)}) copy-start(bf16[2,3,64,512]{3,2,1,0:T(8,128)(2,1)S(1)} %collective-permute-done.13.beside_ref.refs_12_) | copy-start | bytes 1179652
  33.1 6.7 %collective-permute-start.14 = (bf16[2,3,64,256]{3,2,1,0:T(8,128)(2,1)S(1)}, bf16[2,3,64,256]{3,2,1,0:T(8,128)(2,1)S(1)}, u32[]{:S(2)}, u32[]{:S(2)}) collective-permute-start(bf16[2,3,64,256]{3,2,1,0:T(8,128)(2,1)S(1)} %pick_half.3), channel_id=1, source_target_pairs={{0,2},{1,3},{2,0},{3,1},{4,6},{5,7},{6,4},{7,5},{8,10},{9,11},{10,... | collective-permute-start | bytes 589832 | tf_op jit(solution)/shard_map/ppermute | solution.py:356
  34.4 25.2 %copy-start.2 = (bf16[3,3,64,512]{3,2,1,0:T(8,128)(2,1)}, bf16[3,3,64,512]{3,2,1,0:T(8,128)(2,1)S(1)}, u32[]{:S(2)}) copy-start(bf16[3,3,64,512]{3,2,1,0:T(8,128)(2,1)S(1)} %pass_on.1.refs_9_) | copy-start | bytes 1769476
  34.4 13.0 %collective-permute-start.17 = (bf16[3,3,64,512]{3,2,1,0:T(8,128)(2,1)S(1)}, bf16[3,3,64,512]{3,2,1,0:T(8,128)(2,1)S(1)}, u32[]{:S(2)}, u32[]{:S(2)}) collective-permute-start(bf16[3,3,64,512]{3,2,1,0:T(8,128)(2,1)S(1)} %pass_on.1.refs_9_), channel_id=1, source_target_pairs={{0,1},{1,0},{2,3},{3,2},{4,5},{5,4},{6,7},{7,6},{8,9},{9,8},{10,11... | collective-permute-start | bytes 1769480 | tf_op jit(solution)/shard_map/ppermute | solution.py:356
  39.9 19.8 %copy-start.12 = (bf16[2,3,64,256]{3,2,1,0:T(8,128)(2,1)}, bf16[2,3,64,256]{3,2,1,0:T(8,128)(2,1)S(1)}, u32[]{:S(2)}) copy-start(bf16[2,3,64,256]{3,2,1,0:T(8,128)(2,1)S(1)} %collective-permute-done.14.refs_13_) | copy-start | bytes 589828
  44.0 2.2 %collective-permute-start.19 = (bf16[2,3,64,512]{3,2,1,0:T(8,128)(2,1)S(1)}, bf16[2,3,64,512]{3,2,1,0:T(8,128)(2,1)S(1)}, u32[]{:S(2)}, u32[]{:S(2)}) collective-permute-start(bf16[2,3,64,512]{3,2,1,0:T(8,128)(2,1)S(1)} %get-tuple-element.33.own_ref.refs_15_), channel_id=1, source_target_pairs={{0,1},{1,0},{2,3},{3,2},{4,5},{5,4},{6,7},{7,6},{8,9},{9,8},{10,11... | collective-permute-start | bytes 1179656 | tf_op jit(solution)/shard_map/ppermute | solution.py:356
  44.1 7.3 %collective-permute-start.15 = (bf16[3,256,128]{2,1,0:T(8,128)(2,1)S(1)}, bf16[3,256,128]{2,1,0:T(8,128)(2,1)S(1)}, u32[]{:S(2)}, u32[]{:S(2)}) collective-permute-start(bf16[3,256,128]{2,1,0:T(8,128)(2,1)S(1)} %get-tuple-element.31), channel_id=1, source_target_pairs={{0,8},{8,16},{16,24},{24,28},{28,20},{20,12},{12,4},{4,0},{1,9},{9... | collective-permute-start | bytes 589832 | tf_op jit(solution)/shard_map/ppermute | solution.py:439
  44.6 7.0 %collective-permute-start.16 = (bf16[3,256,128]{2,1,0:T(8,128)(2,1)S(1)}, bf16[3,256,128]{2,1,0:T(8,128)(2,1)S(1)}, u32[]{:S(2)}, u32[]{:S(2)}) collective-permute-start(bf16[3,256,128]{2,1,0:T(8,128)(2,1)S(1)} %get-tuple-element.32), channel_id=1, source_target_pairs={{8,0},{16,8},{24,16},{28,24},{20,28},{12,20},{4,12},{0,4},{9,1},{1... | collective-permute-start | bytes 589832 | tf_op jit(solution)/shard_map/ppermute | solution.py:439
  46.2 5.6 %collective-permute-start.18 = (bf16[2,3,64,256]{3,2,1,0:T(8,128)(2,1)S(1)}, bf16[2,3,64,256]{3,2,1,0:T(8,128)(2,1)S(1)}, u32[]{:S(2)}, u32[]{:S(2)}) collective-permute-start(bf16[2,3,64,256]{3,2,1,0:T(8,128)(2,1)S(1)} %collective-permute-done.14.refs_13_), channel_id=1, source_target_pairs={{0,1},{1,0},{2,3},{3,2},{4,5},{5,4},{6,7},{7,6},{8,9},{9,8},{10,11... | collective-permute-start | bytes 589832 | tf_op jit(solution)/shard_map/ppermute | solution.py:356
  46.2 7.4 %collective-permute-start.20 = (bf16[2,3,64,256]{3,2,1,0:T(8,128)(2,1)S(1)}, bf16[2,3,64,256]{3,2,1,0:T(8,128)(2,1)S(1)}, u32[]{:S(2)}, u32[]{:S(2)}) collective-permute-start(bf16[2,3,64,256]{3,2,1,0:T(8,128)(2,1)S(1)} %pick_half.4), channel_id=1, source_target_pairs={{0,2},{1,3},{2,0},{3,1},{4,6},{5,7},{6,4},{7,5},{8,10},{9,11},{10,... | collective-permute-start | bytes 589832 | tf_op jit(solution)/shard_map/ppermute | solution.py:356
  47.4 12.2 %copy-start.11 = (bf16[3,3,64,512]{3,2,1,0:T(8,128)(2,1)}, bf16[3,3,64,512]{3,2,1,0:T(8,128)(2,1)S(1)}, u32[]{:S(2)}) copy-start(bf16[3,3,64,512]{3,2,1,0:T(8,128)(2,1)S(1)} %collective-permute-done.17.refs_10_) | copy-start | bytes 1769476
  51.7 1.9 %collective-permute-start.22 = (bf16[1,3,64,512]{3,2,1,0:T(8,128)(2,1)S(1)}, bf16[1,3,64,512]{3,2,1,0:T(8,128)(2,1)S(1)}, u32[]{:S(2)}, u32[]{:S(2)}) collective-permute-start(bf16[1,3,64,512]{3,2,1,0:T(8,128)(2,1)S(1)} %cut_columns.7.own_ref.refs_19_), channel_id=1, source_target_pairs={{0,1},{1,0},{2,3},{3,2},{4,5},{5,4},{6,7},{7,6},{8,9},{9,8},{10,11... | collective-permute-start | bytes 589832 | tf_op jit(solution)/shard_map/ppermute | solution.py:356
  51.8 7.8 %copy-start.13 = (bf16[2,3,64,256]{3,2,1,0:T(8,128)(2,1)}, bf16[2,3,64,256]{3,2,1,0:T(8,128)(2,1)S(1)}, u32[]{:S(2)}) copy-start(bf16[2,3,64,256]{3,2,1,0:T(8,128)(2,1)S(1)} %collective-permute-done.18.refs_14_) | copy-start | bytes 589828
  53.6 4.7 %collective-permute-start.23 = (bf16[1,3,64,256]{3,2,1,0:T(8,128)(2,1)S(1)}, bf16[1,3,64,256]{3,2,1,0:T(8,128)(2,1)S(1)}, u32[]{:S(2)}, u32[]{:S(2)}) collective-permute-start(bf16[1,3,64,256]{3,2,1,0:T(8,128)(2,1)S(1)} %pick_half.5), channel_id=1, source_target_pairs={{0,2},{1,3},{2,0},{3,1},{4,6},{5,7},{6,4},{7,5},{8,10},{9,11},{10,... | collective-permute-start | bytes 294920 | tf_op jit(solution)/shard_map/ppermute | solution.py:356
  54.8 4.8 %collective-permute-start.21 = (bf16[2,3,64,256]{3,2,1,0:T(8,128)(2,1)S(1)}, bf16[2,3,64,256]{3,2,1,0:T(8,128)(2,1)S(1)}, u32[]{:S(2)}, u32[]{:S(2)}) collective-permute-start(bf16[2,3,64,256]{3,2,1,0:T(8,128)(2,1)S(1)} %collective-permute-done.20.refs_17_), channel_id=1, source_target_pairs={{0,1},{1,0},{2,3},{3,2},{4,5},{5,4},{6,7},{7,6},{8,9},{9,8},{10,11... | collective-permute-start | bytes 589832 | tf_op jit(solution)/shard_map/ppermute | solution.py:356
  58.3 1.3 %collective-permute-start.24 = (bf16[1,3,64,256]{3,2,1,0:T(8,128)(2,1)S(1)}, bf16[1,3,64,256]{3,2,1,0:T(8,128)(2,1)S(1)}, u32[]{:S(2)}, u32[]{:S(2)}) collective-permute-start(bf16[1,3,64,256]{3,2,1,0:T(8,128)(2,1)S(1)} %collective-permute-done.23.refs_21_), channel_id=1, source_target_pairs={{0,1},{1,0},{2,3},{3,2},{4,5},{5,4},{6,7},{7,6},{8,9},{9,8},{10,11... | collective-permute-start | bytes 294920 | tf_op jit(solution)/shard_map/ppermute | solution.py:356
  59.6 1.0 %copy-start.5 = (bf16[2,3,256,128]{3,2,1,0:T(8,128)(2,1)S(1)}, bf16[2,3,256,128]{3,2,1,0:T(8,128)(2,1)}, u32[]{:S(2)}) copy-start(bf16[2,3,256,128]{3,2,1,0:T(8,128)(2,1)} %copy-done.4) | copy-start | bytes 1179652
  60.6 1.0 %copy-start.7 = (bf16[2,3,256,128]{3,2,1,0:T(8,128)(2,1)S(1)}, bf16[2,3,256,128]{3,2,1,0:T(8,128)(2,1)}, u32[]{:S(2)}) copy-start(bf16[2,3,256,128]{3,2,1,0:T(8,128)(2,1)} %copy-done.6) | copy-start | bytes 1179652
  61.6 1.0 %copy-start.9 = (bf16[2,3,256,128]{3,2,1,0:T(8,128)(2,1)S(1)}, bf16[2,3,256,128]{3,2,1,0:T(8,128)(2,1)}, u32[]{:S(2)}) copy-start(bf16[2,3,256,128]{3,2,1,0:T(8,128)(2,1)} %copy-done.8) | copy-start | bytes 1179652

commit v22 on v20

--- a/solution.py
+++ b/solution.py
@@ -226,14 +226,14 @@
             for n in range(groups[k][0])
         ]
 
-    def for_each_group(from_hbm, act):
+    def for_each_group(copied, act):
         for role in range(roles):
 
             @pl.when(role_ref[0] == role)
             def _(role=role):
                 to = 0
-                for k, (count, in_hbm, _) in enumerate(groups):
-                    if in_hbm == from_hbm:
+                for k, (count, by_copy, _) in enumerate(groups):
+                    if by_copy == copied:
                         act(k, role, to)
                     to += count * depth
 
@@ -441,7 +441,7 @@
     one = hop(own, own)
     cut_one = kernel(cut_kernel, columns(3), half, [own, *one], "cut_columns")
     two = hop(after(one[0], *parts), one[1])
-    in_hbm = pass_on(cross(cut_one), role)
+    first_group = pass_on(cross(cut_one), role)
     cut_two = kernel(cut_kernel, columns(2), half, list(two), "cut_columns")
     three = hop(*two)
     in_vmem = pass_on(cross(cut_two), role)
@@ -449,7 +449,7 @@
     cut_three, *halves = kernel(
         cut_last_kernel,
         (columns(2), half_shard, half_shard),
-        after(half, in_hbm[0]),
+        after(half, first_group[0]),
         list(three),
         "cut_columns",
     )
@@ -457,7 +457,7 @@
     three_halves, picked = halves_across(cut_three)
     in_vmem += three_halves
     cut_four = kernel(
-        cut_far_kernel, columns(1), after(half, in_hbm[1], in_vmem[0], picked), list(far), "cut_columns"
+        cut_far_kernel, columns(1), after(half, first_group[1], in_vmem[0], picked), list(far), "cut_columns"
     )
     in_vmem += halves_across(cut_four, three_halves[2])[0]
     groups = ((3, True, 2), (2, False, 2), (2, False, 4), (1, False, 4))
@@ -469,7 +469,7 @@
         out_shape=(jax.ShapeDtypeStruct((3, 3, local_atoms, block), jnp.float32), share),
         in_specs=[SMEM]
         + [VMEM] * len(rows)
-        + [HBM] * len(in_hbm)
+        + [HBM, VMEM]
         + [VMEM] * len(in_vmem)
         + [HBM] * len(parts),
         out_specs=(ANY, ANY),
@@ -492,7 +492,8 @@
     )(
         role,
         *[pinned(value, pltpu.VMEM) for value in rows],
-        *[pinned(value, pltpu.HBM) for value in in_hbm],
+        pinned(first_group[0], pltpu.HBM),
+        pinned(first_group[1], pltpu.VMEM),
         *[pinned(value, pltpu.VMEM) for value in in_vmem],
         *[pinned(value, pltpu.HBM) for value in parts],
     )

time: 67.1 us -> 66.8 us (level)
    unnamed x18 -> x16, local copies, waits for them, and re-layouts: 3.02 us -> 3.02 us
where the time goes in v22:
time: 66.8 us; the launch traced here: 66 us
  starting transfers between devices  25.6 us (38%)
  waiting for transfers between devices  24.3 us (36%)
  Pallas kernels  12.2 us (18%)
  local copies, waits for them, and re-layouts  3.02 us (5%)
  between operations  0.82 us (1%)
    ppermute x14, waiting for transfers between devices, swap(): lax.ppermute(value, 'atoms', [(a, a ^ distance) for a in range(atom_axis)])  11.2 us
    ppermute x14, starting transfers between devices, swap(): lax.ppermute(value, 'atoms', [(a, a ^ distance) for a in range(atom_axis)])  10.3 us
    pallas_call x1, Pallas kernels, per_device(): pl.pallas_call(functools.partial(covariance_kernel, frame_axis, atom_axis...  8.6 us
    ppermute x4, waiting for transfers between devices, hop(): lax.ppermute(down, 'frames', backward)  7.3 us
    ppermute x2, starting transfers between devices, cross(): return [cut, lax.ppermute(cut, axes, pairs(0, 2))]  7.04 us
    ppermute x4, starting transfers between devices, hop(): lax.ppermute(up, 'frames', forward)  5.76 us
    ppermute x4, waiting for transfers between devices, hop(): lax.ppermute(up, 'frames', forward)  3.57 us
    unnamed x16, local copies, waits for them, and re-layouts  3.02 us
  transfers between devices with their start and end apart: 24, of which 16 were waited for; matrix products, arithmetic and copies ran while one was open for 0% of the time, Pallas kernels for 2%

profile of v22, /device:TPU:0, one launch (start us, length us, event | category | flops | bytes accessed | tf_op | source)
XLA Modules:
  0.0 66.0 jit_solution(8631970417759705315)
XLA Ops:
  0.6 1.7 %local_moments.1 = (f32[24,64]{1,0:T(8,128)S(1)}, f32[3,64,1024]{2,1,0:T(8,128)S(1)}, f32[3,1024]{1,0:T(4,128)S(1)}) custom-call(f32[3,64,1024]{2,1,0:T(8,128)} %bitcast.5, f32[3,1024]{1,0:T(4,128)} %ref_hbm.1), custom_call_target="tpu_custom_call" | custom-call | tf_op jit(solution)/shard_map/local_moments/pallas_call | solution.py:342
  2.3 2.4 %collective-permute-start.2 = (f32[24,64]{1,0:T(8,128)S(1)}, f32[24,64]{1,0:T(8,128)S(1)}, u32[]{:S(2)}, u32[]{:S(2)}) collective-permute-start(f32[24,64]{1,0:T(8,128)S(1)} %get-tuple-element.20.refs_0_), channel_id=1, source_target_pairs={{0,3},{1,2},{2,1},{3,0},{4,7},{5,6},{6,5},{7,4},{8,11},{9,10},{10,... | collective-permute-start | bytes 18440 | tf_op jit(solution)/shard_map/ppermute | solution.py:356
  4.7 0.6 collective-permute-start.1
  5.4 0.0 collective-permute-start
  5.4 0.7 %collective-permute-done.2.refs_3_ = f32[24,64]{1,0:T(8,128)S(1)} collective-permute-done((f32[24,64]{1,0:T(8,128)S(1)}, f32[24,64]{1,0:T(8,128)S(1)}, u32[]{:S(2)}, u32[]{:S(2)}) %collective-permute-start.2) | collective-permute-done | bytes 6176 | tf_op jit(solution)/shard_map/ppermute | solution.py:356
  6.1 2.3 %collective-permute-done.1.refs_2_ = f32[24,64]{1,0:T(8,128)S(1)} collective-permute-done((f32[24,64]{1,0:T(8,128)S(1)}, f32[24,64]{1,0:T(8,128)S(1)}, u32[]{:S(2)}, u32[]{:S(2)}) %collective-permute-start.1) | collective-permute-done | bytes 6176 | tf_op jit(solution)/shard_map/ppermute | solution.py:356
  8.4 0.0 collective-permute-done.refs_1_
  8.4 0.6 polar_align.1
  9.0 1.6 %collective-permute-start.3 = (bf16[2,3,256,128]{3,2,1,0:T(8,128)(2,1)S(1)}, bf16[2,3,256,128]{3,2,1,0:T(8,128)(2,1)S(1)}, u32[]{:S(2)}, u32[]{:S(2)}) collective-permute-start(bf16[2,3,256,128]{3,2,1,0:T(8,128)(2,1)S(1)} %get-tuple-element.23.refs_0_), channel_id=1, source_target_pairs={{0,8},{8,16},{16,24},{24,28},{28,20},{20,12},{12,4},{4,0},{1,9},{9... | collective-permute-start | bytes 1179656 | tf_op jit(solution)/shard_map/ppermute | solution.py:439
  10.7 0.4 collective-permute-start.4
  11.1 1.4 %copy-done = bf16[3,1024,256]{2,1,0:T(8,128)(2,1)S(1)} copy-done((bf16[3,1024,256]{2,1,0:T(8,128)(2,1)S(1)}, bf16[3,1024,256]{2,1,0:T(8,128)(2,1)}, u32[]{:S(2)}) %copy-start) | copy-done | bytes 1572888
  12.5 0.5 project.1
  13.0 0.0 copy-start.4
  13.0 0.6 copy-done.4
  13.6 0.0 collective-permute-start.5
  13.6 0.6 collective-permute-start.6
  14.3 1.2 %collective-permute-start.7 = (f32[64,64]{1,0:T(8,128)S(1)}, f32[64,64]{1,0:T(8,128)S(1)}, u32[]{:S(2)}, u32[]{:S(2)}) collective-permute-start(f32[64,64]{1,0:T(8,128)S(1)} %get-tuple-element.28), channel_id=1, source_target_pairs={{0,3},{1,2},{2,1},{3,0},{4,7},{5,6},{6,5},{7,4},{8,11},{9,10},{10,... | collective-permute-start | bytes 49160 | tf_op jit(solution)/shard_map/ppermute | solution.py:356
  15.5 0.0 collective-permute-done.5.refs_22_
  15.5 2.3 %collective-permute-done.6.refs_23_ = f32[64,64]{1,0:T(8,128)S(1)} collective-permute-done((f32[64,64]{1,0:T(8,128)S(1)}, f32[64,64]{1,0:T(8,128)S(1)}, u32[]{:S(2)}, u32[]{:S(2)}) %collective-permute-start.6) | collective-permute-done | bytes 16416 | tf_op jit(solution)/shard_map/ppermute | solution.py:356
  17.8 0.1 collective-permute-done.7.refs_24_
  17.9 1.7 %collective-permute-done.3.refs_1_ = bf16[2,3,256,128]{3,2,1,0:T(8,128)(2,1)S(1)} collective-permute-done((bf16[2,3,256,128]{3,2,1,0:T(8,128)(2,1)S(1)}, bf16[2,3,256,128]{3,2,1,0:T(8,128)(2,1)S(1)}, u32[]{:S(2)}, u32[]{:S(2)}) %collective-permute-start.3) | collective-permute-done | bytes 393248 | tf_op jit(solution)/shard_map/ppermute | solution.py:439
  19.6 1.3 %collective-permute-done.4.refs_2_ = bf16[2,3,256,128]{3,2,1,0:T(8,128)(2,1)S(1)} collective-permute-done((bf16[2,3,256,128]{3,2,1,0:T(8,128)(2,1)S(1)}, bf16[2,3,256,128]{3,2,1,0:T(8,128)(2,1)S(1)}, u32[]{:S(2)}, u32[]{:S(2)}) %collective-permute-start.4) | collective-permute-done | bytes 393248 | tf_op jit(solution)/shard_map/ppermute | solution.py:439
  20.9 0.4 collective-permute-start.9
  21.4 1.6 %collective-permute-start.8 = (bf16[2,3,256,128]{3,2,1,0:T(8,128)(2,1)S(1)}, bf16[2,3,256,128]{3,2,1,0:T(8,128)(2,1)S(1)}, u32[]{:S(2)}, u32[]{:S(2)}) collective-permute-start(bf16[2,3,256,128]{3,2,1,0:T(8,128)(2,1)S(1)} %collective-permute-done.3.refs_1_), channel_id=1, source_target_pairs={{0,8},{8,16},{16,24},{24,28},{28,20},{20,12},{12,4},{4,0},{1,9},{9... | collective-permute-start | bytes 1179656 | tf_op jit(solution)/shard_map/ppermute | solution.py:439
  23.0 0.2 cut_columns.4.refs_0_
  23.2 2.6 %collective-permute-start.12 = (bf16[3,3,64,512]{3,2,1,0:T(8,128)(2,1)S(1)}, bf16[3,3,64,512]{3,2,1,0:T(8,128)(2,1)S(1)}, u32[]{:S(2)}, u32[]{:S(2)}) collective-permute-start(bf16[3,3,64,512]{3,2,1,0:T(8,128)(2,1)S(1)} %cut_columns.4.refs_0_), channel_id=1, source_target_pairs={{0,2},{4,6},{9,11},{13,15},{18,16},{22,20},{27,25},{31,29}} | collective-permute-start | bytes 1769480 | tf_op jit(solution)/shard_map/ppermute | solution.py:418
  25.9 0.0 copy-done.2
  25.9 4.4 %collective-permute-done.9.refs_1_.refs_4_ = bf16[2,3,256,128]{3,2,1,0:T(8,128)(2,1)S(1)} collective-permute-done((bf16[2,3,256,128]{3,2,1,0:T(8,128)(2,1)S(1)}, bf16[2,3,256,128]{3,2,1,0:T(8,128)(2,1)S(1)}, u32[]{:S(2)}, u32[]{:S(2)}) %collective-permute-start.9) | collective-permute-done | bytes 393248 | tf_op jit(solution)/shard_map/ppermute | solution.py:439
  30.3 0.7 %collective-permute-start.11 = (bf16[2,3,256,128]{3,2,1,0:T(8,128)(2,1)S(1)}, bf16[2,3,256,128]{3,2,1,0:T(8,128)(2,1)S(1)}, u32[]{:S(2)}, u32[]{:S(2)}) collective-permute-start(bf16[2,3,256,128]{3,2,1,0:T(8,128)(2,1)S(1)} %collective-permute-done.9.refs_1_.refs_4_), channel_id=1, source_target_pairs={{8,0},{16,8},{24,16},{28,24},{20,28},{12,20},{4,12},{0,4},{9,1},{1... | collective-permute-start | bytes 1179656 | tf_op jit(solution)/shard_map/ppermute | solution.py:439
  31.0 0.0 copy-done.5
  31.0 0.0 copy-done.6
  31.0 0.0 copy-done.7
  31.0 0.0 collective-permute-done.8.refs_0_.refs_3_
  31.0 1.4 %collective-permute-start.10 = (bf16[2,3,256,128]{3,2,1,0:T(8,128)(2,1)S(1)}, bf16[2,3,256,128]{3,2,1,0:T(8,128)(2,1)S(1)}, u32[]{:S(2)}, u32[]{:S(2)}) collective-permute-start(bf16[2,3,256,128]{3,2,1,0:T(8,128)(2,1)S(1)} %collective-permute-done.8.refs_0_.refs_3_), channel_id=1, source_target_pairs={{0,8},{8,16},{16,24},{24,28},{28,20},{20,12},{12,4},{4,0},{1,9},{9... | collective-permute-start | bytes 1179656 | tf_op jit(solution)/shard_map/ppermute | solution.py:439
  32.4 0.8 %collective-permute-done.12.refs_1_ = bf16[3,3,64,512]{3,2,1,0:T(8,128)(2,1)S(1)} collective-permute-done((bf16[3,3,64,512]{3,2,1,0:T(8,128)(2,1)S(1)}, bf16[3,3,64,512]{3,2,1,0:T(8,128)(2,1)S(1)}, u32[]{:S(2)}, u32[]{:S(2)}) %collective-permute-start.12) | collective-permute-done | bytes 589856 | tf_op jit(solution)/shard_map/ppermute | solution.py:418
  33.3 0.1 collective-permute-start.15
  33.4 0.2 cut_columns.6.refs_0_
  33.5 4.4 %collective-permute-start.16 = (bf16[2,3,64,512]{3,2,1,0:T(8,128)(2,1)S(1)}, bf16[2,3,64,512]{3,2,1,0:T(8,128)(2,1)S(1)}, u32[]{:S(2)}, u32[]{:S(2)}) collective-permute-start(bf16[2,3,64,512]{3,2,1,0:T(8,128)(2,1)S(1)} %cut_columns.6.refs_0_), channel_id=1, source_target_pairs={{0,2},{4,6},{9,11},{13,15},{18,16},{22,20},{27,25},{31,29}} | collective-permute-start | bytes 1179656 | tf_op jit(solution)/shard_map/ppermute | solution.py:418
  38.0 0.8 %collective-permute-done.11.down_ref.refs_6_ = bf16[2,3,256,128]{3,2,1,0:T(8,128)(2,1)S(1)} collective-permute-done((bf16[2,3,256,128]{3,2,1,0:T(8,128)(2,1)S(1)}, bf16[2,3,256,128]{3,2,1,0:T(8,128)(2,1)S(1)}, u32[]{:S(2)}, u32[]{:S(2)}) %collective-permute-start.11) | collective-permute-done | bytes 393248 | tf_op jit(solution)/shard_map/ppermute | solution.py:439
  38.7 0.7 %collective-permute-done.10.up_ref.refs_5_ = bf16[2,3,256,128]{3,2,1,0:T(8,128)(2,1)S(1)} collective-permute-done((bf16[2,3,256,128]{3,2,1,0:T(8,128)(2,1)S(1)}, bf16[2,3,256,128]{3,2,1,0:T(8,128)(2,1)S(1)}, u32[]{:S(2)}, u32[]{:S(2)}) %collective-permute-start.10) | collective-permute-done | bytes 393248 | tf_op jit(solution)/shard_map/ppermute | solution.py:439
  39.4 0.2 cut_columns.5
  39.6 0.1 collective-permute-start.18
  39.7 1.2 %collective-permute-start.13 = (bf16[3,256,128]{2,1,0:T(8,128)(2,1)S(1)}, bf16[3,256,128]{2,1,0:T(8,128)(2,1)S(1)}, u32[]{:S(2)}, u32[]{:S(2)}) collective-permute-start(bf16[3,256,128]{2,1,0:T(8,128)(2,1)S(1)} %get-tuple-element.31), channel_id=1, source_target_pairs={{0,8},{8,16},{16,24},{24,28},{28,20},{20,12},{12,4},{4,0},{1,9},{9... | collective-permute-start | bytes 589832 | tf_op jit(solution)/shard_map/ppermute | solution.py:439
  40.9 0.9 %collective-permute-start.14 = (bf16[3,256,128]{2,1,0:T(8,128)(2,1)S(1)}, bf16[3,256,128]{2,1,0:T(8,128)(2,1)S(1)}, u32[]{:S(2)}, u32[]{:S(2)}) collective-permute-start(bf16[3,256,128]{2,1,0:T(8,128)(2,1)S(1)} %get-tuple-element.32), channel_id=1, source_target_pairs={{8,0},{16,8},{24,16},{28,24},{20,28},{12,20},{4,12},{0,4},{9,1},{1... | collective-permute-start | bytes 589832 | tf_op jit(solution)/shard_map/ppermute | solution.py:439
  41.8 1.4 %collective-permute-done.16.refs_1_ = bf16[2,3,64,512]{3,2,1,0:T(8,128)(2,1)S(1)} collective-permute-done((bf16[2,3,64,512]{3,2,1,0:T(8,128)(2,1)S(1)}, bf16[2,3,64,512]{3,2,1,0:T(8,128)(2,1)S(1)}, u32[]{:S(2)}, u32[]{:S(2)}) %collective-permute-start.16) | collective-permute-done | bytes 393248 | tf_op jit(solution)/shard_map/ppermute | solution.py:418
  43.2 0.0 collective-permute-done.18.beside_ref.refs_14_
  43.3 2.5 %collective-permute-start.19 = (bf16[2,3,64,256]{3,2,1,0:T(8,128)(2,1)S(1)}, bf16[2,3,64,256]{3,2,1,0:T(8,128)(2,1)S(1)}, u32[]{:S(2)}, u32[]{:S(2)}) collective-permute-start(bf16[2,3,64,256]{3,2,1,0:T(8,128)(2,1)S(1)} %pick_half.2), channel_id=1, source_target_pairs={{0,2},{1,3},{2,0},{3,1},{4,6},{5,7},{6,4},{7,5},{8,10},{9,11},{10,... | collective-permute-start | bytes 589832 | tf_op jit(solution)/shard_map/ppermute | solution.py:356
  45.8 0.0 collective-permute-done.15.refs_10_
  45.8 1.2 %collective-permute-done.13.up_half.refs_7_ = bf16[3,256,128]{2,1,0:T(8,128)(2,1)S(1)} collective-permute-done((bf16[3,256,128]{2,1,0:T(8,128)(2,1)S(1)}, bf16[3,256,128]{2,1,0:T(8,128)(2,1)S(1)}, u32[]{:S(2)}, u32[]{:S(2)}) %collective-permute-start.13) | collective-permute-done | bytes 196640 | tf_op jit(solution)/shard_map/ppermute | solution.py:439
  47.0 0.8 %collective-permute-done.14.down_half.refs_8_ = bf16[3,256,128]{2,1,0:T(8,128)(2,1)S(1)} collective-permute-done((bf16[3,256,128]{2,1,0:T(8,128)(2,1)S(1)}, bf16[3,256,128]{2,1,0:T(8,128)(2,1)S(1)}, u32[]{:S(2)}, u32[]{:S(2)}) %collective-permute-start.14) | collective-permute-done | bytes 196640 | tf_op jit(solution)/shard_map/ppermute | solution.py:439
  47.8 0.1 cut_columns.7.own_ref.refs_17_
  48.0 0.1 collective-permute-start.21
  48.1 0.5 collective-permute-start.17
  48.6 0.9 %collective-permute-done.19.refs_15_ = bf16[2,3,64,256]{3,2,1,0:T(8,128)(2,1)S(1)} collective-permute-done((bf16[2,3,64,256]{3,2,1,0:T(8,128)(2,1)S(1)}, bf16[2,3,64,256]{3,2,1,0:T(8,128)(2,1)S(1)}, u32[]{:S(2)}, u32[]{:S(2)}) %collective-permute-start.19) | collective-permute-done | bytes 196640 | tf_op jit(solution)/shard_map/ppermute | solution.py:356
  49.5 0.0 collective-permute-start.20
  49.5 0.0 collective-permute-done.21.beside_ref.refs_18_
  49.5 2.1 %collective-permute-start.22 = (bf16[1,3,64,256]{3,2,1,0:T(8,128)(2,1)S(1)}, bf16[1,3,64,256]{3,2,1,0:T(8,128)(2,1)S(1)}, u32[]{:S(2)}, u32[]{:S(2)}) collective-permute-start(bf16[1,3,64,256]{3,2,1,0:T(8,128)(2,1)S(1)} %pick_half.3), channel_id=1, source_target_pairs={{0,2},{1,3},{2,0},{3,1},{4,6},{5,7},{6,4},{7,5},{8,10},{9,11},{10,... | collective-permute-start | bytes 294920 | tf_op jit(solution)/shard_map/ppermute | solution.py:356
  51.6 3.5 %collective-permute-done.22.refs_19_ = bf16[1,3,64,256]{3,2,1,0:T(8,128)(2,1)S(1)} collective-permute-done((bf16[1,3,64,256]{3,2,1,0:T(8,128)(2,1)S(1)}, bf16[1,3,64,256]{3,2,1,0:T(8,128)(2,1)S(1)}, u32[]{:S(2)}, u32[]{:S(2)}) %collective-permute-start.22) | collective-permute-done | bytes 98336 | tf_op jit(solution)/shard_map/ppermute | solution.py:356
  55.0 0.0 collective-permute-start.23
  55.0 0.0 collective-permute-done.17.refs_12_
  55.1 0.0 collective-permute-done.20.refs_16_
  55.1 1.3 %collective-permute-done.23.refs_20_ = bf16[1,3,64,256]{3,2,1,0:T(8,128)(2,1)S(1)} collective-permute-done((bf16[1,3,64,256]{3,2,1,0:T(8,128)(2,1)S(1)}, bf16[1,3,64,256]{3,2,1,0:T(8,128)(2,1)S(1)}, u32[]{:S(2)}, u32[]{:S(2)}) %collective-permute-start.23) | collective-permute-done | bytes 98336 | tf_op jit(solution)/shard_map/ppermute | solution.py:356
  56.4 1.0 %copy-done.3 = bf16[2,3,256,128]{3,2,1,0:T(8,128)(2,1)S(1)} copy-done((bf16[2,3,256,128]{3,2,1,0:T(8,128)(2,1)S(1)}, bf16[2,3,256,128]{3,2,1,0:T(8,128)(2,1)}, u32[]{:S(2)}) %copy-start.3) | copy-done | bytes 393240
  57.3 8.6 %covariance_tile.1 = (f32[3,3,1024,512]{3,2,1,0:T(8,128)}, f32[64,64]{1,0:T(8,128)}) custom-call(s32[1]{0:T(128)} %bitcast.role_ref, bf16[2,3,256,128]{3,2,1,0:T(8,128)(2,1)S(1)} %get-tuple-element.23.refs_0_, bf16[2,3,256,128]{3,2,1,0:T(8,128)(2,1)S(1)} %collective-permute-done.3.refs_1_, bf16[2,3,256,128]{3,2,1,0:T(8,128)(2,1)S(1)} %copy-done.3, ...), custom_call_target="tpu_custom_call" | custom-call | flops 4831838208 | bytes 25165824 | tf_op jit(solution)/shard_map/covariance_tile/pallas_call | solution.py:465
  (12 shorter events, 0.1 us)
Async XLA Ops:
  2.3 3.8 %collective-permute-start.2 = (f32[24,64]{1,0:T(8,128)S(1)}, f32[24,64]{1,0:T(8,128)S(1)}, u32[]{:S(2)}, u32[]{:S(2)}) collective-permute-start(f32[24,64]{1,0:T(8,128)S(1)} %get-tuple-element.20.refs_0_), channel_id=1, source_target_pairs={{0,3},{1,2},{2,1},{3,0},{4,7},{5,6},{6,5},{7,4},{8,11},{9,10},{10,... | collective-permute-start | bytes 18440 | tf_op jit(solution)/shard_map/ppermute | solution.py:356
  4.7 3.7 %collective-permute-start.1 = (f32[24,64]{1,0:T(8,128)S(1)}, f32[24,64]{1,0:T(8,128)S(1)}, u32[]{:S(2)}, u32[]{:S(2)}) collective-permute-start(f32[24,64]{1,0:T(8,128)S(1)} %get-tuple-element.20.refs_0_), channel_id=1, source_target_pairs={{0,2},{1,3},{2,0},{3,1},{4,6},{5,7},{6,4},{7,5},{8,10},{9,11},{10,... | collective-permute-start | bytes 18440 | tf_op jit(solution)/shard_map/ppermute | solution.py:356
  5.4 3.1 %collective-permute-start = (f32[24,64]{1,0:T(8,128)S(1)}, f32[24,64]{1,0:T(8,128)S(1)}, u32[]{:S(2)}, u32[]{:S(2)}) collective-permute-start(f32[24,64]{1,0:T(8,128)S(1)} %get-tuple-element.20.refs_0_), channel_id=1, source_target_pairs={{0,1},{1,0},{2,3},{3,2},{4,5},{5,4},{6,7},{7,6},{8,9},{9,8},{10,11... | collective-permute-start | bytes 18440 | tf_op jit(solution)/shard_map/ppermute | solution.py:356
  9.0 10.6 %collective-permute-start.3 = (bf16[2,3,256,128]{3,2,1,0:T(8,128)(2,1)S(1)}, bf16[2,3,256,128]{3,2,1,0:T(8,128)(2,1)S(1)}, u32[]{:S(2)}, u32[]{:S(2)}) collective-permute-start(bf16[2,3,256,128]{3,2,1,0:T(8,128)(2,1)S(1)} %get-tuple-element.23.refs_0_), channel_id=1, source_target_pairs={{0,8},{8,16},{16,24},{24,28},{28,20},{20,12},{12,4},{4,0},{1,9},{9... | collective-permute-start | bytes 1179656 | tf_op jit(solution)/shard_map/ppermute | solution.py:439
  10.7 10.3 %collective-permute-start.4 = (bf16[2,3,256,128]{3,2,1,0:T(8,128)(2,1)S(1)}, bf16[2,3,256,128]{3,2,1,0:T(8,128)(2,1)S(1)}, u32[]{:S(2)}, u32[]{:S(2)}) collective-permute-start(bf16[2,3,256,128]{3,2,1,0:T(8,128)(2,1)S(1)} %get-tuple-element.23.refs_0_), channel_id=1, source_target_pairs={{8,0},{16,8},{24,16},{28,24},{20,28},{12,20},{4,12},{0,4},{9,1},{1... | collective-permute-start | bytes 1179656 | tf_op jit(solution)/shard_map/ppermute | solution.py:439
  11.1 1.4 %copy-start = (bf16[3,1024,256]{2,1,0:T(8,128)(2,1)S(1)}, bf16[3,1024,256]{2,1,0:T(8,128)(2,1)}, u32[]{:S(2)}) copy-start(bf16[3,1024,256]{2,1,0:T(8,128)(2,1)} %eig_ref.1) | copy-start | bytes 4718596
  13.0 0.6 copy-start.4
  13.6 1.9 %collective-permute-start.5 = (f32[64,64]{1,0:T(8,128)S(1)}, f32[64,64]{1,0:T(8,128)S(1)}, u32[]{:S(2)}, u32[]{:S(2)}) collective-permute-start(f32[64,64]{1,0:T(8,128)S(1)} %get-tuple-element.26), channel_id=1, source_target_pairs={{0,1},{1,0},{2,3},{3,2},{4,5},{5,4},{6,7},{7,6},{8,9},{9,8},{10,11... | collective-permute-start | bytes 49160 | tf_op jit(solution)/shard_map/ppermute | solution.py:356
  13.6 4.2 %collective-permute-start.6 = (f32[64,64]{1,0:T(8,128)S(1)}, f32[64,64]{1,0:T(8,128)S(1)}, u32[]{:S(2)}, u32[]{:S(2)}) collective-permute-start(f32[64,64]{1,0:T(8,128)S(1)} %get-tuple-element.27), channel_id=1, source_target_pairs={{0,2},{1,3},{2,0},{3,1},{4,6},{5,7},{6,4},{7,5},{8,10},{9,11},{10,... | collective-permute-start | bytes 49160 | tf_op jit(solution)/shard_map/ppermute | solution.py:356
  14.3 3.7 %collective-permute-start.7 = (f32[64,64]{1,0:T(8,128)S(1)}, f32[64,64]{1,0:T(8,128)S(1)}, u32[]{:S(2)}, u32[]{:S(2)}) collective-permute-start(f32[64,64]{1,0:T(8,128)S(1)} %get-tuple-element.28), channel_id=1, source_target_pairs={{0,3},{1,2},{2,1},{3,0},{4,7},{5,6},{6,5},{7,4},{8,11},{9,10},{10,... | collective-permute-start | bytes 49160 | tf_op jit(solution)/shard_map/ppermute | solution.py:356
  15.5 15.5 %copy-start.5 = (f32[64,64]{1,0:T(8,128)}, f32[64,64]{1,0:T(8,128)S(1)}, u32[]{:S(2)}) copy-start(f32[64,64]{1,0:T(8,128)S(1)} %collective-permute-done.5.refs_22_) | copy-start | bytes 49156
  17.8 13.2 %copy-start.6 = (f32[64,64]{1,0:T(8,128)}, f32[64,64]{1,0:T(8,128)S(1)}, u32[]{:S(2)}) copy-start(f32[64,64]{1,0:T(8,128)S(1)} %collective-permute-done.6.refs_23_) | copy-start | bytes 49156
  17.9 13.0 %copy-start.7 = (f32[64,64]{1,0:T(8,128)}, f32[64,64]{1,0:T(8,128)S(1)}, u32[]{:S(2)}) copy-start(f32[64,64]{1,0:T(8,128)S(1)} %collective-permute-done.7.refs_24_) | copy-start | bytes 49156
  20.9 4.9 %copy-start.2 = (bf16[2,3,256,128]{3,2,1,0:T(8,128)(2,1)}, bf16[2,3,256,128]{3,2,1,0:T(8,128)(2,1)S(1)}, u32[]{:S(2)}) copy-start(bf16[2,3,256,128]{3,2,1,0:T(8,128)(2,1)S(1)} %collective-permute-done.4.refs_2_) | copy-start | bytes 1179652
  20.9 9.3 %collective-permute-start.9 = (bf16[2,3,256,128]{3,2,1,0:T(8,128)(2,1)S(1)}, bf16[2,3,256,128]{3,2,1,0:T(8,128)(2,1)S(1)}, u32[]{:S(2)}, u32[]{:S(2)}) collective-permute-start(bf16[2,3,256,128]{3,2,1,0:T(8,128)(2,1)S(1)} %collective-permute-done.4.refs_2_), channel_id=1, source_target_pairs={{8,0},{16,8},{24,16},{28,24},{20,28},{12,20},{4,12},{0,4},{9,1},{1... | collective-permute-start | bytes 1179656 | tf_op jit(solution)/shard_map/ppermute | solution.py:439
  21.4 9.6 %collective-permute-start.8 = (bf16[2,3,256,128]{3,2,1,0:T(8,128)(2,1)S(1)}, bf16[2,3,256,128]{3,2,1,0:T(8,128)(2,1)S(1)}, u32[]{:S(2)}, u32[]{:S(2)}) collective-permute-start(bf16[2,3,256,128]{3,2,1,0:T(8,128)(2,1)S(1)} %collective-permute-done.3.refs_1_), channel_id=1, source_target_pairs={{0,8},{8,16},{16,24},{24,28},{28,20},{20,12},{12,4},{4,0},{1,9},{9... | collective-permute-start | bytes 1179656 | tf_op jit(solution)/shard_map/ppermute | solution.py:439
  23.2 10.0 %collective-permute-start.12 = (bf16[3,3,64,512]{3,2,1,0:T(8,128)(2,1)S(1)}, bf16[3,3,64,512]{3,2,1,0:T(8,128)(2,1)S(1)}, u32[]{:S(2)}, u32[]{:S(2)}) collective-permute-start(bf16[3,3,64,512]{3,2,1,0:T(8,128)(2,1)S(1)} %cut_columns.4.refs_0_), channel_id=1, source_target_pairs={{0,2},{4,6},{9,11},{13,15},{18,16},{22,20},{27,25},{31,29}} | collective-permute-start | bytes 1769480 | tf_op jit(solution)/shard_map/ppermute | solution.py:418
  30.3 8.4 %collective-permute-start.11 = (bf16[2,3,256,128]{3,2,1,0:T(8,128)(2,1)S(1)}, bf16[2,3,256,128]{3,2,1,0:T(8,128)(2,1)S(1)}, u32[]{:S(2)}, u32[]{:S(2)}) collective-permute-start(bf16[2,3,256,128]{3,2,1,0:T(8,128)(2,1)S(1)} %collective-permute-done.9.refs_1_.refs_4_), channel_id=1, source_target_pairs={{8,0},{16,8},{24,16},{28,24},{20,28},{12,20},{4,12},{0,4},{9,1},{1... | collective-permute-start | bytes 1179656 | tf_op jit(solution)/shard_map/ppermute | solution.py:439
  31.0 8.4 %collective-permute-start.10 = (bf16[2,3,256,128]{3,2,1,0:T(8,128)(2,1)S(1)}, bf16[2,3,256,128]{3,2,1,0:T(8,128)(2,1)S(1)}, u32[]{:S(2)}, u32[]{:S(2)}) collective-permute-start(bf16[2,3,256,128]{3,2,1,0:T(8,128)(2,1)S(1)} %collective-permute-done.8.refs_0_.refs_3_), channel_id=1, source_target_pairs={{0,8},{8,16},{16,24},{24,28},{28,20},{20,12},{12,4},{4,0},{1,9},{9... | collective-permute-start | bytes 1179656 | tf_op jit(solution)/shard_map/ppermute | solution.py:439
  33.3 23.1 %copy-start.1 = (bf16[3,3,64,512]{3,2,1,0:T(8,128)(2,1)}, bf16[3,3,64,512]{3,2,1,0:T(8,128)(2,1)S(1)}, u32[]{:S(2)}) copy-start(bf16[3,3,64,512]{3,2,1,0:T(8,128)(2,1)S(1)} %pass_on.2.refs_9_) | copy-start | bytes 1769476
  33.3 12.6 %collective-permute-start.15 = (bf16[3,3,64,512]{3,2,1,0:T(8,128)(2,1)S(1)}, bf16[3,3,64,512]{3,2,1,0:T(8,128)(2,1)S(1)}, u32[]{:S(2)}, u32[]{:S(2)}) collective-permute-start(bf16[3,3,64,512]{3,2,1,0:T(8,128)(2,1)S(1)} %pass_on.2.refs_9_), channel_id=1, source_target_pairs={{0,1},{1,0},{2,3},{3,2},{4,5},{5,4},{6,7},{7,6},{8,9},{9,8},{10,11... | collective-permute-start | bytes 1769480 | tf_op jit(solution)/shard_map/ppermute | solution.py:356
  33.5 9.7 %collective-permute-start.16 = (bf16[2,3,64,512]{3,2,1,0:T(8,128)(2,1)S(1)}, bf16[2,3,64,512]{3,2,1,0:T(8,128)(2,1)S(1)}, u32[]{:S(2)}, u32[]{:S(2)}) collective-permute-start(bf16[2,3,64,512]{3,2,1,0:T(8,128)(2,1)S(1)} %cut_columns.6.refs_0_), channel_id=1, source_target_pairs={{0,2},{4,6},{9,11},{13,15},{18,16},{22,20},{27,25},{31,29}} | collective-permute-start | bytes 1179656 | tf_op jit(solution)/shard_map/ppermute | solution.py:418
  39.6 3.6 %collective-permute-start.18 = (bf16[2,3,64,512]{3,2,1,0:T(8,128)(2,1)S(1)}, bf16[2,3,64,512]{3,2,1,0:T(8,128)(2,1)S(1)}, u32[]{:S(2)}, u32[]{:S(2)}) collective-permute-start(bf16[2,3,64,512]{3,2,1,0:T(8,128)(2,1)S(1)} %get-tuple-element.33.own_ref.refs_13_), channel_id=1, source_target_pairs={{0,1},{1,0},{2,3},{3,2},{4,5},{5,4},{6,7},{7,6},{8,9},{9,8},{10,11... | collective-permute-start | bytes 1179656 | tf_op jit(solution)/shard_map/ppermute | solution.py:356
  39.7 7.3 %collective-permute-start.13 = (bf16[3,256,128]{2,1,0:T(8,128)(2,1)S(1)}, bf16[3,256,128]{2,1,0:T(8,128)(2,1)S(1)}, u32[]{:S(2)}, u32[]{:S(2)}) collective-permute-start(bf16[3,256,128]{2,1,0:T(8,128)(2,1)S(1)} %get-tuple-element.31), channel_id=1, source_target_pairs={{0,8},{8,16},{16,24},{24,28},{28,20},{20,12},{12,4},{4,0},{1,9},{9... | collective-permute-start | bytes 589832 | tf_op jit(solution)/shard_map/ppermute | solution.py:439
  40.9 7.0 %collective-permute-start.14 = (bf16[3,256,128]{2,1,0:T(8,128)(2,1)S(1)}, bf16[3,256,128]{2,1,0:T(8,128)(2,1)S(1)}, u32[]{:S(2)}, u32[]{:S(2)}) collective-permute-start(bf16[3,256,128]{2,1,0:T(8,128)(2,1)S(1)} %get-tuple-element.32), channel_id=1, source_target_pairs={{8,0},{16,8},{24,16},{28,24},{20,28},{12,20},{4,12},{0,4},{9,1},{1... | collective-permute-start | bytes 589832 | tf_op jit(solution)/shard_map/ppermute | solution.py:439
  43.3 6.2 %collective-permute-start.19 = (bf16[2,3,64,256]{3,2,1,0:T(8,128)(2,1)S(1)}, bf16[2,3,64,256]{3,2,1,0:T(8,128)(2,1)S(1)}, u32[]{:S(2)}, u32[]{:S(2)}) collective-permute-start(bf16[2,3,64,256]{3,2,1,0:T(8,128)(2,1)S(1)} %pick_half.2), channel_id=1, source_target_pairs={{0,2},{1,3},{2,0},{3,1},{4,6},{5,7},{6,4},{7,5},{8,10},{9,11},{10,... | collective-permute-start | bytes 589832 | tf_op jit(solution)/shard_map/ppermute | solution.py:356
  48.0 1.5 %collective-permute-start.21 = (bf16[1,3,64,512]{3,2,1,0:T(8,128)(2,1)S(1)}, bf16[1,3,64,512]{3,2,1,0:T(8,128)(2,1)S(1)}, u32[]{:S(2)}, u32[]{:S(2)}) collective-permute-start(bf16[1,3,64,512]{3,2,1,0:T(8,128)(2,1)S(1)} %cut_columns.7.own_ref.refs_17_), channel_id=1, source_target_pairs={{0,1},{1,0},{2,3},{3,2},{4,5},{5,4},{6,7},{7,6},{8,9},{9,8},{10,11... | collective-permute-start | bytes 589832 | tf_op jit(solution)/shard_map/ppermute | solution.py:356
  48.1 7.0 %collective-permute-start.17 = (bf16[2,3,64,512]{3,2,1,0:T(8,128)(2,1)S(1)}, bf16[2,3,64,512]{3,2,1,0:T(8,128)(2,1)S(1)}, u32[]{:S(2)}, u32[]{:S(2)}) collective-permute-start(bf16[2,3,64,512]{3,2,1,0:T(8,128)(2,1)S(1)} %pass_on.3.refs_11_), channel_id=1, source_target_pairs={{0,1},{1,0},{2,3},{3,2},{4,5},{5,4},{6,7},{7,6},{8,9},{9,8},{10,11... | collective-permute-start | bytes 1179656 | tf_op jit(solution)/shard_map/ppermute | solution.py:356
  49.5 5.6 %collective-permute-start.20 = (bf16[2,3,64,256]{3,2,1,0:T(8,128)(2,1)S(1)}, bf16[2,3,64,256]{3,2,1,0:T(8,128)(2,1)S(1)}, u32[]{:S(2)}, u32[]{:S(2)}) collective-permute-start(bf16[2,3,64,256]{3,2,1,0:T(8,128)(2,1)S(1)} %collective-permute-done.19.refs_15_), channel_id=1, source_target_pairs={{0,1},{1,0},{2,3},{3,2},{4,5},{5,4},{6,7},{7,6},{8,9},{9,8},{10,11... | collective-permute-start | bytes 589832 | tf_op jit(solution)/shard_map/ppermute | solution.py:356
  49.5 5.5 %collective-permute-start.22 = (bf16[1,3,64,256]{3,2,1,0:T(8,128)(2,1)S(1)}, bf16[1,3,64,256]{3,2,1,0:T(8,128)(2,1)S(1)}, u32[]{:S(2)}, u32[]{:S(2)}) collective-permute-start(bf16[1,3,64,256]{3,2,1,0:T(8,128)(2,1)S(1)} %pick_half.3), channel_id=1, source_target_pairs={{0,2},{1,3},{2,0},{3,1},{4,6},{5,7},{6,4},{7,5},{8,10},{9,11},{10,... | collective-permute-start | bytes 294920 | tf_op jit(solution)/shard_map/ppermute | solution.py:356
  55.0 1.3 %collective-permute-start.23 = (bf16[1,3,64,256]{3,2,1,0:T(8,128)(2,1)S(1)}, bf16[1,3,64,256]{3,2,1,0:T(8,128)(2,1)S(1)}, u32[]{:S(2)}, u32[]{:S(2)}) collective-permute-start(bf16[1,3,64,256]{3,2,1,0:T(8,128)(2,1)S(1)} %collective-permute-done.22.refs_19_), channel_id=1, source_target_pairs={{0,1},{1,0},{2,3},{3,2},{4,5},{5,4},{6,7},{7,6},{8,9},{9,8},{10,11... | collective-permute-start | bytes 294920 | tf_op jit(solution)/shard_map/ppermute | solution.py:356
  56.4 1.0 %copy-start.3 = (bf16[2,3,256,128]{3,2,1,0:T(8,128)(2,1)S(1)}, bf16[2,3,256,128]{3,2,1,0:T(8,128)(2,1)}, u32[]{:S(2)}) copy-start(bf16[2,3,256,128]{3,2,1,0:T(8,128)(2,1)} %copy-done.2) | copy-start | bytes 1179652

commit v23 on v22

--- a/solution.py
+++ b/solution.py
@@ -194,7 +194,10 @@
         arrays.append(refs[:count])
         refs = refs[count:]
     shares, refs = refs[:roles], refs[roles:]
-    out_ref, proj_ref, left, right, done, held, col_sem, out_sem, share_sem = refs
+    out_ref, proj_ref, left, right, done, held, kept, col_sem, out_sem, share_sem = refs
+    keep = pltpu.make_async_copy(shards[0], kept, share_sem.at[roles])
+    keep.start()
+    shards = (kept,) + tuple(shards[1:])
     sums = [
         pltpu.make_async_copy(part, held.at[k], share_sem.at[k]) for k, part in enumerate(shares)
     ]
@@ -266,6 +269,7 @@
 
     for_each_group(True, start)
     for_each_group(False, load)
+    keep.wait()
     assemble(0, 0)
     for_each_group(True, wait)
     def write(c, at, d):
@@ -467,8 +471,8 @@
             covariance_kernel, frame_axis, atom_axis, groups, 1.0 / total_frames
         ),
         out_shape=(jax.ShapeDtypeStruct((3, 3, local_atoms, block), jnp.float32), share),
-        in_specs=[SMEM]
-        + [VMEM] * len(rows)
+        in_specs=[SMEM, HBM]
+        + [VMEM] * (len(rows) - 1)
         + [HBM, VMEM]
         + [VMEM] * len(in_vmem)
         + [HBM] * len(parts),
@@ -478,9 +482,10 @@
             pltpu.VMEM((3, total_frames, block), jnp.bfloat16),
             pltpu.VMEM((2, 3, 2 * run, block), jnp.float32),
             pltpu.VMEM((atom_axis,) + share.shape, jnp.float32),
+            pltpu.VMEM(own.shape, jnp.bfloat16),
             pltpu.SemaphoreType.DMA((2 * frame_axis,)),
             pltpu.SemaphoreType.DMA((2, 3)),
-            pltpu.SemaphoreType.DMA((atom_axis,)),
+            pltpu.SemaphoreType.DMA((atom_axis + 1,)),
         ],
         compiler_params=params(16),
         cost_estimate=pl.CostEstimate(
@@ -491,7 +496,8 @@
         name="covariance_tile",
     )(
         role,
-        *[pinned(value, pltpu.VMEM) for value in rows],
+        pinned(rows[0], pltpu.HBM),
+        *[pinned(value, pltpu.VMEM) for value in rows[1:]],
         pinned(first_group[0], pltpu.HBM),
         pinned(first_group[1], pltpu.VMEM),
         *[pinned(value, pltpu.VMEM) for value in in_vmem],

time: 66.8 us -> 67.2 us (level)
    unnamed x16 -> x18, local copies, waits for them, and re-layouts: 3.02 us -> 3.02 us
where the time goes in v23:
time: 67.2 us; the launch traced here: 66.1 us
  starting transfers between devices  25.6 us (38%)
  waiting for transfers between devices  24.3 us (36%)
  Pallas kernels  12.3 us (18%)
  local copies, waits for them, and re-layouts  3.02 us (4%)
  between operations  0.83 us (1%)
    ppermute x14, waiting for transfers between devices, swap(): lax.ppermute(value, 'atoms', [(a, a ^ distance) for a in range(atom_axis)])  11.2 us
    ppermute x14, starting transfers between devices, swap(): lax.ppermute(value, 'atoms', [(a, a ^ distance) for a in range(atom_axis)])  10.3 us
    pallas_call x1, Pallas kernels, per_device(): pl.pallas_call(functools.partial(covariance_kernel, frame_axis, atom_axis...  8.69 us
    ppermute x4, waiting for transfers between devices, hop(): lax.ppermute(down, 'frames', backward)  7.32 us
    ppermute x2, starting transfers between devices, cross(): return [cut, lax.ppermute(cut, axes, pairs(0, 2))]  7.04 us
    ppermute x4, starting transfers between devices, hop(): lax.ppermute(up, 'frames', forward)  5.78 us
    ppermute x4, waiting for transfers between devices, hop(): lax.ppermute(up, 'frames', forward)  3.55 us
    unnamed x18, local copies, waits for them, and re-layouts  3.02 us
  transfers between devices with their start and end apart: 24, of which 16 were waited for; matrix products, arithmetic and copies ran while one was open for 0% of the time, Pallas kernels for 2%

profile of v23, /device:TPU:0, one launch (start us, length us, event | category | flops | bytes accessed | tf_op | source)
XLA Modules:
  0.0 66.1 jit_solution(3883428750609350698)
XLA Ops:
  0.6 1.7 %local_moments.1 = (f32[24,64]{1,0:T(8,128)S(1)}, f32[3,64,1024]{2,1,0:T(8,128)S(1)}, f32[3,1024]{1,0:T(4,128)S(1)}) custom-call(f32[3,64,1024]{2,1,0:T(8,128)} %bitcast.5, f32[3,1024]{1,0:T(4,128)} %ref_hbm.1), custom_call_target="tpu_custom_call" | custom-call | tf_op jit(solution)/shard_map/local_moments/pallas_call | solution.py:346
  2.3 2.4 %collective-permute-start.2 = (f32[24,64]{1,0:T(8,128)S(1)}, f32[24,64]{1,0:T(8,128)S(1)}, u32[]{:S(2)}, u32[]{:S(2)}) collective-permute-start(f32[24,64]{1,0:T(8,128)S(1)} %get-tuple-element.20.refs_0_), channel_id=1, source_target_pairs={{0,3},{1,2},{2,1},{3,0},{4,7},{5,6},{6,5},{7,4},{8,11},{9,10},{10,... | collective-permute-start | bytes 18440 | tf_op jit(solution)/shard_map/ppermute | solution.py:360
  4.7 0.6 collective-permute-start.1
  5.4 0.0 collective-permute-start
  5.4 0.7 %collective-permute-done.2.refs_3_ = f32[24,64]{1,0:T(8,128)S(1)} collective-permute-done((f32[24,64]{1,0:T(8,128)S(1)}, f32[24,64]{1,0:T(8,128)S(1)}, u32[]{:S(2)}, u32[]{:S(2)}) %collective-permute-start.2) | collective-permute-done | bytes 6176 | tf_op jit(solution)/shard_map/ppermute | solution.py:360
  6.1 2.3 %collective-permute-done.1.refs_2_ = f32[24,64]{1,0:T(8,128)S(1)} collective-permute-done((f32[24,64]{1,0:T(8,128)S(1)}, f32[24,64]{1,0:T(8,128)S(1)}, u32[]{:S(2)}, u32[]{:S(2)}) %collective-permute-start.1) | collective-permute-done | bytes 6176 | tf_op jit(solution)/shard_map/ppermute | solution.py:360
  8.4 0.0 collective-permute-done.refs_1_
  8.4 0.6 polar_align.1
  9.0 0.0 copy-start.2
  9.1 1.6 %collective-permute-start.3 = (bf16[2,3,256,128]{3,2,1,0:T(8,128)(2,1)S(1)}, bf16[2,3,256,128]{3,2,1,0:T(8,128)(2,1)S(1)}, u32[]{:S(2)}, u32[]{:S(2)}) collective-permute-start(bf16[2,3,256,128]{3,2,1,0:T(8,128)(2,1)S(1)} %get-tuple-element.23.refs_0_), channel_id=1, source_target_pairs={{0,8},{8,16},{16,24},{24,28},{28,20},{20,12},{12,4},{4,0},{1,9},{9... | collective-permute-start | bytes 1179656 | tf_op jit(solution)/shard_map/ppermute | solution.py:443
  10.7 0.4 collective-permute-start.4
  11.1 1.4 %copy-done = bf16[3,1024,256]{2,1,0:T(8,128)(2,1)S(1)} copy-done((bf16[3,1024,256]{2,1,0:T(8,128)(2,1)S(1)}, bf16[3,1024,256]{2,1,0:T(8,128)(2,1)}, u32[]{:S(2)}) %copy-start) | copy-done | bytes 1572888
  12.5 0.5 project.1
  13.0 0.0 copy-start.5
  13.0 0.6 copy-done.5
  13.6 0.0 collective-permute-start.5
  13.6 0.6 collective-permute-start.6
  14.3 1.2 %collective-permute-start.7 = (f32[64,64]{1,0:T(8,128)S(1)}, f32[64,64]{1,0:T(8,128)S(1)}, u32[]{:S(2)}, u32[]{:S(2)}) collective-permute-start(f32[64,64]{1,0:T(8,128)S(1)} %get-tuple-element.28), channel_id=1, source_target_pairs={{0,3},{1,2},{2,1},{3,0},{4,7},{5,6},{6,5},{7,4},{8,11},{9,10},{10,... | collective-permute-start | bytes 49160 | tf_op jit(solution)/shard_map/ppermute | solution.py:360
  15.5 0.0 collective-permute-done.5.refs_22_
  15.5 2.3 %collective-permute-done.6.refs_23_ = f32[64,64]{1,0:T(8,128)S(1)} collective-permute-done((f32[64,64]{1,0:T(8,128)S(1)}, f32[64,64]{1,0:T(8,128)S(1)}, u32[]{:S(2)}, u32[]{:S(2)}) %collective-permute-start.6) | collective-permute-done | bytes 16416 | tf_op jit(solution)/shard_map/ppermute | solution.py:360
  17.8 0.1 collective-permute-done.7.refs_24_
  18.0 1.7 %collective-permute-done.3.refs_1_ = bf16[2,3,256,128]{3,2,1,0:T(8,128)(2,1)S(1)} collective-permute-done((bf16[2,3,256,128]{3,2,1,0:T(8,128)(2,1)S(1)}, bf16[2,3,256,128]{3,2,1,0:T(8,128)(2,1)S(1)}, u32[]{:S(2)}, u32[]{:S(2)}) %collective-permute-start.3) | collective-permute-done | bytes 393248 | tf_op jit(solution)/shard_map/ppermute | solution.py:443
  19.7 1.3 %collective-permute-done.4.refs_2_ = bf16[2,3,256,128]{3,2,1,0:T(8,128)(2,1)S(1)} collective-permute-done((bf16[2,3,256,128]{3,2,1,0:T(8,128)(2,1)S(1)}, bf16[2,3,256,128]{3,2,1,0:T(8,128)(2,1)S(1)}, u32[]{:S(2)}, u32[]{:S(2)}) %collective-permute-start.4) | collective-permute-done | bytes 393248 | tf_op jit(solution)/shard_map/ppermute | solution.py:443
  21.0 0.4 collective-permute-start.9
  21.4 1.6 %collective-permute-start.8 = (bf16[2,3,256,128]{3,2,1,0:T(8,128)(2,1)S(1)}, bf16[2,3,256,128]{3,2,1,0:T(8,128)(2,1)S(1)}, u32[]{:S(2)}, u32[]{:S(2)}) collective-permute-start(bf16[2,3,256,128]{3,2,1,0:T(8,128)(2,1)S(1)} %collective-permute-done.3.refs_1_), channel_id=1, source_target_pairs={{0,8},{8,16},{16,24},{24,28},{28,20},{20,12},{12,4},{4,0},{1,9},{9... | collective-permute-start | bytes 1179656 | tf_op jit(solution)/shard_map/ppermute | solution.py:443
  23.0 0.2 cut_columns.4.refs_0_
  23.2 2.6 %collective-permute-start.12 = (bf16[3,3,64,512]{3,2,1,0:T(8,128)(2,1)S(1)}, bf16[3,3,64,512]{3,2,1,0:T(8,128)(2,1)S(1)}, u32[]{:S(2)}, u32[]{:S(2)}) collective-permute-start(bf16[3,3,64,512]{3,2,1,0:T(8,128)(2,1)S(1)} %cut_columns.4.refs_0_), channel_id=1, source_target_pairs={{0,2},{4,6},{9,11},{13,15},{18,16},{22,20},{27,25},{31,29}} | collective-permute-start | bytes 1769480 | tf_op jit(solution)/shard_map/ppermute | solution.py:422
  25.9 4.4 %collective-permute-done.9.refs_1_.refs_4_ = bf16[2,3,256,128]{3,2,1,0:T(8,128)(2,1)S(1)} collective-permute-done((bf16[2,3,256,128]{3,2,1,0:T(8,128)(2,1)S(1)}, bf16[2,3,256,128]{3,2,1,0:T(8,128)(2,1)S(1)}, u32[]{:S(2)}, u32[]{:S(2)}) %collective-permute-start.9) | collective-permute-done | bytes 393248 | tf_op jit(solution)/shard_map/ppermute | solution.py:443
  30.3 0.7 %collective-permute-start.11 = (bf16[2,3,256,128]{3,2,1,0:T(8,128)(2,1)S(1)}, bf16[2,3,256,128]{3,2,1,0:T(8,128)(2,1)S(1)}, u32[]{:S(2)}, u32[]{:S(2)}) collective-permute-start(bf16[2,3,256,128]{3,2,1,0:T(8,128)(2,1)S(1)} %collective-permute-done.9.refs_1_.refs_4_), channel_id=1, source_target_pairs={{8,0},{16,8},{24,16},{28,24},{20,28},{12,20},{4,12},{0,4},{9,1},{1... | collective-permute-start | bytes 1179656 | tf_op jit(solution)/shard_map/ppermute | solution.py:443
  31.0 0.0 copy-done.8
  31.0 0.0 collective-permute-done.8.refs_0_.refs_3_
  31.0 1.4 %collective-permute-start.10 = (bf16[2,3,256,128]{3,2,1,0:T(8,128)(2,1)S(1)}, bf16[2,3,256,128]{3,2,1,0:T(8,128)(2,1)S(1)}, u32[]{:S(2)}, u32[]{:S(2)}) collective-permute-start(bf16[2,3,256,128]{3,2,1,0:T(8,128)(2,1)S(1)} %collective-permute-done.8.refs_0_.refs_3_), channel_id=1, source_target_pairs={{0,8},{8,16},{16,24},{24,28},{28,20},{20,12},{12,4},{4,0},{1,9},{9... | collective-permute-start | bytes 1179656 | tf_op jit(solution)/shard_map/ppermute | solution.py:443
  32.4 0.8 %collective-permute-done.12.refs_1_ = bf16[3,3,64,512]{3,2,1,0:T(8,128)(2,1)S(1)} collective-permute-done((bf16[3,3,64,512]{3,2,1,0:T(8,128)(2,1)S(1)}, bf16[3,3,64,512]{3,2,1,0:T(8,128)(2,1)S(1)}, u32[]{:S(2)}, u32[]{:S(2)}) %collective-permute-start.12) | collective-permute-done | bytes 589856 | tf_op jit(solution)/shard_map/ppermute | solution.py:422
  33.3 0.0 copy-start.1
  33.3 0.1 collective-permute-start.15
  33.4 0.2 cut_columns.6.refs_0_
  33.5 4.4 %collective-permute-start.16 = (bf16[2,3,64,512]{3,2,1,0:T(8,128)(2,1)S(1)}, bf16[2,3,64,512]{3,2,1,0:T(8,128)(2,1)S(1)}, u32[]{:S(2)}, u32[]{:S(2)}) collective-permute-start(bf16[2,3,64,512]{3,2,1,0:T(8,128)(2,1)S(1)} %cut_columns.6.refs_0_), channel_id=1, source_target_pairs={{0,2},{4,6},{9,11},{13,15},{18,16},{22,20},{27,25},{31,29}} | collective-permute-start | bytes 1179656 | tf_op jit(solution)/shard_map/ppermute | solution.py:422
  38.0 0.8 %collective-permute-done.11.down_ref.refs_6_ = bf16[2,3,256,128]{3,2,1,0:T(8,128)(2,1)S(1)} collective-permute-done((bf16[2,3,256,128]{3,2,1,0:T(8,128)(2,1)S(1)}, bf16[2,3,256,128]{3,2,1,0:T(8,128)(2,1)S(1)}, u32[]{:S(2)}, u32[]{:S(2)}) %collective-permute-start.11) | collective-permute-done | bytes 393248 | tf_op jit(solution)/shard_map/ppermute | solution.py:443
  38.7 0.7 %collective-permute-done.10.up_ref.refs_5_ = bf16[2,3,256,128]{3,2,1,0:T(8,128)(2,1)S(1)} collective-permute-done((bf16[2,3,256,128]{3,2,1,0:T(8,128)(2,1)S(1)}, bf16[2,3,256,128]{3,2,1,0:T(8,128)(2,1)S(1)}, u32[]{:S(2)}, u32[]{:S(2)}) %collective-permute-start.10) | collective-permute-done | bytes 393248 | tf_op jit(solution)/shard_map/ppermute | solution.py:443
  39.4 0.2 cut_columns.5
  39.6 0.1 collective-permute-start.18
  39.7 1.2 %collective-permute-start.13 = (bf16[3,256,128]{2,1,0:T(8,128)(2,1)S(1)}, bf16[3,256,128]{2,1,0:T(8,128)(2,1)S(1)}, u32[]{:S(2)}, u32[]{:S(2)}) collective-permute-start(bf16[3,256,128]{2,1,0:T(8,128)(2,1)S(1)} %get-tuple-element.31), channel_id=1, source_target_pairs={{0,8},{8,16},{16,24},{24,28},{28,20},{20,12},{12,4},{4,0},{1,9},{9... | collective-permute-start | bytes 589832 | tf_op jit(solution)/shard_map/ppermute | solution.py:443
  40.9 0.9 %collective-permute-start.14 = (bf16[3,256,128]{2,1,0:T(8,128)(2,1)S(1)}, bf16[3,256,128]{2,1,0:T(8,128)(2,1)S(1)}, u32[]{:S(2)}, u32[]{:S(2)}) collective-permute-start(bf16[3,256,128]{2,1,0:T(8,128)(2,1)S(1)} %get-tuple-element.32), channel_id=1, source_target_pairs={{8,0},{16,8},{24,16},{28,24},{20,28},{12,20},{4,12},{0,4},{9,1},{1... | collective-permute-start | bytes 589832 | tf_op jit(solution)/shard_map/ppermute | solution.py:443
  41.8 1.4 %collective-permute-done.16.refs_1_ = bf16[2,3,64,512]{3,2,1,0:T(8,128)(2,1)S(1)} collective-permute-done((bf16[2,3,64,512]{3,2,1,0:T(8,128)(2,1)S(1)}, bf16[2,3,64,512]{3,2,1,0:T(8,128)(2,1)S(1)}, u32[]{:S(2)}, u32[]{:S(2)}) %collective-permute-start.16) | collective-permute-done | bytes 393248 | tf_op jit(solution)/shard_map/ppermute | solution.py:422
  43.3 0.0 collective-permute-done.18.beside_ref.refs_14_
  43.3 2.5 %collective-permute-start.19 = (bf16[2,3,64,256]{3,2,1,0:T(8,128)(2,1)S(1)}, bf16[2,3,64,256]{3,2,1,0:T(8,128)(2,1)S(1)}, u32[]{:S(2)}, u32[]{:S(2)}) collective-permute-start(bf16[2,3,64,256]{3,2,1,0:T(8,128)(2,1)S(1)} %pick_half.2), channel_id=1, source_target_pairs={{0,2},{1,3},{2,0},{3,1},{4,6},{5,7},{6,4},{7,5},{8,10},{9,11},{10,... | collective-permute-start | bytes 589832 | tf_op jit(solution)/shard_map/ppermute | solution.py:360
  45.8 0.0 collective-permute-done.15.refs_10_
  45.8 1.2 %collective-permute-done.13.up_half.refs_7_ = bf16[3,256,128]{2,1,0:T(8,128)(2,1)S(1)} collective-permute-done((bf16[3,256,128]{2,1,0:T(8,128)(2,1)S(1)}, bf16[3,256,128]{2,1,0:T(8,128)(2,1)S(1)}, u32[]{:S(2)}, u32[]{:S(2)}) %collective-permute-start.13) | collective-permute-done | bytes 196640 | tf_op jit(solution)/shard_map/ppermute | solution.py:443
  47.0 0.8 %collective-permute-done.14.down_half.refs_8_ = bf16[3,256,128]{2,1,0:T(8,128)(2,1)S(1)} collective-permute-done((bf16[3,256,128]{2,1,0:T(8,128)(2,1)S(1)}, bf16[3,256,128]{2,1,0:T(8,128)(2,1)S(1)}, u32[]{:S(2)}, u32[]{:S(2)}) %collective-permute-start.14) | collective-permute-done | bytes 196640 | tf_op jit(solution)/shard_map/ppermute | solution.py:443
  47.8 0.1 cut_columns.7.own_ref.refs_17_
  48.0 0.1 collective-permute-start.21
  48.1 0.5 collective-permute-start.17
  48.6 0.9 %collective-permute-done.19.refs_15_ = bf16[2,3,64,256]{3,2,1,0:T(8,128)(2,1)S(1)} collective-permute-done((bf16[2,3,64,256]{3,2,1,0:T(8,128)(2,1)S(1)}, bf16[2,3,64,256]{3,2,1,0:T(8,128)(2,1)S(1)}, u32[]{:S(2)}, u32[]{:S(2)}) %collective-permute-start.19) | collective-permute-done | bytes 196640 | tf_op jit(solution)/shard_map/ppermute | solution.py:360
  49.5 0.0 collective-permute-start.20
  49.5 0.0 collective-permute-done.21.beside_ref.refs_18_
  49.5 2.1 %collective-permute-start.22 = (bf16[1,3,64,256]{3,2,1,0:T(8,128)(2,1)S(1)}, bf16[1,3,64,256]{3,2,1,0:T(8,128)(2,1)S(1)}, u32[]{:S(2)}, u32[]{:S(2)}) collective-permute-start(bf16[1,3,64,256]{3,2,1,0:T(8,128)(2,1)S(1)} %pick_half.3), channel_id=1, source_target_pairs={{0,2},{1,3},{2,0},{3,1},{4,6},{5,7},{6,4},{7,5},{8,10},{9,11},{10,... | collective-permute-start | bytes 294920 | tf_op jit(solution)/shard_map/ppermute | solution.py:360
  51.6 3.5 %collective-permute-done.22.refs_19_ = bf16[1,3,64,256]{3,2,1,0:T(8,128)(2,1)S(1)} collective-permute-done((bf16[1,3,64,256]{3,2,1,0:T(8,128)(2,1)S(1)}, bf16[1,3,64,256]{3,2,1,0:T(8,128)(2,1)S(1)}, u32[]{:S(2)}, u32[]{:S(2)}) %collective-permute-start.22) | collective-permute-done | bytes 98336 | tf_op jit(solution)/shard_map/ppermute | solution.py:360
  55.1 0.0 collective-permute-start.23
  55.1 0.0 collective-permute-done.17.refs_12_
  55.1 0.0 collective-permute-done.20.refs_16_
  55.1 1.3 %collective-permute-done.23.refs_20_ = bf16[1,3,64,256]{3,2,1,0:T(8,128)(2,1)S(1)} collective-permute-done((bf16[1,3,64,256]{3,2,1,0:T(8,128)(2,1)S(1)}, bf16[1,3,64,256]{3,2,1,0:T(8,128)(2,1)S(1)}, u32[]{:S(2)}, u32[]{:S(2)}) %collective-permute-start.23) | collective-permute-done | bytes 98336 | tf_op jit(solution)/shard_map/ppermute | solution.py:360
  56.4 0.0 copy-done.1
  56.4 1.0 %copy-done.4 = bf16[2,3,256,128]{3,2,1,0:T(8,128)(2,1)S(1)} copy-done((bf16[2,3,256,128]{3,2,1,0:T(8,128)(2,1)S(1)}, bf16[2,3,256,128]{3,2,1,0:T(8,128)(2,1)}, u32[]{:S(2)}) %copy-start.4) | copy-done | bytes 393240
  57.4 8.7 %covariance_tile.1 = (f32[3,3,1024,512]{3,2,1,0:T(8,128)}, f32[64,64]{1,0:T(8,128)}) custom-call(s32[1]{0:T(128)} %bitcast.role_ref, bf16[2,3,256,128]{3,2,1,0:T(8,128)(2,1)} %copy-done.2, bf16[2,3,256,128]{3,2,1,0:T(8,128)(2,1)S(1)} %collective-permute-done.3.refs_1_, bf16[2,3,256,128]{3,2,1,0:T(8,128)(2,1)S(1)} %copy-done.4, ...), custom_call_target="tpu_custom_call" | custom-call | flops 4831838208 | bytes 25165824 | tf_op jit(solution)/shard_map/covariance_tile/pallas_call | solution.py:469
  (14 shorter events, 0.1 us)
Async XLA Ops:
  2.3 3.8 %collective-permute-start.2 = (f32[24,64]{1,0:T(8,128)S(1)}, f32[24,64]{1,0:T(8,128)S(1)}, u32[]{:S(2)}, u32[]{:S(2)}) collective-permute-start(f32[24,64]{1,0:T(8,128)S(1)} %get-tuple-element.20.refs_0_), channel_id=1, source_target_pairs={{0,3},{1,2},{2,1},{3,0},{4,7},{5,6},{6,5},{7,4},{8,11},{9,10},{10,... | collective-permute-start | bytes 18440 | tf_op jit(solution)/shard_map/ppermute | solution.py:360
  4.7 3.7 %collective-permute-start.1 = (f32[24,64]{1,0:T(8,128)S(1)}, f32[24,64]{1,0:T(8,128)S(1)}, u32[]{:S(2)}, u32[]{:S(2)}) collective-permute-start(f32[24,64]{1,0:T(8,128)S(1)} %get-tuple-element.20.refs_0_), channel_id=1, source_target_pairs={{0,2},{1,3},{2,0},{3,1},{4,6},{5,7},{6,4},{7,5},{8,10},{9,11},{10,... | collective-permute-start | bytes 18440 | tf_op jit(solution)/shard_map/ppermute | solution.py:360
  5.4 3.1 %collective-permute-start = (f32[24,64]{1,0:T(8,128)S(1)}, f32[24,64]{1,0:T(8,128)S(1)}, u32[]{:S(2)}, u32[]{:S(2)}) collective-permute-start(f32[24,64]{1,0:T(8,128)S(1)} %get-tuple-element.20.refs_0_), channel_id=1, source_target_pairs={{0,1},{1,0},{2,3},{3,2},{4,5},{5,4},{6,7},{7,6},{8,9},{9,8},{10,11... | collective-permute-start | bytes 18440 | tf_op jit(solution)/shard_map/ppermute | solution.py:360
  9.0 47.3 %copy-start.2 = (bf16[2,3,256,128]{3,2,1,0:T(8,128)(2,1)}, bf16[2,3,256,128]{3,2,1,0:T(8,128)(2,1)S(1)}, u32[]{:S(2)}) copy-start(bf16[2,3,256,128]{3,2,1,0:T(8,128)(2,1)S(1)} %get-tuple-element.23.refs_0_) | copy-start | bytes 1179652
  9.1 10.6 %collective-permute-start.3 = (bf16[2,3,256,128]{3,2,1,0:T(8,128)(2,1)S(1)}, bf16[2,3,256,128]{3,2,1,0:T(8,128)(2,1)S(1)}, u32[]{:S(2)}, u32[]{:S(2)}) collective-permute-start(bf16[2,3,256,128]{3,2,1,0:T(8,128)(2,1)S(1)} %get-tuple-element.23.refs_0_), channel_id=1, source_target_pairs={{0,8},{8,16},{16,24},{24,28},{28,20},{20,12},{12,4},{4,0},{1,9},{9... | collective-permute-start | bytes 1179656 | tf_op jit(solution)/shard_map/ppermute | solution.py:443
  10.7 10.3 %collective-permute-start.4 = (bf16[2,3,256,128]{3,2,1,0:T(8,128)(2,1)S(1)}, bf16[2,3,256,128]{3,2,1,0:T(8,128)(2,1)S(1)}, u32[]{:S(2)}, u32[]{:S(2)}) collective-permute-start(bf16[2,3,256,128]{3,2,1,0:T(8,128)(2,1)S(1)} %get-tuple-element.23.refs_0_), channel_id=1, source_target_pairs={{8,0},{16,8},{24,16},{28,24},{20,28},{12,20},{4,12},{0,4},{9,1},{1... | collective-permute-start | bytes 1179656 | tf_op jit(solution)/shard_map/ppermute | solution.py:443
  11.1 1.4 %copy-start = (bf16[3,1024,256]{2,1,0:T(8,128)(2,1)S(1)}, bf16[3,1024,256]{2,1,0:T(8,128)(2,1)}, u32[]{:S(2)}) copy-start(bf16[3,1024,256]{2,1,0:T(8,128)(2,1)} %eig_ref.1) | copy-start | bytes 4718596
  13.0 0.6 copy-start.5
  13.6 1.9 %collective-permute-start.5 = (f32[64,64]{1,0:T(8,128)S(1)}, f32[64,64]{1,0:T(8,128)S(1)}, u32[]{:S(2)}, u32[]{:S(2)}) collective-permute-start(f32[64,64]{1,0:T(8,128)S(1)} %get-tuple-element.26), channel_id=1, source_target_pairs={{0,1},{1,0},{2,3},{3,2},{4,5},{5,4},{6,7},{7,6},{8,9},{9,8},{10,11... | collective-permute-start | bytes 49160 | tf_op jit(solution)/shard_map/ppermute | solution.py:360
  13.6 4.2 %collective-permute-start.6 = (f32[64,64]{1,0:T(8,128)S(1)}, f32[64,64]{1,0:T(8,128)S(1)}, u32[]{:S(2)}, u32[]{:S(2)}) collective-permute-start(f32[64,64]{1,0:T(8,128)S(1)} %get-tuple-element.27), channel_id=1, source_target_pairs={{0,2},{1,3},{2,0},{3,1},{4,6},{5,7},{6,4},{7,5},{8,10},{9,11},{10,... | collective-permute-start | bytes 49160 | tf_op jit(solution)/shard_map/ppermute | solution.py:360
  14.3 3.7 %collective-permute-start.7 = (f32[64,64]{1,0:T(8,128)S(1)}, f32[64,64]{1,0:T(8,128)S(1)}, u32[]{:S(2)}, u32[]{:S(2)}) collective-permute-start(f32[64,64]{1,0:T(8,128)S(1)} %get-tuple-element.28), channel_id=1, source_target_pairs={{0,3},{1,2},{2,1},{3,0},{4,7},{5,6},{6,5},{7,4},{8,11},{9,10},{10,... | collective-permute-start | bytes 49160 | tf_op jit(solution)/shard_map/ppermute | solution.py:360
  15.5 15.5 %copy-start.6 = (f32[64,64]{1,0:T(8,128)}, f32[64,64]{1,0:T(8,128)S(1)}, u32[]{:S(2)}) copy-start(f32[64,64]{1,0:T(8,128)S(1)} %collective-permute-done.5.refs_22_) | copy-start | bytes 49156
  17.8 13.2 %copy-start.7 = (f32[64,64]{1,0:T(8,128)}, f32[64,64]{1,0:T(8,128)S(1)}, u32[]{:S(2)}) copy-start(f32[64,64]{1,0:T(8,128)S(1)} %collective-permute-done.6.refs_23_) | copy-start | bytes 49156
  18.0 13.0 %copy-start.8 = (f32[64,64]{1,0:T(8,128)}, f32[64,64]{1,0:T(8,128)S(1)}, u32[]{:S(2)}) copy-start(f32[64,64]{1,0:T(8,128)S(1)} %collective-permute-done.7.refs_24_) | copy-start | bytes 49156
  21.0 4.9 %copy-start.3 = (bf16[2,3,256,128]{3,2,1,0:T(8,128)(2,1)}, bf16[2,3,256,128]{3,2,1,0:T(8,128)(2,1)S(1)}, u32[]{:S(2)}) copy-start(bf16[2,3,256,128]{3,2,1,0:T(8,128)(2,1)S(1)} %collective-permute-done.4.refs_2_) | copy-start | bytes 1179652
  21.0 9.3 %collective-permute-start.9 = (bf16[2,3,256,128]{3,2,1,0:T(8,128)(2,1)S(1)}, bf16[2,3,256,128]{3,2,1,0:T(8,128)(2,1)S(1)}, u32[]{:S(2)}, u32[]{:S(2)}) collective-permute-start(bf16[2,3,256,128]{3,2,1,0:T(8,128)(2,1)S(1)} %collective-permute-done.4.refs_2_), channel_id=1, source_target_pairs={{8,0},{16,8},{24,16},{28,24},{20,28},{12,20},{4,12},{0,4},{9,1},{1... | collective-permute-start | bytes 1179656 | tf_op jit(solution)/shard_map/ppermute | solution.py:443
  21.4 9.6 %collective-permute-start.8 = (bf16[2,3,256,128]{3,2,1,0:T(8,128)(2,1)S(1)}, bf16[2,3,256,128]{3,2,1,0:T(8,128)(2,1)S(1)}, u32[]{:S(2)}, u32[]{:S(2)}) collective-permute-start(bf16[2,3,256,128]{3,2,1,0:T(8,128)(2,1)S(1)} %collective-permute-done.3.refs_1_), channel_id=1, source_target_pairs={{0,8},{8,16},{16,24},{24,28},{28,20},{20,12},{12,4},{4,0},{1,9},{9... | collective-permute-start | bytes 1179656 | tf_op jit(solution)/shard_map/ppermute | solution.py:443
  23.2 10.0 %collective-permute-start.12 = (bf16[3,3,64,512]{3,2,1,0:T(8,128)(2,1)S(1)}, bf16[3,3,64,512]{3,2,1,0:T(8,128)(2,1)S(1)}, u32[]{:S(2)}, u32[]{:S(2)}) collective-permute-start(bf16[3,3,64,512]{3,2,1,0:T(8,128)(2,1)S(1)} %cut_columns.4.refs_0_), channel_id=1, source_target_pairs={{0,2},{4,6},{9,11},{13,15},{18,16},{22,20},{27,25},{31,29}} | collective-permute-start | bytes 1769480 | tf_op jit(solution)/shard_map/ppermute | solution.py:422
  30.3 8.4 %collective-permute-start.11 = (bf16[2,3,256,128]{3,2,1,0:T(8,128)(2,1)S(1)}, bf16[2,3,256,128]{3,2,1,0:T(8,128)(2,1)S(1)}, u32[]{:S(2)}, u32[]{:S(2)}) collective-permute-start(bf16[2,3,256,128]{3,2,1,0:T(8,128)(2,1)S(1)} %collective-permute-done.9.refs_1_.refs_4_), channel_id=1, source_target_pairs={{8,0},{16,8},{24,16},{28,24},{20,28},{12,20},{4,12},{0,4},{9,1},{1... | collective-permute-start | bytes 1179656 | tf_op jit(solution)/shard_map/ppermute | solution.py:443
  31.0 8.4 %collective-permute-start.10 = (bf16[2,3,256,128]{3,2,1,0:T(8,128)(2,1)S(1)}, bf16[2,3,256,128]{3,2,1,0:T(8,128)(2,1)S(1)}, u32[]{:S(2)}, u32[]{:S(2)}) collective-permute-start(bf16[2,3,256,128]{3,2,1,0:T(8,128)(2,1)S(1)} %collective-permute-done.8.refs_0_.refs_3_), channel_id=1, source_target_pairs={{0,8},{8,16},{16,24},{24,28},{28,20},{20,12},{12,4},{4,0},{1,9},{9... | collective-permute-start | bytes 1179656 | tf_op jit(solution)/shard_map/ppermute | solution.py:443
  33.3 23.1 %copy-start.1 = (bf16[3,3,64,512]{3,2,1,0:T(8,128)(2,1)}, bf16[3,3,64,512]{3,2,1,0:T(8,128)(2,1)S(1)}, u32[]{:S(2)}) copy-start(bf16[3,3,64,512]{3,2,1,0:T(8,128)(2,1)S(1)} %pass_on.2.refs_9_) | copy-start | bytes 1769476
  33.3 12.6 %collective-permute-start.15 = (bf16[3,3,64,512]{3,2,1,0:T(8,128)(2,1)S(1)}, bf16[3,3,64,512]{3,2,1,0:T(8,128)(2,1)S(1)}, u32[]{:S(2)}, u32[]{:S(2)}) collective-permute-start(bf16[3,3,64,512]{3,2,1,0:T(8,128)(2,1)S(1)} %pass_on.2.refs_9_), channel_id=1, source_target_pairs={{0,1},{1,0},{2,3},{3,2},{4,5},{5,4},{6,7},{7,6},{8,9},{9,8},{10,11... | collective-permute-start | bytes 1769480 | tf_op jit(solution)/shard_map/ppermute | solution.py:360
  33.5 9.7 %collective-permute-start.16 = (bf16[2,3,64,512]{3,2,1,0:T(8,128)(2,1)S(1)}, bf16[2,3,64,512]{3,2,1,0:T(8,128)(2,1)S(1)}, u32[]{:S(2)}, u32[]{:S(2)}) collective-permute-start(bf16[2,3,64,512]{3,2,1,0:T(8,128)(2,1)S(1)} %cut_columns.6.refs_0_), channel_id=1, source_target_pairs={{0,2},{4,6},{9,11},{13,15},{18,16},{22,20},{27,25},{31,29}} | collective-permute-start | bytes 1179656 | tf_op jit(solution)/shard_map/ppermute | solution.py:422
  39.6 3.6 %collective-permute-start.18 = (bf16[2,3,64,512]{3,2,1,0:T(8,128)(2,1)S(1)}, bf16[2,3,64,512]{3,2,1,0:T(8,128)(2,1)S(1)}, u32[]{:S(2)}, u32[]{:S(2)}) collective-permute-start(bf16[2,3,64,512]{3,2,1,0:T(8,128)(2,1)S(1)} %get-tuple-element.33.own_ref.refs_13_), channel_id=1, source_target_pairs={{0,1},{1,0},{2,3},{3,2},{4,5},{5,4},{6,7},{7,6},{8,9},{9,8},{10,11... | collective-permute-start | bytes 1179656 | tf_op jit(solution)/shard_map/ppermute | solution.py:360
  39.7 7.3 %collective-permute-start.13 = (bf16[3,256,128]{2,1,0:T(8,128)(2,1)S(1)}, bf16[3,256,128]{2,1,0:T(8,128)(2,1)S(1)}, u32[]{:S(2)}, u32[]{:S(2)}) collective-permute-start(bf16[3,256,128]{2,1,0:T(8,128)(2,1)S(1)} %get-tuple-element.31), channel_id=1, source_target_pairs={{0,8},{8,16},{16,24},{24,28},{28,20},{20,12},{12,4},{4,0},{1,9},{9... | collective-permute-start | bytes 589832 | tf_op jit(solution)/shard_map/ppermute | solution.py:443
  40.9 7.0 %collective-permute-start.14 = (bf16[3,256,128]{2,1,0:T(8,128)(2,1)S(1)}, bf16[3,256,128]{2,1,0:T(8,128)(2,1)S(1)}, u32[]{:S(2)}, u32[]{:S(2)}) collective-permute-start(bf16[3,256,128]{2,1,0:T(8,128)(2,1)S(1)} %get-tuple-element.32), channel_id=1, source_target_pairs={{8,0},{16,8},{24,16},{28,24},{20,28},{12,20},{4,12},{0,4},{9,1},{1... | collective-permute-start | bytes 589832 | tf_op jit(solution)/shard_map/ppermute | solution.py:443
  43.3 6.2 %collective-permute-start.19 = (bf16[2,3,64,256]{3,2,1,0:T(8,128)(2,1)S(1)}, bf16[2,3,64,256]{3,2,1,0:T(8,128)(2,1)S(1)}, u32[]{:S(2)}, u32[]{:S(2)}) collective-permute-start(bf16[2,3,64,256]{3,2,1,0:T(8,128)(2,1)S(1)} %pick_half.2), channel_id=1, source_target_pairs={{0,2},{1,3},{2,0},{3,1},{4,6},{5,7},{6,4},{7,5},{8,10},{9,11},{10,... | collective-permute-start | bytes 589832 | tf_op jit(solution)/shard_map/ppermute | solution.py:360
  48.0 1.5 %collective-permute-start.21 = (bf16[1,3,64,512]{3,2,1,0:T(8,128)(2,1)S(1)}, bf16[1,3,64,512]{3,2,1,0:T(8,128)(2,1)S(1)}, u32[]{:S(2)}, u32[]{:S(2)}) collective-permute-start(bf16[1,3,64,512]{3,2,1,0:T(8,128)(2,1)S(1)} %cut_columns.7.own_ref.refs_17_), channel_id=1, source_target_pairs={{0,1},{1,0},{2,3},{3,2},{4,5},{5,4},{6,7},{7,6},{8,9},{9,8},{10,11... | collective-permute-start | bytes 589832 | tf_op jit(solution)/shard_map/ppermute | solution.py:360
  48.1 7.0 %collective-permute-start.17 = (bf16[2,3,64,512]{3,2,1,0:T(8,128)(2,1)S(1)}, bf16[2,3,64,512]{3,2,1,0:T(8,128)(2,1)S(1)}, u32[]{:S(2)}, u32[]{:S(2)}) collective-permute-start(bf16[2,3,64,512]{3,2,1,0:T(8,128)(2,1)S(1)} %pass_on.3.refs_11_), channel_id=1, source_target_pairs={{0,1},{1,0},{2,3},{3,2},{4,5},{5,4},{6,7},{7,6},{8,9},{9,8},{10,11... | collective-permute-start | bytes 1179656 | tf_op jit(solution)/shard_map/ppermute | solution.py:360
  49.5 5.6 %collective-permute-start.20 = (bf16[2,3,64,256]{3,2,1,0:T(8,128)(2,1)S(1)}, bf16[2,3,64,256]{3,2,1,0:T(8,128)(2,1)S(1)}, u32[]{:S(2)}, u32[]{:S(2)}) collective-permute-start(bf16[2,3,64,256]{3,2,1,0:T(8,128)(2,1)S(1)} %collective-permute-done.19.refs_15_), channel_id=1, source_target_pairs={{0,1},{1,0},{2,3},{3,2},{4,5},{5,4},{6,7},{7,6},{8,9},{9,8},{10,11... | collective-permute-start | bytes 589832 | tf_op jit(solution)/shard_map/ppermute | solution.py:360
  49.5 5.5 %collective-permute-start.22 = (bf16[1,3,64,256]{3,2,1,0:T(8,128)(2,1)S(1)}, bf16[1,3,64,256]{3,2,1,0:T(8,128)(2,1)S(1)}, u32[]{:S(2)}, u32[]{:S(2)}) collective-permute-start(bf16[1,3,64,256]{3,2,1,0:T(8,128)(2,1)S(1)} %pick_half.3), channel_id=1, source_target_pairs={{0,2},{1,3},{2,0},{3,1},{4,6},{5,7},{6,4},{7,5},{8,10},{9,11},{10,... | collective-permute-start | bytes 294920 | tf_op jit(solution)/shard_map/ppermute | solution.py:360
  55.1 1.3 %collective-permute-start.23 = (bf16[1,3,64,256]{3,2,1,0:T(8,128)(2,1)S(1)}, bf16[1,3,64,256]{3,2,1,0:T(8,128)(2,1)S(1)}, u32[]{:S(2)}, u32[]{:S(2)}) collective-permute-start(bf16[1,3,64,256]{3,2,1,0:T(8,128)(2,1)S(1)} %collective-permute-done.22.refs_19_), channel_id=1, source_target_pairs={{0,1},{1,0},{2,3},{3,2},{4,5},{5,4},{6,7},{7,6},{8,9},{9,8},{10,11... | collective-permute-start | bytes 294920 | tf_op jit(solution)/shard_map/ppermute | solution.py:360
  56.4 1.0 %copy-start.4 = (bf16[2,3,256,128]{3,2,1,0:T(8,128)(2,1)S(1)}, bf16[2,3,256,128]{3,2,1,0:T(8,128)(2,1)}, u32[]{:S(2)}) copy-start(bf16[2,3,256,128]{3,2,1,0:T(8,128)(2,1)} %copy-done.3) | copy-start | bytes 1179652
